TPU v7x, 32 devices: a whole 2x2x4 slice. The times are simulated.
32 devices in a mesh: dp: 16 (over z, x, core), mp: 2 (over y).
Axes of the slice: x: 2, y: 2, z: 4, core: 2. Of those that a mesh axis runs over, the one named last changes fastest.
Arguments:
- tokens: bfloat16 [8192, 768], P('dp'), may hold values from -6 to 6
- segment_ids: int32 [16, 512], P('dp'), may hold values from 0 to 3, never falling along the last dimension, each value on 1 to 256 neighbouring positions
- gain_attn: float32 [768], P('dp'), may hold values from 0.1 to 1.9
- gain_ffn: float32 [768], P('dp'), may hold values from 0.1 to 1.9
- random_scores: float32 [12, 512, 512], P('mp', 'dp'), may hold values from -6 to 6
- w_value: float32 [768, 768], P('dp', 'mp'), may hold values from -0.21875 to 0.21875
- w_output: float32 [768, 768], P('mp', 'dp'), may hold values from -0.875 to 0.875
- w_up: float32 [768, 3072], P('dp', 'mp'), may hold values from -0.21875 to 0.21875
- w_down: float32 [3072, 768], P('mp', 'dp'), may hold values from -0.109375 to 0.109375
- cotangent: bfloat16 [8192, 768], P('dp'), may hold values from -6 to 6
Outputs:
- output: bfloat16 [8192, 768], P('dp')
- grad_tokens: bfloat16 [8192, 768], P('dp')
- grad_gain_attn: float32 [768], P('dp')
- grad_gain_ffn: float32 [768], P('dp')
- grad_scores: float32 [12, 512, 512], P('mp', 'dp')
- grad_value: float32 [768, 768], P('dp', 'mp')
- grad_output: float32 [768, 768], P('mp', 'dp')
- grad_up: float32 [768, 3072], P('dp', 'mp')
- grad_down: float32 [3072, 768], P('mp', 'dp')
Inputs may be any that keep to these rules, and one draw needn't show every extreme that they name: `segment_ids`: within each packed row the ids never fall; each of the 4 documents of a row holds 1 to 256 tokens and one holds exactly 256.
All inputs are finite; a program needn't handle non-finite values.
Results may differ from a plain program's by a relative error of at most 0.015.
Values may be sent and summed in bfloat16 or wider, within the bound.
No kernel may reach another device: no remote copies, remote signals or barrier semaphores. Data moves between devices by JAX's collectives and lax.ppermute only.
A program may use at most 128 MiB of HBM per device.

v0:
```python
import jax
import jax.numpy as jnp
from jax import lax
from jax.sharding import PartitionSpec as P

EPSILON = 1e-06
NEGATIVE = -1e30


def shards(
    tokens,
    segment_ids,
    gain_attn,
    gain_ffn,
    random_scores,
    w_value,
    w_output,
    w_up,
    w_down,
    cotangent,
):
    gathered = (
        lax.all_gather(gain_attn.astype(jnp.bfloat16), "dp", axis=0, tiled=True),
        lax.all_gather(gain_ffn.astype(jnp.bfloat16), "dp", axis=0, tiled=True),
        lax.all_gather(random_scores.astype(jnp.bfloat16), "dp", axis=1, tiled=True),
        lax.all_gather(w_value.astype(jnp.bfloat16), "dp", axis=0, tiled=True),
        lax.all_gather(w_output.astype(jnp.bfloat16), "dp", axis=1, tiled=True),
        lax.all_gather(w_up.astype(jnp.bfloat16), "dp", axis=0, tiled=True),
        lax.all_gather(w_down.astype(jnp.bfloat16), "dp", axis=1, tiled=True),
    )
    gain_one, gain_two, scores_low, value_proj, output_proj, up_proj, down_proj = gathered
    rows_local = segment_ids.shape[0]
    length = segment_ids.shape[1]
    heads_local = scores_low.shape[0]
    head_size = value_proj.shape[1] // heads_local
    scores_full = scores_low.astype(jnp.float32)
    gain_one_f = gain_one.astype(jnp.float32)
    gain_two_f = gain_two.astype(jnp.float32)
    tokens_full = tokens.astype(jnp.float32)
    cot_full = cotangent.astype(jnp.float32)
    share = tokens.shape[0] // lax.axis_size("mp")
    first = lax.axis_index("mp") * share
    tok_here = lax.dynamic_slice_in_dim(tokens_full, first, share, 0)
    cot_here = lax.dynamic_slice_in_dim(cot_full, first, share, 0)
    inv_one = lax.rsqrt(jnp.mean(tok_here * tok_here, axis=-1, keepdims=True) + EPSILON)
    normed_here = (tok_here * inv_one * gain_one_f).astype(jnp.bfloat16)
    normed_one = lax.all_gather(normed_here, "mp", axis=0, tiled=True)
    values = jnp.dot(normed_one, value_proj, preferred_element_type=jnp.float32).astype(
        jnp.bfloat16
    )
    value_rows = values.reshape(rows_local, length, heads_local, head_size)

    def masked_scores(seg_row):
        same = seg_row[:, None] == seg_row[None, :]
        return jnp.where(same[None], scores_full, NEGATIVE)

    def forward_row(pair):
        seg_row, value_row = pair
        masked = masked_scores(seg_row)
        top_score = jnp.max(masked, axis=-1, keepdims=True)
        expo = jnp.exp(masked - top_score)
        total = jnp.sum(expo, axis=-1, keepdims=True)
        probs = expo / total
        log_total = top_score[..., 0] + jnp.log(total[..., 0])
        mixed_row = jnp.einsum(
            "hij,jhc->ihc",
            probs.astype(jnp.bfloat16),
            value_row,
            preferred_element_type=jnp.float32,
        )
        return (mixed_row.reshape(length, heads_local * head_size).astype(jnp.bfloat16), log_total)

    mixed_rows, log_totals = lax.map(forward_row, (segment_ids, value_rows))
    mixed = mixed_rows.reshape(rows_local * length, heads_local * head_size)
    attn_terms = jnp.dot(mixed, output_proj, preferred_element_type=jnp.float32)
    attn = lax.psum_scatter(
        attn_terms.astype(jnp.bfloat16), "mp", scatter_dimension=0, tiled=True
    ).astype(jnp.float32)
    resid = tok_here + attn
    inv_two = lax.rsqrt(jnp.mean(resid * resid, axis=-1, keepdims=True) + EPSILON)
    normed_two_here = (resid * inv_two * gain_two_f).astype(jnp.bfloat16)
    normed_two = lax.all_gather(normed_two_here, "mp", axis=0, tiled=True)
    pre_act = jnp.dot(normed_two, up_proj, preferred_element_type=jnp.float32)
    act_value, gelu_pull = jax.vjp(jax.nn.gelu, pre_act)
    act = act_value.astype(jnp.bfloat16)
    ffn_terms = jnp.dot(act, down_proj, preferred_element_type=jnp.float32)
    ffn_out = lax.psum_scatter(
        ffn_terms.astype(jnp.bfloat16), "mp", scatter_dimension=0, tiled=True
    ).astype(jnp.float32)
    output_here = (resid + ffn_out).astype(jnp.bfloat16)
    grad_down = jnp.dot(act.T, cotangent, preferred_element_type=jnp.float32)
    grad_act = jnp.dot(cotangent, down_proj.T, preferred_element_type=jnp.float32)
    grad_pre = gelu_pull(grad_act)[0].astype(jnp.bfloat16)
    grad_up = jnp.dot(normed_two.T, grad_pre, preferred_element_type=jnp.float32)
    back_terms = jnp.dot(grad_pre, up_proj.T, preferred_element_type=jnp.float32)
    grad_normed_two = lax.psum_scatter(
        back_terms.astype(jnp.bfloat16), "mp", scatter_dimension=0, tiled=True
    ).astype(jnp.float32)
    scaled_two = gain_two_f * grad_normed_two
    grad_gain_two = jnp.sum(grad_normed_two * resid * inv_two, axis=0)
    grad_resid = (
        cot_here
        + inv_two * scaled_two
        - resid * inv_two**3 * jnp.mean(scaled_two * resid, axis=-1, keepdims=True)
    )
    grad_attn_here = grad_resid.astype(jnp.bfloat16)
    output, grad_attn = (
        lax.all_gather(output_here, "mp", axis=0, tiled=True),
        lax.all_gather(grad_attn_here, "mp", axis=0, tiled=True),
    )
    grad_output = jnp.dot(mixed.T, grad_attn, preferred_element_type=jnp.float32)
    grad_mixed = jnp.dot(grad_attn, output_proj.T, preferred_element_type=jnp.float32).astype(
        jnp.bfloat16
    )
    grad_mixed_rows = grad_mixed.reshape(rows_local, length, heads_local, head_size)

    def backward_row(carry, inputs):
        seg_row, log_row, value_row, grad_row = inputs
        masked = masked_scores(seg_row)
        probs = jnp.exp(masked - log_row[..., None])
        grad_probs = jnp.einsum(
            "ihc,jhc->hij", grad_row, value_row, preferred_element_type=jnp.float32
        )
        grad_vals = jnp.einsum(
            "hij,ihc->jhc", probs.astype(jnp.bfloat16), grad_row, preferred_element_type=jnp.float32
        )
        inner = jnp.sum(probs * grad_probs, axis=-1, keepdims=True)
        return (
            carry + probs * (grad_probs - inner),
            grad_vals.reshape(length, heads_local * head_size).astype(jnp.bfloat16),
        )

    start_scores = jnp.zeros(scores_full.shape, jnp.float32)
    grad_scores, grad_value_rows = lax.scan(
        backward_row, start_scores, (segment_ids, log_totals, value_rows, grad_mixed_rows)
    )
    grad_values = grad_value_rows.reshape(rows_local * length, heads_local * head_size)
    grad_value = jnp.dot(normed_one.T, grad_values, preferred_element_type=jnp.float32)
    first_terms = jnp.dot(grad_values, value_proj.T, preferred_element_type=jnp.float32)
    grad_normed_one = lax.psum_scatter(
        first_terms.astype(jnp.bfloat16), "mp", scatter_dimension=0, tiled=True
    ).astype(jnp.float32)
    scaled_one = gain_one_f * grad_normed_one
    grad_gain_one = jnp.sum(grad_normed_one * tok_here * inv_one, axis=0)
    grad_tokens_here = (
        grad_resid
        + inv_one * scaled_one
        - tok_here * inv_one**3 * jnp.mean(scaled_one * tok_here, axis=-1, keepdims=True)
    ).astype(jnp.bfloat16)
    grad_tokens = lax.all_gather(grad_tokens_here, "mp", axis=0, tiled=True)
    summed = (
        lax.psum_scatter(grad_gain_one, "dp", scatter_dimension=0, tiled=True),
        lax.psum_scatter(grad_gain_two, "dp", scatter_dimension=0, tiled=True),
        lax.psum_scatter(grad_scores, "dp", scatter_dimension=1, tiled=True),
        lax.psum_scatter(grad_value, "dp", scatter_dimension=0, tiled=True),
        lax.psum_scatter(grad_output, "dp", scatter_dimension=1, tiled=True),
        lax.psum_scatter(grad_up, "dp", scatter_dimension=0, tiled=True),
        lax.psum_scatter(grad_down, "dp", scatter_dimension=1, tiled=True),
    )
    out_gain_one, out_gain_two, out_scores, out_value, out_output, out_up, out_down = summed
    out_gain_one, out_gain_two = lax.psum((out_gain_one, out_gain_two), "mp")
    return (
        output,
        grad_tokens,
        out_gain_one,
        out_gain_two,
        out_scores,
        out_value,
        out_output,
        out_up,
        out_down,
    )


def solution(mesh):
    in_specs = (
        P("dp", None),
        P("dp", None),
        P("dp"),
        P("dp"),
        P("mp", "dp", None),
        P("dp", "mp"),
        P("mp", "dp"),
        P("dp", "mp"),
        P("mp", "dp"),
        P("dp", None),
    )
    out_specs = (
        P("dp", None),
        P("dp", None),
        P("dp"),
        P("dp"),
        P("mp", "dp", None),
        P("dp", "mp"),
        P("mp", "dp"),
        P("dp", "mp"),
        P("mp", "dp"),
    )
    return jax.shard_map(shards, mesh=mesh, in_specs=in_specs, out_specs=out_specs, check_vma=False)
```

profile of v0, /device:TPU:0, one launch (start us, length us, event | category | flops | bytes accessed | tf_op | source)
XLA Modules:
  0.0 662.2 jit_solution(1509501508696546279)
XLA Ops:
  7.2 1.7 convert_element_type.121
  9.0 1.6 convert_element_type.135
  10.7 0.7 convert_element_type.116
  11.4 0.7 convert_element_type.130
  12.0 1.3 fusion.43
  14.5 35.4 %all-reduce.6 = (bf16[768]{0:T(1024)(128)(2,1)S(1)}, bf16[768]{0:T(1024)(128)(2,1)S(1)}) all-reduce(bf16[768]{0:T(1024)(128)(2,1)S(1)} %dynamic-update-slice, bf16[768]{0:T(1024)(128)(2,1)S(1)} %dynamic-update-slice.1), channel_id=1, replica_groups=mesh['dp'=16,'mp'=2] {'dp'}, use_global_device_ids=true, to_apply=%add | all-reduce | flops 1536 | bytes 6144
  49.8 0.9 convert_element_type.119
  50.7 0.9 convert_element_type.127
  51.6 1.2 fusion.34
  53.4 1.2 fusion.36
  54.6 8.5 %all_gather.37 = bf16[512,768]{1,0:T(8,128)(2,1)S(1)} all-gather(bf16[256,768]{1,0:T(8,128)(2,1)S(1)} %fusion.36), channel_id=1, replica_groups=mesh['dp'=16,'mp'=2] {'mp'}, dimensions={0}, use_global_device_ids=true | all-gather | bytes 1179648 | tf_op jit(solution)/shard_map/all_gather | solution.py:47
  63.3 19.8 %all_gather.38 = bf16[768,384]{1,0:T(8,128)(2,1)S(1)} all-gather(bf16[48,384]{1,0:T(8,128)(2,1)S(1)} %convert_element_type.119), channel_id=1, replica_groups=mesh['dp'=16,'mp'=2] {'dp'}, dimensions={0}, use_global_device_ids=true | all-gather | bytes 626688 | tf_op jit(solution)/shard_map/all_gather | solution.py:26
  83.1 1.3 convolution_convert_fusion.5
  84.3 23.7 %all_gather.40 = bf16[384,768]{0,1:T(8,128)(2,1)} all-gather(bf16[384,48]{0,1:T(8,128)(2,1)S(1)} %convert_element_type.127), channel_id=1, replica_groups=mesh['dp'=16,'mp'=2] {'dp'}, dimensions={1}, use_global_device_ids=true | all-gather | bytes 626688 | tf_op jit(solution)/shard_map/all_gather | solution.py:27
  108.0 3.2 copy.23
  111.2 0.7 fusion
  111.9 1.3 fusion.2
  113.3 1.9 fusion.20
  115.2 0.7 copy-done.17
  115.9 1.5 convolution_convert_fusion.3
  117.5 1.6 convert_element_type.133
  119.3 5.2 fusion.44
  124.4 7.1 %reduce-scatter.10.cloned.1.call-done = bf16[256,768]{1,0:T(8,128)(2,1)} async-done(((bf16[512,768]{1,0:T(8,128)(2,1)}), bf16[256,768]{1,0:T(8,128)(2,1)}) %reduce-scatter.10.cloned.1.call-update) | async-done | bytes 393232 | tf_op jit(solution)/shard_map/reduce_scatter | solution.py:76
  131.6 1.3 multiply_reduce_fusion.1
  132.9 0.6 multiply_multiply_fusion.3
  133.5 1.3 multiply_convert_fusion.1
  134.8 11.8 %all_gather.42 = bf16[512,768]{1,0:T(8,128)(2,1)} all-gather(bf16[256,768]{1,0:T(8,128)(2,1)S(1)} %multiply_convert_fusion.1), channel_id=1, replica_groups=mesh['dp'=16,'mp'=2] {'mp'}, dimensions={0}, use_global_device_ids=true | all-gather | bytes 1179648 | tf_op jit(solution)/shard_map/all_gather | solution.py:82
  146.6 30.3 %all-gather.6.cloned.1.call-done = bf16[768,1536]{1,0:T(8,128)(2,1)} async-done(((bf16[48,1536]{1,0:T(8,128)(2,1)}), bf16[768,1536]{1,0:T(8,128)(2,1)}) %all-gather.6.cloned.1.call-update) | async-done | bytes 2359312 | tf_op jit(solution)/shard_map/all_gather | solution.py:28
  176.9 7.5 %fusion.9 = (bf16[512,1536]{1,0:T(8,128)(2,1)S(1)}, f32[512,1536]{1,0:T(8,128)}) fusion(f32[512,1536]{1,0:T(8,128)} %fusion.44, bf16[512,768]{1,0:T(8,128)(2,1)} %all_gather.42, bf16[768,1536]{1,0:T(8,128)(2,1)} %all-gather.6.cloned.1.call-done), kind=kOutput, calls=%fused_computation.17 | convolution fusion | flops 1223688192 | bytes 11010048 | tf_op jit(solution)/shard_map/dot_general | solution.py:83
  184.4 1.1 copy-done.15
  185.6 2.3 convolution_convert_fusion
  187.9 1.3 log_add_fusion
  189.3 15.0 %reduce-scatter.14.cloned.1.call-done = bf16[256,768]{1,0:T(8,128)(2,1)} async-done(((bf16[512,768]{1,0:T(8,128)(2,1)}), bf16[256,768]{1,0:T(8,128)(2,1)}) %reduce-scatter.14.cloned.1.call-update) | async-done | bytes 393232 | tf_op jit(solution)/shard_map/reduce_scatter | solution.py:96
  204.3 2.1 fusion.31
  206.9 1.6 fusion.41
  208.5 11.5 %all_gather.46 = bf16[512,768]{1,0:T(8,128)(2,1)S(1)} all-gather(bf16[256,768]{1,0:T(8,128)(2,1)S(1)} %fusion.41), channel_id=1, replica_groups=mesh['dp'=16,'mp'=2] {'mp'}, dimensions={0}, use_global_device_ids=true | all-gather | bytes 1179648 | tf_op jit(solution)/shard_map/all_gather | solution.py:109
  220.0 0.9 copy-done.9
  221.5 1.7 fusion.17
  223.2 0.7 copy-done.19
  223.9 1.5 convolution_convert_fusion.2
  225.5 5.5 convolution_convert_fusion.1
  231.3 3.4 multiply_reduce_fusion
  234.7 4.4 subtract_multiply_fusion
  239.1 9.7 %copy.26 = f32[6,512,512]{2,0,1:T(8,128)} copy(f32[6,512,512]{1,2,0:T(8,128)} %subtract_multiply_fusion) | data formatting | bytes 12582912 | tf_op jit(solution)/shard_map/while/body/eval_jaxpr/mul | solution.py:129
  248.9 1.0 copy-done.10
  250.0 1.6 fusion.46
  251.7 1.6 fusion.45
  253.4 5.7 fusion.42
  259.2 1.1 copy-done.6
  260.8 3.5 fusion.47
  265.4 1.3 fusion.33
  266.7 32.8 %all-reduce.4 = (f32[768]{0:T(1024)S(1)}, f32[768]{0:T(1024)S(1)}) all-reduce(f32[768]{0:T(1024)S(1)} %get-tuple-element.71, f32[768]{0:T(1024)S(1)} %copy-done.32), channel_id=6, replica_groups=mesh['dp'=16,'mp'=2] {'dp'}, use_global_device_ids=true, to_apply=%region_11.12.clone | all-reduce | flops 1536 | bytes 12288
  299.8 1.7 fusion.26
  301.5 9.2 %all_gather.47 = bf16[512,768]{1,0:T(8,128)(2,1)S(1)} all-gather(bf16[256,768]{1,0:T(8,128)(2,1)S(1)} %get-tuple-element.79), channel_id=1, replica_groups=mesh['dp'=16,'mp'=2] {'mp'}, dimensions={0}, use_global_device_ids=true | all-gather | bytes 1179648 | tf_op jit(solution)/shard_map/all_gather | solution.py:150
  310.7 8.5 %all_gather.45 = bf16[512,768]{1,0:T(8,128)(2,1)S(1)} all-gather(bf16[256,768]{1,0:T(8,128)(2,1)S(1)} %get-tuple-element.80), channel_id=1, replica_groups=mesh['dp'=16,'mp'=2] {'mp'}, dimensions={0}, use_global_device_ids=true | all-gather | bytes 1179648 | tf_op jit(solution)/shard_map/all_gather | solution.py:108
  319.2 5.4 all-reduce.5
  324.6 47.5 %reduce-scatter.18.cloned.1.call-done = f32[6,32,512]{2,0,1:T(8,128)} async-done(((f32[6,512,512]{2,0,1:T(8,128)}), f32[6,32,512]{2,0,1:T(8,128)}) %reduce-scatter.18.cloned.1.call-update) | async-done | bytes 393232 | tf_op jit(solution)/shard_map/reduce_scatter | solution.py:154
  372.1 2.0 copy.27
  374.1 60.0 %reduce-scatter.22.cloned.1.call-done = f32[384,48]{0,1:T(8,128)} async-done(((f32[384,768]{0,1:T(8,128)}), f32[384,48]{0,1:T(8,128)}) %reduce-scatter.22.cloned.1.call-update) | async-done | bytes 73744 | tf_op jit(solution)/shard_map/reduce_scatter | solution.py:156
  434.1 61.1 %reduce-scatter.20.cloned.1.call-done = f32[48,384]{1,0:T(8,128)} async-done(((f32[768,384]{1,0:T(8,128)}), f32[48,384]{1,0:T(8,128)}) %reduce-scatter.20.cloned.1.call-update) | async-done | bytes 73744 | tf_op jit(solution)/shard_map/reduce_scatter | solution.py:155
  495.1 79.1 %reduce-scatter.26.cloned.1.call-done = f32[1536,48]{0,1:T(8,128)} async-done(((f32[1536,768]{0,1:T(8,128)}), f32[1536,48]{0,1:T(8,128)}) %reduce-scatter.26.cloned.1.call-update) | async-done | bytes 294928 | tf_op jit(solution)/shard_map/reduce_scatter | solution.py:158
  574.2 79.4 %reduce-scatter.24.cloned.1.call-done = f32[48,1536]{1,0:T(8,128)} async-done(((f32[768,1536]{1,0:T(8,128)}), f32[48,1536]{1,0:T(8,128)}) %reduce-scatter.24.cloned.1.call-update) | async-done | bytes 294928 | tf_op jit(solution)/shard_map/reduce_scatter | solution.py:157
  653.6 0.9 copy.34
  654.5 0.9 copy.35
  (117 shorter events, 4.5 us)
Async XLA Ops:
  7.2 55.8 %copy-start.36 = (s32[1,512]{1,0:T(1,128)S(1)}, s32[1,512]{1,0:T(1,128)}, u32[]{:S(2)}) copy-start(s32[1,512]{1,0:T(1,128)} %param.11) | copy-start | bytes 6148
  7.2 100.8 %all-gather.4.cloned.1.call-start = ((), (), s32[]{:S(2)}) async-start(), calls=%async_computation.9 | async-start | bytes 3342336 | tf_op jit(solution)/shard_map/all_gather | solution.py:25
  9.0 110.3 %all-gather.8.cloned.1.call-start = ((), (), s32[]{:S(2)}) async-start(), calls=%async_computation.12 | async-start | bytes 2506752 | tf_op jit(solution)/shard_map/all_gather | solution.py:29
  10.6 120.9 %reduce-scatter.10.cloned.1.call-start = ((), (), s32[]{:S(2)}) async-start(), calls=%async_computation.10 | async-start | bytes 1179648 | tf_op jit(solution)/shard_map/reduce_scatter | solution.py:76
  49.8 13.2 %copy-start.24 = (f32[768]{0:T(1024)}, f32[768]{0:T(1024)S(1)}, u32[]{:S(2)}) copy-start(f32[768]{0:T(1024)S(1)} %convert_element_type.117) | copy-start | bytes 9220
  53.4 9.6 %copy-start.30 = (f32[256]{0:T(256)}, f32[256]{0:T(256)S(1)}, u32[]{:S(2)}) copy-start(f32[256]{0:T(256)S(1)} %get-tuple-element.82) | copy-start | bytes 3076
  63.0 20.0 %copy-start.7 = (bf16[512,768]{1,0:T(8,128)(2,1)}, bf16[512,768]{1,0:T(8,128)(2,1)S(1)}, u32[]{:S(2)}) copy-start(bf16[512,768]{1,0:T(8,128)(2,1)S(1)} %all_gather.37) | copy-start | bytes 2359300
  63.2 50.0 %copy-start.2 = (pred[512,512]{0,1:T(8,128)(4,1)}, pred[512,512]{0,1:T(8,128)(4,1)S(1)}, u32[]{:S(2)}) copy-start(pred[512,512]{0,1:T(8,128)(4,1)S(1)} %broadcast_compare_fusion) | copy-start | bytes 786436
  83.0 1.3 copy-start.11
  111.2 2.1 copy-start.39
  113.2 1.9 copy-start.26
  113.3 2.7 copy-start.13
  115.2 0.8 copy-start.17
  117.4 59.4 %all-gather.6.cloned.1.call-start = ((), (), s32[]{:S(2)}) async-start(), calls=%async_computation.11 | async-start | bytes 2506752 | tf_op jit(solution)/shard_map/all_gather | solution.py:28
  119.2 85.1 %reduce-scatter.14.cloned.1.call-start = ((), (), s32[]{:S(2)}) async-start(), calls=%async_computation.14 | async-start | bytes 1179648 | tf_op jit(solution)/shard_map/reduce_scatter | solution.py:96
  119.2 14.3 %copy-start.22 = (f32[768]{0:T(1024)}, f32[768]{0:T(1024)S(1)}, u32[]{:S(2)}) copy-start(f32[768]{0:T(1024)S(1)} %convert_element_type.131) | copy-start | bytes 9220
  133.5 50.9 %copy-start.28 = (f32[256]{0:T(256)}, f32[256]{0:T(256)S(1)}, u32[]{:S(2)}) copy-start(f32[256]{0:T(256)S(1)} %get-tuple-element.84) | copy-start | bytes 3076
  176.9 8.7 %copy-start.38 = (bf16[768,1536]{1,0:T(8,128)(2,1)S(1)}, bf16[768,1536]{1,0:T(8,128)(2,1)}, u32[]{:S(2)}) copy-start(bf16[768,1536]{1,0:T(8,128)(2,1)} %all-gather.6.cloned.1.call-done) | copy-start | bytes 7077892
  184.4 1.1 copy-start.15
  185.6 18.7 %copy-start.1 = (bf16[256,768]{1,0:T(8,128)(2,1)S(1)}, bf16[256,768]{1,0:T(8,128)(2,1)}, u32[]{:S(2)}) copy-start(bf16[256,768]{1,0:T(8,128)(2,1)} %reduce-scatter.10.cloned.1.call-done) | copy-start | bytes 1179652
  187.9 77.3 %reduce-scatter.16.cloned.1.call-start = ((), (), s32[]{:S(2)}) async-start(), calls=%async_computation.15 | async-start | bytes 1179648 | tf_op jit(solution)/shard_map/reduce_scatter | solution.py:140
  189.3 32.2 %copy-start.27 = (f32[6,512]{1,0:T(8,128)S(1)}, f32[6,512]{1,0:T(8,128)}, u32[]{:S(2)}) copy-start(f32[6,512]{1,0:T(8,128)} %log_add_fusion) | copy-start | bytes 36868
  204.3 16.7 %copy-start.14 = (bf16[384,768]{0,1:T(8,128)(2,1)S(1)}, bf16[384,768]{0,1:T(8,128)(2,1)}, u32[]{:S(2)}) copy-start(bf16[384,768]{0,1:T(8,128)(2,1)} %all_gather.40) | copy-start | bytes 1769476
  204.3 17.2 %copy-start.3 = (pred[512,512]{0,1:T(8,128)(4,1)S(1)}, pred[512,512]{0,1:T(8,128)(4,1)}, u32[]{:S(2)}) copy-start(pred[512,512]{0,1:T(8,128)(4,1)} %copy-done.2) | copy-start | bytes 786436
  206.4 0.6 copy-start.34
  220.0 0.9 copy-start.9
  221.5 1.7 copy-start.40
  221.5 2.4 copy-start.12
  223.2 0.7 copy-start.19
  225.4 74.3 %reduce-scatter.12.cloned.1.call-start = ((), (), s32[]{:S(2)}) async-start(), calls=%async_computation.13 | async-start | bytes 1179648 | tf_op jit(solution)/shard_map/reduce_scatter | solution.py:87
  231.0 141.1 %reduce-scatter.18.cloned.1.call-start = ((), (), s32[]{:S(2)}) async-start(), calls=%async_computation.16 | async-start | bytes 8912896 | tf_op jit(solution)/shard_map/reduce_scatter | solution.py:154
  231.3 3.5 copy-start.4
  248.8 1.1 copy-start.10
  248.8 1.2 copy-start.18
  248.8 2.9 copy-start.8
  248.8 2.9 copy-start.20
  248.8 4.6 copy-start.21
  248.8 185.3 %reduce-scatter.22.cloned.1.call-start = ((), (), s32[]{:S(2)}) async-start(), calls=%async_computation.18 | async-start | bytes 1253376 | tf_op jit(solution)/shard_map/reduce_scatter | solution.py:156
  251.7 243.5 %reduce-scatter.20.cloned.1.call-start = ((), (), s32[]{:S(2)}) async-start(), calls=%async_computation.17 | async-start | bytes 1253376 | tf_op jit(solution)/shard_map/reduce_scatter | solution.py:155
  253.4 320.8 %reduce-scatter.26.cloned.1.call-start = ((), (), s32[]{:S(2)}) async-start(), calls=%async_computation.20 | async-start | bytes 5013504 | tf_op jit(solution)/shard_map/reduce_scatter | solution.py:158
  259.1 1.1 copy-start.6
  259.1 1.7 copy-start.16
  259.1 394.5 %reduce-scatter.24.cloned.1.call-start = ((), (), s32[]{:S(2)}) async-start(), calls=%async_computation.19 | async-start | bytes 5013504 | tf_op jit(solution)/shard_map/reduce_scatter | solution.py:157
  264.3 1.1 copy-start
  264.3 1.1 copy-start.25
  264.3 1.1 copy-start.31
  264.3 2.4 copy-start.32
  264.3 35.4 %copy-start.5 = (bf16[256,768]{1,0:T(8,128)(2,1)S(1)}, bf16[256,768]{1,0:T(8,128)(2,1)}, u32[]{:S(2)}) copy-start(bf16[256,768]{1,0:T(8,128)(2,1)} %reduce-scatter.14.cloned.1.call-done) | copy-start | bytes 1179652
  264.3 35.4 %copy-start.23 = (f32[768]{0:T(1024)S(1)}, f32[768]{0:T(1024)}, u32[]{:S(2)}) copy-start(f32[768]{0:T(1024)} %copy-done.22) | copy-start | bytes 9220
  264.3 35.4 %copy-start.29 = (f32[256]{0:T(256)S(1)}, f32[256]{0:T(256)}, u32[]{:S(2)}) copy-start(f32[256]{0:T(256)} %copy-done.28) | copy-start | bytes 3076
  264.3 35.4 %copy-start.33 = (f32[256]{0:T(256)S(1)}, f32[256]{0:T(256)}, u32[]{:S(2)}) copy-start(f32[256]{0:T(256)} %get-tuple-element.83) | copy-start | bytes 3076
  264.4 35.4 %copy-start.35 = (f32[256]{0:T(256)S(1)}, f32[256]{0:T(256)}, u32[]{:S(2)}) copy-start(f32[256]{0:T(256)} %copy-done.34) | copy-start | bytes 3076
  264.4 35.4 %copy-start.37 = (f32[256]{0:T(256)S(1)}, f32[256]{0:T(256)}, u32[]{:S(2)}) copy-start(f32[256]{0:T(256)} %get-tuple-element.81) | copy-start | bytes 3076
Sparse Core Ops, SparseCore 0:
  10.8 47.9 all-gather.3
  61.1 44.2 all-gather.7
  117.6 13.9 reduce-scatter.9
  134.5 42.3 all-gather.5
  188.0 16.2 reduce-scatter.13
  225.6 17.4 reduce-scatter.15
  245.9 17.4 reduce-scatter.11
  267.5 104.5 reduce-scatter.17
  376.3 57.7 reduce-scatter.21
  438.1 56.9 reduce-scatter.19
  499.6 74.5 reduce-scatter.25
  579.0 74.5 reduce-scatter.23
where the time goes:
time: 663 us; the launch traced here: 662 us
  waiting for transfers between devices  380 us (57%)
  blocking collectives  167 us (25%)
  matrix products  44.7 us (7%)
  other arithmetic  28.8 us (4%)
  local copies, waits for them, and re-layouts  25.8 us (4%)
  between operations  16 us (2%)
    reduce_scatter x1, waiting for transfers between devices, shards(): lax.psum_scatter(grad_up, 'dp', scatter_dimension=0, tiled=True)  79.4 us
    reduce_scatter x1, waiting for transfers between devices, shards(): lax.psum_scatter(grad_down, 'dp', scatter_dimension=1, tiled=True)  79.1 us
    unnamed x2, blocking collectives  68.2 us
    reduce_scatter x1, waiting for transfers between devices, shards(): lax.psum_scatter(grad_value, 'dp', scatter_dimension=0, tiled=True)  61.1 us
    reduce_scatter x1, waiting for transfers between devices, shards(): lax.psum_scatter(grad_output, 'dp', scatter_dimension=1, tiled=True)  60 us
    reduce_scatter x1, waiting for transfers between devices, shards(): lax.psum_scatter(grad_scores, 'dp', scatter_dimension=1, tiled=True)  47.5 us
    all_gather x1, waiting for transfers between devices, shards(): lax.all_gather(w_up.astype(jnp.bfloat16), 'dp', axis=0, tiled=True)  30.3 us
    all_gather x1, blocking collectives, shards(): lax.all_gather(w_output.astype(jnp.bfloat16), 'dp', axis=1, tiled=True)  23.7 us
  transfers between devices with their start and end apart: 12, of which 8 were waited for; matrix products, arithmetic and copies ran while one was open for 11% of the time, Pallas kernels for 0%

commit v1 on v0

v1 whole, which is shorter than its diff:
```python
import jax
import jax.numpy as jnp
from jax import lax
from jax.experimental import pallas as pl
from jax.experimental.pallas import tpu as pltpu
from jax.sharding import PartitionSpec as P

EPSILON = 1e-06
NEGATIVE = -1e30
BF = jnp.bfloat16
F32 = jnp.float32
UNITS = 16
LANES = 128
RING_CHIPS = 8
VMEM_BYTES = 56 * 1024 * 1024
NT = (((1,), (1,)), ((), ()))
TN = (((0,), (0,)), ((), ()))
NN = (((1,), (0,)), ((), ()))


def mm(a, b, dims=NN):
    return lax.dot_general(a, b, dims, preferred_element_type=F32)


def params():
    return pltpu.CompilerParams(vmem_limit_bytes=VMEM_BYTES)


def vmem(count):
    return [pl.BlockSpec(memory_space=pltpu.VMEM)] * count


def smem():
    return pl.BlockSpec(memory_space=pltpu.SMEM)


def hbm(count):
    return [pl.BlockSpec(memory_space=pl.ANY)] * count


def sds(shape, dtype):
    return jax.ShapeDtypeStruct(shape, dtype)


def gelu_pair(x):
    c = 0.7978845608028654
    a = 0.044715
    square = x * x
    t = jnp.tanh(c * x * (1.0 + a * square))
    half = 0.5 * (1.0 + t)
    return x * half, half + 0.5 * x * (1.0 - t * t) * (c * (1.0 + 3.0 * a * square))


def multiple(value, of):
    return pl.multiple_of(value, of)


def pack_first(scores, wv, gain_one, gain_two):
    heads, rows, length = scores.shape
    krows, width = wv.shape

    def kernel(s_ref, wv_ref, ga_ref, gf_ref, out, scr):
        out[: heads * rows, :] = s_ref[...].reshape(heads * rows, length).astype(BF)
        out[heads * rows :, :width] = wv_ref[...].astype(BF)
        scr[...] = jnp.zeros_like(scr)
        scr[0:1, :krows] = ga_ref[...]
        scr[1:2, :krows] = gf_ref[...]
        out[heads * rows :, width:] = scr[...].astype(BF)

    return pl.pallas_call(
        kernel,
        out_shape=sds((heads * rows + krows, length), BF),
        in_specs=vmem(4),
        out_specs=vmem(1)[0],
        scratch_shapes=[pltpu.VMEM((krows, length - width), F32)],
        compiler_params=params(),
        name="pack_first",
    )(scores, wv, gain_one.reshape(1, -1), gain_two.reshape(1, -1))


def pack_second(w_up, w_down, wo_first, wo_second):
    krows, hidden = w_up.shape
    half = wo_first.shape[0]

    def kernel(up_ref, down_ref, one_ref, two_ref, out):
        eye = (
            lax.broadcasted_iota(jnp.int32, (krows, krows), 0)
            == lax.broadcasted_iota(jnp.int32, (krows, krows), 1)
        ).astype(BF)
        out[:, :hidden] = up_ref[...].astype(BF)
        out[:, hidden : 2 * hidden] = mm(eye, down_ref[...].astype(BF), NT).astype(BF)
        out[:, 2 * hidden : 2 * hidden + half] = mm(eye, one_ref[...], NT).astype(BF)
        out[:, 2 * hidden + half :] = mm(eye, two_ref[...], NT).astype(BF)

    return pl.pallas_call(
        kernel,
        out_shape=sds((krows, 2 * hidden + 2 * half), BF),
        in_specs=vmem(4),
        out_specs=vmem(1)[0],
        compiler_params=params(),
        name="pack_second",
    )(w_up, w_down, wo_first, wo_second)


def mixer_forward(where, tokens, seg_row, seg_col, units, heads, width):
    length, model = tokens.shape
    size = width // heads
    rows = length // UNITS
    krows = model // UNITS
    wide = heads * LANES

    def kernel(where_ref, tok_ref, sr_ref, sc_ref, *rest):
        unit = rest[:UNITS]
        e_ref, va_ref, mixed_ref, mixf_ref, rb_ref, n1_ref, gains_ref, wv_ref, pieces = rest[UNITS:]
        for u in range(UNITS):
            d = where_ref[u]
            wv_ref[pl.ds(multiple(d * krows, 16), krows), :] = unit[u][heads * rows :, :width]
            some = unit[u][heads * rows : heads * rows + 16, width:].astype(F32)
            pieces[0, pl.ds(d, 1), :] = some[0:1, :]
            pieces[1, pl.ds(d, 1), :] = some[1:2, :]
        spread = (
            lax.broadcasted_iota(jnp.int32, (LANES, model), 1) % krows
            == lax.broadcasted_iota(jnp.int32, (LANES, model), 0)
        ).astype(BF)
        own = (
            lax.broadcasted_iota(jnp.int32, (UNITS, model), 1) // krows
            == lax.broadcasted_iota(jnp.int32, (UNITS, model), 0)
        )
        gains = []
        for t in range(2):
            full = jnp.where(own, mm(pieces[t].astype(BF), spread), 0.0)
            gains.append(jnp.sum(full, axis=0, keepdims=True))
            gains_ref[t : t + 1, :] = gains[t]
        x = tok_ref[...].astype(F32)
        inv = lax.rsqrt(jnp.mean(x * x, axis=-1, keepdims=True) + EPSILON)
        n1_ref[...] = (x * inv * gains[0]).astype(BF)
        values = mm(n1_ref[...], wv_ref[...]).astype(BF)
        tail = (lax.broadcasted_iota(jnp.int32, (length, LANES - size), 1) < 2).astype(BF)
        for h in range(heads):
            va_ref[:, h * LANES : h * LANES + size] = values[:, h * size : (h + 1) * size]
            va_ref[:, h * LANES + size : (h + 1) * LANES] = tail

        def one_head(h, carry):
            for u in range(UNITS):
                d = where_ref[u]
                at = pl.ds(multiple(d * rows, rows), rows)
                s = unit[u][pl.ds(multiple(h * rows, rows), rows), :].astype(F32)
                same = sc_ref[at, :] == sr_ref[...]
                e_ref[h, at, :] = jnp.where(same, jnp.exp(s), 0.0).astype(BF)
            return carry

        lax.fori_loop(0, heads, one_head, 0)
        for h in range(heads):
            lanes = slice(h * LANES, (h + 1) * LANES)
            sums = mm(e_ref[h], va_ref[:, lanes])
            inverse = 1.0 / sums[:, size : size + 1]
            mixed = sums * inverse
            rb_ref[:, lanes] = jnp.broadcast_to(inverse, (length, LANES))
            mixf_ref[:, lanes] = jnp.where(
                lax.broadcasted_iota(jnp.int32, (length, LANES), 1) < size, mixed, 0.0
            )
            mixed_ref[:, h * size : (h + 1) * size] = mixed[:, :size].astype(BF)

    return pl.pallas_call(
        kernel,
        out_shape=(
            sds((heads, length, length), BF),
            sds((length, wide), BF),
            sds((length, width), BF),
            sds((length, wide), F32),
            sds((length, wide), F32),
            sds((length, model), BF),
            sds((2, model), F32),
            sds((model, width), BF),
        ),
        in_specs=[smem()] + vmem(3 + UNITS),
        out_specs=tuple(vmem(8)),
        scratch_shapes=[pltpu.VMEM((2, UNITS, LANES), F32)],
        compiler_params=params(),
        name="mixer_forward",
    )(where, tokens, seg_row, seg_col, *units)


def ffn_main(place, tokens, mixed_own, mixed_other, cotangent, gains, units, heads):
    length, model = tokens.shape
    width = mixed_own.shape[1]
    krows = model // UNITS
    columns = units[0].shape[1]
    hidden = (columns - 2 * width) // 2
    size = width // heads
    wide = heads * LANES
    chunk = length // 2
    piece = hidden // 3

    def kernel(place_ref, tok_ref, own_ref, other_ref, cot_ref, gains_ref, *rest):
        unit = rest[:UNITS]
        (back_ref, resid_ref, n2_ref, act_ref, gpre_ref, wo_out, w, mixed, acc, sem) = rest[UNITS:]
        copies = []
        for u in range(UNITS):
            to = pl.ds(multiple(place_ref[u] * krows, 16), krows)
            copies.append(pltpu.make_async_copy(unit[u], w.at[to, :], sem.at[u]))
            copies[-1].start()
        first = place_ref[UNITS]
        mixed[:, pl.ds(multiple(first * width, LANES), width)] = own_ref[...]
        mixed[:, pl.ds(multiple((1 - first) * width, LANES), width)] = other_ref[...]
        for copy in copies:
            copy.wait()
        start = multiple(2 * hidden + first * width, LANES)
        wo_own = w[:, pl.ds(start, width)]
        zeros = jnp.zeros((model, LANES - size), BF)
        for h in range(heads):
            wo_out[:, h * LANES : h * LANES + size] = wo_own[:, h * size : (h + 1) * size]
            wo_out[:, h * LANES + size : (h + 1) * LANES] = zeros

        def some_tokens(r, carry):
            at = pl.ds(multiple(r * chunk, chunk), chunk)
            attn = mm(mixed[at, :], w[:, 2 * hidden :], NT)
            resid = tok_ref[at, :].astype(F32) + attn
            resid_ref[at, :] = resid
            inv = lax.rsqrt(jnp.mean(resid * resid, axis=-1, keepdims=True) + EPSILON)
            n2_ref[at, :] = (resid * inv * gains_ref[1:2, :]).astype(BF)
            for j in range(hidden // piece):
                cols = slice(j * piece, (j + 1) * piece)
                down = slice(hidden + j * piece, hidden + (j + 1) * piece)
                pre = mm(n2_ref[at, :], w[:, cols])
                act, slope = gelu_pair(pre)
                act_ref[at, cols] = act.astype(BF)
                gpre_ref[at, cols] = (mm(cot_ref[at, :], w[:, down]) * slope).astype(BF)
                part = mm(gpre_ref[at, cols], w[:, cols], NT)
                if j == 0:
                    acc[...] = part
                else:
                    acc[...] += part
            back_ref[at, :] = acc[...].astype(BF)
            return carry

        lax.fori_loop(0, length // chunk, some_tokens, 0)

    return pl.pallas_call(
        kernel,
        out_shape=(
            sds((length, model), BF),
            sds((length, model), F32),
            sds((length, model), BF),
            sds((length, hidden), BF),
            sds((length, hidden), BF),
            sds((model, wide), BF),
        ),
        in_specs=[smem()] + vmem(5) + hbm(UNITS),
        out_specs=tuple(vmem(6)),
        scratch_shapes=[
            pltpu.VMEM((model, columns), BF),
            pltpu.VMEM((length, 2 * width), BF),
            pltpu.VMEM((chunk, model), F32),
            pltpu.SemaphoreType.DMA((UNITS,)),
        ],
        compiler_params=params(),
        name="ffn_main",
    )(place, tokens, mixed_own, mixed_other, cotangent, gains, *units)


def ffn_grads(where, n2, gpre, act, cotangent):
    length, model = n2.shape
    hidden = act.shape[1]
    krows = model // UNITS
    half = UNITS // 2

    def kernel(where_ref, n2_ref, gpre_ref, act_ref, cot_ref, keep, give, scr, sem):
        piece = hidden // 3
        for j in range(3):
            cols = slice(j * piece, (j + 1) * piece)
            scr[:, cols] = mm(n2_ref[...], gpre_ref[:, cols], TN).astype(BF)
            down = slice(hidden + j * piece, hidden + (j + 1) * piece)
            scr[:, down] = mm(cot_ref[...], act_ref[:, cols], TN).astype(BF)
        copies = []
        for u in range(UNITS):
            at = pl.ds(multiple(where_ref[u] * krows, 16), krows)
            to = keep.at[u] if u < half else give.at[u - half]
            copies.append(pltpu.make_async_copy(scr.at[at, :], to, sem.at[u]))
            copies[-1].start()
        for copy in copies:
            copy.wait()

    shape = sds((half, krows, 2 * hidden), BF)
    return pl.pallas_call(
        kernel,
        out_shape=(shape, shape),
        in_specs=[smem()] + vmem(4),
        out_specs=tuple(hbm(2)),
        scratch_shapes=[pltpu.VMEM((model, 2 * hidden), BF), pltpu.SemaphoreType.DMA((UNITS,))],
        compiler_params=params(),
        name="ffn_grads",
    )(where, n2, gpre, act, cotangent)


def ffn_out(where, act, units, width):
    length, hidden = act.shape
    krows, columns = units[0].shape
    model = krows * UNITS

    def kernel(where_ref, act_ref, *rest):
        unit = rest[:UNITS]
        out, w, sem = rest[UNITS:]
        copies = []
        for u in range(UNITS):
            to = pl.ds(multiple(where_ref[u] * krows, 16), krows)
            source = unit[u].at[:, pl.ds(hidden, hidden)]
            copies.append(pltpu.make_async_copy(source, w.at[to, :], sem.at[u]))
            copies[-1].start()
        for copy in copies:
            copy.wait()
        chunk = length // 2
        for r in range(2):
            at = slice(r * chunk, (r + 1) * chunk)
            out[at, :] = mm(act_ref[at, :], w[...], NT).astype(BF)

    return pl.pallas_call(
        kernel,
        out_shape=sds((length, model), BF),
        in_specs=[smem()] + vmem(1) + hbm(UNITS),
        out_specs=vmem(1)[0],
        scratch_shapes=[pltpu.VMEM((model, hidden), BF), pltpu.SemaphoreType.DMA((UNITS,))],
        compiler_params=params(),
        name="ffn_out",
    )(where, act, *units)


def mixer_back(back_own, back_other, resid, cotangent, gains, wo, mixf, rb, e, n1, wv, tokens):
    length, model = resid.shape
    width = wv.shape[1]
    heads = e.shape[0]
    size = width // heads
    wide = heads * LANES
    chunk = length // 4
    krows = model // UNITS

    def kernel(a_ref, b_ref, res_ref, cot_ref, gains_ref, wo_ref, mixf_ref, rb_ref, e_ref, wv_ref, tok_ref,
               gres_ref, gat_ref, xh_ref, gv_ref, part_ref, ga_ref, gf_ref, gm, acc):
        acc[...] = jnp.zeros_like(acc)

        def some_tokens(r, carry):
            at = pl.ds(multiple(r * chunk, chunk), chunk)
            g2 = a_ref[at, :].astype(F32) + b_ref[at, :].astype(F32)
            res = res_ref[at, :]
            inv = lax.rsqrt(jnp.mean(res * res, axis=-1, keepdims=True) + EPSILON)
            hat = res * inv
            acc[0] += jnp.sum((g2 * hat).reshape(chunk // 8, 8, model), axis=0)
            z = gains_ref[1:2, :] * g2
            corr = jnp.mean(z * hat, axis=-1, keepdims=True)
            gres = cot_ref[at, :].astype(F32) + inv * (z - hat * corr)
            gres_ref[at, :] = gres
            gat_ref[at, :] = gres.astype(BF)
            return carry

        lax.fori_loop(0, length // chunk, some_tokens, 0)
        gm[...] = mm(gat_ref[...], wo_ref[...]).astype(BF)
        lane = lax.broadcasted_iota(jnp.int32, (length, LANES), 1)
        for h in range(heads):
            lanes = slice(h * LANES, (h + 1) * LANES)
            here = gm[:, lanes].astype(F32)
            inner = -jnp.sum(here * mixf_ref[:, lanes], axis=-1, keepdims=True)
            high = inner.astype(BF).astype(F32)
            xh_ref[:, lanes] = jnp.where(
                lane == size, high, jnp.where(lane == size + 1, inner - high, here)
            ).astype(BF)
            scaled = (here * rb_ref[:, lanes]).astype(BF)
            gv_ref[:, h * size : (h + 1) * size] = mm(e_ref[h], scaled, TN)[:, :size].astype(BF)

        def some_back(r, carry):
            at = pl.ds(multiple(r * chunk, chunk), chunk)
            part = mm(gv_ref[at, :], wv_ref[...], NT)
            part_ref[at, :] = part.astype(BF)
            x = tok_ref[at, :].astype(F32)
            inv = lax.rsqrt(jnp.mean(x * x, axis=-1, keepdims=True) + EPSILON)
            acc[1] += jnp.sum((part * (x * inv)).reshape(chunk // 8, 8, model), axis=0)
            return carry

        lax.fori_loop(0, length // chunk, some_back, 0)
        take = (
            lax.broadcasted_iota(jnp.int32, (model, LANES), 0) % krows
            == lax.broadcasted_iota(jnp.int32, (model, LANES), 1)
        ).astype(BF)
        own = (
            lax.broadcasted_iota(jnp.int32, (UNITS, model), 1) // krows
            == lax.broadcasted_iota(jnp.int32, (UNITS, model), 0)
        )
        for t, to in ((0, gf_ref), (1, ga_ref)):
            row = jnp.sum(acc[t], axis=0, keepdims=True)
            high = row.astype(BF).astype(F32)
            pieces = mm(jnp.where(own, high, 0.0).astype(BF), take)
            to[...] = pieces + mm(jnp.where(own, row - high, 0.0).astype(BF), take)

    return pl.pallas_call(
        kernel,
        out_shape=(
            sds((length, model), F32),
            sds((length, model), BF),
            sds((length, wide), BF),
            sds((length, width), BF),
            sds((length, model), BF),
            sds((UNITS, LANES), F32),
            sds((UNITS, LANES), F32),
        ),
        in_specs=vmem(11),
        out_specs=tuple(vmem(7)),
        scratch_shapes=[pltpu.VMEM((length, wide), BF), pltpu.VMEM((2, 8, model), F32)],
        compiler_params=params(),
        name="mixer_back",
    )(back_own, back_other, resid, cotangent, gains, wo, mixf, rb, e, wv, tokens)


def mixer_grads(where, xh, va, e, rb, n1, gv, gat, mixed, ga, ga_other, gf):
    length, model = n1.shape
    heads = e.shape[0]
    width = gv.shape[1]
    rows = length // UNITS
    krows = model // UNITS
    half = UNITS // 2
    deep = heads * rows + 2 * krows

    def kernel(where_ref, xh_ref, va_ref, e_ref, rb_ref, n1_ref, gv_ref, gat_ref, mixed_ref, ga_ref, gb_ref, gf_ref,
               keep, give, ds, wide_v, wide_o, pieces):
        def slot(u):
            return (keep, u) if u < half else (give, u - half)

        def one_head(h, carry):
            lanes = pl.ds(multiple(h * LANES, LANES), LANES)
            d = mm(xh_ref[:, lanes], va_ref[:, lanes], NT)
            for q in range(length // LANES):
                cols = slice(q * LANES, (q + 1) * LANES)
                ds[:, cols] = (e_ref[h, :, cols].astype(F32) * rb_ref[:, lanes] * d[:, cols]).astype(BF)
            for u in range(UNITS):
                ref, k = slot(u)
                at = pl.ds(multiple(where_ref[u] * rows, rows), rows)
                ref[k, pl.ds(multiple(h * rows, rows), rows), :] = ds[at, :]
            return carry

        lax.fori_loop(0, heads, one_head, 0)
        wide_v[...] = mm(n1_ref[...], gv_ref[...], TN).astype(BF)
        wide_o[...] = mm(gat_ref[...], mixed_ref[...], TN).astype(BF)
        pieces[0] = ga_ref[...] + gb_ref[...]
        pieces[1] = gf_ref[...]
        sub = lax.broadcasted_iota(jnp.int32, (krows, LANES), 0)
        top = heads * rows
        for u in range(UNITS):
            ref, k = slot(u)
            d = where_ref[u]
            at = pl.ds(multiple(d * krows, 16), krows)
            ref[k, top : top + krows, :width] = wide_v[at, :]
            ref[k, top + krows :, :width] = wide_o[at, :]
            both = jnp.where(
                sub == 0, pieces[0, pl.ds(d, 1), :], jnp.where(sub == 1, pieces[1, pl.ds(d, 1), :], 0.0)
            )
            ref[k, top : top + krows, width:] = both.astype(BF)
            ref[k, top + krows :, width:] = jnp.zeros((krows, length - width), BF)

    shape = sds((half, deep, length), BF)
    return pl.pallas_call(
        kernel,
        out_shape=(shape, shape),
        in_specs=[smem()] + vmem(11),
        out_specs=tuple(vmem(2)),
        scratch_shapes=[
            pltpu.VMEM((length, length), BF),
            pltpu.VMEM((model, width), BF),
            pltpu.VMEM((model, width), BF),
            pltpu.VMEM((2, UNITS, LANES), F32),
        ],
        compiler_params=params(),
        name="mixer_grads",
    )(where, xh, va, e, rb, n1, gv, gat, mixed, ga, ga_other, gf)


class Ring:
    def __init__(self, size):
        self.size = size
        self.chips = size // 2
        n = self.chips
        self.order = list(range(0, n, 2)) + list(range(n - 1, 0, -2))
        me = lax.axis_index("dp")
        self.core = me % 2
        chip = me // 2
        self.at = jnp.where(chip % 2 == 0, chip // 2, n - 1 - chip // 2)
        self.up = self.pairs(1)
        self.down = self.pairs(-1)
        self.swap = [(d, d ^ 1) for d in range(size)]

    def pairs(self, step):
        n = self.chips
        return [
            (self.order[p] * 2 + c, self.order[(p + step) % n] * 2 + c) for p in range(n) for c in range(2)
        ]

    def device(self, offset, core):
        n = self.chips
        p = (self.at + jnp.asarray(offset, jnp.int32) + n) % n
        chip = jnp.where(p < (n + 1) // 2, 2 * p, 2 * (n - 1 - p) + 1)
        return chip * 2 + core

    def gather(self, unit):
        n = self.chips
        ups, downs = [unit], [unit]
        for step in range(n // 2):
            ups.append(lax.ppermute(ups[-1], "dp", self.up))
            if step < n // 2 - 1:
                downs.append(lax.ppermute(downs[-1], "dp", self.down))
        mine = ups + downs[1:]
        theirs = [lax.ppermute(one, "dp", self.swap) for one in mine]
        return mine + theirs

    def gathered(self):
        n = self.chips
        offsets = [-s for s in range(n // 2 + 1)] + [s for s in range(1, n // 2)]
        return jnp.concatenate([self.device(offsets, self.core), self.device(offsets, 1 - self.core)])

    def scattered(self):
        offsets = list(range(self.chips))
        return jnp.concatenate([self.device(offsets, self.core), self.device(offsets, 1 - self.core)])

    def scatter(self, keep, give):
        n = self.chips
        got = lax.ppermute(give, "dp", self.swap)

        def add(k, *more):
            total = keep[k].astype(F32) + got[k].astype(F32)
            for one in more:
                total = total + one.astype(F32)
            return total

        far = n // 2
        up = lax.ppermute(add(far).astype(BF), "dp", self.up)
        down = lax.ppermute(add(far + 1).astype(BF), "dp", self.down)
        for step in range(1, far):
            up = lax.ppermute(add(far - step, up).astype(BF), "dp", self.up)
            if step < far - 1:
                down = lax.ppermute(add(far + 1 + step, down).astype(BF), "dp", self.down)
        return add(0, up, down)


def shards(
    tokens,
    segment_ids,
    gain_attn,
    gain_ffn,
    random_scores,
    w_value,
    w_output,
    w_up,
    w_down,
    cotangent,
):
    devices = lax.axis_size("dp")
    second = lax.axis_index("mp")
    length = segment_ids.shape[1]
    heads = random_scores.shape[0]
    model = tokens.shape[1]
    width = w_value.shape[1]
    rows = length // UNITS
    krows = model // UNITS
    ring = devices == UNITS and devices // 2 <= RING_CHIPS
    flip = [(0, 1), (1, 0)]

    wo_own = w_output.astype(BF)
    wo_other = lax.ppermute(wo_own, "mp", flip)
    wo_first = jnp.where(second == 0, wo_own, wo_other)
    wo_second = jnp.where(second == 0, wo_other, wo_own)
    if ring:
        net = Ring(devices)
        where_in = net.gathered().astype(jnp.int32)
        where_out = net.scattered().astype(jnp.int32)
        units_one = net.gather(pack_first(random_scores, w_value, gain_attn, gain_ffn))
        units_two = net.gather(pack_second(w_up, w_down, wo_first, wo_second))
    else:
        where_in = jnp.arange(UNITS, dtype=jnp.int32)
        where_out = where_in

        def gather(one, axis=0):
            return lax.all_gather(one.astype(BF), "dp", axis=axis, tiled=True)

        scores = gather(random_scores, 1).reshape(heads, UNITS, rows, length).transpose(1, 0, 2, 3)
        value = gather(w_value).reshape(UNITS, krows, width)
        gains = jnp.stack([gather(gain_attn), gather(gain_ffn)]).reshape(2, UNITS, krows).transpose(1, 0, 2)
        gains = jnp.pad(gains, ((0, 0), (0, krows - 2), (0, length - width - krows)))
        low = jnp.concatenate([value, gains], axis=2)
        both = jnp.concatenate([scores.reshape(UNITS, heads * rows, length), low], axis=1)
        units_one = [both[u] for u in range(UNITS)]
        packed = jnp.concatenate([gather(w_up), gather(w_down.T), gather(wo_first.T), gather(wo_second.T)], axis=1)
        packed = packed.reshape(UNITS, krows, packed.shape[1])
        units_two = [packed[u] for u in range(UNITS)]
    place = jnp.concatenate([where_in, jnp.reshape(second, (1,)).astype(jnp.int32)])

    e, va, mixed, mixf, rb, n1, gains, wv = mixer_forward(
        where_in, tokens, segment_ids, segment_ids.reshape(length, 1), units_one, heads, width
    )
    mixed_other = lax.ppermute(mixed, "mp", flip)
    back, resid, n2, act, gpre, wo = ffn_main(
        place, tokens, mixed, mixed_other, cotangent, gains, units_two, heads
    )
    back_other = lax.ppermute(back, "mp", flip)
    keep_two, give_two = ffn_grads(where_out, n2, gpre, act, cotangent)
    ffn = ffn_out(where_in, act, units_two, width)
    ffn_other = lax.ppermute(ffn, "mp", flip)
    gres, gat, xh, gv, part, ga, gf = mixer_back(
        back, back_other, resid, cotangent, gains, wo, mixf, rb, e, n1, wv, tokens
    )
    ga_other = lax.ppermute(ga, "mp", flip)
    part_other = lax.ppermute(part, "mp", flip)
    keep_one, give_one = mixer_grads(where_out, xh, va, e, rb, n1, gv, gat, mixed, ga, ga_other, gf)

    output = (resid + (ffn.astype(F32) + ffn_other.astype(F32))).astype(BF)
    grad_n1 = part.astype(F32) + part_other.astype(F32)
    x = tokens.astype(F32)
    inv = lax.rsqrt(jnp.mean(x * x, axis=-1, keepdims=True) + EPSILON)
    z = gains[0:1, :] * grad_n1
    hat = x * inv
    grad_tokens = (gres + inv * (z - hat * jnp.mean(z * hat, axis=-1, keepdims=True))).astype(BF)

    top = heads * rows
    if ring:
        two = net.scatter(keep_two, give_two)
        one = net.scatter(keep_one, give_one)
        out_up = two[:, : two.shape[1] // 2]
        out_down = two[:, two.shape[1] // 2 :].T
        out_scores = one[:top].reshape(heads, rows, length)
        out_value = one[top : top + krows, :width]
        out_output = one[top + krows :, :width].T
        out_gain_one = one[top, width : width + krows]
        out_gain_two = one[top + 1, width : width + krows]
    else:

        def scatter(one, axis=0):
            return lax.psum_scatter(one, "dp", scatter_dimension=axis, tiled=True)

        two = jnp.concatenate([keep_two, give_two]).astype(F32).reshape(model, -1)
        one = jnp.concatenate([keep_one, give_one]).astype(F32)
        out_up = scatter(two[:, : two.shape[1] // 2])
        out_down = scatter(two[:, two.shape[1] // 2 :]).T
        scores = one[:, :top].reshape(UNITS, heads, rows, length).transpose(1, 0, 2, 3)
        out_scores = scatter(scores.reshape(heads, length, length), 1)
        out_value = scatter(one[:, top : top + krows, :width].reshape(model, width))
        out_output = scatter(one[:, top + krows :, :width].reshape(model, width)).T
        out_gain_one = scatter(one[:, top, width : width + krows].reshape(model))
        out_gain_two = scatter(one[:, top + 1, width : width + krows].reshape(model))
    return (
        output,
        grad_tokens,
        out_gain_one,
        out_gain_two,
        out_scores,
        out_value,
        out_output,
        out_up,
        out_down,
    )


def solution(mesh):
    in_specs = (
        P("dp", None),
        P("dp", None),
        P("dp"),
        P("dp"),
        P("mp", "dp", None),
        P("dp", "mp"),
        P("mp", "dp"),
        P("dp", "mp"),
        P("mp", "dp"),
        P("dp", None),
    )
    out_specs = (
        P("dp", None),
        P("dp", None),
        P("dp"),
        P("dp"),
        P("mp", "dp", None),
        P("dp", "mp"),
        P("mp", "dp"),
        P("dp", "mp"),
        P("mp", "dp"),
    )
    return jax.shard_map(shards, mesh=mesh, in_specs=in_specs, out_specs=out_specs, check_vma=False)
```

time: 663 us -> 243 us (0.37)
  waiting for transfers between devices: 380 us -> 117 us
  blocking collectives: 167 us -> 0 us
  Pallas kernels: 0 us -> 58.8 us
  matrix products: 44.7 us -> 0 us
  starting transfers between devices: 0.72 us -> 41 us
  local copies, waits for them, and re-layouts: 25.8 us -> 9.43 us
  between operations: 16 us -> 1.11 us
  other arithmetic: 28.8 us -> 15.3 us
    reduce_scatter x9 -> x0, waiting for transfers between devices: 349 us -> none  [the longest x1 79.4 us: shards(): lax.psum_scatter(grad_up, 'dp', scatter_dimension=0, tiled=True)]
    ppermute x0 -> x52, waiting for transfers between devices: none -> 117 us  [the longest x8 27 us: gather(): ups.append(lax.ppermute(ups[-1], 'dp', self.up))]
    all_gather x7 -> x0, blocking collectives: 93 us -> none  [the longest x1 23.7 us: shards(): lax.all_gather(w_output.astype(jnp.bfloat16), 'dp', axis=1, tiled=True)]
    unnamed x2 -> x0, blocking collectives: 68.2 us -> none
    pallas_call x0 -> x8, Pallas kernels: none -> 58.8 us  [the longest x1 13.3 us: ffn_main(): pl.pallas_call(kernel, out_shape=(sds((length, model), BF), sds((length,...]
    dot_general x15 -> x0, matrix products: 44.7 us -> none  [the longest x1 7.54 us: shards(): pre_act = jnp.dot(normed_two, up_proj, preferred_element_type=jnp.float32)]
    ppermute x0 -> x52, starting transfers between devices: none -> 41 us  [the longest x8 11.8 us: gather(): ups.append(lax.ppermute(ups[-1], 'dp', self.up))]
    all_gather x3 -> x0, waiting for transfers between devices: 30.3 us -> none  [the longest x1 30.3 us: shards(): lax.all_gather(w_up.astype(jnp.bfloat16), 'dp', axis=0, tiled=True)]
  transfers between devices with their start and end apart: 12 -> 52, of which waited for: 8 -> 20; matrix products, arithmetic and copies ran while one was open for 11% -> 7% of each run, Pallas kernels for 0% -> 16%
where the time goes in v1:
time: 243 us
  waiting for transfers between devices  117 us (48%)
  Pallas kernels  58.8 us (24%)
  starting transfers between devices  41 us (17%)
  other arithmetic  15.3 us (6%)
  local copies, waits for them, and re-layouts  9.43 us (4%)
    ppermute x8, waiting for transfers between devices, gather(): ups.append(lax.ppermute(ups[-1], 'dp', self.up))  27 us
    ppermute x1, waiting for transfers between devices, shards(): back_other = lax.ppermute(back, 'mp', flip)  19.5 us
    ppermute x1, waiting for transfers between devices, shards(): ffn_other = lax.ppermute(ffn, 'mp', flip)  15.6 us
    pallas_call x1, Pallas kernels, ffn_main(): pl.pallas_call(kernel, out_shape=(sds((length, model), BF), sds((length,...  13.3 us
    ppermute x1, waiting for transfers between devices, shards(): part_other = lax.ppermute(part, 'mp', flip)  12.8 us
    ppermute x6, waiting for transfers between devices, scatter(): up = lax.ppermute(add(far - step, up).astype(BF), 'dp', self.up)  12.1 us
    ppermute x8, starting transfers between devices, gather(): ups.append(lax.ppermute(ups[-1], 'dp', self.up))  11.8 us
    pallas_call x1, Pallas kernels, mixer_back(): pl.pallas_call(kernel, out_shape=(sds((length, model), F32), sds((length,...  10.9 us
  transfers between devices with their start and end apart: 52, of which 20 were waited for; matrix products, arithmetic and copies ran while one was open for 7% of the time, Pallas kernels for 16%

profile of v1, /device:TPU:0, one launch (start us, length us, event | category | flops | bytes accessed | tf_op | source)
XLA Modules:
  0.0 242.7 jit_solution(4398434477703425138)
XLA Ops:
  0.6 1.0 copy.26
  1.6 3.0 %collective-permute-start.16 = (bf16[384,48]{1,0:T(8,128)(2,1)S(1)}, bf16[384,48]{1,0:T(8,128)(2,1)S(1)}, u32[]{:S(2)}, u32[]{:S(2)}) collective-permute-start(bf16[384,48]{1,0:T(8,128)(2,1)S(1)} %copy.26), channel_id=1, source_target_pairs={{0,1},{1,0},{2,3},{3,2},{4,5},{5,4},{6,7},{7,6},{8,9},{9,8},{10,11... | collective-permute-start | bytes 110600 | tf_op jit(solution)/shard_map/ppermute | solution.py:564
  4.7 1.8 pack_first.1.rest_0_
  6.4 1.6 collective-permute-start
  8.5 2.1 copy.27.down_ref
  10.6 0.7 broadcast_select_fusion
  11.3 2.3 pack_second.1.rest_0_
  13.7 1.6 collective-permute-start.17
  15.7 1.6 collective-permute-start.1
  17.8 7.5 %collective-permute-done.17.rest_1_ = bf16[48,3840]{1,0:T(8,128)(2,1)S(1)} collective-permute-done((bf16[48,3840]{1,0:T(8,128)(2,1)}, bf16[48,3840]{1,0:T(8,128)(2,1)S(1)}, u32[]{:S(2)}, u32[]{:S(2)}) %collective-permute-start.17) | collective-permute-done | bytes 368672 | tf_op jit(solution)/shard_map/ppermute | solution.py:504
  25.3 1.6 collective-permute-done.21.rest_5_
  26.9 1.6 collective-permute-start.18
  28.5 1.6 collective-permute-done.1.rest_2_
  30.2 1.6 collective-permute-start.2
  32.7 10.6 %collective-permute-done.2.rest_3_ = bf16[240,512]{1,0:T(8,128)(2,1)S(1)} collective-permute-done((bf16[240,512]{1,0:T(8,128)(2,1)S(1)}, bf16[240,512]{1,0:T(8,128)(2,1)S(1)}, u32[]{:S(2)}, u32[]{:S(2)}) %collective-permute-start.2) | collective-permute-done | bytes 245792 | tf_op jit(solution)/shard_map/ppermute | solution.py:504
  43.3 1.6 collective-permute-start.3
  45.4 1.6 collective-permute-start.19
  47.7 4.6 %collective-permute-done.3.rest_4_ = bf16[240,512]{1,0:T(8,128)(2,1)} collective-permute-done((bf16[240,512]{1,0:T(8,128)(2,1)S(1)}, bf16[240,512]{1,0:T(8,128)(2,1)}, u32[]{:S(2)}, u32[]{:S(2)}) %collective-permute-start.3) | collective-permute-done | bytes 245792 | tf_op jit(solution)/shard_map/ppermute | solution.py:504
  52.3 2.7 %collective-permute-done.22.rest_6_ = bf16[48,3840]{1,0:T(8,128)(2,1)S(1)} collective-permute-done((bf16[48,3840]{1,0:T(8,128)(2,1)S(1)}, bf16[48,3840]{1,0:T(8,128)(2,1)S(1)}, u32[]{:S(2)}, u32[]{:S(2)}) %collective-permute-start.22) | collective-permute-done | bytes 368672 | tf_op jit(solution)/shard_map/ppermute | solution.py:506
  56.2 2.7 %collective-permute-done.19.rest_3_ = bf16[48,3840]{1,0:T(8,128)(2,1)S(1)} collective-permute-done((bf16[48,3840]{1,0:T(8,128)(2,1)S(1)}, bf16[48,3840]{1,0:T(8,128)(2,1)S(1)}, u32[]{:S(2)}, u32[]{:S(2)}) %collective-permute-start.19) | collective-permute-done | bytes 368672 | tf_op jit(solution)/shard_map/ppermute | solution.py:504
  58.9 1.4 collective-permute-start.23
  60.3 0.6 collective-permute-start.20
  60.9 0.9 copy.25.sc_ref
  61.8 0.7 pad_add_fusion.1.where_ref
  62.5 8.5 %mixer_forward.1 = (bf16[6,512,512]{2,1,0:T(8,128)(2,1)}, bf16[512,768]{1,0:T(8,128)(2,1)}, bf16[512,384]{1,0:T(8,128)(2,1)}, f32[512,768]{1,0:T(8,128)}, f32[51...) custom-call(s32[16]{0:T(128)} %pad_add_fusion.1.where_ref, ...), custom_call_target="tpu_custom_call" | custom-call | tf_op jit(solution)/shard_map/mixer_forward/pallas_call | solution.py:164
  74.4 6.3 %collective-permute-done.15.other_ref = bf16[512,384]{1,0:T(8,128)(2,1)S(1)} collective-permute-done((bf16[512,384]{1,0:T(8,128)(2,1)}, bf16[512,384]{1,0:T(8,128)(2,1)S(1)}, u32[]{:S(2)}, u32[]{:S(2)}) %collective-permute-start.15) | collective-permute-done | bytes 393248 | tf_op jit(solution)/shard_map/ppermute | solution.py:595
  80.8 0.7 copy-done.22
  81.6 13.3 %ffn_main.1 = (bf16[512,768]{1,0:T(8,128)(2,1)}, f32[512,768]{1,0:T(8,128)}, bf16[512,768]{1,0:T(8,128)(2,1)}, bf16[512,1536]{1,0:T(8,128)(2,1)}, bf16[512,1536]{1,0:T(8,128)(2,1)}, /*index=5*/bf16[768,768]{1,0:T(8,128)(2,1)}) custom-call(s32[17]{0:T(128)} %pad_add_fusion.place_ref, bf16[512,768]{1,0:T(8,128)(2,1)} %tok_ref.5, ...), custom_call_target="tpu_custom_call" | custom-call | tf_op jit(solution)/shard_map/ffn_main/pallas_call | solution.py:239
  94.9 7.4 %ffn_grads.1 = (bf16[8,48,3072]{2,1,0:T(8,128)(2,1)}, bf16[8,48,3072]{2,1,0:T(8,128)(2,1)}) custom-call(s32[16]{0:T(128)} %pad_add_fusion.2.where_ref, bf16[512,768]{1,0:T(8,128)(2,1)} %get-tuple-element.55.n2_ref, bf16[512,1536]{1,0:T(8,128)(2,1)} %get-tuple-element.56.gpre_ref, bf16[512,1536]{1,0:T(8,128)(2,1)} %get-tuple-element.37.act_ref, ...), custom_call_target="tpu_custom_call" | custom-call | tf_op jit(solution)/shard_map/ffn_grads/pallas_call | solution.py:285
  102.9 19.5 %collective-permute-done.33.b_ref = bf16[512,768]{1,0:T(8,128)(2,1)S(1)} collective-permute-done((bf16[512,768]{1,0:T(8,128)(2,1)S(1)}, bf16[512,768]{1,0:T(8,128)(2,1)S(1)}, u32[]{:S(2)}, u32[]{:S(2)}) %collective-permute-start.33) | collective-permute-done | bytes 786464 | tf_op jit(solution)/shard_map/ppermute | solution.py:599
  122.4 0.9 copy-done.21
  123.3 10.9 %mixer_back.1 = (f32[512,768]{1,0:T(8,128)}, bf16[512,768]{1,0:T(8,128)(2,1)}, bf16[512,768]{1,0:T(8,128)(2,1)}, bf16[512,384]{1,0:T(8,128)(2,1)}, bf16[512,768]...) custom-call(bf16[512,768]{1,0:T(8,128)(2,1)} %get-tuple-element.38.a_ref, bf16[512,768]{1,0:T(8,128)(2,1)} %copy-done.21, ...), custom_call_target="tpu_custom_call" | custom-call | tf_op jit(solution)/shard_map/mixer_back/pallas_call | solution.py:393
  134.8 3.2 %collective-permute-done.35.gb_ref = f32[16,128]{1,0:T(8,128)S(1)} collective-permute-done((f32[16,128]{1,0:T(8,128)}, f32[16,128]{1,0:T(8,128)S(1)}, u32[]{:S(2)}, u32[]{:S(2)}) %collective-permute-start.35) | collective-permute-done | bytes 8224 | tf_op jit(solution)/shard_map/ppermute | solution.py:606
  138.6 8.8 %mixer_grads.1 = (bf16[8,288,512]{2,1,0:T(8,128)(2,1)}, bf16[8,288,512]{2,1,0:T(8,128)(2,1)}) custom-call(s32[16]{0:T(128)} %pad_add_fusion.2.where_ref, bf16[512,768]{1,0:T(8,128)(2,1)} %get-tuple-element.46.xh_ref, bf16[512,768]{1,0:T(8,128)(2,1)} %get-tuple-element.47.va_ref, bf16[6,512,512]{2,1,0:T(8,128)(2,1)} %get-tuple-element.42.e_ref, ...), custom_call_target="tpu_custom_call" | custom-call | tf_op jit(solution)/shard_map/mixer_grads/pallas_call | solution.py:458
  147.5 0.9 fusion.22
  148.3 1.6 collective-permute-start.45
  149.9 5.7 %ffn_out.1 = bf16[512,768]{1,0:T(8,128)(2,1)} custom-call(s32[16]{0:T(128)} %pad_add_fusion.1.where_ref, bf16[512,1536]{1,0:T(8,128)(2,1)} %get-tuple-element.37.act_ref, bf16[48,3840]{1,0:T(8,128)(2,1)} %pack_second.1.rest_0_, bf16[48,3840]{1,0:T(8,128)(2,1)} %copy-done.7, bf16[48,3840]{1,0:T(8,128)(2,1)} %copy-done.10, bf16[48,3840]{1,0:T(8,128)(2,1)} %copy-done.12, ...), custom_call_target="tpu_custom_call" | custom-call | tf_op jit(solution)/shard_map/ffn_out/pallas_call | solution.py:317
  156.3 1.6 collective-permute-start.34
  158.0 1.1 fusion.10
  159.1 1.6 collective-permute-start.46
  160.7 15.6 %collective-permute-done.32 = bf16[512,768]{1,0:T(8,128)(2,1)S(1)} collective-permute-done((bf16[512,768]{1,0:T(8,128)(2,1)}, bf16[512,768]{1,0:T(8,128)(2,1)S(1)}, u32[]{:S(2)}, u32[]{:S(2)}) %collective-permute-start.32) | collective-permute-done | bytes 786464 | tf_op jit(solution)/shard_map/ppermute | solution.py:602
  176.3 1.2 add_convert_fusion
  178.1 1.6 collective-permute-start.47
  179.7 12.8 %collective-permute-done.34 = bf16[512,768]{1,0:T(8,128)(2,1)S(1)} collective-permute-done((bf16[512,768]{1,0:T(8,128)(2,1)S(1)}, bf16[512,768]{1,0:T(8,128)(2,1)S(1)}, u32[]{:S(2)}, u32[]{:S(2)}) %collective-permute-start.34) | collective-permute-done | bytes 786464 | tf_op jit(solution)/shard_map/ppermute | solution.py:607
  193.0 1.2 fusion.20
  194.2 1.6 collective-permute-start.37
  197.0 1.6 collective-permute-start.48
  198.6 5.6 %collective-permute-done.37 = bf16[288,512]{1,0:T(8,128)(2,1)S(1)} collective-permute-done((bf16[288,512]{1,0:T(8,128)(2,1)S(1)}, bf16[288,512]{1,0:T(8,128)(2,1)S(1)}, u32[]{:S(2)}, u32[]{:S(2)}) %collective-permute-start.37) | collective-permute-done | bytes 294944 | tf_op jit(solution)/shard_map/ppermute | solution.py:531
  204.2 1.1 fusion.16
  205.3 1.6 collective-permute-start.38
  207.5 7.7 %collective-permute-done.38 = bf16[288,512]{1,0:T(8,128)(2,1)S(1)} collective-permute-done((bf16[288,512]{1,0:T(8,128)(2,1)S(1)}, bf16[288,512]{1,0:T(8,128)(2,1)S(1)}, u32[]{:S(2)}, u32[]{:S(2)}) %collective-permute-start.38) | collective-permute-done | bytes 294944 | tf_op jit(solution)/shard_map/ppermute | solution.py:534
  215.2 1.1 fusion.17
  216.3 1.6 collective-permute-start.39
  217.9 1.5 fusion.6
  219.4 4.4 %collective-permute-done.39 = bf16[288,512]{1,0:T(8,128)(2,1)S(1)} collective-permute-done((bf16[288,512]{1,0:T(8,128)(2,1)S(1)}, bf16[288,512]{1,0:T(8,128)(2,1)S(1)}, u32[]{:S(2)}, u32[]{:S(2)}) %collective-permute-start.39) | collective-permute-done | bytes 294944 | tf_op jit(solution)/shard_map/ppermute | solution.py:534
  223.7 1.3 fusion.18
  225.7 1.6 collective-permute-start.40
  227.3 4.5 %collective-permute-done.42 = bf16[288,512]{1,0:T(8,128)(2,1)S(1)} collective-permute-done((bf16[288,512]{1,0:T(8,128)(2,1)S(1)}, bf16[288,512]{1,0:T(8,128)(2,1)S(1)}, u32[]{:S(2)}, u32[]{:S(2)}) %collective-permute-start.42) | collective-permute-done | bytes 294944 | tf_op jit(solution)/shard_map/ppermute | solution.py:536
  231.8 1.1 fusion.15
  233.4 0.8 slice_bitcast_fusion
  234.2 5.4 %collective-permute-done.43 = bf16[288,512]{1,0:T(8,128)(2,1)S(1)} collective-permute-done((bf16[288,512]{1,0:T(8,128)(2,1)S(1)}, bf16[288,512]{1,0:T(8,128)(2,1)S(1)}, u32[]{:S(2)}, u32[]{:S(2)}) %collective-permute-start.43) | collective-permute-done | bytes 294944 | tf_op jit(solution)/shard_map/ppermute | solution.py:536
  239.6 1.1 fusion.19
  241.3 0.8 slice.170
  242.0 0.7 slice_bitcast_fusion.1
  (159 shorter events, 15.4 us)
Async XLA Ops:
  1.6 9.0 %collective-permute-start.16 = (bf16[384,48]{1,0:T(8,128)(2,1)S(1)}, bf16[384,48]{1,0:T(8,128)(2,1)S(1)}, u32[]{:S(2)}, u32[]{:S(2)}) collective-permute-start(bf16[384,48]{1,0:T(8,128)(2,1)S(1)} %copy.26), channel_id=1, source_target_pairs={{0,1},{1,0},{2,3},{3,2},{4,5},{5,4},{6,7},{7,6},{8,9},{9,8},{10,11... | collective-permute-start | bytes 110600 | tf_op jit(solution)/shard_map/ppermute | solution.py:564
  6.4 9.2 %collective-permute-start = (bf16[240,512]{1,0:T(8,128)(2,1)}, bf16[240,512]{1,0:T(8,128)(2,1)S(1)}, u32[]{:S(2)}, u32[]{:S(2)}) collective-permute-start(bf16[240,512]{1,0:T(8,128)(2,1)} %pack_first.1.rest_0_), channel_id=1, source_target_pairs={{0,8},{2,10},{8,16},{10,18},{16,24},{18,26},{24,28},{26,30},{28,20... | collective-permute-start | bytes 737288 | tf_op jit(solution)/shard_map/ppermute | solution.py:504
  8.0 7.7 %collective-permute-start.4 = (bf16[240,512]{1,0:T(8,128)(2,1)}, bf16[240,512]{1,0:T(8,128)(2,1)S(1)}, u32[]{:S(2)}, u32[]{:S(2)}) collective-permute-start(bf16[240,512]{1,0:T(8,128)(2,1)} %pack_first.1.rest_0_), channel_id=1, source_target_pairs={{0,4},{2,6},{8,0},{10,2},{16,8},{18,10},{24,16},{26,18},{28,24},{3... | collective-permute-start | bytes 737288 | tf_op jit(solution)/shard_map/ppermute | solution.py:506
  8.5 8.9 %collective-permute-start.7 = (bf16[240,512]{1,0:T(8,128)(2,1)}, bf16[240,512]{1,0:T(8,128)(2,1)S(1)}, u32[]{:S(2)}, u32[]{:S(2)}) collective-permute-start(bf16[240,512]{1,0:T(8,128)(2,1)} %pack_first.1.rest_0_), channel_id=1, source_target_pairs={{0,2},{2,0},{4,6},{6,4},{8,10},{10,8},{12,14},{14,12},{16,18},{18,... | collective-permute-start | bytes 737288 | tf_op jit(solution)/shard_map/ppermute | solution.py:508
  8.5 52.4 %copy-start.38 = (s32[8]{0:T(128)S(1)}, s32[8]{0:T(128)}, u32[]{:S(2)}) copy-start(s32[8]{0:T(128)} %constant.95.clone) | copy-start | bytes 100
  8.5 52.5 %copy-start.37 = (s32[1,512]{1,0:T(1,128)S(1)}, s32[1,512]{1,0:T(1,128)}, u32[]{:S(2)}) copy-start(s32[1,512]{1,0:T(1,128)} %sr_ref.1) | copy-start | bytes 6148
  13.7 11.6 %collective-permute-start.17 = (bf16[48,3840]{1,0:T(8,128)(2,1)}, bf16[48,3840]{1,0:T(8,128)(2,1)S(1)}, u32[]{:S(2)}, u32[]{:S(2)}) collective-permute-start(bf16[48,3840]{1,0:T(8,128)(2,1)} %pack_second.1.rest_0_), channel_id=1, source_target_pairs={{0,8},{2,10},{8,16},{10,18},{16,24},{18,26},{24,28},{26,30},{28,20... | collective-permute-start | bytes 1105928 | tf_op jit(solution)/shard_map/ppermute | solution.py:504
  15.2 11.6 %collective-permute-start.21 = (bf16[48,3840]{1,0:T(8,128)(2,1)}, bf16[48,3840]{1,0:T(8,128)(2,1)S(1)}, u32[]{:S(2)}, u32[]{:S(2)}) collective-permute-start(bf16[48,3840]{1,0:T(8,128)(2,1)} %pack_second.1.rest_0_), channel_id=1, source_target_pairs={{0,4},{2,6},{8,0},{10,2},{16,8},{18,10},{24,16},{26,18},{28,24},{3... | collective-permute-start | bytes 1105928 | tf_op jit(solution)/shard_map/ppermute | solution.py:506
  15.7 29.2 %copy-start.23 = (bf16[240,512]{1,0:T(8,128)(2,1)}, bf16[240,512]{1,0:T(8,128)(2,1)S(1)}, u32[]{:S(2)}) copy-start(bf16[240,512]{1,0:T(8,128)(2,1)S(1)} %collective-permute-done.rest_1_) | copy-start | bytes 737284
  15.7 11.2 %collective-permute-start.24 = (bf16[48,3840]{1,0:T(8,128)(2,1)}, bf16[48,3840]{1,0:T(8,128)(2,1)S(1)}, u32[]{:S(2)}, u32[]{:S(2)}) collective-permute-start(bf16[48,3840]{1,0:T(8,128)(2,1)} %pack_second.1.rest_0_), channel_id=1, source_target_pairs={{0,2},{2,0},{4,6},{6,4},{8,10},{10,8},{12,14},{14,12},{16,18},{18,... | collective-permute-start | bytes 1105928 | tf_op jit(solution)/shard_map/ppermute | solution.py:508
  15.7 29.2 %copy-start.24 = (bf16[240,512]{1,0:T(8,128)(2,1)}, bf16[240,512]{1,0:T(8,128)(2,1)S(1)}, u32[]{:S(2)}) copy-start(bf16[240,512]{1,0:T(8,128)(2,1)S(1)} %collective-permute-done.4.rest_5_) | copy-start | bytes 737284
  15.7 14.5 %collective-permute-start.1 = (bf16[240,512]{1,0:T(8,128)(2,1)S(1)}, bf16[240,512]{1,0:T(8,128)(2,1)S(1)}, u32[]{:S(2)}, u32[]{:S(2)}) collective-permute-start(bf16[240,512]{1,0:T(8,128)(2,1)S(1)} %collective-permute-done.rest_1_), channel_id=1, source_target_pairs={{0,8},{2,10},{8,16},{10,18},{16,24},{18,26},{24,28},{26,30},{28,20... | collective-permute-start | bytes 737288 | tf_op jit(solution)/shard_map/ppermute | solution.py:504
  17.4 14.4 %collective-permute-start.5 = (bf16[240,512]{1,0:T(8,128)(2,1)S(1)}, bf16[240,512]{1,0:T(8,128)(2,1)S(1)}, u32[]{:S(2)}, u32[]{:S(2)}) collective-permute-start(bf16[240,512]{1,0:T(8,128)(2,1)S(1)} %collective-permute-done.4.rest_5_), channel_id=1, source_target_pairs={{0,4},{2,6},{8,0},{10,2},{16,8},{18,10},{24,16},{26,18},{28,24},{3... | collective-permute-start | bytes 737288 | tf_op jit(solution)/shard_map/ppermute | solution.py:506
  25.3 45.7 %copy-start.7 = (bf16[48,3840]{1,0:T(8,128)(2,1)}, bf16[48,3840]{1,0:T(8,128)(2,1)S(1)}, u32[]{:S(2)}) copy-start(bf16[48,3840]{1,0:T(8,128)(2,1)S(1)} %collective-permute-done.17.rest_1_) | copy-start | bytes 1105924
  25.3 7.0 %collective-permute-start.8 = (bf16[240,512]{1,0:T(8,128)(2,1)S(1)}, bf16[240,512]{1,0:T(8,128)(2,1)S(1)}, u32[]{:S(2)}, u32[]{:S(2)}) collective-permute-start(bf16[240,512]{1,0:T(8,128)(2,1)S(1)} %collective-permute-done.rest_1_), channel_id=1, source_target_pairs={{0,2},{2,0},{4,6},{6,4},{8,10},{10,8},{12,14},{14,12},{16,18},{18,... | collective-permute-start | bytes 737288 | tf_op jit(solution)/shard_map/ppermute | solution.py:508
  26.9 44.1 %copy-start.8 = (bf16[48,3840]{1,0:T(8,128)(2,1)}, bf16[48,3840]{1,0:T(8,128)(2,1)S(1)}, u32[]{:S(2)}) copy-start(bf16[48,3840]{1,0:T(8,128)(2,1)S(1)} %collective-permute-done.21.rest_5_) | copy-start | bytes 1105924
  26.9 5.4 %collective-permute-start.12 = (bf16[240,512]{1,0:T(8,128)(2,1)S(1)}, bf16[240,512]{1,0:T(8,128)(2,1)S(1)}, u32[]{:S(2)}, u32[]{:S(2)}) collective-permute-start(bf16[240,512]{1,0:T(8,128)(2,1)S(1)} %collective-permute-done.4.rest_5_), channel_id=1, source_target_pairs={{0,2},{2,0},{4,6},{6,4},{8,10},{10,8},{12,14},{14,12},{16,18},{18,... | collective-permute-start | bytes 737288 | tf_op jit(solution)/shard_map/ppermute | solution.py:508
  26.9 44.1 %copy-start.9 = (bf16[48,3840]{1,0:T(8,128)(2,1)}, bf16[48,3840]{1,0:T(8,128)(2,1)S(1)}, u32[]{:S(2)}) copy-start(bf16[48,3840]{1,0:T(8,128)(2,1)S(1)} %collective-permute-done.24.rest_8_) | copy-start | bytes 1105924
  26.9 18.5 %collective-permute-start.18 = (bf16[48,3840]{1,0:T(8,128)(2,1)S(1)}, bf16[48,3840]{1,0:T(8,128)(2,1)S(1)}, u32[]{:S(2)}, u32[]{:S(2)}) collective-permute-start(bf16[48,3840]{1,0:T(8,128)(2,1)S(1)} %collective-permute-done.17.rest_1_), channel_id=1, source_target_pairs={{0,8},{2,10},{8,16},{10,18},{16,24},{18,26},{24,28},{26,30},{28,20... | collective-permute-start | bytes 1105928 | tf_op jit(solution)/shard_map/ppermute | solution.py:504
  30.2 13.1 %collective-permute-start.2 = (bf16[240,512]{1,0:T(8,128)(2,1)S(1)}, bf16[240,512]{1,0:T(8,128)(2,1)S(1)}, u32[]{:S(2)}, u32[]{:S(2)}) collective-permute-start(bf16[240,512]{1,0:T(8,128)(2,1)S(1)} %collective-permute-done.1.rest_2_), channel_id=1, source_target_pairs={{0,8},{2,10},{8,16},{10,18},{16,24},{18,26},{24,28},{26,30},{28,20... | collective-permute-start | bytes 737288 | tf_op jit(solution)/shard_map/ppermute | solution.py:504
  31.8 13.1 %collective-permute-start.6 = (bf16[240,512]{1,0:T(8,128)(2,1)S(1)}, bf16[240,512]{1,0:T(8,128)(2,1)S(1)}, u32[]{:S(2)}, u32[]{:S(2)}) collective-permute-start(bf16[240,512]{1,0:T(8,128)(2,1)S(1)} %collective-permute-done.5.rest_6_), channel_id=1, source_target_pairs={{0,4},{2,6},{8,0},{10,2},{16,8},{18,10},{24,16},{26,18},{28,24},{3... | collective-permute-start | bytes 737288 | tf_op jit(solution)/shard_map/ppermute | solution.py:506
  32.2 14.8 %collective-permute-start.9 = (bf16[240,512]{1,0:T(8,128)(2,1)S(1)}, bf16[240,512]{1,0:T(8,128)(2,1)S(1)}, u32[]{:S(2)}, u32[]{:S(2)}) collective-permute-start(bf16[240,512]{1,0:T(8,128)(2,1)S(1)} %collective-permute-done.1.rest_2_), channel_id=1, source_target_pairs={{0,2},{2,0},{4,6},{6,4},{8,10},{10,8},{12,14},{14,12},{16,18},{18,... | collective-permute-start | bytes 737288 | tf_op jit(solution)/shard_map/ppermute | solution.py:508
  32.2 14.9 %collective-permute-start.13 = (bf16[240,512]{1,0:T(8,128)(2,1)S(1)}, bf16[240,512]{1,0:T(8,128)(2,1)S(1)}, u32[]{:S(2)}, u32[]{:S(2)}) collective-permute-start(bf16[240,512]{1,0:T(8,128)(2,1)S(1)} %collective-permute-done.5.rest_6_), channel_id=1, source_target_pairs={{0,2},{2,0},{4,6},{6,4},{8,10},{10,8},{12,14},{14,12},{16,18},{18,... | collective-permute-start | bytes 737288 | tf_op jit(solution)/shard_map/ppermute | solution.py:508
  43.3 9.0 %collective-permute-start.3 = (bf16[240,512]{1,0:T(8,128)(2,1)S(1)}, bf16[240,512]{1,0:T(8,128)(2,1)}, u32[]{:S(2)}, u32[]{:S(2)}) collective-permute-start(bf16[240,512]{1,0:T(8,128)(2,1)S(1)} %collective-permute-done.2.rest_3_), channel_id=1, source_target_pairs={{0,8},{2,10},{8,16},{10,18},{16,24},{18,26},{24,28},{26,30},{28,20... | collective-permute-start | bytes 737288 | tf_op jit(solution)/shard_map/ppermute | solution.py:504
  44.9 10.1 %collective-permute-start.22 = (bf16[48,3840]{1,0:T(8,128)(2,1)S(1)}, bf16[48,3840]{1,0:T(8,128)(2,1)S(1)}, u32[]{:S(2)}, u32[]{:S(2)}) collective-permute-start(bf16[48,3840]{1,0:T(8,128)(2,1)S(1)} %collective-permute-done.21.rest_5_), channel_id=1, source_target_pairs={{0,4},{2,6},{8,0},{10,2},{16,8},{18,10},{24,16},{26,18},{28,24},{3... | collective-permute-start | bytes 1105928 | tf_op jit(solution)/shard_map/ppermute | solution.py:506
  45.4 25.6 %copy-start.10 = (bf16[48,3840]{1,0:T(8,128)(2,1)}, bf16[48,3840]{1,0:T(8,128)(2,1)S(1)}, u32[]{:S(2)}) copy-start(bf16[48,3840]{1,0:T(8,128)(2,1)S(1)} %collective-permute-done.18.rest_2_) | copy-start | bytes 1105924
  45.4 13.5 %collective-permute-start.19 = (bf16[48,3840]{1,0:T(8,128)(2,1)S(1)}, bf16[48,3840]{1,0:T(8,128)(2,1)S(1)}, u32[]{:S(2)}, u32[]{:S(2)}) collective-permute-start(bf16[48,3840]{1,0:T(8,128)(2,1)S(1)} %collective-permute-done.18.rest_2_), channel_id=1, source_target_pairs={{0,8},{2,10},{8,16},{10,18},{16,24},{18,26},{24,28},{26,30},{28,20... | collective-permute-start | bytes 1105928 | tf_op jit(solution)/shard_map/ppermute | solution.py:504
  47.0 7.9 %collective-permute-start.10 = (bf16[240,512]{1,0:T(8,128)(2,1)S(1)}, bf16[240,512]{1,0:T(8,128)(2,1)S(1)}, u32[]{:S(2)}, u32[]{:S(2)}) collective-permute-start(bf16[240,512]{1,0:T(8,128)(2,1)S(1)} %collective-permute-done.2.rest_3_), channel_id=1, source_target_pairs={{0,2},{2,0},{4,6},{6,4},{8,10},{10,8},{12,14},{14,12},{16,18},{18,... | collective-permute-start | bytes 737288 | tf_op jit(solution)/shard_map/ppermute | solution.py:508
  47.1 8.6 %collective-permute-start.14 = (bf16[240,512]{1,0:T(8,128)(2,1)S(1)}, bf16[240,512]{1,0:T(8,128)(2,1)}, u32[]{:S(2)}, u32[]{:S(2)}) collective-permute-start(bf16[240,512]{1,0:T(8,128)(2,1)S(1)} %collective-permute-done.6.rest_7_), channel_id=1, source_target_pairs={{0,2},{2,0},{4,6},{6,4},{8,10},{10,8},{12,14},{14,12},{16,18},{18,... | collective-permute-start | bytes 737288 | tf_op jit(solution)/shard_map/ppermute | solution.py:508
  52.3 8.0 %collective-permute-start.11 = (bf16[240,512]{1,0:T(8,128)(2,1)}, bf16[240,512]{1,0:T(8,128)(2,1)}, u32[]{:S(2)}, u32[]{:S(2)}) collective-permute-start(bf16[240,512]{1,0:T(8,128)(2,1)} %collective-permute-done.3.rest_4_), channel_id=1, source_target_pairs={{0,2},{2,0},{4,6},{6,4},{8,10},{10,8},{12,14},{14,12},{16,18},{18,... | collective-permute-start | bytes 737288 | tf_op jit(solution)/shard_map/ppermute | solution.py:508
  55.0 16.4 %copy-start.11 = (bf16[48,3840]{1,0:T(8,128)(2,1)}, bf16[48,3840]{1,0:T(8,128)(2,1)S(1)}, u32[]{:S(2)}) copy-start(bf16[48,3840]{1,0:T(8,128)(2,1)S(1)} %collective-permute-done.22.rest_6_) | copy-start | bytes 1105924
  55.0 16.0 %collective-permute-start.25 = (bf16[48,3840]{1,0:T(8,128)(2,1)S(1)}, bf16[48,3840]{1,0:T(8,128)(2,1)S(1)}, u32[]{:S(2)}, u32[]{:S(2)}) collective-permute-start(bf16[48,3840]{1,0:T(8,128)(2,1)S(1)} %collective-permute-done.17.rest_1_), channel_id=1, source_target_pairs={{0,2},{2,0},{4,6},{6,4},{8,10},{10,8},{12,14},{14,12},{16,18},{18,... | collective-permute-start | bytes 1105928 | tf_op jit(solution)/shard_map/ppermute | solution.py:508
  55.0 16.4 %collective-permute-start.29 = (bf16[48,3840]{1,0:T(8,128)(2,1)S(1)}, bf16[48,3840]{1,0:T(8,128)(2,1)S(1)}, u32[]{:S(2)}, u32[]{:S(2)}) collective-permute-start(bf16[48,3840]{1,0:T(8,128)(2,1)S(1)} %collective-permute-done.21.rest_5_), channel_id=1, source_target_pairs={{0,2},{2,0},{4,6},{6,4},{8,10},{10,8},{12,14},{14,12},{16,18},{18,... | collective-permute-start | bytes 1105928 | tf_op jit(solution)/shard_map/ppermute | solution.py:508
  55.7 16.3 %collective-permute-start.26 = (bf16[48,3840]{1,0:T(8,128)(2,1)S(1)}, bf16[48,3840]{1,0:T(8,128)(2,1)S(1)}, u32[]{:S(2)}, u32[]{:S(2)}) collective-permute-start(bf16[48,3840]{1,0:T(8,128)(2,1)S(1)} %collective-permute-done.18.rest_2_), channel_id=1, source_target_pairs={{0,2},{2,0},{4,6},{6,4},{8,10},{10,8},{12,14},{14,12},{16,18},{18,... | collective-permute-start | bytes 1105928 | tf_op jit(solution)/shard_map/ppermute | solution.py:508
  58.9 12.6 %collective-permute-start.23 = (bf16[48,3840]{1,0:T(8,128)(2,1)S(1)}, bf16[48,3840]{1,0:T(8,128)(2,1)}, u32[]{:S(2)}, u32[]{:S(2)}) collective-permute-start(bf16[48,3840]{1,0:T(8,128)(2,1)S(1)} %collective-permute-done.22.rest_6_), channel_id=1, source_target_pairs={{0,4},{2,6},{8,0},{10,2},{16,8},{18,10},{24,16},{26,18},{28,24},{3... | collective-permute-start | bytes 1105928 | tf_op jit(solution)/shard_map/ppermute | solution.py:506
  60.3 11.8 %collective-permute-start.20 = (bf16[48,3840]{1,0:T(8,128)(2,1)S(1)}, bf16[48,3840]{1,0:T(8,128)(2,1)}, u32[]{:S(2)}, u32[]{:S(2)}) collective-permute-start(bf16[48,3840]{1,0:T(8,128)(2,1)S(1)} %collective-permute-done.19.rest_3_), channel_id=1, source_target_pairs={{0,8},{2,10},{8,16},{10,18},{16,24},{18,26},{24,28},{26,30},{28,20... | collective-permute-start | bytes 1105928 | tf_op jit(solution)/shard_map/ppermute | solution.py:504
  71.0 9.7 %collective-permute-start.15 = (bf16[512,384]{1,0:T(8,128)(2,1)}, bf16[512,384]{1,0:T(8,128)(2,1)S(1)}, u32[]{:S(2)}, u32[]{:S(2)}) collective-permute-start(bf16[512,384]{1,0:T(8,128)(2,1)} %get-tuple-element.34.own_ref.mixed_ref), channel_id=1, source_target_pairs={{0,1},{1,0},{2,3},{3,2},{4,5},{5,4},{6,7},{7,6},{8,9},{9,8},{10,11... | collective-permute-start | bytes 1179656 | tf_op jit(solution)/shard_map/ppermute | solution.py:595
  71.4 2.3 collective-permute-start.30
  71.5 2.7 %collective-permute-start.27 = (bf16[48,3840]{1,0:T(8,128)(2,1)S(1)}, bf16[48,3840]{1,0:T(8,128)(2,1)S(1)}, u32[]{:S(2)}, u32[]{:S(2)}) collective-permute-start(bf16[48,3840]{1,0:T(8,128)(2,1)S(1)} %collective-permute-done.19.rest_3_), channel_id=1, source_target_pairs={{0,2},{2,0},{4,6},{6,4},{8,10},{10,8},{12,14},{14,12},{16,18},{18,... | collective-permute-start | bytes 1105928 | tf_op jit(solution)/shard_map/ppermute | solution.py:508
  72.0 2.4 %collective-permute-start.31 = (bf16[48,3840]{1,0:T(8,128)(2,1)}, bf16[48,3840]{1,0:T(8,128)(2,1)S(1)}, u32[]{:S(2)}, u32[]{:S(2)}) collective-permute-start(bf16[48,3840]{1,0:T(8,128)(2,1)} %collective-permute-done.23.rest_7_), channel_id=1, source_target_pairs={{0,2},{2,0},{4,6},{6,4},{8,10},{10,8},{12,14},{14,12},{16,18},{18,... | collective-permute-start | bytes 1105928 | tf_op jit(solution)/shard_map/ppermute | solution.py:508
  72.1 8.6 %collective-permute-start.28 = (bf16[48,3840]{1,0:T(8,128)(2,1)}, bf16[48,3840]{1,0:T(8,128)(2,1)S(1)}, u32[]{:S(2)}, u32[]{:S(2)}) collective-permute-start(bf16[48,3840]{1,0:T(8,128)(2,1)} %collective-permute-done.20.rest_4_), channel_id=1, source_target_pairs={{0,2},{2,0},{4,6},{6,4},{8,10},{10,8},{12,14},{14,12},{16,18},{18,... | collective-permute-start | bytes 1105928 | tf_op jit(solution)/shard_map/ppermute | solution.py:508
  102.3 45.1 %collective-permute-start.44 = (bf16[8,48,3072]{2,1,0:T(8,128)(2,1)}, bf16[8,48,3072]{2,1,0:T(8,128)(2,1)S(1)}, u32[]{:S(2)}, u32[]{:S(2)}) collective-permute-start(bf16[8,48,3072]{2,1,0:T(8,128)(2,1)} %get-tuple-element.58), channel_id=1, source_target_pairs={{0,2},{2,0},{4,6},{6,4},{8,10},{10,8},{12,14},{14,12},{16,18},{18,... | collective-permute-start | bytes 7077896 | tf_op jit(solution)/shard_map/ppermute | solution.py:522
  102.4 20.0 %collective-permute-start.33 = (bf16[512,768]{1,0:T(8,128)(2,1)S(1)}, bf16[512,768]{1,0:T(8,128)(2,1)S(1)}, u32[]{:S(2)}, u32[]{:S(2)}) collective-permute-start(bf16[512,768]{1,0:T(8,128)(2,1)S(1)} %copy-done.20), channel_id=1, source_target_pairs={{0,1},{1,0},{2,3},{3,2},{4,5},{5,4},{6,7},{7,6},{8,9},{9,8},{10,11... | collective-permute-start | bytes 2359304 | tf_op jit(solution)/shard_map/ppermute | solution.py:599
  134.1 3.9 %collective-permute-start.35 = (f32[16,128]{1,0:T(8,128)}, f32[16,128]{1,0:T(8,128)S(1)}, u32[]{:S(2)}, u32[]{:S(2)}) collective-permute-start(f32[16,128]{1,0:T(8,128)} %get-tuple-element.51.ga_ref), channel_id=1, source_target_pairs={{0,1},{1,0},{2,3},{3,2},{4,5},{5,4},{6,7},{7,6},{8,9},{9,8},{10,11... | collective-permute-start | bytes 24584 | tf_op jit(solution)/shard_map/ppermute | solution.py:606
  147.4 45.6 %collective-permute-start.36 = (bf16[8,288,512]{2,1,0:T(8,128)(2,1)}, bf16[8,288,512]{2,1,0:T(8,128)(2,1)}, u32[]{:S(2)}, u32[]{:S(2)}) collective-permute-start(bf16[8,288,512]{2,1,0:T(8,128)(2,1)} %get-tuple-element.54), channel_id=1, source_target_pairs={{0,2},{2,0},{4,6},{6,4},{8,10},{10,8},{12,14},{14,12},{16,18},{18,... | collective-permute-start | bytes 7077896 | tf_op jit(solution)/shard_map/ppermute | solution.py:522
  148.3 9.7 %collective-permute-start.45 = (bf16[48,3072]{1,0:T(8,128)(2,1)}, bf16[48,3072]{1,0:T(8,128)(2,1)}, u32[]{:S(2)}, u32[]{:S(2)}) collective-permute-start(bf16[48,3072]{1,0:T(8,128)(2,1)} %get-tuple-element.63), channel_id=1, source_target_pairs={{0,8},{2,10},{8,16},{10,18},{16,24},{18,26},{24,28},{26,30},{28,20... | collective-permute-start | bytes 884744 | tf_op jit(solution)/shard_map/ppermute | solution.py:531
  149.9 26.4 %copy-start.1 = (f32[512,768]{1,0:T(8,128)S(1)}, f32[512,768]{1,0:T(8,128)}, u32[]{:S(2)}) copy-start(f32[512,768]{1,0:T(8,128)} %get-tuple-element.36.res_ref) | copy-start | bytes 4718596
  155.6 20.7 %copy-start.3 = (bf16[512,768]{1,0:T(8,128)(2,1)S(1)}, bf16[512,768]{1,0:T(8,128)(2,1)}, u32[]{:S(2)}) copy-start(bf16[512,768]{1,0:T(8,128)(2,1)} %ffn_out.1) | copy-start | bytes 2359300
  155.7 20.7 %collective-permute-start.32 = (bf16[512,768]{1,0:T(8,128)(2,1)}, bf16[512,768]{1,0:T(8,128)(2,1)S(1)}, u32[]{:S(2)}, u32[]{:S(2)}) collective-permute-start(bf16[512,768]{1,0:T(8,128)(2,1)} %ffn_out.1), channel_id=1, source_target_pairs={{0,1},{1,0},{2,3},{3,2},{4,5},{5,4},{6,7},{7,6},{8,9},{9,8},{10,11... | collective-permute-start | bytes 2359304 | tf_op jit(solution)/shard_map/ppermute | solution.py:602
  156.3 36.2 %collective-permute-start.34 = (bf16[512,768]{1,0:T(8,128)(2,1)S(1)}, bf16[512,768]{1,0:T(8,128)(2,1)S(1)}, u32[]{:S(2)}, u32[]{:S(2)}) collective-permute-start(bf16[512,768]{1,0:T(8,128)(2,1)S(1)} %copy-done.2), channel_id=1, source_target_pairs={{0,1},{1,0},{2,3},{3,2},{4,5},{5,4},{6,7},{7,6},{8,9},{9,8},{10,11... | collective-permute-start | bytes 2359304 | tf_op jit(solution)/shard_map/ppermute | solution.py:607
  159.1 18.8 %collective-permute-start.46 = (bf16[48,3072]{1,0:T(8,128)(2,1)S(1)}, bf16[48,3072]{1,0:T(8,128)(2,1)S(1)}, u32[]{:S(2)}, u32[]{:S(2)}) collective-permute-start(bf16[48,3072]{1,0:T(8,128)(2,1)S(1)} %fusion.10), channel_id=1, source_target_pairs={{0,8},{2,10},{8,16},{10,18},{16,24},{18,26},{24,28},{26,30},{28,20... | collective-permute-start | bytes 884744 | tf_op jit(solution)/shard_map/ppermute | solution.py:534
  177.5 18.4 %collective-permute-start.49 = (bf16[48,3072]{1,0:T(8,128)(2,1)S(1)}, bf16[48,3072]{1,0:T(8,128)(2,1)S(1)}, u32[]{:S(2)}, u32[]{:S(2)}) collective-permute-start(bf16[48,3072]{1,0:T(8,128)(2,1)S(1)} %get-tuple-element.64), channel_id=1, source_target_pairs={{0,4},{2,6},{8,0},{10,2},{16,8},{18,10},{24,16},{26,18},{28,24},{3... | collective-permute-start | bytes 884744 | tf_op jit(solution)/shard_map/ppermute | solution.py:532
  178.1 17.8 %collective-permute-start.47 = (bf16[48,3072]{1,0:T(8,128)(2,1)S(1)}, bf16[48,3072]{1,0:T(8,128)(2,1)S(1)}, u32[]{:S(2)}, u32[]{:S(2)}) collective-permute-start(bf16[48,3072]{1,0:T(8,128)(2,1)S(1)} %fusion.11), channel_id=1, source_target_pairs={{0,8},{2,10},{8,16},{10,18},{16,24},{18,26},{24,28},{26,30},{28,20... | collective-permute-start | bytes 884744 | tf_op jit(solution)/shard_map/ppermute | solution.py:534
  194.2 10.0 %collective-permute-start.37 = (bf16[288,512]{1,0:T(8,128)(2,1)S(1)}, bf16[288,512]{1,0:T(8,128)(2,1)S(1)}, u32[]{:S(2)}, u32[]{:S(2)}) collective-permute-start(bf16[288,512]{1,0:T(8,128)(2,1)S(1)} %get-tuple-element.67), channel_id=1, source_target_pairs={{0,8},{2,10},{8,16},{10,18},{16,24},{18,26},{24,28},{26,30},{28,20... | collective-permute-start | bytes 884744 | tf_op jit(solution)/shard_map/ppermute | solution.py:531
  196.1 10.8 %collective-permute-start.50 = (bf16[48,3072]{1,0:T(8,128)(2,1)S(1)}, bf16[48,3072]{1,0:T(8,128)(2,1)S(1)}, u32[]{:S(2)}, u32[]{:S(2)}) collective-permute-start(bf16[48,3072]{1,0:T(8,128)(2,1)S(1)} %get-tuple-element.62), channel_id=1, source_target_pairs={{0,4},{2,6},{8,0},{10,2},{16,8},{18,10},{24,16},{26,18},{28,24},{3... | collective-permute-start | bytes 884744 | tf_op jit(solution)/shard_map/ppermute | solution.py:536
  196.6 22.8 %collective-permute-start.41 = (bf16[288,512]{1,0:T(8,128)(2,1)S(1)}, bf16[288,512]{1,0:T(8,128)(2,1)S(1)}, u32[]{:S(2)}, u32[]{:S(2)}) collective-permute-start(bf16[288,512]{1,0:T(8,128)(2,1)S(1)} %get-tuple-element.68), channel_id=1, source_target_pairs={{0,4},{2,6},{8,0},{10,2},{16,8},{18,10},{24,16},{26,18},{28,24},{3... | collective-permute-start | bytes 884744 | tf_op jit(solution)/shard_map/ppermute | solution.py:532
  197.0 20.9 %copy-start.6 = (f32[512,768]{1,0:T(8,128)S(1)}, f32[512,768]{1,0:T(8,128)}, u32[]{:S(2)}) copy-start(f32[512,768]{1,0:T(8,128)} %get-tuple-element.44) | copy-start | bytes 4718596
  197.0 28.5 %collective-permute-start.48 = (bf16[48,3072]{1,0:T(8,128)(2,1)S(1)}, bf16[48,3072]{1,0:T(8,128)(2,1)S(1)}, u32[]{:S(2)}, u32[]{:S(2)}) collective-permute-start(bf16[48,3072]{1,0:T(8,128)(2,1)S(1)} %get-tuple-element.61), channel_id=1, source_target_pairs={{0,8},{2,10},{8,16},{10,18},{16,24},{18,26},{24,28},{26,30},{28,20... | collective-permute-start | bytes 884744 | tf_op jit(solution)/shard_map/ppermute | solution.py:534
  205.3 9.9 %collective-permute-start.38 = (bf16[288,512]{1,0:T(8,128)(2,1)S(1)}, bf16[288,512]{1,0:T(8,128)(2,1)S(1)}, u32[]{:S(2)}, u32[]{:S(2)}) collective-permute-start(bf16[288,512]{1,0:T(8,128)(2,1)S(1)} %fusion.16), channel_id=1, source_target_pairs={{0,8},{2,10},{8,16},{10,18},{16,24},{18,26},{24,28},{26,30},{28,20... | collective-permute-start | bytes 884744 | tf_op jit(solution)/shard_map/ppermute | solution.py:534
  207.0 18.5 %collective-permute-start.51 = (bf16[48,3072]{1,0:T(8,128)(2,1)S(1)}, bf16[48,3072]{1,0:T(8,128)(2,1)S(1)}, u32[]{:S(2)}, u32[]{:S(2)}) collective-permute-start(bf16[48,3072]{1,0:T(8,128)(2,1)S(1)} %fusion.9), channel_id=1, source_target_pairs={{0,4},{2,6},{8,0},{10,2},{16,8},{18,10},{24,16},{26,18},{28,24},{3... | collective-permute-start | bytes 884744 | tf_op jit(solution)/shard_map/ppermute | solution.py:536
  216.3 7.4 %collective-permute-start.39 = (bf16[288,512]{1,0:T(8,128)(2,1)S(1)}, bf16[288,512]{1,0:T(8,128)(2,1)S(1)}, u32[]{:S(2)}, u32[]{:S(2)}) collective-permute-start(bf16[288,512]{1,0:T(8,128)(2,1)S(1)} %fusion.17), channel_id=1, source_target_pairs={{0,8},{2,10},{8,16},{10,18},{16,24},{18,26},{24,28},{26,30},{28,20... | collective-permute-start | bytes 884744 | tf_op jit(solution)/shard_map/ppermute | solution.py:534
  225.0 6.8 %collective-permute-start.42 = (bf16[288,512]{1,0:T(8,128)(2,1)S(1)}, bf16[288,512]{1,0:T(8,128)(2,1)S(1)}, u32[]{:S(2)}, u32[]{:S(2)}) collective-permute-start(bf16[288,512]{1,0:T(8,128)(2,1)S(1)} %get-tuple-element.66), channel_id=1, source_target_pairs={{0,4},{2,6},{8,0},{10,2},{16,8},{18,10},{24,16},{26,18},{28,24},{3... | collective-permute-start | bytes 884744 | tf_op jit(solution)/shard_map/ppermute | solution.py:536
  225.7 8.6 %collective-permute-start.40 = (bf16[288,512]{1,0:T(8,128)(2,1)S(1)}, bf16[288,512]{1,0:T(8,128)(2,1)S(1)}, u32[]{:S(2)}, u32[]{:S(2)}) collective-permute-start(bf16[288,512]{1,0:T(8,128)(2,1)S(1)} %get-tuple-element.65), channel_id=1, source_target_pairs={{0,8},{2,10},{8,16},{10,18},{16,24},{18,26},{24,28},{26,30},{28,20... | collective-permute-start | bytes 884744 | tf_op jit(solution)/shard_map/ppermute | solution.py:534
  232.9 6.8 %collective-permute-start.43 = (bf16[288,512]{1,0:T(8,128)(2,1)S(1)}, bf16[288,512]{1,0:T(8,128)(2,1)S(1)}, u32[]{:S(2)}, u32[]{:S(2)}) collective-permute-start(bf16[288,512]{1,0:T(8,128)(2,1)S(1)} %fusion.15), channel_id=1, source_target_pairs={{0,4},{2,6},{8,0},{10,2},{16,8},{18,10},{24,16},{26,18},{28,24},{3... | collective-permute-start | bytes 884744 | tf_op jit(solution)/shard_map/ppermute | solution.py:536
  (27 other events, 223.1 us)

commit v2 on v1

v2 whole, which is shorter than its diff:
```python
import jax
import jax.numpy as jnp
from jax import lax
from jax.experimental import pallas as pl
from jax.experimental.pallas import tpu as pltpu
from jax.sharding import PartitionSpec as P

EPSILON = 1e-06
NEGATIVE = -1e30
BF = jnp.bfloat16
F32 = jnp.float32
UNITS = 16
LANES = 128
PARTS = 2
RING_CHIPS = 8
VMEM_BYTES = 20 * 1024 * 1024
NT = (((1,), (1,)), ((), ()))
TN = (((0,), (0,)), ((), ()))
NN = (((1,), (0,)), ((), ()))


def mm(a, b, dims=NN):
    return lax.dot_general(a, b, dims, preferred_element_type=F32)


def run(kernel, name, scalars, arrays, outs, scratch=(), loose=(), loose_outs=(), micros=0):
    held = [pltpu.with_memory_space_constraint(one, pltpu.VMEM) for one in arrays]
    results = [pltpu.VMEM(*one) for one in outs] + [jax.ShapeDtypeStruct(*one) for one in loose_outs]
    specs = [pl.BlockSpec(memory_space=pltpu.SMEM)] * len(scalars)
    specs += [pl.BlockSpec(memory_space=pltpu.VMEM)] * len(arrays)
    specs += [pl.BlockSpec(memory_space=pltpu.HBM)] * len(loose)
    loose = [pltpu.with_memory_space_constraint(one, pltpu.HBM) for one in loose]
    out_specs = [pl.BlockSpec(memory_space=pltpu.VMEM)] * len(outs)
    out_specs += [pl.BlockSpec(memory_space=pl.ANY)] * len(loose_outs)
    return pl.pallas_call(
        kernel,
        out_shape=tuple(results),
        in_specs=specs,
        out_specs=tuple(out_specs),
        scratch_shapes=list(scratch),
        compiler_params=pltpu.CompilerParams(vmem_limit_bytes=VMEM_BYTES),
        cost_estimate=pl.CostEstimate(flops=1 + micros * 1_000_000_000, bytes_accessed=1, transcendentals=0),
        name=name,
    )(*scalars, *held, *loose)


def gelu_pair(x):
    c = 0.7978845608028654
    a = 0.044715
    square = x * x
    t = jnp.tanh(c * x * (1.0 + a * square))
    half = 0.5 * (1.0 + t)
    return x * half, half + 0.5 * x * (1.0 - t * t) * (c * (1.0 + 3.0 * a * square))


def multiple(value, of):
    return pl.multiple_of(value, of)


def fetch(refs, held, sem):
    copies = [pltpu.make_async_copy(ref, to, sem.at[n]) for n, (ref, to) in enumerate(zip(refs, held))]
    for copy in copies:
        copy.start()
    for copy in copies:
        copy.wait()


def pack_first(scores, wv, gain_one, gain_two, wo):
    heads, rows, length = scores.shape
    krows, width = wv.shape
    inputs = (scores, wv, gain_one.reshape(1, -1), gain_two.reshape(1, -1), wo)

    def kernel(*refs):
        out, wo_out, scr = refs[5:8]
        s_ref, wv_ref, ga_ref, gf_ref, wo_ref = refs[8:13]
        fetch(refs[:5], refs[8:13], refs[13])
        out[: heads * rows, :] = s_ref[...].reshape(heads * rows, length).astype(BF)
        out[heads * rows :, :width] = wv_ref[...].astype(BF)
        scr[...] = jnp.zeros_like(scr)
        scr[0:1, :krows] = ga_ref[...]
        scr[1:2, :krows] = gf_ref[...]
        out[heads * rows :, width:] = scr[...].astype(BF)
        wo_out[...] = wo_ref[...].astype(BF)

    return run(
        kernel,
        "pack_first",
        (),
        (),
        (((heads * rows + krows, length), BF), ((krows, width), BF)),
        (
            pltpu.VMEM((krows, length - width), F32),
            *[pltpu.VMEM(one.shape, one.dtype) for one in inputs],
            pltpu.SemaphoreType.DMA((5,)),
        ),
        loose=inputs,
    )


def pack_up(second, w_up, wo_own, wo_other):
    krows, hidden = w_up.shape
    half = wo_own.shape[1]

    def kernel(second_ref, own_ref, other_ref, up_ref, out, held, sem):
        fetch([up_ref], [held], sem)
        first = second_ref[0]
        out[:, :hidden] = held[...].astype(BF)
        out[:, pl.ds(multiple(hidden + first * half, LANES), half)] = own_ref[...]
        out[:, pl.ds(multiple(hidden + (1 - first) * half, LANES), half)] = other_ref[...]

    return run(
        kernel,
        "pack_up",
        (second,),
        (wo_own, wo_other),
        (((krows, hidden + 2 * half), BF),),
        (pltpu.VMEM(w_up.shape, F32), pltpu.SemaphoreType.DMA((1,))),
        loose=(w_up,),
    )[0]


def pack_down(w_down):
    krows, hidden = w_down.shape

    def kernel(down_ref, out, held, sem):
        fetch([down_ref], [held], sem)
        out[...] = held[...].astype(BF)

    return run(
        kernel,
        "pack_down",
        (),
        (),
        (((krows, hidden), BF),),
        (pltpu.VMEM(w_down.shape, F32), pltpu.SemaphoreType.DMA((1,))),
        loose=(w_down,),
    )[0]


def bring(units, where_ref, to, sem):
    rows = to.shape[0] // UNITS
    copies = []
    for u in range(UNITS):
        at = pl.ds(multiple(where_ref[u] * rows, 16), rows)
        copies.append(pltpu.make_async_copy(units[u], to.at[at, :], sem.at[u]))
        copies[-1].start()
    return copies


def mixer_forward(where, tokens, segments, units, heads, width):
    length, model = tokens.shape
    size = width // heads
    rows = length // UNITS
    krows = model // UNITS
    wide = heads * LANES

    deep = heads * rows + krows

    def kernel(where_ref, tok_ref, seg_ref, *rest):
        e_ref, va_ref, mixed_ref, mixf_ref, rb_ref, n1_ref, gains_ref, wv_ref, pieces, unit, same, sem = rest[UNITS:]
        copies = [
            pltpu.make_async_copy(rest[u], unit.at[where_ref[u]], sem.at[u]) for u in range(UNITS)
        ]
        for copy in copies:
            copy.start()
        documents = (seg_ref[...] == lax.broadcasted_iota(jnp.int32, (LANES, length), 0)).astype(BF)
        same[...] = mm(documents, documents, TN)
        for copy in copies:
            copy.wait()
        for d in range(UNITS):
            wv_ref[d * krows : (d + 1) * krows, :] = unit[d, heads * rows :, :width]
            some = unit[d, heads * rows : heads * rows + 16, width:].astype(F32)
            pieces[0, d : d + 1, :] = some[0:1, :]
            pieces[1, d : d + 1, :] = some[1:2, :]
        spread = (
            lax.broadcasted_iota(jnp.int32, (LANES, model), 1) % krows
            == lax.broadcasted_iota(jnp.int32, (LANES, model), 0)
        ).astype(BF)
        own = (
            lax.broadcasted_iota(jnp.int32, (UNITS, model), 1) // krows
            == lax.broadcasted_iota(jnp.int32, (UNITS, model), 0)
        )
        gains = []
        for t in range(2):
            full = jnp.where(own, mm(pieces[t].astype(BF), spread), 0.0)
            gains.append(jnp.sum(full, axis=0, keepdims=True))
            gains_ref[t : t + 1, :] = gains[t]
        x = tok_ref[...].astype(F32)
        inv = lax.rsqrt(jnp.mean(x * x, axis=-1, keepdims=True) + EPSILON)
        n1_ref[...] = (x * inv * gains[0]).astype(BF)
        values = mm(n1_ref[...], wv_ref[...]).astype(BF)
        tail = (lax.broadcasted_iota(jnp.int32, (length, LANES - size), 1) < 2).astype(BF)
        for h in range(heads):
            va_ref[:, h * LANES : h * LANES + size] = values[:, h * size : (h + 1) * size]
            va_ref[:, h * LANES + size : (h + 1) * LANES] = tail

        def one_head(h, carry):
            for d in range(UNITS):
                at = slice(d * rows, (d + 1) * rows)
                s = unit[d, pl.ds(multiple(h * rows, rows), rows), :].astype(F32)
                e_ref[h, at, :] = (jnp.exp(s) * same[at, :]).astype(BF)
            return carry

        lax.fori_loop(0, heads, one_head, 0)
        for h in range(heads):
            lanes = slice(h * LANES, (h + 1) * LANES)
            sums = mm(e_ref[h], va_ref[:, lanes])
            inverse = 1.0 / sums[:, size : size + 1]
            mixed = sums * inverse
            rb_ref[:, lanes] = jnp.broadcast_to(inverse, (length, LANES))
            mixf_ref[:, lanes] = jnp.where(
                lax.broadcasted_iota(jnp.int32, (length, LANES), 1) < size, mixed, 0.0
            )
            mixed_ref[:, h * size : (h + 1) * size] = mixed[:, :size].astype(BF)

    return run(
        kernel,
        "mixer_forward",
        (where,),
        (tokens, segments),
        (
            ((heads, length, length), BF),
            ((length, wide), BF),
            ((length, width), BF),
            ((length, wide), F32),
            ((length, wide), F32),
            ((length, model), BF),
            ((2, model), F32),
            ((model, width), BF),
        ),
        (
            pltpu.VMEM((2, UNITS, LANES), F32),
            pltpu.VMEM((UNITS, deep, length), BF),
            pltpu.VMEM((length, length), F32),
            pltpu.SemaphoreType.DMA((UNITS,)),
        ),
        loose=units,
        micros=6,
    )


def down_weights(where, cotangent, downs):
    length, model = cotangent.shape
    hidden = downs[0].shape[1]
    piece = hidden // 3

    def kernel(where_ref, cot_ref, *rest):
        out, gact, sem = rest[UNITS:]
        for copy in bring(rest[:UNITS], where_ref, out, sem):
            copy.wait()
        for j in range(3):
            cols = slice(j * piece, (j + 1) * piece)
            gact[:, cols] = mm(cot_ref[...], out[:, cols])

    return run(
        kernel,
        "down_weights",
        (where,),
        (cotangent,),
        (((model, hidden), BF), ((length, hidden), F32)),
        (pltpu.SemaphoreType.DMA((UNITS,)),),
        loose=downs,
        micros=4,
    )


def up_weights(where, ups):
    krows, columns = ups[0].shape

    def kernel(where_ref, *rest):
        out, sem = rest[UNITS:]
        for copy in bring(rest[:UNITS], where_ref, out, sem):
            copy.wait()

    return run(
        kernel,
        "up_weights",
        (where,),
        (),
        (((krows * UNITS, columns), BF),),
        (pltpu.SemaphoreType.DMA((UNITS,)),),
        loose=ups,
    )[0]


def ffn_main(second, tokens, mixed_own, mixed_other, gact, gains, w, part, parts):
    length, model = tokens.shape
    width = mixed_own.shape[1]
    hidden = gact.shape[1]
    chunk = length // parts
    piece = hidden // 3
    half = chunk // 2
    at = slice(part * chunk, (part + 1) * chunk)

    def kernel(second_ref, tok_ref, own_ref, other_ref, gact_ref, gains_ref, w_ref,
               back_one, back_two, resid_ref, n2_ref, act_ref, gpre_ref, mixed, acc):
        first = second_ref[0]
        mixed[:, pl.ds(multiple(first * width, LANES), width)] = own_ref[at, :]
        mixed[:, pl.ds(multiple((1 - first) * width, LANES), width)] = other_ref[at, :]
        attn = mm(mixed[...], w_ref[:, hidden:], NT)
        resid = tok_ref[at, :].astype(F32) + attn
        resid_ref[...] = resid
        inv = lax.rsqrt(jnp.mean(resid * resid, axis=-1, keepdims=True) + EPSILON)
        n2_ref[...] = (resid * inv * gains_ref[1:2, :]).astype(BF)
        for j in range(hidden // piece):
            cols = slice(j * piece, (j + 1) * piece)
            act, slope = gelu_pair(mm(n2_ref[...], w_ref[:, cols]))
            act_ref[:, cols] = act.astype(BF)
            gpre_ref[:, cols] = (gact_ref[at, cols] * slope).astype(BF)
            term = mm(gpre_ref[:, cols], w_ref[:, cols], NT)
            if j == 0:
                acc[...] = term
            else:
                acc[...] += term
        back_one[...] = acc[:half, :].astype(BF)
        back_two[...] = acc[half:, :].astype(BF)

    return run(
        kernel,
        "ffn_main",
        (second,),
        (tokens, mixed_own, mixed_other, gact, gains, w),
        (
            ((half, model), BF),
            ((half, model), BF),
            ((chunk, model), F32),
            ((chunk, model), BF),
            ((chunk, hidden), BF),
            ((chunk, hidden), BF),
        ),
        (
            pltpu.VMEM((chunk, 2 * width), BF),
            pltpu.VMEM((chunk, model), F32),
        ),
    )


def slots(keep, first, rest):
    half = UNITS // 2
    far = half // 2
    late = [k for k in range(half) if k not in (far, far + 1)]

    def slot(u):
        if u < half:
            return keep, u
        k = u - half
        return (rest, late.index(k)) if k in late else (first, k - far)

    return slot


def slot_shapes(rows, columns):
    half = UNITS // 2
    return tuple(((count, rows, columns), BF) for count in (half, 2, half - 2))


def ffn_grads(where, n2s, gpres, acts, cotangent):
    parts = len(n2s)
    chunk, model = n2s[0].shape
    hidden = acts[0].shape[1]
    krows = model // UNITS

    def kernel(where_ref, cot_ref, *rest):
        n2, gpre, act = rest[:parts], rest[parts : 2 * parts], rest[2 * parts : 3 * parts]
        slot = slots(*rest[3 * parts : 3 * parts + 3])
        scr, sem = rest[3 * parts + 3 :]
        piece = hidden // 3
        for j in range(3):
            cols = slice(j * piece, (j + 1) * piece)
            down = slice(hidden + j * piece, hidden + (j + 1) * piece)
            one = [mm(n2[r][...], gpre[r][:, cols], TN) for r in range(parts)]
            scr[:, cols] = sum(one).astype(BF)
            two = [mm(cot_ref[r * chunk : (r + 1) * chunk, :], act[r][:, cols], TN) for r in range(parts)]
            scr[:, down] = sum(two).astype(BF)
        copies = []
        for u in range(UNITS):
            at = pl.ds(multiple(where_ref[u] * krows, 16), krows)
            ref, k = slot(u)
            copies.append(pltpu.make_async_copy(scr.at[at, :], ref.at[k], sem.at[u]))
            copies[-1].start()
        for copy in copies:
            copy.wait()

    return run(
        kernel,
        "ffn_grads",
        (where,),
        (cotangent, *n2s, *gpres, *acts),
        (),
        (pltpu.VMEM((model, 2 * hidden), BF), pltpu.SemaphoreType.DMA((UNITS,))),
        loose_outs=slot_shapes(krows, 2 * hidden),
    )


def ffn_out(acts, wd):
    chunk, hidden = acts[0].shape
    model = wd.shape[0]

    def kernel(*refs):
        w_ref, out = refs[-2:]
        for r, act in enumerate(refs[:-2]):
            out[r * chunk : (r + 1) * chunk, :] = mm(act[...], w_ref[...], NT).astype(BF)

    return run(kernel, "ffn_out", (), (*acts, wd), (((chunk * len(acts), model), BF),))[0]


def cut_gain(row, krows):
    model = row.shape[1]
    take = (
        lax.broadcasted_iota(jnp.int32, (model, LANES), 0) % krows
        == lax.broadcasted_iota(jnp.int32, (model, LANES), 1)
    ).astype(BF)
    own = (
        lax.broadcasted_iota(jnp.int32, (UNITS, model), 1) // krows
        == lax.broadcasted_iota(jnp.int32, (UNITS, model), 0)
    )
    high = row.astype(BF).astype(F32)
    pieces = mm(jnp.where(own, high, 0.0).astype(BF), take)
    return pieces + mm(jnp.where(own, row - high, 0.0).astype(BF), take)


def resid_back(second, backs, others, resids, cotangent, gains, w, mixf, heads, size):
    length, model = cotangent.shape
    wide = heads * LANES
    count = len(backs)
    chunk = length // count
    krows = model // UNITS
    parts = len(resids)

    hidden = w.shape[1] - 2 * heads * size

    def kernel(second_ref, cot_ref, gains_ref, w_ref, mixf_ref, *rest):
        mine, other, res_refs = rest[:count], rest[count : 2 * count], rest[2 * count : 2 * count + parts]
        gres_ref, gat_ref, xh_ref, gf_ref, gm = rest[2 * count + parts :]
        total = jnp.zeros((8, model), F32)
        for r in range(count):
            at = slice(r * chunk, (r + 1) * chunk)
            g2 = mine[r][...].astype(F32) + other[r][...].astype(F32)
            per = count // parts
            res = res_refs[r // per][(r % per) * chunk : (r % per + 1) * chunk, :]
            inv = lax.rsqrt(jnp.mean(res * res, axis=-1, keepdims=True) + EPSILON)
            hat = res * inv
            total = total + jnp.sum((g2 * hat).reshape(chunk // 8, 8, model), axis=0)
            z = gains_ref[1:2, :] * g2
            corr = jnp.mean(z * hat, axis=-1, keepdims=True)
            gres = cot_ref[at, :].astype(F32) + inv * (z - hat * corr)
            gres_ref[at, :] = gres
            gat_ref[at, :] = gres.astype(BF)
        own = pl.ds(multiple(hidden + second_ref[0] * heads * size, LANES), heads * size)
        compact = mm(gat_ref[...], w_ref[:, own]).astype(BF)
        gm[...] = jnp.zeros_like(gm)
        for h in range(heads):
            gm[:, h * LANES : h * LANES + size] = compact[:, h * size : (h + 1) * size]
        lane = lax.broadcasted_iota(jnp.int32, (length, LANES), 1)
        for h in range(heads):
            lanes = slice(h * LANES, (h + 1) * LANES)
            here = gm[:, lanes].astype(F32)
            inner = -jnp.sum(here * mixf_ref[:, lanes], axis=-1, keepdims=True)
            high = inner.astype(BF).astype(F32)
            xh_ref[:, lanes] = jnp.where(
                lane == size, high, jnp.where(lane == size + 1, inner - high, here)
            ).astype(BF)
        gf_ref[...] = cut_gain(jnp.sum(total, axis=0, keepdims=True), krows)

    return run(
        kernel,
        "resid_back",
        (second,),
        (cotangent, gains, w, mixf, *backs, *others, *resids),
        (
            ((length, model), F32),
            ((length, model), BF),
            ((length, wide), BF),
            ((UNITS, LANES), F32),
        ),
        (pltpu.VMEM((length, wide), BF),),
    )


def score_grads(where_ref, xh_ref, va_ref, e_ref, rb_ref, ds, slot, first, count, rows):
    length = ds.shape[0]

    def one_head(h, carry):
        lanes = pl.ds(multiple((first + h) * LANES, LANES), LANES)
        d = mm(xh_ref[:, lanes], va_ref[:, lanes], NT)
        for q in range(length // LANES):
            cols = slice(q * LANES, (q + 1) * LANES)
            ds[:, cols] = (e_ref[first + h, :, cols].astype(F32) * rb_ref[:, lanes] * d[:, cols]).astype(BF)
        for u in range(UNITS):
            ref, k = slot(u)
            at = pl.ds(multiple(where_ref[u] * rows, rows), rows)
            ref[k, pl.ds(multiple(h * rows, rows), rows), :] = ds[at, :]
        return carry

    lax.fori_loop(0, count, one_head, 0)


def value_back(xh, rb, e, wv, tokens, size):
    length, model = tokens.shape
    heads = e.shape[0]
    width = heads * size
    chunk = length // 4
    krows = model // UNITS

    def kernel(xh_ref, rb_ref, e_ref, wv_ref, tok_ref, gv_ref, part_ref, ga_ref, acc):
        acc[...] = jnp.zeros_like(acc)
        for h in range(heads):
            lanes = slice(h * LANES, (h + 1) * LANES)
            scaled = (xh_ref[:, lanes].astype(F32) * rb_ref[:, lanes]).astype(BF)
            gv_ref[:, h * size : (h + 1) * size] = mm(e_ref[h], scaled, TN)[:, :size].astype(BF)

        def some_back(r, carry):
            at = pl.ds(multiple(r * chunk, chunk), chunk)
            part = mm(gv_ref[at, :], wv_ref[...], NT)
            part_ref[at, :] = part.astype(BF)
            x = tok_ref[at, :].astype(F32)
            inv = lax.rsqrt(jnp.mean(x * x, axis=-1, keepdims=True) + EPSILON)
            acc[...] += jnp.sum((part * (x * inv)).reshape(chunk // 8, 8, model), axis=0)
            return carry

        lax.fori_loop(0, length // chunk, some_back, 0)
        ga_ref[...] = cut_gain(jnp.sum(acc[...], axis=0, keepdims=True), krows)

    return run(
        kernel,
        "value_back",
        (),
        (xh, rb, e, wv, tokens),
        (
            ((length, width), BF),
            ((length, model), BF),
            ((UNITS, LANES), F32),
        ),
        (pltpu.VMEM((8, model), F32),),
    )


def mixer_grads(where, xh, va, e, rb, n1, gv, gat, mixed, ga, ga_other, gf, first, count):
    length, model = n1.shape
    width = gv.shape[1]
    rows = length // UNITS
    krows = model // UNITS
    top = count * rows
    deep = top + 2 * krows

    def kernel(where_ref, xh_ref, va_ref, e_ref, rb_ref, n1_ref, gv_ref, gat_ref, mixed_ref, ga_ref, gb_ref, gf_ref,
               keep, give, later, ds, wide_v, wide_o, pieces):
        slot = slots(keep, give, later)
        score_grads(where_ref, xh_ref, va_ref, e_ref, rb_ref, ds, slot, first, count, rows)
        wide_v[...] = mm(n1_ref[...], gv_ref[...], TN).astype(BF)
        wide_o[...] = mm(gat_ref[...], mixed_ref[...], TN).astype(BF)
        pieces[0] = ga_ref[...] + gb_ref[...]
        pieces[1] = gf_ref[...]
        sub = lax.broadcasted_iota(jnp.int32, (krows, LANES), 0)
        for u in range(UNITS):
            ref, k = slot(u)
            d = where_ref[u]
            at = pl.ds(multiple(d * krows, 16), krows)
            ref[k, top : top + krows, :width] = wide_v[at, :]
            ref[k, top + krows :, :width] = wide_o[at, :]
            both = jnp.where(
                sub == 0, pieces[0, pl.ds(d, 1), :], jnp.where(sub == 1, pieces[1, pl.ds(d, 1), :], 0.0)
            )
            ref[k, top : top + krows, width:] = both.astype(BF)
            ref[k, top + krows :, width:] = jnp.zeros((krows, length - width), BF)

    return run(
        kernel,
        "mixer_grads",
        (where,),
        (xh, va, e, rb, n1, gv, gat, mixed, ga, ga_other, gf),
        slot_shapes(deep, length),
        (
            pltpu.VMEM((length, length), BF),
            pltpu.VMEM((model, width), BF),
            pltpu.VMEM((model, width), BF),
            pltpu.VMEM((2, UNITS, LANES), F32),
        ),
    )


class Ring:
    def __init__(self, size):
        self.size = size
        self.chips = size // 2
        n = self.chips
        self.order = list(range(0, n, 2)) + list(range(n - 1, 0, -2))
        me = lax.axis_index("dp")
        self.core = me % 2
        chip = me // 2
        self.at = jnp.where(chip % 2 == 0, chip // 2, n - 1 - chip // 2)
        self.up = self.pairs(1)
        self.down = self.pairs(-1)
        self.swap = [(d, d ^ 1) for d in range(size)]

    def pairs(self, step):
        n = self.chips
        return [
            (self.order[p] * 2 + c, self.order[(p + step) % n] * 2 + c) for p in range(n) for c in range(2)
        ]

    def device(self, offset, core):
        n = self.chips
        p = (self.at + jnp.asarray(offset, jnp.int32) + n) % n
        chip = jnp.where(p < (n + 1) // 2, 2 * p, 2 * (n - 1 - p) + 1)
        return chip * 2 + core

    def gathered(self):
        n = self.chips
        offsets = [0]
        for s in range(1, n // 2 + 1):
            offsets.append(-s)
            if s < n // 2:
                offsets.append(s)
        return jnp.concatenate([self.device(offsets, self.core), self.device(offsets, 1 - self.core)])

    def scattered(self):
        offsets = list(range(self.chips))
        return jnp.concatenate([self.device(offsets, self.core), self.device(offsets, 1 - self.core)])


class Gather:
    def __init__(self, ring, unit):
        self.ring = ring
        self.last = [unit, unit]
        self.hops = 0
        self.mine = []
        self.theirs = []
        self.here = [unit]

    def values(self):
        return self.last

    def take(self, values):
        self.last = list(values)

    def hop(self):
        ring = self.ring
        self.hops += 1
        up = lax.ppermute(self.last[0], "dp", ring.up)
        new = [up]
        if self.hops < ring.chips // 2:
            new.append(lax.ppermute(self.last[1], "dp", ring.down))
        self.last = [up, new[-1]]
        self.swap()
        self.here = new

    def swap(self):
        self.theirs += [lax.ppermute(one, "dp", self.ring.swap) for one in self.here]
        self.mine += self.here
        self.here = []

    def finish(self):
        self.swap()
        return self.mine + self.theirs


class Scatter:
    def __init__(self, ring, keep, give, later):
        self.ring = ring
        self.keep = keep
        self.early = lax.ppermute(give, "dp", ring.swap)
        self.later = later
        self.last = []
        self.hops = 0

    def values(self):
        return self.last if self.hops else [self.early]

    def take(self, values):
        if self.hops:
            self.last = list(values)
        else:
            self.early = values[0]

    def total(self, k, *more):
        far = self.ring.chips // 2
        got = self.early[k - far] if k in (far, far + 1) else self.later[k if k < far else k - 2]
        value = self.keep[k].astype(F32) + got.astype(F32)
        for one in more:
            value = value + one.astype(F32)
        return value

    def hop(self):
        ring = self.ring
        far = ring.chips // 2
        self.hops += 1
        if self.hops == 1:
            self.later = lax.ppermute(self.later, "dp", ring.swap)
        up = self.total(far + 1 - self.hops, *self.last[:1]).astype(BF)
        new = [lax.ppermute(up, "dp", ring.up)]
        if self.hops < far:
            down = self.total(far + self.hops, *self.last[1:]).astype(BF)
            new.append(lax.ppermute(down, "dp", ring.down))
        else:
            new.append(self.last[1])
        self.last = new

    def result(self):
        return self.total(0, *self.last)


def together(chains, *more):
    values = [one for chain in chains for one in chain.values()]
    tied = lax.optimization_barrier(tuple(values) + more)
    at = 0
    for chain in chains:
        count = len(chain.values())
        chain.take(tied[at : at + count])
        at += count
    return tied[at:]


def tie(value, *after):
    return lax.optimization_barrier((value,) + after)[0] if after else value


def shards(
    tokens,
    segment_ids,
    gain_attn,
    gain_ffn,
    random_scores,
    w_value,
    w_output,
    w_up,
    w_down,
    cotangent,
):
    devices = lax.axis_size("dp")
    second = lax.axis_index("mp")
    length = segment_ids.shape[1]
    heads = random_scores.shape[0]
    model = tokens.shape[1]
    width = w_value.shape[1]
    size = width // heads
    rows = length // UNITS
    krows = model // UNITS
    ring = devices == UNITS and devices // 2 <= RING_CHIPS
    flip = [(0, 1), (1, 0)]
    second_at = jnp.reshape(second, (1,)).astype(jnp.int32)

    if ring:
        net = Ring(devices)
        far = net.chips // 2
        where_in = net.gathered().astype(jnp.int32)
        where_out = net.scattered().astype(jnp.int32)
        first_unit, wo_own = pack_first(random_scores, w_value, gain_attn, gain_ffn, w_output.T)
        wo_other = lax.ppermute(wo_own, "mp", flip)
        one = Gather(net, first_unit)
        one.hop()
        where_in, where_out, wo_other, up_from = together([one], where_in, where_out, wo_other, w_down.T)
        two = Gather(net, pack_down(up_from))
        one.hop()
        two.hop()
        (up_from,) = together([one, two], w_up)
        three = Gather(net, pack_up(second_at, up_from, wo_own, wo_other))
        for chain in (one, two, three):
            chain.hop()
        together([one, two, three])
        for chain in (one, two, three):
            chain.hop()
        together([one, two, three])
        first = one.finish()
    else:
        where_in = jnp.arange(UNITS, dtype=jnp.int32)
        where_out = where_in

        def gather(one, axis=0):
            return lax.all_gather(one.astype(BF), "dp", axis=axis, tiled=True)

        wo_own = w_output.astype(BF)
        wo_other = lax.ppermute(wo_own, "mp", flip)
        wo_first = jnp.where(second == 0, wo_own, wo_other)
        wo_second = jnp.where(second == 0, wo_other, wo_own)
        scores = gather(random_scores, 1).reshape(heads, UNITS, rows, length).transpose(1, 0, 2, 3)
        value = gather(w_value).reshape(UNITS, krows, width)
        gains = jnp.stack([gather(gain_attn), gather(gain_ffn)]).reshape(2, UNITS, krows).transpose(1, 0, 2)
        gains = jnp.pad(gains, ((0, 0), (0, krows - 2), (0, length - width - krows)))
        low = jnp.concatenate([value, gains], axis=2)
        both = jnp.concatenate([scores.reshape(UNITS, heads * rows, length), low], axis=1)
        up = jnp.concatenate([gather(w_up), gather(wo_first.T), gather(wo_second.T)], axis=1)
        up = up.reshape(UNITS, krows, up.shape[1])
        down = gather(w_down.T).reshape(UNITS, krows, w_down.shape[0])
        first, ups, downs = [[stack[u] for u in range(UNITS)] for stack in (both, up, down)]

    e, va, mixed, mixf, rb, n1, gains, wv = mixer_forward(
        where_in, tokens, segment_ids, first, heads, width
    )
    mixed_other = lax.ppermute(mixed, "mp", flip)
    if ring:
        two.hop()
        three.hop()
        (mixed,) = together([two, three], mixed)
        three.hop()
        downs, ups = two.finish(), three.finish()
    wd, gact = down_weights(where_in, cotangent, downs)
    w = up_weights(where_in, ups)
    backs, others, resids, n2s, acts, gpres = [], [], [], [], [], []
    for part in range(PARTS):
        one, two, resid, n2, act, gpre = ffn_main(
            second_at, tokens, mixed, mixed_other, gact, gains, w, part, PARTS
        )
        for new in (one, two):
            behind = others[-2:-1] if len(others) > 1 else []
            backs.append(new)
            others.append(lax.ppermute(tie(new, *behind), "mp", flip))
        resids.append(resid)
        n2s.append(n2)
        acts.append(act)
        gpres.append(gpre)
    parts_two = ffn_grads(where_out, n2s, gpres, acts, cotangent)
    ffn = ffn_out(acts, wd)
    ffn_other = lax.ppermute(tie(ffn, others[-1]), "mp", flip)
    if ring:
        ffn_sum = Scatter(net, *parts_two)
        together([ffn_sum])
        ffn_sum.hop()
        cotangent, ffn, *others = together([ffn_sum], cotangent, ffn, *others)
        ffn_sum.hop()
    gres, gat, xh, gf = resid_back(
        second_at, backs, others, resids, cotangent, gains, w, mixf, heads, size
    )
    gv, part, ga = value_back(xh, rb, e, wv, tokens, size)
    ga_other = lax.ppermute(ga, "mp", flip)
    part_other = lax.ppermute(part, "mp", flip)
    if ring:
        together([ffn_sum])
        ffn_sum.hop()
    parts_one = mixer_grads(
        where_out, xh, va, e, rb, n1, gv, gat, mixed, ga, ga_other, gf, 0, heads
    )

    top = heads * rows
    if ring:
        score_sum = Scatter(net, *parts_one)
        together([ffn_sum, score_sum])
        ffn_sum.hop()
        score_sum.hop()
        together([ffn_sum, score_sum])
        score_sum.hop()
        two = ffn_sum.result()
        (ffn_other,) = together([score_sum], ffn_other)
        score_sum.hop()
        (part_other,) = together([score_sum], part_other)
        score_sum.hop()
        one = score_sum.result()
        out_up = two[:, : two.shape[1] // 2]
        out_down = two[:, two.shape[1] // 2 :].T
        out_scores = one[:top].reshape(heads, rows, length)
        out_value = one[top : top + krows, :width]
        out_output = one[top + krows :, :width].T
        out_gain_one = one[top, width : width + krows]
        out_gain_two = one[top + 1, width : width + krows]
    else:

        def scatter(one, axis=0):
            return lax.psum_scatter(one, "dp", scatter_dimension=axis, tiled=True)

        def whole(keep, early, late):
            far = UNITS // 4
            return jnp.concatenate([keep, late[:far], early, late[far:]]).astype(F32)

        two = whole(*parts_two).reshape(model, -1)
        one = whole(*parts_one)
        out_up = scatter(two[:, : two.shape[1] // 2])
        out_down = scatter(two[:, two.shape[1] // 2 :]).T
        scores = one[:, :top].reshape(UNITS, heads, rows, length).transpose(1, 0, 2, 3)
        out_scores = scatter(scores.reshape(heads, length, length), 1)
        out_value = scatter(one[:, top : top + krows, :width].reshape(model, width))
        out_output = scatter(one[:, top + krows :, :width].reshape(model, width)).T
        out_gain_one = scatter(one[:, top, width : width + krows].reshape(model))
        out_gain_two = scatter(one[:, top + 1, width : width + krows].reshape(model))
    resid = jnp.concatenate(resids)
    output = (resid + (ffn.astype(F32) + ffn_other.astype(F32))).astype(BF)
    grad_n1 = part.astype(F32) + part_other.astype(F32)
    x = tokens.astype(F32)
    inv = lax.rsqrt(jnp.mean(x * x, axis=-1, keepdims=True) + EPSILON)
    z = gains[0:1, :] * grad_n1
    hat = x * inv
    grad_tokens = (gres + inv * (z - hat * jnp.mean(z * hat, axis=-1, keepdims=True))).astype(BF)

    return (
        output,
        grad_tokens,
        out_gain_one,
        out_gain_two,
        out_scores,
        out_value,
        out_output,
        out_up,
        out_down,
    )


def solution(mesh):
    in_specs = (
        P("dp", None),
        P("dp", None),
        P("dp"),
        P("dp"),
        P("mp", "dp", None),
        P("dp", "mp"),
        P("mp", "dp"),
        P("dp", "mp"),
        P("mp", "dp"),
        P("dp", None),
    )
    out_specs = (
        P("dp", None),
        P("dp", None),
        P("dp"),
        P("dp"),
        P("mp", "dp", None),
        P("dp", "mp"),
        P("mp", "dp"),
        P("dp", "mp"),
        P("mp", "dp"),
    )
    return jax.shard_map(shards, mesh=mesh, in_specs=in_specs, out_specs=out_specs, check_vma=False)
```

time: 243 us -> 197 us (0.81)
  waiting for transfers between devices: 117 us -> 90 us
  Pallas kernels: 58.8 us -> 37.3 us
  starting transfers between devices: 41 us -> 57.1 us
  other arithmetic: 15.3 us -> 5.95 us
  local copies, waits for them, and re-layouts: 9.43 us -> 4.69 us
    pallas_call x8 -> x13, Pallas kernels: 58.8 us -> 37.3 us  [run(): pl.pallas_call(kernel, out_shape=tuple(results), in_specs=specs, out_spec...]
    ppermute x48 -> x68, waiting for transfers between devices: 94.9 us -> 77.2 us  [the longest x12 27.3 us: hop(): up = lax.ppermute(self.last[0], 'dp', ring.up)]
    ppermute x48 -> x68, starting transfers between devices: 35.6 us -> 50.5 us  [the longest x12 18.4 us: hop(): up = lax.ppermute(self.last[0], 'dp', ring.up)]
    convert_element_type x10 -> x8, other arithmetic: 8.08 us -> 1.43 us  [the longest x6 1.21 us: hop(): down = self.total(far + self.hops, *self.last[1:]).astype(BF)]
    ppermute x1, waiting for transfers between devices: 6.29 us -> 0.01 us  [shards(): mixed_other = lax.ppermute(mixed, 'mp', flip)]
    unnamed x80 -> x102, local copies, waits for them, and re-layouts: 5.75 us -> 1.87 us
    ppermute x1, waiting for transfers between devices: 12.8 us -> 9.56 us  [shards(): part_other = lax.ppermute(part, 'mp', flip)]
  transfers between devices with their start and end apart: 52 -> 72, of which waited for: 20 -> 27; matrix products, arithmetic and copies ran while one was open for 7% -> 3% of each run, Pallas kernels for 16% -> 12%
where the time goes in v2:
time: 197 us
  waiting for transfers between devices  90 us (46%)
  starting transfers between devices  57.1 us (29%)
  Pallas kernels  37.3 us (19%)
  other arithmetic  5.95 us (3%)
  local copies, waits for them, and re-layouts  4.69 us (2%)
    pallas_call x13, Pallas kernels, run(): pl.pallas_call(kernel, out_shape=tuple(results), in_specs=specs, out_spec...  37.3 us
    ppermute x12, waiting for transfers between devices, hop(): up = lax.ppermute(self.last[0], 'dp', ring.up)  27.3 us
    ppermute x8, waiting for transfers between devices, hop(): new = [lax.ppermute(up, 'dp', ring.up)]  19.1 us
    ppermute x12, starting transfers between devices, hop(): up = lax.ppermute(self.last[0], 'dp', ring.up)  18.4 us
    ppermute x9, waiting for transfers between devices, hop(): new.append(lax.ppermute(self.last[1], 'dp', ring.down))  11 us
    ppermute x1, waiting for transfers between devices, shards(): part_other = lax.ppermute(part, 'mp', flip)  9.56 us
    ppermute x4, waiting for transfers between devices, shards(): others.append(lax.ppermute(tie(new, *behind), 'mp', flip))  9.09 us
    ppermute x8, starting transfers between devices, hop(): new = [lax.ppermute(up, 'dp', ring.up)]  7.86 us
  transfers between devices with their start and end apart: 72, of which 27 were waited for; matrix products, arithmetic and copies ran while one was open for 3% of the time, Pallas kernels for 12%

profile of v2, /device:TPU:0, one launch (start us, length us, event | category | flops | bytes accessed | tf_op | source)
XLA Modules:
  0.0 196.5 jit_solution(5749593276987771720)
XLA Ops:
  0.7 1.2 pack_first.1
  1.9 3.1 %collective-permute-start = (bf16[240,512]{1,0:T(8,128)(2,1)S(1)}, bf16[240,512]{1,0:T(8,128)(2,1)S(1)}, u32[]{:S(2)}, u32[]{:S(2)}) collective-permute-start(bf16[240,512]{1,0:T(8,128)(2,1)S(1)} %get-tuple-element.93.rest_0_), channel_id=1, source_target_pairs={{0,8},{2,10},{8,16},{10,18},{16,24},{18,26},{24,28},{26,30},{28,20... | collective-permute-start | bytes 737288 | tf_op jit(solution)/shard_map/ppermute | solution.py:640
  5.0 2.0 %collective-permute-start.2 = (bf16[48,384]{1,0:T(8,128)(2,1)S(1)}, bf16[48,384]{1,0:T(8,128)(2,1)S(1)}, u32[]{:S(2)}, u32[]{:S(2)}) collective-permute-start(bf16[48,384]{1,0:T(8,128)(2,1)S(1)} %get-tuple-element.94.own_ref), channel_id=1, source_target_pairs={{0,1},{1,0},{2,3},{3,2},{4,5},{5,4},{6,7},{7,6},{8,9},{9,8},{10,11... | collective-permute-start | bytes 110600 | tf_op jit(solution)/shard_map/ppermute | solution.py:749
  8.9 1.9 collective-permute-done.rest_1_
  10.8 1.5 collective-permute-done.1.rest_2_
  12.4 1.6 collective-permute-start.3
  15.4 1.6 collective-permute-start.5
  17.5 4.6 %collective-permute-done.5.rest_1_ = bf16[48,1536]{1,0:T(8,128)(2,1)S(1)} collective-permute-done((bf16[48,1536]{1,0:T(8,128)(2,1)S(1)}, bf16[48,1536]{1,0:T(8,128)(2,1)S(1)}, u32[]{:S(2)}, u32[]{:S(2)}) %collective-permute-start.5) | collective-permute-done | bytes 147488 | tf_op jit(solution)/shard_map/ppermute | solution.py:640
  22.1 1.3 collective-permute-done.6.rest_2_
  23.4 1.2 pack_up.1.rest_0_
  24.6 1.6 collective-permute-start.11
  27.2 1.6 collective-permute-start.9
  28.8 1.6 collective-permute-start.7
  30.3 4.7 %collective-permute-done.10.rest_4_ = bf16[48,1536]{1,0:T(8,128)(2,1)S(1)} collective-permute-done((bf16[48,1536]{1,0:T(8,128)(2,1)S(1)}, bf16[48,1536]{1,0:T(8,128)(2,1)S(1)}, u32[]{:S(2)}, u32[]{:S(2)}) %collective-permute-start.10) | collective-permute-done | bytes 147488 | tf_op jit(solution)/shard_map/ppermute | solution.py:643
  36.1 1.8 collective-permute-done.7.rest_5_
  37.9 3.3 %collective-permute-done.8.rest_6_ = bf16[240,512]{1,0:T(8,128)(2,1)S(1)} collective-permute-done((bf16[240,512]{1,0:T(8,128)(2,1)S(1)}, bf16[240,512]{1,0:T(8,128)(2,1)S(1)}, u32[]{:S(2)}, u32[]{:S(2)}) %collective-permute-start.8) | collective-permute-done | bytes 245792 | tf_op jit(solution)/shard_map/ppermute | solution.py:643
  41.7 1.5 collective-permute-start.16
  43.9 1.4 collective-permute-start.15
  45.9 1.4 collective-permute-start.17
  47.3 5.9 %collective-permute-done.14.rest_5_ = bf16[48,1536]{1,0:T(8,128)(2,1)S(1)} collective-permute-done((bf16[48,1536]{1,0:T(8,128)(2,1)S(1)}, bf16[48,1536]{1,0:T(8,128)(2,1)S(1)}, u32[]{:S(2)}, u32[]{:S(2)}) %collective-permute-start.14) | collective-permute-done | bytes 147488 | tf_op jit(solution)/shard_map/ppermute | solution.py:640
  54.2 3.4 %collective-permute-done.13.rest_7_ = bf16[240,512]{1,0:T(8,128)(2,1)S(1)} collective-permute-done((bf16[240,512]{1,0:T(8,128)(2,1)S(1)}, bf16[240,512]{1,0:T(8,128)(2,1)S(1)}, u32[]{:S(2)}, u32[]{:S(2)}) %collective-permute-start.13) | collective-permute-done | bytes 245792 | tf_op jit(solution)/shard_map/ppermute | solution.py:640
  57.6 1.5 collective-permute-start.19
  59.7 1.5 collective-permute-start.18
  61.2 7.4 %collective-permute-done.18.rest_7_ = bf16[48,1536]{1,0:T(8,128)(2,1)S(1)} collective-permute-done((bf16[48,1536]{1,0:T(8,128)(2,1)S(1)}, bf16[48,1536]{1,0:T(8,128)(2,1)S(1)}, u32[]{:S(2)}, u32[]{:S(2)}) %collective-permute-start.18) | collective-permute-done | bytes 147488 | tf_op jit(solution)/shard_map/ppermute | solution.py:640
  69.9 6.0 %mixer_forward.1 = (bf16[6,512,512]{2,1,0:T(8,128)(2,1)S(1)}, bf16[512,768]{1,0:T(8,128)(2,1)S(1)}, bf16[512,384]{1,0:T(8,128)(2,1)S(1)}, f32[512,768]{1,0:T(8,1...) custom-call(s32[16]{0:T(128)S(1)} %pad_add_fusion.where_ref, ...), custom_call_target="tpu_custom_call" | custom-call | flops 6000000000 | bytes 1 | tf_op jit(solution)/shard_map/mixer_forward/pallas_call | solution.py:35
  76.6 1.5 collective-permute-start.38
  79.5 1.5 collective-permute-start.29
  81.8 2.4 %collective-permute-done.38.rest_7_ = bf16[48,2304]{1,0:T(8,128)(2,1)S(1)} collective-permute-done((bf16[48,2304]{1,0:T(8,128)(2,1)S(1)}, bf16[48,2304]{1,0:T(8,128)(2,1)S(1)}, u32[]{:S(2)}, u32[]{:S(2)}) %collective-permute-start.38) | collective-permute-done | bytes 221216 | tf_op jit(solution)/shard_map/ppermute | solution.py:640
  84.2 3.8 %down_weights.1 = (bf16[768,1536]{1,0:T(8,128)(2,1)S(1)}, f32[512,1536]{1,0:T(8,128)S(1)}) custom-call(s32[16]{0:T(128)S(1)} %pad_add_fusion.where_ref, bf16[512,768]{1,0:T(8,128)(2,1)S(1)} %copy-done.1, bf16[48,1536]{1,0:T(8,128)(2,1)} %copy-done.3, bf16[48,1536]{1,0:T(8,128)(2,1)} %copy-done.36, bf16[48,1536]{1,0:T(8,128)(2,1)} %copy-done.37, ...), custom_call_target="tpu_custom_call" | custom-call | flops 4000000000 | bytes 1 | tf_op jit(solution)/shard_map/down_weights/pallas_call | solution.py:35
  89.7 2.8 %up_weights.1.w_ref = bf16[768,2304]{1,0:T(8,128)(2,1)S(1)} custom-call(s32[16]{0:T(128)S(1)} %pad_add_fusion.where_ref, bf16[48,2304]{1,0:T(8,128)(2,1)} %copy-done.2, bf16[48,2304]{1,0:T(8,128)(2,1)} %copy-done.6, bf16[48,2304]{1,0:T(8,128)(2,1)} %copy-done.7, bf16[48,2304]{1,0:T(8,128)(2,1)} %copy-done.8, bf16[48,2304]{1,0:T(8,128)(2,1)} %copy-done.9, ...), custom_call_target="tpu_custom_call" | custom-call | flops 1 | bytes 1 | tf_op jit(solution)/shard_map/up_weights/pallas_call | solution.py:35
  92.4 3.1 %ffn_main.2 = (bf16[128,768]{1,0:T(8,128)(2,1)S(1)}, bf16[128,768]{1,0:T(8,128)(2,1)S(1)}, f32[256,768]{1,0:T(8,128)S(1)}, bf16[256,768]{1,0:T(8,128)(2,1)S(1)},...) custom-call(s32[1]{0:T(128)} %bitcast.second_ref, bf16[512,768]{1,0:T(8,128)(2,1)S(1)} %copy-done, ...), custom_call_target="tpu_custom_call" | custom-call | flops 1 | bytes 1 | tf_op jit(solution)/shard_map/ffn_main/pallas_call | solution.py:35
  95.5 3.1 %ffn_main.3 = (bf16[128,768]{1,0:T(8,128)(2,1)S(1)}, bf16[128,768]{1,0:T(8,128)(2,1)S(1)}, f32[256,768]{1,0:T(8,128)S(1)}, bf16[256,768]{1,0:T(8,128)(2,1)S(1)},...) custom-call(s32[1]{0:T(128)} %bitcast.second_ref, bf16[512,768]{1,0:T(8,128)(2,1)S(1)} %copy-done, ...), custom_call_target="tpu_custom_call" | custom-call | flops 1 | bytes 1 | tf_op jit(solution)/shard_map/ffn_main/pallas_call | solution.py:35
  98.6 4.4 %ffn_grads.1 = (bf16[8,48,3072]{2,1,0:T(8,128)(2,1)S(1)}, bf16[2,48,3072]{2,1,0:T(8,128)(2,1)S(1)}, bf16[6,48,3072]{2,1,0:T(8,128)(2,1)S(1)}) custom-call(s32[16]{0:T(128)S(1)} %pad_add_fusion.1.where_ref, bf16[512,768]{1,0:T(8,128)(2,1)S(1)} %copy-done.1, bf16[256,768]{1,0:T(8,128)(2,1)S(1)} %get-tuple-element.121.rest_0_, ...), custom_call_target="tpu_custom_call" | custom-call | flops 1 | bytes 1 | tf_op jit(solution)/shard_map/ffn_grads/pallas_call | solution.py:35
  103.6 1.5 collective-permute-start.51
  105.7 2.1 %collective-permute-done.47 = bf16[2,48,3072]{2,1,0:T(8,128)(2,1)S(1)} collective-permute-done((bf16[2,48,3072]{2,1,0:T(8,128)(2,1)S(1)}, bf16[2,48,3072]{2,1,0:T(8,128)(2,1)S(1)}, u32[]{:S(2)}, u32[]{:S(2)}) %collective-permute-start.47) | collective-permute-done | bytes 589856 | tf_op jit(solution)/shard_map/ppermute | solution.py:662
  107.9 1.6 collective-permute-start.48
  110.0 1.4 collective-permute-done.51.rest_5_
  111.3 1.5 collective-permute-start.53
  112.9 2.7 %collective-permute-done.50.rest_4_ = bf16[128,768]{1,0:T(8,128)(2,1)S(1)} collective-permute-done((bf16[128,768]{1,0:T(8,128)(2,1)S(1)}, bf16[128,768]{1,0:T(8,128)(2,1)S(1)}, u32[]{:S(2)}, u32[]{:S(2)}) %collective-permute-start.50) | collective-permute-done | bytes 196640 | tf_op jit(solution)/shard_map/ppermute | solution.py:807
  115.6 1.5 collective-permute-start.52
  117.1 1.4 ffn_out.1
  118.5 1.3 collective-permute-done.53.rest_7_
  119.8 3.8 %collective-permute-done.52.rest_6_ = bf16[128,768]{1,0:T(8,128)(2,1)S(1)} collective-permute-done((bf16[128,768]{1,0:T(8,128)(2,1)S(1)}, bf16[128,768]{1,0:T(8,128)(2,1)S(1)}, u32[]{:S(2)}, u32[]{:S(2)}) %collective-permute-start.52) | collective-permute-done | bytes 196640 | tf_op jit(solution)/shard_map/ppermute | solution.py:807
  123.8 1.5 collective-permute-start.57
  125.9 2.9 %resid_back.1 = (f32[512,768]{1,0:T(8,128)S(1)}, bf16[512,768]{1,0:T(8,128)(2,1)S(1)}, bf16[512,768]{1,0:T(8,128)(2,1)S(1)}, f32[16,128]{1,0:T(8,128)S(1)}) custom-call(s32[1]{0:T(128)} %bitcast.second_ref, bf16[512,768]{1,0:T(8,128)(2,1)S(1)} %copy-done.1, f32[2,768]{1,0:T(2,128)S(1)} %get-tuple-element.116.gains_ref, ...), custom_call_target="tpu_custom_call" | custom-call | flops 1 | bytes 1 | tf_op jit(solution)/shard_map/resid_back/pallas_call | solution.py:35
  128.8 2.8 %value_back.1 = (bf16[512,384]{1,0:T(8,128)(2,1)S(1)}, bf16[512,768]{1,0:T(8,128)(2,1)S(1)}, f32[16,128]{1,0:T(8,128)S(1)}) custom-call(bf16[512,768]{1,0:T(8,128)(2,1)S(1)} %get-tuple-element.143.xh_ref, f32[512,768]{1,0:T(8,128)S(1)} %get-tuple-element.146.rb_ref, bf16[6,512,512]{2,1,0:T(8,128)(2,1)S(1)} %get-tuple-element.145.e_ref, ...), custom_call_target="tpu_custom_call" | custom-call | flops 1 | bytes 1 | tf_op jit(solution)/shard_map/value_back/pallas_call | solution.py:35
  131.6 1.6 collective-permute-start.54
  133.1 2.1 %collective-permute-done.54.gb_ref = f32[16,128]{1,0:T(8,128)S(1)} collective-permute-done((f32[16,128]{1,0:T(8,128)S(1)}, f32[16,128]{1,0:T(8,128)S(1)}, u32[]{:S(2)}, u32[]{:S(2)}) %collective-permute-start.54) | collective-permute-done | bytes 8224 | tf_op jit(solution)/shard_map/ppermute | solution.py:825
  135.3 3.6 %mixer_grads.1 = (bf16[8,288,512]{2,1,0:T(8,128)(2,1)S(1)}, bf16[2,288,512]{2,1,0:T(8,128)(2,1)S(1)}, bf16[6,288,512]{2,1,0:T(8,128)(2,1)S(1)}) custom-call(s32[16]{0:T(128)S(1)} %pad_add_fusion.1.where_ref, bf16[512,768]{1,0:T(8,128)(2,1)S(1)} %get-tuple-element.143.xh_ref, bf16[512,768]{1,0:T(8,128)(2,1)S(1)} %get-tuple-element.144.va_ref, ...), custom_call_target="tpu_custom_call" | custom-call | flops 1 | bytes 1 | tf_op jit(solution)/shard_map/mixer_grads/pallas_call | solution.py:35
  139.7 1.5 collective-permute-start.59
  142.0 6.7 %collective-permute-done.59 = bf16[48,3072]{1,0:T(8,128)(2,1)S(1)} collective-permute-done((bf16[48,3072]{1,0:T(8,128)(2,1)S(1)}, bf16[48,3072]{1,0:T(8,128)(2,1)S(1)}, u32[]{:S(2)}, u32[]{:S(2)}) %collective-permute-start.59) | collective-permute-done | bytes 294944 | tf_op jit(solution)/shard_map/ppermute | solution.py:691
  148.8 1.2 collective-permute-done.60
  150.8 1.4 collective-permute-start.64
  153.1 1.6 collective-permute-start.67
  154.6 5.5 %collective-permute-done.63 = bf16[288,512]{1,0:T(8,128)(2,1)S(1)} collective-permute-done((bf16[288,512]{1,0:T(8,128)(2,1)S(1)}, bf16[288,512]{1,0:T(8,128)(2,1)S(1)}, u32[]{:S(2)}, u32[]{:S(2)}) %collective-permute-start.63) | collective-permute-done | bytes 294944 | tf_op jit(solution)/shard_map/ppermute | solution.py:691
  160.2 1.5 collective-permute-start.70
  161.7 2.7 %collective-permute-done.62 = bf16[48,3072]{1,0:T(8,128)(2,1)S(1)} collective-permute-done((bf16[48,3072]{1,0:T(8,128)(2,1)S(1)}, bf16[48,3072]{1,0:T(8,128)(2,1)S(1)}, u32[]{:S(2)}, u32[]{:S(2)}) %collective-permute-start.62) | collective-permute-done | bytes 294944 | tf_op jit(solution)/shard_map/ppermute | solution.py:691
  165.3 1.4 collective-permute-start.66
  166.8 6.8 %collective-permute-done.67 = bf16[512,768]{1,0:T(8,128)(2,1)S(1)} collective-permute-done((bf16[512,768]{1,0:T(8,128)(2,1)S(1)}, bf16[512,768]{1,0:T(8,128)(2,1)S(1)}, u32[]{:S(2)}, u32[]{:S(2)}) %collective-permute-start.67) | collective-permute-done | bytes 786464 | tf_op jit(solution)/shard_map/ppermute | solution.py:814
  174.4 1.6 collective-permute-start.69
  176.8 1.2 fusion.8
  177.9 9.6 %collective-permute-done.70 = bf16[512,768]{1,0:T(8,128)(2,1)S(1)} collective-permute-done((bf16[512,768]{1,0:T(8,128)(2,1)S(1)}, bf16[512,768]{1,0:T(8,128)(2,1)S(1)}, u32[]{:S(2)}, u32[]{:S(2)}) %collective-permute-start.70) | collective-permute-done | bytes 786464 | tf_op jit(solution)/shard_map/ppermute | solution.py:826
  188.8 1.5 fusion.6
  190.3 4.1 %collective-permute-done.71 = bf16[288,512]{1,0:T(8,128)(2,1)S(1)} collective-permute-done((bf16[288,512]{1,0:T(8,128)(2,1)S(1)}, bf16[288,512]{1,0:T(8,128)(2,1)S(1)}, u32[]{:S(2)}, u32[]{:S(2)}) %collective-permute-start.71) | collective-permute-done | bytes 294944 | tf_op jit(solution)/shard_map/ppermute | solution.py:691
  (221 shorter events, 26.5 us)
Async XLA Ops:
  1.9 8.9 %collective-permute-start = (bf16[240,512]{1,0:T(8,128)(2,1)S(1)}, bf16[240,512]{1,0:T(8,128)(2,1)S(1)}, u32[]{:S(2)}, u32[]{:S(2)}) collective-permute-start(bf16[240,512]{1,0:T(8,128)(2,1)S(1)} %get-tuple-element.93.rest_0_), channel_id=1, source_target_pairs={{0,8},{2,10},{8,16},{10,18},{16,24},{18,26},{24,28},{26,30},{28,20... | collective-permute-start | bytes 737288 | tf_op jit(solution)/shard_map/ppermute | solution.py:640
  5.0 7.4 %collective-permute-start.1 = (bf16[240,512]{1,0:T(8,128)(2,1)S(1)}, bf16[240,512]{1,0:T(8,128)(2,1)S(1)}, u32[]{:S(2)}, u32[]{:S(2)}) collective-permute-start(bf16[240,512]{1,0:T(8,128)(2,1)S(1)} %get-tuple-element.93.rest_0_), channel_id=1, source_target_pairs={{0,4},{2,6},{8,0},{10,2},{16,8},{18,10},{24,16},{26,18},{28,24},{3... | collective-permute-start | bytes 737288 | tf_op jit(solution)/shard_map/ppermute | solution.py:643
  12.4 11.0 %collective-permute-start.3 = (bf16[240,512]{1,0:T(8,128)(2,1)S(1)}, bf16[240,512]{1,0:T(8,128)(2,1)S(1)}, u32[]{:S(2)}, u32[]{:S(2)}) collective-permute-start(bf16[240,512]{1,0:T(8,128)(2,1)S(1)} %collective-permute-done.rest_1_), channel_id=1, source_target_pairs={{0,8},{2,10},{8,16},{10,18},{16,24},{18,26},{24,28},{26,30},{28,20... | collective-permute-start | bytes 737288 | tf_op jit(solution)/shard_map/ppermute | solution.py:640
  14.0 9.4 %collective-permute-start.4 = (bf16[240,512]{1,0:T(8,128)(2,1)S(1)}, bf16[240,512]{1,0:T(8,128)(2,1)S(1)}, u32[]{:S(2)}, u32[]{:S(2)}) collective-permute-start(bf16[240,512]{1,0:T(8,128)(2,1)S(1)} %collective-permute-done.1.rest_2_), channel_id=1, source_target_pairs={{0,4},{2,6},{8,0},{10,2},{16,8},{18,10},{24,16},{26,18},{28,24},{3... | collective-permute-start | bytes 737288 | tf_op jit(solution)/shard_map/ppermute | solution.py:643
  15.4 6.6 %collective-permute-start.5 = (bf16[48,1536]{1,0:T(8,128)(2,1)S(1)}, bf16[48,1536]{1,0:T(8,128)(2,1)S(1)}, u32[]{:S(2)}, u32[]{:S(2)}) collective-permute-start(bf16[48,1536]{1,0:T(8,128)(2,1)S(1)} %pack_down.1.rest_0_), channel_id=1, source_target_pairs={{0,8},{2,10},{8,16},{10,18},{16,24},{18,26},{24,28},{26,30},{28,20... | collective-permute-start | bytes 442376 | tf_op jit(solution)/shard_map/ppermute | solution.py:640
  17.1 6.3 %collective-permute-start.6 = (bf16[48,1536]{1,0:T(8,128)(2,1)S(1)}, bf16[48,1536]{1,0:T(8,128)(2,1)S(1)}, u32[]{:S(2)}, u32[]{:S(2)}) collective-permute-start(bf16[48,1536]{1,0:T(8,128)(2,1)S(1)} %pack_down.1.rest_0_), channel_id=1, source_target_pairs={{0,4},{2,6},{8,0},{10,2},{16,8},{18,10},{24,16},{26,18},{28,24},{3... | collective-permute-start | bytes 442376 | tf_op jit(solution)/shard_map/ppermute | solution.py:643
  24.6 10.9 %collective-permute-start.11 = (bf16[48,2304]{1,0:T(8,128)(2,1)S(1)}, bf16[48,2304]{1,0:T(8,128)(2,1)S(1)}, u32[]{:S(2)}, u32[]{:S(2)}) collective-permute-start(bf16[48,2304]{1,0:T(8,128)(2,1)S(1)} %pack_up.1.rest_0_), channel_id=1, source_target_pairs={{0,8},{2,10},{8,16},{10,18},{16,24},{18,26},{24,28},{26,30},{28,20... | collective-permute-start | bytes 663560 | tf_op jit(solution)/shard_map/ppermute | solution.py:640
  26.3 9.7 %collective-permute-start.12 = (bf16[48,2304]{1,0:T(8,128)(2,1)S(1)}, bf16[48,2304]{1,0:T(8,128)(2,1)S(1)}, u32[]{:S(2)}, u32[]{:S(2)}) collective-permute-start(bf16[48,2304]{1,0:T(8,128)(2,1)S(1)} %pack_up.1.rest_0_), channel_id=1, source_target_pairs={{0,4},{2,6},{8,0},{10,2},{16,8},{18,10},{24,16},{26,18},{28,24},{3... | collective-permute-start | bytes 663560 | tf_op jit(solution)/shard_map/ppermute | solution.py:643
  26.7 8.3 %collective-permute-start.10 = (bf16[48,1536]{1,0:T(8,128)(2,1)S(1)}, bf16[48,1536]{1,0:T(8,128)(2,1)S(1)}, u32[]{:S(2)}, u32[]{:S(2)}) collective-permute-start(bf16[48,1536]{1,0:T(8,128)(2,1)S(1)} %collective-permute-done.6.rest_2_), channel_id=1, source_target_pairs={{0,4},{2,6},{8,0},{10,2},{16,8},{18,10},{24,16},{26,18},{28,24},{3... | collective-permute-start | bytes 442376 | tf_op jit(solution)/shard_map/ppermute | solution.py:643
  27.2 8.3 %collective-permute-start.9 = (bf16[48,1536]{1,0:T(8,128)(2,1)S(1)}, bf16[48,1536]{1,0:T(8,128)(2,1)S(1)}, u32[]{:S(2)}, u32[]{:S(2)}) collective-permute-start(bf16[48,1536]{1,0:T(8,128)(2,1)S(1)} %collective-permute-done.5.rest_1_), channel_id=1, source_target_pairs={{0,8},{2,10},{8,16},{10,18},{16,24},{18,26},{24,28},{26,30},{28,20... | collective-permute-start | bytes 442376 | tf_op jit(solution)/shard_map/ppermute | solution.py:640
  28.8 9.1 %collective-permute-start.7 = (bf16[240,512]{1,0:T(8,128)(2,1)S(1)}, bf16[240,512]{1,0:T(8,128)(2,1)S(1)}, u32[]{:S(2)}, u32[]{:S(2)}) collective-permute-start(bf16[240,512]{1,0:T(8,128)(2,1)S(1)} %collective-permute-done.3.rest_3_), channel_id=1, source_target_pairs={{0,8},{2,10},{8,16},{10,18},{16,24},{18,26},{24,28},{26,30},{28,20... | collective-permute-start | bytes 737288 | tf_op jit(solution)/shard_map/ppermute | solution.py:640
  35.0 6.2 %collective-permute-start.8 = (bf16[240,512]{1,0:T(8,128)(2,1)S(1)}, bf16[240,512]{1,0:T(8,128)(2,1)S(1)}, u32[]{:S(2)}, u32[]{:S(2)}) collective-permute-start(bf16[240,512]{1,0:T(8,128)(2,1)S(1)} %collective-permute-done.4.rest_4_), channel_id=1, source_target_pairs={{0,4},{2,6},{8,0},{10,2},{16,8},{18,10},{24,16},{26,18},{28,24},{3... | collective-permute-start | bytes 737288 | tf_op jit(solution)/shard_map/ppermute | solution.py:643
  35.5 5.8 %collective-permute-start.21 = (bf16[240,512]{1,0:T(8,128)(2,1)S(1)}, bf16[240,512]{1,0:T(8,128)(2,1)S(1)}, u32[]{:S(2)}, u32[]{:S(2)}) collective-permute-start(bf16[240,512]{1,0:T(8,128)(2,1)S(1)} %get-tuple-element.93.rest_0_), channel_id=1, source_target_pairs={{0,2},{2,0},{4,6},{6,4},{8,10},{10,8},{12,14},{14,12},{16,18},{18,... | collective-permute-start | bytes 737288 | tf_op jit(solution)/shard_map/ppermute | solution.py:649
  35.5 7.7 %collective-permute-start.22 = (bf16[240,512]{1,0:T(8,128)(2,1)S(1)}, bf16[240,512]{1,0:T(8,128)(2,1)S(1)}, u32[]{:S(2)}, u32[]{:S(2)}) collective-permute-start(bf16[240,512]{1,0:T(8,128)(2,1)S(1)} %collective-permute-done.rest_1_), channel_id=1, source_target_pairs={{0,2},{2,0},{4,6},{6,4},{8,10},{10,8},{12,14},{14,12},{16,18},{18,... | collective-permute-start | bytes 737288 | tf_op jit(solution)/shard_map/ppermute | solution.py:649
  36.0 7.9 %collective-permute-start.23 = (bf16[240,512]{1,0:T(8,128)(2,1)S(1)}, bf16[240,512]{1,0:T(8,128)(2,1)S(1)}, u32[]{:S(2)}, u32[]{:S(2)}) collective-permute-start(bf16[240,512]{1,0:T(8,128)(2,1)S(1)} %collective-permute-done.1.rest_2_), channel_id=1, source_target_pairs={{0,2},{2,0},{4,6},{6,4},{8,10},{10,8},{12,14},{14,12},{16,18},{18,... | collective-permute-start | bytes 737288 | tf_op jit(solution)/shard_map/ppermute | solution.py:649
  41.2 4.1 %collective-permute-start.31 = (bf16[48,1536]{1,0:T(8,128)(2,1)S(1)}, bf16[48,1536]{1,0:T(8,128)(2,1)S(1)}, u32[]{:S(2)}, u32[]{:S(2)}) collective-permute-start(bf16[48,1536]{1,0:T(8,128)(2,1)S(1)} %collective-permute-done.5.rest_1_), channel_id=1, source_target_pairs={{0,2},{2,0},{4,6},{6,4},{8,10},{10,8},{12,14},{14,12},{16,18},{18,... | collective-permute-start | bytes 442376 | tf_op jit(solution)/shard_map/ppermute | solution.py:649
  41.2 4.7 %collective-permute-start.32 = (bf16[48,1536]{1,0:T(8,128)(2,1)S(1)}, bf16[48,1536]{1,0:T(8,128)(2,1)S(1)}, u32[]{:S(2)}, u32[]{:S(2)}) collective-permute-start(bf16[48,1536]{1,0:T(8,128)(2,1)S(1)} %collective-permute-done.6.rest_2_), channel_id=1, source_target_pairs={{0,2},{2,0},{4,6},{6,4},{8,10},{10,8},{12,14},{14,12},{16,18},{18,... | collective-permute-start | bytes 442376 | tf_op jit(solution)/shard_map/ppermute | solution.py:649
  41.7 12.0 %collective-permute-start.16 = (bf16[48,2304]{1,0:T(8,128)(2,1)S(1)}, bf16[48,2304]{1,0:T(8,128)(2,1)S(1)}, u32[]{:S(2)}, u32[]{:S(2)}) collective-permute-start(bf16[48,2304]{1,0:T(8,128)(2,1)S(1)} %collective-permute-done.11.rest_1_), channel_id=1, source_target_pairs={{0,8},{2,10},{8,16},{10,18},{16,24},{18,26},{24,28},{26,30},{28,20... | collective-permute-start | bytes 663560 | tf_op jit(solution)/shard_map/ppermute | solution.py:640
  43.2 9.9 %collective-permute-start.14 = (bf16[48,1536]{1,0:T(8,128)(2,1)S(1)}, bf16[48,1536]{1,0:T(8,128)(2,1)S(1)}, u32[]{:S(2)}, u32[]{:S(2)}) collective-permute-start(bf16[48,1536]{1,0:T(8,128)(2,1)S(1)} %collective-permute-done.9.rest_3_), channel_id=1, source_target_pairs={{0,8},{2,10},{8,16},{10,18},{16,24},{18,26},{24,28},{26,30},{28,20... | collective-permute-start | bytes 442376 | tf_op jit(solution)/shard_map/ppermute | solution.py:640
  43.9 9.3 %collective-permute-start.15 = (bf16[48,1536]{1,0:T(8,128)(2,1)S(1)}, bf16[48,1536]{1,0:T(8,128)(2,1)S(1)}, u32[]{:S(2)}, u32[]{:S(2)}) collective-permute-start(bf16[48,1536]{1,0:T(8,128)(2,1)S(1)} %collective-permute-done.10.rest_4_), channel_id=1, source_target_pairs={{0,4},{2,6},{8,0},{10,2},{16,8},{18,10},{24,16},{26,18},{28,24},{3... | collective-permute-start | bytes 442376 | tf_op jit(solution)/shard_map/ppermute | solution.py:643
  45.3 12.3 %collective-permute-start.13 = (bf16[240,512]{1,0:T(8,128)(2,1)S(1)}, bf16[240,512]{1,0:T(8,128)(2,1)S(1)}, u32[]{:S(2)}, u32[]{:S(2)}) collective-permute-start(bf16[240,512]{1,0:T(8,128)(2,1)S(1)} %collective-permute-done.7.rest_5_), channel_id=1, source_target_pairs={{0,8},{2,10},{8,16},{10,18},{16,24},{18,26},{24,28},{26,30},{28,20... | collective-permute-start | bytes 737288 | tf_op jit(solution)/shard_map/ppermute | solution.py:640
  45.9 8.0 %collective-permute-start.17 = (bf16[48,2304]{1,0:T(8,128)(2,1)S(1)}, bf16[48,2304]{1,0:T(8,128)(2,1)S(1)}, u32[]{:S(2)}, u32[]{:S(2)}) collective-permute-start(bf16[48,2304]{1,0:T(8,128)(2,1)S(1)} %collective-permute-done.12.rest_2_), channel_id=1, source_target_pairs={{0,4},{2,6},{8,0},{10,2},{16,8},{18,10},{24,16},{26,18},{28,24},{3... | collective-permute-start | bytes 663560 | tf_op jit(solution)/shard_map/ppermute | solution.py:643
  53.2 4.4 %collective-permute-start.24 = (bf16[240,512]{1,0:T(8,128)(2,1)S(1)}, bf16[240,512]{1,0:T(8,128)(2,1)S(1)}, u32[]{:S(2)}, u32[]{:S(2)}) collective-permute-start(bf16[240,512]{1,0:T(8,128)(2,1)S(1)} %collective-permute-done.3.rest_3_), channel_id=1, source_target_pairs={{0,2},{2,0},{4,6},{6,4},{8,10},{10,8},{12,14},{14,12},{16,18},{18,... | collective-permute-start | bytes 737288 | tf_op jit(solution)/shard_map/ppermute | solution.py:649
  53.2 5.9 %collective-permute-start.25 = (bf16[240,512]{1,0:T(8,128)(2,1)S(1)}, bf16[240,512]{1,0:T(8,128)(2,1)S(1)}, u32[]{:S(2)}, u32[]{:S(2)}) collective-permute-start(bf16[240,512]{1,0:T(8,128)(2,1)S(1)} %collective-permute-done.4.rest_4_), channel_id=1, source_target_pairs={{0,2},{2,0},{4,6},{6,4},{8,10},{10,8},{12,14},{14,12},{16,18},{18,... | collective-permute-start | bytes 737288 | tf_op jit(solution)/shard_map/ppermute | solution.py:649
  53.7 6.0 %collective-permute-start.26 = (bf16[240,512]{1,0:T(8,128)(2,1)S(1)}, bf16[240,512]{1,0:T(8,128)(2,1)S(1)}, u32[]{:S(2)}, u32[]{:S(2)}) collective-permute-start(bf16[240,512]{1,0:T(8,128)(2,1)S(1)} %collective-permute-done.7.rest_5_), channel_id=1, source_target_pairs={{0,2},{2,0},{4,6},{6,4},{8,10},{10,8},{12,14},{14,12},{16,18},{18,... | collective-permute-start | bytes 737288 | tf_op jit(solution)/shard_map/ppermute | solution.py:649
  53.9 7.3 %collective-permute-start.27 = (bf16[240,512]{1,0:T(8,128)(2,1)S(1)}, bf16[240,512]{1,0:T(8,128)(2,1)S(1)}, u32[]{:S(2)}, u32[]{:S(2)}) collective-permute-start(bf16[240,512]{1,0:T(8,128)(2,1)S(1)} %collective-permute-done.8.rest_6_), channel_id=1, source_target_pairs={{0,2},{2,0},{4,6},{6,4},{8,10},{10,8},{12,14},{14,12},{16,18},{18,... | collective-permute-start | bytes 737288 | tf_op jit(solution)/shard_map/ppermute | solution.py:649
  57.6 11.6 %collective-permute-start.28 = (bf16[240,512]{1,0:T(8,128)(2,1)S(1)}, bf16[240,512]{1,0:T(8,128)(2,1)S(1)}, u32[]{:S(2)}, u32[]{:S(2)}) collective-permute-start(bf16[240,512]{1,0:T(8,128)(2,1)S(1)} %collective-permute-done.13.rest_7_), channel_id=1, source_target_pairs={{0,2},{2,0},{4,6},{6,4},{8,10},{10,8},{12,14},{14,12},{16,18},{18,... | collective-permute-start | bytes 737288 | tf_op jit(solution)/shard_map/ppermute | solution.py:649
  57.6 11.0 %collective-permute-start.19 = (bf16[48,2304]{1,0:T(8,128)(2,1)S(1)}, bf16[48,2304]{1,0:T(8,128)(2,1)S(1)}, u32[]{:S(2)}, u32[]{:S(2)}) collective-permute-start(bf16[48,2304]{1,0:T(8,128)(2,1)S(1)} %collective-permute-done.16.rest_3_), channel_id=1, source_target_pairs={{0,8},{2,10},{8,16},{10,18},{16,24},{18,26},{24,28},{26,30},{28,20... | collective-permute-start | bytes 663560 | tf_op jit(solution)/shard_map/ppermute | solution.py:640
  59.2 10.0 %collective-permute-start.20 = (bf16[48,2304]{1,0:T(8,128)(2,1)S(1)}, bf16[48,2304]{1,0:T(8,128)(2,1)S(1)}, u32[]{:S(2)}, u32[]{:S(2)}) collective-permute-start(bf16[48,2304]{1,0:T(8,128)(2,1)S(1)} %collective-permute-done.17.rest_4_), channel_id=1, source_target_pairs={{0,4},{2,6},{8,0},{10,2},{16,8},{18,10},{24,16},{26,18},{28,24},{3... | collective-permute-start | bytes 663560 | tf_op jit(solution)/shard_map/ppermute | solution.py:643
  59.7 8.9 %collective-permute-start.18 = (bf16[48,1536]{1,0:T(8,128)(2,1)S(1)}, bf16[48,1536]{1,0:T(8,128)(2,1)S(1)}, u32[]{:S(2)}, u32[]{:S(2)}) collective-permute-start(bf16[48,1536]{1,0:T(8,128)(2,1)S(1)} %collective-permute-done.14.rest_5_), channel_id=1, source_target_pairs={{0,8},{2,10},{8,16},{10,18},{16,24},{18,26},{24,28},{26,30},{28,20... | collective-permute-start | bytes 442376 | tf_op jit(solution)/shard_map/ppermute | solution.py:640
  61.2 14.9 %collective-permute-start.39 = (bf16[48,2304]{1,0:T(8,128)(2,1)S(1)}, bf16[48,2304]{1,0:T(8,128)(2,1)S(1)}, u32[]{:S(2)}, u32[]{:S(2)}) collective-permute-start(bf16[48,2304]{1,0:T(8,128)(2,1)S(1)} %pack_up.1.rest_0_), channel_id=1, source_target_pairs={{0,2},{2,0},{4,6},{6,4},{8,10},{10,8},{12,14},{14,12},{16,18},{18,... | collective-permute-start | bytes 663560 | tf_op jit(solution)/shard_map/ppermute | solution.py:649
  68.6 8.0 %collective-permute-start.33 = (bf16[48,1536]{1,0:T(8,128)(2,1)S(1)}, bf16[48,1536]{1,0:T(8,128)(2,1)S(1)}, u32[]{:S(2)}, u32[]{:S(2)}) collective-permute-start(bf16[48,1536]{1,0:T(8,128)(2,1)S(1)} %collective-permute-done.9.rest_3_), channel_id=1, source_target_pairs={{0,2},{2,0},{4,6},{6,4},{8,10},{10,8},{12,14},{14,12},{16,18},{18,... | collective-permute-start | bytes 442376 | tf_op jit(solution)/shard_map/ppermute | solution.py:649
  68.6 9.5 %collective-permute-start.34 = (bf16[48,1536]{1,0:T(8,128)(2,1)S(1)}, bf16[48,1536]{1,0:T(8,128)(2,1)S(1)}, u32[]{:S(2)}, u32[]{:S(2)}) collective-permute-start(bf16[48,1536]{1,0:T(8,128)(2,1)S(1)} %collective-permute-done.10.rest_4_), channel_id=1, source_target_pairs={{0,2},{2,0},{4,6},{6,4},{8,10},{10,8},{12,14},{14,12},{16,18},{18,... | collective-permute-start | bytes 442376 | tf_op jit(solution)/shard_map/ppermute | solution.py:649
  69.1 9.0 %collective-permute-start.40 = (bf16[48,2304]{1,0:T(8,128)(2,1)S(1)}, bf16[48,2304]{1,0:T(8,128)(2,1)S(1)}, u32[]{:S(2)}, u32[]{:S(2)}) collective-permute-start(bf16[48,2304]{1,0:T(8,128)(2,1)S(1)} %collective-permute-done.11.rest_1_), channel_id=1, source_target_pairs={{0,2},{2,0},{4,6},{6,4},{8,10},{10,8},{12,14},{14,12},{16,18},{18,... | collective-permute-start | bytes 663560 | tf_op jit(solution)/shard_map/ppermute | solution.py:649
  69.2 9.5 %collective-permute-start.41 = (bf16[48,2304]{1,0:T(8,128)(2,1)S(1)}, bf16[48,2304]{1,0:T(8,128)(2,1)S(1)}, u32[]{:S(2)}, u32[]{:S(2)}) collective-permute-start(bf16[48,2304]{1,0:T(8,128)(2,1)S(1)} %collective-permute-done.12.rest_2_), channel_id=1, source_target_pairs={{0,2},{2,0},{4,6},{6,4},{8,10},{10,8},{12,14},{14,12},{16,18},{18,... | collective-permute-start | bytes 663560 | tf_op jit(solution)/shard_map/ppermute | solution.py:649
  76.1 5.0 %collective-permute-start.42 = (bf16[48,2304]{1,0:T(8,128)(2,1)S(1)}, bf16[48,2304]{1,0:T(8,128)(2,1)S(1)}, u32[]{:S(2)}, u32[]{:S(2)}) collective-permute-start(bf16[48,2304]{1,0:T(8,128)(2,1)S(1)} %collective-permute-done.16.rest_3_), channel_id=1, source_target_pairs={{0,2},{2,0},{4,6},{6,4},{8,10},{10,8},{12,14},{14,12},{16,18},{18,... | collective-permute-start | bytes 663560 | tf_op jit(solution)/shard_map/ppermute | solution.py:649
  76.6 7.6 %collective-permute-start.38 = (bf16[48,2304]{1,0:T(8,128)(2,1)S(1)}, bf16[48,2304]{1,0:T(8,128)(2,1)S(1)}, u32[]{:S(2)}, u32[]{:S(2)}) collective-permute-start(bf16[48,2304]{1,0:T(8,128)(2,1)S(1)} %collective-permute-done.19.rest_5_), channel_id=1, source_target_pairs={{0,8},{2,10},{8,16},{10,18},{16,24},{18,26},{24,28},{26,30},{28,20... | collective-permute-start | bytes 663560 | tf_op jit(solution)/shard_map/ppermute | solution.py:640
  79.5 12.9 %collective-permute-start.29 = (bf16[512,384]{1,0:T(8,128)(2,1)S(1)}, bf16[512,384]{1,0:T(8,128)(2,1)S(1)}, u32[]{:S(2)}, u32[]{:S(2)}) collective-permute-start(bf16[512,384]{1,0:T(8,128)(2,1)S(1)} %get-tuple-element.114.own_ref.mixed_ref), channel_id=1, source_target_pairs={{0,1},{1,0},{2,3},{3,2},{4,5},{5,4},{6,7},{7,6},{8,9},{9,8},{10,11... | collective-permute-start | bytes 1179656 | tf_op jit(solution)/shard_map/ppermute | solution.py:790
  81.0 7.0 %collective-permute-start.43 = (bf16[48,2304]{1,0:T(8,128)(2,1)S(1)}, bf16[48,2304]{1,0:T(8,128)(2,1)S(1)}, u32[]{:S(2)}, u32[]{:S(2)}) collective-permute-start(bf16[48,2304]{1,0:T(8,128)(2,1)S(1)} %collective-permute-done.17.rest_4_), channel_id=1, source_target_pairs={{0,2},{2,0},{4,6},{6,4},{8,10},{10,8},{12,14},{14,12},{16,18},{18,... | collective-permute-start | bytes 663560 | tf_op jit(solution)/shard_map/ppermute | solution.py:649
  81.2 7.0 %collective-permute-start.44 = (bf16[48,2304]{1,0:T(8,128)(2,1)S(1)}, bf16[48,2304]{1,0:T(8,128)(2,1)S(1)}, u32[]{:S(2)}, u32[]{:S(2)}) collective-permute-start(bf16[48,2304]{1,0:T(8,128)(2,1)S(1)} %collective-permute-done.19.rest_5_), channel_id=1, source_target_pairs={{0,2},{2,0},{4,6},{6,4},{8,10},{10,8},{12,14},{14,12},{16,18},{18,... | collective-permute-start | bytes 663560 | tf_op jit(solution)/shard_map/ppermute | solution.py:649
  81.7 6.4 %collective-permute-start.45 = (bf16[48,2304]{1,0:T(8,128)(2,1)S(1)}, bf16[48,2304]{1,0:T(8,128)(2,1)S(1)}, u32[]{:S(2)}, u32[]{:S(2)}) collective-permute-start(bf16[48,2304]{1,0:T(8,128)(2,1)S(1)} %collective-permute-done.20.rest_6_), channel_id=1, source_target_pairs={{0,2},{2,0},{4,6},{6,4},{8,10},{10,8},{12,14},{14,12},{16,18},{18,... | collective-permute-start | bytes 663560 | tf_op jit(solution)/shard_map/ppermute | solution.py:649
  103.0 20.5 %collective-permute-start.56 = (bf16[6,48,3072]{2,1,0:T(8,128)(2,1)S(1)}, bf16[6,48,3072]{2,1,0:T(8,128)(2,1)S(1)}, u32[]{:S(2)}, u32[]{:S(2)}) collective-permute-start(bf16[6,48,3072]{2,1,0:T(8,128)(2,1)S(1)} %get-tuple-element.155), channel_id=1, source_target_pairs={{0,2},{2,0},{4,6},{6,4},{8,10},{10,8},{12,14},{14,12},{16,18},{18,... | collective-permute-start | bytes 5308424 | tf_op jit(solution)/shard_map/ppermute | solution.py:689
  103.6 4.2 %collective-permute-start.47 = (bf16[2,48,3072]{2,1,0:T(8,128)(2,1)S(1)}, bf16[2,48,3072]{2,1,0:T(8,128)(2,1)S(1)}, u32[]{:S(2)}, u32[]{:S(2)}) collective-permute-start(bf16[2,48,3072]{2,1,0:T(8,128)(2,1)S(1)} %get-tuple-element.128), channel_id=1, source_target_pairs={{0,2},{2,0},{4,6},{6,4},{8,10},{10,8},{12,14},{14,12},{16,18},{18,... | collective-permute-start | bytes 1769480 | tf_op jit(solution)/shard_map/ppermute | solution.py:662
  103.6 7.7 %collective-permute-start.51 = (bf16[128,768]{1,0:T(8,128)(2,1)S(1)}, bf16[128,768]{1,0:T(8,128)(2,1)S(1)}, u32[]{:S(2)}, u32[]{:S(2)}) collective-permute-start(bf16[128,768]{1,0:T(8,128)(2,1)S(1)} %get-tuple-element.131.rest_1_), channel_id=1, source_target_pairs={{0,1},{1,0},{2,3},{3,2},{4,5},{5,4},{6,7},{7,6},{8,9},{9,8},{10,11... | collective-permute-start | bytes 589832 | tf_op jit(solution)/shard_map/ppermute | solution.py:807
  105.2 10.4 %collective-permute-start.50 = (bf16[128,768]{1,0:T(8,128)(2,1)S(1)}, bf16[128,768]{1,0:T(8,128)(2,1)S(1)}, u32[]{:S(2)}, u32[]{:S(2)}) collective-permute-start(bf16[128,768]{1,0:T(8,128)(2,1)S(1)} %get-tuple-element.130.rest_0_), channel_id=1, source_target_pairs={{0,1},{1,0},{2,3},{3,2},{4,5},{5,4},{6,7},{7,6},{8,9},{9,8},{10,11... | collective-permute-start | bytes 589832 | tf_op jit(solution)/shard_map/ppermute | solution.py:807
  107.9 15.7 %collective-permute-start.48 = (bf16[48,3072]{1,0:T(8,128)(2,1)S(1)}, bf16[48,3072]{1,0:T(8,128)(2,1)S(1)}, u32[]{:S(2)}, u32[]{:S(2)}) collective-permute-start(bf16[48,3072]{1,0:T(8,128)(2,1)S(1)} %get-tuple-element.190), channel_id=1, source_target_pairs={{0,8},{2,10},{8,16},{10,18},{16,24},{18,26},{24,28},{26,30},{28,20... | collective-permute-start | bytes 884744 | tf_op jit(solution)/shard_map/ppermute | solution.py:691
  109.4 14.1 %collective-permute-start.49 = (bf16[48,3072]{1,0:T(8,128)(2,1)S(1)}, bf16[48,3072]{1,0:T(8,128)(2,1)S(1)}, u32[]{:S(2)}, u32[]{:S(2)}) collective-permute-start(bf16[48,3072]{1,0:T(8,128)(2,1)S(1)} %get-tuple-element.189), channel_id=1, source_target_pairs={{0,4},{2,6},{8,0},{10,2},{16,8},{18,10},{24,16},{26,18},{28,24},{3... | collective-permute-start | bytes 884744 | tf_op jit(solution)/shard_map/ppermute | solution.py:694
  111.3 8.4 %collective-permute-start.53 = (bf16[128,768]{1,0:T(8,128)(2,1)S(1)}, bf16[128,768]{1,0:T(8,128)(2,1)S(1)}, u32[]{:S(2)}, u32[]{:S(2)}) collective-permute-start(bf16[128,768]{1,0:T(8,128)(2,1)S(1)} %get-tuple-element.135.rest_3_), channel_id=1, source_target_pairs={{0,1},{1,0},{2,3},{3,2},{4,5},{5,4},{6,7},{7,6},{8,9},{9,8},{10,11... | collective-permute-start | bytes 589832 | tf_op jit(solution)/shard_map/ppermute | solution.py:807
  115.6 8.0 %collective-permute-start.52 = (bf16[128,768]{1,0:T(8,128)(2,1)S(1)}, bf16[128,768]{1,0:T(8,128)(2,1)S(1)}, u32[]{:S(2)}, u32[]{:S(2)}) collective-permute-start(bf16[128,768]{1,0:T(8,128)(2,1)S(1)} %get-tuple-element.133.rest_2_), channel_id=1, source_target_pairs={{0,1},{1,0},{2,3},{3,2},{4,5},{5,4},{6,7},{7,6},{8,9},{9,8},{10,11... | collective-permute-start | bytes 589832 | tf_op jit(solution)/shard_map/ppermute | solution.py:807
  123.8 15.7 %collective-permute-start.57 = (bf16[48,3072]{1,0:T(8,128)(2,1)S(1)}, bf16[48,3072]{1,0:T(8,128)(2,1)S(1)}, u32[]{:S(2)}, u32[]{:S(2)}) collective-permute-start(bf16[48,3072]{1,0:T(8,128)(2,1)S(1)} %get-tuple-element.186), channel_id=1, source_target_pairs={{0,8},{2,10},{8,16},{10,18},{16,24},{18,26},{24,28},{26,30},{28,20... | collective-permute-start | bytes 884744 | tf_op jit(solution)/shard_map/ppermute | solution.py:691
  125.3 14.2 %collective-permute-start.58 = (bf16[48,3072]{1,0:T(8,128)(2,1)S(1)}, bf16[48,3072]{1,0:T(8,128)(2,1)S(1)}, u32[]{:S(2)}, u32[]{:S(2)}) collective-permute-start(bf16[48,3072]{1,0:T(8,128)(2,1)S(1)} %get-tuple-element.185), channel_id=1, source_target_pairs={{0,4},{2,6},{8,0},{10,2},{16,8},{18,10},{24,16},{26,18},{28,24},{3... | collective-permute-start | bytes 884744 | tf_op jit(solution)/shard_map/ppermute | solution.py:694
  139.0 25.4 %collective-permute-start.55 = (bf16[6,288,512]{2,1,0:T(8,128)(2,1)S(1)}, bf16[6,288,512]{2,1,0:T(8,128)(2,1)S(1)}, u32[]{:S(2)}, u32[]{:S(2)}) collective-permute-start(bf16[6,288,512]{2,1,0:T(8,128)(2,1)S(1)} %get-tuple-element.154), channel_id=1, source_target_pairs={{0,2},{2,0},{4,6},{6,4},{8,10},{10,8},{12,14},{14,12},{16,18},{18,... | collective-permute-start | bytes 5308424 | tf_op jit(solution)/shard_map/ppermute | solution.py:689
  139.7 9.0 %collective-permute-start.59 = (bf16[48,3072]{1,0:T(8,128)(2,1)S(1)}, bf16[48,3072]{1,0:T(8,128)(2,1)S(1)}, u32[]{:S(2)}, u32[]{:S(2)}) collective-permute-start(bf16[48,3072]{1,0:T(8,128)(2,1)S(1)} %get-tuple-element.184), channel_id=1, source_target_pairs={{0,8},{2,10},{8,16},{10,18},{16,24},{18,26},{24,28},{26,30},{28,20... | collective-permute-start | bytes 884744 | tf_op jit(solution)/shard_map/ppermute | solution.py:691
  141.3 8.7 %collective-permute-start.60 = (bf16[48,3072]{1,0:T(8,128)(2,1)S(1)}, bf16[48,3072]{1,0:T(8,128)(2,1)S(1)}, u32[]{:S(2)}, u32[]{:S(2)}) collective-permute-start(bf16[48,3072]{1,0:T(8,128)(2,1)S(1)} %get-tuple-element.183), channel_id=1, source_target_pairs={{0,4},{2,6},{8,0},{10,2},{16,8},{18,10},{24,16},{26,18},{28,24},{3... | collective-permute-start | bytes 884744 | tf_op jit(solution)/shard_map/ppermute | solution.py:694
  150.2 10.0 %collective-permute-start.63 = (bf16[288,512]{1,0:T(8,128)(2,1)S(1)}, bf16[288,512]{1,0:T(8,128)(2,1)S(1)}, u32[]{:S(2)}, u32[]{:S(2)}) collective-permute-start(bf16[288,512]{1,0:T(8,128)(2,1)S(1)} %get-tuple-element.188), channel_id=1, source_target_pairs={{0,8},{2,10},{8,16},{10,18},{16,24},{18,26},{24,28},{26,30},{28,20... | collective-permute-start | bytes 884744 | tf_op jit(solution)/shard_map/ppermute | solution.py:691
  150.8 10.8 %collective-permute-start.64 = (bf16[288,512]{1,0:T(8,128)(2,1)S(1)}, bf16[288,512]{1,0:T(8,128)(2,1)S(1)}, u32[]{:S(2)}, u32[]{:S(2)}) collective-permute-start(bf16[288,512]{1,0:T(8,128)(2,1)S(1)} %get-tuple-element.187), channel_id=1, source_target_pairs={{0,4},{2,6},{8,0},{10,2},{16,8},{18,10},{24,16},{26,18},{28,24},{3... | collective-permute-start | bytes 884744 | tf_op jit(solution)/shard_map/ppermute | solution.py:694
  152.3 12.0 %collective-permute-start.62 = (bf16[48,3072]{1,0:T(8,128)(2,1)S(1)}, bf16[48,3072]{1,0:T(8,128)(2,1)S(1)}, u32[]{:S(2)}, u32[]{:S(2)}) collective-permute-start(bf16[48,3072]{1,0:T(8,128)(2,1)S(1)} %fusion.19), channel_id=1, source_target_pairs={{0,8},{2,10},{8,16},{10,18},{16,24},{18,26},{24,28},{26,30},{28,20... | collective-permute-start | bytes 884744 | tf_op jit(solution)/shard_map/ppermute | solution.py:691
  153.1 20.5 %collective-permute-start.67 = (bf16[512,768]{1,0:T(8,128)(2,1)S(1)}, bf16[512,768]{1,0:T(8,128)(2,1)S(1)}, u32[]{:S(2)}, u32[]{:S(2)}) collective-permute-start(bf16[512,768]{1,0:T(8,128)(2,1)S(1)} %ffn_out.1), channel_id=1, source_target_pairs={{0,1},{1,0},{2,3},{3,2},{4,5},{5,4},{6,7},{7,6},{8,9},{9,8},{10,11... | collective-permute-start | bytes 2359304 | tf_op jit(solution)/shard_map/ppermute | solution.py:814
  160.2 27.4 %collective-permute-start.70 = (bf16[512,768]{1,0:T(8,128)(2,1)S(1)}, bf16[512,768]{1,0:T(8,128)(2,1)S(1)}, u32[]{:S(2)}, u32[]{:S(2)}) collective-permute-start(bf16[512,768]{1,0:T(8,128)(2,1)S(1)} %get-tuple-element.169), channel_id=1, source_target_pairs={{0,1},{1,0},{2,3},{3,2},{4,5},{5,4},{6,7},{7,6},{8,9},{9,8},{10,11... | collective-permute-start | bytes 2359304 | tf_op jit(solution)/shard_map/ppermute | solution.py:826
  164.6 9.0 %collective-permute-start.65 = (bf16[288,512]{1,0:T(8,128)(2,1)S(1)}, bf16[288,512]{1,0:T(8,128)(2,1)S(1)}, u32[]{:S(2)}, u32[]{:S(2)}) collective-permute-start(bf16[288,512]{1,0:T(8,128)(2,1)S(1)} %get-tuple-element.182), channel_id=1, source_target_pairs={{0,8},{2,10},{8,16},{10,18},{16,24},{18,26},{24,28},{26,30},{28,20... | collective-permute-start | bytes 884744 | tf_op jit(solution)/shard_map/ppermute | solution.py:691
  165.3 8.3 %collective-permute-start.66 = (bf16[288,512]{1,0:T(8,128)(2,1)S(1)}, bf16[288,512]{1,0:T(8,128)(2,1)S(1)}, u32[]{:S(2)}, u32[]{:S(2)}) collective-permute-start(bf16[288,512]{1,0:T(8,128)(2,1)S(1)} %get-tuple-element.181), channel_id=1, source_target_pairs={{0,4},{2,6},{8,0},{10,2},{16,8},{18,10},{24,16},{26,18},{28,24},{3... | collective-permute-start | bytes 884744 | tf_op jit(solution)/shard_map/ppermute | solution.py:694
  173.8 13.7 %collective-permute-start.68 = (bf16[288,512]{1,0:T(8,128)(2,1)S(1)}, bf16[288,512]{1,0:T(8,128)(2,1)S(1)}, u32[]{:S(2)}, u32[]{:S(2)}) collective-permute-start(bf16[288,512]{1,0:T(8,128)(2,1)S(1)} %get-tuple-element.180), channel_id=1, source_target_pairs={{0,8},{2,10},{8,16},{10,18},{16,24},{18,26},{24,28},{26,30},{28,20... | collective-permute-start | bytes 884744 | tf_op jit(solution)/shard_map/ppermute | solution.py:691
  174.4 13.2 %collective-permute-start.69 = (bf16[288,512]{1,0:T(8,128)(2,1)S(1)}, bf16[288,512]{1,0:T(8,128)(2,1)S(1)}, u32[]{:S(2)}, u32[]{:S(2)}) collective-permute-start(bf16[288,512]{1,0:T(8,128)(2,1)S(1)} %get-tuple-element.179), channel_id=1, source_target_pairs={{0,4},{2,6},{8,0},{10,2},{16,8},{18,10},{24,16},{26,18},{28,24},{3... | collective-permute-start | bytes 884744 | tf_op jit(solution)/shard_map/ppermute | solution.py:694
  187.6 6.8 %collective-permute-start.71 = (bf16[288,512]{1,0:T(8,128)(2,1)S(1)}, bf16[288,512]{1,0:T(8,128)(2,1)S(1)}, u32[]{:S(2)}, u32[]{:S(2)}) collective-permute-start(bf16[288,512]{1,0:T(8,128)(2,1)S(1)} %fusion.10), channel_id=1, source_target_pairs={{0,8},{2,10},{8,16},{10,18},{16,24},{18,26},{24,28},{26,30},{28,20... | collective-permute-start | bytes 884744 | tf_op jit(solution)/shard_map/ppermute | solution.py:691
  (59 other events, 1374.7 us)

commit v3 on v2

v3 whole, which is shorter than its diff:
```python
import jax
import jax.numpy as jnp
from jax import lax
from jax.experimental import pallas as pl
from jax.experimental.pallas import tpu as pltpu
from jax.sharding import PartitionSpec as P

EPSILON = 1e-06
NEGATIVE = -1e30
BF = jnp.bfloat16
F32 = jnp.float32
UNITS = 16
LANES = 128
PARTS = 2
RING_CHIPS = 8
VMEM_BYTES = 20 * 1024 * 1024
NT = (((1,), (1,)), ((), ()))
TN = (((0,), (0,)), ((), ()))
NN = (((1,), (0,)), ((), ()))


def mm(a, b, dims=NN):
    return lax.dot_general(a, b, dims, preferred_element_type=F32)


def run(kernel, name, scalars, arrays, outs, scratch=(), loose=(), loose_outs=(), micros=0, aliases=None):
    held = [pltpu.with_memory_space_constraint(one, pltpu.VMEM) for one in arrays]
    results = [pltpu.VMEM(*one) for one in outs] + [jax.ShapeDtypeStruct(*one) for one in loose_outs]
    specs = [pl.BlockSpec(memory_space=pltpu.SMEM)] * len(scalars)
    specs += [pl.BlockSpec(memory_space=pltpu.VMEM)] * len(arrays)
    specs += [pl.BlockSpec(memory_space=pltpu.HBM)] * len(loose)
    loose = [pltpu.with_memory_space_constraint(one, pltpu.HBM) for one in loose]
    out_specs = [pl.BlockSpec(memory_space=pltpu.VMEM)] * len(outs)
    out_specs += [pl.BlockSpec(memory_space=pl.ANY)] * len(loose_outs)
    return pl.pallas_call(
        kernel,
        out_shape=tuple(results),
        in_specs=specs,
        out_specs=tuple(out_specs),
        scratch_shapes=list(scratch),
        compiler_params=pltpu.CompilerParams(vmem_limit_bytes=VMEM_BYTES),
        cost_estimate=pl.CostEstimate(flops=1 + micros * 1_000_000_000, bytes_accessed=1, transcendentals=0),
        input_output_aliases=aliases or {},
        name=name,
    )(*scalars, *held, *loose)


def gelu_pair(x):
    c = 0.7978845608028654
    a = 0.044715
    square = x * x
    t = jnp.tanh(c * x * (1.0 + a * square))
    half = 0.5 * (1.0 + t)
    return x * half, half + 0.5 * x * (1.0 - t * t) * (c * (1.0 + 3.0 * a * square))


def multiple(value, of):
    return pl.multiple_of(value, of)


class Unit:
    def __init__(self, heads, rows, krows, length, model, width, hidden):
        self.scores = heads * rows
        self.krows = krows
        self.length = length
        self.width = width
        self.hidden = hidden
        self.wide = width + model
        self.blocks = [("ffn", n * length) for n in range(2 * hidden // length)]
        self.blocks += [("proj", n * length) for n in range(self.wide // length)]
        self.tail = self.wide % length
        self.last = self.scores + krows * len(self.blocks)
        self.fold = krows // 3
        self.deep = self.last + self.fold
        self.cut = self.scores + krows * (2 * hidden // length // 3)
        self.gain_lane = 3 * self.tail

    def ffn_parts(self):
        parts = []
        for n, (kind, first) in enumerate(self.blocks):
            at = self.scores + n * self.krows
            if kind == "ffn":
                parts.append((at, 0, 0, first, self.krows, self.length))
            else:
                skip = max(self.width - first, 0)
                column = 2 * self.hidden + first + skip - self.width
                parts.append((at, skip, 0, column, self.krows, self.length - skip))
        for n in range(3):
            column = 2 * self.hidden + self.wide - self.tail - self.width
            parts.append((self.last, n * self.tail, n * self.fold, column, self.fold, self.tail))
        return parts

    def value_row(self):
        return self.scores + [kind for kind, _ in self.blocks].index("proj") * self.krows


def pack_unit(plan, scores, w_up, w_down):
    inputs = (scores, w_up, w_down)
    krows, length = plan.krows, plan.length
    per = plan.hidden // length

    def kernel(*refs):
        out, held, sem = refs[3], refs[4:7], refs[7]
        fetch(refs[:3], held, sem)
        s_ref, up_ref, down_ref = held
        out[: plan.scores, :] = s_ref[...].reshape(plan.scores, length).astype(BF)
        for n, (kind, column) in enumerate(plan.blocks):
            if kind == "ffn":
                at = slice(plan.scores + n * krows, plan.scores + (n + 1) * krows)
                ref, first = (up_ref, column) if n < per else (down_ref, column - plan.hidden)
                out[at, :] = ref[:, first : first + length].astype(BF)

    return run(
        kernel,
        "pack_unit",
        (),
        (),
        (((plan.deep, length), BF),),
        (*[pltpu.VMEM(one.shape, one.dtype) for one in inputs], pltpu.SemaphoreType.DMA((3,))),
        loose=inputs,
    )[0]


def pack_rest(plan, second, unit, wv, gain_one, gain_two, wo_own, wo_other):
    inputs = (wv, gain_one.reshape(1, -1), gain_two.reshape(1, -1), wo_own)
    krows, length, width = plan.krows, plan.length, plan.width

    def kernel(second_ref, other_ref, old, *rest):
        out, wide, gains = rest[4:7]
        held, sem = rest[7:11], rest[11]
        fetch(rest[:4], held, sem)
        wv_ref, ga_ref, gf_ref, own_ref = held
        first = second_ref[0]
        wide[:, :width] = wv_ref[...].astype(BF)
        wide[:, pl.ds(multiple(width + first * width, LANES), width)] = own_ref[...].astype(BF)
        wide[:, pl.ds(multiple(width + (1 - first) * width, LANES), width)] = other_ref[...].astype(BF)
        for n, (kind, column) in enumerate(plan.blocks):
            if kind == "proj":
                at = slice(plan.scores + n * krows, plan.scores + (n + 1) * krows)
                out[at, :] = wide[:, column : column + length]
        for n in range(3):
            lanes = slice(n * plan.tail, (n + 1) * plan.tail)
            out[plan.last :, lanes] = wide[n * plan.fold : (n + 1) * plan.fold, plan.wide - plan.tail :]
        gains[...] = jnp.zeros_like(gains)
        gains[0:1, :krows] = ga_ref[...]
        gains[1:2, :krows] = gf_ref[...]
        out[plan.last :, plan.gain_lane :] = gains[...].astype(BF)

    return run(
        kernel,
        "pack_rest",
        (second,),
        (wo_other, unit),
        (((plan.deep, length), BF),),
        (
            pltpu.VMEM((krows, plan.wide), BF),
            pltpu.VMEM((plan.fold, length - plan.gain_lane), F32),
            *[pltpu.VMEM(one.shape, one.dtype) for one in inputs],
            pltpu.SemaphoreType.DMA((4,)),
        ),
        loose=inputs,
        aliases={2: 0},
    )[0]


def fetch(refs, held, sem):
    copies = [pltpu.make_async_copy(ref, to, sem.at[n]) for n, (ref, to) in enumerate(zip(refs, held))]
    for copy in copies:
        copy.start()
    for copy in copies:
        copy.wait()


def pick(units, shares, where_ref, parts, target, sem):
    copies = []
    for n, (u, first, rows) in enumerate(shares):
        owner = where_ref[u]
        for m, part in enumerate(parts):
            row, column, count, columns = part[0], part[1], part[-2], part[-1]
            if first <= row and row + count <= first + rows:
                source = units[n].at[pl.ds(row - first, count), pl.ds(column, columns)]
                copies.append(pltpu.make_async_copy(source, target(m, owner), sem.at[u, m]))
                copies[-1].start()
    return copies


def mixer_rows(plan, units, shares, where_ref, seg_ref, e_ref, unit, same, sem):
    heads, length, _ = e_ref.shape
    rows = length // UNITS
    top = heads * rows
    mine = [n for n, (_, first, _) in enumerate(shares) if first == 0]

    def target(m, owner):
        return unit.at[pl.ds(multiple(owner * top, top), top), :]

    copies = pick([units[n] for n in mine], [shares[n] for n in mine], where_ref, [(0, 0, top, length)], target, sem)

    def write():
        documents = (seg_ref[...] == lax.broadcasted_iota(jnp.int32, (LANES, length), 0)).astype(BF)
        same[...] = mm(documents, documents, TN)
        for copy in copies:
            copy.wait()

        def one_head(h, carry):
            for n in mine:
                owner = where_ref[shares[n][0]]
                at = pl.ds(multiple(owner * rows, rows), rows)
                s = unit[pl.ds(multiple(owner * top + h * rows, rows), rows), :].astype(F32)
                e_ref[h, at, :] = (jnp.exp(s) * same[at, :]).astype(BF)
            return carry

        lax.fori_loop(0, heads, one_head, 0)

    return write


def mixer_first(plan, where, segments, units, shares, heads):
    length = segments.shape[1]
    rows = length // UNITS

    def kernel(where_ref, seg_ref, *rest):
        e_ref, unit, same, sem = rest[len(units) :]
        mixer_rows(plan, rest[: len(units)], shares, where_ref, seg_ref, e_ref, unit, same, sem)()

    return run(
        kernel,
        "mixer_first",
        (where,),
        (segments,),
        (((heads, length, length), BF),),
        (
            pltpu.VMEM((heads * length, length), BF),
            pltpu.VMEM((length, length), F32),
            pltpu.SemaphoreType.DMA((UNITS, 1)),
        ),
        loose=units,
    )[0]


def mixer_forward(plan, where, tokens, segments, e, units, shares, late, heads, width):
    length, model = tokens.shape
    size = width // heads
    krows = model // UNITS
    wide = heads * LANES
    parts = [
        (plan.value_row(), 0, krows, width),
        (plan.last, plan.gain_lane, plan.fold, LANES),
    ]
    count = len(units)

    def kernel(where_ref, tok_ref, seg_ref, e_old, *rest):
        unit_refs = rest[:count]
        e_ref, va_ref, mixed_ref, mixf_ref, rb_ref, n1_ref, gains_ref, wv_ref, pieces, unit, low, same, sem, more = rest[count:]

        def target(m, owner):
            if m == 0:
                return wv_ref.at[pl.ds(multiple(owner * krows, 16), krows), :]
            return low.at[owner]

        copies = pick(unit_refs, shares, where_ref, parts, target, sem)
        now = [n for n in range(count) if n in late]
        write = mixer_rows(
            plan, [unit_refs[n] for n in now], [shares[n] for n in now], where_ref, seg_ref, e_ref, unit, same, more
        )
        for copy in copies:
            copy.wait()
        for d in range(UNITS):
            some = low[d].astype(F32)
            pieces[0, d : d + 1, :] = some[0:1, :]
            pieces[1, d : d + 1, :] = some[1:2, :]
        spread = (
            lax.broadcasted_iota(jnp.int32, (LANES, model), 1) % krows
            == lax.broadcasted_iota(jnp.int32, (LANES, model), 0)
        ).astype(BF)
        own = (
            lax.broadcasted_iota(jnp.int32, (UNITS, model), 1) // krows
            == lax.broadcasted_iota(jnp.int32, (UNITS, model), 0)
        )
        gains = []
        for t in range(2):
            full = jnp.where(own, mm(pieces[t].astype(BF), spread), 0.0)
            gains.append(jnp.sum(full, axis=0, keepdims=True))
            gains_ref[t : t + 1, :] = gains[t]
        x = tok_ref[...].astype(F32)
        inv = lax.rsqrt(jnp.mean(x * x, axis=-1, keepdims=True) + EPSILON)
        n1_ref[...] = (x * inv * gains[0]).astype(BF)
        values = mm(n1_ref[...], wv_ref[...]).astype(BF)
        tail = (lax.broadcasted_iota(jnp.int32, (length, LANES - size), 1) < 2).astype(BF)
        for h in range(heads):
            va_ref[:, h * LANES : h * LANES + size] = values[:, h * size : (h + 1) * size]
            va_ref[:, h * LANES + size : (h + 1) * LANES] = tail

        write()
        for h in range(heads):
            lanes = slice(h * LANES, (h + 1) * LANES)
            sums = mm(e_ref[h], va_ref[:, lanes])
            inverse = 1.0 / sums[:, size : size + 1]
            mixed = sums * inverse
            rb_ref[:, lanes] = jnp.broadcast_to(inverse, (length, LANES))
            mixf_ref[:, lanes] = jnp.where(
                lax.broadcasted_iota(jnp.int32, (length, LANES), 1) < size, mixed, 0.0
            )
            mixed_ref[:, h * size : (h + 1) * size] = mixed[:, :size].astype(BF)

    return run(
        kernel,
        "mixer_forward",
        (where,),
        (tokens, segments, e),
        (
            ((heads, length, length), BF),
            ((length, wide), BF),
            ((length, width), BF),
            ((length, wide), F32),
            ((length, wide), F32),
            ((length, model), BF),
            ((2, model), F32),
            ((model, width), BF),
        ),
        (
            pltpu.VMEM((2, UNITS, LANES), F32),
            pltpu.VMEM((heads * length, length), BF),
            pltpu.VMEM((UNITS, plan.fold, LANES), BF),
            pltpu.VMEM((length, length), F32),
            pltpu.SemaphoreType.DMA((UNITS, len(parts))),
            pltpu.SemaphoreType.DMA((UNITS, 1)),
        ),
        loose=units,
        aliases={3: 0},
    )


def second_weights(plan, where, cotangent, units, shares):
    length, model = cotangent.shape
    hidden, krows = plan.hidden, plan.krows
    piece = hidden // 3
    parts = plan.ffn_parts()

    def kernel(where_ref, cot_ref, *rest):
        out, gact, sem = rest[len(units) :]

        def target(m, owner):
            _, _, row, column, rows, columns = parts[m]
            return out.at[pl.ds(multiple(owner * krows + row, 16), rows), pl.ds(column, columns)]

        for copy in pick(rest[: len(units)], shares, where_ref, parts, target, sem):
            copy.wait()
        for j in range(3):
            cols = slice(j * piece, (j + 1) * piece)
            gact[:, cols] = mm(cot_ref[...], out[:, hidden + j * piece : hidden + (j + 1) * piece])

    return run(
        kernel,
        "second_weights",
        (where,),
        (cotangent,),
        (((model, 2 * hidden + model), BF), ((length, hidden), F32)),
        (pltpu.SemaphoreType.DMA((UNITS, len(parts))),),
        loose=units,
    )


def ffn_main(second, tokens, mixed_own, mixed_other, gact, gains, w, part, parts, pieces):
    length, model = tokens.shape
    width = mixed_own.shape[1]
    hidden = gact.shape[1]
    chunk = length // parts
    piece = hidden // 3
    at = slice(part * chunk, (part + 1) * chunk)

    def kernel(second_ref, tok_ref, own_ref, other_ref, gact_ref, gains_ref, w_ref,
               *rest):
        backs = rest[:pieces]
        resid_ref, n2_ref, act_ref, gpre_ref, mixed, acc = rest[pieces:]
        first = second_ref[0]
        mixed[:, pl.ds(multiple(first * width, LANES), width)] = own_ref[at, :]
        mixed[:, pl.ds(multiple((1 - first) * width, LANES), width)] = other_ref[at, :]
        attn = mm(mixed[...], w_ref[:, 2 * hidden :], NT)
        resid = tok_ref[at, :].astype(F32) + attn
        resid_ref[...] = resid
        inv = lax.rsqrt(jnp.mean(resid * resid, axis=-1, keepdims=True) + EPSILON)
        n2_ref[...] = (resid * inv * gains_ref[1:2, :]).astype(BF)
        for j in range(hidden // piece):
            cols = slice(j * piece, (j + 1) * piece)
            act, slope = gelu_pair(mm(n2_ref[...], w_ref[:, cols]))
            act_ref[:, cols] = act.astype(BF)
            gpre_ref[:, cols] = (gact_ref[at, cols] * slope).astype(BF)
            term = mm(gpre_ref[:, cols], w_ref[:, cols], NT)
            if j == 0:
                acc[...] = term
            else:
                acc[...] += term
        for n, back_ref in enumerate(backs):
            back_ref[...] = acc[n * (chunk // pieces) : (n + 1) * (chunk // pieces), :].astype(BF)

    return run(
        kernel,
        "ffn_main",
        (second,),
        (tokens, mixed_own, mixed_other, gact, gains, w),
        (
            *[((chunk // pieces, model), BF)] * pieces,
            ((chunk, model), F32),
            ((chunk, model), BF),
            ((chunk, hidden), BF),
            ((chunk, hidden), BF),
        ),
        (
            pltpu.VMEM((chunk, 2 * width), BF),
            pltpu.VMEM((chunk, model), F32),
        ),
    )


def late_groups():
    half = UNITS // 2
    far = half // 2
    groups = [[far + 1 - hop, far - 1 + hop] for hop in range(2, far + 1)]
    return groups + [[0]]


def late_place(k):
    return next((g, group.index(k)) for g, group in enumerate(late_groups()) if k in group)


def slots(refs):
    half = UNITS // 2
    keep, one, two, *later = refs
    columns = keep.shape[2]

    def slot(u):
        if u < half:
            return [(keep.at[u], 0, columns)]
        k = u - half
        if k == half // 2:
            return [(one, 0, columns // 2), (two, columns // 2, columns // 2)]
        group, place = late_place(k)
        return [(later[group].at[place], 0, columns)]

    return slot


def slot_shapes(rows, columns):
    early = ((rows, columns // 2), BF)
    later = [((len(group), rows, columns), BF) for group in late_groups()]
    return [((UNITS // 2, rows, columns), BF), early, early, *later]


SLOTS = 3 + len(late_groups())


def far_sum(far, keep, early, second):
    _, rows, columns = keep.shape
    half = columns // 2

    def kernel(keep_ref, early_ref, second_ref, up, down):
        for out, one, at in ((up, early_ref, slice(0, half)), (down, second_ref, slice(half, columns))):
            out[...] = (keep_ref[far, :, at].astype(F32) + one[...].astype(F32)).astype(BF)

    return run(kernel, "far_sum", (), (keep, early, second), [((rows, half), BF)] * 2)


def next_sums(far, keep, later, up, down):
    _, rows, columns = keep.shape
    half = columns // 2

    def kernel(keep_ref, later_ref, up_ref, down_ref, up_out, down_out):
        for out, one, k, mine in ((up_out, up_ref, far - 1, 0), (down_out, down_ref, far + 1, 1)):
            for n in range(2):
                at = slice(n * half, (n + 1) * half)
                total = keep_ref[k, :, at].astype(F32) + later_ref[late_place(k)[1], :, at].astype(F32)
                if n == mine:
                    total = total + one[...].astype(F32)
                out[:, at] = total.astype(BF)

    return run(kernel, "next_sums", (), (keep, later, up, down), [((rows, columns), BF)] * 2)


def result_kernel(name, keep, later, up, down, shapes, cut):
    def kernel(keep_ref, later_ref, up_ref, down_ref, *rest):
        outs, held, sem = rest[: len(shapes)], rest[len(shapes) : -1], rest[-1]

        def total(rows, columns):
            value = keep_ref[0, rows, columns].astype(F32) + later_ref[late_place(0)[1], rows, columns].astype(F32)
            return value + up_ref[rows, columns].astype(F32) + down_ref[rows, columns].astype(F32)

        copies = []
        for n, (out, to) in enumerate(zip(outs, held)):
            cut(n, to, total)
            copies.append(pltpu.make_async_copy(to, out, sem.at[n]))
            copies[-1].start()
        for copy in copies:
            copy.wait()

    return run(
        kernel,
        name,
        (),
        (keep, later, up, down),
        (),
        (*[pltpu.VMEM(shape, F32) for shape in shapes], pltpu.SemaphoreType.DMA((len(shapes),))),
        loose_outs=[(shape, F32) for shape in shapes],
    )


def ffn_result(keep, later, up, down):
    _, rows, columns = keep.shape
    half = columns // 2

    def cut(n, to, total):
        to[...] = total(slice(None), slice(n * half, (n + 1) * half))

    return result_kernel("ffn_result", keep, later, up, down, [(rows, half)] * 2, cut)


def mixer_result(keep, later, up, down, heads, krows, width):
    _, deep, length = keep.shape
    top = deep - 2 * krows
    rows = top // heads
    shapes = [(heads, rows, length), (krows, width), (krows, width), (1, krows), (1, krows)]

    def cut(n, to, total):
        if n == 0:
            for h in range(heads):
                to[h] = total(slice(h * rows, (h + 1) * rows), slice(None))
        elif n < 3:
            to[...] = total(slice(top + (n - 1) * krows, top + n * krows), slice(0, width))
        else:
            to[...] = total(slice(top, top + 16), slice(width, length))[n - 3 : n - 2, :krows]

    return result_kernel("mixer_result", keep, later, up, down, shapes, cut)


def ffn_grads(where, n2s, gpres, acts, cotangent):
    parts = len(n2s)
    chunk, model = n2s[0].shape
    hidden = acts[0].shape[1]
    krows = model // UNITS

    def kernel(where_ref, cot_ref, *rest):
        n2, gpre, act = rest[:parts], rest[parts : 2 * parts], rest[2 * parts : 3 * parts]
        slot = slots(rest[3 * parts : 3 * parts + SLOTS])
        scr, sem = rest[3 * parts + SLOTS :]
        piece = hidden // 3
        for j in range(3):
            cols = slice(j * piece, (j + 1) * piece)
            down = slice(hidden + j * piece, hidden + (j + 1) * piece)
            one = [mm(n2[r][...], gpre[r][:, cols], TN) for r in range(parts)]
            scr[:, cols] = sum(one).astype(BF)
            two = [mm(cot_ref[r * chunk : (r + 1) * chunk, :], act[r][:, cols], TN) for r in range(parts)]
            scr[:, down] = sum(two).astype(BF)
        copies = []
        for u in range(UNITS):
            at = pl.ds(multiple(where_ref[u] * krows, 16), krows)
            for n, (to, first, many) in enumerate(slot(u)):
                copies.append(pltpu.make_async_copy(scr.at[at, pl.ds(first, many)], to, sem.at[u, n]))
                copies[-1].start()
        for copy in copies:
            copy.wait()

    return run(
        kernel,
        "ffn_grads",
        (where,),
        (cotangent, *n2s, *gpres, *acts),
        (),
        (pltpu.VMEM((model, 2 * hidden), BF), pltpu.SemaphoreType.DMA((UNITS, 2))),
        loose_outs=slot_shapes(krows, 2 * hidden),
    )


def ffn_out(acts, w):
    chunk, hidden = acts[0].shape
    model = w.shape[0]

    def kernel(*refs):
        parts = len(refs) // 2
        for act, out in zip(refs[:parts], refs[parts + 1 :]):
            out[...] = mm(act[...], refs[parts][:, hidden : 2 * hidden], NT).astype(BF)

    return run(kernel, "ffn_out", (), (*acts, w), [((chunk, model), BF)] * len(acts))


def cut_gain(row, krows):
    model = row.shape[1]
    take = (
        lax.broadcasted_iota(jnp.int32, (model, LANES), 0) % krows
        == lax.broadcasted_iota(jnp.int32, (model, LANES), 1)
    ).astype(BF)
    own = (
        lax.broadcasted_iota(jnp.int32, (UNITS, model), 1) // krows
        == lax.broadcasted_iota(jnp.int32, (UNITS, model), 0)
    )
    high = row.astype(BF).astype(F32)
    pieces = mm(jnp.where(own, high, 0.0).astype(BF), take)
    return pieces + mm(jnp.where(own, row - high, 0.0).astype(BF), take)


def resid_back(second, backs, others, resids, cotangent, gains, w, mixf, heads, size):
    length, model = cotangent.shape
    wide = heads * LANES
    count = len(backs)
    krows = model // UNITS
    parts = len(resids)

    hidden = w.shape[1] - 2 * heads * size

    def kernel(second_ref, cot_ref, gains_ref, w_ref, mixf_ref, *rest):
        mine, other, res_refs = rest[:count], rest[count : 2 * count], rest[2 * count : 2 * count + parts]
        gres_ref, gat_ref, xh_ref, gf_ref, gm = rest[2 * count + parts :]
        total = jnp.zeros((8, model), F32)
        begin = 0
        for r in range(count):
            chunk = mine[r].shape[0]
            at = slice(begin, begin + chunk)
            g2 = mine[r][...].astype(F32) + other[r][...].astype(F32)
            whole = length // parts
            res = res_refs[begin // whole][begin % whole : begin % whole + chunk, :]
            begin += chunk
            inv = lax.rsqrt(jnp.mean(res * res, axis=-1, keepdims=True) + EPSILON)
            hat = res * inv
            total = total + jnp.sum((g2 * hat).reshape(chunk // 8, 8, model), axis=0)
            z = gains_ref[1:2, :] * g2
            corr = jnp.mean(z * hat, axis=-1, keepdims=True)
            gres = cot_ref[at, :].astype(F32) + inv * (z - hat * corr)
            gres_ref[at, :] = gres
            gat_ref[at, :] = gres.astype(BF)
        own = pl.ds(multiple(hidden + second_ref[0] * heads * size, LANES), heads * size)
        compact = mm(gat_ref[...], w_ref[:, own]).astype(BF)
        gm[...] = jnp.zeros_like(gm)
        for h in range(heads):
            gm[:, h * LANES : h * LANES + size] = compact[:, h * size : (h + 1) * size]
        lane = lax.broadcasted_iota(jnp.int32, (length, LANES), 1)
        for h in range(heads):
            lanes = slice(h * LANES, (h + 1) * LANES)
            here = gm[:, lanes].astype(F32)
            inner = -jnp.sum(here * mixf_ref[:, lanes], axis=-1, keepdims=True)
            high = inner.astype(BF).astype(F32)
            xh_ref[:, lanes] = jnp.where(
                lane == size, high, jnp.where(lane == size + 1, inner - high, here)
            ).astype(BF)
        gf_ref[...] = cut_gain(jnp.sum(total, axis=0, keepdims=True), krows)

    return run(
        kernel,
        "resid_back",
        (second,),
        (cotangent, gains, w, mixf, *backs, *others, *resids),
        (
            ((length, model), F32),
            ((length, model), BF),
            ((length, wide), BF),
            ((UNITS, LANES), F32),
        ),
        (pltpu.VMEM((length, wide), BF),),
    )


def score_grads(where_ref, xh_ref, va_ref, e_ref, rb_ref, ds, slot, begin, count, rows):
    length = ds.shape[0]

    def one_head(h, carry):
        lanes = pl.ds(multiple((begin + h) * LANES, LANES), LANES)
        d = mm(xh_ref[:, lanes], va_ref[:, lanes], NT)
        for q in range(length // LANES):
            cols = slice(q * LANES, (q + 1) * LANES)
            ds[:, cols] = (e_ref[begin + h, :, cols].astype(F32) * rb_ref[:, lanes] * d[:, cols]).astype(BF)
        for u in range(UNITS):
            at = pl.ds(multiple(where_ref[u] * rows, rows), rows)
            for to, first, many in slot(u):
                to[pl.ds(multiple(h * rows, rows), rows), :] = ds[at, first : first + many]
        return carry

    lax.fori_loop(0, count, one_head, 0)


def value_back(xh, rb, e, wv, tokens, size):
    length, model = tokens.shape
    heads = e.shape[0]
    width = heads * size
    chunk = length // 2
    krows = model // UNITS

    def kernel(xh_ref, rb_ref, e_ref, wv_ref, tok_ref, gv_ref, part_one, part_two, ga_ref, acc):
        acc[...] = jnp.zeros_like(acc)
        for h in range(heads):
            lanes = slice(h * LANES, (h + 1) * LANES)
            scaled = (xh_ref[:, lanes].astype(F32) * rb_ref[:, lanes]).astype(BF)
            gv_ref[:, h * size : (h + 1) * size] = mm(e_ref[h], scaled, TN)[:, :size].astype(BF)

        for r, part_ref in enumerate((part_one, part_two)):
            at = slice(r * chunk, (r + 1) * chunk)
            part = mm(gv_ref[at, :], wv_ref[...], NT)
            part_ref[...] = part.astype(BF)
            x = tok_ref[at, :].astype(F32)
            inv = lax.rsqrt(jnp.mean(x * x, axis=-1, keepdims=True) + EPSILON)
            acc[...] += jnp.sum((part * (x * inv)).reshape(chunk // 8, 8, model), axis=0)
        ga_ref[...] = cut_gain(jnp.sum(acc[...], axis=0, keepdims=True), krows)

    return run(
        kernel,
        "value_back",
        (),
        (xh, rb, e, wv, tokens),
        (
            ((length, width), BF),
            ((chunk, model), BF),
            ((chunk, model), BF),
            ((UNITS, LANES), F32),
        ),
        (pltpu.VMEM((8, model), F32),),
    )


def mixer_grads(where, xh, va, e, rb, krows):
    heads, length, _ = e.shape
    rows = length // UNITS
    deep = heads * rows + 2 * krows

    def kernel(where_ref, xh_ref, va_ref, e_ref, rb_ref, *rest):
        outs, ds = rest[:-1], rest[-1]
        score_grads(where_ref, xh_ref, va_ref, e_ref, rb_ref, ds, slots(outs), 0, heads, rows)
        for u in range(UNITS):
            for to, _, many in slots(outs)(u):
                to[heads * rows :, :] = jnp.zeros((2 * krows, many), BF)

    return run(
        kernel,
        "mixer_grads",
        (where,),
        (xh, va, e, rb),
        slot_shapes(deep, length),
        (pltpu.VMEM((length, length), BF),),
    )


def weight_grads(where, parts, n1, gv, gat, mixed, ga, ga_other, gf):
    model = n1.shape[1]
    width = gv.shape[1]
    krows = model // UNITS
    deep, length = parts[0].shape[1:]
    top = deep - 2 * krows

    def kernel(where_ref, n1_ref, gv_ref, gat_ref, mixed_ref, ga_ref, gb_ref, gf_ref, *rest):
        slot = slots(rest[SLOTS : 2 * SLOTS])
        wide_v, wide_o, pieces = rest[2 * SLOTS :]
        wide_v[:, :width] = mm(n1_ref[...], gv_ref[...], TN).astype(BF)
        wide_o[:, :width] = mm(gat_ref[...], mixed_ref[...], TN).astype(BF)
        wide_o[:, width:] = jnp.zeros((model, length - width), BF)
        pieces[0] = ga_ref[...] + gb_ref[...]
        pieces[1] = gf_ref[...]
        sub = lax.broadcasted_iota(jnp.int32, (krows, LANES), 0)
        for d in range(UNITS):
            both = jnp.where(
                sub == 0, pieces[0, d : d + 1, :], jnp.where(sub == 1, pieces[1, d : d + 1, :], 0.0)
            )
            wide_v[d * krows : (d + 1) * krows, width:] = both.astype(BF)
        for u in range(UNITS):
            at = pl.ds(multiple(where_ref[u] * krows, 16), krows)
            for to, first, many in slot(u):
                to[top : top + krows, :] = wide_v[at, first : first + many]
                to[top + krows :, :] = wide_o[at, first : first + many]

    return run(
        kernel,
        "weight_grads",
        (where,),
        (n1, gv, gat, mixed, ga, ga_other, gf, *parts),
        slot_shapes(deep, length),
        (
            pltpu.VMEM((model, length), BF),
            pltpu.VMEM((model, length), BF),
            pltpu.VMEM((2, UNITS, LANES), F32),
        ),
        aliases={8 + n: n for n in range(SLOTS)},
    )


class Ring:
    def __init__(self, size):
        self.size = size
        self.chips = size // 2
        n = self.chips
        self.order = list(range(0, n, 2)) + list(range(n - 1, 0, -2))
        me = lax.axis_index("dp")
        self.core = me % 2
        chip = me // 2
        self.at = jnp.where(chip % 2 == 0, chip // 2, n - 1 - chip // 2)
        self.up = self.pairs(1)
        self.down = self.pairs(-1)
        self.swap = [(d, d ^ 1) for d in range(size)]

    def pairs(self, step):
        n = self.chips
        return [
            (self.order[p] * 2 + c, self.order[(p + step) % n] * 2 + c) for p in range(n) for c in range(2)
        ]

    def device(self, offset, core):
        n = self.chips
        p = (self.at + jnp.asarray(offset, jnp.int32) + n) % n
        chip = jnp.where(p < (n + 1) // 2, 2 * p, 2 * (n - 1 - p) + 1)
        return chip * 2 + core

    def gathered(self):
        n = self.chips
        offsets = [0]
        for s in range(1, n // 2):
            offsets += [-s, s]
        offsets.append(n // 2)
        return jnp.concatenate([self.device(offsets, self.core), self.device(offsets, 1 - self.core)])

    def scattered(self):
        offsets = list(range(self.chips))
        return jnp.concatenate([self.device(offsets, self.core), self.device(offsets, 1 - self.core)])


class Gather:
    def __init__(self, ring, unit, cut):
        self.ring = ring
        self.rows = unit.shape[0]
        self.cut = cut
        self.last = [unit, unit]
        self.hops = 0
        self.mine = []
        self.theirs = []
        self.here = [unit]

    def values(self):
        return self.last

    def take(self, values):
        self.last = list(values)

    def hop(self):
        ring = self.ring
        self.hops += 1
        up, down = self.last
        if self.hops == ring.chips // 2:
            up, down = up[: self.cut], down[self.cut :]
        self.last = [lax.ppermute(up, "dp", ring.up), lax.ppermute(down, "dp", ring.down)]
        self.swap()
        self.here = self.last

    def swap(self):
        self.theirs += [lax.ppermute(one, "dp", self.ring.swap) for one in self.here]
        self.mine += self.here
        self.here = []

    def finish(self):
        self.swap()
        return self.mine + self.theirs

    def shares(self):
        n = self.ring.chips
        own = [(u, 0, self.rows) for u in range(n - 1)]
        own += [(n - 1, 0, self.cut), (n - 1, self.cut, self.rows - self.cut)]
        return own + [(u + n, first, rows) for u, first, rows in own]


class Scatter:
    def __init__(self, ring, keep, *give):
        self.ring = ring
        self.keep = keep
        early, self.later = give[:2], list(give[2:])
        self.early = [lax.ppermute(one, "dp", ring.swap) for one in early]
        self.last = []
        self.hops = 0

    def values(self):
        return self.last if self.hops else self.early

    def take(self, values):
        if self.hops:
            self.last = list(values)
        else:
            self.early = list(values)

    def total(self, k, one):
        group, place = late_place(k)
        got = self.later[group][place]
        return (self.keep[k].astype(F32) + got.astype(F32) + one.astype(F32)).astype(BF)

    def hop(self):
        ring = self.ring
        far = ring.chips // 2
        self.hops += 1
        if self.hops == 1:
            up, down = far_sum(far, self.keep, *self.early)
            self.later = [lax.ppermute(tie(one, up), "dp", ring.swap) for one in self.later]
        elif self.hops == 2:
            up, down = next_sums(far, self.keep, self.later[0], *self.last)
        else:
            up = self.total(far + 1 - self.hops, self.last[0])
            down = self.total(far - 1 + self.hops, self.last[1])
        self.last = [lax.ppermute(up, "dp", ring.up), lax.ppermute(down, "dp", ring.down)]

    def result(self):
        return self.keep, self.later[-1], *self.last


def together(chains, *more):
    values = [one for chain in chains for one in chain.values()]
    tied = lax.optimization_barrier(tuple(values) + more)
    at = 0
    for chain in chains:
        count = len(chain.values())
        chain.take(tied[at : at + count])
        at += count
    return tied[at:]


def tie(value, *after):
    return lax.optimization_barrier((value,) + after)[0] if after else value


def shards(
    tokens,
    segment_ids,
    gain_attn,
    gain_ffn,
    random_scores,
    w_value,
    w_output,
    w_up,
    w_down,
    cotangent,
):
    devices = lax.axis_size("dp")
    second = lax.axis_index("mp")
    length = segment_ids.shape[1]
    heads = random_scores.shape[0]
    model = tokens.shape[1]
    width = w_value.shape[1]
    size = width // heads
    rows = length // UNITS
    krows = model // UNITS
    ring = devices == UNITS and devices // 2 <= RING_CHIPS
    flip = [(0, 1), (1, 0)]
    second_at = jnp.reshape(second, (1,)).astype(jnp.int32)
    plan = Unit(heads, rows, krows, length, model, width, w_up.shape[1])

    if ring:
        net = Ring(devices)
        far = net.chips // 2
        where_in = net.gathered().astype(jnp.int32)
        where_out = net.scattered().astype(jnp.int32)
        wo_other = lax.ppermute(w_output.T, "mp", flip)
        unit = pack_unit(plan, random_scores, w_up, w_down.T)
        unit = pack_rest(plan, second_at, unit, w_value, gain_attn, gain_ffn, w_output.T, wo_other)
        one = Gather(net, unit, plan.cut)
        one.hop()
        where_in, where_out = together([one], where_in, where_out)
        for step in range(1, far - 1):
            one.hop()
            together([one])
        there = one.mine + one.theirs
        shares = one.shares()
        half = len(shares) // 2
        early = [n for n in range(len(one.mine))] + [half + n for n in range(len(one.theirs))]
        one.hop()
        e = mixer_first(plan, where_in, segment_ids, there, [shares[n] for n in early], heads)
        (e,) = together([one], e)
        units = one.finish()
        late = [n for n in range(len(shares)) if n not in early]
    else:
        where_in = jnp.arange(UNITS, dtype=jnp.int32)
        where_out = where_in

        def gather(one, axis=0):
            return lax.all_gather(one.astype(BF), "dp", axis=axis, tiled=True)

        wo_own = w_output.T.astype(BF)
        wo_other = lax.ppermute(wo_own, "mp", flip)
        halves = [jnp.where(second == n, wo_own, wo_other) for n in range(2)]
        scores = gather(random_scores, 1).reshape(heads, UNITS, rows, length).transpose(1, 0, 2, 3)
        wide = [gather(one) for one in (w_value, *halves)]
        wide = jnp.concatenate(wide, axis=1).reshape(UNITS, krows, plan.wide)
        ffn = jnp.concatenate([gather(w_up), gather(w_down.T)], axis=1).reshape(UNITS, krows, -1)
        stack = [scores.reshape(UNITS, heads * rows, length)]
        for kind, column in plan.blocks:
            stack.append((ffn if kind == "ffn" else wide)[:, :, column : column + length])
        gains = jnp.stack([gather(gain_attn), gather(gain_ffn)]).reshape(2, UNITS, krows).transpose(1, 0, 2)
        gains = jnp.pad(gains, ((0, 0), (0, plan.fold - 2), (0, length - plan.gain_lane - krows)))
        tail = wide[:, :, plan.wide - plan.tail :].reshape(UNITS, 3, plan.fold, plan.tail)
        stack.append(jnp.concatenate([tail[:, 0], tail[:, 1], tail[:, 2], gains], axis=2))
        whole = jnp.concatenate(stack, axis=1)
        units = [whole[u] for u in range(UNITS)]
        shares = [(u, 0, plan.deep) for u in range(UNITS)]
        early, late = list(range(UNITS // 2)), list(range(UNITS // 2, UNITS))
        e = mixer_first(plan, where_in, segment_ids, units[: UNITS // 2], shares[: UNITS // 2], heads)

    e, va, mixed, mixf, rb, n1, gains, wv = mixer_forward(
        plan, where_in, tokens, segment_ids, e, units, shares, late, heads, width
    )
    mixed_other = lax.ppermute(mixed, "mp", flip)
    w, gact = second_weights(plan, where_in, cotangent, units, shares)
    backs, others, resids, n2s, acts, gpres = [], [], [], [], [], []
    for part in range(PARTS):
        *new, resid, n2, act, gpre = ffn_main(
            second_at, tokens, mixed, mixed_other, gact, gains, w, part, PARTS, 1
        )
        for back in new:
            backs.append(back)
            others.append(lax.ppermute(tie(back, *others[-1:]), "mp", flip))
        resids.append(resid)
        n2s.append(n2)
        acts.append(act)
        gpres.append(gpre)
    parts_two = ffn_grads(where_out, n2s, gpres, acts, cotangent)
    ffn = list(ffn_out(acts, w))
    ffn_other = []
    if ring:
        ffn_sum = Scatter(net, *parts_two)
        ffn_sum.hop()
        ffn_sum.hop()
        cotangent, *both = lax.optimization_barrier((cotangent, *ffn, *others))
        ffn, others = both[:PARTS], both[PARTS:]
        ffn_other.append(lax.ppermute(ffn[0], "mp", flip))
    gres, gat, xh, gf = resid_back(
        second_at, backs, others, resids, cotangent, gains, w, mixf, heads, size
    )
    gv, part_one, part_two, ga = value_back(xh, rb, e, wv, tokens, size)
    ga_other = lax.ppermute(ga, "mp", flip)
    if ring:
        ffn_other[0], ffn[1] = together([ffn_sum], ffn_other[0], ffn[1])
        ffn_sum.hop()
        ffn_other.append(lax.ppermute(ffn[1], "mp", flip))
    parts_one = mixer_grads(where_out, xh, va, e, rb, krows)
    parts_one = weight_grads(where_out, parts_one, n1, gv, gat, mixed, ga, ga_other, gf)

    top = heads * rows
    if ring:
        score_sum = Scatter(net, *parts_one)
        ffn_other[1], part_one = together([ffn_sum, score_sum], ffn_other[1], part_one)
        ffn_sum.hop()
        score_sum.hop()
        part_other = [lax.ppermute(part_one, "mp", flip)]
        part_other[0], part_two = together([ffn_sum, score_sum], part_other[0], part_two)
        score_sum.hop()
        part_other.append(lax.ppermute(part_two, "mp", flip))
        together([score_sum])
        score_sum.hop()
        out_up, out_down = ffn_result(*ffn_sum.result())
        (part_other[1],) = together([score_sum], part_other[1])
        score_sum.hop()
        out_scores, out_value, out_output, *out_gains = mixer_result(*score_sum.result(), heads, krows, width)
        out_down, out_output = out_down.T, out_output.T
        out_gain_one, out_gain_two = [one.reshape(krows) for one in out_gains]
    else:
        ffn_other = [lax.ppermute(one, "mp", flip) for one in ffn]
        part_other = [lax.ppermute(one, "mp", flip) for one in (part_one, part_two)]

        def scatter(one, axis=0):
            return lax.psum_scatter(one, "dp", scatter_dimension=axis, tiled=True)

        def whole(keep, early, second, *later):
            far = UNITS // 4
            given = []
            for k in range(UNITS // 2):
                group, place = late_place(k) if k != far else (0, 0)
                one = later[group][place] if k != far else jnp.concatenate([early, second], axis=1)
                given.append(one)
            return jnp.concatenate([keep, jnp.stack(given)]).astype(F32)

        two = whole(*parts_two).reshape(model, -1)
        one = whole(*parts_one)
        out_up = scatter(two[:, : two.shape[1] // 2])
        out_down = scatter(two[:, two.shape[1] // 2 :]).T
        scores = one[:, :top].reshape(UNITS, heads, rows, length).transpose(1, 0, 2, 3)
        out_scores = scatter(scores.reshape(heads, length, length), 1)
        out_value = scatter(one[:, top : top + krows, :width].reshape(model, width))
        out_output = scatter(one[:, top + krows :, :width].reshape(model, width)).T
        out_gain_one = scatter(one[:, top, width : width + krows].reshape(model))
        out_gain_two = scatter(one[:, top + 1, width : width + krows].reshape(model))
    outputs = [
        (resid + (mine.astype(F32) + other.astype(F32))).astype(BF)
        for resid, mine, other in zip(resids, ffn, ffn_other)
    ]
    output = jnp.concatenate(outputs)
    backs = []
    for r, (mine, other) in enumerate(zip((part_one, part_two), part_other)):
        grad_n1 = mine.astype(F32) + other.astype(F32)
        at = slice(r * mine.shape[0], (r + 1) * mine.shape[0])
        x = tokens[at].astype(F32)
        inv = lax.rsqrt(jnp.mean(x * x, axis=-1, keepdims=True) + EPSILON)
        z = gains[0:1, :] * grad_n1
        hat = x * inv
        backs.append((gres[at] + inv * (z - hat * jnp.mean(z * hat, axis=-1, keepdims=True))).astype(BF))
    grad_tokens = jnp.concatenate(backs)
    return (
        output,
        grad_tokens,
        out_gain_one,
        out_gain_two,
        out_scores,
        out_value,
        out_output,
        out_up,
        out_down,
    )


def solution(mesh):
    in_specs = (
        P("dp", None),
        P("dp", None),
        P("dp"),
        P("dp"),
        P("mp", "dp", None),
        P("dp", "mp"),
        P("mp", "dp"),
        P("dp", "mp"),
        P("mp", "dp"),
        P("dp", None),
    )
    out_specs = (
        P("dp", None),
        P("dp", None),
        P("dp"),
        P("dp"),
        P("mp", "dp", None),
        P("dp", "mp"),
        P("mp", "dp"),
        P("dp", "mp"),
        P("mp", "dp"),
    )
    return jax.shard_map(shards, mesh=mesh, in_specs=in_specs, out_specs=out_specs, check_vma=False)
```

time: 197 us -> 177 us (0.90)
  starting transfers between devices: 57.1 us -> 41.7 us
  waiting for transfers between devices: 90 us -> 85.7 us
  Pallas kernels: 37.3 us -> 40.2 us
    ppermute x46 -> x43, starting transfers between devices: 49.1 us -> 37.5 us  [the longest x12 16.8 us: hop(): lax.ppermute(down, 'dp', ring.down)]
    ppermute x46 -> x43, waiting for transfers between devices: 87.2 us -> 82 us  [the longest x12 34.3 us: hop(): lax.ppermute(up, 'dp', ring.up)]
    ppermute x24 -> x9, starting transfers between devices: 4.92 us -> 1.12 us  [swap(): lax.ppermute(one, 'dp', self.ring.swap)]
    ppermute x1, waiting for transfers between devices: 0.01 us -> 3.61 us  [shards(): mixed_other = lax.ppermute(mixed, 'mp', flip)]
    pallas_call x13 -> x19, Pallas kernels: 37.3 us -> 40.2 us  [run(): pl.pallas_call(kernel, out_shape=tuple(results), in_specs=specs, out_spec...]
    convert_element_type x10 -> x7, other arithmetic: 4.05 us -> 1.77 us  [the longest x4 0.91 us: total(): (self.keep[k].astype(F32) + got.astype(F32) + one.astype(F32)).astype(BF)]
    ppermute x1, waiting for transfers between devices: 2.13 us -> 0.01 us  [shards(): ga_other = lax.ppermute(ga, 'mp', flip)]
  transfers between devices with their start and end apart: 72 -> 54, of which waited for: 27 -> 24; matrix products, arithmetic and copies ran while one was open for 3% -> 3% of each run, Pallas kernels for 12% -> 17%
where the time goes in v3:
time: 177 us; the launch traced here: 176 us
  waiting for transfers between devices  85.7 us (48%)
  starting transfers between devices  41.7 us (24%)
  Pallas kernels  40.2 us (23%)
  other arithmetic  4.59 us (3%)
  local copies, waits for them, and re-layouts  2.79 us (2%)
    pallas_call x19, Pallas kernels, run(): pl.pallas_call(kernel, out_shape=tuple(results), in_specs=specs, out_spec...  40.2 us
    ppermute x12, waiting for transfers between devices, hop(): lax.ppermute(up, 'dp', ring.up)  34.3 us
    ppermute x12, waiting for transfers between devices, hop(): lax.ppermute(down, 'dp', ring.down)  33.4 us
    ppermute x12, starting transfers between devices, hop(): lax.ppermute(down, 'dp', ring.down)  16.8 us
    ppermute x12, starting transfers between devices, hop(): lax.ppermute(up, 'dp', ring.up)  9.72 us
    ppermute x2, waiting for transfers between devices, shards(): others.append(lax.ppermute(tie(back, *others[-1:]), 'mp', flip))  6.97 us
    ppermute x1, waiting for transfers between devices, shards(): part_other.append(lax.ppermute(part_two, 'mp', flip))  3.61 us
    ppermute x1, waiting for transfers between devices, shards(): mixed_other = lax.ppermute(mixed, 'mp', flip)  3.61 us
  transfers between devices with their start and end apart: 54, of which 24 were waited for; matrix products, arithmetic and copies ran while one was open for 3% of the time, Pallas kernels for 17%

profile of v3, /device:TPU:0, one launch (start us, length us, event | category | flops | bytes accessed | tf_op | source)
XLA Modules:
  0.0 176.4 jit_solution(11236142060541485418)
XLA Ops:
  0.7 3.0 %collective-permute-start = (f32[48,384]{1,0:T(8,128)}, f32[48,384]{1,0:T(8,128)S(1)}, u32[]{:S(2)}, u32[]{:S(2)}) collective-permute-start(f32[48,384]{1,0:T(8,128)} %bitcast.42), channel_id=1, source_target_pairs={{0,1},{1,0},{2,3},{3,2},{4,5},{5,4},{6,7},{7,6},{8,9},{9,8},{10,11... | collective-permute-start | bytes 221192 | tf_op jit(solution)/shard_map/ppermute | solution.py:948
  3.7 1.2 pack_unit.1.old
  5.0 1.2 collective-permute-done.other_ref
  6.2 1.0 pack_rest.1.rest_0_
  7.3 2.0 %collective-permute-start.2 = (bf16[592,512]{1,0:T(8,128)(2,1)S(1)}, bf16[592,512]{1,0:T(8,128)(2,1)S(1)}, u32[]{:S(2)}, u32[]{:S(2)}) collective-permute-start(bf16[592,512]{1,0:T(8,128)(2,1)S(1)} %pack_rest.1.rest_0_), channel_id=1, source_target_pairs={{0,4},{2,6},{8,0},{10,2},{16,8},{18,10},{24,16},{26,18},{28,24},{3... | collective-permute-start | bytes 1818632 | tf_op jit(solution)/shard_map/ppermute | solution.py:841
  9.7 12.3 %collective-permute-done.2.rest_2_ = bf16[592,512]{1,0:T(8,128)(2,1)S(1)} collective-permute-done((bf16[592,512]{1,0:T(8,128)(2,1)S(1)}, bf16[592,512]{1,0:T(8,128)(2,1)S(1)}, u32[]{:S(2)}, u32[]{:S(2)}) %collective-permute-start.2) | collective-permute-done | bytes 606240 | tf_op jit(solution)/shard_map/ppermute | solution.py:841
  21.9 1.4 collective-permute-done.1.rest_1_
  23.7 1.6 collective-permute-start.4
  25.3 11.4 %collective-permute-done.3.rest_3_ = bf16[592,512]{1,0:T(8,128)(2,1)S(1)} collective-permute-done((bf16[592,512]{1,0:T(8,128)(2,1)S(1)}, bf16[592,512]{1,0:T(8,128)(2,1)S(1)}, u32[]{:S(2)}, u32[]{:S(2)}) %collective-permute-start.3) | collective-permute-done | bytes 606240 | tf_op jit(solution)/shard_map/ppermute | solution.py:841
  36.8 1.6 collective-permute-start.5
  39.4 10.0 %collective-permute-done.5.rest_5_ = bf16[592,512]{1,0:T(8,128)(2,1)S(1)} collective-permute-done((bf16[592,512]{1,0:T(8,128)(2,1)S(1)}, bf16[592,512]{1,0:T(8,128)(2,1)S(1)}, u32[]{:S(2)}, u32[]{:S(2)}) %collective-permute-start.5) | collective-permute-done | bytes 606240 | tf_op jit(solution)/shard_map/ppermute | solution.py:841
  49.4 0.8 collective-permute-done.6.rest_6_
  50.2 1.0 collective-permute-start.8
  51.9 1.1 collective-permute-start.7
  53.0 6.3 %collective-permute-done.8.rest_8_ = bf16[304,512]{1,0:T(8,128)(2,1)S(1)} collective-permute-done((bf16[304,512]{1,0:T(8,128)(2,1)S(1)}, bf16[304,512]{1,0:T(8,128)(2,1)S(1)}, u32[]{:S(2)}, u32[]{:S(2)}) %collective-permute-start.8) | collective-permute-done | bytes 311328 | tf_op jit(solution)/shard_map/ppermute | solution.py:841
  59.2 2.0 %collective-permute-done.7.rest_7_ = bf16[288,512]{1,0:T(8,128)(2,1)S(1)} collective-permute-done((bf16[288,512]{1,0:T(8,128)(2,1)S(1)}, bf16[288,512]{1,0:T(8,128)(2,1)S(1)}, u32[]{:S(2)}, u32[]{:S(2)}) %collective-permute-start.7) | collective-permute-done | bytes 294944 | tf_op jit(solution)/shard_map/ppermute | solution.py:841
  61.4 0.8 copy-done.12
  62.2 3.0 %mixer_first.1.e_old = bf16[6,512,512]{2,1,0:T(8,128)(2,1)S(1)} custom-call(s32[16]{0:T(128)S(1)} %pad_add_fusion.where_ref, s32[1,512]{1,0:T(1,128)S(1)} %copy-done.3, bf16[592,512]{1,0:T(8,128)(2,1)} %copy-done.1, bf16[592,512]{1,0:T(8,128)(2,1)} %copy-done.5, bf16[592,512]{1,0:T(8,128)(2,1)} %copy-done.4, bf16[592,512]{1,0:T(8,128)(2,1)} %copy-done.6, ...), custom_call_target="tpu_custom_call" | custom-call | flops 1 | bytes 1 | tf_op jit(solution)/shard_map/mixer_first/pallas_call | solution.py:35
  67.2 4.9 %mixer_forward.1 = (bf16[6,512,512]{2,1,0:T(8,128)(2,1)S(1)}, bf16[512,768]{1,0:T(8,128)(2,1)S(1)}, bf16[512,384]{1,0:T(8,128)(2,1)S(1)}, f32[512,768]{1,0:T(8,1...) custom-call(s32[16]{0:T(128)S(1)} %pad_add_fusion.where_ref, ...), custom_call_target="tpu_custom_call", output_to_operand_aliasing={{0}: (3, {})} | custom-call | flops 1 | bytes 1 | tf_op jit(solution)/shard_map/mixer_forward/pallas_call | solution.py:35
  72.1 1.6 collective-permute-start.18
  73.7 6.4 %second_weights.1 = (bf16[768,3840]{1,0:T(8,128)(2,1)S(1)}, f32[512,1536]{1,0:T(8,128)S(1)}) custom-call(s32[16]{0:T(128)S(1)} %pad_add_fusion.where_ref, bf16[512,768]{1,0:T(8,128)(2,1)S(1)} %copy-done.2, bf16[592,512]{1,0:T(8,128)(2,1)} %copy-done.1, bf16[592,512]{1,0:T(8,128)(2,1)} %copy-done.5, bf16[592,512]{1,0:T(8,128)(2,1)} %copy-done.4, ...), custom_call_target="tpu_custom_call" | custom-call | flops 1 | bytes 1 | tf_op jit(solution)/shard_map/second_weights/pallas_call | solution.py:35
  80.1 3.6 %collective-permute-done.18.other_ref = bf16[512,384]{1,0:T(8,128)(2,1)S(1)} collective-permute-done((bf16[512,384]{1,0:T(8,128)(2,1)S(1)}, bf16[512,384]{1,0:T(8,128)(2,1)S(1)}, u32[]{:S(2)}, u32[]{:S(2)}) %collective-permute-start.18) | collective-permute-done | bytes 393248 | tf_op jit(solution)/shard_map/ppermute | solution.py:996
  83.7 3.1 %ffn_main.2 = (bf16[256,768]{1,0:T(8,128)(2,1)S(1)}, f32[256,768]{1,0:T(8,128)S(1)}, bf16[256,768]{1,0:T(8,128)(2,1)S(1)}, bf16[256,1536]{1,0:T(8,128)(2,1)S(1)}, bf16[256,1536]{1,0:T(8,128)(2,1)S(1)}) custom-call(s32[1]{0:T(128)} %bitcast.second_ref, bf16[512,768]{1,0:T(8,128)(2,1)S(1)} %copy-done, ...), custom_call_target="tpu_custom_call" | custom-call | flops 1 | bytes 1 | tf_op jit(solution)/shard_map/ffn_main/pallas_call | solution.py:35
  86.8 1.6 collective-permute-start.19
  88.3 3.1 %ffn_main.3 = (bf16[256,768]{1,0:T(8,128)(2,1)S(1)}, f32[256,768]{1,0:T(8,128)S(1)}, bf16[256,768]{1,0:T(8,128)(2,1)S(1)}, bf16[256,1536]{1,0:T(8,128)(2,1)S(1)}, bf16[256,1536]{1,0:T(8,128)(2,1)S(1)}) custom-call(s32[1]{0:T(128)} %bitcast.second_ref, bf16[512,768]{1,0:T(8,128)(2,1)S(1)} %copy-done, ...), custom_call_target="tpu_custom_call" | custom-call | flops 1 | bytes 1 | tf_op jit(solution)/shard_map/ffn_main/pallas_call | solution.py:35
  91.4 4.7 %ffn_grads.1 = (bf16[8,48,3072]{2,1,0:T(8,128)(2,1)S(1)}, bf16[48,1536]{1,0:T(8,128)(2,1)S(1)}, bf16[48,1536]{1,0:T(8,128)(2,1)S(1)}, bf16[2,48,3072]{2,1,0:T(8,...) custom-call(s32[16]{0:T(128)S(1)} %pad_add_fusion.1.where_ref, ...), custom_call_target="tpu_custom_call" | custom-call | flops 1 | bytes 1 | tf_op jit(solution)/shard_map/ffn_grads/pallas_call | solution.py:35
  96.7 0.9 collective-permute-done.21.early_ref
  98.2 0.8 collective-permute-start.20
  99.1 1.6 collective-permute-start.25
  101.1 1.4 ffn_out.1
  102.5 7.0 %collective-permute-done.20.rest_3_ = bf16[256,768]{1,0:T(8,128)(2,1)S(1)} collective-permute-done((bf16[256,768]{1,0:T(8,128)(2,1)S(1)}, bf16[256,768]{1,0:T(8,128)(2,1)S(1)}, u32[]{:S(2)}, u32[]{:S(2)}) %collective-permute-start.20) | collective-permute-done | bytes 393248 | tf_op jit(solution)/shard_map/ppermute | solution.py:1005
  110.2 1.1 collective-permute-start.26
  111.3 1.0 collective-permute-start.27
  112.3 2.9 %resid_back.1 = (f32[512,768]{1,0:T(8,128)S(1)}, bf16[512,768]{1,0:T(8,128)(2,1)S(1)}, bf16[512,768]{1,0:T(8,128)(2,1)S(1)}, f32[16,128]{1,0:T(8,128)S(1)}) custom-call(s32[1]{0:T(128)} %bitcast.second_ref, bf16[512,768]{1,0:T(8,128)(2,1)S(1)} %copy-done.2, f32[2,768]{1,0:T(2,128)S(1)} %get-tuple-element.129.gains_ref, ...), custom_call_target="tpu_custom_call" | custom-call | flops 1 | bytes 1 | tf_op jit(solution)/shard_map/resid_back/pallas_call | solution.py:35
  115.2 1.8 %value_back.1 = (bf16[512,384]{1,0:T(8,128)(2,1)S(1)}, bf16[256,768]{1,0:T(8,128)(2,1)S(1)}, bf16[256,768]{1,0:T(8,128)(2,1)S(1)}, f32[16,128]{1,0:T(8,128)S(1)}) custom-call(bf16[512,768]{1,0:T(8,128)(2,1)S(1)} %get-tuple-element.167.xh_ref, f32[512,768]{1,0:T(8,128)S(1)} %get-tuple-element.168.rb_ref, bf16[6,512,512]{2,1,0:T(8,128)(2,1)S(1)} %get-tuple-element.169.e_ref, ...), custom_call_target="tpu_custom_call" | custom-call | flops 1 | bytes 1 | tf_op jit(solution)/shard_map/value_back/pallas_call | solution.py:35
  117.0 1.6 collective-permute-start.32
  118.6 2.7 %mixer_grads.1 = (bf16[8,288,512]{2,1,0:T(8,128)(2,1)S(1)}, bf16[288,256]{1,0:T(8,128)(2,1)S(1)}, bf16[288,256]{1,0:T(8,128)(2,1)S(1)}, bf16[2,288,512]{2,1,0:T(...) custom-call(s32[16]{0:T(128)S(1)} %pad_add_fusion.1.where_ref, ...), custom_call_target="tpu_custom_call" | custom-call | flops 1 | bytes 1 | tf_op jit(solution)/shard_map/mixer_grads/pallas_call | solution.py:35
  121.3 1.6 weight_grads.1
  123.5 0.9 collective-permute-start.35
  124.7 1.6 collective-permute-start.31
  126.8 1.4 collective-permute-done.34.second_ref
  128.1 5.3 %collective-permute-done.31 = bf16[48,3072]{1,0:T(8,128)(2,1)S(1)} collective-permute-done((bf16[48,3072]{1,0:T(8,128)(2,1)S(1)}, bf16[48,3072]{1,0:T(8,128)(2,1)S(1)}, u32[]{:S(2)}, u32[]{:S(2)}) %collective-permute-start.31) | collective-permute-done | bytes 294944 | tf_op jit(solution)/shard_map/ppermute | solution.py:896
  133.5 1.3 collective-permute-done.30
  134.8 1.0 collective-permute-start.39
  135.8 1.1 collective-permute-start.40
  136.9 1.1 collective-permute-start.41
  138.3 1.6 collective-permute-start.38
  139.9 1.1 collective-permute-done.40.down_ref
  140.9 2.0 %collective-permute-start.37 = (bf16[48,3072]{1,0:T(8,128)(2,1)S(1)}, bf16[48,3072]{1,0:T(8,128)(2,1)S(1)}, u32[]{:S(2)}, u32[]{:S(2)}) collective-permute-start(bf16[48,3072]{1,0:T(8,128)(2,1)S(1)} %get-tuple-element.240), channel_id=1, source_target_pairs={{0,8},{2,10},{8,16},{10,18},{16,24},{18,26},{24,28},{26,30},{28,20... | collective-permute-start | bytes 884744 | tf_op jit(solution)/shard_map/ppermute | solution.py:896
  143.2 4.5 %collective-permute-done.38.down_ref = bf16[48,3072]{1,0:T(8,128)(2,1)S(1)} collective-permute-done((bf16[48,3072]{1,0:T(8,128)(2,1)S(1)}, bf16[48,3072]{1,0:T(8,128)(2,1)S(1)}, u32[]{:S(2)}, u32[]{:S(2)}) %collective-permute-start.38) | collective-permute-done | bytes 294944 | tf_op jit(solution)/shard_map/ppermute | solution.py:896
  147.7 1.3 collective-permute-done.37.up_ref
  149.9 1.4 collective-permute-start.45
  152.1 4.7 %collective-permute-done.44 = bf16[288,512]{1,0:T(8,128)(2,1)S(1)} collective-permute-done((bf16[288,512]{1,0:T(8,128)(2,1)S(1)}, bf16[288,512]{1,0:T(8,128)(2,1)S(1)}, u32[]{:S(2)}, u32[]{:S(2)}) %collective-permute-start.44) | collective-permute-done | bytes 294944 | tf_op jit(solution)/shard_map/ppermute | solution.py:896
  156.8 0.8 collective-permute-start.48
  157.8 1.7 collective-permute-start.47
  160.0 0.9 pad_maximum_fusion
  160.9 0.9 ffn_result.1
  161.8 3.6 %collective-permute-done.48 = bf16[256,768]{1,0:T(8,128)(2,1)S(1)} collective-permute-done((bf16[256,768]{1,0:T(8,128)(2,1)S(1)}, bf16[256,768]{1,0:T(8,128)(2,1)S(1)}, u32[]{:S(2)}, u32[]{:S(2)}) %collective-permute-start.48) | collective-permute-done | bytes 393248 | tf_op jit(solution)/shard_map/ppermute | solution.py:1041
  165.4 0.8 collective-permute-done.46
  167.0 1.5 collective-permute-start.52
  169.7 0.9 pad_maximum_fusion.1
  170.6 3.2 %collective-permute-done.52.down_ref = bf16[288,512]{1,0:T(8,128)(2,1)S(1)} collective-permute-done((bf16[288,512]{1,0:T(8,128)(2,1)S(1)}, bf16[288,512]{1,0:T(8,128)(2,1)S(1)}, u32[]{:S(2)}, u32[]{:S(2)}) %collective-permute-start.52) | collective-permute-done | bytes 294944 | tf_op jit(solution)/shard_map/ppermute | solution.py:896
  173.8 1.5 collective-permute-done.51.up_ref
  175.3 0.9 mixer_result.1
  (129 shorter events, 12.9 us)
Async XLA Ops:
  0.7 61.6 %copy-start.3 = (s32[1,512]{1,0:T(1,128)S(1)}, s32[1,512]{1,0:T(1,128)}, u32[]{:S(2)}) copy-start(s32[1,512]{1,0:T(1,128)} %seg_ref.3) | copy-start | bytes 6148
  0.7 5.6 %collective-permute-start = (f32[48,384]{1,0:T(8,128)}, f32[48,384]{1,0:T(8,128)S(1)}, u32[]{:S(2)}, u32[]{:S(2)}) collective-permute-start(f32[48,384]{1,0:T(8,128)} %bitcast.42), channel_id=1, source_target_pairs={{0,1},{1,0},{2,3},{3,2},{4,5},{5,4},{6,7},{7,6},{8,9},{9,8},{10,11... | collective-permute-start | bytes 221192 | tf_op jit(solution)/shard_map/ppermute | solution.py:948
  7.3 54.0 %copy-start.1 = (bf16[592,512]{1,0:T(8,128)(2,1)}, bf16[592,512]{1,0:T(8,128)(2,1)S(1)}, u32[]{:S(2)}) copy-start(bf16[592,512]{1,0:T(8,128)(2,1)S(1)} %pack_rest.1.rest_0_) | copy-start | bytes 1818628
  7.3 14.7 %collective-permute-start.2 = (bf16[592,512]{1,0:T(8,128)(2,1)S(1)}, bf16[592,512]{1,0:T(8,128)(2,1)S(1)}, u32[]{:S(2)}, u32[]{:S(2)}) collective-permute-start(bf16[592,512]{1,0:T(8,128)(2,1)S(1)} %pack_rest.1.rest_0_), channel_id=1, source_target_pairs={{0,4},{2,6},{8,0},{10,2},{16,8},{18,10},{24,16},{26,18},{28,24},{3... | collective-permute-start | bytes 1818632 | tf_op jit(solution)/shard_map/ppermute | solution.py:841
  9.3 14.0 %collective-permute-start.1 = (bf16[592,512]{1,0:T(8,128)(2,1)S(1)}, bf16[592,512]{1,0:T(8,128)(2,1)S(1)}, u32[]{:S(2)}, u32[]{:S(2)}) collective-permute-start(bf16[592,512]{1,0:T(8,128)(2,1)S(1)} %pack_rest.1.rest_0_), channel_id=1, source_target_pairs={{0,8},{2,10},{8,16},{10,18},{16,24},{18,26},{24,28},{26,30},{28,20... | collective-permute-start | bytes 1818632 | tf_op jit(solution)/shard_map/ppermute | solution.py:841
  21.9 39.4 %copy-start.4 = (bf16[592,512]{1,0:T(8,128)(2,1)}, bf16[592,512]{1,0:T(8,128)(2,1)S(1)}, u32[]{:S(2)}) copy-start(bf16[592,512]{1,0:T(8,128)(2,1)S(1)} %collective-permute-done.2.rest_2_) | copy-start | bytes 1818628
  23.3 38.0 %copy-start.5 = (bf16[592,512]{1,0:T(8,128)(2,1)}, bf16[592,512]{1,0:T(8,128)(2,1)S(1)}, u32[]{:S(2)}) copy-start(bf16[592,512]{1,0:T(8,128)(2,1)S(1)} %collective-permute-done.1.rest_1_) | copy-start | bytes 1818628
  23.3 13.4 %collective-permute-start.3 = (bf16[592,512]{1,0:T(8,128)(2,1)S(1)}, bf16[592,512]{1,0:T(8,128)(2,1)S(1)}, u32[]{:S(2)}, u32[]{:S(2)}) collective-permute-start(bf16[592,512]{1,0:T(8,128)(2,1)S(1)} %collective-permute-done.1.rest_1_), channel_id=1, source_target_pairs={{0,8},{2,10},{8,16},{10,18},{16,24},{18,26},{24,28},{26,30},{28,20... | collective-permute-start | bytes 1818632 | tf_op jit(solution)/shard_map/ppermute | solution.py:841
  23.7 13.1 %collective-permute-start.4 = (bf16[592,512]{1,0:T(8,128)(2,1)S(1)}, bf16[592,512]{1,0:T(8,128)(2,1)S(1)}, u32[]{:S(2)}, u32[]{:S(2)}) collective-permute-start(bf16[592,512]{1,0:T(8,128)(2,1)S(1)} %collective-permute-done.2.rest_2_), channel_id=1, source_target_pairs={{0,4},{2,6},{8,0},{10,2},{16,8},{18,10},{24,16},{26,18},{28,24},{3... | collective-permute-start | bytes 1818632 | tf_op jit(solution)/shard_map/ppermute | solution.py:841
  36.7 24.6 %copy-start.6 = (bf16[592,512]{1,0:T(8,128)(2,1)}, bf16[592,512]{1,0:T(8,128)(2,1)S(1)}, u32[]{:S(2)}) copy-start(bf16[592,512]{1,0:T(8,128)(2,1)S(1)} %collective-permute-done.3.rest_3_) | copy-start | bytes 1818628
  36.8 24.5 %copy-start.7 = (bf16[592,512]{1,0:T(8,128)(2,1)}, bf16[592,512]{1,0:T(8,128)(2,1)S(1)}, u32[]{:S(2)}) copy-start(bf16[592,512]{1,0:T(8,128)(2,1)S(1)} %collective-permute-done.4.rest_4_) | copy-start | bytes 1818628
  36.8 12.6 %collective-permute-start.5 = (bf16[592,512]{1,0:T(8,128)(2,1)S(1)}, bf16[592,512]{1,0:T(8,128)(2,1)S(1)}, u32[]{:S(2)}, u32[]{:S(2)}) collective-permute-start(bf16[592,512]{1,0:T(8,128)(2,1)S(1)} %collective-permute-done.3.rest_3_), channel_id=1, source_target_pairs={{0,8},{2,10},{8,16},{10,18},{16,24},{18,26},{24,28},{26,30},{28,20... | collective-permute-start | bytes 1818632 | tf_op jit(solution)/shard_map/ppermute | solution.py:841
  38.4 11.7 %collective-permute-start.6 = (bf16[592,512]{1,0:T(8,128)(2,1)S(1)}, bf16[592,512]{1,0:T(8,128)(2,1)S(1)}, u32[]{:S(2)}, u32[]{:S(2)}) collective-permute-start(bf16[592,512]{1,0:T(8,128)(2,1)S(1)} %collective-permute-done.4.rest_4_), channel_id=1, source_target_pairs={{0,4},{2,6},{8,0},{10,2},{16,8},{18,10},{24,16},{26,18},{28,24},{3... | collective-permute-start | bytes 1818632 | tf_op jit(solution)/shard_map/ppermute | solution.py:841
  38.8 12.4 %collective-permute-start.9 = (bf16[592,512]{1,0:T(8,128)(2,1)S(1)}, bf16[592,512]{1,0:T(8,128)(2,1)S(1)}, u32[]{:S(2)}, u32[]{:S(2)}) collective-permute-start(bf16[592,512]{1,0:T(8,128)(2,1)S(1)} %pack_rest.1.rest_0_), channel_id=1, source_target_pairs={{0,2},{2,0},{4,6},{6,4},{8,10},{10,8},{12,14},{14,12},{16,18},{18,... | collective-permute-start | bytes 1818632 | tf_op jit(solution)/shard_map/ppermute | solution.py:846
  38.8 12.4 %collective-permute-start.11 = (bf16[592,512]{1,0:T(8,128)(2,1)S(1)}, bf16[592,512]{1,0:T(8,128)(2,1)S(1)}, u32[]{:S(2)}, u32[]{:S(2)}) collective-permute-start(bf16[592,512]{1,0:T(8,128)(2,1)S(1)} %collective-permute-done.2.rest_2_), channel_id=1, source_target_pairs={{0,2},{2,0},{4,6},{6,4},{8,10},{10,8},{12,14},{14,12},{16,18},{18,... | collective-permute-start | bytes 1818632 | tf_op jit(solution)/shard_map/ppermute | solution.py:846
  39.3 12.4 %collective-permute-start.10 = (bf16[592,512]{1,0:T(8,128)(2,1)S(1)}, bf16[592,512]{1,0:T(8,128)(2,1)S(1)}, u32[]{:S(2)}, u32[]{:S(2)}) collective-permute-start(bf16[592,512]{1,0:T(8,128)(2,1)S(1)} %collective-permute-done.1.rest_1_), channel_id=1, source_target_pairs={{0,2},{2,0},{4,6},{6,4},{8,10},{10,8},{12,14},{14,12},{16,18},{18,... | collective-permute-start | bytes 1818632 | tf_op jit(solution)/shard_map/ppermute | solution.py:846
  49.4 16.0 %copy-start.14 = (bf16[592,512]{1,0:T(8,128)(2,1)}, bf16[592,512]{1,0:T(8,128)(2,1)S(1)}, u32[]{:S(2)}) copy-start(bf16[592,512]{1,0:T(8,128)(2,1)S(1)} %collective-permute-done.5.rest_5_) | copy-start | bytes 1818628
  49.4 2.5 %collective-permute-start.12 = (bf16[592,512]{1,0:T(8,128)(2,1)S(1)}, bf16[592,512]{1,0:T(8,128)(2,1)S(1)}, u32[]{:S(2)}, u32[]{:S(2)}) collective-permute-start(bf16[592,512]{1,0:T(8,128)(2,1)S(1)} %collective-permute-done.3.rest_3_), channel_id=1, source_target_pairs={{0,2},{2,0},{4,6},{6,4},{8,10},{10,8},{12,14},{14,12},{16,18},{18,... | collective-permute-start | bytes 1818632 | tf_op jit(solution)/shard_map/ppermute | solution.py:846
  50.1 15.2 %copy-start.13 = (bf16[592,512]{1,0:T(8,128)(2,1)}, bf16[592,512]{1,0:T(8,128)(2,1)S(1)}, u32[]{:S(2)}) copy-start(bf16[592,512]{1,0:T(8,128)(2,1)S(1)} %collective-permute-done.6.rest_6_) | copy-start | bytes 1818628
  50.2 9.1 %collective-permute-start.8 = (bf16[304,512]{1,0:T(8,128)(2,1)S(1)}, bf16[304,512]{1,0:T(8,128)(2,1)S(1)}, u32[]{:S(2)}, u32[]{:S(2)}) collective-permute-start(bf16[304,512]{1,0:T(8,128)(2,1)S(1)} %slice.71), channel_id=1, source_target_pairs={{0,4},{2,6},{8,0},{10,2},{16,8},{18,10},{24,16},{26,18},{28,24},{3... | collective-permute-start | bytes 933896 | tf_op jit(solution)/shard_map/ppermute | solution.py:841
  51.2 10.1 %copy-start.8 = (bf16[592,512]{1,0:T(8,128)(2,1)}, bf16[592,512]{1,0:T(8,128)(2,1)S(1)}, u32[]{:S(2)}) copy-start(bf16[592,512]{1,0:T(8,128)(2,1)S(1)} %collective-permute-done.9.rest_5_.rest_9_) | copy-start | bytes 1818628
  51.2 10.1 %collective-permute-start.13 = (bf16[592,512]{1,0:T(8,128)(2,1)S(1)}, bf16[592,512]{1,0:T(8,128)(2,1)S(1)}, u32[]{:S(2)}, u32[]{:S(2)}) collective-permute-start(bf16[592,512]{1,0:T(8,128)(2,1)S(1)} %collective-permute-done.4.rest_4_), channel_id=1, source_target_pairs={{0,2},{2,0},{4,6},{6,4},{8,10},{10,8},{12,14},{14,12},{16,18},{18,... | collective-permute-start | bytes 1818632 | tf_op jit(solution)/shard_map/ppermute | solution.py:846
  51.3 14.0 %collective-permute-start.14 = (bf16[592,512]{1,0:T(8,128)(2,1)S(1)}, bf16[592,512]{1,0:T(8,128)(2,1)S(1)}, u32[]{:S(2)}, u32[]{:S(2)}) collective-permute-start(bf16[592,512]{1,0:T(8,128)(2,1)S(1)} %collective-permute-done.5.rest_5_), channel_id=1, source_target_pairs={{0,2},{2,0},{4,6},{6,4},{8,10},{10,8},{12,14},{14,12},{16,18},{18,... | collective-permute-start | bytes 1818632 | tf_op jit(solution)/shard_map/ppermute | solution.py:846
  51.7 13.6 %collective-permute-start.15 = (bf16[592,512]{1,0:T(8,128)(2,1)S(1)}, bf16[592,512]{1,0:T(8,128)(2,1)S(1)}, u32[]{:S(2)}, u32[]{:S(2)}) collective-permute-start(bf16[592,512]{1,0:T(8,128)(2,1)S(1)} %collective-permute-done.6.rest_6_), channel_id=1, source_target_pairs={{0,2},{2,0},{4,6},{6,4},{8,10},{10,8},{12,14},{14,12},{16,18},{18,... | collective-permute-start | bytes 1818632 | tf_op jit(solution)/shard_map/ppermute | solution.py:846
  51.8 15.4 %copy-start = (bf16[512,768]{1,0:T(8,128)(2,1)S(1)}, bf16[512,768]{1,0:T(8,128)(2,1)}, u32[]{:S(2)}) copy-start(bf16[512,768]{1,0:T(8,128)(2,1)} %tok_ref.7) | copy-start | bytes 2359300
  51.9 9.4 %collective-permute-start.7 = (bf16[288,512]{1,0:T(8,128)(2,1)S(1)}, bf16[288,512]{1,0:T(8,128)(2,1)S(1)}, u32[]{:S(2)}, u32[]{:S(2)}) collective-permute-start(bf16[288,512]{1,0:T(8,128)(2,1)S(1)} %slice.70), channel_id=1, source_target_pairs={{0,8},{2,10},{8,16},{10,18},{16,24},{18,26},{24,28},{26,30},{28,20... | collective-permute-start | bytes 884744 | tf_op jit(solution)/shard_map/ppermute | solution.py:841
  59.2 6.1 %collective-permute-start.17 = (bf16[304,512]{1,0:T(8,128)(2,1)S(1)}, bf16[304,512]{1,0:T(8,128)(2,1)S(1)}, u32[]{:S(2)}, u32[]{:S(2)}) collective-permute-start(bf16[304,512]{1,0:T(8,128)(2,1)S(1)} %collective-permute-done.8.rest_8_), channel_id=1, source_target_pairs={{0,2},{2,0},{4,6},{6,4},{8,10},{10,8},{12,14},{14,12},{16,18},{18,... | collective-permute-start | bytes 933896 | tf_op jit(solution)/shard_map/ppermute | solution.py:846
  61.3 4.0 %collective-permute-start.16 = (bf16[288,512]{1,0:T(8,128)(2,1)S(1)}, bf16[288,512]{1,0:T(8,128)(2,1)S(1)}, u32[]{:S(2)}, u32[]{:S(2)}) collective-permute-start(bf16[288,512]{1,0:T(8,128)(2,1)S(1)} %collective-permute-done.7.rest_7_), channel_id=1, source_target_pairs={{0,2},{2,0},{4,6},{6,4},{8,10},{10,8},{12,14},{14,12},{16,18},{18,... | collective-permute-start | bytes 884744 | tf_op jit(solution)/shard_map/ppermute | solution.py:846
  72.1 11.6 %collective-permute-start.18 = (bf16[512,384]{1,0:T(8,128)(2,1)S(1)}, bf16[512,384]{1,0:T(8,128)(2,1)S(1)}, u32[]{:S(2)}, u32[]{:S(2)}) collective-permute-start(bf16[512,384]{1,0:T(8,128)(2,1)S(1)} %get-tuple-element.127.own_ref.mixed_ref), channel_id=1, source_target_pairs={{0,1},{1,0},{2,3},{3,2},{4,5},{5,4},{6,7},{7,6},{8,9},{9,8},{10,11... | collective-permute-start | bytes 1179656 | tf_op jit(solution)/shard_map/ppermute | solution.py:996
  86.8 11.5 %collective-permute-start.19 = (bf16[256,768]{1,0:T(8,128)(2,1)S(1)}, bf16[256,768]{1,0:T(8,128)(2,1)S(1)}, u32[]{:S(2)}, u32[]{:S(2)}) collective-permute-start(bf16[256,768]{1,0:T(8,128)(2,1)S(1)} %get-tuple-element.136.rest_0_), channel_id=1, source_target_pairs={{0,1},{1,0},{2,3},{3,2},{4,5},{5,4},{6,7},{7,6},{8,9},{9,8},{10,11... | collective-permute-start | bytes 1179656 | tf_op jit(solution)/shard_map/ppermute | solution.py:1005
  96.1 1.4 collective-permute-start.21
  96.2 1.6 collective-permute-start.22
  97.9 12.1 %collective-permute-start.23 = (bf16[2,48,3072]{2,1,0:T(8,128)(2,1)S(1)}, bf16[2,48,3072]{2,1,0:T(8,128)(2,1)S(1)}, u32[]{:S(2)}, u32[]{:S(2)}) collective-permute-start(bf16[2,48,3072]{2,1,0:T(8,128)(2,1)S(1)} %get-tuple-element.150), channel_id=1, source_target_pairs={{0,2},{2,0},{4,6},{6,4},{8,10},{10,8},{12,14},{14,12},{16,18},{18,... | collective-permute-start | bytes 1769480 | tf_op jit(solution)/shard_map/ppermute | solution.py:890
  98.2 11.2 %collective-permute-start.20 = (bf16[256,768]{1,0:T(8,128)(2,1)S(1)}, bf16[256,768]{1,0:T(8,128)(2,1)S(1)}, u32[]{:S(2)}, u32[]{:S(2)}) collective-permute-start(bf16[256,768]{1,0:T(8,128)(2,1)S(1)} %get-tuple-element.138.rest_1_), channel_id=1, source_target_pairs={{0,1},{1,0},{2,3},{3,2},{4,5},{5,4},{6,7},{7,6},{8,9},{9,8},{10,11... | collective-permute-start | bytes 1179656 | tf_op jit(solution)/shard_map/ppermute | solution.py:1005
  99.1 25.4 %collective-permute-start.29 = (bf16[2,48,3072]{2,1,0:T(8,128)(2,1)S(1)}, bf16[2,48,3072]{2,1,0:T(8,128)(2,1)S(1)}, u32[]{:S(2)}, u32[]{:S(2)}) collective-permute-start(bf16[2,48,3072]{2,1,0:T(8,128)(2,1)S(1)} %get-tuple-element.159), channel_id=1, source_target_pairs={{0,2},{2,0},{4,6},{6,4},{8,10},{10,8},{12,14},{14,12},{16,18},{18,... | collective-permute-start | bytes 1769480 | tf_op jit(solution)/shard_map/ppermute | solution.py:890
  99.1 10.9 %collective-permute-start.25 = (bf16[48,1536]{1,0:T(8,128)(2,1)S(1)}, bf16[48,1536]{1,0:T(8,128)(2,1)S(1)}, u32[]{:S(2)}, u32[]{:S(2)}) collective-permute-start(bf16[48,1536]{1,0:T(8,128)(2,1)S(1)} %get-tuple-element.151), channel_id=1, source_target_pairs={{0,4},{2,6},{8,0},{10,2},{16,8},{18,10},{24,16},{26,18},{28,24},{3... | collective-permute-start | bytes 442376 | tf_op jit(solution)/shard_map/ppermute | solution.py:896
  100.7 9.3 %collective-permute-start.24 = (bf16[48,1536]{1,0:T(8,128)(2,1)S(1)}, bf16[48,1536]{1,0:T(8,128)(2,1)S(1)}, u32[]{:S(2)}, u32[]{:S(2)}) collective-permute-start(bf16[48,1536]{1,0:T(8,128)(2,1)S(1)} %get-tuple-element.149), channel_id=1, source_target_pairs={{0,8},{2,10},{8,16},{10,18},{16,24},{18,26},{24,28},{26,30},{28,20... | collective-permute-start | bytes 442376 | tf_op jit(solution)/shard_map/ppermute | solution.py:896
  109.5 14.1 %collective-permute-start.28 = (bf16[256,768]{1,0:T(8,128)(2,1)S(1)}, bf16[256,768]{1,0:T(8,128)(2,1)S(1)}, u32[]{:S(2)}, u32[]{:S(2)}) collective-permute-start(bf16[256,768]{1,0:T(8,128)(2,1)S(1)} %get-tuple-element.139), channel_id=1, source_target_pairs={{0,1},{1,0},{2,3},{3,2},{4,5},{5,4},{6,7},{7,6},{8,9},{9,8},{10,11... | collective-permute-start | bytes 1179656 | tf_op jit(solution)/shard_map/ppermute | solution.py:1019
  110.2 12.8 %collective-permute-start.26 = (bf16[48,3072]{1,0:T(8,128)(2,1)S(1)}, bf16[48,3072]{1,0:T(8,128)(2,1)S(1)}, u32[]{:S(2)}, u32[]{:S(2)}) collective-permute-start(bf16[48,3072]{1,0:T(8,128)(2,1)S(1)} %get-tuple-element.152), channel_id=1, source_target_pairs={{0,8},{2,10},{8,16},{10,18},{16,24},{18,26},{24,28},{26,30},{28,20... | collective-permute-start | bytes 884744 | tf_op jit(solution)/shard_map/ppermute | solution.py:896
  111.3 12.2 %collective-permute-start.27 = (bf16[48,3072]{1,0:T(8,128)(2,1)S(1)}, bf16[48,3072]{1,0:T(8,128)(2,1)S(1)}, u32[]{:S(2)}, u32[]{:S(2)}) collective-permute-start(bf16[48,3072]{1,0:T(8,128)(2,1)S(1)} %get-tuple-element.153), channel_id=1, source_target_pairs={{0,4},{2,6},{8,0},{10,2},{16,8},{18,10},{24,16},{26,18},{28,24},{3... | collective-permute-start | bytes 884744 | tf_op jit(solution)/shard_map/ppermute | solution.py:896
  117.0 4.2 %collective-permute-start.32 = (f32[16,128]{1,0:T(8,128)S(1)}, f32[16,128]{1,0:T(8,128)S(1)}, u32[]{:S(2)}, u32[]{:S(2)}) collective-permute-start(f32[16,128]{1,0:T(8,128)S(1)} %get-tuple-element.173.ga_ref), channel_id=1, source_target_pairs={{0,1},{1,0},{2,3},{3,2},{4,5},{5,4},{6,7},{7,6},{8,9},{9,8},{10,11... | collective-permute-start | bytes 24584 | tf_op jit(solution)/shard_map/ppermute | solution.py:1024
  121.2 16.8 %collective-permute-start.36 = (bf16[2,48,3072]{2,1,0:T(8,128)(2,1)S(1)}, bf16[2,48,3072]{2,1,0:T(8,128)(2,1)S(1)}, u32[]{:S(2)}, u32[]{:S(2)}) collective-permute-start(bf16[2,48,3072]{2,1,0:T(8,128)(2,1)S(1)} %get-tuple-element.190), channel_id=1, source_target_pairs={{0,2},{2,0},{4,6},{6,4},{8,10},{10,8},{12,14},{14,12},{16,18},{18,... | collective-permute-start | bytes 1769480 | tf_op jit(solution)/shard_map/ppermute | solution.py:890
  123.0 3.8 %collective-permute-start.33 = (bf16[288,256]{1,0:T(8,128)(2,1)S(1)}, bf16[288,256]{1,0:T(8,128)(2,1)S(1)}, u32[]{:S(2)}, u32[]{:S(2)}) collective-permute-start(bf16[288,256]{1,0:T(8,128)(2,1)S(1)} %get-tuple-element.183), channel_id=1, source_target_pairs={{0,2},{2,0},{4,6},{6,4},{8,10},{10,8},{12,14},{14,12},{16,18},{18,... | collective-permute-start | bytes 442376 | tf_op jit(solution)/shard_map/ppermute | solution.py:866
  123.5 11.2 %collective-permute-start.35 = (bf16[256,768]{1,0:T(8,128)(2,1)S(1)}, bf16[256,768]{1,0:T(8,128)(2,1)S(1)}, u32[]{:S(2)}, u32[]{:S(2)}) collective-permute-start(bf16[256,768]{1,0:T(8,128)(2,1)S(1)} %get-tuple-element.157), channel_id=1, source_target_pairs={{0,1},{1,0},{2,3},{3,2},{4,5},{5,4},{6,7},{7,6},{8,9},{9,8},{10,11... | collective-permute-start | bytes 1179656 | tf_op jit(solution)/shard_map/ppermute | solution.py:1028
  124.7 8.8 %collective-permute-start.31 = (bf16[48,3072]{1,0:T(8,128)(2,1)S(1)}, bf16[48,3072]{1,0:T(8,128)(2,1)S(1)}, u32[]{:S(2)}, u32[]{:S(2)}) collective-permute-start(bf16[48,3072]{1,0:T(8,128)(2,1)S(1)} %get-tuple-element.241), channel_id=1, source_target_pairs={{0,4},{2,6},{8,0},{10,2},{16,8},{18,10},{24,16},{26,18},{28,24},{3... | collective-permute-start | bytes 884744 | tf_op jit(solution)/shard_map/ppermute | solution.py:896
  126.3 8.4 %collective-permute-start.30 = (bf16[48,3072]{1,0:T(8,128)(2,1)S(1)}, bf16[48,3072]{1,0:T(8,128)(2,1)S(1)}, u32[]{:S(2)}, u32[]{:S(2)}) collective-permute-start(bf16[48,3072]{1,0:T(8,128)(2,1)S(1)} %get-tuple-element.242), channel_id=1, source_target_pairs={{0,8},{2,10},{8,16},{10,18},{16,24},{18,26},{24,28},{26,30},{28,20... | collective-permute-start | bytes 884744 | tf_op jit(solution)/shard_map/ppermute | solution.py:896
  126.8 1.4 collective-permute-start.34
  134.8 8.3 %collective-permute-start.39 = (bf16[288,256]{1,0:T(8,128)(2,1)S(1)}, bf16[288,256]{1,0:T(8,128)(2,1)S(1)}, u32[]{:S(2)}, u32[]{:S(2)}) collective-permute-start(bf16[288,256]{1,0:T(8,128)(2,1)S(1)} %get-tuple-element.196), channel_id=1, source_target_pairs={{0,8},{2,10},{8,16},{10,18},{16,24},{18,26},{24,28},{26,30},{28,20... | collective-permute-start | bytes 442376 | tf_op jit(solution)/shard_map/ppermute | solution.py:896
  135.8 5.1 %collective-permute-start.40 = (bf16[288,256]{1,0:T(8,128)(2,1)S(1)}, bf16[288,256]{1,0:T(8,128)(2,1)S(1)}, u32[]{:S(2)}, u32[]{:S(2)}) collective-permute-start(bf16[288,256]{1,0:T(8,128)(2,1)S(1)} %get-tuple-element.197), channel_id=1, source_target_pairs={{0,4},{2,6},{8,0},{10,2},{16,8},{18,10},{24,16},{26,18},{28,24},{3... | collective-permute-start | bytes 442376 | tf_op jit(solution)/shard_map/ppermute | solution.py:896
  136.9 12.1 %collective-permute-start.41 = (bf16[256,768]{1,0:T(8,128)(2,1)S(1)}, bf16[256,768]{1,0:T(8,128)(2,1)S(1)}, u32[]{:S(2)}, u32[]{:S(2)}) collective-permute-start(bf16[256,768]{1,0:T(8,128)(2,1)S(1)} %get-tuple-element.188), channel_id=1, source_target_pairs={{0,1},{1,0},{2,3},{3,2},{4,5},{5,4},{6,7},{7,6},{8,9},{9,8},{10,11... | collective-permute-start | bytes 1179656 | tf_op jit(solution)/shard_map/ppermute | solution.py:1038
  138.0 11.0 %collective-permute-start.43 = (bf16[2,288,512]{2,1,0:T(8,128)(2,1)S(1)}, bf16[2,288,512]{2,1,0:T(8,128)(2,1)S(1)}, u32[]{:S(2)}, u32[]{:S(2)}) collective-permute-start(bf16[2,288,512]{2,1,0:T(8,128)(2,1)S(1)} %get-tuple-element.204), channel_id=1, source_target_pairs={{0,2},{2,0},{4,6},{6,4},{8,10},{10,8},{12,14},{14,12},{16,18},{18,... | collective-permute-start | bytes 1769480 | tf_op jit(solution)/shard_map/ppermute | solution.py:890
  138.3 9.5 %collective-permute-start.38 = (bf16[48,3072]{1,0:T(8,128)(2,1)S(1)}, bf16[48,3072]{1,0:T(8,128)(2,1)S(1)}, u32[]{:S(2)}, u32[]{:S(2)}) collective-permute-start(bf16[48,3072]{1,0:T(8,128)(2,1)S(1)} %get-tuple-element.239), channel_id=1, source_target_pairs={{0,4},{2,6},{8,0},{10,2},{16,8},{18,10},{24,16},{26,18},{28,24},{3... | collective-permute-start | bytes 884744 | tf_op jit(solution)/shard_map/ppermute | solution.py:896
  140.9 8.1 %collective-permute-start.37 = (bf16[48,3072]{1,0:T(8,128)(2,1)S(1)}, bf16[48,3072]{1,0:T(8,128)(2,1)S(1)}, u32[]{:S(2)}, u32[]{:S(2)}) collective-permute-start(bf16[48,3072]{1,0:T(8,128)(2,1)S(1)} %get-tuple-element.240), channel_id=1, source_target_pairs={{0,8},{2,10},{8,16},{10,18},{16,24},{18,26},{24,28},{26,30},{28,20... | collective-permute-start | bytes 884744 | tf_op jit(solution)/shard_map/ppermute | solution.py:896
  143.1 14.4 %collective-permute-start.42 = (bf16[2,288,512]{2,1,0:T(8,128)(2,1)S(1)}, bf16[2,288,512]{2,1,0:T(8,128)(2,1)S(1)}, u32[]{:S(2)}, u32[]{:S(2)}) collective-permute-start(bf16[2,288,512]{2,1,0:T(8,128)(2,1)S(1)} %get-tuple-element.202), channel_id=1, source_target_pairs={{0,2},{2,0},{4,6},{6,4},{8,10},{10,8},{12,14},{14,12},{16,18},{18,... | collective-permute-start | bytes 1769480 | tf_op jit(solution)/shard_map/ppermute | solution.py:890
  149.2 7.5 %collective-permute-start.44 = (bf16[288,512]{1,0:T(8,128)(2,1)S(1)}, bf16[288,512]{1,0:T(8,128)(2,1)S(1)}, u32[]{:S(2)}, u32[]{:S(2)}) collective-permute-start(bf16[288,512]{1,0:T(8,128)(2,1)S(1)} %get-tuple-element.207), channel_id=1, source_target_pairs={{0,8},{2,10},{8,16},{10,18},{16,24},{18,26},{24,28},{26,30},{28,20... | collective-permute-start | bytes 884744 | tf_op jit(solution)/shard_map/ppermute | solution.py:896
  149.9 7.6 %collective-permute-start.45 = (bf16[288,512]{1,0:T(8,128)(2,1)S(1)}, bf16[288,512]{1,0:T(8,128)(2,1)S(1)}, u32[]{:S(2)}, u32[]{:S(2)}) collective-permute-start(bf16[288,512]{1,0:T(8,128)(2,1)S(1)} %get-tuple-element.208), channel_id=1, source_target_pairs={{0,4},{2,6},{8,0},{10,2},{16,8},{18,10},{24,16},{26,18},{28,24},{3... | collective-permute-start | bytes 884744 | tf_op jit(solution)/shard_map/ppermute | solution.py:896
  151.3 9.6 %collective-permute-start.53 = (bf16[1,48,3072]{2,1,0:T(8,128)(2,1)S(1)}, bf16[1,48,3072]{2,1,0:T(8,128)(2,1)S(1)}, u32[]{:S(2)}, u32[]{:S(2)}) collective-permute-start(bf16[1,48,3072]{2,1,0:T(8,128)(2,1)S(1)} %get-tuple-element.224), channel_id=1, source_target_pairs={{0,2},{2,0},{4,6},{6,4},{8,10},{10,8},{12,14},{14,12},{16,18},{18,... | collective-permute-start | bytes 884744 | tf_op jit(solution)/shard_map/ppermute | solution.py:890
  151.5 19.1 %collective-permute-start.49 = (bf16[1,288,512]{2,1,0:T(8,128)(2,1)S(1)}, bf16[1,288,512]{2,1,0:T(8,128)(2,1)S(1)}, u32[]{:S(2)}, u32[]{:S(2)}) collective-permute-start(bf16[1,288,512]{2,1,0:T(8,128)(2,1)S(1)} %get-tuple-element.213), channel_id=1, source_target_pairs={{0,2},{2,0},{4,6},{6,4},{8,10},{10,8},{12,14},{14,12},{16,18},{18,... | collective-permute-start | bytes 884744 | tf_op jit(solution)/shard_map/ppermute | solution.py:890
  156.8 8.7 %collective-permute-start.48 = (bf16[256,768]{1,0:T(8,128)(2,1)S(1)}, bf16[256,768]{1,0:T(8,128)(2,1)S(1)}, u32[]{:S(2)}, u32[]{:S(2)}) collective-permute-start(bf16[256,768]{1,0:T(8,128)(2,1)S(1)} %get-tuple-element.200), channel_id=1, source_target_pairs={{0,1},{1,0},{2,3},{3,2},{4,5},{5,4},{6,7},{7,6},{8,9},{9,8},{10,11... | collective-permute-start | bytes 1179656 | tf_op jit(solution)/shard_map/ppermute | solution.py:1041
  157.8 7.7 %collective-permute-start.47 = (bf16[288,512]{1,0:T(8,128)(2,1)S(1)}, bf16[288,512]{1,0:T(8,128)(2,1)S(1)}, u32[]{:S(2)}, u32[]{:S(2)}) collective-permute-start(bf16[288,512]{1,0:T(8,128)(2,1)S(1)} %get-tuple-element.237), channel_id=1, source_target_pairs={{0,4},{2,6},{8,0},{10,2},{16,8},{18,10},{24,16},{26,18},{28,24},{3... | collective-permute-start | bytes 884744 | tf_op jit(solution)/shard_map/ppermute | solution.py:896
  159.5 6.7 %collective-permute-start.46 = (bf16[288,512]{1,0:T(8,128)(2,1)S(1)}, bf16[288,512]{1,0:T(8,128)(2,1)S(1)}, u32[]{:S(2)}, u32[]{:S(2)}) collective-permute-start(bf16[288,512]{1,0:T(8,128)(2,1)S(1)} %get-tuple-element.238), channel_id=1, source_target_pairs={{0,8},{2,10},{8,16},{10,18},{16,24},{18,26},{24,28},{26,30},{28,20... | collective-permute-start | bytes 884744 | tf_op jit(solution)/shard_map/ppermute | solution.py:896
  160.9 5.8 %collective-permute-start.50 = (bf16[2,288,512]{2,1,0:T(8,128)(2,1)S(1)}, bf16[2,288,512]{2,1,0:T(8,128)(2,1)S(1)}, u32[]{:S(2)}, u32[]{:S(2)}) collective-permute-start(bf16[2,288,512]{2,1,0:T(8,128)(2,1)S(1)} %get-tuple-element.215), channel_id=1, source_target_pairs={{0,2},{2,0},{4,6},{6,4},{8,10},{10,8},{12,14},{14,12},{16,18},{18,... | collective-permute-start | bytes 1769480 | tf_op jit(solution)/shard_map/ppermute | solution.py:890
  167.0 6.8 %collective-permute-start.52 = (bf16[288,512]{1,0:T(8,128)(2,1)S(1)}, bf16[288,512]{1,0:T(8,128)(2,1)S(1)}, u32[]{:S(2)}, u32[]{:S(2)}) collective-permute-start(bf16[288,512]{1,0:T(8,128)(2,1)S(1)} %get-tuple-element.235), channel_id=1, source_target_pairs={{0,4},{2,6},{8,0},{10,2},{16,8},{18,10},{24,16},{26,18},{28,24},{3... | collective-permute-start | bytes 884744 | tf_op jit(solution)/shard_map/ppermute | solution.py:896
  168.5 6.7 %collective-permute-start.51 = (bf16[288,512]{1,0:T(8,128)(2,1)S(1)}, bf16[288,512]{1,0:T(8,128)(2,1)S(1)}, u32[]{:S(2)}, u32[]{:S(2)}) collective-permute-start(bf16[288,512]{1,0:T(8,128)(2,1)S(1)} %get-tuple-element.236), channel_id=1, source_target_pairs={{0,8},{2,10},{8,16},{10,18},{16,24},{18,26},{24,28},{26,30},{28,20... | collective-permute-start | bytes 884744 | tf_op jit(solution)/shard_map/ppermute | solution.py:896
  (12 other events, 61.1 us)

commit v4 on v3

--- a/solution.py
+++ b/solution.py
@@ -23,13 +23,14 @@
     return lax.dot_general(a, b, dims, preferred_element_type=F32)
 
 
-def run(kernel, name, scalars, arrays, outs, scratch=(), loose=(), loose_outs=(), micros=0, aliases=None):
+def run(kernel, name, scalars, arrays, outs, scratch=(), loose=(), loose_outs=(), aliases=None, near=0):
     held = [pltpu.with_memory_space_constraint(one, pltpu.VMEM) for one in arrays]
     results = [pltpu.VMEM(*one) for one in outs] + [jax.ShapeDtypeStruct(*one) for one in loose_outs]
     specs = [pl.BlockSpec(memory_space=pltpu.SMEM)] * len(scalars)
     specs += [pl.BlockSpec(memory_space=pltpu.VMEM)] * len(arrays)
-    specs += [pl.BlockSpec(memory_space=pltpu.HBM)] * len(loose)
-    loose = [pltpu.with_memory_space_constraint(one, pltpu.HBM) for one in loose]
+    far = len(loose) - near
+    specs += [pl.BlockSpec(memory_space=pltpu.HBM)] * far + [pl.BlockSpec(memory_space=pl.ANY)] * near
+    loose = [pltpu.with_memory_space_constraint(one, pltpu.HBM) for one in loose[:far]] + list(loose[far:])
     out_specs = [pl.BlockSpec(memory_space=pltpu.VMEM)] * len(outs)
     out_specs += [pl.BlockSpec(memory_space=pl.ANY)] * len(loose_outs)
     return pl.pallas_call(
@@ -39,7 +40,7 @@
         out_specs=tuple(out_specs),
         scratch_shapes=list(scratch),
         compiler_params=pltpu.CompilerParams(vmem_limit_bytes=VMEM_BYTES),
-        cost_estimate=pl.CostEstimate(flops=1 + micros * 1_000_000_000, bytes_accessed=1, transcendentals=0),
+        cost_estimate=pl.CostEstimate(flops=1, bytes_accessed=1, transcendentals=0),
         input_output_aliases=aliases or {},
         name=name,
     )(*scalars, *held, *loose)
@@ -94,53 +95,55 @@
         return self.scores + [kind for kind, _ in self.blocks].index("proj") * self.krows
 
 
-def pack_unit(plan, scores, w_up, w_down):
-    inputs = (scores, w_up, w_down)
-    krows, length = plan.krows, plan.length
+def other_parts(plan, first):
+    begin = plan.width + first * plan.width
+    parts = []
+    for n, (kind, column) in enumerate(plan.blocks):
+        low, high = max(begin, column), min(begin + plan.width, column + plan.length)
+        if kind == "proj" and low < high:
+            parts.append((plan.scores + n * plan.krows, low - column, 0, low - begin, plan.krows, high - low))
+    low = max(begin, plan.wide - plan.tail)
+    if low < begin + plan.width:
+        for n in range(3):
+            lanes = n * plan.tail + low - (plan.wide - plan.tail)
+            parts.append((plan.last, lanes, n * plan.fold, low - begin, plan.fold, begin + plan.width - low))
+    return parts
+
+
+def put_half(plan, out, half_ref, first):
+    for row, lane, at, column, rows, lanes in other_parts(plan, first):
+        out[row : row + rows, lane : lane + lanes] = half_ref[at : at + rows, column : column + lanes]
+
+
+def pack_unit(plan, second, scores, wv, gain_one, gain_two, w_up, w_down, wo):
+    inputs = (scores, wv, gain_one.reshape(1, -1), gain_two.reshape(1, -1), w_up, w_down, wo)
+    count = len(inputs)
+    krows, length, width = plan.krows, plan.length, plan.width
     per = plan.hidden // length
-
-    def kernel(*refs):
-        out, held, sem = refs[3], refs[4:7], refs[7]
-        fetch(refs[:3], held, sem)
-        s_ref, up_ref, down_ref = held
+    assert plan.tail <= width
+
+    def kernel(second_ref, *rest):
+        out, wo_out, gains = rest[count : count + 3]
+        held, sem = rest[count + 3 : -1], rest[-1]
+        fetch(rest[:count], held, sem)
+        s_ref, wv_ref, ga_ref, gf_ref, up_ref, down_ref, own_ref = held
         out[: plan.scores, :] = s_ref[...].reshape(plan.scores, length).astype(BF)
         for n, (kind, column) in enumerate(plan.blocks):
+            at = slice(plan.scores + n * krows, plan.scores + (n + 1) * krows)
             if kind == "ffn":
-                at = slice(plan.scores + n * krows, plan.scores + (n + 1) * krows)
                 ref, first = (up_ref, column) if n < per else (down_ref, column - plan.hidden)
                 out[at, :] = ref[:, first : first + length].astype(BF)
-
-    return run(
-        kernel,
-        "pack_unit",
-        (),
-        (),
-        (((plan.deep, length), BF),),
-        (*[pltpu.VMEM(one.shape, one.dtype) for one in inputs], pltpu.SemaphoreType.DMA((3,))),
-        loose=inputs,
-    )[0]
-
-
-def pack_rest(plan, second, unit, wv, gain_one, gain_two, wo_own, wo_other):
-    inputs = (wv, gain_one.reshape(1, -1), gain_two.reshape(1, -1), wo_own)
-    krows, length, width = plan.krows, plan.length, plan.width
-
-    def kernel(second_ref, other_ref, old, *rest):
-        out, wide, gains = rest[4:7]
-        held, sem = rest[7:11], rest[11]
-        fetch(rest[:4], held, sem)
-        wv_ref, ga_ref, gf_ref, own_ref = held
-        first = second_ref[0]
-        wide[:, :width] = wv_ref[...].astype(BF)
-        wide[:, pl.ds(multiple(width + first * width, LANES), width)] = own_ref[...].astype(BF)
-        wide[:, pl.ds(multiple(width + (1 - first) * width, LANES), width)] = other_ref[...].astype(BF)
-        for n, (kind, column) in enumerate(plan.blocks):
-            if kind == "proj":
-                at = slice(plan.scores + n * krows, plan.scores + (n + 1) * krows)
-                out[at, :] = wide[:, column : column + length]
-        for n in range(3):
-            lanes = slice(n * plan.tail, (n + 1) * plan.tail)
-            out[plan.last :, lanes] = wide[n * plan.fold : (n + 1) * plan.fold, plan.wide - plan.tail :]
+            else:
+                out[at, :] = jnp.zeros((krows, length), BF)
+        out[plan.last :, : plan.gain_lane] = jnp.zeros((plan.fold, plan.gain_lane), BF)
+        out[plan.value_row() : plan.value_row() + krows, :width] = wv_ref[...].astype(BF)
+        wo_out[...] = own_ref[...].astype(BF)
+        for place in range(2):
+
+            @pl.when(second_ref[0] == place)
+            def _():
+                put_half(plan, out, wo_out, place)
+
         gains[...] = jnp.zeros_like(gains)
         gains[0:1, :krows] = ga_ref[...]
         gains[1:2, :krows] = gf_ref[...]
@@ -148,19 +151,38 @@
 
     return run(
         kernel,
-        "pack_rest",
+        "pack_unit",
         (second,),
-        (wo_other, unit),
-        (((plan.deep, length), BF),),
+        (),
+        (((plan.deep, length), BF), ((krows, width), BF)),
         (
-            pltpu.VMEM((krows, plan.wide), BF),
             pltpu.VMEM((plan.fold, length - plan.gain_lane), F32),
             *[pltpu.VMEM(one.shape, one.dtype) for one in inputs],
-            pltpu.SemaphoreType.DMA((4,)),
+            pltpu.SemaphoreType.DMA((count,)),
         ),
         loose=inputs,
-        aliases={2: 0},
-    )[0]
+    )
+
+
+def fill_units(plan, second, units, others):
+    count = len(units)
+
+    def kernel(second_ref, *rest):
+        for place in range(2):
+
+            @pl.when(second_ref[0] == 1 - place)
+            def _():
+                for n in range(count):
+                    put_half(plan, rest[2 * count + n], rest[count + n], place)
+
+    return run(
+        kernel,
+        "fill_units",
+        (second,),
+        (*units, *others),
+        [(one.shape, BF) for one in units],
+        aliases={1 + n: n for n in range(count)},
+    )
 
 
 def fetch(refs, held, sem):
@@ -214,54 +236,70 @@
     return write
 
 
-def mixer_first(plan, where, segments, units, shares, heads):
-    length = segments.shape[1]
+def low_parts(plan):
+    return [
+        (plan.value_row(), 0, plan.krows, plan.width),
+        (plan.last, plan.gain_lane, plan.fold, LANES),
+    ]
+
+
+def bring_low(plan, units, shares, where_ref, wv_ref, low_ref, sem):
+    krows = plan.krows
+
+    def target(m, owner):
+        if m == 0:
+            return wv_ref.at[pl.ds(multiple(owner * krows, 16), krows), :]
+        return low_ref.at[owner]
+
+    return pick(units, shares, where_ref, low_parts(plan), target, sem)
+
+
+def mixer_first(plan, where, tokens, segments, units, shares, heads):
+    length, model = tokens.shape
     rows = length // UNITS
 
-    def kernel(where_ref, seg_ref, *rest):
-        e_ref, unit, same, sem = rest[len(units) :]
-        mixer_rows(plan, rest[: len(units)], shares, where_ref, seg_ref, e_ref, unit, same, sem)()
+    def kernel(where_ref, tok_ref, seg_ref, *rest):
+        e_ref, wv_ref, low_ref, hat_ref, unit, same, sem, more = rest[len(units) :]
+        write = mixer_rows(plan, rest[: len(units)], shares, where_ref, seg_ref, e_ref, unit, same, sem)
+        copies = bring_low(plan, rest[: len(units)], shares, where_ref, wv_ref, low_ref, more)
+        x = tok_ref[...].astype(F32)
+        hat_ref[...] = x * lax.rsqrt(jnp.mean(x * x, axis=-1, keepdims=True) + EPSILON)
+        write()
+        for copy in copies:
+            copy.wait()
 
     return run(
         kernel,
         "mixer_first",
         (where,),
-        (segments,),
-        (((heads, length, length), BF),),
+        (tokens, segments),
+        (
+            ((heads, length, length), BF),
+            ((model, plan.width), BF),
+            ((UNITS, plan.fold, LANES), BF),
+            ((length, model), F32),
+        ),
         (
             pltpu.VMEM((heads * length, length), BF),
             pltpu.VMEM((length, length), F32),
             pltpu.SemaphoreType.DMA((UNITS, 1)),
+            pltpu.SemaphoreType.DMA((UNITS, 2)),
         ),
         loose=units,
-    )[0]
-
-
-def mixer_forward(plan, where, tokens, segments, e, units, shares, late, heads, width):
-    length, model = tokens.shape
+    )
+
+
+def mixer_forward(plan, where, segments, early, units, shares, heads, width):
+    length, model = early[3].shape
     size = width // heads
     krows = model // UNITS
     wide = heads * LANES
-    parts = [
-        (plan.value_row(), 0, krows, width),
-        (plan.last, plan.gain_lane, plan.fold, LANES),
-    ]
     count = len(units)
 
-    def kernel(where_ref, tok_ref, seg_ref, e_old, *rest):
-        unit_refs = rest[:count]
-        e_ref, va_ref, mixed_ref, mixf_ref, rb_ref, n1_ref, gains_ref, wv_ref, pieces, unit, low, same, sem, more = rest[count:]
-
-        def target(m, owner):
-            if m == 0:
-                return wv_ref.at[pl.ds(multiple(owner * krows, 16), krows), :]
-            return low.at[owner]
-
-        copies = pick(unit_refs, shares, where_ref, parts, target, sem)
-        now = [n for n in range(count) if n in late]
-        write = mixer_rows(
-            plan, [unit_refs[n] for n in now], [shares[n] for n in now], where_ref, seg_ref, e_ref, unit, same, more
-        )
+    def kernel(where_ref, seg_ref, e_old, wv_old, low_old, hat_ref, *rest):
+        e_ref, wv_ref, low, va_ref, mixed_ref, sums_ref, n1_ref, gains_ref, pieces, unit, same, sem, more = rest[count:]
+        copies = bring_low(plan, rest[:count], shares, where_ref, wv_ref, low, sem)
+        write = mixer_rows(plan, rest[:count], shares, where_ref, seg_ref, e_ref, unit, same, more)
         for copy in copies:
             copy.wait()
         for d in range(UNITS):
@@ -281,9 +319,7 @@
             full = jnp.where(own, mm(pieces[t].astype(BF), spread), 0.0)
             gains.append(jnp.sum(full, axis=0, keepdims=True))
             gains_ref[t : t + 1, :] = gains[t]
-        x = tok_ref[...].astype(F32)
-        inv = lax.rsqrt(jnp.mean(x * x, axis=-1, keepdims=True) + EPSILON)
-        n1_ref[...] = (x * inv * gains[0]).astype(BF)
+        n1_ref[...] = (hat_ref[...] * gains[0]).astype(BF)
         values = mm(n1_ref[...], wv_ref[...]).astype(BF)
         tail = (lax.broadcasted_iota(jnp.int32, (length, LANES - size), 1) < 2).astype(BF)
         for h in range(heads):
@@ -294,56 +330,58 @@
         for h in range(heads):
             lanes = slice(h * LANES, (h + 1) * LANES)
             sums = mm(e_ref[h], va_ref[:, lanes])
-            inverse = 1.0 / sums[:, size : size + 1]
-            mixed = sums * inverse
-            rb_ref[:, lanes] = jnp.broadcast_to(inverse, (length, LANES))
-            mixf_ref[:, lanes] = jnp.where(
-                lax.broadcasted_iota(jnp.int32, (length, LANES), 1) < size, mixed, 0.0
-            )
-            mixed_ref[:, h * size : (h + 1) * size] = mixed[:, :size].astype(BF)
+            sums_ref[:, lanes] = sums
+            mixed_ref[:, h * size : (h + 1) * size] = (sums * (1.0 / sums[:, size : size + 1]))[:, :size].astype(BF)
 
     return run(
         kernel,
         "mixer_forward",
         (where,),
-        (tokens, segments, e),
+        (segments, *early),
         (
             ((heads, length, length), BF),
+            ((model, width), BF),
+            ((UNITS, plan.fold, LANES), BF),
             ((length, wide), BF),
             ((length, width), BF),
             ((length, wide), F32),
-            ((length, wide), F32),
             ((length, model), BF),
             ((2, model), F32),
-            ((model, width), BF),
         ),
         (
             pltpu.VMEM((2, UNITS, LANES), F32),
             pltpu.VMEM((heads * length, length), BF),
-            pltpu.VMEM((UNITS, plan.fold, LANES), BF),
             pltpu.VMEM((length, length), F32),
-            pltpu.SemaphoreType.DMA((UNITS, len(parts))),
+            pltpu.SemaphoreType.DMA((UNITS, 2)),
             pltpu.SemaphoreType.DMA((UNITS, 1)),
         ),
         loose=units,
-        aliases={3: 0},
-    )
-
-
-def second_weights(plan, where, cotangent, units, shares):
+        aliases={2: 0, 3: 1, 4: 2},
+        near=len(units),
+    )
+
+
+def second_weights(plan, where, cotangent, sums, units, shares, near, size):
     length, model = cotangent.shape
     hidden, krows = plan.hidden, plan.krows
     piece = hidden // 3
     parts = plan.ffn_parts()
 
-    def kernel(where_ref, cot_ref, *rest):
-        out, gact, sem = rest[len(units) :]
+    def kernel(where_ref, cot_ref, sums_ref, *rest):
+        out, gact, mixf_ref, rb_ref, sem = rest[len(units) :]
 
         def target(m, owner):
             _, _, row, column, rows, columns = parts[m]
             return out.at[pl.ds(multiple(owner * krows + row, 16), rows), pl.ds(column, columns)]
 
-        for copy in pick(rest[: len(units)], shares, where_ref, parts, target, sem):
+        copies = pick(rest[: len(units)], shares, where_ref, parts, target, sem)
+        inside = lax.broadcasted_iota(jnp.int32, (length, LANES), 1) < size
+        for h in range(sums.shape[1] // LANES):
+            lanes = slice(h * LANES, (h + 1) * LANES)
+            inverse = jnp.broadcast_to(1.0 / sums_ref[:, h * LANES + size : h * LANES + size + 1], (length, LANES))
+            rb_ref[:, lanes] = inverse
+            mixf_ref[:, lanes] = jnp.where(inside, sums_ref[:, lanes] * inverse, 0.0)
+        for copy in copies:
             copy.wait()
         for j in range(3):
             cols = slice(j * piece, (j + 1) * piece)
@@ -353,10 +391,11 @@
         kernel,
         "second_weights",
         (where,),
-        (cotangent,),
-        (((model, 2 * hidden + model), BF), ((length, hidden), F32)),
+        (cotangent, sums),
+        (((model, 2 * hidden + model), BF), ((length, hidden), F32), (sums.shape, F32), (sums.shape, F32)),
         (pltpu.SemaphoreType.DMA((UNITS, len(parts))),),
         loose=units,
+        near=near,
     )
 
 
@@ -412,76 +451,62 @@
     )
 
 
-def late_groups():
+def late_units(first):
+    return [k for k in range(UNITS // 2) if k not in first]
+
+
+def slots(refs, first, pieces):
     half = UNITS // 2
-    far = half // 2
-    groups = [[far + 1 - hop, far - 1 + hop] for hop in range(2, far + 1)]
-    return groups + [[0]]
-
-
-def late_place(k):
-    return next((g, group.index(k)) for g, group in enumerate(late_groups()) if k in group)
-
-
-def slots(refs):
-    half = UNITS // 2
-    keep, one, two, *later = refs
-    columns = keep.shape[2]
+    count = len(first) * pieces
+    keep, early, later = refs[0], refs[1 : 1 + count], refs[1 + count :]
+    late = late_units(first)
 
     def slot(u):
         if u < half:
-            return [(keep.at[u], 0, columns)]
+            return [keep.at[u]]
         k = u - half
-        if k == half // 2:
-            return [(one, 0, columns // 2), (two, columns // 2, columns // 2)]
-        group, place = late_place(k)
-        return [(later[group].at[place], 0, columns)]
+        if k in first:
+            at = first.index(k) * pieces
+            return early[at : at + pieces]
+        n = late.index(k)
+        return [later[0].at[n] if len(later) == 1 else later[n]]
 
     return slot
 
 
-def slot_shapes(rows, columns):
-    early = ((rows, columns // 2), BF)
-    later = [((len(group), rows, columns), BF) for group in late_groups()]
-    return [((UNITS // 2, rows, columns), BF), early, early, *later]
-
-
-SLOTS = 3 + len(late_groups())
-
-
-def far_sum(far, keep, early, second):
+def slot_shapes(rows, columns, first, pieces, apart):
+    half = UNITS // 2
+    cuts = [(rows, columns)] if pieces == 1 else [(rows - SMALL, columns), (SMALL, columns)]
+    early = [(cut, BF) for _ in first for cut in cuts]
+    count = half - len(first)
+    later = [((rows, columns), BF)] * count if apart else [((count, rows, columns), BF)]
+    return [((half, rows, columns), BF), *early, *later]
+
+
+SMALL = 16
+FFN_FIRST = [UNITS // 4, UNITS // 4 - 1]
+MIXER_FIRST = [UNITS // 4]
+
+
+def pieces_sum(k, keep, pieces):
     _, rows, columns = keep.shape
-    half = columns // 2
-
-    def kernel(keep_ref, early_ref, second_ref, up, down):
-        for out, one, at in ((up, early_ref, slice(0, half)), (down, second_ref, slice(half, columns))):
-            out[...] = (keep_ref[far, :, at].astype(F32) + one[...].astype(F32)).astype(BF)
-
-    return run(kernel, "far_sum", (), (keep, early, second), [((rows, half), BF)] * 2)
-
-
-def next_sums(far, keep, later, up, down):
-    _, rows, columns = keep.shape
-    half = columns // 2
-
-    def kernel(keep_ref, later_ref, up_ref, down_ref, up_out, down_out):
-        for out, one, k, mine in ((up_out, up_ref, far - 1, 0), (down_out, down_ref, far + 1, 1)):
-            for n in range(2):
-                at = slice(n * half, (n + 1) * half)
-                total = keep_ref[k, :, at].astype(F32) + later_ref[late_place(k)[1], :, at].astype(F32)
-                if n == mine:
-                    total = total + one[...].astype(F32)
-                out[:, at] = total.astype(BF)
-
-    return run(kernel, "next_sums", (), (keep, later, up, down), [((rows, columns), BF)] * 2)
-
-
-def result_kernel(name, keep, later, up, down, shapes, cut):
-    def kernel(keep_ref, later_ref, up_ref, down_ref, *rest):
+
+    def kernel(keep_ref, *refs):
+        begin = 0
+        for one in refs[:-1]:
+            at = slice(begin, begin + one.shape[0])
+            begin = at.stop
+            refs[-1][at, :] = (keep_ref[k, at, :].astype(F32) + one[...].astype(F32)).astype(BF)
+
+    return run(kernel, "pieces_sum", (), (keep, *pieces), [((rows, columns), BF)])[0]
+
+
+def result_kernel(name, keep, own, up, down, shapes, cut):
+    def kernel(keep_ref, own_ref, up_ref, down_ref, *rest):
         outs, held, sem = rest[: len(shapes)], rest[len(shapes) : -1], rest[-1]
 
         def total(rows, columns):
-            value = keep_ref[0, rows, columns].astype(F32) + later_ref[late_place(0)[1], rows, columns].astype(F32)
+            value = keep_ref[0, rows, columns].astype(F32) + own_ref[rows, columns].astype(F32)
             return value + up_ref[rows, columns].astype(F32) + down_ref[rows, columns].astype(F32)
 
         copies = []
@@ -496,24 +521,24 @@
         kernel,
         name,
         (),
-        (keep, later, up, down),
+        (keep, own, up, down),
         (),
         (*[pltpu.VMEM(shape, F32) for shape in shapes], pltpu.SemaphoreType.DMA((len(shapes),))),
         loose_outs=[(shape, F32) for shape in shapes],
     )
 
 
-def ffn_result(keep, later, up, down):
+def ffn_result(keep, own, up, down):
     _, rows, columns = keep.shape
     half = columns // 2
 
     def cut(n, to, total):
         to[...] = total(slice(None), slice(n * half, (n + 1) * half))
 
-    return result_kernel("ffn_result", keep, later, up, down, [(rows, half)] * 2, cut)
-
-
-def mixer_result(keep, later, up, down, heads, krows, width):
+    return result_kernel("ffn_result", keep, own, up, down, [(rows, half)] * 2, cut)
+
+
+def mixer_result(keep, own, up, down, heads, krows, width):
     _, deep, length = keep.shape
     top = deep - 2 * krows
     rows = top // heads
@@ -528,19 +553,20 @@
         else:
             to[...] = total(slice(top, top + 16), slice(width, length))[n - 3 : n - 2, :krows]
 
-    return result_kernel("mixer_result", keep, later, up, down, shapes, cut)
-
-
-def ffn_grads(where, n2s, gpres, acts, cotangent):
+    return result_kernel("mixer_result", keep, own, up, down, shapes, cut)
+
+
+def ffn_grads(where, n2s, gpres, acts, cotangent, w):
     parts = len(n2s)
     chunk, model = n2s[0].shape
     hidden = acts[0].shape[1]
     krows = model // UNITS
 
-    def kernel(where_ref, cot_ref, *rest):
+    def kernel(where_ref, cot_ref, w_ref, *rest):
         n2, gpre, act = rest[:parts], rest[parts : 2 * parts], rest[2 * parts : 3 * parts]
-        slot = slots(rest[3 * parts : 3 * parts + SLOTS])
-        scr, sem = rest[3 * parts + SLOTS :]
+        out_ref = rest[3 * parts]
+        slot = slots(rest[3 * parts + 1 : -2], FFN_FIRST, 1)
+        scr, sem = rest[-2:]
         piece = hidden // 3
         for j in range(3):
             cols = slice(j * piece, (j + 1) * piece)
@@ -552,9 +578,11 @@
         copies = []
         for u in range(UNITS):
             at = pl.ds(multiple(where_ref[u] * krows, 16), krows)
-            for n, (to, first, many) in enumerate(slot(u)):
-                copies.append(pltpu.make_async_copy(scr.at[at, pl.ds(first, many)], to, sem.at[u, n]))
-                copies[-1].start()
+            (to,) = slot(u)
+            copies.append(pltpu.make_async_copy(scr.at[at, :], to, sem.at[u]))
+            copies[-1].start()
+        for r in range(parts):
+            out_ref[r * chunk : (r + 1) * chunk, :] = mm(act[r][...], w_ref[:, hidden : 2 * hidden], NT).astype(BF)
         for copy in copies:
             copy.wait()
 
@@ -562,23 +590,11 @@
         kernel,
         "ffn_grads",
         (where,),
-        (cotangent, *n2s, *gpres, *acts),
-        (),
-        (pltpu.VMEM((model, 2 * hidden), BF), pltpu.SemaphoreType.DMA((UNITS, 2))),
-        loose_outs=slot_shapes(krows, 2 * hidden),
-    )
-
-
-def ffn_out(acts, w):
-    chunk, hidden = acts[0].shape
-    model = w.shape[0]
-
-    def kernel(*refs):
-        parts = len(refs) // 2
-        for act, out in zip(refs[:parts], refs[parts + 1 :]):
-            out[...] = mm(act[...], refs[parts][:, hidden : 2 * hidden], NT).astype(BF)
-
-    return run(kernel, "ffn_out", (), (*acts, w), [((chunk, model), BF)] * len(acts))
+        (cotangent, w, *n2s, *gpres, *acts),
+        (((chunk * parts, model), BF),),
+        (pltpu.VMEM((model, 2 * hidden), BF), pltpu.SemaphoreType.DMA((UNITS,))),
+        loose_outs=slot_shapes(krows, 2 * hidden, FFN_FIRST, 1, False),
+    )
 
 
 def cut_gain(row, krows):
@@ -662,23 +678,22 @@
     def one_head(h, carry):
         lanes = pl.ds(multiple((begin + h) * LANES, LANES), LANES)
         d = mm(xh_ref[:, lanes], va_ref[:, lanes], NT)
+        inverse = rb_ref[:, lanes]
         for q in range(length // LANES):
             cols = slice(q * LANES, (q + 1) * LANES)
-            ds[:, cols] = (e_ref[begin + h, :, cols].astype(F32) * rb_ref[:, lanes] * d[:, cols]).astype(BF)
+            ds[:, cols] = (e_ref[begin + h, :, cols].astype(F32) * inverse * d[:, cols]).astype(BF)
         for u in range(UNITS):
             at = pl.ds(multiple(where_ref[u] * rows, rows), rows)
-            for to, first, many in slot(u):
-                to[pl.ds(multiple(h * rows, rows), rows), :] = ds[at, first : first + many]
+            slot(u)[0][pl.ds(multiple(h * rows, rows), rows), :] = ds[at, :]
         return carry
 
     lax.fori_loop(0, count, one_head, 0)
 
 
-def value_back(xh, rb, e, wv, tokens, size):
+def value_back(xh, rb, e, wv, tokens, size, cut):
     length, model = tokens.shape
     heads = e.shape[0]
     width = heads * size
-    chunk = length // 2
     krows = model // UNITS
 
     def kernel(xh_ref, rb_ref, e_ref, wv_ref, tok_ref, gv_ref, part_one, part_two, ga_ref, acc):
@@ -688,14 +703,15 @@
             scaled = (xh_ref[:, lanes].astype(F32) * rb_ref[:, lanes]).astype(BF)
             gv_ref[:, h * size : (h + 1) * size] = mm(e_ref[h], scaled, TN)[:, :size].astype(BF)
 
-        for r, part_ref in enumerate((part_one, part_two)):
-            at = slice(r * chunk, (r + 1) * chunk)
+        for at, part_ref in ((slice(0, cut), part_one), (slice(cut, length), part_two)):
             part = mm(gv_ref[at, :], wv_ref[...], NT)
             part_ref[...] = part.astype(BF)
             x = tok_ref[at, :].astype(F32)
             inv = lax.rsqrt(jnp.mean(x * x, axis=-1, keepdims=True) + EPSILON)
-            acc[...] += jnp.sum((part * (x * inv)).reshape(chunk // 8, 8, model), axis=0)
-        ga_ref[...] = cut_gain(jnp.sum(acc[...], axis=0, keepdims=True), krows)
+            acc[...] += jnp.sum((part * (x * inv)).reshape((at.stop - at.start) // 8, 8, model), axis=0)
+
+        ga_ref[...] = jnp.zeros_like(ga_ref)
+        ga_ref[:UNITS, :] = cut_gain(jnp.sum(acc[...], axis=0, keepdims=True), krows)
 
     return run(
         kernel,
@@ -704,9 +720,9 @@
         (xh, rb, e, wv, tokens),
         (
             ((length, width), BF),
-            ((chunk, model), BF),
-            ((chunk, model), BF),
-            ((UNITS, LANES), F32),
+            ((cut, model), BF),
+            ((length - cut, model), BF),
+            ((4 * UNITS, LANES), F32),
         ),
         (pltpu.VMEM((8, model), F32),),
     )
@@ -719,17 +735,18 @@
 
     def kernel(where_ref, xh_ref, va_ref, e_ref, rb_ref, *rest):
         outs, ds = rest[:-1], rest[-1]
-        score_grads(where_ref, xh_ref, va_ref, e_ref, rb_ref, ds, slots(outs), 0, heads, rows)
+        score_grads(where_ref, xh_ref, va_ref, e_ref, rb_ref, ds, slots(outs, MIXER_FIRST, 2), 0, heads, rows)
         for u in range(UNITS):
-            for to, _, many in slots(outs)(u):
-                to[heads * rows :, :] = jnp.zeros((2 * krows, many), BF)
+            for n, to in enumerate(slots(outs, MIXER_FIRST, 2)(u)):
+                begin = 0 if n else heads * rows
+                to[begin:, :] = jnp.zeros((to.shape[0] - begin, length), BF)
 
     return run(
         kernel,
         "mixer_grads",
         (where,),
         (xh, va, e, rb),
-        slot_shapes(deep, length),
+        slot_shapes(deep, length, MIXER_FIRST, 2, False),
         (pltpu.VMEM((length, length), BF),),
     )
 
@@ -742,12 +759,12 @@
     top = deep - 2 * krows
 
     def kernel(where_ref, n1_ref, gv_ref, gat_ref, mixed_ref, ga_ref, gb_ref, gf_ref, *rest):
-        slot = slots(rest[SLOTS : 2 * SLOTS])
-        wide_v, wide_o, pieces = rest[2 * SLOTS :]
+        slot = slots(rest[len(parts) : 2 * len(parts)], MIXER_FIRST, 2)
+        wide_v, wide_o, pieces = rest[2 * len(parts) :]
         wide_v[:, :width] = mm(n1_ref[...], gv_ref[...], TN).astype(BF)
         wide_o[:, :width] = mm(gat_ref[...], mixed_ref[...], TN).astype(BF)
         wide_o[:, width:] = jnp.zeros((model, length - width), BF)
-        pieces[0] = ga_ref[...] + gb_ref[...]
+        pieces[0] = ga_ref[:UNITS, :] + gb_ref[:UNITS, :]
         pieces[1] = gf_ref[...]
         sub = lax.broadcasted_iota(jnp.int32, (krows, LANES), 0)
         for d in range(UNITS):
@@ -757,22 +774,26 @@
             wide_v[d * krows : (d + 1) * krows, width:] = both.astype(BF)
         for u in range(UNITS):
             at = pl.ds(multiple(where_ref[u] * krows, 16), krows)
-            for to, first, many in slot(u):
-                to[top : top + krows, :] = wide_v[at, first : first + many]
-                to[top + krows :, :] = wide_o[at, first : first + many]
+            to, *small = slot(u)
+            to[top : top + krows, :] = wide_v[at, :]
+            if small:
+                to[top + krows :, :] = wide_o[pl.ds(multiple(where_ref[u] * krows, 16), krows - SMALL), :]
+                small[0][...] = wide_o[pl.ds(multiple(where_ref[u] * krows + krows - SMALL, 16), SMALL), :]
+            else:
+                to[top + krows :, :] = wide_o[at, :]
 
     return run(
         kernel,
         "weight_grads",
         (where,),
         (n1, gv, gat, mixed, ga, ga_other, gf, *parts),
-        slot_shapes(deep, length),
+        slot_shapes(deep, length, MIXER_FIRST, 2, False),
         (
             pltpu.VMEM((model, length), BF),
             pltpu.VMEM((model, length), BF),
             pltpu.VMEM((2, UNITS, LANES), F32),
         ),
-        aliases={8 + n: n for n in range(SLOTS)},
+        aliases={8 + n: n for n in range(len(parts))},
     )
 
 
@@ -832,14 +853,15 @@
     def take(self, values):
         self.last = list(values)
 
-    def hop(self):
+    def hop(self, swap=True):
         ring = self.ring
         self.hops += 1
         up, down = self.last
         if self.hops == ring.chips // 2:
             up, down = up[: self.cut], down[self.cut :]
         self.last = [lax.ppermute(up, "dp", ring.up), lax.ppermute(down, "dp", ring.down)]
-        self.swap()
+        if swap:
+            self.swap()
         self.here = self.last
 
     def swap(self):
@@ -859,44 +881,46 @@
 
 
 class Scatter:
-    def __init__(self, ring, keep, *give):
+    def __init__(self, ring, first, pieces, keep, *give):
         self.ring = ring
         self.keep = keep
-        early, self.later = give[:2], list(give[2:])
-        self.early = [lax.ppermute(one, "dp", ring.swap) for one in early]
-        self.last = []
-        self.hops = 0
+        count = len(first) * pieces
+        swapped = [lax.ppermute(one, "dp", ring.swap) for one in give[:count]]
+        self.early = {k: swapped[n * pieces : (n + 1) * pieces] for n, k in enumerate(first)}
+        self.first = first
+        self.late = late_units(first)
+        self.later = give[count:]
+        self.got = {}
+        self.last = {}
 
     def values(self):
-        return self.last if self.hops else self.early
+        return list(self.last.values()) if self.last else [one for k in self.first for one in self.early[k]]
 
     def take(self, values):
-        if self.hops:
-            self.last = list(values)
+        if self.last:
+            self.last = dict(zip(self.last, values))
         else:
-            self.early = list(values)
-
-    def total(self, k, one):
-        group, place = late_place(k)
-        got = self.later[group][place]
-        return (self.keep[k].astype(F32) + got.astype(F32) + one.astype(F32)).astype(BF)
-
-    def hop(self):
-        ring = self.ring
-        far = ring.chips // 2
-        self.hops += 1
-        if self.hops == 1:
-            up, down = far_sum(far, self.keep, *self.early)
-            self.later = [lax.ppermute(tie(one, up), "dp", ring.swap) for one in self.later]
-        elif self.hops == 2:
-            up, down = next_sums(far, self.keep, self.later[0], *self.last)
+            pieces = len(values) // len(self.first)
+            self.early = {k: values[n * pieces : (n + 1) * pieces] for n, k in enumerate(self.first)}
+
+    def swap_all(self, *after):
+        stack = lax.ppermute(tie(self.later[0], *after), "dp", self.ring.swap)
+        self.got = {k: stack[n] for n, k in enumerate(self.late)}
+
+    def hop(self, way, k):
+        if k in self.early and len(self.early[k]) > 1:
+            value = pieces_sum(k, self.keep, self.early[k]).astype(F32)
         else:
-            up = self.total(far + 1 - self.hops, self.last[0])
-            down = self.total(far - 1 + self.hops, self.last[1])
-        self.last = [lax.ppermute(up, "dp", ring.up), lax.ppermute(down, "dp", ring.down)]
+            got = self.early[k][0] if k in self.early else self.got[k]
+            value = self.keep[k].astype(F32) + got.astype(F32)
+        if way in self.last:
+            value = value + self.last[way].astype(F32)
+        value = value.astype(BF)
+        self.last[way] = lax.ppermute(value, "dp", self.ring.up if way == "up" else self.ring.down)
+        return value
 
     def result(self):
-        return self.keep, self.later[-1], *self.last
+        return self.keep, self.got[0], self.last["up"], self.last["down"]
 
 
 def together(chains, *more):
@@ -945,24 +969,36 @@
         far = net.chips // 2
         where_in = net.gathered().astype(jnp.int32)
         where_out = net.scattered().astype(jnp.int32)
-        wo_other = lax.ppermute(w_output.T, "mp", flip)
-        unit = pack_unit(plan, random_scores, w_up, w_down.T)
-        unit = pack_rest(plan, second_at, unit, w_value, gain_attn, gain_ffn, w_output.T, wo_other)
+        unit, wo_own = pack_unit(
+            plan, second_at, random_scores, w_value, gain_attn, gain_ffn, w_up, w_down.T, w_output.T
+        )
         one = Gather(net, unit, plan.cut)
-        one.hop()
-        where_in, where_out = together([one], where_in, where_out)
+        one.hop(False)
+        wo_other = lax.ppermute(tie(wo_own, where_in, where_out), "mp", flip)
+        wo_next = [lax.ppermute(wo_other, "dp", way) for way in (net.up, net.down)]
+        one.here = list(fill_units(plan, second_at, [unit], [wo_other]))
+        one.swap()
+        wo_next = together([one], *wo_next)
+        one.last = list(fill_units(plan, second_at, one.last, wo_next))
+        one.here = one.last
         for step in range(1, far - 1):
             one.hop()
             together([one])
+            one.here = one.last
         there = one.mine + one.theirs
         shares = one.shares()
         half = len(shares) // 2
         early = [n for n in range(len(one.mine))] + [half + n for n in range(len(one.theirs))]
         one.hop()
-        e = mixer_first(plan, where_in, segment_ids, there, [shares[n] for n in early], heads)
-        (e,) = together([one], e)
+        begun = mixer_first(plan, where_in, tokens, segment_ids, there, [shares[n] for n in early], heads)
+        begun = together([one], *begun)
+        one.here = one.last
         units = one.finish()
         late = [n for n in range(len(shares)) if n not in early]
+        near = late
+        order = [n for n in range(len(shares)) if n not in near] + near
+        units, shares = [units[n] for n in order], [shares[n] for n in order]
+        late = [n for n, old in enumerate(order) if old in late]
     else:
         where_in = jnp.arange(UNITS, dtype=jnp.int32)
         where_out = where_in
@@ -987,14 +1023,14 @@
         whole = jnp.concatenate(stack, axis=1)
         units = [whole[u] for u in range(UNITS)]
         shares = [(u, 0, plan.deep) for u in range(UNITS)]
-        early, late = list(range(UNITS // 2)), list(range(UNITS // 2, UNITS))
-        e = mixer_first(plan, where_in, segment_ids, units[: UNITS // 2], shares[: UNITS // 2], heads)
-
-    e, va, mixed, mixf, rb, n1, gains, wv = mixer_forward(
-        plan, where_in, tokens, segment_ids, e, units, shares, late, heads, width
+        early, late, near = list(range(UNITS // 2)), list(range(UNITS // 2, UNITS)), []
+        begun = mixer_first(plan, where_in, tokens, segment_ids, units[: UNITS // 2], shares[: UNITS // 2], heads)
+
+    e, wv, _, va, mixed, sums, n1, gains = mixer_forward(
+        plan, where_in, segment_ids, begun, [units[n] for n in late], [shares[n] for n in late], heads, width
     )
     mixed_other = lax.ppermute(mixed, "mp", flip)
-    w, gact = second_weights(plan, where_in, cotangent, units, shares)
+    w, gact, mixf, rb = second_weights(plan, where_in, cotangent, sums, units, shares, len(near), size)
     backs, others, resids, n2s, acts, gpres = [], [], [], [], [], []
     for part in range(PARTS):
         *new, resid, n2, act, gpre = ffn_main(
@@ -1007,64 +1043,72 @@
         n2s.append(n2)
         acts.append(act)
         gpres.append(gpre)
-    parts_two = ffn_grads(where_out, n2s, gpres, acts, cotangent)
-    ffn = list(ffn_out(acts, w))
-    ffn_other = []
+    ffn, *parts_two = ffn_grads(where_out, n2s, gpres, acts, cotangent, w)
     if ring:
-        ffn_sum = Scatter(net, *parts_two)
-        ffn_sum.hop()
-        ffn_sum.hop()
-        cotangent, *both = lax.optimization_barrier((cotangent, *ffn, *others))
-        ffn, others = both[:PARTS], both[PARTS:]
-        ffn_other.append(lax.ppermute(ffn[0], "mp", flip))
+        ffn_sum = Scatter(net, FFN_FIRST, 1, *parts_two)
+        ffn_sum.swap_all(others[0], *ffn_sum.values())
+        for step in range(2):
+            ffn_sum.hop("down", far + step)
+            ffn_sum.hop("up", far - 1 - step)
+            together([ffn_sum])
     gres, gat, xh, gf = resid_back(
         second_at, backs, others, resids, cotangent, gains, w, mixf, heads, size
     )
-    gv, part_one, part_two, ga = value_back(xh, rb, e, wv, tokens, size)
+    ffn_cut = 7 * length // 16
+    ffn_one, ffn_two = ffn[:ffn_cut], ffn[ffn_cut:]
+    one_other = lax.ppermute(tie(ffn_one, xh), "mp", flip)
+    gv, part_one, part_two, ga = value_back(xh, rb, e, wv, tokens, size, length // 2)
     ga_other = lax.ppermute(ga, "mp", flip)
     if ring:
-        ffn_other[0], ffn[1] = together([ffn_sum], ffn_other[0], ffn[1])
-        ffn_sum.hop()
-        ffn_other.append(lax.ppermute(ffn[1], "mp", flip))
+        for step in range(2, far - 1):
+            ffn_sum.hop("down", far + step)
+            ffn_sum.hop("up", far - 1 - step)
     parts_one = mixer_grads(where_out, xh, va, e, rb, krows)
     parts_one = weight_grads(where_out, parts_one, n1, gv, gat, mixed, ga, ga_other, gf)
 
     top = heads * rows
     if ring:
-        score_sum = Scatter(net, *parts_one)
-        ffn_other[1], part_one = together([ffn_sum, score_sum], ffn_other[1], part_one)
-        ffn_sum.hop()
-        score_sum.hop()
-        part_other = [lax.ppermute(part_one, "mp", flip)]
-        part_other[0], part_two = together([ffn_sum, score_sum], part_other[0], part_two)
-        score_sum.hop()
-        part_other.append(lax.ppermute(part_two, "mp", flip))
-        together([score_sum])
-        score_sum.hop()
+        score_sum = Scatter(net, MIXER_FIRST, 2, *parts_one)
+        one_other, ffn_two = together([ffn_sum, score_sum], one_other, ffn_two)
+        value = score_sum.hop("up", far)
+        ffn_sum.hop("down", 2 * far - 1)
+        score_sum.swap_all(value)
+        two_other = lax.ppermute(ffn_two, "mp", flip)
+        part_one, part_two = together([ffn_sum, score_sum], part_one, part_two)
+        for step in range(1, far):
+            score_sum.hop("up", far - step)
+            score_sum.hop("down", far + step)
+            if step == 1:
+                part_other = [lax.ppermute(part_one, "mp", flip)]
+                two_other, part_two = together([score_sum], two_other, part_two)
+            elif step < far - 1:
+                part_other.append(lax.ppermute(part_two, "mp", flip))
+                (part_other[0],) = together([score_sum], part_other[0])
         out_up, out_down = ffn_result(*ffn_sum.result())
-        (part_other[1],) = together([score_sum], part_other[1])
-        score_sum.hop()
         out_scores, out_value, out_output, *out_gains = mixer_result(*score_sum.result(), heads, krows, width)
         out_down, out_output = out_down.T, out_output.T
         out_gain_one, out_gain_two = [one.reshape(krows) for one in out_gains]
     else:
-        ffn_other = [lax.ppermute(one, "mp", flip) for one in ffn]
+        two_other = lax.ppermute(ffn_two, "mp", flip)
         part_other = [lax.ppermute(one, "mp", flip) for one in (part_one, part_two)]
 
         def scatter(one, axis=0):
             return lax.psum_scatter(one, "dp", scatter_dimension=axis, tiled=True)
 
-        def whole(keep, early, second, *later):
-            far = UNITS // 4
+        def whole(first, pieces, keep, *give):
+            late = late_units(first)
+            early, later = give[: len(first) * pieces], give[len(first) * pieces :]
             given = []
             for k in range(UNITS // 2):
-                group, place = late_place(k) if k != far else (0, 0)
-                one = later[group][place] if k != far else jnp.concatenate([early, second], axis=1)
-                given.append(one)
+                if k in first:
+                    at = first.index(k) * pieces
+                    given.append(jnp.concatenate(early[at : at + pieces]))
+                else:
+                    given.append(later[0][late.index(k)] if len(later) == 1 else later[late.index(k)])
             return jnp.concatenate([keep, jnp.stack(given)]).astype(F32)
 
-        two = whole(*parts_two).reshape(model, -1)
-        one = whole(*parts_one)
+        two = whole(FFN_FIRST, 1, *parts_two).reshape(model, -1)
+        one = whole(MIXER_FIRST, 2, *parts_one)
         out_up = scatter(two[:, : two.shape[1] // 2])
         out_down = scatter(two[:, two.shape[1] // 2 :]).T
         scores = one[:, :top].reshape(UNITS, heads, rows, length).transpose(1, 0, 2, 3)
@@ -1073,15 +1117,14 @@
         out_output = scatter(one[:, top + krows :, :width].reshape(model, width)).T
         out_gain_one = scatter(one[:, top, width : width + krows].reshape(model))
         out_gain_two = scatter(one[:, top + 1, width : width + krows].reshape(model))
-    outputs = [
-        (resid + (mine.astype(F32) + other.astype(F32))).astype(BF)
-        for resid, mine, other in zip(resids, ffn, ffn_other)
-    ]
-    output = jnp.concatenate(outputs)
+    ffn_other = jnp.concatenate([one_other, two_other])
+    output = (jnp.concatenate(resids) + (ffn.astype(F32) + ffn_other.astype(F32))).astype(BF)
     backs = []
-    for r, (mine, other) in enumerate(zip((part_one, part_two), part_other)):
+    begin = 0
+    for mine, other in zip((part_one, part_two), part_other):
         grad_n1 = mine.astype(F32) + other.astype(F32)
-        at = slice(r * mine.shape[0], (r + 1) * mine.shape[0])
+        at = slice(begin, begin + mine.shape[0])
+        begin = at.stop
         x = tokens[at].astype(F32)
         inv = lax.rsqrt(jnp.mean(x * x, axis=-1, keepdims=True) + EPSILON)
         z = gains[0:1, :] * grad_n1

time: 177 us -> 162 us (0.915)
  waiting for transfers between devices: 85.7 us -> 76.1 us
  starting transfers between devices: 41.7 us -> 38.7 us
    ppermute x15 -> x25, waiting for transfers between devices: 3.71 us -> 40.5 us  [the longest x14 26.9 us: hop(): lax.ppermute(value, 'dp', self.ring.up if way == 'up' else self.ring.down)]
    ppermute x12 -> x4, waiting for transfers between devices: 33.4 us -> 2.68 us  [hop(): lax.ppermute(down, 'dp', ring.down)]
    ppermute x12 -> x4, starting transfers between devices: 16.8 us -> 1.4 us  [hop(): lax.ppermute(down, 'dp', ring.down)]
    ppermute x15 -> x25, starting transfers between devices: 6.71 us -> 21.3 us  [the longest x14 14.7 us: hop(): lax.ppermute(value, 'dp', self.ring.up if way == 'up' else self.ring.down)]
    ppermute x12 -> x4, waiting for transfers between devices: 34.3 us -> 24.4 us  [hop(): lax.ppermute(up, 'dp', ring.up)]
    ppermute x2, waiting for transfers between devices: 6.97 us -> 1.09 us  [shards(): others.append(lax.ppermute(tie(back, *others[-1:]), 'mp', flip))]
    ppermute x1, waiting for transfers between devices: 3.61 us -> 1.02 us  [shards(): part_other.append(lax.ppermute(part_two, 'mp', flip))]
    ppermute x12 -> x4, starting transfers between devices: 9.72 us -> 7.91 us  [hop(): lax.ppermute(up, 'dp', ring.up)]
  transfers between devices with their start and end apart: 54 -> 48, of which waited for: 24 -> 28; matrix products, arithmetic and copies ran while one was open for 3% -> 4% of each run, Pallas kernels for 17% -> 18%
where the time goes in v4:
time: 162 us
  waiting for transfers between devices  76.1 us (47%)
  Pallas kernels  39.1 us (24%)
  starting transfers between devices  38.7 us (24%)
  other arithmetic  5.64 us (3%)
    pallas_call x16, Pallas kernels, run(): pl.pallas_call(kernel, out_shape=tuple(results), in_specs=specs, out_spec...  39.1 us
    ppermute x14, waiting for transfers between devices, hop(): lax.ppermute(value, 'dp', self.ring.up if way == 'up' else self.ring.down)  26.9 us
    ppermute x4, waiting for transfers between devices, hop(): lax.ppermute(up, 'dp', ring.up)  24.4 us
    ppermute x14, starting transfers between devices, hop(): lax.ppermute(value, 'dp', self.ring.up if way == 'up' else self.ring.down)  14.7 us
    ppermute x2, waiting for transfers between devices, shards(): wo_next = [lax.ppermute(wo_other, 'dp', way) for way in (net.up, net.down)]  9.06 us
    ppermute x4, starting transfers between devices, hop(): lax.ppermute(up, 'dp', ring.up)  7.91 us
    ppermute x1, waiting for transfers between devices, shards(): mixed_other = lax.ppermute(mixed, 'mp', flip)  3.89 us
  transfers between devices with their start and end apart: 48, of which 28 were waited for; matrix products, arithmetic and copies ran while one was open for 4% of the time, Pallas kernels for 18%

profile of v4, /device:TPU:0, one launch (start us, length us, event | category | flops | bytes accessed | tf_op | source)
XLA Modules:
  0.0 162.2 jit_solution(1433088152525740635)
XLA Ops:
  0.6 1.4 pack_unit.1
  2.0 3.1 %collective-permute-start = (bf16[592,512]{1,0:T(8,128)(2,1)S(1)}, bf16[592,512]{1,0:T(8,128)(2,1)S(1)}, u32[]{:S(2)}, u32[]{:S(2)}) collective-permute-start(bf16[592,512]{1,0:T(8,128)(2,1)S(1)} %get-tuple-element.107.rest_0_), channel_id=1, source_target_pairs={{0,8},{2,10},{8,16},{10,18},{16,24},{18,26},{24,28},{26,30},{28,20... | collective-permute-start | bytes 1818632 | tf_op jit(solution)/shard_map/ppermute | solution.py:862
  5.1 0.7 broadcast_add_fusion.3
  6.0 2.0 %collective-permute-start.2 = (bf16[48,384]{1,0:T(8,128)(2,1)S(1)}, bf16[48,384]{1,0:T(8,128)(2,1)S(1)}, u32[]{:S(2)}, u32[]{:S(2)}) collective-permute-start(bf16[48,384]{1,0:T(8,128)(2,1)S(1)} %get-tuple-element.109), channel_id=1, source_target_pairs={{0,1},{1,0},{2,3},{3,2},{4,5},{5,4},{6,7},{7,6},{8,9},{9,8},{10,11... | collective-permute-start | bytes 110600 | tf_op jit(solution)/shard_map/ppermute | solution.py:977
  8.0 2.0 %collective-permute-done.2.rest_1_ = bf16[48,384]{1,0:T(8,128)(2,1)S(1)} collective-permute-done((bf16[48,384]{1,0:T(8,128)(2,1)S(1)}, bf16[48,384]{1,0:T(8,128)(2,1)S(1)}, u32[]{:S(2)}, u32[]{:S(2)}) %collective-permute-start.2) | collective-permute-done | bytes 36896 | tf_op jit(solution)/shard_map/ppermute | solution.py:977
  10.0 2.0 %collective-permute-start.3 = (bf16[48,384]{1,0:T(8,128)(2,1)S(1)}, bf16[48,384]{1,0:T(8,128)(2,1)S(1)}, u32[]{:S(2)}, u32[]{:S(2)}) collective-permute-start(bf16[48,384]{1,0:T(8,128)(2,1)S(1)} %collective-permute-done.2.rest_1_), channel_id=1, source_target_pairs={{0,8},{2,10},{8,16},{10,18},{16,24},{18,26},{24,28},{26,30},{28,20... | collective-permute-start | bytes 110600 | tf_op jit(solution)/shard_map/ppermute | solution.py:978
  12.0 7.5 %collective-permute-done.3.rest_2_ = bf16[48,384]{1,0:T(8,128)(2,1)S(1)} collective-permute-done((bf16[48,384]{1,0:T(8,128)(2,1)S(1)}, bf16[48,384]{1,0:T(8,128)(2,1)S(1)}, u32[]{:S(2)}, u32[]{:S(2)}) %collective-permute-start.3) | collective-permute-done | bytes 36896 | tf_op jit(solution)/shard_map/ppermute | solution.py:978
  19.5 1.5 collective-permute-done.4.rest_3_
  21.1 1.6 %collective-permute-start.5 = (bf16[592,512]{1,0:T(8,128)(2,1)S(1)}, bf16[592,512]{1,0:T(8,128)(2,1)S(1)}, u32[]{:S(2)}, u32[]{:S(2)}) collective-permute-start(bf16[592,512]{1,0:T(8,128)(2,1)S(1)} %get-tuple-element.114.rest_1_), channel_id=1, source_target_pairs={{0,8},{2,10},{8,16},{10,18},{16,24},{18,26},{24,28},{26,30},{28,20... | collective-permute-start | bytes 1818632 | tf_op jit(solution)/shard_map/ppermute | solution.py:862
  23.2 12.2 %collective-permute-done.5.rest_3_ = bf16[592,512]{1,0:T(8,128)(2,1)S(1)} collective-permute-done((bf16[592,512]{1,0:T(8,128)(2,1)S(1)}, bf16[592,512]{1,0:T(8,128)(2,1)S(1)}, u32[]{:S(2)}, u32[]{:S(2)}) %collective-permute-start.5) | collective-permute-done | bytes 606240 | tf_op jit(solution)/shard_map/ppermute | solution.py:862
  35.4 1.3 collective-permute-done.6.rest_4_
  36.7 1.6 collective-permute-start.7
  39.3 10.4 %collective-permute-done.7.rest_0_.rest_10_ = bf16[592,512]{1,0:T(8,128)(2,1)S(1)} collective-permute-done((bf16[592,512]{1,0:T(8,128)(2,1)S(1)}, bf16[592,512]{1,0:T(8,128)(2,1)S(1)}, u32[]{:S(2)}, u32[]{:S(2)}) %collective-permute-start.7) | collective-permute-done | bytes 606240 | tf_op jit(solution)/shard_map/ppermute | solution.py:862
  49.7 1.3 collective-permute-done.8.rest_1_.rest_11_
  51.6 1.6 %collective-permute-start.9 = (bf16[288,512]{1,0:T(8,128)(2,1)S(1)}, bf16[288,512]{1,0:T(8,128)(2,1)S(1)}, u32[]{:S(2)}, u32[]{:S(2)}) collective-permute-start(bf16[288,512]{1,0:T(8,128)(2,1)S(1)} %slice.106), channel_id=1, source_target_pairs={{0,8},{2,10},{8,16},{10,18},{16,24},{18,26},{24,28},{26,30},{28,20... | collective-permute-start | bytes 884744 | tf_op jit(solution)/shard_map/ppermute | solution.py:862
  54.3 0.9 copy-done.12
  55.1 3.8 %mixer_first.1 = (bf16[6,512,512]{2,1,0:T(8,128)(2,1)S(1)}, bf16[768,384]{1,0:T(8,128)(2,1)S(1)}, bf16[16,16,128]{2,1,0:T(8,128)(2,1)S(1)}, f32[512,768]{1,0:T(8,128)S(1)}) custom-call(s32[16]{0:T(128)S(1)} %pad_add_fusion.where_ref, bf16[512,768]{1,0:T(8,128)(2,1)S(1)} %copy-done, s32[1,512]{1,0:T(1,128)S(1)} %copy-done.5, bf16[592,512]{1,0:T(8,128)(2,1)} %copy-done.2, ...), custom_call_target="tpu_custom_call" | custom-call | flops 1 | bytes 1 | tf_op jit(solution)/shard_map/mixer_first/pallas_call | solution.py:36
  59.0 1.8 %collective-permute-done.9.rest_2_.rest_12_ = bf16[288,512]{1,0:T(8,128)(2,1)S(1)} collective-permute-done((bf16[288,512]{1,0:T(8,128)(2,1)S(1)}, bf16[288,512]{1,0:T(8,128)(2,1)S(1)}, u32[]{:S(2)}, u32[]{:S(2)}) %collective-permute-start.9) | collective-permute-done | bytes 294944 | tf_op jit(solution)/shard_map/ppermute | solution.py:862
  61.4 1.5 collective-permute-done.18.rest_6_.rest_16_
  62.9 5.2 %mixer_forward.1 = (bf16[6,512,512]{2,1,0:T(8,128)(2,1)S(1)}, bf16[768,384]{1,0:T(8,128)(2,1)S(1)}, bf16[16,16,128]{2,1,0:T(8,128)(2,1)S(1)}, bf16[512,768]{1,0:...) custom-call(s32[16]{0:T(128)S(1)} %pad_add_fusion.where_ref, ...), custom_call_target="tpu_custom_call", output_to_operand_aliasing={{0}: (2, {}), {1}: (3, {}), {2}: (4, {})} | custom-call | flops 1 | bytes 1 | tf_op jit(solution)/shard_map/mixer_forward/pallas_call | solution.py:36
  68.1 1.6 collective-permute-start.20
  69.7 5.7 %second_weights.1 = (bf16[768,3840]{1,0:T(8,128)(2,1)S(1)}, f32[512,1536]{1,0:T(8,128)S(1)}, f32[512,768]{1,0:T(8,128)S(1)}, f32[512,768]{1,0:T(8,128)S(1)}) custom-call(s32[16]{0:T(128)S(1)} %pad_add_fusion.where_ref, bf16[512,768]{1,0:T(8,128)(2,1)S(1)} %copy-done.1, f32[512,768]{1,0:T(8,128)S(1)} %get-tuple-element.131.sums_ref, ...), custom_call_target="tpu_custom_call" | custom-call | flops 1 | bytes 1 | tf_op jit(solution)/shard_map/second_weights/pallas_call | solution.py:36
  75.4 3.9 %collective-permute-done.20.other_ref = bf16[512,384]{1,0:T(8,128)(2,1)S(1)} collective-permute-done((bf16[512,384]{1,0:T(8,128)(2,1)S(1)}, bf16[512,384]{1,0:T(8,128)(2,1)S(1)}, u32[]{:S(2)}, u32[]{:S(2)}) %collective-permute-start.20) | collective-permute-done | bytes 393248 | tf_op jit(solution)/shard_map/ppermute | solution.py:1032
  79.3 3.1 %ffn_main.2 = (bf16[256,768]{1,0:T(8,128)(2,1)S(1)}, f32[256,768]{1,0:T(8,128)S(1)}, bf16[256,768]{1,0:T(8,128)(2,1)S(1)}, bf16[256,1536]{1,0:T(8,128)(2,1)S(1)}, bf16[256,1536]{1,0:T(8,128)(2,1)S(1)}) custom-call(s32[1]{0:T(128)} %bitcast.second_ref, bf16[512,768]{1,0:T(8,128)(2,1)S(1)} %copy-done, ...), custom_call_target="tpu_custom_call" | custom-call | flops 1 | bytes 1 | tf_op jit(solution)/shard_map/ffn_main/pallas_call | solution.py:36
  82.4 1.6 collective-permute-start.21
  84.0 3.0 %ffn_main.3 = (bf16[256,768]{1,0:T(8,128)(2,1)S(1)}, f32[256,768]{1,0:T(8,128)S(1)}, bf16[256,768]{1,0:T(8,128)(2,1)S(1)}, bf16[256,1536]{1,0:T(8,128)(2,1)S(1)}, bf16[256,1536]{1,0:T(8,128)(2,1)S(1)}) custom-call(s32[1]{0:T(128)} %bitcast.second_ref, bf16[512,768]{1,0:T(8,128)(2,1)S(1)} %copy-done, ...), custom_call_target="tpu_custom_call" | custom-call | flops 1 | bytes 1 | tf_op jit(solution)/shard_map/ffn_main/pallas_call | solution.py:36
  87.0 6.0 %ffn_grads.1 = (bf16[512,768]{1,0:T(8,128)(2,1)S(1)}, bf16[8,48,3072]{2,1,0:T(8,128)(2,1)S(1)}, bf16[48,3072]{1,0:T(8,128)(2,1)S(1)}, bf16[48,3072]{1,0:T(8,128)(2,1)S(1)}, bf16[6,48,3072]{2,1,0:T(8,128)(2,1)S(1)}) custom-call(s32[16]{0:T(128)S(1)} %pad_add_fusion.1.where_ref, bf16[512,768]{1,0:T(8,128)(2,1)S(1)} %copy-done.1, ...), custom_call_target="tpu_custom_call" | custom-call | flops 1 | bytes 1 | tf_op jit(solution)/shard_map/ffn_grads/pallas_call | solution.py:36
  93.6 1.1 collective-permute-done.22
  95.9 1.6 collective-permute-start.26
  98.0 6.7 %collective-permute-done.25 = bf16[48,3072]{1,0:T(8,128)(2,1)S(1)} collective-permute-done((bf16[48,3072]{1,0:T(8,128)(2,1)S(1)}, bf16[48,3072]{1,0:T(8,128)(2,1)S(1)}, u32[]{:S(2)}, u32[]{:S(2)}) %collective-permute-start.25) | collective-permute-done | bytes 294944 | tf_op jit(solution)/shard_map/ppermute | solution.py:919
  105.1 0.8 collective-permute-start.27
  106.0 1.2 collective-permute-start.28
  107.2 1.1 collective-permute-done.31.rest_3_
  108.3 2.9 %resid_back.1 = (f32[512,768]{1,0:T(8,128)S(1)}, bf16[512,768]{1,0:T(8,128)(2,1)S(1)}, bf16[512,768]{1,0:T(8,128)(2,1)S(1)}, f32[16,128]{1,0:T(8,128)S(1)}) custom-call(s32[1]{0:T(128)} %bitcast.second_ref, bf16[512,768]{1,0:T(8,128)(2,1)S(1)} %copy-done.1, f32[2,768]{1,0:T(2,128)S(1)} %get-tuple-element.133.gains_ref, ...), custom_call_target="tpu_custom_call" | custom-call | flops 1 | bytes 1 | tf_op jit(solution)/shard_map/resid_back/pallas_call | solution.py:36
  111.2 0.6 collective-permute-start.35
  111.8 1.8 %value_back.1 = (bf16[512,384]{1,0:T(8,128)(2,1)S(1)}, bf16[256,768]{1,0:T(8,128)(2,1)S(1)}, bf16[256,768]{1,0:T(8,128)(2,1)S(1)}, f32[64,128]{1,0:T(8,128)S(1)}) custom-call(bf16[512,768]{1,0:T(8,128)(2,1)S(1)} %get-tuple-element.158.xh_ref, f32[512,768]{1,0:T(8,128)S(1)} %get-tuple-element.159.rb_ref, bf16[6,512,512]{2,1,0:T(8,128)(2,1)S(1)} %get-tuple-element.160.e_ref, ...), custom_call_target="tpu_custom_call" | custom-call | flops 1 | bytes 1 | tf_op jit(solution)/shard_map/value_back/pallas_call | solution.py:36
  113.6 1.6 collective-permute-start.32
  115.9 1.6 collective-permute-start.30
  117.5 2.7 %mixer_grads.1 = (bf16[8,288,512]{2,1,0:T(8,128)(2,1)S(1)}, bf16[272,512]{1,0:T(8,128)(2,1)S(1)}, bf16[16,512]{1,0:T(8,128)(2,1)S(1)}, bf16[7,288,512]{2,1,0:T(8,128)(2,1)S(1)}) custom-call(s32[16]{0:T(128)S(1)} %pad_add_fusion.1.where_ref, bf16[512,768]{1,0:T(8,128)(2,1)S(1)} %get-tuple-element.158.xh_ref, bf16[512,768]{1,0:T(8,128)(2,1)S(1)} %get-tuple-element.166.va_ref, ...), custom_call_target="tpu_custom_call" | custom-call | flops 1 | bytes 1 | tf_op jit(solution)/shard_map/mixer_grads/pallas_call | solution.py:36
  120.2 0.7 collective-permute-done.32.gb_ref
  120.9 1.6 weight_grads.1
  123.1 1.0 collective-permute-done.34.refs_1_
  124.7 1.6 collective-permute-start.38
  126.4 0.6 collective-permute-start.37
  127.0 0.6 collective-permute-start.41
  127.5 6.5 %collective-permute-done.38 = bf16[288,512]{1,0:T(8,128)(2,1)S(1)} collective-permute-done((bf16[288,512]{1,0:T(8,128)(2,1)S(1)}, bf16[288,512]{1,0:T(8,128)(2,1)S(1)}, u32[]{:S(2)}, u32[]{:S(2)}) %collective-permute-start.38) | collective-permute-done | bytes 294944 | tf_op jit(solution)/shard_map/ppermute | solution.py:919
  134.0 1.4 collective-permute-done.37.down_ref
  135.5 0.6 collective-permute-start.40
  136.2 1.6 collective-permute-start.39
  137.8 0.6 collective-permute-start.44
  138.3 0.9 ffn_result.1
  139.3 4.4 %collective-permute-done.40 = bf16[288,512]{1,0:T(8,128)(2,1)S(1)} collective-permute-done((bf16[288,512]{1,0:T(8,128)(2,1)S(1)}, bf16[288,512]{1,0:T(8,128)(2,1)S(1)}, u32[]{:S(2)}, u32[]{:S(2)}) %collective-permute-start.40) | collective-permute-done | bytes 294944 | tf_op jit(solution)/shard_map/ppermute | solution.py:919
  144.3 1.6 collective-permute-start.42
  146.4 0.6 collective-permute-start.45
  147.0 1.1 fusion
  148.4 2.9 %collective-permute-done.42 = bf16[288,512]{1,0:T(8,128)(2,1)S(1)} collective-permute-done((bf16[288,512]{1,0:T(8,128)(2,1)S(1)}, bf16[288,512]{1,0:T(8,128)(2,1)S(1)}, u32[]{:S(2)}, u32[]{:S(2)}) %collective-permute-start.42) | collective-permute-done | bytes 294944 | tf_op jit(solution)/shard_map/ppermute | solution.py:919
  151.3 1.3 collective-permute-done.43
  152.9 1.5 collective-permute-start.46
  154.9 1.0 collective-permute-done.45
  156.5 0.6 fusion.14
  157.1 0.9 pad_maximum_fusion
  158.0 1.6 collective-permute-done.46.up_ref
  159.6 1.5 collective-permute-done.47.down_ref
  161.1 0.9 mixer_result.1
  (102 shorter events, 11.4 us)
Async XLA Ops:
  2.0 19.0 %collective-permute-start = (bf16[592,512]{1,0:T(8,128)(2,1)S(1)}, bf16[592,512]{1,0:T(8,128)(2,1)S(1)}, u32[]{:S(2)}, u32[]{:S(2)}) collective-permute-start(bf16[592,512]{1,0:T(8,128)(2,1)S(1)} %get-tuple-element.107.rest_0_), channel_id=1, source_target_pairs={{0,8},{2,10},{8,16},{10,18},{16,24},{18,26},{24,28},{26,30},{28,20... | collective-permute-start | bytes 1818632 | tf_op jit(solution)/shard_map/ppermute | solution.py:862
  5.1 15.9 %collective-permute-start.1 = (bf16[592,512]{1,0:T(8,128)(2,1)S(1)}, bf16[592,512]{1,0:T(8,128)(2,1)S(1)}, u32[]{:S(2)}, u32[]{:S(2)}) collective-permute-start(bf16[592,512]{1,0:T(8,128)(2,1)S(1)} %get-tuple-element.107.rest_0_), channel_id=1, source_target_pairs={{0,4},{2,6},{8,0},{10,2},{16,8},{18,10},{24,16},{26,18},{28,24},{3... | collective-permute-start | bytes 1818632 | tf_op jit(solution)/shard_map/ppermute | solution.py:862
  6.0 49.2 %copy-start = (bf16[512,768]{1,0:T(8,128)(2,1)S(1)}, bf16[512,768]{1,0:T(8,128)(2,1)}, u32[]{:S(2)}) copy-start(bf16[512,768]{1,0:T(8,128)(2,1)} %tok_ref.7) | copy-start | bytes 2359300
  6.0 49.2 %copy-start.5 = (s32[1,512]{1,0:T(1,128)S(1)}, s32[1,512]{1,0:T(1,128)}, u32[]{:S(2)}) copy-start(s32[1,512]{1,0:T(1,128)} %seg_ref.3) | copy-start | bytes 6148
  6.0 4.0 %collective-permute-start.2 = (bf16[48,384]{1,0:T(8,128)(2,1)S(1)}, bf16[48,384]{1,0:T(8,128)(2,1)S(1)}, u32[]{:S(2)}, u32[]{:S(2)}) collective-permute-start(bf16[48,384]{1,0:T(8,128)(2,1)S(1)} %get-tuple-element.109), channel_id=1, source_target_pairs={{0,1},{1,0},{2,3},{3,2},{4,5},{5,4},{6,7},{7,6},{8,9},{9,8},{10,11... | collective-permute-start | bytes 110600 | tf_op jit(solution)/shard_map/ppermute | solution.py:977
  10.0 9.5 %collective-permute-start.3 = (bf16[48,384]{1,0:T(8,128)(2,1)S(1)}, bf16[48,384]{1,0:T(8,128)(2,1)S(1)}, u32[]{:S(2)}, u32[]{:S(2)}) collective-permute-start(bf16[48,384]{1,0:T(8,128)(2,1)S(1)} %collective-permute-done.2.rest_1_), channel_id=1, source_target_pairs={{0,8},{2,10},{8,16},{10,18},{16,24},{18,26},{24,28},{26,30},{28,20... | collective-permute-start | bytes 110600 | tf_op jit(solution)/shard_map/ppermute | solution.py:978
  12.0 9.1 %collective-permute-start.4 = (bf16[48,384]{1,0:T(8,128)(2,1)S(1)}, bf16[48,384]{1,0:T(8,128)(2,1)S(1)}, u32[]{:S(2)}, u32[]{:S(2)}) collective-permute-start(bf16[48,384]{1,0:T(8,128)(2,1)S(1)} %collective-permute-done.2.rest_1_), channel_id=1, source_target_pairs={{0,4},{2,6},{8,0},{10,2},{16,8},{18,10},{24,16},{26,18},{28,24},{3... | collective-permute-start | bytes 110600 | tf_op jit(solution)/shard_map/ppermute | solution.py:978
  21.1 32.7 %copy-start.3 = (bf16[592,512]{1,0:T(8,128)(2,1)}, bf16[592,512]{1,0:T(8,128)(2,1)S(1)}, u32[]{:S(2)}) copy-start(bf16[592,512]{1,0:T(8,128)(2,1)S(1)} %get-tuple-element.114.rest_1_) | copy-start | bytes 1818628
  21.1 32.7 %copy-start.4 = (bf16[592,512]{1,0:T(8,128)(2,1)}, bf16[592,512]{1,0:T(8,128)(2,1)S(1)}, u32[]{:S(2)}) copy-start(bf16[592,512]{1,0:T(8,128)(2,1)S(1)} %get-tuple-element.115.rest_2_) | copy-start | bytes 1818628
  21.1 14.3 %collective-permute-start.5 = (bf16[592,512]{1,0:T(8,128)(2,1)S(1)}, bf16[592,512]{1,0:T(8,128)(2,1)S(1)}, u32[]{:S(2)}, u32[]{:S(2)}) collective-permute-start(bf16[592,512]{1,0:T(8,128)(2,1)S(1)} %get-tuple-element.114.rest_1_), channel_id=1, source_target_pairs={{0,8},{2,10},{8,16},{10,18},{16,24},{18,26},{24,28},{26,30},{28,20... | collective-permute-start | bytes 1818632 | tf_op jit(solution)/shard_map/ppermute | solution.py:862
  22.7 13.9 %collective-permute-start.6 = (bf16[592,512]{1,0:T(8,128)(2,1)S(1)}, bf16[592,512]{1,0:T(8,128)(2,1)S(1)}, u32[]{:S(2)}, u32[]{:S(2)}) collective-permute-start(bf16[592,512]{1,0:T(8,128)(2,1)S(1)} %get-tuple-element.115.rest_2_), channel_id=1, source_target_pairs={{0,4},{2,6},{8,0},{10,2},{16,8},{18,10},{24,16},{26,18},{28,24},{3... | collective-permute-start | bytes 1818632 | tf_op jit(solution)/shard_map/ppermute | solution.py:862
  35.4 18.4 %copy-start.6 = (bf16[592,512]{1,0:T(8,128)(2,1)}, bf16[592,512]{1,0:T(8,128)(2,1)S(1)}, u32[]{:S(2)}) copy-start(bf16[592,512]{1,0:T(8,128)(2,1)S(1)} %collective-permute-done.5.rest_3_) | copy-start | bytes 1818628
  36.7 17.1 %copy-start.7 = (bf16[592,512]{1,0:T(8,128)(2,1)}, bf16[592,512]{1,0:T(8,128)(2,1)S(1)}, u32[]{:S(2)}) copy-start(bf16[592,512]{1,0:T(8,128)(2,1)S(1)} %collective-permute-done.6.rest_4_) | copy-start | bytes 1818628
  36.7 13.0 %collective-permute-start.7 = (bf16[592,512]{1,0:T(8,128)(2,1)S(1)}, bf16[592,512]{1,0:T(8,128)(2,1)S(1)}, u32[]{:S(2)}, u32[]{:S(2)}) collective-permute-start(bf16[592,512]{1,0:T(8,128)(2,1)S(1)} %collective-permute-done.5.rest_3_), channel_id=1, source_target_pairs={{0,8},{2,10},{8,16},{10,18},{16,24},{18,26},{24,28},{26,30},{28,20... | collective-permute-start | bytes 1818632 | tf_op jit(solution)/shard_map/ppermute | solution.py:862
  38.2 12.7 %collective-permute-start.8 = (bf16[592,512]{1,0:T(8,128)(2,1)S(1)}, bf16[592,512]{1,0:T(8,128)(2,1)S(1)}, u32[]{:S(2)}, u32[]{:S(2)}) collective-permute-start(bf16[592,512]{1,0:T(8,128)(2,1)S(1)} %collective-permute-done.6.rest_4_), channel_id=1, source_target_pairs={{0,4},{2,6},{8,0},{10,2},{16,8},{18,10},{24,16},{26,18},{28,24},{3... | collective-permute-start | bytes 1818632 | tf_op jit(solution)/shard_map/ppermute | solution.py:862
  38.7 12.3 %collective-permute-start.12 = (bf16[592,512]{1,0:T(8,128)(2,1)S(1)}, bf16[592,512]{1,0:T(8,128)(2,1)S(1)}, u32[]{:S(2)}, u32[]{:S(2)}) collective-permute-start(bf16[592,512]{1,0:T(8,128)(2,1)S(1)} %get-tuple-element.114.rest_1_), channel_id=1, source_target_pairs={{0,2},{2,0},{4,6},{6,4},{8,10},{10,8},{12,14},{14,12},{16,18},{18,... | collective-permute-start | bytes 1818632 | tf_op jit(solution)/shard_map/ppermute | solution.py:868
  38.7 12.9 %collective-permute-start.13 = (bf16[592,512]{1,0:T(8,128)(2,1)S(1)}, bf16[592,512]{1,0:T(8,128)(2,1)S(1)}, u32[]{:S(2)}, u32[]{:S(2)}) collective-permute-start(bf16[592,512]{1,0:T(8,128)(2,1)S(1)} %get-tuple-element.115.rest_2_), channel_id=1, source_target_pairs={{0,2},{2,0},{4,6},{6,4},{8,10},{10,8},{12,14},{14,12},{16,18},{18,... | collective-permute-start | bytes 1818632 | tf_op jit(solution)/shard_map/ppermute | solution.py:868
  39.2 14.6 %copy-start.2 = (bf16[592,512]{1,0:T(8,128)(2,1)}, bf16[592,512]{1,0:T(8,128)(2,1)S(1)}, u32[]{:S(2)}) copy-start(bf16[592,512]{1,0:T(8,128)(2,1)S(1)} %fill_units.3.rest_0_) | copy-start | bytes 1818628
  39.2 14.0 %collective-permute-start.11 = (bf16[592,512]{1,0:T(8,128)(2,1)S(1)}, bf16[592,512]{1,0:T(8,128)(2,1)S(1)}, u32[]{:S(2)}, u32[]{:S(2)}) collective-permute-start(bf16[592,512]{1,0:T(8,128)(2,1)S(1)} %fill_units.3.rest_0_), channel_id=1, source_target_pairs={{0,2},{2,0},{4,6},{6,4},{8,10},{10,8},{12,14},{14,12},{16,18},{18,... | collective-permute-start | bytes 1818632 | tf_op jit(solution)/shard_map/ppermute | solution.py:868
  49.7 3.5 %collective-permute-start.14 = (bf16[592,512]{1,0:T(8,128)(2,1)S(1)}, bf16[592,512]{1,0:T(8,128)(2,1)S(1)}, u32[]{:S(2)}, u32[]{:S(2)}) collective-permute-start(bf16[592,512]{1,0:T(8,128)(2,1)S(1)} %collective-permute-done.5.rest_3_), channel_id=1, source_target_pairs={{0,2},{2,0},{4,6},{6,4},{8,10},{10,8},{12,14},{14,12},{16,18},{18,... | collective-permute-start | bytes 1818632 | tf_op jit(solution)/shard_map/ppermute | solution.py:868
  51.0 2.7 %collective-permute-start.15 = (bf16[592,512]{1,0:T(8,128)(2,1)S(1)}, bf16[592,512]{1,0:T(8,128)(2,1)S(1)}, u32[]{:S(2)}, u32[]{:S(2)}) collective-permute-start(bf16[592,512]{1,0:T(8,128)(2,1)S(1)} %collective-permute-done.6.rest_4_), channel_id=1, source_target_pairs={{0,2},{2,0},{4,6},{6,4},{8,10},{10,8},{12,14},{14,12},{16,18},{18,... | collective-permute-start | bytes 1818632 | tf_op jit(solution)/shard_map/ppermute | solution.py:868
  51.0 2.8 %copy-start.8 = (bf16[592,512]{1,0:T(8,128)(2,1)}, bf16[592,512]{1,0:T(8,128)(2,1)S(1)}, u32[]{:S(2)}) copy-start(bf16[592,512]{1,0:T(8,128)(2,1)S(1)} %collective-permute-done.12.rest_6_) | copy-start | bytes 1818628
  51.0 9.8 %collective-permute-start.10 = (bf16[304,512]{1,0:T(8,128)(2,1)S(1)}, bf16[304,512]{1,0:T(8,128)(2,1)S(1)}, u32[]{:S(2)}, u32[]{:S(2)}) collective-permute-start(bf16[304,512]{1,0:T(8,128)(2,1)S(1)} %slice.107), channel_id=1, source_target_pairs={{0,4},{2,6},{8,0},{10,2},{16,8},{18,10},{24,16},{26,18},{28,24},{3... | collective-permute-start | bytes 933896 | tf_op jit(solution)/shard_map/ppermute | solution.py:862
  51.6 2.2 %copy-start.9 = (bf16[592,512]{1,0:T(8,128)(2,1)}, bf16[592,512]{1,0:T(8,128)(2,1)S(1)}, u32[]{:S(2)}) copy-start(bf16[592,512]{1,0:T(8,128)(2,1)S(1)} %collective-permute-done.13.rest_7_) | copy-start | bytes 1818628
  51.6 9.2 %collective-permute-start.9 = (bf16[288,512]{1,0:T(8,128)(2,1)S(1)}, bf16[288,512]{1,0:T(8,128)(2,1)S(1)}, u32[]{:S(2)}, u32[]{:S(2)}) collective-permute-start(bf16[288,512]{1,0:T(8,128)(2,1)S(1)} %slice.106), channel_id=1, source_target_pairs={{0,8},{2,10},{8,16},{10,18},{16,24},{18,26},{24,28},{26,30},{28,20... | collective-permute-start | bytes 884744 | tf_op jit(solution)/shard_map/ppermute | solution.py:862
  53.2 0.8 copy-start.10
  53.2 9.7 %collective-permute-start.16 = (bf16[592,512]{1,0:T(8,128)(2,1)S(1)}, bf16[592,512]{1,0:T(8,128)(2,1)S(1)}, u32[]{:S(2)}, u32[]{:S(2)}) collective-permute-start(bf16[592,512]{1,0:T(8,128)(2,1)S(1)} %collective-permute-done.7.rest_0_.rest_10_), channel_id=1, source_target_pairs={{0,2},{2,0},{4,6},{6,4},{8,10},{10,8},{12,14},{14,12},{16,18},{18,... | collective-permute-start | bytes 1818632 | tf_op jit(solution)/shard_map/ppermute | solution.py:868
  53.2 1.0 copy-start.11
  53.3 9.7 %collective-permute-start.17 = (bf16[592,512]{1,0:T(8,128)(2,1)S(1)}, bf16[592,512]{1,0:T(8,128)(2,1)S(1)}, u32[]{:S(2)}, u32[]{:S(2)}) collective-permute-start(bf16[592,512]{1,0:T(8,128)(2,1)S(1)} %collective-permute-done.8.rest_1_.rest_11_), channel_id=1, source_target_pairs={{0,2},{2,0},{4,6},{6,4},{8,10},{10,8},{12,14},{14,12},{16,18},{18,... | collective-permute-start | bytes 1818632 | tf_op jit(solution)/shard_map/ppermute | solution.py:868
  54.3 0.9 copy-start.12
  60.9 8.8 %copy-start.1 = (bf16[512,768]{1,0:T(8,128)(2,1)S(1)}, bf16[512,768]{1,0:T(8,128)(2,1)}, u32[]{:S(2)}) copy-start(bf16[512,768]{1,0:T(8,128)(2,1)} %cot_ref.5) | copy-start | bytes 2359300
  60.9 2.0 %collective-permute-start.19 = (bf16[304,512]{1,0:T(8,128)(2,1)S(1)}, bf16[304,512]{1,0:T(8,128)(2,1)S(1)}, u32[]{:S(2)}, u32[]{:S(2)}) collective-permute-start(bf16[304,512]{1,0:T(8,128)(2,1)S(1)} %collective-permute-done.10.rest_3_.rest_13_), channel_id=1, source_target_pairs={{0,2},{2,0},{4,6},{6,4},{8,10},{10,8},{12,14},{14,12},{16,18},{18,... | collective-permute-start | bytes 933896 | tf_op jit(solution)/shard_map/ppermute | solution.py:868
  60.9 2.0 %collective-permute-start.18 = (bf16[288,512]{1,0:T(8,128)(2,1)S(1)}, bf16[288,512]{1,0:T(8,128)(2,1)S(1)}, u32[]{:S(2)}, u32[]{:S(2)}) collective-permute-start(bf16[288,512]{1,0:T(8,128)(2,1)S(1)} %collective-permute-done.9.rest_2_.rest_12_), channel_id=1, source_target_pairs={{0,2},{2,0},{4,6},{6,4},{8,10},{10,8},{12,14},{14,12},{16,18},{18,... | collective-permute-start | bytes 884744 | tf_op jit(solution)/shard_map/ppermute | solution.py:868
  68.1 11.2 %collective-permute-start.20 = (bf16[512,384]{1,0:T(8,128)(2,1)S(1)}, bf16[512,384]{1,0:T(8,128)(2,1)S(1)}, u32[]{:S(2)}, u32[]{:S(2)}) collective-permute-start(bf16[512,384]{1,0:T(8,128)(2,1)S(1)} %get-tuple-element.130.own_ref.mixed_ref), channel_id=1, source_target_pairs={{0,1},{1,0},{2,3},{3,2},{4,5},{5,4},{6,7},{7,6},{8,9},{9,8},{10,11... | collective-permute-start | bytes 1179656 | tf_op jit(solution)/shard_map/ppermute | solution.py:1032
  82.4 12.8 %collective-permute-start.21 = (bf16[256,768]{1,0:T(8,128)(2,1)S(1)}, bf16[256,768]{1,0:T(8,128)(2,1)S(1)}, u32[]{:S(2)}, u32[]{:S(2)}) collective-permute-start(bf16[256,768]{1,0:T(8,128)(2,1)S(1)} %get-tuple-element.146.rest_0_), channel_id=1, source_target_pairs={{0,1},{1,0},{2,3},{3,2},{4,5},{5,4},{6,7},{7,6},{8,9},{9,8},{10,11... | collective-permute-start | bytes 1179656 | tf_op jit(solution)/shard_map/ppermute | solution.py:1041
  93.1 1.6 %collective-permute-start.22 = (bf16[48,3072]{1,0:T(8,128)(2,1)S(1)}, bf16[48,3072]{1,0:T(8,128)(2,1)S(1)}, u32[]{:S(2)}, u32[]{:S(2)}) collective-permute-start(bf16[48,3072]{1,0:T(8,128)(2,1)S(1)} %get-tuple-element.147), channel_id=1, source_target_pairs={{0,2},{2,0},{4,6},{6,4},{8,10},{10,8},{12,14},{14,12},{16,18},{18,... | collective-permute-start | bytes 884744 | tf_op jit(solution)/shard_map/ppermute | solution.py:888
  93.1 2.0 %collective-permute-start.23 = (bf16[48,3072]{1,0:T(8,128)(2,1)S(1)}, bf16[48,3072]{1,0:T(8,128)(2,1)S(1)}, u32[]{:S(2)}, u32[]{:S(2)}) collective-permute-start(bf16[48,3072]{1,0:T(8,128)(2,1)S(1)} %get-tuple-element.148), channel_id=1, source_target_pairs={{0,2},{2,0},{4,6},{6,4},{8,10},{10,8},{12,14},{14,12},{16,18},{18,... | collective-permute-start | bytes 884744 | tf_op jit(solution)/shard_map/ppermute | solution.py:888
  95.1 9.8 %collective-permute-start.24 = (bf16[6,48,3072]{2,1,0:T(8,128)(2,1)S(1)}, bf16[6,48,3072]{2,1,0:T(8,128)(2,1)S(1)}, u32[]{:S(2)}, u32[]{:S(2)}) collective-permute-start(bf16[6,48,3072]{2,1,0:T(8,128)(2,1)S(1)} %get-tuple-element.149), channel_id=1, source_target_pairs={{0,2},{2,0},{4,6},{6,4},{8,10},{10,8},{12,14},{14,12},{16,18},{18,... | collective-permute-start | bytes 5308424 | tf_op jit(solution)/shard_map/ppermute | solution.py:907
  95.4 9.3 %collective-permute-start.25 = (bf16[48,3072]{1,0:T(8,128)(2,1)S(1)}, bf16[48,3072]{1,0:T(8,128)(2,1)S(1)}, u32[]{:S(2)}, u32[]{:S(2)}) collective-permute-start(bf16[48,3072]{1,0:T(8,128)(2,1)S(1)} %get-tuple-element.222), channel_id=1, source_target_pairs={{0,4},{2,6},{8,0},{10,2},{16,8},{18,10},{24,16},{26,18},{28,24},{3... | collective-permute-start | bytes 884744 | tf_op jit(solution)/shard_map/ppermute | solution.py:919
  95.9 9.0 %collective-permute-start.26 = (bf16[48,3072]{1,0:T(8,128)(2,1)S(1)}, bf16[48,3072]{1,0:T(8,128)(2,1)S(1)}, u32[]{:S(2)}, u32[]{:S(2)}) collective-permute-start(bf16[48,3072]{1,0:T(8,128)(2,1)S(1)} %get-tuple-element.221), channel_id=1, source_target_pairs={{0,8},{2,10},{8,16},{10,18},{16,24},{18,26},{24,28},{26,30},{28,20... | collective-permute-start | bytes 884744 | tf_op jit(solution)/shard_map/ppermute | solution.py:919
  97.5 10.8 %collective-permute-start.31 = (bf16[256,768]{1,0:T(8,128)(2,1)S(1)}, bf16[256,768]{1,0:T(8,128)(2,1)S(1)}, u32[]{:S(2)}, u32[]{:S(2)}) collective-permute-start(bf16[256,768]{1,0:T(8,128)(2,1)S(1)} %get-tuple-element.157.rest_1_), channel_id=1, source_target_pairs={{0,1},{1,0},{2,3},{3,2},{4,5},{5,4},{6,7},{7,6},{8,9},{9,8},{10,11... | collective-permute-start | bytes 1179656 | tf_op jit(solution)/shard_map/ppermute | solution.py:1041
  105.1 10.0 %collective-permute-start.27 = (bf16[48,3072]{1,0:T(8,128)(2,1)S(1)}, bf16[48,3072]{1,0:T(8,128)(2,1)S(1)}, u32[]{:S(2)}, u32[]{:S(2)}) collective-permute-start(bf16[48,3072]{1,0:T(8,128)(2,1)S(1)} %get-tuple-element.218), channel_id=1, source_target_pairs={{0,4},{2,6},{8,0},{10,2},{16,8},{18,10},{24,16},{26,18},{28,24},{3... | collective-permute-start | bytes 884744 | tf_op jit(solution)/shard_map/ppermute | solution.py:919
  106.0 9.2 %collective-permute-start.28 = (bf16[48,3072]{1,0:T(8,128)(2,1)S(1)}, bf16[48,3072]{1,0:T(8,128)(2,1)S(1)}, u32[]{:S(2)}, u32[]{:S(2)}) collective-permute-start(bf16[48,3072]{1,0:T(8,128)(2,1)S(1)} %get-tuple-element.217), channel_id=1, source_target_pairs={{0,8},{2,10},{8,16},{10,18},{16,24},{18,26},{24,28},{26,30},{28,20... | collective-permute-start | bytes 884744 | tf_op jit(solution)/shard_map/ppermute | solution.py:919
  111.2 12.9 %collective-permute-start.35 = (bf16[224,768]{1,0:T(8,128)(2,1)S(1)}, bf16[224,768]{1,0:T(8,128)(2,1)S(1)}, u32[]{:S(2)}, u32[]{:S(2)}) collective-permute-start(bf16[224,768]{1,0:T(8,128)(2,1)S(1)} %slice.118), channel_id=1, source_target_pairs={{0,1},{1,0},{2,3},{3,2},{4,5},{5,4},{6,7},{7,6},{8,9},{9,8},{10,11... | collective-permute-start | bytes 1032200 | tf_op jit(solution)/shard_map/ppermute | solution.py:1059
  113.6 7.3 %collective-permute-start.32 = (f32[64,128]{1,0:T(8,128)S(1)}, f32[64,128]{1,0:T(8,128)S(1)}, u32[]{:S(2)}, u32[]{:S(2)}) collective-permute-start(f32[64,128]{1,0:T(8,128)S(1)} %get-tuple-element.164.ga_ref), channel_id=1, source_target_pairs={{0,1},{1,0},{2,3},{3,2},{4,5},{5,4},{6,7},{7,6},{8,9},{9,8},{10,11... | collective-permute-start | bytes 98312 | tf_op jit(solution)/shard_map/ppermute | solution.py:1061
  115.4 8.7 %collective-permute-start.29 = (bf16[48,3072]{1,0:T(8,128)(2,1)S(1)}, bf16[48,3072]{1,0:T(8,128)(2,1)S(1)}, u32[]{:S(2)}, u32[]{:S(2)}) collective-permute-start(bf16[48,3072]{1,0:T(8,128)(2,1)S(1)} %get-tuple-element.216), channel_id=1, source_target_pairs={{0,4},{2,6},{8,0},{10,2},{16,8},{18,10},{24,16},{26,18},{28,24},{3... | collective-permute-start | bytes 884744 | tf_op jit(solution)/shard_map/ppermute | solution.py:919
  115.9 8.3 %collective-permute-start.30 = (bf16[48,3072]{1,0:T(8,128)(2,1)S(1)}, bf16[48,3072]{1,0:T(8,128)(2,1)S(1)}, u32[]{:S(2)}, u32[]{:S(2)}) collective-permute-start(bf16[48,3072]{1,0:T(8,128)(2,1)S(1)} %get-tuple-element.215), channel_id=1, source_target_pairs={{0,8},{2,10},{8,16},{10,18},{16,24},{18,26},{24,28},{26,30},{28,20... | collective-permute-start | bytes 884744 | tf_op jit(solution)/shard_map/ppermute | solution.py:919
  122.5 1.7 %collective-permute-start.33 = (bf16[272,512]{1,0:T(8,128)(2,1)S(1)}, bf16[272,512]{1,0:T(8,128)(2,1)S(1)}, u32[]{:S(2)}, u32[]{:S(2)}) collective-permute-start(bf16[272,512]{1,0:T(8,128)(2,1)S(1)} %get-tuple-element.171), channel_id=1, source_target_pairs={{0,2},{2,0},{4,6},{6,4},{8,10},{10,8},{12,14},{14,12},{16,18},{18,... | collective-permute-start | bytes 835592 | tf_op jit(solution)/shard_map/ppermute | solution.py:888
  122.6 1.6 collective-permute-start.34
  124.2 11.2 %collective-permute-start.36 = (bf16[7,288,512]{2,1,0:T(8,128)(2,1)S(1)}, bf16[7,288,512]{2,1,0:T(8,128)(2,1)S(1)}, u32[]{:S(2)}, u32[]{:S(2)}) collective-permute-start(bf16[7,288,512]{2,1,0:T(8,128)(2,1)S(1)} %get-tuple-element.179), channel_id=1, source_target_pairs={{0,2},{2,0},{4,6},{6,4},{8,10},{10,8},{12,14},{14,12},{16,18},{18,... | collective-permute-start | bytes 6193160 | tf_op jit(solution)/shard_map/ppermute | solution.py:907
  124.7 9.3 %collective-permute-start.38 = (bf16[288,512]{1,0:T(8,128)(2,1)S(1)}, bf16[288,512]{1,0:T(8,128)(2,1)S(1)}, u32[]{:S(2)}, u32[]{:S(2)}) collective-permute-start(bf16[288,512]{1,0:T(8,128)(2,1)S(1)} %pieces_sum.1), channel_id=1, source_target_pairs={{0,8},{2,10},{8,16},{10,18},{16,24},{18,26},{24,28},{26,30},{28,20... | collective-permute-start | bytes 884744 | tf_op jit(solution)/shard_map/ppermute | solution.py:919
  126.4 9.0 %collective-permute-start.37 = (bf16[48,3072]{1,0:T(8,128)(2,1)S(1)}, bf16[48,3072]{1,0:T(8,128)(2,1)S(1)}, u32[]{:S(2)}, u32[]{:S(2)}) collective-permute-start(bf16[48,3072]{1,0:T(8,128)(2,1)S(1)} %fusion.23), channel_id=1, source_target_pairs={{0,4},{2,6},{8,0},{10,2},{16,8},{18,10},{24,16},{26,18},{28,24},{3... | collective-permute-start | bytes 884744 | tf_op jit(solution)/shard_map/ppermute | solution.py:919
  127.0 12.3 %collective-permute-start.41 = (bf16[288,768]{1,0:T(8,128)(2,1)S(1)}, bf16[288,768]{1,0:T(8,128)(2,1)S(1)}, u32[]{:S(2)}, u32[]{:S(2)}) collective-permute-start(bf16[288,768]{1,0:T(8,128)(2,1)S(1)} %slice.119), channel_id=1, source_target_pairs={{0,1},{1,0},{2,3},{3,2},{4,5},{5,4},{6,7},{7,6},{8,9},{9,8},{10,11... | collective-permute-start | bytes 1327112 | tf_op jit(solution)/shard_map/ppermute | solution.py:1076
  135.5 8.2 %collective-permute-start.40 = (bf16[288,512]{1,0:T(8,128)(2,1)S(1)}, bf16[288,512]{1,0:T(8,128)(2,1)S(1)}, u32[]{:S(2)}, u32[]{:S(2)}) collective-permute-start(bf16[288,512]{1,0:T(8,128)(2,1)S(1)} %fusion.29), channel_id=1, source_target_pairs={{0,4},{2,6},{8,0},{10,2},{16,8},{18,10},{24,16},{26,18},{28,24},{3... | collective-permute-start | bytes 884744 | tf_op jit(solution)/shard_map/ppermute | solution.py:919
  136.2 7.9 %collective-permute-start.39 = (bf16[288,512]{1,0:T(8,128)(2,1)S(1)}, bf16[288,512]{1,0:T(8,128)(2,1)S(1)}, u32[]{:S(2)}, u32[]{:S(2)}) collective-permute-start(bf16[288,512]{1,0:T(8,128)(2,1)S(1)} %fusion.24), channel_id=1, source_target_pairs={{0,8},{2,10},{8,16},{10,18},{16,24},{18,26},{24,28},{26,30},{28,20... | collective-permute-start | bytes 884744 | tf_op jit(solution)/shard_map/ppermute | solution.py:919
  137.8 10.6 %collective-permute-start.44 = (bf16[256,768]{1,0:T(8,128)(2,1)S(1)}, bf16[256,768]{1,0:T(8,128)(2,1)S(1)}, u32[]{:S(2)}, u32[]{:S(2)}) collective-permute-start(bf16[256,768]{1,0:T(8,128)(2,1)S(1)} %get-tuple-element.189), channel_id=1, source_target_pairs={{0,1},{1,0},{2,3},{3,2},{4,5},{5,4},{6,7},{7,6},{8,9},{9,8},{10,11... | collective-permute-start | bytes 1179656 | tf_op jit(solution)/shard_map/ppermute | solution.py:1082
  144.3 7.0 %collective-permute-start.42 = (bf16[288,512]{1,0:T(8,128)(2,1)S(1)}, bf16[288,512]{1,0:T(8,128)(2,1)S(1)}, u32[]{:S(2)}, u32[]{:S(2)}) collective-permute-start(bf16[288,512]{1,0:T(8,128)(2,1)S(1)} %get-tuple-element.214), channel_id=1, source_target_pairs={{0,8},{2,10},{8,16},{10,18},{16,24},{18,26},{24,28},{26,30},{28,20... | collective-permute-start | bytes 884744 | tf_op jit(solution)/shard_map/ppermute | solution.py:919
  145.9 6.7 %collective-permute-start.43 = (bf16[288,512]{1,0:T(8,128)(2,1)S(1)}, bf16[288,512]{1,0:T(8,128)(2,1)S(1)}, u32[]{:S(2)}, u32[]{:S(2)}) collective-permute-start(bf16[288,512]{1,0:T(8,128)(2,1)S(1)} %get-tuple-element.213), channel_id=1, source_target_pairs={{0,4},{2,6},{8,0},{10,2},{16,8},{18,10},{24,16},{26,18},{28,24},{3... | collective-permute-start | bytes 884744 | tf_op jit(solution)/shard_map/ppermute | solution.py:919
  146.4 9.5 %collective-permute-start.45 = (bf16[256,768]{1,0:T(8,128)(2,1)S(1)}, bf16[256,768]{1,0:T(8,128)(2,1)S(1)}, u32[]{:S(2)}, u32[]{:S(2)}) collective-permute-start(bf16[256,768]{1,0:T(8,128)(2,1)S(1)} %get-tuple-element.193), channel_id=1, source_target_pairs={{0,1},{1,0},{2,3},{3,2},{4,5},{5,4},{6,7},{7,6},{8,9},{9,8},{10,11... | collective-permute-start | bytes 1179656 | tf_op jit(solution)/shard_map/ppermute | solution.py:1085
  152.9 6.8 %collective-permute-start.46 = (bf16[288,512]{1,0:T(8,128)(2,1)S(1)}, bf16[288,512]{1,0:T(8,128)(2,1)S(1)}, u32[]{:S(2)}, u32[]{:S(2)}) collective-permute-start(bf16[288,512]{1,0:T(8,128)(2,1)S(1)} %get-tuple-element.212), channel_id=1, source_target_pairs={{0,8},{2,10},{8,16},{10,18},{16,24},{18,26},{24,28},{26,30},{28,20... | collective-permute-start | bytes 884744 | tf_op jit(solution)/shard_map/ppermute | solution.py:919
  154.4 6.7 %collective-permute-start.47 = (bf16[288,512]{1,0:T(8,128)(2,1)S(1)}, bf16[288,512]{1,0:T(8,128)(2,1)S(1)}, u32[]{:S(2)}, u32[]{:S(2)}) collective-permute-start(bf16[288,512]{1,0:T(8,128)(2,1)S(1)} %get-tuple-element.211), channel_id=1, source_target_pairs={{0,4},{2,6},{8,0},{10,2},{16,8},{18,10},{24,16},{26,18},{28,24},{3... | collective-permute-start | bytes 884744 | tf_op jit(solution)/shard_map/ppermute | solution.py:919

commit v5 on v4

--- a/solution.py
+++ b/solution.py
@@ -206,34 +206,24 @@
     return copies
 
 
-def mixer_rows(plan, units, shares, where_ref, seg_ref, e_ref, unit, same, sem):
+def document_mask(seg_ref, same):
+    length = same.shape[0]
+    documents = (seg_ref[...] == lax.broadcasted_iota(jnp.int32, (LANES, length), 0)).astype(BF)
+    same[...] = mm(documents, documents, TN)
+
+
+def exponentials(where_ref, shares, sources, e_ref, same):
     heads, length, _ = e_ref.shape
     rows = length // UNITS
-    top = heads * rows
-    mine = [n for n, (_, first, _) in enumerate(shares) if first == 0]
-
-    def target(m, owner):
-        return unit.at[pl.ds(multiple(owner * top, top), top), :]
-
-    copies = pick([units[n] for n in mine], [shares[n] for n in mine], where_ref, [(0, 0, top, length)], target, sem)
-
-    def write():
-        documents = (seg_ref[...] == lax.broadcasted_iota(jnp.int32, (LANES, length), 0)).astype(BF)
-        same[...] = mm(documents, documents, TN)
-        for copy in copies:
-            copy.wait()
-
-        def one_head(h, carry):
-            for n in mine:
-                owner = where_ref[shares[n][0]]
-                at = pl.ds(multiple(owner * rows, rows), rows)
-                s = unit[pl.ds(multiple(owner * top + h * rows, rows), rows), :].astype(F32)
-                e_ref[h, at, :] = (jnp.exp(s) * same[at, :]).astype(BF)
-            return carry
-
-        lax.fori_loop(0, heads, one_head, 0)
-
-    return write
+
+    def one_head(h, carry):
+        for (u, _, _), (ref, first) in zip(shares, sources):
+            at = pl.ds(multiple(where_ref[u] * rows, rows), rows)
+            s = ref[pl.ds(multiple(first + h * rows, rows), rows), :].astype(F32)
+            e_ref[h, at, :] = (jnp.exp(s) * same[at, :]).astype(BF)
+        return carry
+
+    lax.fori_loop(0, heads, one_head, 0)
 
 
 def low_parts(plan):
@@ -260,11 +250,20 @@
 
     def kernel(where_ref, tok_ref, seg_ref, *rest):
         e_ref, wv_ref, low_ref, hat_ref, unit, same, sem, more = rest[len(units) :]
-        write = mixer_rows(plan, rest[: len(units)], shares, where_ref, seg_ref, e_ref, unit, same, sem)
+        top = heads * rows
+
+        def target(m, owner):
+            return unit.at[pl.ds(multiple(owner * top, top), top), :]
+
+        came = pick(rest[: len(units)], shares, where_ref, [(0, 0, top, length)], target, sem)
         copies = bring_low(plan, rest[: len(units)], shares, where_ref, wv_ref, low_ref, more)
+        document_mask(seg_ref, same)
         x = tok_ref[...].astype(F32)
         hat_ref[...] = x * lax.rsqrt(jnp.mean(x * x, axis=-1, keepdims=True) + EPSILON)
-        write()
+        for copy in came:
+            copy.wait()
+        sources = [(unit, where_ref[u] * top) for u, _, _ in shares]
+        exponentials(where_ref, shares, sources, e_ref, same)
         for copy in copies:
             copy.wait()
 
@@ -297,11 +296,18 @@
     count = len(units)
 
     def kernel(where_ref, seg_ref, e_old, wv_old, low_old, hat_ref, *rest):
-        e_ref, wv_ref, low, va_ref, mixed_ref, sums_ref, n1_ref, gains_ref, pieces, unit, same, sem, more = rest[count:]
-        copies = bring_low(plan, rest[:count], shares, where_ref, wv_ref, low, sem)
-        write = mixer_rows(plan, rest[:count], shares, where_ref, seg_ref, e_ref, unit, same, more)
-        for copy in copies:
-            copy.wait()
+        e_ref, wv_ref, low, va_ref, sums_ref, n1_ref, gains_ref, *mixed, pieces, same = rest[count:]
+        for (u, first, rows), ref in zip(shares, rest[:count]):
+            for m, (row, lane, deep, lanes) in enumerate(low_parts(plan)):
+                if first <= row < first + rows:
+                    part = ref[row - first : row - first + deep, lane : lane + lanes]
+                    if m == 0:
+                        wv_ref[pl.ds(multiple(where_ref[u] * krows, 16), krows), :] = part
+                    else:
+                        low[where_ref[u]] = part
+        document_mask(seg_ref, same)
+        scored = [n for n in range(count) if shares[n][1] == 0]
+        exponentials(where_ref, [shares[n] for n in scored], [(rest[n], 0) for n in scored], e_ref, same)
         for d in range(UNITS):
             some = low[d].astype(F32)
             pieces[0, d : d + 1, :] = some[0:1, :]
@@ -326,49 +332,46 @@
             va_ref[:, h * LANES : h * LANES + size] = values[:, h * size : (h + 1) * size]
             va_ref[:, h * LANES + size : (h + 1) * LANES] = tail
 
-        write()
         for h in range(heads):
             lanes = slice(h * LANES, (h + 1) * LANES)
             sums = mm(e_ref[h], va_ref[:, lanes])
             sums_ref[:, lanes] = sums
-            mixed_ref[:, h * size : (h + 1) * size] = (sums * (1.0 / sums[:, size : size + 1]))[:, :size].astype(BF)
+            values = (sums * (1.0 / sums[:, size : size + 1]))[:, :size].astype(BF)
+            for part, mixed_ref in enumerate(mixed):
+                some = slice(part * (length // PARTS), (part + 1) * (length // PARTS))
+                mixed_ref[:, h * size : (h + 1) * size] = values[some, :]
 
     return run(
         kernel,
         "mixer_forward",
         (where,),
-        (segments, *early),
+        (segments, *early, *units),
         (
             ((heads, length, length), BF),
             ((model, width), BF),
             ((UNITS, plan.fold, LANES), BF),
             ((length, wide), BF),
-            ((length, width), BF),
             ((length, wide), F32),
             ((length, model), BF),
             ((2, model), F32),
+            *[((length // PARTS, width), BF)] * PARTS,
         ),
         (
             pltpu.VMEM((2, UNITS, LANES), F32),
-            pltpu.VMEM((heads * length, length), BF),
             pltpu.VMEM((length, length), F32),
-            pltpu.SemaphoreType.DMA((UNITS, 2)),
-            pltpu.SemaphoreType.DMA((UNITS, 1)),
         ),
-        loose=units,
         aliases={2: 0, 3: 1, 4: 2},
-        near=len(units),
-    )
-
-
-def second_weights(plan, where, cotangent, sums, units, shares, near, size):
+    )
+
+
+def second_weights(plan, where, second, cotangent, sums, units, shares, near, size):
     length, model = cotangent.shape
-    hidden, krows = plan.hidden, plan.krows
+    hidden, krows, width = plan.hidden, plan.krows, plan.width
     piece = hidden // 3
     parts = plan.ffn_parts()
 
-    def kernel(where_ref, cot_ref, sums_ref, *rest):
-        out, gact, mixf_ref, rb_ref, sem = rest[len(units) :]
+    def kernel(where_ref, second_ref, cot_ref, sums_ref, *rest):
+        out, gact, mixf_ref, rb_ref, own_ref, sem = rest[len(units) :]
 
         def target(m, owner):
             _, _, row, column, rows, columns = parts[m]
@@ -386,13 +389,23 @@
         for j in range(3):
             cols = slice(j * piece, (j + 1) * piece)
             gact[:, cols] = mm(cot_ref[...], out[:, hidden + j * piece : hidden + (j + 1) * piece])
+        own = out[:, pl.ds(multiple(2 * hidden + second_ref[0] * width, LANES), width)]
+        own_ref[...] = jnp.zeros_like(own_ref)
+        for h in range(width // size):
+            own_ref[:, h * LANES : h * LANES + size] = own[:, h * size : (h + 1) * size]
 
     return run(
         kernel,
         "second_weights",
-        (where,),
+        (where, second),
         (cotangent, sums),
-        (((model, 2 * hidden + model), BF), ((length, hidden), F32), (sums.shape, F32), (sums.shape, F32)),
+        (
+            ((model, 2 * hidden + model), BF),
+            ((length, hidden), F32),
+            (sums.shape, F32),
+            (sums.shape, F32),
+            ((model, sums.shape[1]), BF),
+        ),
         (pltpu.SemaphoreType.DMA((UNITS, len(parts))),),
         loose=units,
         near=near,
@@ -412,8 +425,8 @@
         backs = rest[:pieces]
         resid_ref, n2_ref, act_ref, gpre_ref, mixed, acc = rest[pieces:]
         first = second_ref[0]
-        mixed[:, pl.ds(multiple(first * width, LANES), width)] = own_ref[at, :]
-        mixed[:, pl.ds(multiple((1 - first) * width, LANES), width)] = other_ref[at, :]
+        mixed[:, pl.ds(multiple(first * width, LANES), width)] = own_ref[...]
+        mixed[:, pl.ds(multiple((1 - first) * width, LANES), width)] = other_ref[...]
         attn = mm(mixed[...], w_ref[:, 2 * hidden :], NT)
         resid = tok_ref[at, :].astype(F32) + attn
         resid_ref[...] = resid
@@ -476,29 +489,14 @@
 
 def slot_shapes(rows, columns, first, pieces, apart):
     half = UNITS // 2
-    cuts = [(rows, columns)] if pieces == 1 else [(rows - SMALL, columns), (SMALL, columns)]
-    early = [(cut, BF) for _ in first for cut in cuts]
+    early = [((rows, columns), BF)] * (len(first) * pieces)
     count = half - len(first)
     later = [((rows, columns), BF)] * count if apart else [((count, rows, columns), BF)]
     return [((half, rows, columns), BF), *early, *later]
 
 
-SMALL = 16
 FFN_FIRST = [UNITS // 4, UNITS // 4 - 1]
 MIXER_FIRST = [UNITS // 4]
-
-
-def pieces_sum(k, keep, pieces):
-    _, rows, columns = keep.shape
-
-    def kernel(keep_ref, *refs):
-        begin = 0
-        for one in refs[:-1]:
-            at = slice(begin, begin + one.shape[0])
-            begin = at.stop
-            refs[-1][at, :] = (keep_ref[k, at, :].astype(F32) + one[...].astype(F32)).astype(BF)
-
-    return run(kernel, "pieces_sum", (), (keep, *pieces), [((rows, columns), BF)])[0]
 
 
 def result_kernel(name, keep, own, up, down, shapes, cut):
@@ -540,32 +538,60 @@
 
 def mixer_result(keep, own, up, down, heads, krows, width):
     _, deep, length = keep.shape
-    top = deep - 2 * krows
+    top = deep - low_rows(krows)
     rows = top // heads
+    lead, half, fold = length - width, length // 2, krows // 3
     shapes = [(heads, rows, length), (krows, width), (krows, width), (1, krows), (1, krows)]
 
     def cut(n, to, total):
+        low = top + krows
         if n == 0:
             for h in range(heads):
                 to[h] = total(slice(h * rows, (h + 1) * rows), slice(None))
-        elif n < 3:
-            to[...] = total(slice(top + (n - 1) * krows, top + n * krows), slice(0, width))
+        elif n == 1:
+            to[...] = total(slice(top, low), slice(0, width))
+        elif n == 2:
+            to[:, :lead] = total(slice(top, low), slice(width, length))
+            for m in range(3):
+                some = slice(low + m // 2 * fold, low + (m // 2 + 1) * fold)
+                to[m * fold : (m + 1) * fold, lead:] = total(some, slice(m % 2 * half, (m % 2 + 1) * half))
         else:
-            to[...] = total(slice(top, top + 16), slice(width, length))[n - 3 : n - 2, :krows]
+            to[...] = total(slice(low + fold, low + 2 * fold), slice(half, half + LANES))[n - 3 : n - 2, :krows]
 
     return result_kernel("mixer_result", keep, own, up, down, shapes, cut)
 
 
-def ffn_grads(where, n2s, gpres, acts, cotangent, w):
+def ffn_out(acts, w, cut):
+    chunk, hidden = acts[0].shape
+    model = w.shape[0]
+    length = chunk * len(acts)
+
+    def kernel(*refs):
+        w_ref, out = refs[-4:-3][0], refs[-1]
+        for r, act in enumerate(refs[:-4]):
+            out[r * chunk : (r + 1) * chunk, :] = mm(act[...], w_ref[:, hidden : 2 * hidden], NT).astype(BF)
+        refs[-3][...] = out[:cut, :]
+        refs[-2][...] = out[cut:, :]
+
+    return run(
+        kernel,
+        "ffn_out",
+        (),
+        (*acts, w),
+        (((cut, model), BF), ((length - cut, model), BF)),
+        (pltpu.VMEM((length, model), BF),),
+    )
+
+
+def ffn_grads(where, n2s, gpres, acts, cotangent):
     parts = len(n2s)
     chunk, model = n2s[0].shape
     hidden = acts[0].shape[1]
     krows = model // UNITS
 
-    def kernel(where_ref, cot_ref, w_ref, *rest):
+    def kernel(where_ref, cot_ref, *rest):
         n2, gpre, act = rest[:parts], rest[parts : 2 * parts], rest[2 * parts : 3 * parts]
-        out_ref = rest[3 * parts]
-        slot = slots(rest[3 * parts + 1 : -2], FFN_FIRST, 1)
+        slot = slots(rest[3 * parts : -2], FFN_FIRST, 1)
         scr, sem = rest[-2:]
         piece = hidden // 3
         for j in range(3):
@@ -581,8 +607,6 @@
             (to,) = slot(u)
             copies.append(pltpu.make_async_copy(scr.at[at, :], to, sem.at[u]))
             copies[-1].start()
-        for r in range(parts):
-            out_ref[r * chunk : (r + 1) * chunk, :] = mm(act[r][...], w_ref[:, hidden : 2 * hidden], NT).astype(BF)
         for copy in copies:
             copy.wait()
 
@@ -590,8 +614,8 @@
         kernel,
         "ffn_grads",
         (where,),
-        (cotangent, w, *n2s, *gpres, *acts),
-        (((chunk * parts, model), BF),),
+        (cotangent, *n2s, *gpres, *acts),
+        (),
         (pltpu.VMEM((model, 2 * hidden), BF), pltpu.SemaphoreType.DMA((UNITS,))),
         loose_outs=slot_shapes(krows, 2 * hidden, FFN_FIRST, 1, False),
     )
@@ -612,16 +636,15 @@
     return pieces + mm(jnp.where(own, row - high, 0.0).astype(BF), take)
 
 
-def resid_back(second, backs, others, resids, cotangent, gains, w, mixf, heads, size):
+def resid_back(backs, others, resids, cotangent, gains, wo, mixf, heads, size):
     length, model = cotangent.shape
     wide = heads * LANES
     count = len(backs)
     krows = model // UNITS
     parts = len(resids)
 
-    hidden = w.shape[1] - 2 * heads * size
-
-    def kernel(second_ref, cot_ref, gains_ref, w_ref, mixf_ref, *rest):
+
+    def kernel(cot_ref, gains_ref, wo_ref, mixf_ref, *rest):
         mine, other, res_refs = rest[:count], rest[count : 2 * count], rest[2 * count : 2 * count + parts]
         gres_ref, gat_ref, xh_ref, gf_ref, gm = rest[2 * count + parts :]
         total = jnp.zeros((8, model), F32)
@@ -641,11 +664,7 @@
             gres = cot_ref[at, :].astype(F32) + inv * (z - hat * corr)
             gres_ref[at, :] = gres
             gat_ref[at, :] = gres.astype(BF)
-        own = pl.ds(multiple(hidden + second_ref[0] * heads * size, LANES), heads * size)
-        compact = mm(gat_ref[...], w_ref[:, own]).astype(BF)
-        gm[...] = jnp.zeros_like(gm)
-        for h in range(heads):
-            gm[:, h * LANES : h * LANES + size] = compact[:, h * size : (h + 1) * size]
+        gm[...] = mm(gat_ref[...], wo_ref[...]).astype(BF)
         lane = lax.broadcasted_iota(jnp.int32, (length, LANES), 1)
         for h in range(heads):
             lanes = slice(h * LANES, (h + 1) * LANES)
@@ -660,8 +679,8 @@
     return run(
         kernel,
         "resid_back",
-        (second,),
-        (cotangent, gains, w, mixf, *backs, *others, *resids),
+        (),
+        (cotangent, gains, wo, mixf, *backs, *others, *resids),
         (
             ((length, model), F32),
             ((length, model), BF),
@@ -728,72 +747,83 @@
     )
 
 
+def low_rows(krows):
+    return krows + 2 * (krows // 3)
+
+
 def mixer_grads(where, xh, va, e, rb, krows):
     heads, length, _ = e.shape
     rows = length // UNITS
-    deep = heads * rows + 2 * krows
+    deep = heads * rows + low_rows(krows)
 
     def kernel(where_ref, xh_ref, va_ref, e_ref, rb_ref, *rest):
         outs, ds = rest[:-1], rest[-1]
-        score_grads(where_ref, xh_ref, va_ref, e_ref, rb_ref, ds, slots(outs, MIXER_FIRST, 2), 0, heads, rows)
+        score_grads(where_ref, xh_ref, va_ref, e_ref, rb_ref, ds, slots(outs, MIXER_FIRST, 1), 0, heads, rows)
         for u in range(UNITS):
-            for n, to in enumerate(slots(outs, MIXER_FIRST, 2)(u)):
-                begin = 0 if n else heads * rows
-                to[begin:, :] = jnp.zeros((to.shape[0] - begin, length), BF)
+            for to in slots(outs, MIXER_FIRST, 1)(u):
+                to[heads * rows :, :] = jnp.zeros((low_rows(krows), length), BF)
 
     return run(
         kernel,
         "mixer_grads",
         (where,),
         (xh, va, e, rb),
-        slot_shapes(deep, length, MIXER_FIRST, 2, False),
+        slot_shapes(deep, length, MIXER_FIRST, 1, False),
         (pltpu.VMEM((length, length), BF),),
     )
 
 
 def weight_grads(where, parts, n1, gv, gat, mixed, ga, ga_other, gf):
+    length = n1.shape[0]
+    chunk = mixed[0].shape[0]
     model = n1.shape[1]
     width = gv.shape[1]
     krows = model // UNITS
     deep, length = parts[0].shape[1:]
-    top = deep - 2 * krows
-
-    def kernel(where_ref, n1_ref, gv_ref, gat_ref, mixed_ref, ga_ref, gb_ref, gf_ref, *rest):
-        slot = slots(rest[len(parts) : 2 * len(parts)], MIXER_FIRST, 2)
-        wide_v, wide_o, pieces = rest[2 * len(parts) :]
-        wide_v[:, :width] = mm(n1_ref[...], gv_ref[...], TN).astype(BF)
-        wide_o[:, :width] = mm(gat_ref[...], mixed_ref[...], TN).astype(BF)
-        wide_o[:, width:] = jnp.zeros((model, length - width), BF)
+    top = deep - low_rows(krows)
+    lead, half, fold = length - width, length // 2, krows // 3
+    assert width - lead == half
+
+    def kernel(where_ref, n1_ref, gv_ref, gat_ref, ga_ref, gb_ref, gf_ref, *rest):
+        mixed_refs, rest = rest[: len(mixed)], rest[len(mixed) :]
+        slot = slots(rest[len(parts) : 2 * len(parts)], MIXER_FIRST, 1)
+        wide, other, folded, pieces = rest[2 * len(parts) :]
+        wide[:, :width] = mm(n1_ref[...], gv_ref[...], TN).astype(BF)
+        some = [mm(gat_ref[n * chunk : (n + 1) * chunk, :], one[...], TN) for n, one in enumerate(mixed_refs)]
+        other[...] = sum(some).astype(BF)
+        wide[:, width:] = other[:, :lead]
         pieces[0] = ga_ref[:UNITS, :] + gb_ref[:UNITS, :]
         pieces[1] = gf_ref[...]
-        sub = lax.broadcasted_iota(jnp.int32, (krows, LANES), 0)
+        sub = lax.broadcasted_iota(jnp.int32, (fold, LANES), 0)
         for d in range(UNITS):
+            for n in range(3):
+                at = slice(d * krows + n * fold, d * krows + (n + 1) * fold)
+                to = slice((2 * d + n // 2) * fold, (2 * d + n // 2 + 1) * fold)
+                folded[to, (n % 2) * half : (n % 2 + 1) * half] = other[at, lead:]
             both = jnp.where(
                 sub == 0, pieces[0, d : d + 1, :], jnp.where(sub == 1, pieces[1, d : d + 1, :], 0.0)
             )
-            wide_v[d * krows : (d + 1) * krows, width:] = both.astype(BF)
+            at = slice((2 * d + 1) * fold, (2 * d + 2) * fold)
+            folded[at, half : half + LANES] = both.astype(BF)
+            folded[at, half + LANES :] = jnp.zeros((fold, half - LANES), BF)
         for u in range(UNITS):
-            at = pl.ds(multiple(where_ref[u] * krows, 16), krows)
-            to, *small = slot(u)
-            to[top : top + krows, :] = wide_v[at, :]
-            if small:
-                to[top + krows :, :] = wide_o[pl.ds(multiple(where_ref[u] * krows, 16), krows - SMALL), :]
-                small[0][...] = wide_o[pl.ds(multiple(where_ref[u] * krows + krows - SMALL, 16), SMALL), :]
-            else:
-                to[top + krows :, :] = wide_o[at, :]
+            (to,) = slot(u)
+            to[top : top + krows, :] = wide[pl.ds(multiple(where_ref[u] * krows, 16), krows), :]
+            to[top + krows :, :] = folded[pl.ds(multiple(where_ref[u] * 2 * fold, 16), 2 * fold), :]
 
     return run(
         kernel,
         "weight_grads",
         (where,),
-        (n1, gv, gat, mixed, ga, ga_other, gf, *parts),
-        slot_shapes(deep, length, MIXER_FIRST, 2, False),
+        (n1, gv, gat, ga, ga_other, gf, *mixed, *parts),
+        slot_shapes(deep, length, MIXER_FIRST, 1, False),
         (
             pltpu.VMEM((model, length), BF),
-            pltpu.VMEM((model, length), BF),
+            pltpu.VMEM((model, width), BF),
+            pltpu.VMEM((UNITS * 2 * fold, length), BF),
             pltpu.VMEM((2, UNITS, LANES), F32),
         ),
-        aliases={8 + n: n for n in range(len(parts))},
+        aliases={7 + len(mixed) + n: n for n in range(len(parts))},
     )
 
 
@@ -908,11 +938,8 @@
         self.got = {k: stack[n] for n, k in enumerate(self.late)}
 
     def hop(self, way, k):
-        if k in self.early and len(self.early[k]) > 1:
-            value = pieces_sum(k, self.keep, self.early[k]).astype(F32)
-        else:
-            got = self.early[k][0] if k in self.early else self.got[k]
-            value = self.keep[k].astype(F32) + got.astype(F32)
+        got = self.early[k][0] if k in self.early else self.got[k]
+        value = self.keep[k].astype(F32) + got.astype(F32)
         if way in self.last:
             value = value + self.last[way].astype(F32)
         value = value.astype(BF)
@@ -1026,15 +1053,15 @@
         early, late, near = list(range(UNITS // 2)), list(range(UNITS // 2, UNITS)), []
         begun = mixer_first(plan, where_in, tokens, segment_ids, units[: UNITS // 2], shares[: UNITS // 2], heads)
 
-    e, wv, _, va, mixed, sums, n1, gains = mixer_forward(
+    e, wv, _, va, sums, n1, gains, *mixed = mixer_forward(
         plan, where_in, segment_ids, begun, [units[n] for n in late], [shares[n] for n in late], heads, width
     )
-    mixed_other = lax.ppermute(mixed, "mp", flip)
-    w, gact, mixf, rb = second_weights(plan, where_in, cotangent, sums, units, shares, len(near), size)
+    mixed_other = [lax.ppermute(one, "mp", flip) for one in mixed]
+    w, gact, mixf, rb, wo = second_weights(plan, where_in, second_at, cotangent, sums, units, shares, len(near), size)
     backs, others, resids, n2s, acts, gpres = [], [], [], [], [], []
     for part in range(PARTS):
         *new, resid, n2, act, gpre = ffn_main(
-            second_at, tokens, mixed, mixed_other, gact, gains, w, part, PARTS, 1
+            second_at, tokens, mixed[part], mixed_other[part], gact, gains, w, part, PARTS, 1
         )
         for back in new:
             backs.append(back)
@@ -1043,19 +1070,18 @@
         n2s.append(n2)
         acts.append(act)
         gpres.append(gpre)
-    ffn, *parts_two = ffn_grads(where_out, n2s, gpres, acts, cotangent, w)
+    parts_two = ffn_grads(where_out, n2s, gpres, acts, cotangent)
+    ffn_one, ffn_two = ffn_out(acts, w, 7 * length // 16)
     if ring:
         ffn_sum = Scatter(net, FFN_FIRST, 1, *parts_two)
         ffn_sum.swap_all(others[0], *ffn_sum.values())
         for step in range(2):
             ffn_sum.hop("down", far + step)
             ffn_sum.hop("up", far - 1 - step)
-            together([ffn_sum])
+            ffn_one, ffn_two = together([ffn_sum], ffn_one, ffn_two)
     gres, gat, xh, gf = resid_back(
-        second_at, backs, others, resids, cotangent, gains, w, mixf, heads, size
-    )
-    ffn_cut = 7 * length // 16
-    ffn_one, ffn_two = ffn[:ffn_cut], ffn[ffn_cut:]
+        backs, others, resids, cotangent, gains, wo, mixf, heads, size
+    )
     one_other = lax.ppermute(tie(ffn_one, xh), "mp", flip)
     gv, part_one, part_two, ga = value_back(xh, rb, e, wv, tokens, size, length // 2)
     ga_other = lax.ppermute(ga, "mp", flip)
@@ -1068,7 +1094,7 @@
 
     top = heads * rows
     if ring:
-        score_sum = Scatter(net, MIXER_FIRST, 2, *parts_one)
+        score_sum = Scatter(net, MIXER_FIRST, 1, *parts_one)
         one_other, ffn_two = together([ffn_sum, score_sum], one_other, ffn_two)
         value = score_sum.hop("up", far)
         ffn_sum.hop("down", 2 * far - 1)
@@ -1108,15 +1134,19 @@
             return jnp.concatenate([keep, jnp.stack(given)]).astype(F32)
 
         two = whole(FFN_FIRST, 1, *parts_two).reshape(model, -1)
-        one = whole(MIXER_FIRST, 2, *parts_one)
+        one = whole(MIXER_FIRST, 1, *parts_one)
         out_up = scatter(two[:, : two.shape[1] // 2])
         out_down = scatter(two[:, two.shape[1] // 2 :]).T
         scores = one[:, :top].reshape(UNITS, heads, rows, length).transpose(1, 0, 2, 3)
         out_scores = scatter(scores.reshape(heads, length, length), 1)
         out_value = scatter(one[:, top : top + krows, :width].reshape(model, width))
-        out_output = scatter(one[:, top + krows :, :width].reshape(model, width)).T
-        out_gain_one = scatter(one[:, top, width : width + krows].reshape(model))
-        out_gain_two = scatter(one[:, top + 1, width : width + krows].reshape(model))
+        low, fold, half = top + krows, krows // 3, length // 2
+        folded = [one[:, low + n // 2 * fold : low + (n // 2 + 1) * fold, n % 2 * half :][:, :, :half] for n in range(3)]
+        other = jnp.concatenate([one[:, top:low, width:], jnp.concatenate(folded, axis=1)], axis=2)
+        out_output = scatter(other.reshape(model, width)).T
+        out_gain_one = scatter(one[:, low + fold, half : half + krows].reshape(model))
+        out_gain_two = scatter(one[:, low + fold + 1, half : half + krows].reshape(model))
+    ffn = jnp.concatenate([ffn_one, ffn_two])
     ffn_other = jnp.concatenate([one_other, two_other])
     output = (jnp.concatenate(resids) + (ffn.astype(F32) + ffn_other.astype(F32))).astype(BF)
     backs = []

time: 162 us -> 155 us (0.957)
  waiting for transfers between devices: 76.1 us -> 70.2 us
  Pallas kernels: 39.1 us -> 36.4 us
    ppermute x14, waiting for transfers between devices: 26.9 us -> 22.7 us  [hop(): lax.ppermute(value, 'dp', self.ring.up if way == 'up' else self.ring.down)]
    ppermute x1 -> x2, waiting for transfers between devices: 3.89 us -> 0.01 us  [shards(): mixed_other = [lax.ppermute(one, 'mp', flip) for one in mixed]]
    pallas_call x16, Pallas kernels: 39.1 us -> 36.4 us  [run(): pl.pallas_call(kernel, out_shape=tuple(results), in_specs=specs, out_spec...]
  transfers between devices with their start and end apart: 48 -> 48, of which waited for: 28 -> 26; matrix products, arithmetic and copies ran while one was open for 4% -> 4% of each run, Pallas kernels for 18% -> 20%
where the time goes in v5:
time: 155 us
  waiting for transfers between devices  70.2 us (45%)
  starting transfers between devices  39.8 us (26%)
  Pallas kernels  36.4 us (23%)
  other arithmetic  5.73 us (4%)
    pallas_call x16, Pallas kernels, run(): pl.pallas_call(kernel, out_shape=tuple(results), in_specs=specs, out_spec...  36.4 us
    ppermute x4, waiting for transfers between devices, hop(): lax.ppermute(up, 'dp', ring.up)  24.4 us
    ppermute x14, waiting for transfers between devices, hop(): lax.ppermute(value, 'dp', self.ring.up if way == 'up' else self.ring.down)  22.7 us
    ppermute x14, starting transfers between devices, hop(): lax.ppermute(value, 'dp', self.ring.up if way == 'up' else self.ring.down)  14.7 us
    ppermute x2, waiting for transfers between devices, shards(): wo_next = [lax.ppermute(wo_other, 'dp', way) for way in (net.up, net.down)]  9.06 us
    ppermute x4, starting transfers between devices, hop(): lax.ppermute(up, 'dp', ring.up)  7.91 us
  transfers between devices with their start and end apart: 48, of which 26 were waited for; matrix products, arithmetic and copies ran while one was open for 4% of the time, Pallas kernels for 20%

profile of v5, /device:TPU:0, one launch (start us, length us, event | category | flops | bytes accessed | tf_op | source)
XLA Modules:
  0.0 154.7 jit_solution(13974722715578067734)
XLA Ops:
  0.6 1.4 pack_unit.1
  2.0 3.1 %collective-permute-start = (bf16[592,512]{1,0:T(8,128)(2,1)S(1)}, bf16[592,512]{1,0:T(8,128)(2,1)S(1)}, u32[]{:S(2)}, u32[]{:S(2)}) collective-permute-start(bf16[592,512]{1,0:T(8,128)(2,1)S(1)} %get-tuple-element.111.rest_0_), channel_id=1, source_target_pairs={{0,8},{2,10},{8,16},{10,18},{16,24},{18,26},{24,28},{26,30},{28,20... | collective-permute-start | bytes 1818632 | tf_op jit(solution)/shard_map/ppermute | solution.py:892
  5.1 0.7 broadcast_add_fusion.3
  6.0 2.0 %collective-permute-start.2 = (bf16[48,384]{1,0:T(8,128)(2,1)S(1)}, bf16[48,384]{1,0:T(8,128)(2,1)S(1)}, u32[]{:S(2)}, u32[]{:S(2)}) collective-permute-start(bf16[48,384]{1,0:T(8,128)(2,1)S(1)} %get-tuple-element.113), channel_id=1, source_target_pairs={{0,1},{1,0},{2,3},{3,2},{4,5},{5,4},{6,7},{7,6},{8,9},{9,8},{10,11... | collective-permute-start | bytes 110600 | tf_op jit(solution)/shard_map/ppermute | solution.py:1004
  8.0 2.0 %collective-permute-done.2.rest_1_ = bf16[48,384]{1,0:T(8,128)(2,1)S(1)} collective-permute-done((bf16[48,384]{1,0:T(8,128)(2,1)S(1)}, bf16[48,384]{1,0:T(8,128)(2,1)S(1)}, u32[]{:S(2)}, u32[]{:S(2)}) %collective-permute-start.2) | collective-permute-done | bytes 36896 | tf_op jit(solution)/shard_map/ppermute | solution.py:1004
  10.0 2.0 %collective-permute-start.3 = (bf16[48,384]{1,0:T(8,128)(2,1)S(1)}, bf16[48,384]{1,0:T(8,128)(2,1)S(1)}, u32[]{:S(2)}, u32[]{:S(2)}) collective-permute-start(bf16[48,384]{1,0:T(8,128)(2,1)S(1)} %collective-permute-done.2.rest_1_), channel_id=1, source_target_pairs={{0,8},{2,10},{8,16},{10,18},{16,24},{18,26},{24,28},{26,30},{28,20... | collective-permute-start | bytes 110600 | tf_op jit(solution)/shard_map/ppermute | solution.py:1005
  12.0 7.5 %collective-permute-done.3.rest_2_ = bf16[48,384]{1,0:T(8,128)(2,1)S(1)} collective-permute-done((bf16[48,384]{1,0:T(8,128)(2,1)S(1)}, bf16[48,384]{1,0:T(8,128)(2,1)S(1)}, u32[]{:S(2)}, u32[]{:S(2)}) %collective-permute-start.3) | collective-permute-done | bytes 36896 | tf_op jit(solution)/shard_map/ppermute | solution.py:1005
  19.5 1.5 collective-permute-done.4.rest_3_
  21.1 1.6 %collective-permute-start.5 = (bf16[592,512]{1,0:T(8,128)(2,1)S(1)}, bf16[592,512]{1,0:T(8,128)(2,1)S(1)}, u32[]{:S(2)}, u32[]{:S(2)}) collective-permute-start(bf16[592,512]{1,0:T(8,128)(2,1)S(1)} %get-tuple-element.118.rest_1_), channel_id=1, source_target_pairs={{0,8},{2,10},{8,16},{10,18},{16,24},{18,26},{24,28},{26,30},{28,20... | collective-permute-start | bytes 1818632 | tf_op jit(solution)/shard_map/ppermute | solution.py:892
  23.2 12.2 %collective-permute-done.5.rest_3_ = bf16[592,512]{1,0:T(8,128)(2,1)S(1)} collective-permute-done((bf16[592,512]{1,0:T(8,128)(2,1)S(1)}, bf16[592,512]{1,0:T(8,128)(2,1)S(1)}, u32[]{:S(2)}, u32[]{:S(2)}) %collective-permute-start.5) | collective-permute-done | bytes 606240 | tf_op jit(solution)/shard_map/ppermute | solution.py:892
  35.4 1.3 collective-permute-done.6.rest_4_
  36.7 1.6 %collective-permute-start.7 = (bf16[592,512]{1,0:T(8,128)(2,1)S(1)}, bf16[592,512]{1,0:T(8,128)(2,1)S(1)}, u32[]{:S(2)}, u32[]{:S(2)}) collective-permute-start(bf16[592,512]{1,0:T(8,128)(2,1)S(1)} %collective-permute-done.5.rest_3_), channel_id=1, source_target_pairs={{0,8},{2,10},{8,16},{10,18},{16,24},{18,26},{24,28},{26,30},{28,20... | collective-permute-start | bytes 1818632 | tf_op jit(solution)/shard_map/ppermute | solution.py:892
  39.3 10.4 %collective-permute-done.7.rest_0_.rest_10_ = bf16[592,512]{1,0:T(8,128)(2,1)S(1)} collective-permute-done((bf16[592,512]{1,0:T(8,128)(2,1)S(1)}, bf16[592,512]{1,0:T(8,128)(2,1)S(1)}, u32[]{:S(2)}, u32[]{:S(2)}) %collective-permute-start.7) | collective-permute-done | bytes 606240 | tf_op jit(solution)/shard_map/ppermute | solution.py:892
  49.7 1.3 collective-permute-done.8.rest_1_.rest_11_
  51.6 1.6 %collective-permute-start.9 = (bf16[288,512]{1,0:T(8,128)(2,1)S(1)}, bf16[288,512]{1,0:T(8,128)(2,1)S(1)}, u32[]{:S(2)}, u32[]{:S(2)}) collective-permute-start(bf16[288,512]{1,0:T(8,128)(2,1)S(1)} %slice.103), channel_id=1, source_target_pairs={{0,8},{2,10},{8,16},{10,18},{16,24},{18,26},{24,28},{26,30},{28,20... | collective-permute-start | bytes 884744 | tf_op jit(solution)/shard_map/ppermute | solution.py:892
  54.3 0.9 copy-done.12
  55.1 3.8 %mixer_first.1 = (bf16[6,512,512]{2,1,0:T(8,128)(2,1)S(1)}, bf16[768,384]{1,0:T(8,128)(2,1)S(1)}, bf16[16,16,128]{2,1,0:T(8,128)(2,1)S(1)}, f32[512,768]{1,0:T(8,128)S(1)}) custom-call(s32[16]{0:T(128)S(1)} %pad_add_fusion.where_ref, bf16[512,768]{1,0:T(8,128)(2,1)S(1)} %copy-done, s32[1,512]{1,0:T(1,128)S(1)} %copy-done.5, bf16[592,512]{1,0:T(8,128)(2,1)} %copy-done.2, ...), custom_call_target="tpu_custom_call" | custom-call | flops 1 | bytes 1 | tf_op jit(solution)/shard_map/mixer_first/pallas_call | solution.py:36
  58.9 1.8 %collective-permute-done.9.rest_2_.rest_12_ = bf16[288,512]{1,0:T(8,128)(2,1)S(1)} collective-permute-done((bf16[288,512]{1,0:T(8,128)(2,1)S(1)}, bf16[288,512]{1,0:T(8,128)(2,1)S(1)}, u32[]{:S(2)}, u32[]{:S(2)}) %collective-permute-start.9) | collective-permute-done | bytes 294944 | tf_op jit(solution)/shard_map/ppermute | solution.py:892
  61.4 1.5 collective-permute-done.18.rest_6_.rest_16_
  62.9 3.2 %mixer_forward.1 = (bf16[6,512,512]{2,1,0:T(8,128)(2,1)S(1)}, bf16[768,384]{1,0:T(8,128)(2,1)S(1)}, bf16[16,16,128]{2,1,0:T(8,128)(2,1)S(1)}, bf16[512,768]{1,0:...) custom-call(s32[16]{0:T(128)S(1)} %pad_add_fusion.where_ref, ...), custom_call_target="tpu_custom_call", output_to_operand_aliasing={{0}: (2, {}), {1}: (3, {}), {2}: (4, {})} | custom-call | flops 1 | bytes 1 | tf_op jit(solution)/shard_map/mixer_forward/pallas_call | solution.py:36
  66.2 1.6 %collective-permute-start.20 = (bf16[256,384]{1,0:T(8,128)(2,1)S(1)}, bf16[256,384]{1,0:T(8,128)(2,1)S(1)}, u32[]{:S(2)}, u32[]{:S(2)}) collective-permute-start(bf16[256,384]{1,0:T(8,128)(2,1)S(1)} %get-tuple-element.134.own_ref.rest_0_), channel_id=1, source_target_pairs={{0,1},{1,0},{2,3},{3,2},{4,5},{5,4},{6,7},{7,6},{8,9},{9,8},{10,11... | collective-permute-start | bytes 589832 | tf_op jit(solution)/shard_map/ppermute | solution.py:1059
  68.2 5.8 %second_weights.1 = (bf16[768,3840]{1,0:T(8,128)(2,1)S(1)}, f32[512,1536]{1,0:T(8,128)S(1)}, f32[512,768]{1,0:T(8,128)S(1)}, f32[512,768]{1,0:T(8,128)S(1)}, bf16[768,768]{1,0:T(8,128)(2,1)S(1)}) custom-call(s32[16]{0:T(128)S(1)} %pad_add_fusion.where_ref, s32[1]{0:T(128)} %bitcast.second_ref, bf16[512,768]{1,0:T(8,128)(2,1)S(1)} %copy-done.1, ...), custom_call_target="tpu_custom_call" | custom-call | flops 1 | bytes 1 | tf_op jit(solution)/shard_map/second_weights/pallas_call | solution.py:36
  74.0 3.0 %ffn_main.2 = (bf16[256,768]{1,0:T(8,128)(2,1)S(1)}, f32[256,768]{1,0:T(8,128)S(1)}, bf16[256,768]{1,0:T(8,128)(2,1)S(1)}, bf16[256,1536]{1,0:T(8,128)(2,1)S(1)}, bf16[256,1536]{1,0:T(8,128)(2,1)S(1)}) custom-call(s32[1]{0:T(128)} %bitcast.second_ref, bf16[512,768]{1,0:T(8,128)(2,1)S(1)} %copy-done, bf16[256,384]{1,0:T(8,128)(2,1)S(1)} %get-tuple-element.134.own_ref.rest_0_, ...), custom_call_target="tpu_custom_call" | custom-call | flops 1 | bytes 1 | tf_op jit(solution)/shard_map/ffn_main/pallas_call | solution.py:36
  77.1 1.6 %collective-permute-start.22 = (bf16[256,768]{1,0:T(8,128)(2,1)S(1)}, bf16[256,768]{1,0:T(8,128)(2,1)S(1)}, u32[]{:S(2)}, u32[]{:S(2)}) collective-permute-start(bf16[256,768]{1,0:T(8,128)(2,1)S(1)} %get-tuple-element.150.rest_0_), channel_id=1, source_target_pairs={{0,1},{1,0},{2,3},{3,2},{4,5},{5,4},{6,7},{7,6},{8,9},{9,8},{10,11... | collective-permute-start | bytes 1179656 | tf_op jit(solution)/shard_map/ppermute | solution.py:1068
  78.7 3.1 %ffn_main.3 = (bf16[256,768]{1,0:T(8,128)(2,1)S(1)}, f32[256,768]{1,0:T(8,128)S(1)}, bf16[256,768]{1,0:T(8,128)(2,1)S(1)}, bf16[256,1536]{1,0:T(8,128)(2,1)S(1)}, bf16[256,1536]{1,0:T(8,128)(2,1)S(1)}) custom-call(s32[1]{0:T(128)} %bitcast.second_ref, bf16[512,768]{1,0:T(8,128)(2,1)S(1)} %copy-done, bf16[256,384]{1,0:T(8,128)(2,1)S(1)} %get-tuple-element.140.own_ref.rest_1_, ...), custom_call_target="tpu_custom_call" | custom-call | flops 1 | bytes 1 | tf_op jit(solution)/shard_map/ffn_main/pallas_call | solution.py:36
  81.8 4.6 %ffn_grads.1 = (bf16[8,48,3072]{2,1,0:T(8,128)(2,1)S(1)}, bf16[48,3072]{1,0:T(8,128)(2,1)S(1)}, bf16[48,3072]{1,0:T(8,128)(2,1)S(1)}, bf16[6,48,3072]{2,1,0:T(8,128)(2,1)S(1)}) custom-call(s32[16]{0:T(128)S(1)} %pad_add_fusion.1.where_ref, bf16[512,768]{1,0:T(8,128)(2,1)S(1)} %copy-done.1, bf16[256,768]{1,0:T(8,128)(2,1)S(1)} %get-tuple-element.142.rest_0_, ...), custom_call_target="tpu_custom_call" | custom-call | flops 1 | bytes 1 | tf_op jit(solution)/shard_map/ffn_grads/pallas_call | solution.py:36
  87.0 1.1 collective-permute-done.23
  89.3 1.6 %collective-permute-start.27 = (bf16[48,3072]{1,0:T(8,128)(2,1)S(1)}, bf16[48,3072]{1,0:T(8,128)(2,1)S(1)}, u32[]{:S(2)}, u32[]{:S(2)}) collective-permute-start(bf16[48,3072]{1,0:T(8,128)(2,1)S(1)} %get-tuple-element.229), channel_id=1, source_target_pairs={{0,8},{2,10},{8,16},{10,18},{16,24},{18,26},{24,28},{26,30},{28,20... | collective-permute-start | bytes 884744 | tf_op jit(solution)/shard_map/ppermute | solution.py:946
  90.8 1.4 ffn_out.1
  92.3 0.7 collective-permute-start.32
  93.0 5.1 %collective-permute-done.26 = bf16[48,3072]{1,0:T(8,128)(2,1)S(1)} collective-permute-done((bf16[48,3072]{1,0:T(8,128)(2,1)S(1)}, bf16[48,3072]{1,0:T(8,128)(2,1)S(1)}, u32[]{:S(2)}, u32[]{:S(2)}) %collective-permute-start.26) | collective-permute-done | bytes 294944 | tf_op jit(solution)/shard_map/ppermute | solution.py:946
  98.5 0.8 collective-permute-start.28
  99.3 1.3 collective-permute-start.29
  100.6 2.6 %collective-permute-done.32.rest_3_ = bf16[256,768]{1,0:T(8,128)(2,1)S(1)} collective-permute-done((bf16[256,768]{1,0:T(8,128)(2,1)S(1)}, bf16[256,768]{1,0:T(8,128)(2,1)S(1)}, u32[]{:S(2)}, u32[]{:S(2)}) %collective-permute-start.32) | collective-permute-done | bytes 393248 | tf_op jit(solution)/shard_map/ppermute | solution.py:1068
  103.2 2.1 %resid_back.1 = (f32[512,768]{1,0:T(8,128)S(1)}, bf16[512,768]{1,0:T(8,128)(2,1)S(1)}, bf16[512,768]{1,0:T(8,128)(2,1)S(1)}, f32[16,128]{1,0:T(8,128)S(1)}) custom-call(bf16[512,768]{1,0:T(8,128)(2,1)S(1)} %copy-done.1, f32[2,768]{1,0:T(2,128)S(1)} %get-tuple-element.137.gains_ref, bf16[768,768]{1,0:T(8,128)(2,1)S(1)} %get-tuple-element.164.wo_ref, ...), custom_call_target="tpu_custom_call" | custom-call | flops 1 | bytes 1 | tf_op jit(solution)/shard_map/resid_back/pallas_call | solution.py:36
  105.2 1.8 %value_back.1 = (bf16[512,384]{1,0:T(8,128)(2,1)S(1)}, bf16[256,768]{1,0:T(8,128)(2,1)S(1)}, bf16[256,768]{1,0:T(8,128)(2,1)S(1)}, f32[64,128]{1,0:T(8,128)S(1)}) custom-call(bf16[512,768]{1,0:T(8,128)(2,1)S(1)} %get-tuple-element.168.xh_ref, f32[512,768]{1,0:T(8,128)S(1)} %get-tuple-element.169.rb_ref, bf16[6,512,512]{2,1,0:T(8,128)(2,1)S(1)} %get-tuple-element.170.e_ref, ...), custom_call_target="tpu_custom_call" | custom-call | flops 1 | bytes 1 | tf_op jit(solution)/shard_map/value_back/pallas_call | solution.py:36
  107.0 0.9 collective-permute-start.33
  107.9 1.2 collective-permute-start.35
  109.3 0.7 collective-permute-start.30
  110.0 1.3 collective-permute-start.31
  111.4 2.6 %mixer_grads.1 = (bf16[8,272,512]{2,1,0:T(8,128)(2,1)S(1)}, bf16[272,512]{1,0:T(8,128)(2,1)S(1)}, bf16[7,272,512]{2,1,0:T(8,128)(2,1)S(1)}) custom-call(s32[16]{0:T(128)S(1)} %pad_add_fusion.1.where_ref, bf16[512,768]{1,0:T(8,128)(2,1)S(1)} %get-tuple-element.168.xh_ref, bf16[512,768]{1,0:T(8,128)(2,1)S(1)} %get-tuple-element.176.va_ref, ...), custom_call_target="tpu_custom_call" | custom-call | flops 1 | bytes 1 | tf_op jit(solution)/shard_map/mixer_grads/pallas_call | solution.py:36
  114.0 1.7 %weight_grads.1 = (bf16[8,272,512]{2,1,0:T(8,128)(2,1)S(1)}, bf16[272,512]{1,0:T(8,128)(2,1)S(1)}, bf16[7,272,512]{2,1,0:T(8,128)(2,1)S(1)}) custom-call(s32[16]{0:T(128)S(1)} %pad_add_fusion.1.where_ref, bf16[512,768]{1,0:T(8,128)(2,1)S(1)} %get-tuple-element.163.n1_ref, ...), custom_call_target="tpu_custom_call", output_to_operand_aliasing={{0}: (9, {}), {1}: (10, {}), {2}: (11, {})} | custom-call | flops 1 | bytes 1 | tf_op jit(solution)/shard_map/weight_grads/pallas_call | solution.py:36
  115.9 1.5 collective-permute-done.34
  117.9 1.6 %collective-permute-start.38 = (bf16[272,512]{1,0:T(8,128)(2,1)S(1)}, bf16[272,512]{1,0:T(8,128)(2,1)S(1)}, u32[]{:S(2)}, u32[]{:S(2)}) collective-permute-start(bf16[272,512]{1,0:T(8,128)(2,1)S(1)} %fusion.24), channel_id=1, source_target_pairs={{0,8},{2,10},{8,16},{10,18},{16,24},{18,26},{24,28},{26,30},{28,20... | collective-permute-start | bytes 835592 | tf_op jit(solution)/shard_map/ppermute | solution.py:946
  119.6 0.6 collective-permute-start.37
  120.2 0.9 collective-permute-start.41
  121.1 5.8 %collective-permute-done.38 = bf16[272,512]{1,0:T(8,128)(2,1)S(1)} collective-permute-done((bf16[272,512]{1,0:T(8,128)(2,1)S(1)}, bf16[272,512]{1,0:T(8,128)(2,1)S(1)}, u32[]{:S(2)}, u32[]{:S(2)}) %collective-permute-start.38) | collective-permute-done | bytes 278560 | tf_op jit(solution)/shard_map/ppermute | solution.py:946
  126.9 1.7 %collective-permute-done.37.down_ref = bf16[48,3072]{1,0:T(8,128)(2,1)S(1)} collective-permute-done((bf16[48,3072]{1,0:T(8,128)(2,1)S(1)}, bf16[48,3072]{1,0:T(8,128)(2,1)S(1)}, u32[]{:S(2)}, u32[]{:S(2)}) %collective-permute-start.37) | collective-permute-done | bytes 294944 | tf_op jit(solution)/shard_map/ppermute | solution.py:946
  128.7 0.6 collective-permute-start.40
  129.4 1.5 collective-permute-start.39
  131.0 0.9 collective-permute-start.44
  131.9 0.9 ffn_result.1
  132.8 3.8 %collective-permute-done.40 = bf16[272,512]{1,0:T(8,128)(2,1)S(1)} collective-permute-done((bf16[272,512]{1,0:T(8,128)(2,1)S(1)}, bf16[272,512]{1,0:T(8,128)(2,1)S(1)}, u32[]{:S(2)}, u32[]{:S(2)}) %collective-permute-start.40) | collective-permute-done | bytes 278560 | tf_op jit(solution)/shard_map/ppermute | solution.py:946
  137.2 1.5 collective-permute-start.42
  139.3 0.9 collective-permute-start.45
  140.2 1.2 fusion
  142.0 1.9 %collective-permute-done.42 = bf16[272,512]{1,0:T(8,128)(2,1)S(1)} collective-permute-done((bf16[272,512]{1,0:T(8,128)(2,1)S(1)}, bf16[272,512]{1,0:T(8,128)(2,1)S(1)}, u32[]{:S(2)}, u32[]{:S(2)}) %collective-permute-start.42) | collective-permute-done | bytes 278560 | tf_op jit(solution)/shard_map/ppermute | solution.py:946
  143.9 1.4 collective-permute-done.43
  145.5 1.6 %collective-permute-start.46 = (bf16[272,512]{1,0:T(8,128)(2,1)S(1)}, bf16[272,512]{1,0:T(8,128)(2,1)S(1)}, u32[]{:S(2)}, u32[]{:S(2)}) collective-permute-start(bf16[272,512]{1,0:T(8,128)(2,1)S(1)} %get-tuple-element.220), channel_id=1, source_target_pairs={{0,8},{2,10},{8,16},{10,18},{16,24},{18,26},{24,28},{26,30},{28,20... | collective-permute-start | bytes 835592 | tf_op jit(solution)/shard_map/ppermute | solution.py:946
  147.6 1.6 %collective-permute-done.45 = bf16[256,768]{1,0:T(8,128)(2,1)S(1)} collective-permute-done((bf16[256,768]{1,0:T(8,128)(2,1)S(1)}, bf16[256,768]{1,0:T(8,128)(2,1)S(1)}, u32[]{:S(2)}, u32[]{:S(2)}) %collective-permute-start.45) | collective-permute-done | bytes 393248 | tf_op jit(solution)/shard_map/ppermute | solution.py:1111
  150.3 0.9 pad_maximum_fusion
  151.2 0.9 collective-permute-done.46.up_ref
  152.1 1.5 collective-permute-done.47.down_ref
  153.6 0.9 mixer_result.1
  (101 shorter events, 11.3 us)
Async XLA Ops:
  2.0 19.0 %collective-permute-start = (bf16[592,512]{1,0:T(8,128)(2,1)S(1)}, bf16[592,512]{1,0:T(8,128)(2,1)S(1)}, u32[]{:S(2)}, u32[]{:S(2)}) collective-permute-start(bf16[592,512]{1,0:T(8,128)(2,1)S(1)} %get-tuple-element.111.rest_0_), channel_id=1, source_target_pairs={{0,8},{2,10},{8,16},{10,18},{16,24},{18,26},{24,28},{26,30},{28,20... | collective-permute-start | bytes 1818632 | tf_op jit(solution)/shard_map/ppermute | solution.py:892
  5.1 15.9 %collective-permute-start.1 = (bf16[592,512]{1,0:T(8,128)(2,1)S(1)}, bf16[592,512]{1,0:T(8,128)(2,1)S(1)}, u32[]{:S(2)}, u32[]{:S(2)}) collective-permute-start(bf16[592,512]{1,0:T(8,128)(2,1)S(1)} %get-tuple-element.111.rest_0_), channel_id=1, source_target_pairs={{0,4},{2,6},{8,0},{10,2},{16,8},{18,10},{24,16},{26,18},{28,24},{3... | collective-permute-start | bytes 1818632 | tf_op jit(solution)/shard_map/ppermute | solution.py:892
  6.0 49.2 %copy-start = (bf16[512,768]{1,0:T(8,128)(2,1)S(1)}, bf16[512,768]{1,0:T(8,128)(2,1)}, u32[]{:S(2)}) copy-start(bf16[512,768]{1,0:T(8,128)(2,1)} %tok_ref.7) | copy-start | bytes 2359300
  6.0 49.2 %copy-start.5 = (s32[1,512]{1,0:T(1,128)S(1)}, s32[1,512]{1,0:T(1,128)}, u32[]{:S(2)}) copy-start(s32[1,512]{1,0:T(1,128)} %seg_ref.3) | copy-start | bytes 6148
  6.0 4.0 %collective-permute-start.2 = (bf16[48,384]{1,0:T(8,128)(2,1)S(1)}, bf16[48,384]{1,0:T(8,128)(2,1)S(1)}, u32[]{:S(2)}, u32[]{:S(2)}) collective-permute-start(bf16[48,384]{1,0:T(8,128)(2,1)S(1)} %get-tuple-element.113), channel_id=1, source_target_pairs={{0,1},{1,0},{2,3},{3,2},{4,5},{5,4},{6,7},{7,6},{8,9},{9,8},{10,11... | collective-permute-start | bytes 110600 | tf_op jit(solution)/shard_map/ppermute | solution.py:1004
  10.0 9.5 %collective-permute-start.3 = (bf16[48,384]{1,0:T(8,128)(2,1)S(1)}, bf16[48,384]{1,0:T(8,128)(2,1)S(1)}, u32[]{:S(2)}, u32[]{:S(2)}) collective-permute-start(bf16[48,384]{1,0:T(8,128)(2,1)S(1)} %collective-permute-done.2.rest_1_), channel_id=1, source_target_pairs={{0,8},{2,10},{8,16},{10,18},{16,24},{18,26},{24,28},{26,30},{28,20... | collective-permute-start | bytes 110600 | tf_op jit(solution)/shard_map/ppermute | solution.py:1005
  12.0 9.1 %collective-permute-start.4 = (bf16[48,384]{1,0:T(8,128)(2,1)S(1)}, bf16[48,384]{1,0:T(8,128)(2,1)S(1)}, u32[]{:S(2)}, u32[]{:S(2)}) collective-permute-start(bf16[48,384]{1,0:T(8,128)(2,1)S(1)} %collective-permute-done.2.rest_1_), channel_id=1, source_target_pairs={{0,4},{2,6},{8,0},{10,2},{16,8},{18,10},{24,16},{26,18},{28,24},{3... | collective-permute-start | bytes 110600 | tf_op jit(solution)/shard_map/ppermute | solution.py:1005
  21.1 32.7 %copy-start.3 = (bf16[592,512]{1,0:T(8,128)(2,1)}, bf16[592,512]{1,0:T(8,128)(2,1)S(1)}, u32[]{:S(2)}) copy-start(bf16[592,512]{1,0:T(8,128)(2,1)S(1)} %get-tuple-element.118.rest_1_) | copy-start | bytes 1818628
  21.1 32.7 %copy-start.4 = (bf16[592,512]{1,0:T(8,128)(2,1)}, bf16[592,512]{1,0:T(8,128)(2,1)S(1)}, u32[]{:S(2)}) copy-start(bf16[592,512]{1,0:T(8,128)(2,1)S(1)} %get-tuple-element.119.rest_2_) | copy-start | bytes 1818628
  21.1 14.3 %collective-permute-start.5 = (bf16[592,512]{1,0:T(8,128)(2,1)S(1)}, bf16[592,512]{1,0:T(8,128)(2,1)S(1)}, u32[]{:S(2)}, u32[]{:S(2)}) collective-permute-start(bf16[592,512]{1,0:T(8,128)(2,1)S(1)} %get-tuple-element.118.rest_1_), channel_id=1, source_target_pairs={{0,8},{2,10},{8,16},{10,18},{16,24},{18,26},{24,28},{26,30},{28,20... | collective-permute-start | bytes 1818632 | tf_op jit(solution)/shard_map/ppermute | solution.py:892
  22.7 13.9 %collective-permute-start.6 = (bf16[592,512]{1,0:T(8,128)(2,1)S(1)}, bf16[592,512]{1,0:T(8,128)(2,1)S(1)}, u32[]{:S(2)}, u32[]{:S(2)}) collective-permute-start(bf16[592,512]{1,0:T(8,128)(2,1)S(1)} %get-tuple-element.119.rest_2_), channel_id=1, source_target_pairs={{0,4},{2,6},{8,0},{10,2},{16,8},{18,10},{24,16},{26,18},{28,24},{3... | collective-permute-start | bytes 1818632 | tf_op jit(solution)/shard_map/ppermute | solution.py:892
  35.4 18.4 %copy-start.6 = (bf16[592,512]{1,0:T(8,128)(2,1)}, bf16[592,512]{1,0:T(8,128)(2,1)S(1)}, u32[]{:S(2)}) copy-start(bf16[592,512]{1,0:T(8,128)(2,1)S(1)} %collective-permute-done.5.rest_3_) | copy-start | bytes 1818628
  36.7 17.1 %copy-start.7 = (bf16[592,512]{1,0:T(8,128)(2,1)}, bf16[592,512]{1,0:T(8,128)(2,1)S(1)}, u32[]{:S(2)}) copy-start(bf16[592,512]{1,0:T(8,128)(2,1)S(1)} %collective-permute-done.6.rest_4_) | copy-start | bytes 1818628
  36.7 13.0 %collective-permute-start.7 = (bf16[592,512]{1,0:T(8,128)(2,1)S(1)}, bf16[592,512]{1,0:T(8,128)(2,1)S(1)}, u32[]{:S(2)}, u32[]{:S(2)}) collective-permute-start(bf16[592,512]{1,0:T(8,128)(2,1)S(1)} %collective-permute-done.5.rest_3_), channel_id=1, source_target_pairs={{0,8},{2,10},{8,16},{10,18},{16,24},{18,26},{24,28},{26,30},{28,20... | collective-permute-start | bytes 1818632 | tf_op jit(solution)/shard_map/ppermute | solution.py:892
  38.2 12.7 %collective-permute-start.8 = (bf16[592,512]{1,0:T(8,128)(2,1)S(1)}, bf16[592,512]{1,0:T(8,128)(2,1)S(1)}, u32[]{:S(2)}, u32[]{:S(2)}) collective-permute-start(bf16[592,512]{1,0:T(8,128)(2,1)S(1)} %collective-permute-done.6.rest_4_), channel_id=1, source_target_pairs={{0,4},{2,6},{8,0},{10,2},{16,8},{18,10},{24,16},{26,18},{28,24},{3... | collective-permute-start | bytes 1818632 | tf_op jit(solution)/shard_map/ppermute | solution.py:892
  38.7 12.3 %collective-permute-start.12 = (bf16[592,512]{1,0:T(8,128)(2,1)S(1)}, bf16[592,512]{1,0:T(8,128)(2,1)S(1)}, u32[]{:S(2)}, u32[]{:S(2)}) collective-permute-start(bf16[592,512]{1,0:T(8,128)(2,1)S(1)} %get-tuple-element.118.rest_1_), channel_id=1, source_target_pairs={{0,2},{2,0},{4,6},{6,4},{8,10},{10,8},{12,14},{14,12},{16,18},{18,... | collective-permute-start | bytes 1818632 | tf_op jit(solution)/shard_map/ppermute | solution.py:898
  38.7 12.9 %collective-permute-start.13 = (bf16[592,512]{1,0:T(8,128)(2,1)S(1)}, bf16[592,512]{1,0:T(8,128)(2,1)S(1)}, u32[]{:S(2)}, u32[]{:S(2)}) collective-permute-start(bf16[592,512]{1,0:T(8,128)(2,1)S(1)} %get-tuple-element.119.rest_2_), channel_id=1, source_target_pairs={{0,2},{2,0},{4,6},{6,4},{8,10},{10,8},{12,14},{14,12},{16,18},{18,... | collective-permute-start | bytes 1818632 | tf_op jit(solution)/shard_map/ppermute | solution.py:898
  39.2 14.6 %copy-start.2 = (bf16[592,512]{1,0:T(8,128)(2,1)}, bf16[592,512]{1,0:T(8,128)(2,1)S(1)}, u32[]{:S(2)}) copy-start(bf16[592,512]{1,0:T(8,128)(2,1)S(1)} %fill_units.3.rest_0_) | copy-start | bytes 1818628
  39.2 14.0 %collective-permute-start.11 = (bf16[592,512]{1,0:T(8,128)(2,1)S(1)}, bf16[592,512]{1,0:T(8,128)(2,1)S(1)}, u32[]{:S(2)}, u32[]{:S(2)}) collective-permute-start(bf16[592,512]{1,0:T(8,128)(2,1)S(1)} %fill_units.3.rest_0_), channel_id=1, source_target_pairs={{0,2},{2,0},{4,6},{6,4},{8,10},{10,8},{12,14},{14,12},{16,18},{18,... | collective-permute-start | bytes 1818632 | tf_op jit(solution)/shard_map/ppermute | solution.py:898
  49.7 3.5 %collective-permute-start.14 = (bf16[592,512]{1,0:T(8,128)(2,1)S(1)}, bf16[592,512]{1,0:T(8,128)(2,1)S(1)}, u32[]{:S(2)}, u32[]{:S(2)}) collective-permute-start(bf16[592,512]{1,0:T(8,128)(2,1)S(1)} %collective-permute-done.5.rest_3_), channel_id=1, source_target_pairs={{0,2},{2,0},{4,6},{6,4},{8,10},{10,8},{12,14},{14,12},{16,18},{18,... | collective-permute-start | bytes 1818632 | tf_op jit(solution)/shard_map/ppermute | solution.py:898
  51.0 2.7 %collective-permute-start.15 = (bf16[592,512]{1,0:T(8,128)(2,1)S(1)}, bf16[592,512]{1,0:T(8,128)(2,1)S(1)}, u32[]{:S(2)}, u32[]{:S(2)}) collective-permute-start(bf16[592,512]{1,0:T(8,128)(2,1)S(1)} %collective-permute-done.6.rest_4_), channel_id=1, source_target_pairs={{0,2},{2,0},{4,6},{6,4},{8,10},{10,8},{12,14},{14,12},{16,18},{18,... | collective-permute-start | bytes 1818632 | tf_op jit(solution)/shard_map/ppermute | solution.py:898
  51.0 2.8 %copy-start.8 = (bf16[592,512]{1,0:T(8,128)(2,1)}, bf16[592,512]{1,0:T(8,128)(2,1)S(1)}, u32[]{:S(2)}) copy-start(bf16[592,512]{1,0:T(8,128)(2,1)S(1)} %collective-permute-done.12.rest_6_) | copy-start | bytes 1818628
  51.0 9.8 %collective-permute-start.10 = (bf16[304,512]{1,0:T(8,128)(2,1)S(1)}, bf16[304,512]{1,0:T(8,128)(2,1)S(1)}, u32[]{:S(2)}, u32[]{:S(2)}) collective-permute-start(bf16[304,512]{1,0:T(8,128)(2,1)S(1)} %slice.104), channel_id=1, source_target_pairs={{0,4},{2,6},{8,0},{10,2},{16,8},{18,10},{24,16},{26,18},{28,24},{3... | collective-permute-start | bytes 933896 | tf_op jit(solution)/shard_map/ppermute | solution.py:892
  51.6 2.2 %copy-start.9 = (bf16[592,512]{1,0:T(8,128)(2,1)}, bf16[592,512]{1,0:T(8,128)(2,1)S(1)}, u32[]{:S(2)}) copy-start(bf16[592,512]{1,0:T(8,128)(2,1)S(1)} %collective-permute-done.13.rest_7_) | copy-start | bytes 1818628
  51.6 9.2 %collective-permute-start.9 = (bf16[288,512]{1,0:T(8,128)(2,1)S(1)}, bf16[288,512]{1,0:T(8,128)(2,1)S(1)}, u32[]{:S(2)}, u32[]{:S(2)}) collective-permute-start(bf16[288,512]{1,0:T(8,128)(2,1)S(1)} %slice.103), channel_id=1, source_target_pairs={{0,8},{2,10},{8,16},{10,18},{16,24},{18,26},{24,28},{26,30},{28,20... | collective-permute-start | bytes 884744 | tf_op jit(solution)/shard_map/ppermute | solution.py:892
  53.2 0.8 copy-start.10
  53.2 9.7 %collective-permute-start.16 = (bf16[592,512]{1,0:T(8,128)(2,1)S(1)}, bf16[592,512]{1,0:T(8,128)(2,1)S(1)}, u32[]{:S(2)}, u32[]{:S(2)}) collective-permute-start(bf16[592,512]{1,0:T(8,128)(2,1)S(1)} %collective-permute-done.7.rest_0_.rest_10_), channel_id=1, source_target_pairs={{0,2},{2,0},{4,6},{6,4},{8,10},{10,8},{12,14},{14,12},{16,18},{18,... | collective-permute-start | bytes 1818632 | tf_op jit(solution)/shard_map/ppermute | solution.py:898
  53.2 1.0 copy-start.11
  53.3 9.7 %collective-permute-start.17 = (bf16[592,512]{1,0:T(8,128)(2,1)S(1)}, bf16[592,512]{1,0:T(8,128)(2,1)S(1)}, u32[]{:S(2)}, u32[]{:S(2)}) collective-permute-start(bf16[592,512]{1,0:T(8,128)(2,1)S(1)} %collective-permute-done.8.rest_1_.rest_11_), channel_id=1, source_target_pairs={{0,2},{2,0},{4,6},{6,4},{8,10},{10,8},{12,14},{14,12},{16,18},{18,... | collective-permute-start | bytes 1818632 | tf_op jit(solution)/shard_map/ppermute | solution.py:898
  54.3 0.9 copy-start.12
  60.9 7.4 %copy-start.1 = (bf16[512,768]{1,0:T(8,128)(2,1)S(1)}, bf16[512,768]{1,0:T(8,128)(2,1)}, u32[]{:S(2)}) copy-start(bf16[512,768]{1,0:T(8,128)(2,1)} %cot_ref.5) | copy-start | bytes 2359300
  60.9 2.0 %collective-permute-start.19 = (bf16[304,512]{1,0:T(8,128)(2,1)S(1)}, bf16[304,512]{1,0:T(8,128)(2,1)S(1)}, u32[]{:S(2)}, u32[]{:S(2)}) collective-permute-start(bf16[304,512]{1,0:T(8,128)(2,1)S(1)} %collective-permute-done.10.rest_3_.rest_13_), channel_id=1, source_target_pairs={{0,2},{2,0},{4,6},{6,4},{8,10},{10,8},{12,14},{14,12},{16,18},{18,... | collective-permute-start | bytes 933896 | tf_op jit(solution)/shard_map/ppermute | solution.py:898
  60.9 2.0 %collective-permute-start.18 = (bf16[288,512]{1,0:T(8,128)(2,1)S(1)}, bf16[288,512]{1,0:T(8,128)(2,1)S(1)}, u32[]{:S(2)}, u32[]{:S(2)}) collective-permute-start(bf16[288,512]{1,0:T(8,128)(2,1)S(1)} %collective-permute-done.9.rest_2_.rest_12_), channel_id=1, source_target_pairs={{0,2},{2,0},{4,6},{6,4},{8,10},{10,8},{12,14},{14,12},{16,18},{18,... | collective-permute-start | bytes 884744 | tf_op jit(solution)/shard_map/ppermute | solution.py:898
  66.2 7.9 %collective-permute-start.20 = (bf16[256,384]{1,0:T(8,128)(2,1)S(1)}, bf16[256,384]{1,0:T(8,128)(2,1)S(1)}, u32[]{:S(2)}, u32[]{:S(2)}) collective-permute-start(bf16[256,384]{1,0:T(8,128)(2,1)S(1)} %get-tuple-element.134.own_ref.rest_0_), channel_id=1, source_target_pairs={{0,1},{1,0},{2,3},{3,2},{4,5},{5,4},{6,7},{7,6},{8,9},{9,8},{10,11... | collective-permute-start | bytes 589832 | tf_op jit(solution)/shard_map/ppermute | solution.py:1059
  67.8 10.9 %collective-permute-start.21 = (bf16[256,384]{1,0:T(8,128)(2,1)S(1)}, bf16[256,384]{1,0:T(8,128)(2,1)S(1)}, u32[]{:S(2)}, u32[]{:S(2)}) collective-permute-start(bf16[256,384]{1,0:T(8,128)(2,1)S(1)} %get-tuple-element.140.own_ref.rest_1_), channel_id=1, source_target_pairs={{0,1},{1,0},{2,3},{3,2},{4,5},{5,4},{6,7},{7,6},{8,9},{9,8},{10,11... | collective-permute-start | bytes 589832 | tf_op jit(solution)/shard_map/ppermute | solution.py:1059
  77.1 11.4 %collective-permute-start.22 = (bf16[256,768]{1,0:T(8,128)(2,1)S(1)}, bf16[256,768]{1,0:T(8,128)(2,1)S(1)}, u32[]{:S(2)}, u32[]{:S(2)}) collective-permute-start(bf16[256,768]{1,0:T(8,128)(2,1)S(1)} %get-tuple-element.150.rest_0_), channel_id=1, source_target_pairs={{0,1},{1,0},{2,3},{3,2},{4,5},{5,4},{6,7},{7,6},{8,9},{9,8},{10,11... | collective-permute-start | bytes 1179656 | tf_op jit(solution)/shard_map/ppermute | solution.py:1068
  86.4 1.6 %collective-permute-start.23 = (bf16[48,3072]{1,0:T(8,128)(2,1)S(1)}, bf16[48,3072]{1,0:T(8,128)(2,1)S(1)}, u32[]{:S(2)}, u32[]{:S(2)}) collective-permute-start(bf16[48,3072]{1,0:T(8,128)(2,1)S(1)} %get-tuple-element.151), channel_id=1, source_target_pairs={{0,2},{2,0},{4,6},{6,4},{8,10},{10,8},{12,14},{14,12},{16,18},{18,... | collective-permute-start | bytes 884744 | tf_op jit(solution)/shard_map/ppermute | solution.py:918
  86.5 2.0 %collective-permute-start.24 = (bf16[48,3072]{1,0:T(8,128)(2,1)S(1)}, bf16[48,3072]{1,0:T(8,128)(2,1)S(1)}, u32[]{:S(2)}, u32[]{:S(2)}) collective-permute-start(bf16[48,3072]{1,0:T(8,128)(2,1)S(1)} %get-tuple-element.152), channel_id=1, source_target_pairs={{0,2},{2,0},{4,6},{6,4},{8,10},{10,8},{12,14},{14,12},{16,18},{18,... | collective-permute-start | bytes 884744 | tf_op jit(solution)/shard_map/ppermute | solution.py:918
  88.5 9.8 %collective-permute-start.25 = (bf16[6,48,3072]{2,1,0:T(8,128)(2,1)S(1)}, bf16[6,48,3072]{2,1,0:T(8,128)(2,1)S(1)}, u32[]{:S(2)}, u32[]{:S(2)}) collective-permute-start(bf16[6,48,3072]{2,1,0:T(8,128)(2,1)S(1)} %get-tuple-element.153), channel_id=1, source_target_pairs={{0,2},{2,0},{4,6},{6,4},{8,10},{10,8},{12,14},{14,12},{16,18},{18,... | collective-permute-start | bytes 5308424 | tf_op jit(solution)/shard_map/ppermute | solution.py:937
  88.8 9.3 %collective-permute-start.26 = (bf16[48,3072]{1,0:T(8,128)(2,1)S(1)}, bf16[48,3072]{1,0:T(8,128)(2,1)S(1)}, u32[]{:S(2)}, u32[]{:S(2)}) collective-permute-start(bf16[48,3072]{1,0:T(8,128)(2,1)S(1)} %get-tuple-element.230), channel_id=1, source_target_pairs={{0,4},{2,6},{8,0},{10,2},{16,8},{18,10},{24,16},{26,18},{28,24},{3... | collective-permute-start | bytes 884744 | tf_op jit(solution)/shard_map/ppermute | solution.py:946
  89.3 9.0 %collective-permute-start.27 = (bf16[48,3072]{1,0:T(8,128)(2,1)S(1)}, bf16[48,3072]{1,0:T(8,128)(2,1)S(1)}, u32[]{:S(2)}, u32[]{:S(2)}) collective-permute-start(bf16[48,3072]{1,0:T(8,128)(2,1)S(1)} %get-tuple-element.229), channel_id=1, source_target_pairs={{0,8},{2,10},{8,16},{10,18},{16,24},{18,26},{24,28},{26,30},{28,20... | collective-permute-start | bytes 884744 | tf_op jit(solution)/shard_map/ppermute | solution.py:946
  92.3 10.9 %collective-permute-start.32 = (bf16[256,768]{1,0:T(8,128)(2,1)S(1)}, bf16[256,768]{1,0:T(8,128)(2,1)S(1)}, u32[]{:S(2)}, u32[]{:S(2)}) collective-permute-start(bf16[256,768]{1,0:T(8,128)(2,1)S(1)} %get-tuple-element.167.rest_1_), channel_id=1, source_target_pairs={{0,1},{1,0},{2,3},{3,2},{4,5},{5,4},{6,7},{7,6},{8,9},{9,8},{10,11... | collective-permute-start | bytes 1179656 | tf_op jit(solution)/shard_map/ppermute | solution.py:1068
  98.5 9.4 %collective-permute-start.28 = (bf16[48,3072]{1,0:T(8,128)(2,1)S(1)}, bf16[48,3072]{1,0:T(8,128)(2,1)S(1)}, u32[]{:S(2)}, u32[]{:S(2)}) collective-permute-start(bf16[48,3072]{1,0:T(8,128)(2,1)S(1)} %get-tuple-element.226), channel_id=1, source_target_pairs={{0,4},{2,6},{8,0},{10,2},{16,8},{18,10},{24,16},{26,18},{28,24},{3... | collective-permute-start | bytes 884744 | tf_op jit(solution)/shard_map/ppermute | solution.py:946
  99.3 8.6 %collective-permute-start.29 = (bf16[48,3072]{1,0:T(8,128)(2,1)S(1)}, bf16[48,3072]{1,0:T(8,128)(2,1)S(1)}, u32[]{:S(2)}, u32[]{:S(2)}) collective-permute-start(bf16[48,3072]{1,0:T(8,128)(2,1)S(1)} %get-tuple-element.225), channel_id=1, source_target_pairs={{0,8},{2,10},{8,16},{10,18},{16,24},{18,26},{24,28},{26,30},{28,20... | collective-permute-start | bytes 884744 | tf_op jit(solution)/shard_map/ppermute | solution.py:946
  107.0 7.0 %collective-permute-start.33 = (f32[64,128]{1,0:T(8,128)S(1)}, f32[64,128]{1,0:T(8,128)S(1)}, u32[]{:S(2)}, u32[]{:S(2)}) collective-permute-start(f32[64,128]{1,0:T(8,128)S(1)} %get-tuple-element.174.ga_ref), channel_id=1, source_target_pairs={{0,1},{1,0},{2,3},{3,2},{4,5},{5,4},{6,7},{7,6},{8,9},{9,8},{10,11... | collective-permute-start | bytes 98312 | tf_op jit(solution)/shard_map/ppermute | solution.py:1087
  107.9 9.5 %collective-permute-start.35 = (bf16[224,768]{1,0:T(8,128)(2,1)S(1)}, bf16[224,768]{1,0:T(8,128)(2,1)S(1)}, u32[]{:S(2)}, u32[]{:S(2)}) collective-permute-start(bf16[224,768]{1,0:T(8,128)(2,1)S(1)} %get-tuple-element.181), channel_id=1, source_target_pairs={{0,1},{1,0},{2,3},{3,2},{4,5},{5,4},{6,7},{7,6},{8,9},{9,8},{10,11... | collective-permute-start | bytes 1032200 | tf_op jit(solution)/shard_map/ppermute | solution.py:1085
  109.3 8.1 %collective-permute-start.30 = (bf16[48,3072]{1,0:T(8,128)(2,1)S(1)}, bf16[48,3072]{1,0:T(8,128)(2,1)S(1)}, u32[]{:S(2)}, u32[]{:S(2)}) collective-permute-start(bf16[48,3072]{1,0:T(8,128)(2,1)S(1)} %get-tuple-element.224), channel_id=1, source_target_pairs={{0,4},{2,6},{8,0},{10,2},{16,8},{18,10},{24,16},{26,18},{28,24},{3... | collective-permute-start | bytes 884744 | tf_op jit(solution)/shard_map/ppermute | solution.py:946
  110.0 7.4 %collective-permute-start.31 = (bf16[48,3072]{1,0:T(8,128)(2,1)S(1)}, bf16[48,3072]{1,0:T(8,128)(2,1)S(1)}, u32[]{:S(2)}, u32[]{:S(2)}) collective-permute-start(bf16[48,3072]{1,0:T(8,128)(2,1)S(1)} %get-tuple-element.223), channel_id=1, source_target_pairs={{0,8},{2,10},{8,16},{10,18},{16,24},{18,26},{24,28},{26,30},{28,20... | collective-permute-start | bytes 884744 | tf_op jit(solution)/shard_map/ppermute | solution.py:946
  115.8 1.6 %collective-permute-start.34 = (bf16[272,512]{1,0:T(8,128)(2,1)S(1)}, bf16[272,512]{1,0:T(8,128)(2,1)S(1)}, u32[]{:S(2)}, u32[]{:S(2)}) collective-permute-start(bf16[272,512]{1,0:T(8,128)(2,1)S(1)} %get-tuple-element.180), channel_id=1, source_target_pairs={{0,2},{2,0},{4,6},{6,4},{8,10},{10,8},{12,14},{14,12},{16,18},{18,... | collective-permute-start | bytes 835592 | tf_op jit(solution)/shard_map/ppermute | solution.py:918
  117.5 11.2 %collective-permute-start.36 = (bf16[7,272,512]{2,1,0:T(8,128)(2,1)S(1)}, bf16[7,272,512]{2,1,0:T(8,128)(2,1)S(1)}, u32[]{:S(2)}, u32[]{:S(2)}) collective-permute-start(bf16[7,272,512]{2,1,0:T(8,128)(2,1)S(1)} %get-tuple-element.188), channel_id=1, source_target_pairs={{0,2},{2,0},{4,6},{6,4},{8,10},{10,8},{12,14},{14,12},{16,18},{18,... | collective-permute-start | bytes 5849096 | tf_op jit(solution)/shard_map/ppermute | solution.py:937
  117.9 9.0 %collective-permute-start.38 = (bf16[272,512]{1,0:T(8,128)(2,1)S(1)}, bf16[272,512]{1,0:T(8,128)(2,1)S(1)}, u32[]{:S(2)}, u32[]{:S(2)}) collective-permute-start(bf16[272,512]{1,0:T(8,128)(2,1)S(1)} %fusion.24), channel_id=1, source_target_pairs={{0,8},{2,10},{8,16},{10,18},{16,24},{18,26},{24,28},{26,30},{28,20... | collective-permute-start | bytes 835592 | tf_op jit(solution)/shard_map/ppermute | solution.py:946
  119.6 9.0 %collective-permute-start.37 = (bf16[48,3072]{1,0:T(8,128)(2,1)S(1)}, bf16[48,3072]{1,0:T(8,128)(2,1)S(1)}, u32[]{:S(2)}, u32[]{:S(2)}) collective-permute-start(bf16[48,3072]{1,0:T(8,128)(2,1)S(1)} %fusion.19), channel_id=1, source_target_pairs={{0,4},{2,6},{8,0},{10,2},{16,8},{18,10},{24,16},{26,18},{28,24},{3... | collective-permute-start | bytes 884744 | tf_op jit(solution)/shard_map/ppermute | solution.py:946
  120.2 12.6 %collective-permute-start.41 = (bf16[288,768]{1,0:T(8,128)(2,1)S(1)}, bf16[288,768]{1,0:T(8,128)(2,1)S(1)}, u32[]{:S(2)}, u32[]{:S(2)}) collective-permute-start(bf16[288,768]{1,0:T(8,128)(2,1)S(1)} %get-tuple-element.183), channel_id=1, source_target_pairs={{0,1},{1,0},{2,3},{3,2},{4,5},{5,4},{6,7},{7,6},{8,9},{9,8},{10,11... | collective-permute-start | bytes 1327112 | tf_op jit(solution)/shard_map/ppermute | solution.py:1102
  128.7 7.9 %collective-permute-start.40 = (bf16[272,512]{1,0:T(8,128)(2,1)S(1)}, bf16[272,512]{1,0:T(8,128)(2,1)S(1)}, u32[]{:S(2)}, u32[]{:S(2)}) collective-permute-start(bf16[272,512]{1,0:T(8,128)(2,1)S(1)} %fusion.30), channel_id=1, source_target_pairs={{0,4},{2,6},{8,0},{10,2},{16,8},{18,10},{24,16},{26,18},{28,24},{3... | collective-permute-start | bytes 835592 | tf_op jit(solution)/shard_map/ppermute | solution.py:946
  129.4 7.6 %collective-permute-start.39 = (bf16[272,512]{1,0:T(8,128)(2,1)S(1)}, bf16[272,512]{1,0:T(8,128)(2,1)S(1)}, u32[]{:S(2)}, u32[]{:S(2)}) collective-permute-start(bf16[272,512]{1,0:T(8,128)(2,1)S(1)} %fusion.29), channel_id=1, source_target_pairs={{0,8},{2,10},{8,16},{10,18},{16,24},{18,26},{24,28},{26,30},{28,20... | collective-permute-start | bytes 835592 | tf_op jit(solution)/shard_map/ppermute | solution.py:946
  131.0 11.0 %collective-permute-start.44 = (bf16[256,768]{1,0:T(8,128)(2,1)S(1)}, bf16[256,768]{1,0:T(8,128)(2,1)S(1)}, u32[]{:S(2)}, u32[]{:S(2)}) collective-permute-start(bf16[256,768]{1,0:T(8,128)(2,1)S(1)} %get-tuple-element.197), channel_id=1, source_target_pairs={{0,1},{1,0},{2,3},{3,2},{4,5},{5,4},{6,7},{7,6},{8,9},{9,8},{10,11... | collective-permute-start | bytes 1179656 | tf_op jit(solution)/shard_map/ppermute | solution.py:1108
  137.2 6.7 %collective-permute-start.42 = (bf16[272,512]{1,0:T(8,128)(2,1)S(1)}, bf16[272,512]{1,0:T(8,128)(2,1)S(1)}, u32[]{:S(2)}, u32[]{:S(2)}) collective-permute-start(bf16[272,512]{1,0:T(8,128)(2,1)S(1)} %get-tuple-element.222), channel_id=1, source_target_pairs={{0,8},{2,10},{8,16},{10,18},{16,24},{18,26},{24,28},{26,30},{28,20... | collective-permute-start | bytes 835592 | tf_op jit(solution)/shard_map/ppermute | solution.py:946
  138.8 6.5 %collective-permute-start.43 = (bf16[272,512]{1,0:T(8,128)(2,1)S(1)}, bf16[272,512]{1,0:T(8,128)(2,1)S(1)}, u32[]{:S(2)}, u32[]{:S(2)}) collective-permute-start(bf16[272,512]{1,0:T(8,128)(2,1)S(1)} %get-tuple-element.221), channel_id=1, source_target_pairs={{0,4},{2,6},{8,0},{10,2},{16,8},{18,10},{24,16},{26,18},{28,24},{3... | collective-permute-start | bytes 835592 | tf_op jit(solution)/shard_map/ppermute | solution.py:946
  139.3 9.9 %collective-permute-start.45 = (bf16[256,768]{1,0:T(8,128)(2,1)S(1)}, bf16[256,768]{1,0:T(8,128)(2,1)S(1)}, u32[]{:S(2)}, u32[]{:S(2)}) collective-permute-start(bf16[256,768]{1,0:T(8,128)(2,1)S(1)} %get-tuple-element.201), channel_id=1, source_target_pairs={{0,1},{1,0},{2,3},{3,2},{4,5},{5,4},{6,7},{7,6},{8,9},{9,8},{10,11... | collective-permute-start | bytes 1179656 | tf_op jit(solution)/shard_map/ppermute | solution.py:1111
  145.5 6.6 %collective-permute-start.46 = (bf16[272,512]{1,0:T(8,128)(2,1)S(1)}, bf16[272,512]{1,0:T(8,128)(2,1)S(1)}, u32[]{:S(2)}, u32[]{:S(2)}) collective-permute-start(bf16[272,512]{1,0:T(8,128)(2,1)S(1)} %get-tuple-element.220), channel_id=1, source_target_pairs={{0,8},{2,10},{8,16},{10,18},{16,24},{18,26},{24,28},{26,30},{28,20... | collective-permute-start | bytes 835592 | tf_op jit(solution)/shard_map/ppermute | solution.py:946
  147.1 6.5 %collective-permute-start.47 = (bf16[272,512]{1,0:T(8,128)(2,1)S(1)}, bf16[272,512]{1,0:T(8,128)(2,1)S(1)}, u32[]{:S(2)}, u32[]{:S(2)}) collective-permute-start(bf16[272,512]{1,0:T(8,128)(2,1)S(1)} %get-tuple-element.219), channel_id=1, source_target_pairs={{0,4},{2,6},{8,0},{10,2},{16,8},{18,10},{24,16},{26,18},{28,24},{3... | collective-permute-start | bytes 835592 | tf_op jit(solution)/shard_map/ppermute | solution.py:946

commit v6 on v5

--- a/solution.py
+++ b/solution.py
@@ -366,6 +366,7 @@
 
 def second_weights(plan, where, second, cotangent, sums, units, shares, near, size):
     length, model = cotangent.shape
+    wide = sums.shape[1]
     hidden, krows, width = plan.hidden, plan.krows, plan.width
     piece = hidden // 3
     parts = plan.ffn_parts()
@@ -379,7 +380,7 @@
 
         copies = pick(rest[: len(units)], shares, where_ref, parts, target, sem)
         inside = lax.broadcasted_iota(jnp.int32, (length, LANES), 1) < size
-        for h in range(sums.shape[1] // LANES):
+        for h in range(wide // LANES):
             lanes = slice(h * LANES, (h + 1) * LANES)
             inverse = jnp.broadcast_to(1.0 / sums_ref[:, h * LANES + size : h * LANES + size + 1], (length, LANES))
             rb_ref[:, lanes] = inverse
@@ -404,7 +405,7 @@
             ((length, hidden), F32),
             (sums.shape, F32),
             (sums.shape, F32),
-            ((model, sums.shape[1]), BF),
+            ((model, wide), BF),
         ),
         (pltpu.SemaphoreType.DMA((UNITS, len(parts))),),
         loose=units,
@@ -412,7 +413,7 @@
     )
 
 
-def ffn_main(second, tokens, mixed_own, mixed_other, gact, gains, w, part, parts, pieces):
+def ffn_main(second, tokens, mixed_own, mixed_other, gact, gains, w, part, parts, before):
     length, model = tokens.shape
     width = mixed_own.shape[1]
     hidden = gact.shape[1]
@@ -420,10 +421,8 @@
     piece = hidden // 3
     at = slice(part * chunk, (part + 1) * chunk)
 
-    def kernel(second_ref, tok_ref, own_ref, other_ref, gact_ref, gains_ref, w_ref,
-               *rest):
-        backs = rest[:pieces]
-        resid_ref, n2_ref, act_ref, gpre_ref, mixed, acc = rest[pieces:]
+    def kernel(second_ref, tok_ref, own_ref, other_ref, gact_ref, gains_ref, w_ref, *rest):
+        back_ref, resid_ref, n2_ref, act_ref, gpre_ref, mixed, acc = rest[len(before) :]
         first = second_ref[0]
         mixed[:, pl.ds(multiple(first * width, LANES), width)] = own_ref[...]
         mixed[:, pl.ds(multiple((1 - first) * width, LANES), width)] = other_ref[...]
@@ -431,36 +430,36 @@
         resid = tok_ref[at, :].astype(F32) + attn
         resid_ref[...] = resid
         inv = lax.rsqrt(jnp.mean(resid * resid, axis=-1, keepdims=True) + EPSILON)
-        n2_ref[...] = (resid * inv * gains_ref[1:2, :]).astype(BF)
+        n2_ref[at, :] = (resid * inv * gains_ref[1:2, :]).astype(BF)
         for j in range(hidden // piece):
             cols = slice(j * piece, (j + 1) * piece)
-            act, slope = gelu_pair(mm(n2_ref[...], w_ref[:, cols]))
-            act_ref[:, cols] = act.astype(BF)
-            gpre_ref[:, cols] = (gact_ref[at, cols] * slope).astype(BF)
-            term = mm(gpre_ref[:, cols], w_ref[:, cols], NT)
+            act, slope = gelu_pair(mm(n2_ref[at, :], w_ref[:, cols]))
+            act_ref[at, cols] = act.astype(BF)
+            gpre_ref[at, cols] = (gact_ref[at, cols] * slope).astype(BF)
+            term = mm(gpre_ref[at, cols], w_ref[:, cols], NT)
             if j == 0:
                 acc[...] = term
             else:
                 acc[...] += term
-        for n, back_ref in enumerate(backs):
-            back_ref[...] = acc[n * (chunk // pieces) : (n + 1) * (chunk // pieces), :].astype(BF)
+        back_ref[...] = acc[...].astype(BF)
 
     return run(
         kernel,
         "ffn_main",
         (second,),
-        (tokens, mixed_own, mixed_other, gact, gains, w),
+        (tokens, mixed_own, mixed_other, gact, gains, w, *before),
         (
-            *[((chunk // pieces, model), BF)] * pieces,
+            ((chunk, model), BF),
             ((chunk, model), F32),
-            ((chunk, model), BF),
-            ((chunk, hidden), BF),
-            ((chunk, hidden), BF),
+            ((length, model), BF),
+            ((length, hidden), BF),
+            ((length, hidden), BF),
         ),
         (
             pltpu.VMEM((chunk, 2 * width), BF),
             pltpu.VMEM((chunk, model), F32),
         ),
+        aliases={7 + n: 2 + n for n in range(len(before))},
     )
 
 
@@ -561,46 +560,30 @@
     return result_kernel("mixer_result", keep, own, up, down, shapes, cut)
 
 
-def ffn_out(acts, w, cut):
-    chunk, hidden = acts[0].shape
+def ffn_out(act, w, cut):
+    length, hidden = act.shape
     model = w.shape[0]
-    length = chunk * len(acts)
-
-    def kernel(*refs):
-        w_ref, out = refs[-4:-3][0], refs[-1]
-        for r, act in enumerate(refs[:-4]):
-            out[r * chunk : (r + 1) * chunk, :] = mm(act[...], w_ref[:, hidden : 2 * hidden], NT).astype(BF)
-        refs[-3][...] = out[:cut, :]
-        refs[-2][...] = out[cut:, :]
-
-    return run(
-        kernel,
-        "ffn_out",
-        (),
-        (*acts, w),
-        (((cut, model), BF), ((length - cut, model), BF)),
-        (pltpu.VMEM((length, model), BF),),
-    )
-
-
-def ffn_grads(where, n2s, gpres, acts, cotangent):
-    parts = len(n2s)
-    chunk, model = n2s[0].shape
-    hidden = acts[0].shape[1]
+
+    def kernel(act_ref, w_ref, one, two):
+        one[...] = mm(act_ref[:cut, :], w_ref[:, hidden : 2 * hidden], NT).astype(BF)
+        two[...] = mm(act_ref[cut:, :], w_ref[:, hidden : 2 * hidden], NT).astype(BF)
+
+    return run(kernel, "ffn_out", (), (act, w), (((cut, model), BF), ((length - cut, model), BF)))
+
+
+def ffn_grads(where, n2, gpre, act, cotangent):
+    model, hidden = n2.shape[1], act.shape[1]
     krows = model // UNITS
 
-    def kernel(where_ref, cot_ref, *rest):
-        n2, gpre, act = rest[:parts], rest[parts : 2 * parts], rest[2 * parts : 3 * parts]
-        slot = slots(rest[3 * parts : -2], FFN_FIRST, 1)
+    def kernel(where_ref, cot_ref, n2_ref, gpre_ref, act_ref, *rest):
+        slot = slots(rest[:-2], FFN_FIRST, 1)
         scr, sem = rest[-2:]
         piece = hidden // 3
         for j in range(3):
             cols = slice(j * piece, (j + 1) * piece)
             down = slice(hidden + j * piece, hidden + (j + 1) * piece)
-            one = [mm(n2[r][...], gpre[r][:, cols], TN) for r in range(parts)]
-            scr[:, cols] = sum(one).astype(BF)
-            two = [mm(cot_ref[r * chunk : (r + 1) * chunk, :], act[r][:, cols], TN) for r in range(parts)]
-            scr[:, down] = sum(two).astype(BF)
+            scr[:, cols] = mm(n2_ref[...], gpre_ref[:, cols], TN).astype(BF)
+            scr[:, down] = mm(cot_ref[...], act_ref[:, cols], TN).astype(BF)
         copies = []
         for u in range(UNITS):
             at = pl.ds(multiple(where_ref[u] * krows, 16), krows)
@@ -614,7 +597,7 @@
         kernel,
         "ffn_grads",
         (where,),
-        (cotangent, *n2s, *gpres, *acts),
+        (cotangent, n2, gpre, act),
         (),
         (pltpu.VMEM((model, 2 * hidden), BF), pltpu.SemaphoreType.DMA((UNITS,))),
         loose_outs=slot_shapes(krows, 2 * hidden, FFN_FIRST, 1, False),
@@ -636,91 +619,80 @@
     return pieces + mm(jnp.where(own, row - high, 0.0).astype(BF), take)
 
 
-def resid_back(backs, others, resids, cotangent, gains, wo, mixf, heads, size):
-    length, model = cotangent.shape
+def resid_back(back, other, resid, cotangent, gains, wo, mixf, part, heads, size, before):
+    chunk, model = resid.shape
     wide = heads * LANES
-    count = len(backs)
-    krows = model // UNITS
-    parts = len(resids)
-
-
-    def kernel(cot_ref, gains_ref, wo_ref, mixf_ref, *rest):
-        mine, other, res_refs = rest[:count], rest[count : 2 * count], rest[2 * count : 2 * count + parts]
-        gres_ref, gat_ref, xh_ref, gf_ref, gm = rest[2 * count + parts :]
-        total = jnp.zeros((8, model), F32)
-        begin = 0
-        for r in range(count):
-            chunk = mine[r].shape[0]
-            at = slice(begin, begin + chunk)
-            g2 = mine[r][...].astype(F32) + other[r][...].astype(F32)
-            whole = length // parts
-            res = res_refs[begin // whole][begin % whole : begin % whole + chunk, :]
-            begin += chunk
-            inv = lax.rsqrt(jnp.mean(res * res, axis=-1, keepdims=True) + EPSILON)
-            hat = res * inv
-            total = total + jnp.sum((g2 * hat).reshape(chunk // 8, 8, model), axis=0)
-            z = gains_ref[1:2, :] * g2
-            corr = jnp.mean(z * hat, axis=-1, keepdims=True)
-            gres = cot_ref[at, :].astype(F32) + inv * (z - hat * corr)
-            gres_ref[at, :] = gres
-            gat_ref[at, :] = gres.astype(BF)
+    at = slice(part * chunk, (part + 1) * chunk)
+
+    def kernel(cot_ref, gains_ref, wo_ref, mixf_ref, back_ref, other_ref, res_ref, *rest):
+        gres_ref, gat_ref, xh_ref, gain_ref, gm = rest[len(before) :]
+        g2 = back_ref[...].astype(F32) + other_ref[...].astype(F32)
+        res = res_ref[...]
+        inv = lax.rsqrt(jnp.mean(res * res, axis=-1, keepdims=True) + EPSILON)
+        hat = res * inv
+        total = jnp.sum((g2 * hat).reshape(chunk // 8, 8, model), axis=0)
+        gain_ref[...] = total + rest[0][...] if before else total
+        z = gains_ref[1:2, :] * g2
+        corr = jnp.mean(z * hat, axis=-1, keepdims=True)
+        gres = cot_ref[at, :].astype(F32) + inv * (z - hat * corr)
+        gres_ref[...] = gres
+        gat_ref[...] = gres.astype(BF)
         gm[...] = mm(gat_ref[...], wo_ref[...]).astype(BF)
-        lane = lax.broadcasted_iota(jnp.int32, (length, LANES), 1)
+        lane = lax.broadcasted_iota(jnp.int32, (chunk, LANES), 1)
         for h in range(heads):
             lanes = slice(h * LANES, (h + 1) * LANES)
             here = gm[:, lanes].astype(F32)
-            inner = -jnp.sum(here * mixf_ref[:, lanes], axis=-1, keepdims=True)
+            inner = -jnp.sum(here * mixf_ref[at, lanes], axis=-1, keepdims=True)
             high = inner.astype(BF).astype(F32)
             xh_ref[:, lanes] = jnp.where(
                 lane == size, high, jnp.where(lane == size + 1, inner - high, here)
             ).astype(BF)
-        gf_ref[...] = cut_gain(jnp.sum(total, axis=0, keepdims=True), krows)
 
     return run(
         kernel,
         "resid_back",
         (),
-        (cotangent, gains, wo, mixf, *backs, *others, *resids),
+        (cotangent, gains, wo, mixf, back, other, resid, *before),
         (
-            ((length, model), F32),
-            ((length, model), BF),
-            ((length, wide), BF),
-            ((UNITS, LANES), F32),
+            ((chunk, model), F32),
+            ((chunk, model), BF),
+            ((chunk, wide), BF),
+            ((8, model), F32),
         ),
-        (pltpu.VMEM((length, wide), BF),),
-    )
-
-
-def score_grads(where_ref, xh_ref, va_ref, e_ref, rb_ref, ds, slot, begin, count, rows):
-    length = ds.shape[0]
-
-    def one_head(h, carry):
-        lanes = pl.ds(multiple((begin + h) * LANES, LANES), LANES)
-        d = mm(xh_ref[:, lanes], va_ref[:, lanes], NT)
-        inverse = rb_ref[:, lanes]
-        for q in range(length // LANES):
-            cols = slice(q * LANES, (q + 1) * LANES)
-            ds[:, cols] = (e_ref[begin + h, :, cols].astype(F32) * inverse * d[:, cols]).astype(BF)
-        for u in range(UNITS):
-            at = pl.ds(multiple(where_ref[u] * rows, rows), rows)
-            slot(u)[0][pl.ds(multiple(h * rows, rows), rows), :] = ds[at, :]
-        return carry
-
-    lax.fori_loop(0, count, one_head, 0)
-
-
-def value_back(xh, rb, e, wv, tokens, size, cut):
+        (pltpu.VMEM((chunk, wide), BF),),
+    )
+
+
+def value_terms(xh_ref, rb_ref, e_ref, at, h):
+    lanes = slice(h * LANES, (h + 1) * LANES)
+    scaled = (xh_ref[:, lanes].astype(F32) * rb_ref[at, lanes]).astype(BF)
+    return mm(e_ref[h, at, :], scaled, TN)
+
+
+def value_first(xh, rb, e, size):
+    heads, length, _ = e.shape
+    at = slice(0, xh.shape[0])
+
+    def kernel(xh_ref, rb_ref, e_ref, out):
+        for h in range(heads):
+            out[:, h * size : (h + 1) * size] = value_terms(xh_ref, rb_ref, e_ref, at, h)[:, :size]
+
+    return run(kernel, "value_first", (), (xh, rb, e), (((length, heads * size), F32),))[0]
+
+
+def value_back(xh, first, rb, e, wv, tokens, size, cut):
     length, model = tokens.shape
     heads = e.shape[0]
     width = heads * size
     krows = model // UNITS
-
-    def kernel(xh_ref, rb_ref, e_ref, wv_ref, tok_ref, gv_ref, part_one, part_two, ga_ref, acc):
+    last = slice(length - xh.shape[0], length)
+
+    def kernel(xh_ref, first_ref, rb_ref, e_ref, wv_ref, tok_ref, gv_ref, part_one, part_two, ga_ref, acc):
         acc[...] = jnp.zeros_like(acc)
         for h in range(heads):
-            lanes = slice(h * LANES, (h + 1) * LANES)
-            scaled = (xh_ref[:, lanes].astype(F32) * rb_ref[:, lanes]).astype(BF)
-            gv_ref[:, h * size : (h + 1) * size] = mm(e_ref[h], scaled, TN)[:, :size].astype(BF)
+            cols = slice(h * size, (h + 1) * size)
+            term = value_terms(xh_ref, rb_ref, e_ref, last, h)[:, :size]
+            gv_ref[:, cols] = (first_ref[:, cols] + term).astype(BF)
 
         for at, part_ref in ((slice(0, cut), part_one), (slice(cut, length), part_two)):
             part = mm(gv_ref[at, :], wv_ref[...], NT)
@@ -736,7 +708,7 @@
         kernel,
         "value_back",
         (),
-        (xh, rb, e, wv, tokens),
+        (xh, first, rb, e, wv, tokens),
         (
             ((length, width), BF),
             ((cut, model), BF),
@@ -751,31 +723,47 @@
     return krows + 2 * (krows // 3)
 
 
-def mixer_grads(where, xh, va, e, rb, krows):
+def mixer_grads(where, xh, va, e, rb, krows, part, before):
     heads, length, _ = e.shape
     rows = length // UNITS
+    chunk = xh.shape[0]
+    owners = chunk // rows
+    at = slice(part * chunk, (part + 1) * chunk)
     deep = heads * rows + low_rows(krows)
 
     def kernel(where_ref, xh_ref, va_ref, e_ref, rb_ref, *rest):
-        outs, ds = rest[:-1], rest[-1]
-        score_grads(where_ref, xh_ref, va_ref, e_ref, rb_ref, ds, slots(outs, MIXER_FIRST, 1), 0, heads, rows)
+        outs, ds = rest[len(before) : -1], rest[-1]
+        slot = slots(outs, MIXER_FIRST, 1)
+
+        for h in range(heads):
+            lanes = slice(h * LANES, (h + 1) * LANES)
+            d = mm(xh_ref[:, lanes], va_ref[:, lanes], NT)
+            inverse = rb_ref[at, lanes]
+            for q in range(length // LANES):
+                cols = slice(q * LANES, (q + 1) * LANES)
+                ds[h, :, cols] = (e_ref[h, at, cols].astype(F32) * inverse * d[:, cols]).astype(BF)
         for u in range(UNITS):
-            for to in slots(outs, MIXER_FIRST, 1)(u):
-                to[heads * rows :, :] = jnp.zeros((low_rows(krows), length), BF)
+            owner = where_ref[u] - part * owners
+
+            @pl.when((owner >= 0) & (owner < owners))
+            def _(u=u, owner=owner):
+                some = pl.ds(multiple(owner * rows, rows), rows)
+                for h in range(heads):
+                    slot(u)[0][h * rows : (h + 1) * rows, :] = ds[h, some, :]
 
     return run(
         kernel,
         "mixer_grads",
         (where,),
-        (xh, va, e, rb),
+        (xh, va, e, rb, *before),
         slot_shapes(deep, length, MIXER_FIRST, 1, False),
-        (pltpu.VMEM((length, length), BF),),
-    )
-
-
-def weight_grads(where, parts, n1, gv, gat, mixed, ga, ga_other, gf):
+        (pltpu.VMEM((heads, chunk, length), BF),),
+        aliases={5 + n: n for n in range(len(before))},
+    )
+
+
+def weight_grads(where, parts, n1, gv, gats, mixed, ga, ga_other, gain):
     length = n1.shape[0]
-    chunk = mixed[0].shape[0]
     model = n1.shape[1]
     width = gv.shape[1]
     krows = model // UNITS
@@ -784,16 +772,16 @@
     lead, half, fold = length - width, length // 2, krows // 3
     assert width - lead == half
 
-    def kernel(where_ref, n1_ref, gv_ref, gat_ref, ga_ref, gb_ref, gf_ref, *rest):
-        mixed_refs, rest = rest[: len(mixed)], rest[len(mixed) :]
+    def kernel(where_ref, n1_ref, gv_ref, ga_ref, gb_ref, gain_ref, *rest):
+        gat_refs, mixed_refs, rest = rest[: len(mixed)], rest[len(mixed) : 2 * len(mixed)], rest[2 * len(mixed) :]
         slot = slots(rest[len(parts) : 2 * len(parts)], MIXER_FIRST, 1)
         wide, other, folded, pieces = rest[2 * len(parts) :]
         wide[:, :width] = mm(n1_ref[...], gv_ref[...], TN).astype(BF)
-        some = [mm(gat_ref[n * chunk : (n + 1) * chunk, :], one[...], TN) for n, one in enumerate(mixed_refs)]
+        some = [mm(gat_ref[...], one[...], TN) for gat_ref, one in zip(gat_refs, mixed_refs)]
         other[...] = sum(some).astype(BF)
         wide[:, width:] = other[:, :lead]
         pieces[0] = ga_ref[:UNITS, :] + gb_ref[:UNITS, :]
-        pieces[1] = gf_ref[...]
+        pieces[1] = cut_gain(jnp.sum(gain_ref[...], axis=0, keepdims=True), krows)
         sub = lax.broadcasted_iota(jnp.int32, (fold, LANES), 0)
         for d in range(UNITS):
             for n in range(3):
@@ -815,7 +803,7 @@
         kernel,
         "weight_grads",
         (where,),
-        (n1, gv, gat, ga, ga_other, gf, *mixed, *parts),
+        (n1, gv, ga, ga_other, gain, *gats, *mixed, *parts),
         slot_shapes(deep, length, MIXER_FIRST, 1, False),
         (
             pltpu.VMEM((model, length), BF),
@@ -823,7 +811,7 @@
             pltpu.VMEM((UNITS * 2 * fold, length), BF),
             pltpu.VMEM((2, UNITS, LANES), F32),
         ),
-        aliases={7 + len(mixed) + n: n for n in range(len(parts))},
+        aliases={6 + 2 * len(mixed) + n: n for n in range(len(parts))},
     )
 
 
@@ -1058,39 +1046,42 @@
     )
     mixed_other = [lax.ppermute(one, "mp", flip) for one in mixed]
     w, gact, mixf, rb, wo = second_weights(plan, where_in, second_at, cotangent, sums, units, shares, len(near), size)
-    backs, others, resids, n2s, acts, gpres = [], [], [], [], [], []
+    backs, others, resids, kept = [], [], [], []
     for part in range(PARTS):
-        *new, resid, n2, act, gpre = ffn_main(
-            second_at, tokens, mixed[part], mixed_other[part], gact, gains, w, part, PARTS, 1
+        back, resid, *kept = ffn_main(
+            second_at, tokens, mixed[part], mixed_other[part], gact, gains, w, part, PARTS, kept
         )
-        for back in new:
-            backs.append(back)
-            others.append(lax.ppermute(tie(back, *others[-1:]), "mp", flip))
+        backs.append(back)
+        others.append(lax.ppermute(tie(back, *others[-1:]), "mp", flip))
         resids.append(resid)
-        n2s.append(n2)
-        acts.append(act)
-        gpres.append(gpre)
-    parts_two = ffn_grads(where_out, n2s, gpres, acts, cotangent)
-    ffn_one, ffn_two = ffn_out(acts, w, 7 * length // 16)
+    n2, act, gpre = kept
+    parts_two = ffn_grads(where_out, n2, gpre, act, cotangent)
+    early = resid_back(backs[0], others[0], resids[0], cotangent, gains, wo, mixf, 0, heads, size, [])
+    ffn_one, ffn_two = ffn_out(tie(act, *early), w, 3 * length // 8)
     if ring:
         ffn_sum = Scatter(net, FFN_FIRST, 1, *parts_two)
         ffn_sum.swap_all(others[0], *ffn_sum.values())
         for step in range(2):
             ffn_sum.hop("down", far + step)
             ffn_sum.hop("up", far - 1 - step)
-            ffn_one, ffn_two = together([ffn_sum], ffn_one, ffn_two)
-    gres, gat, xh, gf = resid_back(
-        backs, others, resids, cotangent, gains, wo, mixf, heads, size
-    )
+            if step == 0:
+                ffn_one, ffn_two, *early = together([ffn_sum], ffn_one, ffn_two, *early)
+    first_values = value_first(early[2], rb, e, size)
+    parts_one = mixer_grads(where_out, early[2], va, e, rb, krows, 0, [])
+    cot_late = tie(cotangent, first_values, *parts_one)
+    final = resid_back(backs[1], others[1], resids[1], cot_late, gains, wo, mixf, 1, heads, size, early[3:])
+    gres, gats = (early[0], final[0]), (early[1], final[1])
+    xh = final[2]
     one_other = lax.ppermute(tie(ffn_one, xh), "mp", flip)
-    gv, part_one, part_two, ga = value_back(xh, rb, e, wv, tokens, size, length // 2)
+    gv, part_one, part_two, ga = value_back(xh, first_values, rb, e, wv, tokens, size, length // 2)
     ga_other = lax.ppermute(ga, "mp", flip)
     if ring:
+        together([ffn_sum])
         for step in range(2, far - 1):
             ffn_sum.hop("down", far + step)
             ffn_sum.hop("up", far - 1 - step)
-    parts_one = mixer_grads(where_out, xh, va, e, rb, krows)
-    parts_one = weight_grads(where_out, parts_one, n1, gv, gat, mixed, ga, ga_other, gf)
+    parts_one = mixer_grads(where_out, xh, va, e, rb, krows, 1, parts_one)
+    parts_one = weight_grads(where_out, parts_one, n1, gv, gats, mixed, ga, ga_other, final[3])
 
     top = heads * rows
     if ring:
@@ -1100,13 +1091,13 @@
         ffn_sum.hop("down", 2 * far - 1)
         score_sum.swap_all(value)
         two_other = lax.ppermute(ffn_two, "mp", flip)
-        part_one, part_two = together([ffn_sum, score_sum], part_one, part_two)
+        part_one, part_two = together([score_sum], part_one, part_two)
         for step in range(1, far):
             score_sum.hop("up", far - step)
             score_sum.hop("down", far + step)
             if step == 1:
                 part_other = [lax.ppermute(part_one, "mp", flip)]
-                two_other, part_two = together([score_sum], two_other, part_two)
+                two_other, part_two = together([ffn_sum, score_sum], two_other, part_two)
             elif step < far - 1:
                 part_other.append(lax.ppermute(part_two, "mp", flip))
                 (part_other[0],) = together([score_sum], part_other[0])
@@ -1159,7 +1150,7 @@
         inv = lax.rsqrt(jnp.mean(x * x, axis=-1, keepdims=True) + EPSILON)
         z = gains[0:1, :] * grad_n1
         hat = x * inv
-        backs.append((gres[at] + inv * (z - hat * jnp.mean(z * hat, axis=-1, keepdims=True))).astype(BF))
+        backs.append((gres[len(backs)] + inv * (z - hat * jnp.mean(z * hat, axis=-1, keepdims=True))).astype(BF))
     grad_tokens = jnp.concatenate(backs)
     return (
         output,

time: 155 us -> 152 us (0.981)
  waiting for transfers between devices: 70.2 us -> 65.6 us
    ppermute x14, waiting for transfers between devices: 22.7 us -> 14 us  [hop(): lax.ppermute(value, 'dp', self.ring.up if way == 'up' else self.ring.down)]
    ppermute x1, waiting for transfers between devices: 0.01 us -> 3.78 us  [shards(): two_other = lax.ppermute(ffn_two, 'mp', flip)]
    ppermute x2, waiting for transfers between devices: 2.58 us -> 0.01 us  [shards(): others.append(lax.ppermute(tie(back, *others[-1:]), 'mp', flip))]
    ppermute x1, waiting for transfers between devices: 1.57 us -> 3.46 us  [shards(): part_other.append(lax.ppermute(part_two, 'mp', flip))]
    pallas_call x16 -> x19, Pallas kernels: 36.4 us -> 37.3 us  [run(): pl.pallas_call(kernel, out_shape=tuple(results), in_specs=specs, out_spec...]
  transfers between devices with their start and end apart: 48 -> 48, of which waited for: 26 -> 26; matrix products, arithmetic and copies ran while one was open for 4% -> 4% of each run, Pallas kernels for 20% -> 21%
where the time goes in v6:
time: 152 us
  waiting for transfers between devices  65.6 us (43%)
  starting transfers between devices  40.4 us (27%)
  Pallas kernels  37.3 us (25%)
  other arithmetic  5.72 us (4%)
    pallas_call x19, Pallas kernels, run(): pl.pallas_call(kernel, out_shape=tuple(results), in_specs=specs, out_spec...  37.3 us
    ppermute x4, waiting for transfers between devices, hop(): lax.ppermute(up, 'dp', ring.up)  24.4 us
    ppermute x14, starting transfers between devices, hop(): lax.ppermute(value, 'dp', self.ring.up if way == 'up' else self.ring.down)  14.7 us
    ppermute x14, waiting for transfers between devices, hop(): lax.ppermute(value, 'dp', self.ring.up if way == 'up' else self.ring.down)  14 us
    ppermute x2, waiting for transfers between devices, shards(): wo_next = [lax.ppermute(wo_other, 'dp', way) for way in (net.up, net.down)]  9.06 us
    ppermute x4, starting transfers between devices, hop(): lax.ppermute(up, 'dp', ring.up)  7.91 us
    ppermute x1, waiting for transfers between devices, shards(): two_other = lax.ppermute(ffn_two, 'mp', flip)  3.78 us
    ppermute x1, waiting for transfers between devices, shards(): part_other.append(lax.ppermute(part_two, 'mp', flip))  3.46 us
  transfers between devices with their start and end apart: 48, of which 26 were waited for; matrix products, arithmetic and copies ran while one was open for 4% of the time, Pallas kernels for 21%

profile of v6, /device:TPU:0, one launch (start us, length us, event | category | flops | bytes accessed | tf_op | source)
XLA Modules:
  0.0 151.7 jit_solution(7494837365370325615)
XLA Ops:
  0.6 1.4 pack_unit.1
  2.0 3.1 %collective-permute-start = (bf16[592,512]{1,0:T(8,128)(2,1)S(1)}, bf16[592,512]{1,0:T(8,128)(2,1)S(1)}, u32[]{:S(2)}, u32[]{:S(2)}) collective-permute-start(bf16[592,512]{1,0:T(8,128)(2,1)S(1)} %get-tuple-element.122.rest_0_), channel_id=1, source_target_pairs={{0,8},{2,10},{8,16},{10,18},{16,24},{18,26},{24,28},{26,30},{28,20... | collective-permute-start | bytes 1818632 | tf_op jit(solution)/shard_map/ppermute | solution.py:880
  5.1 0.7 broadcast_add_fusion.3
  6.0 2.0 %collective-permute-start.2 = (bf16[48,384]{1,0:T(8,128)(2,1)S(1)}, bf16[48,384]{1,0:T(8,128)(2,1)S(1)}, u32[]{:S(2)}, u32[]{:S(2)}) collective-permute-start(bf16[48,384]{1,0:T(8,128)(2,1)S(1)} %get-tuple-element.124), channel_id=1, source_target_pairs={{0,1},{1,0},{2,3},{3,2},{4,5},{5,4},{6,7},{7,6},{8,9},{9,8},{10,11... | collective-permute-start | bytes 110600 | tf_op jit(solution)/shard_map/ppermute | solution.py:992
  8.0 2.0 %collective-permute-done.2.rest_1_ = bf16[48,384]{1,0:T(8,128)(2,1)S(1)} collective-permute-done((bf16[48,384]{1,0:T(8,128)(2,1)S(1)}, bf16[48,384]{1,0:T(8,128)(2,1)S(1)}, u32[]{:S(2)}, u32[]{:S(2)}) %collective-permute-start.2) | collective-permute-done | bytes 36896 | tf_op jit(solution)/shard_map/ppermute | solution.py:992
  10.0 2.0 %collective-permute-start.3 = (bf16[48,384]{1,0:T(8,128)(2,1)S(1)}, bf16[48,384]{1,0:T(8,128)(2,1)S(1)}, u32[]{:S(2)}, u32[]{:S(2)}) collective-permute-start(bf16[48,384]{1,0:T(8,128)(2,1)S(1)} %collective-permute-done.2.rest_1_), channel_id=1, source_target_pairs={{0,8},{2,10},{8,16},{10,18},{16,24},{18,26},{24,28},{26,30},{28,20... | collective-permute-start | bytes 110600 | tf_op jit(solution)/shard_map/ppermute | solution.py:993
  12.0 7.5 %collective-permute-done.3.rest_2_ = bf16[48,384]{1,0:T(8,128)(2,1)S(1)} collective-permute-done((bf16[48,384]{1,0:T(8,128)(2,1)S(1)}, bf16[48,384]{1,0:T(8,128)(2,1)S(1)}, u32[]{:S(2)}, u32[]{:S(2)}) %collective-permute-start.3) | collective-permute-done | bytes 36896 | tf_op jit(solution)/shard_map/ppermute | solution.py:993
  19.5 1.5 %collective-permute-done.4.rest_3_ = bf16[48,384]{1,0:T(8,128)(2,1)S(1)} collective-permute-done((bf16[48,384]{1,0:T(8,128)(2,1)S(1)}, bf16[48,384]{1,0:T(8,128)(2,1)S(1)}, u32[]{:S(2)}, u32[]{:S(2)}) %collective-permute-start.4) | collective-permute-done | bytes 36896 | tf_op jit(solution)/shard_map/ppermute | solution.py:993
  21.1 1.6 %collective-permute-start.5 = (bf16[592,512]{1,0:T(8,128)(2,1)S(1)}, bf16[592,512]{1,0:T(8,128)(2,1)S(1)}, u32[]{:S(2)}, u32[]{:S(2)}) collective-permute-start(bf16[592,512]{1,0:T(8,128)(2,1)S(1)} %get-tuple-element.129.rest_1_), channel_id=1, source_target_pairs={{0,8},{2,10},{8,16},{10,18},{16,24},{18,26},{24,28},{26,30},{28,20... | collective-permute-start | bytes 1818632 | tf_op jit(solution)/shard_map/ppermute | solution.py:880
  23.2 12.2 %collective-permute-done.5.rest_3_ = bf16[592,512]{1,0:T(8,128)(2,1)S(1)} collective-permute-done((bf16[592,512]{1,0:T(8,128)(2,1)S(1)}, bf16[592,512]{1,0:T(8,128)(2,1)S(1)}, u32[]{:S(2)}, u32[]{:S(2)}) %collective-permute-start.5) | collective-permute-done | bytes 606240 | tf_op jit(solution)/shard_map/ppermute | solution.py:880
  35.4 1.3 collective-permute-done.6.rest_4_
  36.7 1.6 %collective-permute-start.7 = (bf16[592,512]{1,0:T(8,128)(2,1)S(1)}, bf16[592,512]{1,0:T(8,128)(2,1)S(1)}, u32[]{:S(2)}, u32[]{:S(2)}) collective-permute-start(bf16[592,512]{1,0:T(8,128)(2,1)S(1)} %collective-permute-done.5.rest_3_), channel_id=1, source_target_pairs={{0,8},{2,10},{8,16},{10,18},{16,24},{18,26},{24,28},{26,30},{28,20... | collective-permute-start | bytes 1818632 | tf_op jit(solution)/shard_map/ppermute | solution.py:880
  39.3 10.4 %collective-permute-done.7.rest_0_.rest_10_ = bf16[592,512]{1,0:T(8,128)(2,1)S(1)} collective-permute-done((bf16[592,512]{1,0:T(8,128)(2,1)S(1)}, bf16[592,512]{1,0:T(8,128)(2,1)S(1)}, u32[]{:S(2)}, u32[]{:S(2)}) %collective-permute-start.7) | collective-permute-done | bytes 606240 | tf_op jit(solution)/shard_map/ppermute | solution.py:880
  49.7 1.3 collective-permute-done.8.rest_1_.rest_11_
  51.6 1.6 %collective-permute-start.9 = (bf16[288,512]{1,0:T(8,128)(2,1)S(1)}, bf16[288,512]{1,0:T(8,128)(2,1)S(1)}, u32[]{:S(2)}, u32[]{:S(2)}) collective-permute-start(bf16[288,512]{1,0:T(8,128)(2,1)S(1)} %slice.97), channel_id=1, source_target_pairs={{0,8},{2,10},{8,16},{10,18},{16,24},{18,26},{24,28},{26,30},{28,20... | collective-permute-start | bytes 884744 | tf_op jit(solution)/shard_map/ppermute | solution.py:880
  54.3 0.9 copy-done.12
  55.1 3.8 %mixer_first.1 = (bf16[6,512,512]{2,1,0:T(8,128)(2,1)S(1)}, bf16[768,384]{1,0:T(8,128)(2,1)S(1)}, bf16[16,16,128]{2,1,0:T(8,128)(2,1)S(1)}, f32[512,768]{1,0:T(8,128)S(1)}) custom-call(s32[16]{0:T(128)S(1)} %pad_add_fusion.where_ref, bf16[512,768]{1,0:T(8,128)(2,1)S(1)} %copy-done, s32[1,512]{1,0:T(1,128)S(1)} %copy-done.5, bf16[592,512]{1,0:T(8,128)(2,1)} %copy-done.2, ...), custom_call_target="tpu_custom_call" | custom-call | flops 1 | bytes 1 | tf_op jit(solution)/shard_map/mixer_first/pallas_call | solution.py:36
  58.9 1.8 %collective-permute-done.9.rest_2_.rest_12_ = bf16[288,512]{1,0:T(8,128)(2,1)S(1)} collective-permute-done((bf16[288,512]{1,0:T(8,128)(2,1)S(1)}, bf16[288,512]{1,0:T(8,128)(2,1)S(1)}, u32[]{:S(2)}, u32[]{:S(2)}) %collective-permute-start.9) | collective-permute-done | bytes 294944 | tf_op jit(solution)/shard_map/ppermute | solution.py:880
  61.4 1.5 collective-permute-done.18.rest_6_.rest_16_
  62.9 3.3 %mixer_forward.1 = (bf16[6,512,512]{2,1,0:T(8,128)(2,1)S(1)}, bf16[768,384]{1,0:T(8,128)(2,1)S(1)}, bf16[16,16,128]{2,1,0:T(8,128)(2,1)S(1)}, bf16[512,768]{1,0:...) custom-call(s32[16]{0:T(128)S(1)} %pad_add_fusion.where_ref, ...), custom_call_target="tpu_custom_call", output_to_operand_aliasing={{0}: (2, {}), {1}: (3, {}), {2}: (4, {})} | custom-call | flops 1 | bytes 1 | tf_op jit(solution)/shard_map/mixer_forward/pallas_call | solution.py:36
  66.2 1.6 %collective-permute-start.20 = (bf16[256,384]{1,0:T(8,128)(2,1)S(1)}, bf16[256,384]{1,0:T(8,128)(2,1)S(1)}, u32[]{:S(2)}, u32[]{:S(2)}) collective-permute-start(bf16[256,384]{1,0:T(8,128)(2,1)S(1)} %get-tuple-element.145.own_ref.rest_2_), channel_id=1, source_target_pairs={{0,1},{1,0},{2,3},{3,2},{4,5},{5,4},{6,7},{7,6},{8,9},{9,8},{10,11... | collective-permute-start | bytes 589832 | tf_op jit(solution)/shard_map/ppermute | solution.py:1047
  68.3 5.8 %second_weights.1 = (bf16[768,3840]{1,0:T(8,128)(2,1)S(1)}, f32[512,1536]{1,0:T(8,128)S(1)}, f32[512,768]{1,0:T(8,128)S(1)}, f32[512,768]{1,0:T(8,128)S(1)}, bf16[768,768]{1,0:T(8,128)(2,1)S(1)}) custom-call(s32[16]{0:T(128)S(1)} %pad_add_fusion.where_ref, s32[1]{0:T(128)} %bitcast.second_ref, bf16[512,768]{1,0:T(8,128)(2,1)S(1)} %copy-done.1, ...), custom_call_target="tpu_custom_call" | custom-call | flops 1 | bytes 1 | tf_op jit(solution)/shard_map/second_weights/pallas_call | solution.py:36
  74.1 3.1 %ffn_main.2 = (bf16[256,768]{1,0:T(8,128)(2,1)S(1)}, f32[256,768]{1,0:T(8,128)S(1)}, bf16[512,768]{1,0:T(8,128)(2,1)S(1)}, bf16[512,1536]{1,0:T(8,128)(2,1)S(1)}, bf16[512,1536]{1,0:T(8,128)(2,1)S(1)}) custom-call(s32[1]{0:T(128)} %bitcast.second_ref, bf16[512,768]{1,0:T(8,128)(2,1)S(1)} %copy-done, bf16[256,384]{1,0:T(8,128)(2,1)S(1)} %get-tuple-element.145.own_ref.rest_2_, ...), custom_call_target="tpu_custom_call" | custom-call | flops 1 | bytes 1 | tf_op jit(solution)/shard_map/ffn_main/pallas_call | solution.py:36
  77.1 1.6 %collective-permute-start.26 = (bf16[256,768]{1,0:T(8,128)(2,1)S(1)}, bf16[256,768]{1,0:T(8,128)(2,1)S(1)}, u32[]{:S(2)}, u32[]{:S(2)}) collective-permute-start(bf16[256,768]{1,0:T(8,128)(2,1)S(1)} %get-tuple-element.164.back_ref), channel_id=1, source_target_pairs={{0,1},{1,0},{2,3},{3,2},{4,5},{5,4},{6,7},{7,6},{8,9},{9,8},{10,11... | collective-permute-start | bytes 1179656 | tf_op jit(solution)/shard_map/ppermute | solution.py:1055
  78.7 3.1 %ffn_main.3 = (bf16[256,768]{1,0:T(8,128)(2,1)S(1)}, f32[256,768]{1,0:T(8,128)S(1)}, bf16[512,768]{1,0:T(8,128)(2,1)S(1)}, bf16[512,1536]{1,0:T(8,128)(2,1)S(1)}, bf16[512,1536]{1,0:T(8,128)(2,1)S(1)}) custom-call(s32[1]{0:T(128)} %bitcast.second_ref, bf16[512,768]{1,0:T(8,128)(2,1)S(1)} %copy-done, ...), custom_call_target="tpu_custom_call", output_to_operand_aliasing={{2}: (7, {}), {3}: (8, {}), {4}: (9, {})} | custom-call | flops 1 | bytes 1 | tf_op jit(solution)/shard_map/ffn_main/pallas_call | solution.py:36
  81.8 4.6 %ffn_grads.1 = (bf16[8,48,3072]{2,1,0:T(8,128)(2,1)S(1)}, bf16[48,3072]{1,0:T(8,128)(2,1)S(1)}, bf16[48,3072]{1,0:T(8,128)(2,1)S(1)}, bf16[6,48,3072]{2,1,0:T(8,128)(2,1)S(1)}) custom-call(s32[16]{0:T(128)S(1)} %pad_add_fusion.1.where_ref, bf16[512,768]{1,0:T(8,128)(2,1)S(1)} %copy-done.1, bf16[512,768]{1,0:T(8,128)(2,1)S(1)} %get-tuple-element.156.n2_ref, ...), custom_call_target="tpu_custom_call" | custom-call | flops 1 | bytes 1 | tf_op jit(solution)/shard_map/ffn_grads/pallas_call | solution.py:36
  87.0 1.1 collective-permute-done.22
  89.3 1.6 %collective-permute-start.25 = (bf16[48,3072]{1,0:T(8,128)(2,1)S(1)}, bf16[48,3072]{1,0:T(8,128)(2,1)S(1)}, u32[]{:S(2)}, u32[]{:S(2)}) collective-permute-start(bf16[48,3072]{1,0:T(8,128)(2,1)S(1)} %get-tuple-element.249), channel_id=1, source_target_pairs={{0,8},{2,10},{8,16},{10,18},{16,24},{18,26},{24,28},{26,30},{28,20... | collective-permute-start | bytes 884744 | tf_op jit(solution)/shard_map/ppermute | solution.py:934
  90.9 0.7 collective-permute-start.32
  91.6 1.1 resid_back.2
  92.7 1.7 %ffn_out.1 = (bf16[192,768]{1,0:T(8,128)(2,1)S(1)}, bf16[320,768]{1,0:T(8,128)(2,1)S(1)}) custom-call(bf16[512,1536]{1,0:T(8,128)(2,1)S(1)} %get-tuple-element.169.act_ref, bf16[768,3840]{1,0:T(8,128)(2,1)S(1)} %get-tuple-element.149.w_ref), custom_call_target="tpu_custom_call" | custom-call | flops 1 | bytes 1 | tf_op jit(solution)/shard_map/ffn_out/pallas_call | solution.py:36
  94.4 3.8 %collective-permute-done.23 = bf16[48,3072]{1,0:T(8,128)(2,1)S(1)} collective-permute-done((bf16[48,3072]{1,0:T(8,128)(2,1)S(1)}, bf16[48,3072]{1,0:T(8,128)(2,1)S(1)}, u32[]{:S(2)}, u32[]{:S(2)}) %collective-permute-start.23) | collective-permute-done | bytes 294944 | tf_op jit(solution)/shard_map/ppermute | solution.py:934
  98.5 0.8 collective-permute-start.28
  99.3 1.3 collective-permute-start.29
  100.6 0.7 value_first.1.first_ref
  101.3 1.4 mixer_grads.2
  102.7 1.1 resid_back.3
  103.8 0.9 collective-permute-start.35
  104.7 1.4 value_back.1
  106.2 1.3 collective-permute-start.33
  107.6 1.4 collective-permute-start.30
  109.1 0.7 collective-permute-start.31
  109.7 1.4 mixer_grads.3
  111.1 1.3 collective-permute-done.33.gb_ref
  112.4 1.7 %weight_grads.1 = (bf16[8,272,512]{2,1,0:T(8,128)(2,1)S(1)}, bf16[272,512]{1,0:T(8,128)(2,1)S(1)}, bf16[7,272,512]{2,1,0:T(8,128)(2,1)S(1)}) custom-call(s32[16]{0:T(128)S(1)} %pad_add_fusion.1.where_ref, bf16[512,768]{1,0:T(8,128)(2,1)S(1)} %get-tuple-element.179.n1_ref, ...), custom_call_target="tpu_custom_call", output_to_operand_aliasing={{0}: (10, {}), {1}: (11, {}), {2}: (12, {})} | custom-call | flops 1 | bytes 1 | tf_op jit(solution)/shard_map/weight_grads/pallas_call | solution.py:36
  114.2 1.5 %collective-permute-done.34 = bf16[272,512]{1,0:T(8,128)(2,1)S(1)} collective-permute-done((bf16[272,512]{1,0:T(8,128)(2,1)S(1)}, bf16[272,512]{1,0:T(8,128)(2,1)S(1)}, u32[]{:S(2)}, u32[]{:S(2)}) %collective-permute-start.34) | collective-permute-done | bytes 278560 | tf_op jit(solution)/shard_map/ppermute | solution.py:906
  116.3 1.5 %collective-permute-start.38 = (bf16[272,512]{1,0:T(8,128)(2,1)S(1)}, bf16[272,512]{1,0:T(8,128)(2,1)S(1)}, u32[]{:S(2)}, u32[]{:S(2)}) collective-permute-start(bf16[272,512]{1,0:T(8,128)(2,1)S(1)} %fusion.24), channel_id=1, source_target_pairs={{0,8},{2,10},{8,16},{10,18},{16,24},{18,26},{24,28},{26,30},{28,20... | collective-permute-start | bytes 835592 | tf_op jit(solution)/shard_map/ppermute | solution.py:934
  118.5 1.1 collective-permute-start.41
  119.6 5.8 %collective-permute-done.38 = bf16[272,512]{1,0:T(8,128)(2,1)S(1)} collective-permute-done((bf16[272,512]{1,0:T(8,128)(2,1)S(1)}, bf16[272,512]{1,0:T(8,128)(2,1)S(1)}, u32[]{:S(2)}, u32[]{:S(2)}) %collective-permute-start.38) | collective-permute-done | bytes 278560 | tf_op jit(solution)/shard_map/ppermute | solution.py:934
  125.4 1.6 %collective-permute-start.40 = (bf16[272,512]{1,0:T(8,128)(2,1)S(1)}, bf16[272,512]{1,0:T(8,128)(2,1)S(1)}, u32[]{:S(2)}, u32[]{:S(2)}) collective-permute-start(bf16[272,512]{1,0:T(8,128)(2,1)S(1)} %fusion.30), channel_id=1, source_target_pairs={{0,4},{2,6},{8,0},{10,2},{16,8},{18,10},{24,16},{26,18},{28,24},{3... | collective-permute-start | bytes 835592 | tf_op jit(solution)/shard_map/ppermute | solution.py:934
  127.7 1.2 collective-permute-start.44
  128.8 3.8 %collective-permute-done.41 = bf16[320,768]{1,0:T(8,128)(2,1)S(1)} collective-permute-done((bf16[320,768]{1,0:T(8,128)(2,1)S(1)}, bf16[320,768]{1,0:T(8,128)(2,1)S(1)}, u32[]{:S(2)}, u32[]{:S(2)}) %collective-permute-start.41) | collective-permute-done | bytes 491552 | tf_op jit(solution)/shard_map/ppermute | solution.py:1093
  132.6 1.1 collective-permute-done.40
  133.7 1.5 collective-permute-done.39
  135.9 1.6 %collective-permute-start.43 = (bf16[272,512]{1,0:T(8,128)(2,1)S(1)}, bf16[272,512]{1,0:T(8,128)(2,1)S(1)}, u32[]{:S(2)}, u32[]{:S(2)}) collective-permute-start(bf16[272,512]{1,0:T(8,128)(2,1)S(1)} %get-tuple-element.243), channel_id=1, source_target_pairs={{0,4},{2,6},{8,0},{10,2},{16,8},{18,10},{24,16},{26,18},{28,24},{3... | collective-permute-start | bytes 835592 | tf_op jit(solution)/shard_map/ppermute | solution.py:934
  137.5 1.2 collective-permute-start.45
  138.7 0.9 ffn_result.1
  139.6 1.2 fusion
  141.0 1.5 collective-permute-done.42
  142.8 1.2 collective-permute-start.46
  144.1 0.9 collective-permute-start.47
  144.9 3.5 %collective-permute-done.45 = bf16[256,768]{1,0:T(8,128)(2,1)S(1)} collective-permute-done((bf16[256,768]{1,0:T(8,128)(2,1)S(1)}, bf16[256,768]{1,0:T(8,128)(2,1)S(1)}, u32[]{:S(2)}, u32[]{:S(2)}) %collective-permute-start.45) | collective-permute-done | bytes 393248 | tf_op jit(solution)/shard_map/ppermute | solution.py:1102
  149.5 0.9 pad_maximum_fusion
  150.6 0.9 mixer_result.1
  (104 shorter events, 11.3 us)
Async XLA Ops:
  2.0 19.0 %collective-permute-start = (bf16[592,512]{1,0:T(8,128)(2,1)S(1)}, bf16[592,512]{1,0:T(8,128)(2,1)S(1)}, u32[]{:S(2)}, u32[]{:S(2)}) collective-permute-start(bf16[592,512]{1,0:T(8,128)(2,1)S(1)} %get-tuple-element.122.rest_0_), channel_id=1, source_target_pairs={{0,8},{2,10},{8,16},{10,18},{16,24},{18,26},{24,28},{26,30},{28,20... | collective-permute-start | bytes 1818632 | tf_op jit(solution)/shard_map/ppermute | solution.py:880
  5.1 15.9 %collective-permute-start.1 = (bf16[592,512]{1,0:T(8,128)(2,1)S(1)}, bf16[592,512]{1,0:T(8,128)(2,1)S(1)}, u32[]{:S(2)}, u32[]{:S(2)}) collective-permute-start(bf16[592,512]{1,0:T(8,128)(2,1)S(1)} %get-tuple-element.122.rest_0_), channel_id=1, source_target_pairs={{0,4},{2,6},{8,0},{10,2},{16,8},{18,10},{24,16},{26,18},{28,24},{3... | collective-permute-start | bytes 1818632 | tf_op jit(solution)/shard_map/ppermute | solution.py:880
  6.0 49.2 %copy-start = (bf16[512,768]{1,0:T(8,128)(2,1)S(1)}, bf16[512,768]{1,0:T(8,128)(2,1)}, u32[]{:S(2)}) copy-start(bf16[512,768]{1,0:T(8,128)(2,1)} %tok_ref.7) | copy-start | bytes 2359300
  6.0 49.2 %copy-start.5 = (s32[1,512]{1,0:T(1,128)S(1)}, s32[1,512]{1,0:T(1,128)}, u32[]{:S(2)}) copy-start(s32[1,512]{1,0:T(1,128)} %seg_ref.3) | copy-start | bytes 6148
  6.0 4.0 %collective-permute-start.2 = (bf16[48,384]{1,0:T(8,128)(2,1)S(1)}, bf16[48,384]{1,0:T(8,128)(2,1)S(1)}, u32[]{:S(2)}, u32[]{:S(2)}) collective-permute-start(bf16[48,384]{1,0:T(8,128)(2,1)S(1)} %get-tuple-element.124), channel_id=1, source_target_pairs={{0,1},{1,0},{2,3},{3,2},{4,5},{5,4},{6,7},{7,6},{8,9},{9,8},{10,11... | collective-permute-start | bytes 110600 | tf_op jit(solution)/shard_map/ppermute | solution.py:992
  10.0 9.5 %collective-permute-start.3 = (bf16[48,384]{1,0:T(8,128)(2,1)S(1)}, bf16[48,384]{1,0:T(8,128)(2,1)S(1)}, u32[]{:S(2)}, u32[]{:S(2)}) collective-permute-start(bf16[48,384]{1,0:T(8,128)(2,1)S(1)} %collective-permute-done.2.rest_1_), channel_id=1, source_target_pairs={{0,8},{2,10},{8,16},{10,18},{16,24},{18,26},{24,28},{26,30},{28,20... | collective-permute-start | bytes 110600 | tf_op jit(solution)/shard_map/ppermute | solution.py:993
  12.0 9.1 %collective-permute-start.4 = (bf16[48,384]{1,0:T(8,128)(2,1)S(1)}, bf16[48,384]{1,0:T(8,128)(2,1)S(1)}, u32[]{:S(2)}, u32[]{:S(2)}) collective-permute-start(bf16[48,384]{1,0:T(8,128)(2,1)S(1)} %collective-permute-done.2.rest_1_), channel_id=1, source_target_pairs={{0,4},{2,6},{8,0},{10,2},{16,8},{18,10},{24,16},{26,18},{28,24},{3... | collective-permute-start | bytes 110600 | tf_op jit(solution)/shard_map/ppermute | solution.py:993
  21.1 32.7 %copy-start.3 = (bf16[592,512]{1,0:T(8,128)(2,1)}, bf16[592,512]{1,0:T(8,128)(2,1)S(1)}, u32[]{:S(2)}) copy-start(bf16[592,512]{1,0:T(8,128)(2,1)S(1)} %get-tuple-element.129.rest_1_) | copy-start | bytes 1818628
  21.1 32.7 %copy-start.4 = (bf16[592,512]{1,0:T(8,128)(2,1)}, bf16[592,512]{1,0:T(8,128)(2,1)S(1)}, u32[]{:S(2)}) copy-start(bf16[592,512]{1,0:T(8,128)(2,1)S(1)} %get-tuple-element.130.rest_2_) | copy-start | bytes 1818628
  21.1 14.3 %collective-permute-start.5 = (bf16[592,512]{1,0:T(8,128)(2,1)S(1)}, bf16[592,512]{1,0:T(8,128)(2,1)S(1)}, u32[]{:S(2)}, u32[]{:S(2)}) collective-permute-start(bf16[592,512]{1,0:T(8,128)(2,1)S(1)} %get-tuple-element.129.rest_1_), channel_id=1, source_target_pairs={{0,8},{2,10},{8,16},{10,18},{16,24},{18,26},{24,28},{26,30},{28,20... | collective-permute-start | bytes 1818632 | tf_op jit(solution)/shard_map/ppermute | solution.py:880
  22.7 13.9 %collective-permute-start.6 = (bf16[592,512]{1,0:T(8,128)(2,1)S(1)}, bf16[592,512]{1,0:T(8,128)(2,1)S(1)}, u32[]{:S(2)}, u32[]{:S(2)}) collective-permute-start(bf16[592,512]{1,0:T(8,128)(2,1)S(1)} %get-tuple-element.130.rest_2_), channel_id=1, source_target_pairs={{0,4},{2,6},{8,0},{10,2},{16,8},{18,10},{24,16},{26,18},{28,24},{3... | collective-permute-start | bytes 1818632 | tf_op jit(solution)/shard_map/ppermute | solution.py:880
  35.4 18.4 %copy-start.6 = (bf16[592,512]{1,0:T(8,128)(2,1)}, bf16[592,512]{1,0:T(8,128)(2,1)S(1)}, u32[]{:S(2)}) copy-start(bf16[592,512]{1,0:T(8,128)(2,1)S(1)} %collective-permute-done.5.rest_3_) | copy-start | bytes 1818628
  36.7 17.1 %copy-start.7 = (bf16[592,512]{1,0:T(8,128)(2,1)}, bf16[592,512]{1,0:T(8,128)(2,1)S(1)}, u32[]{:S(2)}) copy-start(bf16[592,512]{1,0:T(8,128)(2,1)S(1)} %collective-permute-done.6.rest_4_) | copy-start | bytes 1818628
  36.7 13.0 %collective-permute-start.7 = (bf16[592,512]{1,0:T(8,128)(2,1)S(1)}, bf16[592,512]{1,0:T(8,128)(2,1)S(1)}, u32[]{:S(2)}, u32[]{:S(2)}) collective-permute-start(bf16[592,512]{1,0:T(8,128)(2,1)S(1)} %collective-permute-done.5.rest_3_), channel_id=1, source_target_pairs={{0,8},{2,10},{8,16},{10,18},{16,24},{18,26},{24,28},{26,30},{28,20... | collective-permute-start | bytes 1818632 | tf_op jit(solution)/shard_map/ppermute | solution.py:880
  38.2 12.7 %collective-permute-start.8 = (bf16[592,512]{1,0:T(8,128)(2,1)S(1)}, bf16[592,512]{1,0:T(8,128)(2,1)S(1)}, u32[]{:S(2)}, u32[]{:S(2)}) collective-permute-start(bf16[592,512]{1,0:T(8,128)(2,1)S(1)} %collective-permute-done.6.rest_4_), channel_id=1, source_target_pairs={{0,4},{2,6},{8,0},{10,2},{16,8},{18,10},{24,16},{26,18},{28,24},{3... | collective-permute-start | bytes 1818632 | tf_op jit(solution)/shard_map/ppermute | solution.py:880
  38.7 12.3 %collective-permute-start.12 = (bf16[592,512]{1,0:T(8,128)(2,1)S(1)}, bf16[592,512]{1,0:T(8,128)(2,1)S(1)}, u32[]{:S(2)}, u32[]{:S(2)}) collective-permute-start(bf16[592,512]{1,0:T(8,128)(2,1)S(1)} %get-tuple-element.129.rest_1_), channel_id=1, source_target_pairs={{0,2},{2,0},{4,6},{6,4},{8,10},{10,8},{12,14},{14,12},{16,18},{18,... | collective-permute-start | bytes 1818632 | tf_op jit(solution)/shard_map/ppermute | solution.py:886
  38.7 12.9 %collective-permute-start.13 = (bf16[592,512]{1,0:T(8,128)(2,1)S(1)}, bf16[592,512]{1,0:T(8,128)(2,1)S(1)}, u32[]{:S(2)}, u32[]{:S(2)}) collective-permute-start(bf16[592,512]{1,0:T(8,128)(2,1)S(1)} %get-tuple-element.130.rest_2_), channel_id=1, source_target_pairs={{0,2},{2,0},{4,6},{6,4},{8,10},{10,8},{12,14},{14,12},{16,18},{18,... | collective-permute-start | bytes 1818632 | tf_op jit(solution)/shard_map/ppermute | solution.py:886
  39.2 14.6 %copy-start.2 = (bf16[592,512]{1,0:T(8,128)(2,1)}, bf16[592,512]{1,0:T(8,128)(2,1)S(1)}, u32[]{:S(2)}) copy-start(bf16[592,512]{1,0:T(8,128)(2,1)S(1)} %fill_units.3.rest_0_) | copy-start | bytes 1818628
  39.2 14.0 %collective-permute-start.11 = (bf16[592,512]{1,0:T(8,128)(2,1)S(1)}, bf16[592,512]{1,0:T(8,128)(2,1)S(1)}, u32[]{:S(2)}, u32[]{:S(2)}) collective-permute-start(bf16[592,512]{1,0:T(8,128)(2,1)S(1)} %fill_units.3.rest_0_), channel_id=1, source_target_pairs={{0,2},{2,0},{4,6},{6,4},{8,10},{10,8},{12,14},{14,12},{16,18},{18,... | collective-permute-start | bytes 1818632 | tf_op jit(solution)/shard_map/ppermute | solution.py:886
  49.7 3.5 %collective-permute-start.14 = (bf16[592,512]{1,0:T(8,128)(2,1)S(1)}, bf16[592,512]{1,0:T(8,128)(2,1)S(1)}, u32[]{:S(2)}, u32[]{:S(2)}) collective-permute-start(bf16[592,512]{1,0:T(8,128)(2,1)S(1)} %collective-permute-done.5.rest_3_), channel_id=1, source_target_pairs={{0,2},{2,0},{4,6},{6,4},{8,10},{10,8},{12,14},{14,12},{16,18},{18,... | collective-permute-start | bytes 1818632 | tf_op jit(solution)/shard_map/ppermute | solution.py:886
  51.0 2.7 %collective-permute-start.15 = (bf16[592,512]{1,0:T(8,128)(2,1)S(1)}, bf16[592,512]{1,0:T(8,128)(2,1)S(1)}, u32[]{:S(2)}, u32[]{:S(2)}) collective-permute-start(bf16[592,512]{1,0:T(8,128)(2,1)S(1)} %collective-permute-done.6.rest_4_), channel_id=1, source_target_pairs={{0,2},{2,0},{4,6},{6,4},{8,10},{10,8},{12,14},{14,12},{16,18},{18,... | collective-permute-start | bytes 1818632 | tf_op jit(solution)/shard_map/ppermute | solution.py:886
  51.0 2.8 %copy-start.8 = (bf16[592,512]{1,0:T(8,128)(2,1)}, bf16[592,512]{1,0:T(8,128)(2,1)S(1)}, u32[]{:S(2)}) copy-start(bf16[592,512]{1,0:T(8,128)(2,1)S(1)} %collective-permute-done.12.rest_6_) | copy-start | bytes 1818628
  51.0 9.8 %collective-permute-start.10 = (bf16[304,512]{1,0:T(8,128)(2,1)S(1)}, bf16[304,512]{1,0:T(8,128)(2,1)S(1)}, u32[]{:S(2)}, u32[]{:S(2)}) collective-permute-start(bf16[304,512]{1,0:T(8,128)(2,1)S(1)} %slice.98), channel_id=1, source_target_pairs={{0,4},{2,6},{8,0},{10,2},{16,8},{18,10},{24,16},{26,18},{28,24},{3... | collective-permute-start | bytes 933896 | tf_op jit(solution)/shard_map/ppermute | solution.py:880
  51.6 2.2 %copy-start.9 = (bf16[592,512]{1,0:T(8,128)(2,1)}, bf16[592,512]{1,0:T(8,128)(2,1)S(1)}, u32[]{:S(2)}) copy-start(bf16[592,512]{1,0:T(8,128)(2,1)S(1)} %collective-permute-done.13.rest_7_) | copy-start | bytes 1818628
  51.6 9.2 %collective-permute-start.9 = (bf16[288,512]{1,0:T(8,128)(2,1)S(1)}, bf16[288,512]{1,0:T(8,128)(2,1)S(1)}, u32[]{:S(2)}, u32[]{:S(2)}) collective-permute-start(bf16[288,512]{1,0:T(8,128)(2,1)S(1)} %slice.97), channel_id=1, source_target_pairs={{0,8},{2,10},{8,16},{10,18},{16,24},{18,26},{24,28},{26,30},{28,20... | collective-permute-start | bytes 884744 | tf_op jit(solution)/shard_map/ppermute | solution.py:880
  53.2 0.8 copy-start.10
  53.2 9.7 %collective-permute-start.16 = (bf16[592,512]{1,0:T(8,128)(2,1)S(1)}, bf16[592,512]{1,0:T(8,128)(2,1)S(1)}, u32[]{:S(2)}, u32[]{:S(2)}) collective-permute-start(bf16[592,512]{1,0:T(8,128)(2,1)S(1)} %collective-permute-done.7.rest_0_.rest_10_), channel_id=1, source_target_pairs={{0,2},{2,0},{4,6},{6,4},{8,10},{10,8},{12,14},{14,12},{16,18},{18,... | collective-permute-start | bytes 1818632 | tf_op jit(solution)/shard_map/ppermute | solution.py:886
  53.2 1.0 copy-start.11
  53.3 9.7 %collective-permute-start.17 = (bf16[592,512]{1,0:T(8,128)(2,1)S(1)}, bf16[592,512]{1,0:T(8,128)(2,1)S(1)}, u32[]{:S(2)}, u32[]{:S(2)}) collective-permute-start(bf16[592,512]{1,0:T(8,128)(2,1)S(1)} %collective-permute-done.8.rest_1_.rest_11_), channel_id=1, source_target_pairs={{0,2},{2,0},{4,6},{6,4},{8,10},{10,8},{12,14},{14,12},{16,18},{18,... | collective-permute-start | bytes 1818632 | tf_op jit(solution)/shard_map/ppermute | solution.py:886
  54.3 0.9 copy-start.12
  60.9 7.4 %copy-start.1 = (bf16[512,768]{1,0:T(8,128)(2,1)S(1)}, bf16[512,768]{1,0:T(8,128)(2,1)}, u32[]{:S(2)}) copy-start(bf16[512,768]{1,0:T(8,128)(2,1)} %cot_ref.6) | copy-start | bytes 2359300
  60.9 2.0 %collective-permute-start.19 = (bf16[304,512]{1,0:T(8,128)(2,1)S(1)}, bf16[304,512]{1,0:T(8,128)(2,1)S(1)}, u32[]{:S(2)}, u32[]{:S(2)}) collective-permute-start(bf16[304,512]{1,0:T(8,128)(2,1)S(1)} %collective-permute-done.10.rest_3_.rest_13_), channel_id=1, source_target_pairs={{0,2},{2,0},{4,6},{6,4},{8,10},{10,8},{12,14},{14,12},{16,18},{18,... | collective-permute-start | bytes 933896 | tf_op jit(solution)/shard_map/ppermute | solution.py:886
  60.9 2.0 %collective-permute-start.18 = (bf16[288,512]{1,0:T(8,128)(2,1)S(1)}, bf16[288,512]{1,0:T(8,128)(2,1)S(1)}, u32[]{:S(2)}, u32[]{:S(2)}) collective-permute-start(bf16[288,512]{1,0:T(8,128)(2,1)S(1)} %collective-permute-done.9.rest_2_.rest_12_), channel_id=1, source_target_pairs={{0,2},{2,0},{4,6},{6,4},{8,10},{10,8},{12,14},{14,12},{16,18},{18,... | collective-permute-start | bytes 884744 | tf_op jit(solution)/shard_map/ppermute | solution.py:886
  66.2 7.9 %collective-permute-start.20 = (bf16[256,384]{1,0:T(8,128)(2,1)S(1)}, bf16[256,384]{1,0:T(8,128)(2,1)S(1)}, u32[]{:S(2)}, u32[]{:S(2)}) collective-permute-start(bf16[256,384]{1,0:T(8,128)(2,1)S(1)} %get-tuple-element.145.own_ref.rest_2_), channel_id=1, source_target_pairs={{0,1},{1,0},{2,3},{3,2},{4,5},{5,4},{6,7},{7,6},{8,9},{9,8},{10,11... | collective-permute-start | bytes 589832 | tf_op jit(solution)/shard_map/ppermute | solution.py:1047
  67.8 11.0 %collective-permute-start.21 = (bf16[256,384]{1,0:T(8,128)(2,1)S(1)}, bf16[256,384]{1,0:T(8,128)(2,1)S(1)}, u32[]{:S(2)}, u32[]{:S(2)}) collective-permute-start(bf16[256,384]{1,0:T(8,128)(2,1)S(1)} %get-tuple-element.151.own_ref.rest_3_), channel_id=1, source_target_pairs={{0,1},{1,0},{2,3},{3,2},{4,5},{5,4},{6,7},{7,6},{8,9},{9,8},{10,11... | collective-permute-start | bytes 589832 | tf_op jit(solution)/shard_map/ppermute | solution.py:1047
  77.1 11.4 %collective-permute-start.26 = (bf16[256,768]{1,0:T(8,128)(2,1)S(1)}, bf16[256,768]{1,0:T(8,128)(2,1)S(1)}, u32[]{:S(2)}, u32[]{:S(2)}) collective-permute-start(bf16[256,768]{1,0:T(8,128)(2,1)S(1)} %get-tuple-element.164.back_ref), channel_id=1, source_target_pairs={{0,1},{1,0},{2,3},{3,2},{4,5},{5,4},{6,7},{7,6},{8,9},{9,8},{10,11... | collective-permute-start | bytes 1179656 | tf_op jit(solution)/shard_map/ppermute | solution.py:1055
  86.4 1.6 %collective-permute-start.22 = (bf16[48,3072]{1,0:T(8,128)(2,1)S(1)}, bf16[48,3072]{1,0:T(8,128)(2,1)S(1)}, u32[]{:S(2)}, u32[]{:S(2)}) collective-permute-start(bf16[48,3072]{1,0:T(8,128)(2,1)S(1)} %get-tuple-element.160), channel_id=1, source_target_pairs={{0,2},{2,0},{4,6},{6,4},{8,10},{10,8},{12,14},{14,12},{16,18},{18,... | collective-permute-start | bytes 884744 | tf_op jit(solution)/shard_map/ppermute | solution.py:906
  86.5 2.0 %collective-permute-start.24 = (bf16[48,3072]{1,0:T(8,128)(2,1)S(1)}, bf16[48,3072]{1,0:T(8,128)(2,1)S(1)}, u32[]{:S(2)}, u32[]{:S(2)}) collective-permute-start(bf16[48,3072]{1,0:T(8,128)(2,1)S(1)} %get-tuple-element.161), channel_id=1, source_target_pairs={{0,2},{2,0},{4,6},{6,4},{8,10},{10,8},{12,14},{14,12},{16,18},{18,... | collective-permute-start | bytes 884744 | tf_op jit(solution)/shard_map/ppermute | solution.py:906
  88.5 9.8 %collective-permute-start.27 = (bf16[6,48,3072]{2,1,0:T(8,128)(2,1)S(1)}, bf16[6,48,3072]{2,1,0:T(8,128)(2,1)S(1)}, u32[]{:S(2)}, u32[]{:S(2)}) collective-permute-start(bf16[6,48,3072]{2,1,0:T(8,128)(2,1)S(1)} %get-tuple-element.174), channel_id=1, source_target_pairs={{0,2},{2,0},{4,6},{6,4},{8,10},{10,8},{12,14},{14,12},{16,18},{18,... | collective-permute-start | bytes 5308424 | tf_op jit(solution)/shard_map/ppermute | solution.py:925
  88.8 9.3 %collective-permute-start.23 = (bf16[48,3072]{1,0:T(8,128)(2,1)S(1)}, bf16[48,3072]{1,0:T(8,128)(2,1)S(1)}, u32[]{:S(2)}, u32[]{:S(2)}) collective-permute-start(bf16[48,3072]{1,0:T(8,128)(2,1)S(1)} %get-tuple-element.250), channel_id=1, source_target_pairs={{0,4},{2,6},{8,0},{10,2},{16,8},{18,10},{24,16},{26,18},{28,24},{3... | collective-permute-start | bytes 884744 | tf_op jit(solution)/shard_map/ppermute | solution.py:934
  89.3 9.0 %collective-permute-start.25 = (bf16[48,3072]{1,0:T(8,128)(2,1)S(1)}, bf16[48,3072]{1,0:T(8,128)(2,1)S(1)}, u32[]{:S(2)}, u32[]{:S(2)}) collective-permute-start(bf16[48,3072]{1,0:T(8,128)(2,1)S(1)} %get-tuple-element.249), channel_id=1, source_target_pairs={{0,8},{2,10},{8,16},{10,18},{16,24},{18,26},{24,28},{26,30},{28,20... | collective-permute-start | bytes 884744 | tf_op jit(solution)/shard_map/ppermute | solution.py:934
  90.9 11.8 %collective-permute-start.32 = (bf16[256,768]{1,0:T(8,128)(2,1)S(1)}, bf16[256,768]{1,0:T(8,128)(2,1)S(1)}, u32[]{:S(2)}, u32[]{:S(2)}) collective-permute-start(bf16[256,768]{1,0:T(8,128)(2,1)S(1)} %get-tuple-element.189.back_ref), channel_id=1, source_target_pairs={{0,1},{1,0},{2,3},{3,2},{4,5},{5,4},{6,7},{7,6},{8,9},{9,8},{10,11... | collective-permute-start | bytes 1179656 | tf_op jit(solution)/shard_map/ppermute | solution.py:1055
  98.5 8.9 %collective-permute-start.28 = (bf16[48,3072]{1,0:T(8,128)(2,1)S(1)}, bf16[48,3072]{1,0:T(8,128)(2,1)S(1)}, u32[]{:S(2)}, u32[]{:S(2)}) collective-permute-start(bf16[48,3072]{1,0:T(8,128)(2,1)S(1)} %get-tuple-element.248), channel_id=1, source_target_pairs={{0,4},{2,6},{8,0},{10,2},{16,8},{18,10},{24,16},{26,18},{28,24},{3... | collective-permute-start | bytes 884744 | tf_op jit(solution)/shard_map/ppermute | solution.py:934
  99.3 8.1 %collective-permute-start.29 = (bf16[48,3072]{1,0:T(8,128)(2,1)S(1)}, bf16[48,3072]{1,0:T(8,128)(2,1)S(1)}, u32[]{:S(2)}, u32[]{:S(2)}) collective-permute-start(bf16[48,3072]{1,0:T(8,128)(2,1)S(1)} %get-tuple-element.247), channel_id=1, source_target_pairs={{0,8},{2,10},{8,16},{10,18},{16,24},{18,26},{24,28},{26,30},{28,20... | collective-permute-start | bytes 884744 | tf_op jit(solution)/shard_map/ppermute | solution.py:934
  103.8 10.3 %collective-permute-start.35 = (bf16[192,768]{1,0:T(8,128)(2,1)S(1)}, bf16[192,768]{1,0:T(8,128)(2,1)S(1)}, u32[]{:S(2)}, u32[]{:S(2)}) collective-permute-start(bf16[192,768]{1,0:T(8,128)(2,1)S(1)} %get-tuple-element.202), channel_id=1, source_target_pairs={{0,1},{1,0},{2,3},{3,2},{4,5},{5,4},{6,7},{7,6},{8,9},{9,8},{10,11... | collective-permute-start | bytes 884744 | tf_op jit(solution)/shard_map/ppermute | solution.py:1075
  106.2 6.2 %collective-permute-start.33 = (f32[64,128]{1,0:T(8,128)S(1)}, f32[64,128]{1,0:T(8,128)S(1)}, u32[]{:S(2)}, u32[]{:S(2)}) collective-permute-start(f32[64,128]{1,0:T(8,128)S(1)} %get-tuple-element.194.ga_ref), channel_id=1, source_target_pairs={{0,1},{1,0},{2,3},{3,2},{4,5},{5,4},{6,7},{7,6},{8,9},{9,8},{10,11... | collective-permute-start | bytes 98312 | tf_op jit(solution)/shard_map/ppermute | solution.py:1077
  107.6 8.1 %collective-permute-start.30 = (bf16[48,3072]{1,0:T(8,128)(2,1)S(1)}, bf16[48,3072]{1,0:T(8,128)(2,1)S(1)}, u32[]{:S(2)}, u32[]{:S(2)}) collective-permute-start(bf16[48,3072]{1,0:T(8,128)(2,1)S(1)} %get-tuple-element.246), channel_id=1, source_target_pairs={{0,4},{2,6},{8,0},{10,2},{16,8},{18,10},{24,16},{26,18},{28,24},{3... | collective-permute-start | bytes 884744 | tf_op jit(solution)/shard_map/ppermute | solution.py:934
  109.1 6.7 %collective-permute-start.31 = (bf16[48,3072]{1,0:T(8,128)(2,1)S(1)}, bf16[48,3072]{1,0:T(8,128)(2,1)S(1)}, u32[]{:S(2)}, u32[]{:S(2)}) collective-permute-start(bf16[48,3072]{1,0:T(8,128)(2,1)S(1)} %get-tuple-element.245), channel_id=1, source_target_pairs={{0,8},{2,10},{8,16},{10,18},{16,24},{18,26},{24,28},{26,30},{28,20... | collective-permute-start | bytes 884744 | tf_op jit(solution)/shard_map/ppermute | solution.py:934
  114.1 1.6 %collective-permute-start.34 = (bf16[272,512]{1,0:T(8,128)(2,1)S(1)}, bf16[272,512]{1,0:T(8,128)(2,1)S(1)}, u32[]{:S(2)}, u32[]{:S(2)}) collective-permute-start(bf16[272,512]{1,0:T(8,128)(2,1)S(1)} %get-tuple-element.201), channel_id=1, source_target_pairs={{0,2},{2,0},{4,6},{6,4},{8,10},{10,8},{12,14},{14,12},{16,18},{18,... | collective-permute-start | bytes 835592 | tf_op jit(solution)/shard_map/ppermute | solution.py:906
  115.9 9.5 %collective-permute-start.37 = (bf16[7,272,512]{2,1,0:T(8,128)(2,1)S(1)}, bf16[7,272,512]{2,1,0:T(8,128)(2,1)S(1)}, u32[]{:S(2)}, u32[]{:S(2)}) collective-permute-start(bf16[7,272,512]{2,1,0:T(8,128)(2,1)S(1)} %get-tuple-element.211), channel_id=1, source_target_pairs={{0,2},{2,0},{4,6},{6,4},{8,10},{10,8},{12,14},{14,12},{16,18},{18,... | collective-permute-start | bytes 5849096 | tf_op jit(solution)/shard_map/ppermute | solution.py:925
  116.3 9.1 %collective-permute-start.38 = (bf16[272,512]{1,0:T(8,128)(2,1)S(1)}, bf16[272,512]{1,0:T(8,128)(2,1)S(1)}, u32[]{:S(2)}, u32[]{:S(2)}) collective-permute-start(bf16[272,512]{1,0:T(8,128)(2,1)S(1)} %fusion.24), channel_id=1, source_target_pairs={{0,8},{2,10},{8,16},{10,18},{16,24},{18,26},{24,28},{26,30},{28,20... | collective-permute-start | bytes 835592 | tf_op jit(solution)/shard_map/ppermute | solution.py:934
  117.9 10.9 %collective-permute-start.36 = (bf16[48,3072]{1,0:T(8,128)(2,1)S(1)}, bf16[48,3072]{1,0:T(8,128)(2,1)S(1)}, u32[]{:S(2)}, u32[]{:S(2)}) collective-permute-start(bf16[48,3072]{1,0:T(8,128)(2,1)S(1)} %fusion.19), channel_id=1, source_target_pairs={{0,4},{2,6},{8,0},{10,2},{16,8},{18,10},{24,16},{26,18},{28,24},{3... | collective-permute-start | bytes 884744 | tf_op jit(solution)/shard_map/ppermute | solution.py:934
  118.5 14.1 %collective-permute-start.41 = (bf16[320,768]{1,0:T(8,128)(2,1)S(1)}, bf16[320,768]{1,0:T(8,128)(2,1)S(1)}, u32[]{:S(2)}, u32[]{:S(2)}) collective-permute-start(bf16[320,768]{1,0:T(8,128)(2,1)S(1)} %get-tuple-element.204), channel_id=1, source_target_pairs={{0,1},{1,0},{2,3},{3,2},{4,5},{5,4},{6,7},{7,6},{8,9},{9,8},{10,11... | collective-permute-start | bytes 1474568 | tf_op jit(solution)/shard_map/ppermute | solution.py:1093
  125.4 8.3 %collective-permute-start.40 = (bf16[272,512]{1,0:T(8,128)(2,1)S(1)}, bf16[272,512]{1,0:T(8,128)(2,1)S(1)}, u32[]{:S(2)}, u32[]{:S(2)}) collective-permute-start(bf16[272,512]{1,0:T(8,128)(2,1)S(1)} %fusion.30), channel_id=1, source_target_pairs={{0,4},{2,6},{8,0},{10,2},{16,8},{18,10},{24,16},{26,18},{28,24},{3... | collective-permute-start | bytes 835592 | tf_op jit(solution)/shard_map/ppermute | solution.py:934
  127.1 8.0 %collective-permute-start.39 = (bf16[272,512]{1,0:T(8,128)(2,1)S(1)}, bf16[272,512]{1,0:T(8,128)(2,1)S(1)}, u32[]{:S(2)}, u32[]{:S(2)}) collective-permute-start(bf16[272,512]{1,0:T(8,128)(2,1)S(1)} %fusion.29), channel_id=1, source_target_pairs={{0,8},{2,10},{8,16},{10,18},{16,24},{18,26},{24,28},{26,30},{28,20... | collective-permute-start | bytes 835592 | tf_op jit(solution)/shard_map/ppermute | solution.py:934
  127.7 13.4 %collective-permute-start.44 = (bf16[256,768]{1,0:T(8,128)(2,1)S(1)}, bf16[256,768]{1,0:T(8,128)(2,1)S(1)}, u32[]{:S(2)}, u32[]{:S(2)}) collective-permute-start(bf16[256,768]{1,0:T(8,128)(2,1)S(1)} %get-tuple-element.218), channel_id=1, source_target_pairs={{0,1},{1,0},{2,3},{3,2},{4,5},{5,4},{6,7},{7,6},{8,9},{9,8},{10,11... | collective-permute-start | bytes 1179656 | tf_op jit(solution)/shard_map/ppermute | solution.py:1099
  135.4 7.1 %collective-permute-start.42 = (bf16[272,512]{1,0:T(8,128)(2,1)S(1)}, bf16[272,512]{1,0:T(8,128)(2,1)S(1)}, u32[]{:S(2)}, u32[]{:S(2)}) collective-permute-start(bf16[272,512]{1,0:T(8,128)(2,1)S(1)} %get-tuple-element.244), channel_id=1, source_target_pairs={{0,8},{2,10},{8,16},{10,18},{16,24},{18,26},{24,28},{26,30},{28,20... | collective-permute-start | bytes 835592 | tf_op jit(solution)/shard_map/ppermute | solution.py:934
  135.9 6.7 %collective-permute-start.43 = (bf16[272,512]{1,0:T(8,128)(2,1)S(1)}, bf16[272,512]{1,0:T(8,128)(2,1)S(1)}, u32[]{:S(2)}, u32[]{:S(2)}) collective-permute-start(bf16[272,512]{1,0:T(8,128)(2,1)S(1)} %get-tuple-element.243), channel_id=1, source_target_pairs={{0,4},{2,6},{8,0},{10,2},{16,8},{18,10},{24,16},{26,18},{28,24},{3... | collective-permute-start | bytes 835592 | tf_op jit(solution)/shard_map/ppermute | solution.py:934
  137.5 10.9 %collective-permute-start.45 = (bf16[256,768]{1,0:T(8,128)(2,1)S(1)}, bf16[256,768]{1,0:T(8,128)(2,1)S(1)}, u32[]{:S(2)}, u32[]{:S(2)}) collective-permute-start(bf16[256,768]{1,0:T(8,128)(2,1)S(1)} %get-tuple-element.223), channel_id=1, source_target_pairs={{0,1},{1,0},{2,3},{3,2},{4,5},{5,4},{6,7},{7,6},{8,9},{9,8},{10,11... | collective-permute-start | bytes 1179656 | tf_op jit(solution)/shard_map/ppermute | solution.py:1102
  142.8 7.6 %collective-permute-start.46 = (bf16[272,512]{1,0:T(8,128)(2,1)S(1)}, bf16[272,512]{1,0:T(8,128)(2,1)S(1)}, u32[]{:S(2)}, u32[]{:S(2)}) collective-permute-start(bf16[272,512]{1,0:T(8,128)(2,1)S(1)} %get-tuple-element.242), channel_id=1, source_target_pairs={{0,8},{2,10},{8,16},{10,18},{16,24},{18,26},{24,28},{26,30},{28,20... | collective-permute-start | bytes 835592 | tf_op jit(solution)/shard_map/ppermute | solution.py:934
  144.1 6.5 %collective-permute-start.47 = (bf16[272,512]{1,0:T(8,128)(2,1)S(1)}, bf16[272,512]{1,0:T(8,128)(2,1)S(1)}, u32[]{:S(2)}, u32[]{:S(2)}) collective-permute-start(bf16[272,512]{1,0:T(8,128)(2,1)S(1)} %get-tuple-element.241), channel_id=1, source_target_pairs={{0,4},{2,6},{8,0},{10,2},{16,8},{18,10},{24,16},{26,18},{28,24},{3... | collective-permute-start | bytes 835592 | tf_op jit(solution)/shard_map/ppermute | solution.py:934

commit v7 on v6

--- a/solution.py
+++ b/solution.py
@@ -75,21 +75,27 @@
         self.deep = self.last + self.fold
         self.cut = self.scores + krows * (2 * hidden // length // 3)
         self.gain_lane = 3 * self.tail
-
-    def ffn_parts(self):
+        self.head = self.value_row()
+
+    def projection_parts(self):
         parts = []
         for n, (kind, first) in enumerate(self.blocks):
             at = self.scores + n * self.krows
-            if kind == "ffn":
-                parts.append((at, 0, 0, first, self.krows, self.length))
-            else:
+            if kind == "proj":
                 skip = max(self.width - first, 0)
-                column = 2 * self.hidden + first + skip - self.width
-                parts.append((at, skip, 0, column, self.krows, self.length - skip))
+                parts.append((at, skip, 0, first + skip - self.width, self.krows, self.length - skip))
         for n in range(3):
-            column = 2 * self.hidden + self.wide - self.tail - self.width
+            column = self.wide - self.tail - self.width
             parts.append((self.last, n * self.tail, n * self.fold, column, self.fold, self.tail))
         return parts
+
+    def ffn_blocks(self, first, rows):
+        inside = [
+            n
+            for n, (kind, _) in enumerate(self.blocks)
+            if kind == "ffn" and first <= self.scores + n * self.krows < first + rows
+        ]
+        return (inside[0], len(inside)) if inside else (0, 0)
 
     def value_row(self):
         return self.scores + [kind for kind, _ in self.blocks].index("proj") * self.krows
@@ -110,9 +116,10 @@
     return parts
 
 
-def put_half(plan, out, half_ref, first):
+def put_half(plan, low, half_ref, first):
     for row, lane, at, column, rows, lanes in other_parts(plan, first):
-        out[row : row + rows, lane : lane + lanes] = half_ref[at : at + rows, column : column + lanes]
+        row = row - plan.head
+        low[row : row + rows, lane : lane + lanes] = half_ref[at : at + rows, column : column + lanes]
 
 
 def pack_unit(plan, second, scores, wv, gain_one, gain_two, w_up, w_down, wo):
@@ -123,8 +130,8 @@
     assert plan.tail <= width
 
     def kernel(second_ref, *rest):
-        out, wo_out, gains = rest[count : count + 3]
-        held, sem = rest[count + 3 : -1], rest[-1]
+        out, low, wo_out, gains = rest[count : count + 4]
+        held, sem = rest[count + 4 : -1], rest[-1]
         fetch(rest[:count], held, sem)
         s_ref, wv_ref, ga_ref, gf_ref, up_ref, down_ref, own_ref = held
         out[: plan.scores, :] = s_ref[...].reshape(plan.scores, length).astype(BF)
@@ -133,28 +140,26 @@
             if kind == "ffn":
                 ref, first = (up_ref, column) if n < per else (down_ref, column - plan.hidden)
                 out[at, :] = ref[:, first : first + length].astype(BF)
-            else:
-                out[at, :] = jnp.zeros((krows, length), BF)
-        out[plan.last :, : plan.gain_lane] = jnp.zeros((plan.fold, plan.gain_lane), BF)
-        out[plan.value_row() : plan.value_row() + krows, :width] = wv_ref[...].astype(BF)
+        low[...] = jnp.zeros_like(low)
+        low[:krows, :width] = wv_ref[...].astype(BF)
         wo_out[...] = own_ref[...].astype(BF)
         for place in range(2):
 
             @pl.when(second_ref[0] == place)
             def _():
-                put_half(plan, out, wo_out, place)
+                put_half(plan, low, wo_out, place)
 
         gains[...] = jnp.zeros_like(gains)
         gains[0:1, :krows] = ga_ref[...]
         gains[1:2, :krows] = gf_ref[...]
-        out[plan.last :, plan.gain_lane :] = gains[...].astype(BF)
+        low[plan.last - plan.head :, plan.gain_lane :] = gains[...].astype(BF)
 
     return run(
         kernel,
         "pack_unit",
         (second,),
         (),
-        (((plan.deep, length), BF), ((krows, width), BF)),
+        (((plan.head, length), BF), ((plan.deep - plan.head, length), BF), ((krows, width), BF)),
         (
             pltpu.VMEM((plan.fold, length - plan.gain_lane), F32),
             *[pltpu.VMEM(one.shape, one.dtype) for one in inputs],
@@ -164,25 +169,27 @@
     )
 
 
-def fill_units(plan, second, units, others):
-    count = len(units)
-
-    def kernel(second_ref, *rest):
+def fill_low(plan, second, low, other):
+    def kernel(second_ref, old, other_ref, out):
         for place in range(2):
 
             @pl.when(second_ref[0] == 1 - place)
             def _():
-                for n in range(count):
-                    put_half(plan, rest[2 * count + n], rest[count + n], place)
-
-    return run(
-        kernel,
-        "fill_units",
-        (second,),
-        (*units, *others),
-        [(one.shape, BF) for one in units],
-        aliases={1 + n: n for n in range(count)},
-    )
+                put_half(plan, out, other_ref, place)
+
+    return run(kernel, "fill_low", (second,), (low, other), ((low.shape, BF),), aliases={1: 0})[0]
+
+
+def join_units(plan, uppers, lowers):
+    count = len(uppers)
+
+    def kernel(*refs):
+        for n in range(count):
+            out = refs[2 * count + n]
+            out[: plan.head, :] = refs[n][...]
+            out[plan.head :, :] = refs[count + n][...]
+
+    return run(kernel, "join_units", (), (*uppers, *lowers), [((plan.deep, plan.length), BF)] * count)
 
 
 def fetch(refs, held, sem):
@@ -368,17 +375,25 @@
     length, model = cotangent.shape
     wide = sums.shape[1]
     hidden, krows, width = plan.hidden, plan.krows, plan.width
-    piece = hidden // 3
-    parts = plan.ffn_parts()
+    parts = plan.projection_parts()
+    blocks = 2 * hidden // length
 
     def kernel(where_ref, second_ref, cot_ref, sums_ref, *rest):
-        out, gact, mixf_ref, rb_ref, own_ref, sem = rest[len(units) :]
+        out, wo_ref, gact, mixf_ref, rb_ref, own_ref, sem, more = rest[len(units) :]
 
         def target(m, owner):
             _, _, row, column, rows, columns = parts[m]
-            return out.at[pl.ds(multiple(owner * krows + row, 16), rows), pl.ds(column, columns)]
-
-        copies = pick(rest[: len(units)], shares, where_ref, parts, target, sem)
+            return wo_ref.at[pl.ds(multiple(owner * krows + row, 16), rows), pl.ds(column, columns)]
+
+        copies = []
+        for n, (u, first, rows) in enumerate(shares):
+            begin, count = plan.ffn_blocks(first, rows)
+            if count:
+                source = rest[n].at[pl.ds(plan.scores + begin * krows - first, count * krows), :]
+                to = out.at[pl.ds(begin, count), pl.ds(multiple(where_ref[u] * krows, 16), krows), :]
+                copies.append(pltpu.make_async_copy(source.reshape(count, krows, length), to, more.at[n]))
+                copies[-1].start()
+        copies += pick(rest[: len(units)], shares, where_ref, parts, target, sem)
         inside = lax.broadcasted_iota(jnp.int32, (length, LANES), 1) < size
         for h in range(wide // LANES):
             lanes = slice(h * LANES, (h + 1) * LANES)
@@ -387,10 +402,9 @@
             mixf_ref[:, lanes] = jnp.where(inside, sums_ref[:, lanes] * inverse, 0.0)
         for copy in copies:
             copy.wait()
-        for j in range(3):
-            cols = slice(j * piece, (j + 1) * piece)
-            gact[:, cols] = mm(cot_ref[...], out[:, hidden + j * piece : hidden + (j + 1) * piece])
-        own = out[:, pl.ds(multiple(2 * hidden + second_ref[0] * width, LANES), width)]
+        for j in range(blocks // 2):
+            gact[:, j * length : (j + 1) * length] = mm(cot_ref[...], out[blocks // 2 + j])
+        own = wo_ref[:, pl.ds(multiple(second_ref[0] * width, LANES), width)]
         own_ref[...] = jnp.zeros_like(own_ref)
         for h in range(width // size):
             own_ref[:, h * LANES : h * LANES + size] = own[:, h * size : (h + 1) * size]
@@ -401,53 +415,54 @@
         (where, second),
         (cotangent, sums),
         (
-            ((model, 2 * hidden + model), BF),
+            ((blocks, model, length), BF),
+            ((model, model), BF),
             ((length, hidden), F32),
             (sums.shape, F32),
             (sums.shape, F32),
             ((model, wide), BF),
         ),
-        (pltpu.SemaphoreType.DMA((UNITS, len(parts))),),
+        (pltpu.SemaphoreType.DMA((UNITS, len(parts))), pltpu.SemaphoreType.DMA((len(units),))),
         loose=units,
         near=near,
     )
 
 
-def ffn_main(second, tokens, mixed_own, mixed_other, gact, gains, w, part, parts, before):
+def ffn_main(second, tokens, mixed_own, mixed_other, gact, gains, w, wo, part, parts, before):
     length, model = tokens.shape
     width = mixed_own.shape[1]
     hidden = gact.shape[1]
     chunk = length // parts
-    piece = hidden // 3
+    piece = w.shape[2]
     at = slice(part * chunk, (part + 1) * chunk)
 
-    def kernel(second_ref, tok_ref, own_ref, other_ref, gact_ref, gains_ref, w_ref, *rest):
-        back_ref, resid_ref, n2_ref, act_ref, gpre_ref, mixed, acc = rest[len(before) :]
+    def kernel(second_ref, tok_ref, own_ref, other_ref, gact_ref, gains_ref, w_ref, wo_ref, *rest):
+        back_ref, resid_ref, n2_ref, act_ref, gpre_ref, mixed = rest[len(before) :]
         first = second_ref[0]
         mixed[:, pl.ds(multiple(first * width, LANES), width)] = own_ref[...]
         mixed[:, pl.ds(multiple((1 - first) * width, LANES), width)] = other_ref[...]
-        attn = mm(mixed[...], w_ref[:, 2 * hidden :], NT)
+        attn = mm(mixed[...], wo_ref[...], NT)
         resid = tok_ref[at, :].astype(F32) + attn
         resid_ref[...] = resid
         inv = lax.rsqrt(jnp.mean(resid * resid, axis=-1, keepdims=True) + EPSILON)
-        n2_ref[at, :] = (resid * inv * gains_ref[1:2, :]).astype(BF)
+        n2 = (resid * inv * gains_ref[1:2, :]).astype(BF)
+        n2_ref[at, :] = n2
+        terms = []
+        pres = [mm(n2, w_ref[j]) for j in range(hidden // piece)]
         for j in range(hidden // piece):
             cols = slice(j * piece, (j + 1) * piece)
-            act, slope = gelu_pair(mm(n2_ref[at, :], w_ref[:, cols]))
+            act, slope = gelu_pair(pres[j])
             act_ref[at, cols] = act.astype(BF)
-            gpre_ref[at, cols] = (gact_ref[at, cols] * slope).astype(BF)
-            term = mm(gpre_ref[at, cols], w_ref[:, cols], NT)
-            if j == 0:
-                acc[...] = term
-            else:
-                acc[...] += term
-        back_ref[...] = acc[...].astype(BF)
+            gpre = (gact_ref[at, cols] * slope).astype(BF)
+            gpre_ref[at, cols] = gpre
+            terms.append(mm(gpre, w_ref[j], NT))
+        back_ref[...] = sum(terms).astype(BF)
 
     return run(
         kernel,
         "ffn_main",
         (second,),
-        (tokens, mixed_own, mixed_other, gact, gains, w, *before),
+        (tokens, mixed_own, mixed_other, gact, gains, w, wo, *before),
         (
             ((chunk, model), BF),
             ((chunk, model), F32),
@@ -457,9 +472,8 @@
         ),
         (
             pltpu.VMEM((chunk, 2 * width), BF),
-            pltpu.VMEM((chunk, model), F32),
         ),
-        aliases={7 + n: 2 + n for n in range(len(before))},
+        aliases={8 + n: 2 + n for n in range(len(before))},
     )
 
 
@@ -562,11 +576,14 @@
 
 def ffn_out(act, w, cut):
     length, hidden = act.shape
-    model = w.shape[0]
+    blocks, model, piece = w.shape
 
     def kernel(act_ref, w_ref, one, two):
-        one[...] = mm(act_ref[:cut, :], w_ref[:, hidden : 2 * hidden], NT).astype(BF)
-        two[...] = mm(act_ref[cut:, :], w_ref[:, hidden : 2 * hidden], NT).astype(BF)
+        for out, at in ((one, slice(0, cut)), (two, slice(cut, length))):
+            terms = [
+                mm(act_ref[at, j * piece : (j + 1) * piece], w_ref[blocks // 2 + j], NT) for j in range(blocks // 2)
+            ]
+            out[...] = sum(terms).astype(BF)
 
     return run(kernel, "ffn_out", (), (act, w), (((cut, model), BF), ((length - cut, model), BF)))
 
@@ -584,23 +601,18 @@
             down = slice(hidden + j * piece, hidden + (j + 1) * piece)
             scr[:, cols] = mm(n2_ref[...], gpre_ref[:, cols], TN).astype(BF)
             scr[:, down] = mm(cot_ref[...], act_ref[:, cols], TN).astype(BF)
-        copies = []
         for u in range(UNITS):
             at = pl.ds(multiple(where_ref[u] * krows, 16), krows)
             (to,) = slot(u)
-            copies.append(pltpu.make_async_copy(scr.at[at, :], to, sem.at[u]))
-            copies[-1].start()
-        for copy in copies:
-            copy.wait()
+            to[...] = scr[at, :]
 
     return run(
         kernel,
         "ffn_grads",
         (where,),
         (cotangent, n2, gpre, act),
-        (),
+        slot_shapes(krows, 2 * hidden, FFN_FIRST, 1, False),
         (pltpu.VMEM((model, 2 * hidden), BF), pltpu.SemaphoreType.DMA((UNITS,))),
-        loose_outs=slot_shapes(krows, 2 * hidden, FFN_FIRST, 1, False),
     )
 
 
@@ -871,15 +883,18 @@
     def take(self, values):
         self.last = list(values)
 
-    def hop(self, swap=True):
+    def arrived(self, units):
+        self.hops = 1
+        self.last = self.here = list(units)
+
+    def hop(self):
         ring = self.ring
         self.hops += 1
         up, down = self.last
         if self.hops == ring.chips // 2:
             up, down = up[: self.cut], down[self.cut :]
         self.last = [lax.ppermute(up, "dp", ring.up), lax.ppermute(down, "dp", ring.down)]
-        if swap:
-            self.swap()
+        self.swap()
         self.here = self.last
 
     def swap(self):
@@ -984,18 +999,19 @@
         far = net.chips // 2
         where_in = net.gathered().astype(jnp.int32)
         where_out = net.scattered().astype(jnp.int32)
-        unit, wo_own = pack_unit(
+        upper, lower, wo_own = pack_unit(
             plan, second_at, random_scores, w_value, gain_attn, gain_ffn, w_up, w_down.T, w_output.T
         )
+        ways = (net.up, net.down)
+        uppers = [lax.ppermute(upper, "dp", way) for way in ways]
+        wo_other = lax.ppermute(tie(wo_own, where_in, where_out), "mp", flip)
+        lower = fill_low(plan, second_at, lower, wo_other)
+        lowers = [lax.ppermute(lower, "dp", way) for way in ways]
+        (unit,) = join_units(plan, [upper], [lower])
         one = Gather(net, unit, plan.cut)
-        one.hop(False)
-        wo_other = lax.ppermute(tie(wo_own, where_in, where_out), "mp", flip)
-        wo_next = [lax.ppermute(wo_other, "dp", way) for way in (net.up, net.down)]
-        one.here = list(fill_units(plan, second_at, [unit], [wo_other]))
         one.swap()
-        wo_next = together([one], *wo_next)
-        one.last = list(fill_units(plan, second_at, one.last, wo_next))
-        one.here = one.last
+        uppers[0], uppers[1], *lowers = lax.optimization_barrier((*uppers, *lowers))
+        one.arrived(join_units(plan, uppers, lowers))
         for step in range(1, far - 1):
             one.hop()
             together([one])
@@ -1045,11 +1061,11 @@
         plan, where_in, segment_ids, begun, [units[n] for n in late], [shares[n] for n in late], heads, width
     )
     mixed_other = [lax.ppermute(one, "mp", flip) for one in mixed]
-    w, gact, mixf, rb, wo = second_weights(plan, where_in, second_at, cotangent, sums, units, shares, len(near), size)
+    w, wo_whole, gact, mixf, rb, wo = second_weights(plan, where_in, second_at, cotangent, sums, units, shares, len(near), size)
     backs, others, resids, kept = [], [], [], []
     for part in range(PARTS):
         back, resid, *kept = ffn_main(
-            second_at, tokens, mixed[part], mixed_other[part], gact, gains, w, part, PARTS, kept
+            second_at, tokens, mixed[part], mixed_other[part], gact, gains, w, wo_whole, part, PARTS, kept
         )
         backs.append(back)
         others.append(lax.ppermute(tie(back, *others[-1:]), "mp", flip))
@@ -1058,6 +1074,8 @@
     parts_two = ffn_grads(where_out, n2, gpre, act, cotangent)
     early = resid_back(backs[0], others[0], resids[0], cotangent, gains, wo, mixf, 0, heads, size, [])
     ffn_one, ffn_two = ffn_out(tie(act, *early), w, 3 * length // 8)
+    first_values = value_first(early[2], rb, e, size)
+    parts_one = mixer_grads(where_out, early[2], va, e, rb, krows, 0, [])
     if ring:
         ffn_sum = Scatter(net, FFN_FIRST, 1, *parts_two)
         ffn_sum.swap_all(others[0], *ffn_sum.values())
@@ -1065,16 +1083,17 @@
             ffn_sum.hop("down", far + step)
             ffn_sum.hop("up", far - 1 - step)
             if step == 0:
-                ffn_one, ffn_two, *early = together([ffn_sum], ffn_one, ffn_two, *early)
-    first_values = value_first(early[2], rb, e, size)
-    parts_one = mixer_grads(where_out, early[2], va, e, rb, krows, 0, [])
+                ffn_one, ffn_two, first_values, *more = together(
+                    [ffn_sum], ffn_one, ffn_two, first_values, *early, *parts_one
+                )
+                early, parts_one = more[: len(early)], more[len(early) :]
     cot_late = tie(cotangent, first_values, *parts_one)
     final = resid_back(backs[1], others[1], resids[1], cot_late, gains, wo, mixf, 1, heads, size, early[3:])
     gres, gats = (early[0], final[0]), (early[1], final[1])
     xh = final[2]
-    one_other = lax.ppermute(tie(ffn_one, xh), "mp", flip)
     gv, part_one, part_two, ga = value_back(xh, first_values, rb, e, wv, tokens, size, length // 2)
     ga_other = lax.ppermute(ga, "mp", flip)
+    one_other = lax.ppermute(tie(ffn_one, ga), "mp", flip)
     if ring:
         together([ffn_sum])
         for step in range(2, far - 1):

time: 152 us -> 149 us (0.980)
  waiting for transfers between devices: 65.6 us -> 62.5 us
  starting transfers between devices: 40.4 us -> 43 us
  Pallas kernels: 37.3 us -> 35.2 us
    ppermute x4 -> x3, starting transfers between devices: 7.91 us -> 4.83 us  [hop(): lax.ppermute(up, 'dp', ring.up)]
    ppermute x3 -> x5, starting transfers between devices: 2.93 us -> 5.73 us  [the longest x2 3.08 us: shards(): uppers = [lax.ppermute(upper, 'dp', way) for way in ways]]
    pallas_call x19 -> x20, Pallas kernels: 37.3 us -> 35.2 us  [run(): pl.pallas_call(kernel, out_shape=tuple(results), in_specs=specs, out_spec...]
    ppermute x14, waiting for transfers between devices: 14 us -> 12.4 us  [hop(): lax.ppermute(value, 'dp', self.ring.up if way == 'up' else self.ring.down)]
    ppermute x3 -> x5, waiting for transfers between devices: 9.06 us -> 9.28 us  [the longest x2 8.23 us: shards(): lowers = [lax.ppermute(lower, 'dp', way) for way in ways]]
    ppermute x4 -> x3, waiting for transfers between devices: 24.4 us -> 24.4 us  [hop(): lax.ppermute(up, 'dp', ring.up)]
  transfers between devices with their start and end apart: 48 -> 48, of which waited for: 26 -> 29; matrix products, arithmetic and copies ran while one was open for 4% -> 4% of each run, Pallas kernels for 21% -> 20%
where the time goes in v7:
time: 149 us
  waiting for transfers between devices  62.5 us (42%)
  starting transfers between devices  43 us (29%)
  Pallas kernels  35.2 us (24%)
  other arithmetic  5.71 us (4%)
    pallas_call x20, Pallas kernels, run(): pl.pallas_call(kernel, out_shape=tuple(results), in_specs=specs, out_spec...  35.2 us
    ppermute x3, waiting for transfers between devices, hop(): lax.ppermute(up, 'dp', ring.up)  24.4 us
    ppermute x14, starting transfers between devices, hop(): lax.ppermute(value, 'dp', self.ring.up if way == 'up' else self.ring.down)  14.7 us
    ppermute x14, waiting for transfers between devices, hop(): lax.ppermute(value, 'dp', self.ring.up if way == 'up' else self.ring.down)  12.4 us
    ppermute x2, waiting for transfers between devices, shards(): lowers = [lax.ppermute(lower, 'dp', way) for way in ways]  8.23 us
    ppermute x3, starting transfers between devices, hop(): lax.ppermute(up, 'dp', ring.up)  4.83 us
    ppermute x1, waiting for transfers between devices, shards(): part_other.append(lax.ppermute(part_two, 'mp', flip))  3.35 us
    ppermute x2, starting transfers between devices, shards(): uppers = [lax.ppermute(upper, 'dp', way) for way in ways]  3.08 us
  transfers between devices with their start and end apart: 48, of which 29 were waited for; matrix products, arithmetic and copies ran while one was open for 4% of the time, Pallas kernels for 20%

profile of v7, /device:TPU:0, one launch (start us, length us, event | category | flops | bytes accessed | tf_op | source)
XLA Modules:
  0.0 149.1 jit_solution(5232554364723485774)
XLA Ops:
  0.6 1.4 pack_unit.1
  2.0 3.1 %collective-permute-start = (bf16[480,512]{1,0:T(8,128)(2,1)S(1)}, bf16[480,512]{1,0:T(8,128)(2,1)S(1)}, u32[]{:S(2)}, u32[]{:S(2)}) collective-permute-start(bf16[480,512]{1,0:T(8,128)(2,1)S(1)} %get-tuple-element.127.refs_0_), channel_id=1, source_target_pairs={{0,8},{2,10},{8,16},{10,18},{16,24},{18,26},{24,28},{26,30},{28,20... | collective-permute-start | bytes 1474568 | tf_op jit(solution)/shard_map/ppermute | solution.py:1006
  5.1 0.7 broadcast_add_fusion.3
  6.0 2.0 %collective-permute-start.2 = (bf16[48,384]{1,0:T(8,128)(2,1)S(1)}, bf16[48,384]{1,0:T(8,128)(2,1)S(1)}, u32[]{:S(2)}, u32[]{:S(2)}) collective-permute-start(bf16[48,384]{1,0:T(8,128)(2,1)S(1)} %get-tuple-element.130), channel_id=1, source_target_pairs={{0,1},{1,0},{2,3},{3,2},{4,5},{5,4},{6,7},{7,6},{8,9},{9,8},{10,11... | collective-permute-start | bytes 110600 | tf_op jit(solution)/shard_map/ppermute | solution.py:1007
  7.9 2.0 %collective-permute-done.2.other_ref = bf16[48,384]{1,0:T(8,128)(2,1)S(1)} collective-permute-done((bf16[48,384]{1,0:T(8,128)(2,1)S(1)}, bf16[48,384]{1,0:T(8,128)(2,1)S(1)}, u32[]{:S(2)}, u32[]{:S(2)}) %collective-permute-start.2) | collective-permute-done | bytes 36896 | tf_op jit(solution)/shard_map/ppermute | solution.py:1007
  9.9 2.1 %collective-permute-start.3 = (bf16[112,512]{1,0:T(8,128)(2,1)S(1)}, bf16[112,512]{1,0:T(8,128)(2,1)S(1)}, u32[]{:S(2)}, u32[]{:S(2)}) collective-permute-start(bf16[112,512]{1,0:T(8,128)(2,1)S(1)} %fill_low.1.refs_1_), channel_id=1, source_target_pairs={{0,8},{2,10},{8,16},{10,18},{16,24},{18,26},{24,28},{26,30},{28,20... | collective-permute-start | bytes 344072 | tf_op jit(solution)/shard_map/ppermute | solution.py:1009
  12.0 6.7 %collective-permute-done.3.refs_2_ = bf16[112,512]{1,0:T(8,128)(2,1)S(1)} collective-permute-done((bf16[112,512]{1,0:T(8,128)(2,1)S(1)}, bf16[112,512]{1,0:T(8,128)(2,1)S(1)}, u32[]{:S(2)}, u32[]{:S(2)}) %collective-permute-start.3) | collective-permute-done | bytes 114720 | tf_op jit(solution)/shard_map/ppermute | solution.py:1009
  18.7 1.5 %collective-permute-done.4.refs_3_ = bf16[112,512]{1,0:T(8,128)(2,1)S(1)} collective-permute-done((bf16[112,512]{1,0:T(8,128)(2,1)S(1)}, bf16[112,512]{1,0:T(8,128)(2,1)S(1)}, u32[]{:S(2)}, u32[]{:S(2)}) %collective-permute-start.4) | collective-permute-done | bytes 114720 | tf_op jit(solution)/shard_map/ppermute | solution.py:1009
  20.4 1.6 %collective-permute-start.5 = (bf16[592,512]{1,0:T(8,128)(2,1)S(1)}, bf16[592,512]{1,0:T(8,128)(2,1)S(1)}, u32[]{:S(2)}, u32[]{:S(2)}) collective-permute-start(bf16[592,512]{1,0:T(8,128)(2,1)S(1)} %get-tuple-element.135.rest_1_), channel_id=1, source_target_pairs={{0,8},{2,10},{8,16},{10,18},{16,24},{18,26},{24,28},{26,30},{28,20... | collective-permute-start | bytes 1818632 | tf_op jit(solution)/shard_map/ppermute | solution.py:896
  22.5 12.2 %collective-permute-done.5.rest_3_ = bf16[592,512]{1,0:T(8,128)(2,1)S(1)} collective-permute-done((bf16[592,512]{1,0:T(8,128)(2,1)S(1)}, bf16[592,512]{1,0:T(8,128)(2,1)S(1)}, u32[]{:S(2)}, u32[]{:S(2)}) %collective-permute-start.5) | collective-permute-done | bytes 606240 | tf_op jit(solution)/shard_map/ppermute | solution.py:896
  34.7 1.3 collective-permute-done.6.rest_4_
  36.0 1.6 %collective-permute-start.7 = (bf16[592,512]{1,0:T(8,128)(2,1)S(1)}, bf16[592,512]{1,0:T(8,128)(2,1)S(1)}, u32[]{:S(2)}, u32[]{:S(2)}) collective-permute-start(bf16[592,512]{1,0:T(8,128)(2,1)S(1)} %collective-permute-done.5.rest_3_), channel_id=1, source_target_pairs={{0,8},{2,10},{8,16},{10,18},{16,24},{18,26},{24,28},{26,30},{28,20... | collective-permute-start | bytes 1818632 | tf_op jit(solution)/shard_map/ppermute | solution.py:896
  38.7 10.3 %collective-permute-done.7.rest_0_.rest_10_ = bf16[592,512]{1,0:T(8,128)(2,1)S(1)} collective-permute-done((bf16[592,512]{1,0:T(8,128)(2,1)S(1)}, bf16[592,512]{1,0:T(8,128)(2,1)S(1)}, u32[]{:S(2)}, u32[]{:S(2)}) %collective-permute-start.7) | collective-permute-done | bytes 606240 | tf_op jit(solution)/shard_map/ppermute | solution.py:896
  49.0 1.3 collective-permute-done.8.rest_1_.rest_11_
  50.9 1.6 %collective-permute-start.9 = (bf16[288,512]{1,0:T(8,128)(2,1)S(1)}, bf16[288,512]{1,0:T(8,128)(2,1)S(1)}, u32[]{:S(2)}, u32[]{:S(2)}) collective-permute-start(bf16[288,512]{1,0:T(8,128)(2,1)S(1)} %slice.97), channel_id=1, source_target_pairs={{0,8},{2,10},{8,16},{10,18},{16,24},{18,26},{24,28},{26,30},{28,20... | collective-permute-start | bytes 884744 | tf_op jit(solution)/shard_map/ppermute | solution.py:896
  53.5 0.9 copy-done.12
  54.4 3.8 %mixer_first.1 = (bf16[6,512,512]{2,1,0:T(8,128)(2,1)S(1)}, bf16[768,384]{1,0:T(8,128)(2,1)S(1)}, bf16[16,16,128]{2,1,0:T(8,128)(2,1)S(1)}, f32[512,768]{1,0:T(8,128)S(1)}) custom-call(s32[16]{0:T(128)S(1)} %pad_add_fusion.where_ref, bf16[512,768]{1,0:T(8,128)(2,1)S(1)} %copy-done, s32[1,512]{1,0:T(1,128)S(1)} %copy-done.5, bf16[592,512]{1,0:T(8,128)(2,1)} %copy-done.2, ...), custom_call_target="tpu_custom_call" | custom-call | flops 1 | bytes 1 | tf_op jit(solution)/shard_map/mixer_first/pallas_call | solution.py:36
  58.2 1.9 %collective-permute-done.9.rest_2_.rest_12_ = bf16[288,512]{1,0:T(8,128)(2,1)S(1)} collective-permute-done((bf16[288,512]{1,0:T(8,128)(2,1)S(1)}, bf16[288,512]{1,0:T(8,128)(2,1)S(1)}, u32[]{:S(2)}, u32[]{:S(2)}) %collective-permute-start.9) | collective-permute-done | bytes 294944 | tf_op jit(solution)/shard_map/ppermute | solution.py:896
  60.7 1.5 %collective-permute-done.18.rest_6_.rest_16_ = bf16[288,512]{1,0:T(8,128)(2,1)S(1)} collective-permute-done((bf16[288,512]{1,0:T(8,128)(2,1)S(1)}, bf16[288,512]{1,0:T(8,128)(2,1)S(1)}, u32[]{:S(2)}, u32[]{:S(2)}) %collective-permute-start.18) | collective-permute-done | bytes 294944 | tf_op jit(solution)/shard_map/ppermute | solution.py:901
  62.2 3.2 %mixer_forward.1 = (bf16[6,512,512]{2,1,0:T(8,128)(2,1)S(1)}, bf16[768,384]{1,0:T(8,128)(2,1)S(1)}, bf16[16,16,128]{2,1,0:T(8,128)(2,1)S(1)}, bf16[512,768]{1,0:...) custom-call(s32[16]{0:T(128)S(1)} %pad_add_fusion.where_ref, ...), custom_call_target="tpu_custom_call", output_to_operand_aliasing={{0}: (2, {}), {1}: (3, {}), {2}: (4, {})} | custom-call | flops 1 | bytes 1 | tf_op jit(solution)/shard_map/mixer_forward/pallas_call | solution.py:36
  65.4 1.6 %collective-permute-start.20 = (bf16[256,384]{1,0:T(8,128)(2,1)S(1)}, bf16[256,384]{1,0:T(8,128)(2,1)S(1)}, u32[]{:S(2)}, u32[]{:S(2)}) collective-permute-start(bf16[256,384]{1,0:T(8,128)(2,1)S(1)} %get-tuple-element.151.own_ref.rest_2_), channel_id=1, source_target_pairs={{0,1},{1,0},{2,3},{3,2},{4,5},{5,4},{6,7},{7,6},{8,9},{9,8},{10,11... | collective-permute-start | bytes 589832 | tf_op jit(solution)/shard_map/ppermute | solution.py:1063
  67.5 5.0 %second_weights.1 = (bf16[6,768,512]{2,1,0:T(8,128)(2,1)S(1)}, bf16[768,768]{1,0:T(8,128)(2,1)S(1)}, f32[512,1536]{1,0:T(8,128)S(1)}, f32[512,768]{1,0:T(8,128)S...) custom-call(s32[16]{0:T(128)S(1)} %pad_add_fusion.where_ref, s32[1]{0:T(128)} %bitcast.second_ref, ...), custom_call_target="tpu_custom_call" | custom-call | flops 1 | bytes 1 | tf_op jit(solution)/shard_map/second_weights/pallas_call | solution.py:36
  72.6 0.7 collective-permute-done.20.other_ref
  73.2 2.7 %ffn_main.2 = (bf16[256,768]{1,0:T(8,128)(2,1)S(1)}, f32[256,768]{1,0:T(8,128)S(1)}, bf16[512,768]{1,0:T(8,128)(2,1)S(1)}, bf16[512,1536]{1,0:T(8,128)(2,1)S(1)}, bf16[512,1536]{1,0:T(8,128)(2,1)S(1)}) custom-call(s32[1]{0:T(128)} %bitcast.second_ref, bf16[512,768]{1,0:T(8,128)(2,1)S(1)} %copy-done, bf16[256,384]{1,0:T(8,128)(2,1)S(1)} %get-tuple-element.151.own_ref.rest_2_, ...), custom_call_target="tpu_custom_call" | custom-call | flops 1 | bytes 1 | tf_op jit(solution)/shard_map/ffn_main/pallas_call | solution.py:36
  76.0 1.6 %collective-permute-start.26 = (bf16[256,768]{1,0:T(8,128)(2,1)S(1)}, bf16[256,768]{1,0:T(8,128)(2,1)S(1)}, u32[]{:S(2)}, u32[]{:S(2)}) collective-permute-start(bf16[256,768]{1,0:T(8,128)(2,1)S(1)} %get-tuple-element.171.back_ref), channel_id=1, source_target_pairs={{0,1},{1,0},{2,3},{3,2},{4,5},{5,4},{6,7},{7,6},{8,9},{9,8},{10,11... | collective-permute-start | bytes 1179656 | tf_op jit(solution)/shard_map/ppermute | solution.py:1071
  77.6 2.7 %ffn_main.3 = (bf16[256,768]{1,0:T(8,128)(2,1)S(1)}, f32[256,768]{1,0:T(8,128)S(1)}, bf16[512,768]{1,0:T(8,128)(2,1)S(1)}, bf16[512,1536]{1,0:T(8,128)(2,1)S(1)}, bf16[512,1536]{1,0:T(8,128)(2,1)S(1)}) custom-call(s32[1]{0:T(128)} %bitcast.second_ref, bf16[512,768]{1,0:T(8,128)(2,1)S(1)} %copy-done, ...), custom_call_target="tpu_custom_call", output_to_operand_aliasing={{2}: (8, {}), {3}: (9, {}), {4}: (10, {})} | custom-call | flops 1 | bytes 1 | tf_op jit(solution)/shard_map/ffn_main/pallas_call | solution.py:36
  80.3 3.6 %ffn_grads.1 = (bf16[8,48,3072]{2,1,0:T(8,128)(2,1)S(1)}, bf16[48,3072]{1,0:T(8,128)(2,1)S(1)}, bf16[48,3072]{1,0:T(8,128)(2,1)S(1)}, bf16[6,48,3072]{2,1,0:T(8,128)(2,1)S(1)}) custom-call(s32[16]{0:T(128)S(1)} %pad_add_fusion.1.where_ref, bf16[512,768]{1,0:T(8,128)(2,1)S(1)} %copy-done.1, bf16[512,768]{1,0:T(8,128)(2,1)S(1)} %get-tuple-element.163.n2_ref, ...), custom_call_target="tpu_custom_call" | custom-call | flops 1 | bytes 1 | tf_op jit(solution)/shard_map/ffn_grads/pallas_call | solution.py:36
  84.5 1.1 collective-permute-done.22
  86.8 1.6 %collective-permute-start.25 = (bf16[48,3072]{1,0:T(8,128)(2,1)S(1)}, bf16[48,3072]{1,0:T(8,128)(2,1)S(1)}, u32[]{:S(2)}, u32[]{:S(2)}) collective-permute-start(bf16[48,3072]{1,0:T(8,128)(2,1)S(1)} %get-tuple-element.259), channel_id=1, source_target_pairs={{0,8},{2,10},{8,16},{10,18},{16,24},{18,26},{24,28},{26,30},{28,20... | collective-permute-start | bytes 884744 | tf_op jit(solution)/shard_map/ppermute | solution.py:949
  88.4 1.3 collective-permute-start.32
  89.7 1.1 resid_back.2
  90.8 0.7 value_first.1.first_ref
  91.5 1.6 %mixer_grads.2 = (bf16[8,272,512]{2,1,0:T(8,128)(2,1)S(1)}, bf16[272,512]{1,0:T(8,128)(2,1)S(1)}, bf16[7,272,512]{2,1,0:T(8,128)(2,1)S(1)}) custom-call(s32[16]{0:T(128)S(1)} %pad_add_fusion.1.where_ref, bf16[256,768]{1,0:T(8,128)(2,1)S(1)} %get-tuple-element.174.xh_ref, bf16[512,768]{1,0:T(8,128)(2,1)S(1)} %get-tuple-element.181.va_ref, ...), custom_call_target="tpu_custom_call" | custom-call | flops 1 | bytes 1 | tf_op jit(solution)/shard_map/mixer_grads/pallas_call | solution.py:36
  93.1 1.7 %ffn_out.1 = (bf16[192,768]{1,0:T(8,128)(2,1)S(1)}, bf16[320,768]{1,0:T(8,128)(2,1)S(1)}) custom-call(bf16[512,1536]{1,0:T(8,128)(2,1)S(1)} %get-tuple-element.176.act_ref, bf16[6,768,512]{2,1,0:T(8,128)(2,1)S(1)} %get-tuple-element.155.w_ref), custom_call_target="tpu_custom_call" | custom-call | flops 1 | bytes 1 | tf_op jit(solution)/shard_map/ffn_out/pallas_call | solution.py:36
  94.8 0.8 collective-permute-done.23
  96.0 0.9 collective-permute-start.28
  96.9 1.2 collective-permute-start.29
  98.1 1.1 collective-permute-done.32.other_ref
  99.2 1.1 resid_back.3
  100.3 1.4 value_back.1
  101.8 1.5 %collective-permute-start.33 = (f32[64,128]{1,0:T(8,128)S(1)}, f32[64,128]{1,0:T(8,128)S(1)}, u32[]{:S(2)}, u32[]{:S(2)}) collective-permute-start(f32[64,128]{1,0:T(8,128)S(1)} %get-tuple-element.204.ga_ref), channel_id=1, source_target_pairs={{0,1},{1,0},{2,3},{3,2},{4,5},{5,4},{6,7},{7,6},{8,9},{9,8},{10,11... | collective-permute-start | bytes 98312 | tf_op jit(solution)/shard_map/ppermute | solution.py:1095
  105.0 1.5 %collective-permute-start.30 = (bf16[48,3072]{1,0:T(8,128)(2,1)S(1)}, bf16[48,3072]{1,0:T(8,128)(2,1)S(1)}, u32[]{:S(2)}, u32[]{:S(2)}) collective-permute-start(bf16[48,3072]{1,0:T(8,128)(2,1)S(1)} %get-tuple-element.256), channel_id=1, source_target_pairs={{0,4},{2,6},{8,0},{10,2},{16,8},{18,10},{24,16},{26,18},{28,24},{3... | collective-permute-start | bytes 884744 | tf_op jit(solution)/shard_map/ppermute | solution.py:949
  107.1 1.4 mixer_grads.3
  108.5 1.7 %weight_grads.1 = (bf16[8,272,512]{2,1,0:T(8,128)(2,1)S(1)}, bf16[272,512]{1,0:T(8,128)(2,1)S(1)}, bf16[7,272,512]{2,1,0:T(8,128)(2,1)S(1)}) custom-call(s32[16]{0:T(128)S(1)} %pad_add_fusion.1.where_ref, bf16[512,768]{1,0:T(8,128)(2,1)S(1)} %get-tuple-element.192.n1_ref, ...), custom_call_target="tpu_custom_call", output_to_operand_aliasing={{0}: (10, {}), {1}: (11, {}), {2}: (12, {})} | custom-call | flops 1 | bytes 1 | tf_op jit(solution)/shard_map/weight_grads/pallas_call | solution.py:36
  110.3 1.0 collective-permute-done.35
  112.1 1.2 collective-permute-done.31.up_ref
  114.5 1.5 collective-permute-start.36
  115.9 1.7 %collective-permute-start.41 = (bf16[320,768]{1,0:T(8,128)(2,1)S(1)}, bf16[320,768]{1,0:T(8,128)(2,1)S(1)}, u32[]{:S(2)}, u32[]{:S(2)}) collective-permute-start(bf16[320,768]{1,0:T(8,128)(2,1)S(1)} %get-tuple-element.214), channel_id=1, source_target_pairs={{0,1},{1,0},{2,3},{3,2},{4,5},{5,4},{6,7},{7,6},{8,9},{9,8},{10,11... | collective-permute-start | bytes 1474568 | tf_op jit(solution)/shard_map/ppermute | solution.py:1112
  117.7 5.1 %collective-permute-done.38 = bf16[272,512]{1,0:T(8,128)(2,1)S(1)} collective-permute-done((bf16[272,512]{1,0:T(8,128)(2,1)S(1)}, bf16[272,512]{1,0:T(8,128)(2,1)S(1)}, u32[]{:S(2)}, u32[]{:S(2)}) %collective-permute-start.38) | collective-permute-done | bytes 278560 | tf_op jit(solution)/shard_map/ppermute | solution.py:949
  122.9 1.6 %collective-permute-start.40 = (bf16[272,512]{1,0:T(8,128)(2,1)S(1)}, bf16[272,512]{1,0:T(8,128)(2,1)S(1)}, u32[]{:S(2)}, u32[]{:S(2)}) collective-permute-start(bf16[272,512]{1,0:T(8,128)(2,1)S(1)} %fusion.30), channel_id=1, source_target_pairs={{0,4},{2,6},{8,0},{10,2},{16,8},{18,10},{24,16},{26,18},{28,24},{3... | collective-permute-start | bytes 835592 | tf_op jit(solution)/shard_map/ppermute | solution.py:949
  125.2 1.8 %collective-permute-start.44 = (bf16[256,768]{1,0:T(8,128)(2,1)S(1)}, bf16[256,768]{1,0:T(8,128)(2,1)S(1)}, u32[]{:S(2)}, u32[]{:S(2)}) collective-permute-start(bf16[256,768]{1,0:T(8,128)(2,1)S(1)} %get-tuple-element.228), channel_id=1, source_target_pairs={{0,1},{1,0},{2,3},{3,2},{4,5},{5,4},{6,7},{7,6},{8,9},{9,8},{10,11... | collective-permute-start | bytes 1179656 | tf_op jit(solution)/shard_map/ppermute | solution.py:1118
  127.0 3.1 %collective-permute-done.41 = bf16[320,768]{1,0:T(8,128)(2,1)S(1)} collective-permute-done((bf16[320,768]{1,0:T(8,128)(2,1)S(1)}, bf16[320,768]{1,0:T(8,128)(2,1)S(1)}, u32[]{:S(2)}, u32[]{:S(2)}) %collective-permute-start.41) | collective-permute-done | bytes 491552 | tf_op jit(solution)/shard_map/ppermute | solution.py:1112
  130.0 1.2 collective-permute-done.40
  131.2 1.5 collective-permute-done.39
  133.4 1.6 %collective-permute-start.43 = (bf16[272,512]{1,0:T(8,128)(2,1)S(1)}, bf16[272,512]{1,0:T(8,128)(2,1)S(1)}, u32[]{:S(2)}, u32[]{:S(2)}) collective-permute-start(bf16[272,512]{1,0:T(8,128)(2,1)S(1)} %get-tuple-element.253), channel_id=1, source_target_pairs={{0,4},{2,6},{8,0},{10,2},{16,8},{18,10},{24,16},{26,18},{28,24},{3... | collective-permute-start | bytes 835592 | tf_op jit(solution)/shard_map/ppermute | solution.py:949
  135.0 1.8 %collective-permute-start.45 = (bf16[256,768]{1,0:T(8,128)(2,1)S(1)}, bf16[256,768]{1,0:T(8,128)(2,1)S(1)}, u32[]{:S(2)}, u32[]{:S(2)}) collective-permute-start(bf16[256,768]{1,0:T(8,128)(2,1)S(1)} %get-tuple-element.233), channel_id=1, source_target_pairs={{0,1},{1,0},{2,3},{3,2},{4,5},{5,4},{6,7},{7,6},{8,9},{9,8},{10,11... | collective-permute-start | bytes 1179656 | tf_op jit(solution)/shard_map/ppermute | solution.py:1121
  136.8 0.9 ffn_result.1
  137.7 1.2 fusion
  138.9 1.1 collective-permute-done.42
  140.4 0.6 collective-permute-start.46
  141.1 1.4 collective-permute-start.47
  142.5 3.4 %collective-permute-done.45 = bf16[256,768]{1,0:T(8,128)(2,1)S(1)} collective-permute-done((bf16[256,768]{1,0:T(8,128)(2,1)S(1)}, bf16[256,768]{1,0:T(8,128)(2,1)S(1)}, u32[]{:S(2)}, u32[]{:S(2)}) %collective-permute-start.45) | collective-permute-done | bytes 393248 | tf_op jit(solution)/shard_map/ppermute | solution.py:1121
  147.0 0.9 pad_maximum_fusion
  148.0 0.9 mixer_result.1
  (105 shorter events, 13.9 us)
Async XLA Ops:
  2.0 18.2 %collective-permute-start = (bf16[480,512]{1,0:T(8,128)(2,1)S(1)}, bf16[480,512]{1,0:T(8,128)(2,1)S(1)}, u32[]{:S(2)}, u32[]{:S(2)}) collective-permute-start(bf16[480,512]{1,0:T(8,128)(2,1)S(1)} %get-tuple-element.127.refs_0_), channel_id=1, source_target_pairs={{0,8},{2,10},{8,16},{10,18},{16,24},{18,26},{24,28},{26,30},{28,20... | collective-permute-start | bytes 1474568 | tf_op jit(solution)/shard_map/ppermute | solution.py:1006
  5.1 15.1 %collective-permute-start.1 = (bf16[480,512]{1,0:T(8,128)(2,1)S(1)}, bf16[480,512]{1,0:T(8,128)(2,1)S(1)}, u32[]{:S(2)}, u32[]{:S(2)}) collective-permute-start(bf16[480,512]{1,0:T(8,128)(2,1)S(1)} %get-tuple-element.127.refs_0_), channel_id=1, source_target_pairs={{0,4},{2,6},{8,0},{10,2},{16,8},{18,10},{24,16},{26,18},{28,24},{3... | collective-permute-start | bytes 1474568 | tf_op jit(solution)/shard_map/ppermute | solution.py:1006
  6.0 4.0 %collective-permute-start.2 = (bf16[48,384]{1,0:T(8,128)(2,1)S(1)}, bf16[48,384]{1,0:T(8,128)(2,1)S(1)}, u32[]{:S(2)}, u32[]{:S(2)}) collective-permute-start(bf16[48,384]{1,0:T(8,128)(2,1)S(1)} %get-tuple-element.130), channel_id=1, source_target_pairs={{0,1},{1,0},{2,3},{3,2},{4,5},{5,4},{6,7},{7,6},{8,9},{9,8},{10,11... | collective-permute-start | bytes 110600 | tf_op jit(solution)/shard_map/ppermute | solution.py:1007
  9.9 44.4 %copy-start = (bf16[512,768]{1,0:T(8,128)(2,1)S(1)}, bf16[512,768]{1,0:T(8,128)(2,1)}, u32[]{:S(2)}) copy-start(bf16[512,768]{1,0:T(8,128)(2,1)} %tok_ref.7) | copy-start | bytes 2359300
  9.9 44.4 %copy-start.5 = (s32[1,512]{1,0:T(1,128)S(1)}, s32[1,512]{1,0:T(1,128)}, u32[]{:S(2)}) copy-start(s32[1,512]{1,0:T(1,128)} %seg_ref.3) | copy-start | bytes 6148
  9.9 8.8 %collective-permute-start.3 = (bf16[112,512]{1,0:T(8,128)(2,1)S(1)}, bf16[112,512]{1,0:T(8,128)(2,1)S(1)}, u32[]{:S(2)}, u32[]{:S(2)}) collective-permute-start(bf16[112,512]{1,0:T(8,128)(2,1)S(1)} %fill_low.1.refs_1_), channel_id=1, source_target_pairs={{0,8},{2,10},{8,16},{10,18},{16,24},{18,26},{24,28},{26,30},{28,20... | collective-permute-start | bytes 344072 | tf_op jit(solution)/shard_map/ppermute | solution.py:1009
  12.0 8.2 %collective-permute-start.4 = (bf16[112,512]{1,0:T(8,128)(2,1)S(1)}, bf16[112,512]{1,0:T(8,128)(2,1)S(1)}, u32[]{:S(2)}, u32[]{:S(2)}) collective-permute-start(bf16[112,512]{1,0:T(8,128)(2,1)S(1)} %fill_low.1.refs_1_), channel_id=1, source_target_pairs={{0,4},{2,6},{8,0},{10,2},{16,8},{18,10},{24,16},{26,18},{28,24},{3... | collective-permute-start | bytes 344072 | tf_op jit(solution)/shard_map/ppermute | solution.py:1009
  20.3 32.7 %copy-start.3 = (bf16[592,512]{1,0:T(8,128)(2,1)}, bf16[592,512]{1,0:T(8,128)(2,1)S(1)}, u32[]{:S(2)}) copy-start(bf16[592,512]{1,0:T(8,128)(2,1)S(1)} %get-tuple-element.135.rest_1_) | copy-start | bytes 1818628
  20.4 32.7 %copy-start.4 = (bf16[592,512]{1,0:T(8,128)(2,1)}, bf16[592,512]{1,0:T(8,128)(2,1)S(1)}, u32[]{:S(2)}) copy-start(bf16[592,512]{1,0:T(8,128)(2,1)S(1)} %get-tuple-element.136.rest_2_) | copy-start | bytes 1818628
  20.4 14.3 %collective-permute-start.5 = (bf16[592,512]{1,0:T(8,128)(2,1)S(1)}, bf16[592,512]{1,0:T(8,128)(2,1)S(1)}, u32[]{:S(2)}, u32[]{:S(2)}) collective-permute-start(bf16[592,512]{1,0:T(8,128)(2,1)S(1)} %get-tuple-element.135.rest_1_), channel_id=1, source_target_pairs={{0,8},{2,10},{8,16},{10,18},{16,24},{18,26},{24,28},{26,30},{28,20... | collective-permute-start | bytes 1818632 | tf_op jit(solution)/shard_map/ppermute | solution.py:896
  22.0 13.9 %collective-permute-start.6 = (bf16[592,512]{1,0:T(8,128)(2,1)S(1)}, bf16[592,512]{1,0:T(8,128)(2,1)S(1)}, u32[]{:S(2)}, u32[]{:S(2)}) collective-permute-start(bf16[592,512]{1,0:T(8,128)(2,1)S(1)} %get-tuple-element.136.rest_2_), channel_id=1, source_target_pairs={{0,4},{2,6},{8,0},{10,2},{16,8},{18,10},{24,16},{26,18},{28,24},{3... | collective-permute-start | bytes 1818632 | tf_op jit(solution)/shard_map/ppermute | solution.py:896
  34.7 18.4 %copy-start.6 = (bf16[592,512]{1,0:T(8,128)(2,1)}, bf16[592,512]{1,0:T(8,128)(2,1)S(1)}, u32[]{:S(2)}) copy-start(bf16[592,512]{1,0:T(8,128)(2,1)S(1)} %collective-permute-done.5.rest_3_) | copy-start | bytes 1818628
  36.0 17.1 %copy-start.7 = (bf16[592,512]{1,0:T(8,128)(2,1)}, bf16[592,512]{1,0:T(8,128)(2,1)S(1)}, u32[]{:S(2)}) copy-start(bf16[592,512]{1,0:T(8,128)(2,1)S(1)} %collective-permute-done.6.rest_4_) | copy-start | bytes 1818628
  36.0 13.0 %collective-permute-start.7 = (bf16[592,512]{1,0:T(8,128)(2,1)S(1)}, bf16[592,512]{1,0:T(8,128)(2,1)S(1)}, u32[]{:S(2)}, u32[]{:S(2)}) collective-permute-start(bf16[592,512]{1,0:T(8,128)(2,1)S(1)} %collective-permute-done.5.rest_3_), channel_id=1, source_target_pairs={{0,8},{2,10},{8,16},{10,18},{16,24},{18,26},{24,28},{26,30},{28,20... | collective-permute-start | bytes 1818632 | tf_op jit(solution)/shard_map/ppermute | solution.py:896
  37.5 12.7 %collective-permute-start.8 = (bf16[592,512]{1,0:T(8,128)(2,1)S(1)}, bf16[592,512]{1,0:T(8,128)(2,1)S(1)}, u32[]{:S(2)}, u32[]{:S(2)}) collective-permute-start(bf16[592,512]{1,0:T(8,128)(2,1)S(1)} %collective-permute-done.6.rest_4_), channel_id=1, source_target_pairs={{0,4},{2,6},{8,0},{10,2},{16,8},{18,10},{24,16},{26,18},{28,24},{3... | collective-permute-start | bytes 1818632 | tf_op jit(solution)/shard_map/ppermute | solution.py:896
  38.0 15.0 %copy-start.2 = (bf16[592,512]{1,0:T(8,128)(2,1)}, bf16[592,512]{1,0:T(8,128)(2,1)S(1)}, u32[]{:S(2)}) copy-start(bf16[592,512]{1,0:T(8,128)(2,1)S(1)} %join_units.3.rest_0_) | copy-start | bytes 1818628
  38.0 12.3 %collective-permute-start.11 = (bf16[592,512]{1,0:T(8,128)(2,1)S(1)}, bf16[592,512]{1,0:T(8,128)(2,1)S(1)}, u32[]{:S(2)}, u32[]{:S(2)}) collective-permute-start(bf16[592,512]{1,0:T(8,128)(2,1)S(1)} %join_units.3.rest_0_), channel_id=1, source_target_pairs={{0,2},{2,0},{4,6},{6,4},{8,10},{10,8},{12,14},{14,12},{16,18},{18,... | collective-permute-start | bytes 1818632 | tf_op jit(solution)/shard_map/ppermute | solution.py:901
  38.1 12.7 %collective-permute-start.12 = (bf16[592,512]{1,0:T(8,128)(2,1)S(1)}, bf16[592,512]{1,0:T(8,128)(2,1)S(1)}, u32[]{:S(2)}, u32[]{:S(2)}) collective-permute-start(bf16[592,512]{1,0:T(8,128)(2,1)S(1)} %get-tuple-element.135.rest_1_), channel_id=1, source_target_pairs={{0,2},{2,0},{4,6},{6,4},{8,10},{10,8},{12,14},{14,12},{16,18},{18,... | collective-permute-start | bytes 1818632 | tf_op jit(solution)/shard_map/ppermute | solution.py:901
  38.6 13.9 %collective-permute-start.13 = (bf16[592,512]{1,0:T(8,128)(2,1)S(1)}, bf16[592,512]{1,0:T(8,128)(2,1)S(1)}, u32[]{:S(2)}, u32[]{:S(2)}) collective-permute-start(bf16[592,512]{1,0:T(8,128)(2,1)S(1)} %get-tuple-element.136.rest_2_), channel_id=1, source_target_pairs={{0,2},{2,0},{4,6},{6,4},{8,10},{10,8},{12,14},{14,12},{16,18},{18,... | collective-permute-start | bytes 1818632 | tf_op jit(solution)/shard_map/ppermute | solution.py:901
  49.0 3.5 %collective-permute-start.14 = (bf16[592,512]{1,0:T(8,128)(2,1)S(1)}, bf16[592,512]{1,0:T(8,128)(2,1)S(1)}, u32[]{:S(2)}, u32[]{:S(2)}) collective-permute-start(bf16[592,512]{1,0:T(8,128)(2,1)S(1)} %collective-permute-done.5.rest_3_), channel_id=1, source_target_pairs={{0,2},{2,0},{4,6},{6,4},{8,10},{10,8},{12,14},{14,12},{16,18},{18,... | collective-permute-start | bytes 1818632 | tf_op jit(solution)/shard_map/ppermute | solution.py:901
  50.3 2.7 %collective-permute-start.15 = (bf16[592,512]{1,0:T(8,128)(2,1)S(1)}, bf16[592,512]{1,0:T(8,128)(2,1)S(1)}, u32[]{:S(2)}, u32[]{:S(2)}) collective-permute-start(bf16[592,512]{1,0:T(8,128)(2,1)S(1)} %collective-permute-done.6.rest_4_), channel_id=1, source_target_pairs={{0,2},{2,0},{4,6},{6,4},{8,10},{10,8},{12,14},{14,12},{16,18},{18,... | collective-permute-start | bytes 1818632 | tf_op jit(solution)/shard_map/ppermute | solution.py:901
  50.3 2.8 %copy-start.8 = (bf16[592,512]{1,0:T(8,128)(2,1)}, bf16[592,512]{1,0:T(8,128)(2,1)S(1)}, u32[]{:S(2)}) copy-start(bf16[592,512]{1,0:T(8,128)(2,1)S(1)} %collective-permute-done.11.rest_5_) | copy-start | bytes 1818628
  50.3 9.8 %collective-permute-start.10 = (bf16[304,512]{1,0:T(8,128)(2,1)S(1)}, bf16[304,512]{1,0:T(8,128)(2,1)S(1)}, u32[]{:S(2)}, u32[]{:S(2)}) collective-permute-start(bf16[304,512]{1,0:T(8,128)(2,1)S(1)} %slice.98), channel_id=1, source_target_pairs={{0,4},{2,6},{8,0},{10,2},{16,8},{18,10},{24,16},{26,18},{28,24},{3... | collective-permute-start | bytes 933896 | tf_op jit(solution)/shard_map/ppermute | solution.py:896
  50.9 2.2 %copy-start.9 = (bf16[592,512]{1,0:T(8,128)(2,1)}, bf16[592,512]{1,0:T(8,128)(2,1)S(1)}, u32[]{:S(2)}) copy-start(bf16[592,512]{1,0:T(8,128)(2,1)S(1)} %collective-permute-done.12.rest_6_) | copy-start | bytes 1818628
  50.9 9.2 %collective-permute-start.9 = (bf16[288,512]{1,0:T(8,128)(2,1)S(1)}, bf16[288,512]{1,0:T(8,128)(2,1)S(1)}, u32[]{:S(2)}, u32[]{:S(2)}) collective-permute-start(bf16[288,512]{1,0:T(8,128)(2,1)S(1)} %slice.97), channel_id=1, source_target_pairs={{0,8},{2,10},{8,16},{10,18},{16,24},{18,26},{24,28},{26,30},{28,20... | collective-permute-start | bytes 884744 | tf_op jit(solution)/shard_map/ppermute | solution.py:896
  52.5 0.8 copy-start.10
  52.5 9.7 %collective-permute-start.16 = (bf16[592,512]{1,0:T(8,128)(2,1)S(1)}, bf16[592,512]{1,0:T(8,128)(2,1)S(1)}, u32[]{:S(2)}, u32[]{:S(2)}) collective-permute-start(bf16[592,512]{1,0:T(8,128)(2,1)S(1)} %collective-permute-done.7.rest_0_.rest_10_), channel_id=1, source_target_pairs={{0,2},{2,0},{4,6},{6,4},{8,10},{10,8},{12,14},{14,12},{16,18},{18,... | collective-permute-start | bytes 1818632 | tf_op jit(solution)/shard_map/ppermute | solution.py:901
  52.5 1.0 copy-start.11
  52.5 9.7 %collective-permute-start.17 = (bf16[592,512]{1,0:T(8,128)(2,1)S(1)}, bf16[592,512]{1,0:T(8,128)(2,1)S(1)}, u32[]{:S(2)}, u32[]{:S(2)}) collective-permute-start(bf16[592,512]{1,0:T(8,128)(2,1)S(1)} %collective-permute-done.8.rest_1_.rest_11_), channel_id=1, source_target_pairs={{0,2},{2,0},{4,6},{6,4},{8,10},{10,8},{12,14},{14,12},{16,18},{18,... | collective-permute-start | bytes 1818632 | tf_op jit(solution)/shard_map/ppermute | solution.py:901
  53.5 0.9 copy-start.12
  60.2 7.4 %copy-start.1 = (bf16[512,768]{1,0:T(8,128)(2,1)S(1)}, bf16[512,768]{1,0:T(8,128)(2,1)}, u32[]{:S(2)}) copy-start(bf16[512,768]{1,0:T(8,128)(2,1)} %cot_ref.6) | copy-start | bytes 2359300
  60.2 2.0 %collective-permute-start.19 = (bf16[304,512]{1,0:T(8,128)(2,1)S(1)}, bf16[304,512]{1,0:T(8,128)(2,1)S(1)}, u32[]{:S(2)}, u32[]{:S(2)}) collective-permute-start(bf16[304,512]{1,0:T(8,128)(2,1)S(1)} %collective-permute-done.10.rest_3_.rest_13_), channel_id=1, source_target_pairs={{0,2},{2,0},{4,6},{6,4},{8,10},{10,8},{12,14},{14,12},{16,18},{18,... | collective-permute-start | bytes 933896 | tf_op jit(solution)/shard_map/ppermute | solution.py:901
  60.2 2.0 %collective-permute-start.18 = (bf16[288,512]{1,0:T(8,128)(2,1)S(1)}, bf16[288,512]{1,0:T(8,128)(2,1)S(1)}, u32[]{:S(2)}, u32[]{:S(2)}) collective-permute-start(bf16[288,512]{1,0:T(8,128)(2,1)S(1)} %collective-permute-done.9.rest_2_.rest_12_), channel_id=1, source_target_pairs={{0,2},{2,0},{4,6},{6,4},{8,10},{10,8},{12,14},{14,12},{16,18},{18,... | collective-permute-start | bytes 884744 | tf_op jit(solution)/shard_map/ppermute | solution.py:901
  65.4 7.8 %collective-permute-start.20 = (bf16[256,384]{1,0:T(8,128)(2,1)S(1)}, bf16[256,384]{1,0:T(8,128)(2,1)S(1)}, u32[]{:S(2)}, u32[]{:S(2)}) collective-permute-start(bf16[256,384]{1,0:T(8,128)(2,1)S(1)} %get-tuple-element.151.own_ref.rest_2_), channel_id=1, source_target_pairs={{0,1},{1,0},{2,3},{3,2},{4,5},{5,4},{6,7},{7,6},{8,9},{9,8},{10,11... | collective-permute-start | bytes 589832 | tf_op jit(solution)/shard_map/ppermute | solution.py:1063
  67.0 10.5 %collective-permute-start.21 = (bf16[256,384]{1,0:T(8,128)(2,1)S(1)}, bf16[256,384]{1,0:T(8,128)(2,1)S(1)}, u32[]{:S(2)}, u32[]{:S(2)}) collective-permute-start(bf16[256,384]{1,0:T(8,128)(2,1)S(1)} %get-tuple-element.158.own_ref.rest_3_), channel_id=1, source_target_pairs={{0,1},{1,0},{2,3},{3,2},{4,5},{5,4},{6,7},{7,6},{8,9},{9,8},{10,11... | collective-permute-start | bytes 589832 | tf_op jit(solution)/shard_map/ppermute | solution.py:1063
  76.0 10.0 %collective-permute-start.26 = (bf16[256,768]{1,0:T(8,128)(2,1)S(1)}, bf16[256,768]{1,0:T(8,128)(2,1)S(1)}, u32[]{:S(2)}, u32[]{:S(2)}) collective-permute-start(bf16[256,768]{1,0:T(8,128)(2,1)S(1)} %get-tuple-element.171.back_ref), channel_id=1, source_target_pairs={{0,1},{1,0},{2,3},{3,2},{4,5},{5,4},{6,7},{7,6},{8,9},{9,8},{10,11... | collective-permute-start | bytes 1179656 | tf_op jit(solution)/shard_map/ppermute | solution.py:1071
  83.9 1.6 %collective-permute-start.22 = (bf16[48,3072]{1,0:T(8,128)(2,1)S(1)}, bf16[48,3072]{1,0:T(8,128)(2,1)S(1)}, u32[]{:S(2)}, u32[]{:S(2)}) collective-permute-start(bf16[48,3072]{1,0:T(8,128)(2,1)S(1)} %get-tuple-element.167), channel_id=1, source_target_pairs={{0,2},{2,0},{4,6},{6,4},{8,10},{10,8},{12,14},{14,12},{16,18},{18,... | collective-permute-start | bytes 884744 | tf_op jit(solution)/shard_map/ppermute | solution.py:921
  84.0 2.0 %collective-permute-start.24 = (bf16[48,3072]{1,0:T(8,128)(2,1)S(1)}, bf16[48,3072]{1,0:T(8,128)(2,1)S(1)}, u32[]{:S(2)}, u32[]{:S(2)}) collective-permute-start(bf16[48,3072]{1,0:T(8,128)(2,1)S(1)} %get-tuple-element.168), channel_id=1, source_target_pairs={{0,2},{2,0},{4,6},{6,4},{8,10},{10,8},{12,14},{14,12},{16,18},{18,... | collective-permute-start | bytes 884744 | tf_op jit(solution)/shard_map/ppermute | solution.py:921
  86.0 9.8 %collective-permute-start.27 = (bf16[6,48,3072]{2,1,0:T(8,128)(2,1)S(1)}, bf16[6,48,3072]{2,1,0:T(8,128)(2,1)S(1)}, u32[]{:S(2)}, u32[]{:S(2)}) collective-permute-start(bf16[6,48,3072]{2,1,0:T(8,128)(2,1)S(1)} %get-tuple-element.187), channel_id=1, source_target_pairs={{0,2},{2,0},{4,6},{6,4},{8,10},{10,8},{12,14},{14,12},{16,18},{18,... | collective-permute-start | bytes 5308424 | tf_op jit(solution)/shard_map/ppermute | solution.py:940
  86.3 9.3 %collective-permute-start.23 = (bf16[48,3072]{1,0:T(8,128)(2,1)S(1)}, bf16[48,3072]{1,0:T(8,128)(2,1)S(1)}, u32[]{:S(2)}, u32[]{:S(2)}) collective-permute-start(bf16[48,3072]{1,0:T(8,128)(2,1)S(1)} %get-tuple-element.260), channel_id=1, source_target_pairs={{0,4},{2,6},{8,0},{10,2},{16,8},{18,10},{24,16},{26,18},{28,24},{3... | collective-permute-start | bytes 884744 | tf_op jit(solution)/shard_map/ppermute | solution.py:949
  86.8 9.0 %collective-permute-start.25 = (bf16[48,3072]{1,0:T(8,128)(2,1)S(1)}, bf16[48,3072]{1,0:T(8,128)(2,1)S(1)}, u32[]{:S(2)}, u32[]{:S(2)}) collective-permute-start(bf16[48,3072]{1,0:T(8,128)(2,1)S(1)} %get-tuple-element.259), channel_id=1, source_target_pairs={{0,8},{2,10},{8,16},{10,18},{16,24},{18,26},{24,28},{26,30},{28,20... | collective-permute-start | bytes 884744 | tf_op jit(solution)/shard_map/ppermute | solution.py:949
  88.4 10.8 %collective-permute-start.32 = (bf16[256,768]{1,0:T(8,128)(2,1)S(1)}, bf16[256,768]{1,0:T(8,128)(2,1)S(1)}, u32[]{:S(2)}, u32[]{:S(2)}) collective-permute-start(bf16[256,768]{1,0:T(8,128)(2,1)S(1)} %get-tuple-element.199.back_ref), channel_id=1, source_target_pairs={{0,1},{1,0},{2,3},{3,2},{4,5},{5,4},{6,7},{7,6},{8,9},{9,8},{10,11... | collective-permute-start | bytes 1179656 | tf_op jit(solution)/shard_map/ppermute | solution.py:1071
  96.0 8.4 %collective-permute-start.28 = (bf16[48,3072]{1,0:T(8,128)(2,1)S(1)}, bf16[48,3072]{1,0:T(8,128)(2,1)S(1)}, u32[]{:S(2)}, u32[]{:S(2)}) collective-permute-start(bf16[48,3072]{1,0:T(8,128)(2,1)S(1)} %get-tuple-element.258), channel_id=1, source_target_pairs={{0,4},{2,6},{8,0},{10,2},{16,8},{18,10},{24,16},{26,18},{28,24},{3... | collective-permute-start | bytes 884744 | tf_op jit(solution)/shard_map/ppermute | solution.py:949
  96.9 8.0 %collective-permute-start.29 = (bf16[48,3072]{1,0:T(8,128)(2,1)S(1)}, bf16[48,3072]{1,0:T(8,128)(2,1)S(1)}, u32[]{:S(2)}, u32[]{:S(2)}) collective-permute-start(bf16[48,3072]{1,0:T(8,128)(2,1)S(1)} %get-tuple-element.257), channel_id=1, source_target_pairs={{0,8},{2,10},{8,16},{10,18},{16,24},{18,26},{24,28},{26,30},{28,20... | collective-permute-start | bytes 884744 | tf_op jit(solution)/shard_map/ppermute | solution.py:949
  101.8 6.7 %collective-permute-start.33 = (f32[64,128]{1,0:T(8,128)S(1)}, f32[64,128]{1,0:T(8,128)S(1)}, u32[]{:S(2)}, u32[]{:S(2)}) collective-permute-start(f32[64,128]{1,0:T(8,128)S(1)} %get-tuple-element.204.ga_ref), channel_id=1, source_target_pairs={{0,1},{1,0},{2,3},{3,2},{4,5},{5,4},{6,7},{7,6},{8,9},{9,8},{10,11... | collective-permute-start | bytes 98312 | tf_op jit(solution)/shard_map/ppermute | solution.py:1095
  103.3 8.1 %collective-permute-start.35 = (bf16[192,768]{1,0:T(8,128)(2,1)S(1)}, bf16[192,768]{1,0:T(8,128)(2,1)S(1)}, u32[]{:S(2)}, u32[]{:S(2)}) collective-permute-start(bf16[192,768]{1,0:T(8,128)(2,1)S(1)} %get-tuple-element.212), channel_id=1, source_target_pairs={{0,1},{1,0},{2,3},{3,2},{4,5},{5,4},{6,7},{7,6},{8,9},{9,8},{10,11... | collective-permute-start | bytes 884744 | tf_op jit(solution)/shard_map/ppermute | solution.py:1096
  105.0 7.1 %collective-permute-start.30 = (bf16[48,3072]{1,0:T(8,128)(2,1)S(1)}, bf16[48,3072]{1,0:T(8,128)(2,1)S(1)}, u32[]{:S(2)}, u32[]{:S(2)}) collective-permute-start(bf16[48,3072]{1,0:T(8,128)(2,1)S(1)} %get-tuple-element.256), channel_id=1, source_target_pairs={{0,4},{2,6},{8,0},{10,2},{16,8},{18,10},{24,16},{26,18},{28,24},{3... | collective-permute-start | bytes 884744 | tf_op jit(solution)/shard_map/ppermute | solution.py:949
  106.6 6.7 %collective-permute-start.31 = (bf16[48,3072]{1,0:T(8,128)(2,1)S(1)}, bf16[48,3072]{1,0:T(8,128)(2,1)S(1)}, u32[]{:S(2)}, u32[]{:S(2)}) collective-permute-start(bf16[48,3072]{1,0:T(8,128)(2,1)S(1)} %get-tuple-element.255), channel_id=1, source_target_pairs={{0,8},{2,10},{8,16},{10,18},{16,24},{18,26},{24,28},{26,30},{28,20... | collective-permute-start | bytes 884744 | tf_op jit(solution)/shard_map/ppermute | solution.py:949
  110.2 1.6 %collective-permute-start.34 = (bf16[272,512]{1,0:T(8,128)(2,1)S(1)}, bf16[272,512]{1,0:T(8,128)(2,1)S(1)}, u32[]{:S(2)}, u32[]{:S(2)}) collective-permute-start(bf16[272,512]{1,0:T(8,128)(2,1)S(1)} %get-tuple-element.211), channel_id=1, source_target_pairs={{0,2},{2,0},{4,6},{6,4},{8,10},{10,8},{12,14},{14,12},{16,18},{18,... | collective-permute-start | bytes 835592 | tf_op jit(solution)/shard_map/ppermute | solution.py:921
  113.4 9.5 %collective-permute-start.37 = (bf16[7,272,512]{2,1,0:T(8,128)(2,1)S(1)}, bf16[7,272,512]{2,1,0:T(8,128)(2,1)S(1)}, u32[]{:S(2)}, u32[]{:S(2)}) collective-permute-start(bf16[7,272,512]{2,1,0:T(8,128)(2,1)S(1)} %get-tuple-element.221), channel_id=1, source_target_pairs={{0,2},{2,0},{4,6},{6,4},{8,10},{10,8},{12,14},{14,12},{16,18},{18,... | collective-permute-start | bytes 5849096 | tf_op jit(solution)/shard_map/ppermute | solution.py:940
  113.7 9.1 %collective-permute-start.38 = (bf16[272,512]{1,0:T(8,128)(2,1)S(1)}, bf16[272,512]{1,0:T(8,128)(2,1)S(1)}, u32[]{:S(2)}, u32[]{:S(2)}) collective-permute-start(bf16[272,512]{1,0:T(8,128)(2,1)S(1)} %fusion.24), channel_id=1, source_target_pairs={{0,8},{2,10},{8,16},{10,18},{16,24},{18,26},{24,28},{26,30},{28,20... | collective-permute-start | bytes 835592 | tf_op jit(solution)/shard_map/ppermute | solution.py:949
  114.5 12.5 %collective-permute-start.36 = (bf16[48,3072]{1,0:T(8,128)(2,1)S(1)}, bf16[48,3072]{1,0:T(8,128)(2,1)S(1)}, u32[]{:S(2)}, u32[]{:S(2)}) collective-permute-start(bf16[48,3072]{1,0:T(8,128)(2,1)S(1)} %fusion.19), channel_id=1, source_target_pairs={{0,4},{2,6},{8,0},{10,2},{16,8},{18,10},{24,16},{26,18},{28,24},{3... | collective-permute-start | bytes 884744 | tf_op jit(solution)/shard_map/ppermute | solution.py:949
  115.9 14.1 %collective-permute-start.41 = (bf16[320,768]{1,0:T(8,128)(2,1)S(1)}, bf16[320,768]{1,0:T(8,128)(2,1)S(1)}, u32[]{:S(2)}, u32[]{:S(2)}) collective-permute-start(bf16[320,768]{1,0:T(8,128)(2,1)S(1)} %get-tuple-element.214), channel_id=1, source_target_pairs={{0,1},{1,0},{2,3},{3,2},{4,5},{5,4},{6,7},{7,6},{8,9},{9,8},{10,11... | collective-permute-start | bytes 1474568 | tf_op jit(solution)/shard_map/ppermute | solution.py:1112
  122.9 8.3 %collective-permute-start.40 = (bf16[272,512]{1,0:T(8,128)(2,1)S(1)}, bf16[272,512]{1,0:T(8,128)(2,1)S(1)}, u32[]{:S(2)}, u32[]{:S(2)}) collective-permute-start(bf16[272,512]{1,0:T(8,128)(2,1)S(1)} %fusion.30), channel_id=1, source_target_pairs={{0,4},{2,6},{8,0},{10,2},{16,8},{18,10},{24,16},{26,18},{28,24},{3... | collective-permute-start | bytes 835592 | tf_op jit(solution)/shard_map/ppermute | solution.py:949
  124.6 8.0 %collective-permute-start.39 = (bf16[272,512]{1,0:T(8,128)(2,1)S(1)}, bf16[272,512]{1,0:T(8,128)(2,1)S(1)}, u32[]{:S(2)}, u32[]{:S(2)}) collective-permute-start(bf16[272,512]{1,0:T(8,128)(2,1)S(1)} %fusion.29), channel_id=1, source_target_pairs={{0,8},{2,10},{8,16},{10,18},{16,24},{18,26},{24,28},{26,30},{28,20... | collective-permute-start | bytes 835592 | tf_op jit(solution)/shard_map/ppermute | solution.py:949
  125.2 13.7 %collective-permute-start.44 = (bf16[256,768]{1,0:T(8,128)(2,1)S(1)}, bf16[256,768]{1,0:T(8,128)(2,1)S(1)}, u32[]{:S(2)}, u32[]{:S(2)}) collective-permute-start(bf16[256,768]{1,0:T(8,128)(2,1)S(1)} %get-tuple-element.228), channel_id=1, source_target_pairs={{0,1},{1,0},{2,3},{3,2},{4,5},{5,4},{6,7},{7,6},{8,9},{9,8},{10,11... | collective-permute-start | bytes 1179656 | tf_op jit(solution)/shard_map/ppermute | solution.py:1118
  132.9 7.1 %collective-permute-start.42 = (bf16[272,512]{1,0:T(8,128)(2,1)S(1)}, bf16[272,512]{1,0:T(8,128)(2,1)S(1)}, u32[]{:S(2)}, u32[]{:S(2)}) collective-permute-start(bf16[272,512]{1,0:T(8,128)(2,1)S(1)} %get-tuple-element.254), channel_id=1, source_target_pairs={{0,8},{2,10},{8,16},{10,18},{16,24},{18,26},{24,28},{26,30},{28,20... | collective-permute-start | bytes 835592 | tf_op jit(solution)/shard_map/ppermute | solution.py:949
  133.4 6.8 %collective-permute-start.43 = (bf16[272,512]{1,0:T(8,128)(2,1)S(1)}, bf16[272,512]{1,0:T(8,128)(2,1)S(1)}, u32[]{:S(2)}, u32[]{:S(2)}) collective-permute-start(bf16[272,512]{1,0:T(8,128)(2,1)S(1)} %get-tuple-element.253), channel_id=1, source_target_pairs={{0,4},{2,6},{8,0},{10,2},{16,8},{18,10},{24,16},{26,18},{28,24},{3... | collective-permute-start | bytes 835592 | tf_op jit(solution)/shard_map/ppermute | solution.py:949
  135.0 10.9 %collective-permute-start.45 = (bf16[256,768]{1,0:T(8,128)(2,1)S(1)}, bf16[256,768]{1,0:T(8,128)(2,1)S(1)}, u32[]{:S(2)}, u32[]{:S(2)}) collective-permute-start(bf16[256,768]{1,0:T(8,128)(2,1)S(1)} %get-tuple-element.233), channel_id=1, source_target_pairs={{0,1},{1,0},{2,3},{3,2},{4,5},{5,4},{6,7},{7,6},{8,9},{9,8},{10,11... | collective-permute-start | bytes 1179656 | tf_op jit(solution)/shard_map/ppermute | solution.py:1121
  140.4 7.5 %collective-permute-start.46 = (bf16[272,512]{1,0:T(8,128)(2,1)S(1)}, bf16[272,512]{1,0:T(8,128)(2,1)S(1)}, u32[]{:S(2)}, u32[]{:S(2)}) collective-permute-start(bf16[272,512]{1,0:T(8,128)(2,1)S(1)} %get-tuple-element.252), channel_id=1, source_target_pairs={{0,8},{2,10},{8,16},{10,18},{16,24},{18,26},{24,28},{26,30},{28,20... | collective-permute-start | bytes 835592 | tf_op jit(solution)/shard_map/ppermute | solution.py:949
  141.1 6.9 %collective-permute-start.47 = (bf16[272,512]{1,0:T(8,128)(2,1)S(1)}, bf16[272,512]{1,0:T(8,128)(2,1)S(1)}, u32[]{:S(2)}, u32[]{:S(2)}) collective-permute-start(bf16[272,512]{1,0:T(8,128)(2,1)S(1)} %get-tuple-element.251), channel_id=1, source_target_pairs={{0,4},{2,6},{8,0},{10,2},{16,8},{18,10},{24,16},{26,18},{28,24},{3... | collective-permute-start | bytes 835592 | tf_op jit(solution)/shard_map/ppermute | solution.py:949

commit v8 on v7

--- a/solution.py
+++ b/solution.py
@@ -729,6 +729,35 @@
         ),
         (pltpu.VMEM((8, model), F32),),
     )
+
+
+def token_grads(mine, other, gres, tokens, gains, part, before):
+    chunk, model = mine.shape
+    length = tokens.shape[0]
+    at = slice(part * chunk, (part + 1) * chunk)
+
+    def kernel(mine_ref, other_ref, gres_ref, tok_ref, gains_ref, *rest):
+        out, held, sem = rest[len(before) :]
+        x = tok_ref[at, :].astype(F32)
+        inv = lax.rsqrt(jnp.mean(x * x, axis=-1, keepdims=True) + EPSILON)
+        hat = x * inv
+        z = gains_ref[0:1, :] * (mine_ref[...].astype(F32) + other_ref[...].astype(F32))
+        held[...] = (gres_ref[...] + inv * (z - hat * jnp.mean(z * hat, axis=-1, keepdims=True))).astype(BF)
+        copy = pltpu.make_async_copy(held, out.at[at, :], sem)
+        copy.start()
+        copy.wait()
+
+    return run(
+        kernel,
+        "token_grads",
+        (),
+        (mine, other, gres, tokens, gains),
+        (),
+        (pltpu.VMEM((chunk, model), BF), pltpu.SemaphoreType.DMA),
+        loose=before,
+        loose_outs=(((length, model), BF),),
+        aliases={5: 0} if before else None,
+    )[0]
 
 
 def low_rows(krows):
@@ -1159,18 +1188,10 @@
     ffn = jnp.concatenate([ffn_one, ffn_two])
     ffn_other = jnp.concatenate([one_other, two_other])
     output = (jnp.concatenate(resids) + (ffn.astype(F32) + ffn_other.astype(F32))).astype(BF)
-    backs = []
-    begin = 0
-    for mine, other in zip((part_one, part_two), part_other):
-        grad_n1 = mine.astype(F32) + other.astype(F32)
-        at = slice(begin, begin + mine.shape[0])
-        begin = at.stop
-        x = tokens[at].astype(F32)
-        inv = lax.rsqrt(jnp.mean(x * x, axis=-1, keepdims=True) + EPSILON)
-        z = gains[0:1, :] * grad_n1
-        hat = x * inv
-        backs.append((gres[len(backs)] + inv * (z - hat * jnp.mean(z * hat, axis=-1, keepdims=True))).astype(BF))
-    grad_tokens = jnp.concatenate(backs)
+    written = []
+    for part, (mine, other) in enumerate(zip((part_one, part_two), part_other)):
+        written = [token_grads(mine, other, gres[part], tokens, gains, part, written)]
+    (grad_tokens,) = written
     return (
         output,
         grad_tokens,

time: 149 us -> 149 us (level)
  other arithmetic: 5.71 us -> 3.4 us
  Pallas kernels: 35.2 us -> 37.5 us
    ppermute x1, waiting for transfers between devices: 3.35 us -> 0.17 us  [shards(): part_other.append(lax.ppermute(part_two, 'mp', flip))]
    pallas_call x20 -> x22, Pallas kernels: 35.2 us -> 37.5 us  [run(): pl.pallas_call(kernel, out_shape=tuple(results), in_specs=specs, out_spec...]
    ppermute x1, waiting for transfers between devices: 0.01 us -> 1.77 us  [shards(): part_other = [lax.ppermute(part_one, 'mp', flip)]]
  transfers between devices with their start and end apart: 48 -> 48, of which waited for: 29 -> 31; matrix products, arithmetic and copies ran while one was open for 4% -> 2% of each run, Pallas kernels for 20% -> 22%
where the time goes in v8:
time: 149 us; the launch traced here: 148 us
  waiting for transfers between devices  61.8 us (41%)
  starting transfers between devices  42.9 us (29%)
  Pallas kernels  37.5 us (25%)
  other arithmetic  3.4 us (2%)
    pallas_call x22, Pallas kernels, run(): pl.pallas_call(kernel, out_shape=tuple(results), in_specs=specs, out_spec...  37.5 us
    ppermute x3, waiting for transfers between devices, hop(): lax.ppermute(up, 'dp', ring.up)  24.4 us
    ppermute x14, starting transfers between devices, hop(): lax.ppermute(value, 'dp', self.ring.up if way == 'up' else self.ring.down)  14.7 us
    ppermute x14, waiting for transfers between devices, hop(): lax.ppermute(value, 'dp', self.ring.up if way == 'up' else self.ring.down)  13 us
    ppermute x2, waiting for transfers between devices, shards(): lowers = [lax.ppermute(lower, 'dp', way) for way in ways]  8.23 us
    ppermute x3, starting transfers between devices, hop(): lax.ppermute(up, 'dp', ring.up)  4.83 us
    ppermute x1, waiting for transfers between devices, shards(): two_other = lax.ppermute(ffn_two, 'mp', flip)  3.22 us
    ppermute x2, starting transfers between devices, shards(): uppers = [lax.ppermute(upper, 'dp', way) for way in ways]  3.08 us
  transfers between devices with their start and end apart: 48, of which 31 were waited for; matrix products, arithmetic and copies ran while one was open for 2% of the time, Pallas kernels for 22%

profile of v8, /device:TPU:0, one launch (start us, length us, event | category | flops | bytes accessed | tf_op | source)
XLA Modules:
  0.0 148.3 jit_solution(4254831545712692035)
XLA Ops:
  0.6 1.4 pack_unit.1
  2.0 3.1 %collective-permute-start = (bf16[480,512]{1,0:T(8,128)(2,1)S(1)}, bf16[480,512]{1,0:T(8,128)(2,1)S(1)}, u32[]{:S(2)}, u32[]{:S(2)}) collective-permute-start(bf16[480,512]{1,0:T(8,128)(2,1)S(1)} %get-tuple-element.127.refs_0_), channel_id=1, source_target_pairs={{0,8},{2,10},{8,16},{10,18},{16,24},{18,26},{24,28},{26,30},{28,20... | collective-permute-start | bytes 1474568 | tf_op jit(solution)/shard_map/ppermute | solution.py:1035
  5.1 0.7 broadcast_add_fusion.3
  6.0 2.0 %collective-permute-start.2 = (bf16[48,384]{1,0:T(8,128)(2,1)S(1)}, bf16[48,384]{1,0:T(8,128)(2,1)S(1)}, u32[]{:S(2)}, u32[]{:S(2)}) collective-permute-start(bf16[48,384]{1,0:T(8,128)(2,1)S(1)} %get-tuple-element.130), channel_id=1, source_target_pairs={{0,1},{1,0},{2,3},{3,2},{4,5},{5,4},{6,7},{7,6},{8,9},{9,8},{10,11... | collective-permute-start | bytes 110600 | tf_op jit(solution)/shard_map/ppermute | solution.py:1036
  7.9 2.0 %collective-permute-done.2.other_ref = bf16[48,384]{1,0:T(8,128)(2,1)S(1)} collective-permute-done((bf16[48,384]{1,0:T(8,128)(2,1)S(1)}, bf16[48,384]{1,0:T(8,128)(2,1)S(1)}, u32[]{:S(2)}, u32[]{:S(2)}) %collective-permute-start.2) | collective-permute-done | bytes 36896 | tf_op jit(solution)/shard_map/ppermute | solution.py:1036
  9.9 2.1 %collective-permute-start.3 = (bf16[112,512]{1,0:T(8,128)(2,1)S(1)}, bf16[112,512]{1,0:T(8,128)(2,1)S(1)}, u32[]{:S(2)}, u32[]{:S(2)}) collective-permute-start(bf16[112,512]{1,0:T(8,128)(2,1)S(1)} %fill_low.1.refs_1_), channel_id=1, source_target_pairs={{0,8},{2,10},{8,16},{10,18},{16,24},{18,26},{24,28},{26,30},{28,20... | collective-permute-start | bytes 344072 | tf_op jit(solution)/shard_map/ppermute | solution.py:1038
  12.0 6.7 %collective-permute-done.3.refs_2_ = bf16[112,512]{1,0:T(8,128)(2,1)S(1)} collective-permute-done((bf16[112,512]{1,0:T(8,128)(2,1)S(1)}, bf16[112,512]{1,0:T(8,128)(2,1)S(1)}, u32[]{:S(2)}, u32[]{:S(2)}) %collective-permute-start.3) | collective-permute-done | bytes 114720 | tf_op jit(solution)/shard_map/ppermute | solution.py:1038
  18.7 1.5 %collective-permute-done.4.refs_3_ = bf16[112,512]{1,0:T(8,128)(2,1)S(1)} collective-permute-done((bf16[112,512]{1,0:T(8,128)(2,1)S(1)}, bf16[112,512]{1,0:T(8,128)(2,1)S(1)}, u32[]{:S(2)}, u32[]{:S(2)}) %collective-permute-start.4) | collective-permute-done | bytes 114720 | tf_op jit(solution)/shard_map/ppermute | solution.py:1038
  20.4 1.6 %collective-permute-start.5 = (bf16[592,512]{1,0:T(8,128)(2,1)S(1)}, bf16[592,512]{1,0:T(8,128)(2,1)S(1)}, u32[]{:S(2)}, u32[]{:S(2)}) collective-permute-start(bf16[592,512]{1,0:T(8,128)(2,1)S(1)} %get-tuple-element.135.rest_1_), channel_id=1, source_target_pairs={{0,8},{2,10},{8,16},{10,18},{16,24},{18,26},{24,28},{26,30},{28,20... | collective-permute-start | bytes 1818632 | tf_op jit(solution)/shard_map/ppermute | solution.py:925
  22.5 12.2 %collective-permute-done.5.rest_3_ = bf16[592,512]{1,0:T(8,128)(2,1)S(1)} collective-permute-done((bf16[592,512]{1,0:T(8,128)(2,1)S(1)}, bf16[592,512]{1,0:T(8,128)(2,1)S(1)}, u32[]{:S(2)}, u32[]{:S(2)}) %collective-permute-start.5) | collective-permute-done | bytes 606240 | tf_op jit(solution)/shard_map/ppermute | solution.py:925
  34.7 1.3 collective-permute-done.6.rest_4_
  36.0 1.6 %collective-permute-start.7 = (bf16[592,512]{1,0:T(8,128)(2,1)S(1)}, bf16[592,512]{1,0:T(8,128)(2,1)S(1)}, u32[]{:S(2)}, u32[]{:S(2)}) collective-permute-start(bf16[592,512]{1,0:T(8,128)(2,1)S(1)} %collective-permute-done.5.rest_3_), channel_id=1, source_target_pairs={{0,8},{2,10},{8,16},{10,18},{16,24},{18,26},{24,28},{26,30},{28,20... | collective-permute-start | bytes 1818632 | tf_op jit(solution)/shard_map/ppermute | solution.py:925
  38.7 10.3 %collective-permute-done.7.rest_0_.rest_10_ = bf16[592,512]{1,0:T(8,128)(2,1)S(1)} collective-permute-done((bf16[592,512]{1,0:T(8,128)(2,1)S(1)}, bf16[592,512]{1,0:T(8,128)(2,1)S(1)}, u32[]{:S(2)}, u32[]{:S(2)}) %collective-permute-start.7) | collective-permute-done | bytes 606240 | tf_op jit(solution)/shard_map/ppermute | solution.py:925
  49.0 1.3 collective-permute-done.8.rest_1_.rest_11_
  50.9 1.6 %collective-permute-start.9 = (bf16[288,512]{1,0:T(8,128)(2,1)S(1)}, bf16[288,512]{1,0:T(8,128)(2,1)S(1)}, u32[]{:S(2)}, u32[]{:S(2)}) collective-permute-start(bf16[288,512]{1,0:T(8,128)(2,1)S(1)} %slice.87), channel_id=1, source_target_pairs={{0,8},{2,10},{8,16},{10,18},{16,24},{18,26},{24,28},{26,30},{28,20... | collective-permute-start | bytes 884744 | tf_op jit(solution)/shard_map/ppermute | solution.py:925
  53.5 0.8 copy-done.12
  54.4 3.8 %mixer_first.1 = (bf16[6,512,512]{2,1,0:T(8,128)(2,1)S(1)}, bf16[768,384]{1,0:T(8,128)(2,1)S(1)}, bf16[16,16,128]{2,1,0:T(8,128)(2,1)S(1)}, f32[512,768]{1,0:T(8,128)S(1)}) custom-call(s32[16]{0:T(128)S(1)} %pad_add_fusion.where_ref, bf16[512,768]{1,0:T(8,128)(2,1)S(1)} %copy-done, s32[1,512]{1,0:T(1,128)S(1)} %copy-done.5, bf16[592,512]{1,0:T(8,128)(2,1)} %copy-done.2, ...), custom_call_target="tpu_custom_call" | custom-call | flops 1 | bytes 1 | tf_op jit(solution)/shard_map/mixer_first/pallas_call | solution.py:36
  58.2 1.9 %collective-permute-done.9.rest_2_.rest_12_ = bf16[288,512]{1,0:T(8,128)(2,1)S(1)} collective-permute-done((bf16[288,512]{1,0:T(8,128)(2,1)S(1)}, bf16[288,512]{1,0:T(8,128)(2,1)S(1)}, u32[]{:S(2)}, u32[]{:S(2)}) %collective-permute-start.9) | collective-permute-done | bytes 294944 | tf_op jit(solution)/shard_map/ppermute | solution.py:925
  60.7 1.5 %collective-permute-done.18.rest_6_.rest_16_ = bf16[288,512]{1,0:T(8,128)(2,1)S(1)} collective-permute-done((bf16[288,512]{1,0:T(8,128)(2,1)S(1)}, bf16[288,512]{1,0:T(8,128)(2,1)S(1)}, u32[]{:S(2)}, u32[]{:S(2)}) %collective-permute-start.18) | collective-permute-done | bytes 294944 | tf_op jit(solution)/shard_map/ppermute | solution.py:930
  62.2 3.2 %mixer_forward.1 = (bf16[6,512,512]{2,1,0:T(8,128)(2,1)S(1)}, bf16[768,384]{1,0:T(8,128)(2,1)S(1)}, bf16[16,16,128]{2,1,0:T(8,128)(2,1)S(1)}, bf16[512,768]{1,0:...) custom-call(s32[16]{0:T(128)S(1)} %pad_add_fusion.where_ref, ...), custom_call_target="tpu_custom_call", output_to_operand_aliasing={{0}: (2, {}), {1}: (3, {}), {2}: (4, {})} | custom-call | flops 1 | bytes 1 | tf_op jit(solution)/shard_map/mixer_forward/pallas_call | solution.py:36
  65.4 1.6 %collective-permute-start.20 = (bf16[256,384]{1,0:T(8,128)(2,1)S(1)}, bf16[256,384]{1,0:T(8,128)(2,1)S(1)}, u32[]{:S(2)}, u32[]{:S(2)}) collective-permute-start(bf16[256,384]{1,0:T(8,128)(2,1)S(1)} %get-tuple-element.151.own_ref.rest_2_), channel_id=1, source_target_pairs={{0,1},{1,0},{2,3},{3,2},{4,5},{5,4},{6,7},{7,6},{8,9},{9,8},{10,11... | collective-permute-start | bytes 589832 | tf_op jit(solution)/shard_map/ppermute | solution.py:1092
  67.5 5.0 %second_weights.1 = (bf16[6,768,512]{2,1,0:T(8,128)(2,1)S(1)}, bf16[768,768]{1,0:T(8,128)(2,1)S(1)}, f32[512,1536]{1,0:T(8,128)S(1)}, f32[512,768]{1,0:T(8,128)S...) custom-call(s32[16]{0:T(128)S(1)} %pad_add_fusion.where_ref, s32[1]{0:T(128)} %bitcast.second_ref, ...), custom_call_target="tpu_custom_call" | custom-call | flops 1 | bytes 1 | tf_op jit(solution)/shard_map/second_weights/pallas_call | solution.py:36
  72.6 0.7 collective-permute-done.20.other_ref
  73.2 2.7 %ffn_main.2 = (bf16[256,768]{1,0:T(8,128)(2,1)S(1)}, f32[256,768]{1,0:T(8,128)S(1)}, bf16[512,768]{1,0:T(8,128)(2,1)S(1)}, bf16[512,1536]{1,0:T(8,128)(2,1)S(1)}, bf16[512,1536]{1,0:T(8,128)(2,1)S(1)}) custom-call(s32[1]{0:T(128)} %bitcast.second_ref, bf16[512,768]{1,0:T(8,128)(2,1)S(1)} %copy-done, bf16[256,384]{1,0:T(8,128)(2,1)S(1)} %get-tuple-element.151.own_ref.rest_2_, ...), custom_call_target="tpu_custom_call" | custom-call | flops 1 | bytes 1 | tf_op jit(solution)/shard_map/ffn_main/pallas_call | solution.py:36
  76.0 1.6 %collective-permute-start.26 = (bf16[256,768]{1,0:T(8,128)(2,1)S(1)}, bf16[256,768]{1,0:T(8,128)(2,1)S(1)}, u32[]{:S(2)}, u32[]{:S(2)}) collective-permute-start(bf16[256,768]{1,0:T(8,128)(2,1)S(1)} %get-tuple-element.171.back_ref), channel_id=1, source_target_pairs={{0,1},{1,0},{2,3},{3,2},{4,5},{5,4},{6,7},{7,6},{8,9},{9,8},{10,11... | collective-permute-start | bytes 1179656 | tf_op jit(solution)/shard_map/ppermute | solution.py:1100
  77.6 2.7 %ffn_main.3 = (bf16[256,768]{1,0:T(8,128)(2,1)S(1)}, f32[256,768]{1,0:T(8,128)S(1)}, bf16[512,768]{1,0:T(8,128)(2,1)S(1)}, bf16[512,1536]{1,0:T(8,128)(2,1)S(1)}, bf16[512,1536]{1,0:T(8,128)(2,1)S(1)}) custom-call(s32[1]{0:T(128)} %bitcast.second_ref, bf16[512,768]{1,0:T(8,128)(2,1)S(1)} %copy-done, ...), custom_call_target="tpu_custom_call", output_to_operand_aliasing={{2}: (8, {}), {3}: (9, {}), {4}: (10, {})} | custom-call | flops 1 | bytes 1 | tf_op jit(solution)/shard_map/ffn_main/pallas_call | solution.py:36
  80.3 3.6 %ffn_grads.1 = (bf16[8,48,3072]{2,1,0:T(8,128)(2,1)S(1)}, bf16[48,3072]{1,0:T(8,128)(2,1)S(1)}, bf16[48,3072]{1,0:T(8,128)(2,1)S(1)}, bf16[6,48,3072]{2,1,0:T(8,128)(2,1)S(1)}) custom-call(s32[16]{0:T(128)S(1)} %pad_add_fusion.1.where_ref, bf16[512,768]{1,0:T(8,128)(2,1)S(1)} %copy-done.1, bf16[512,768]{1,0:T(8,128)(2,1)S(1)} %get-tuple-element.163.n2_ref, ...), custom_call_target="tpu_custom_call" | custom-call | flops 1 | bytes 1 | tf_op jit(solution)/shard_map/ffn_grads/pallas_call | solution.py:36
  84.5 1.1 collective-permute-done.22
  86.8 1.6 %collective-permute-start.25 = (bf16[48,3072]{1,0:T(8,128)(2,1)S(1)}, bf16[48,3072]{1,0:T(8,128)(2,1)S(1)}, u32[]{:S(2)}, u32[]{:S(2)}) collective-permute-start(bf16[48,3072]{1,0:T(8,128)(2,1)S(1)} %get-tuple-element.255), channel_id=1, source_target_pairs={{0,8},{2,10},{8,16},{10,18},{16,24},{18,26},{24,28},{26,30},{28,20... | collective-permute-start | bytes 884744 | tf_op jit(solution)/shard_map/ppermute | solution.py:978
  88.4 1.3 collective-permute-start.32
  89.7 1.1 resid_back.2
  90.8 0.7 value_first.1.first_ref
  91.5 1.6 %mixer_grads.2 = (bf16[8,272,512]{2,1,0:T(8,128)(2,1)S(1)}, bf16[272,512]{1,0:T(8,128)(2,1)S(1)}, bf16[7,272,512]{2,1,0:T(8,128)(2,1)S(1)}) custom-call(s32[16]{0:T(128)S(1)} %pad_add_fusion.1.where_ref, bf16[256,768]{1,0:T(8,128)(2,1)S(1)} %get-tuple-element.174.xh_ref, bf16[512,768]{1,0:T(8,128)(2,1)S(1)} %get-tuple-element.181.va_ref, ...), custom_call_target="tpu_custom_call" | custom-call | flops 1 | bytes 1 | tf_op jit(solution)/shard_map/mixer_grads/pallas_call | solution.py:36
  93.1 1.7 %ffn_out.1 = (bf16[192,768]{1,0:T(8,128)(2,1)S(1)}, bf16[320,768]{1,0:T(8,128)(2,1)S(1)}) custom-call(bf16[512,1536]{1,0:T(8,128)(2,1)S(1)} %get-tuple-element.176.act_ref, bf16[6,768,512]{2,1,0:T(8,128)(2,1)S(1)} %get-tuple-element.155.w_ref), custom_call_target="tpu_custom_call" | custom-call | flops 1 | bytes 1 | tf_op jit(solution)/shard_map/ffn_out/pallas_call | solution.py:36
  94.8 0.8 collective-permute-done.23
  96.0 0.9 collective-permute-start.28
  96.9 1.2 collective-permute-start.29
  98.1 1.1 collective-permute-done.32.other_ref
  99.2 1.1 resid_back.3
  100.3 1.4 value_back.1
  101.7 1.5 %collective-permute-start.33 = (f32[64,128]{1,0:T(8,128)S(1)}, f32[64,128]{1,0:T(8,128)S(1)}, u32[]{:S(2)}, u32[]{:S(2)}) collective-permute-start(f32[64,128]{1,0:T(8,128)S(1)} %get-tuple-element.204.ga_ref), channel_id=1, source_target_pairs={{0,1},{1,0},{2,3},{3,2},{4,5},{5,4},{6,7},{7,6},{8,9},{9,8},{10,11... | collective-permute-start | bytes 98312 | tf_op jit(solution)/shard_map/ppermute | solution.py:1124
  105.0 1.5 %collective-permute-start.30 = (bf16[48,3072]{1,0:T(8,128)(2,1)S(1)}, bf16[48,3072]{1,0:T(8,128)(2,1)S(1)}, u32[]{:S(2)}, u32[]{:S(2)}) collective-permute-start(bf16[48,3072]{1,0:T(8,128)(2,1)S(1)} %get-tuple-element.252), channel_id=1, source_target_pairs={{0,4},{2,6},{8,0},{10,2},{16,8},{18,10},{24,16},{26,18},{28,24},{3... | collective-permute-start | bytes 884744 | tf_op jit(solution)/shard_map/ppermute | solution.py:978
  107.1 1.4 mixer_grads.3
  108.5 1.7 %weight_grads.1 = (bf16[8,272,512]{2,1,0:T(8,128)(2,1)S(1)}, bf16[272,512]{1,0:T(8,128)(2,1)S(1)}, bf16[7,272,512]{2,1,0:T(8,128)(2,1)S(1)}) custom-call(s32[16]{0:T(128)S(1)} %pad_add_fusion.1.where_ref, bf16[512,768]{1,0:T(8,128)(2,1)S(1)} %get-tuple-element.192.n1_ref, ...), custom_call_target="tpu_custom_call", output_to_operand_aliasing={{0}: (10, {}), {1}: (11, {}), {2}: (12, {})} | custom-call | flops 1 | bytes 1 | tf_op jit(solution)/shard_map/weight_grads/pallas_call | solution.py:36
  110.3 1.0 collective-permute-done.35
  112.1 1.2 collective-permute-done.31.up_ref
  114.2 1.5 collective-permute-start.36
  115.7 1.7 %collective-permute-start.41 = (bf16[320,768]{1,0:T(8,128)(2,1)S(1)}, bf16[320,768]{1,0:T(8,128)(2,1)S(1)}, u32[]{:S(2)}, u32[]{:S(2)}) collective-permute-start(bf16[320,768]{1,0:T(8,128)(2,1)S(1)} %get-tuple-element.214), channel_id=1, source_target_pairs={{0,1},{1,0},{2,3},{3,2},{4,5},{5,4},{6,7},{7,6},{8,9},{9,8},{10,11... | collective-permute-start | bytes 1474568 | tf_op jit(solution)/shard_map/ppermute | solution.py:1141
  117.4 5.1 %collective-permute-done.38 = bf16[272,512]{1,0:T(8,128)(2,1)S(1)} collective-permute-done((bf16[272,512]{1,0:T(8,128)(2,1)S(1)}, bf16[272,512]{1,0:T(8,128)(2,1)S(1)}, u32[]{:S(2)}, u32[]{:S(2)}) %collective-permute-start.38) | collective-permute-done | bytes 278560 | tf_op jit(solution)/shard_map/ppermute | solution.py:978
  122.6 1.6 %collective-permute-start.40 = (bf16[272,512]{1,0:T(8,128)(2,1)S(1)}, bf16[272,512]{1,0:T(8,128)(2,1)S(1)}, u32[]{:S(2)}, u32[]{:S(2)}) collective-permute-start(bf16[272,512]{1,0:T(8,128)(2,1)S(1)} %fusion.14), channel_id=1, source_target_pairs={{0,4},{2,6},{8,0},{10,2},{16,8},{18,10},{24,16},{26,18},{28,24},{3... | collective-permute-start | bytes 835592 | tf_op jit(solution)/shard_map/ppermute | solution.py:978
  124.8 1.7 %collective-permute-start.45 = (bf16[256,768]{1,0:T(8,128)(2,1)S(1)}, bf16[256,768]{1,0:T(8,128)(2,1)S(1)}, u32[]{:S(2)}, u32[]{:S(2)}) collective-permute-start(bf16[256,768]{1,0:T(8,128)(2,1)S(1)} %get-tuple-element.229.mine_ref), channel_id=1, source_target_pairs={{0,1},{1,0},{2,3},{3,2},{4,5},{5,4},{6,7},{7,6},{8,9},{9,8},{10,11... | collective-permute-start | bytes 1179656 | tf_op jit(solution)/shard_map/ppermute | solution.py:1147
  126.6 3.2 %collective-permute-done.41 = bf16[320,768]{1,0:T(8,128)(2,1)S(1)} collective-permute-done((bf16[320,768]{1,0:T(8,128)(2,1)S(1)}, bf16[320,768]{1,0:T(8,128)(2,1)S(1)}, u32[]{:S(2)}, u32[]{:S(2)}) %collective-permute-start.41) | collective-permute-done | bytes 491552 | tf_op jit(solution)/shard_map/ppermute | solution.py:1141
  129.8 1.1 collective-permute-done.40
  130.9 1.5 collective-permute-done.39
  133.0 1.6 %collective-permute-start.44 = (bf16[272,512]{1,0:T(8,128)(2,1)S(1)}, bf16[272,512]{1,0:T(8,128)(2,1)S(1)}, u32[]{:S(2)}, u32[]{:S(2)}) collective-permute-start(bf16[272,512]{1,0:T(8,128)(2,1)S(1)} %get-tuple-element.249), channel_id=1, source_target_pairs={{0,4},{2,6},{8,0},{10,2},{16,8},{18,10},{24,16},{26,18},{28,24},{3... | collective-permute-start | bytes 835592 | tf_op jit(solution)/shard_map/ppermute | solution.py:978
  134.6 1.8 %collective-permute-start.42 = (bf16[256,768]{1,0:T(8,128)(2,1)S(1)}, bf16[256,768]{1,0:T(8,128)(2,1)S(1)}, u32[]{:S(2)}, u32[]{:S(2)}) collective-permute-start(bf16[256,768]{1,0:T(8,128)(2,1)S(1)} %get-tuple-element.227.mine_ref), channel_id=1, source_target_pairs={{0,1},{1,0},{2,3},{3,2},{4,5},{5,4},{6,7},{7,6},{8,9},{9,8},{10,11... | collective-permute-start | bytes 1179656 | tf_op jit(solution)/shard_map/ppermute | solution.py:1150
  136.4 1.8 %collective-permute-done.45.other_ref = bf16[256,768]{1,0:T(8,128)(2,1)S(1)} collective-permute-done((bf16[256,768]{1,0:T(8,128)(2,1)S(1)}, bf16[256,768]{1,0:T(8,128)(2,1)S(1)}, u32[]{:S(2)}, u32[]{:S(2)}) %collective-permute-start.45) | collective-permute-done | bytes 393248 | tf_op jit(solution)/shard_map/ppermute | solution.py:1147
  138.2 1.4 collective-permute-done.43
  140.6 1.4 collective-permute-start.47
  142.1 0.9 ffn_result.1
  143.0 1.2 fusion
  144.2 1.2 token_grads.2.rest_0_
  145.6 1.2 token_grads.3
  147.2 0.9 mixer_result.1
  (99 shorter events, 13.9 us)
Async XLA Ops:
  2.0 18.2 %collective-permute-start = (bf16[480,512]{1,0:T(8,128)(2,1)S(1)}, bf16[480,512]{1,0:T(8,128)(2,1)S(1)}, u32[]{:S(2)}, u32[]{:S(2)}) collective-permute-start(bf16[480,512]{1,0:T(8,128)(2,1)S(1)} %get-tuple-element.127.refs_0_), channel_id=1, source_target_pairs={{0,8},{2,10},{8,16},{10,18},{16,24},{18,26},{24,28},{26,30},{28,20... | collective-permute-start | bytes 1474568 | tf_op jit(solution)/shard_map/ppermute | solution.py:1035
  5.1 15.1 %collective-permute-start.1 = (bf16[480,512]{1,0:T(8,128)(2,1)S(1)}, bf16[480,512]{1,0:T(8,128)(2,1)S(1)}, u32[]{:S(2)}, u32[]{:S(2)}) collective-permute-start(bf16[480,512]{1,0:T(8,128)(2,1)S(1)} %get-tuple-element.127.refs_0_), channel_id=1, source_target_pairs={{0,4},{2,6},{8,0},{10,2},{16,8},{18,10},{24,16},{26,18},{28,24},{3... | collective-permute-start | bytes 1474568 | tf_op jit(solution)/shard_map/ppermute | solution.py:1035
  6.0 4.0 %collective-permute-start.2 = (bf16[48,384]{1,0:T(8,128)(2,1)S(1)}, bf16[48,384]{1,0:T(8,128)(2,1)S(1)}, u32[]{:S(2)}, u32[]{:S(2)}) collective-permute-start(bf16[48,384]{1,0:T(8,128)(2,1)S(1)} %get-tuple-element.130), channel_id=1, source_target_pairs={{0,1},{1,0},{2,3},{3,2},{4,5},{5,4},{6,7},{7,6},{8,9},{9,8},{10,11... | collective-permute-start | bytes 110600 | tf_op jit(solution)/shard_map/ppermute | solution.py:1036
  9.9 44.4 %copy-start = (bf16[512,768]{1,0:T(8,128)(2,1)S(1)}, bf16[512,768]{1,0:T(8,128)(2,1)}, u32[]{:S(2)}) copy-start(bf16[512,768]{1,0:T(8,128)(2,1)} %tok_ref.11) | copy-start | bytes 2359300
  9.9 44.4 %copy-start.5 = (s32[1,512]{1,0:T(1,128)S(1)}, s32[1,512]{1,0:T(1,128)}, u32[]{:S(2)}) copy-start(s32[1,512]{1,0:T(1,128)} %seg_ref.3) | copy-start | bytes 6148
  9.9 8.8 %collective-permute-start.3 = (bf16[112,512]{1,0:T(8,128)(2,1)S(1)}, bf16[112,512]{1,0:T(8,128)(2,1)S(1)}, u32[]{:S(2)}, u32[]{:S(2)}) collective-permute-start(bf16[112,512]{1,0:T(8,128)(2,1)S(1)} %fill_low.1.refs_1_), channel_id=1, source_target_pairs={{0,8},{2,10},{8,16},{10,18},{16,24},{18,26},{24,28},{26,30},{28,20... | collective-permute-start | bytes 344072 | tf_op jit(solution)/shard_map/ppermute | solution.py:1038
  12.0 8.2 %collective-permute-start.4 = (bf16[112,512]{1,0:T(8,128)(2,1)S(1)}, bf16[112,512]{1,0:T(8,128)(2,1)S(1)}, u32[]{:S(2)}, u32[]{:S(2)}) collective-permute-start(bf16[112,512]{1,0:T(8,128)(2,1)S(1)} %fill_low.1.refs_1_), channel_id=1, source_target_pairs={{0,4},{2,6},{8,0},{10,2},{16,8},{18,10},{24,16},{26,18},{28,24},{3... | collective-permute-start | bytes 344072 | tf_op jit(solution)/shard_map/ppermute | solution.py:1038
  20.3 32.7 %copy-start.3 = (bf16[592,512]{1,0:T(8,128)(2,1)}, bf16[592,512]{1,0:T(8,128)(2,1)S(1)}, u32[]{:S(2)}) copy-start(bf16[592,512]{1,0:T(8,128)(2,1)S(1)} %get-tuple-element.135.rest_1_) | copy-start | bytes 1818628
  20.4 32.7 %copy-start.4 = (bf16[592,512]{1,0:T(8,128)(2,1)}, bf16[592,512]{1,0:T(8,128)(2,1)S(1)}, u32[]{:S(2)}) copy-start(bf16[592,512]{1,0:T(8,128)(2,1)S(1)} %get-tuple-element.136.rest_2_) | copy-start | bytes 1818628
  20.4 14.3 %collective-permute-start.5 = (bf16[592,512]{1,0:T(8,128)(2,1)S(1)}, bf16[592,512]{1,0:T(8,128)(2,1)S(1)}, u32[]{:S(2)}, u32[]{:S(2)}) collective-permute-start(bf16[592,512]{1,0:T(8,128)(2,1)S(1)} %get-tuple-element.135.rest_1_), channel_id=1, source_target_pairs={{0,8},{2,10},{8,16},{10,18},{16,24},{18,26},{24,28},{26,30},{28,20... | collective-permute-start | bytes 1818632 | tf_op jit(solution)/shard_map/ppermute | solution.py:925
  22.0 13.9 %collective-permute-start.6 = (bf16[592,512]{1,0:T(8,128)(2,1)S(1)}, bf16[592,512]{1,0:T(8,128)(2,1)S(1)}, u32[]{:S(2)}, u32[]{:S(2)}) collective-permute-start(bf16[592,512]{1,0:T(8,128)(2,1)S(1)} %get-tuple-element.136.rest_2_), channel_id=1, source_target_pairs={{0,4},{2,6},{8,0},{10,2},{16,8},{18,10},{24,16},{26,18},{28,24},{3... | collective-permute-start | bytes 1818632 | tf_op jit(solution)/shard_map/ppermute | solution.py:925
  34.7 18.4 %copy-start.6 = (bf16[592,512]{1,0:T(8,128)(2,1)}, bf16[592,512]{1,0:T(8,128)(2,1)S(1)}, u32[]{:S(2)}) copy-start(bf16[592,512]{1,0:T(8,128)(2,1)S(1)} %collective-permute-done.5.rest_3_) | copy-start | bytes 1818628
  36.0 17.1 %copy-start.7 = (bf16[592,512]{1,0:T(8,128)(2,1)}, bf16[592,512]{1,0:T(8,128)(2,1)S(1)}, u32[]{:S(2)}) copy-start(bf16[592,512]{1,0:T(8,128)(2,1)S(1)} %collective-permute-done.6.rest_4_) | copy-start | bytes 1818628
  36.0 13.0 %collective-permute-start.7 = (bf16[592,512]{1,0:T(8,128)(2,1)S(1)}, bf16[592,512]{1,0:T(8,128)(2,1)S(1)}, u32[]{:S(2)}, u32[]{:S(2)}) collective-permute-start(bf16[592,512]{1,0:T(8,128)(2,1)S(1)} %collective-permute-done.5.rest_3_), channel_id=1, source_target_pairs={{0,8},{2,10},{8,16},{10,18},{16,24},{18,26},{24,28},{26,30},{28,20... | collective-permute-start | bytes 1818632 | tf_op jit(solution)/shard_map/ppermute | solution.py:925
  37.5 12.7 %collective-permute-start.8 = (bf16[592,512]{1,0:T(8,128)(2,1)S(1)}, bf16[592,512]{1,0:T(8,128)(2,1)S(1)}, u32[]{:S(2)}, u32[]{:S(2)}) collective-permute-start(bf16[592,512]{1,0:T(8,128)(2,1)S(1)} %collective-permute-done.6.rest_4_), channel_id=1, source_target_pairs={{0,4},{2,6},{8,0},{10,2},{16,8},{18,10},{24,16},{26,18},{28,24},{3... | collective-permute-start | bytes 1818632 | tf_op jit(solution)/shard_map/ppermute | solution.py:925
  38.0 15.0 %copy-start.2 = (bf16[592,512]{1,0:T(8,128)(2,1)}, bf16[592,512]{1,0:T(8,128)(2,1)S(1)}, u32[]{:S(2)}) copy-start(bf16[592,512]{1,0:T(8,128)(2,1)S(1)} %join_units.3.rest_0_) | copy-start | bytes 1818628
  38.0 12.3 %collective-permute-start.11 = (bf16[592,512]{1,0:T(8,128)(2,1)S(1)}, bf16[592,512]{1,0:T(8,128)(2,1)S(1)}, u32[]{:S(2)}, u32[]{:S(2)}) collective-permute-start(bf16[592,512]{1,0:T(8,128)(2,1)S(1)} %join_units.3.rest_0_), channel_id=1, source_target_pairs={{0,2},{2,0},{4,6},{6,4},{8,10},{10,8},{12,14},{14,12},{16,18},{18,... | collective-permute-start | bytes 1818632 | tf_op jit(solution)/shard_map/ppermute | solution.py:930
  38.1 12.7 %collective-permute-start.12 = (bf16[592,512]{1,0:T(8,128)(2,1)S(1)}, bf16[592,512]{1,0:T(8,128)(2,1)S(1)}, u32[]{:S(2)}, u32[]{:S(2)}) collective-permute-start(bf16[592,512]{1,0:T(8,128)(2,1)S(1)} %get-tuple-element.135.rest_1_), channel_id=1, source_target_pairs={{0,2},{2,0},{4,6},{6,4},{8,10},{10,8},{12,14},{14,12},{16,18},{18,... | collective-permute-start | bytes 1818632 | tf_op jit(solution)/shard_map/ppermute | solution.py:930
  38.6 13.9 %collective-permute-start.13 = (bf16[592,512]{1,0:T(8,128)(2,1)S(1)}, bf16[592,512]{1,0:T(8,128)(2,1)S(1)}, u32[]{:S(2)}, u32[]{:S(2)}) collective-permute-start(bf16[592,512]{1,0:T(8,128)(2,1)S(1)} %get-tuple-element.136.rest_2_), channel_id=1, source_target_pairs={{0,2},{2,0},{4,6},{6,4},{8,10},{10,8},{12,14},{14,12},{16,18},{18,... | collective-permute-start | bytes 1818632 | tf_op jit(solution)/shard_map/ppermute | solution.py:930
  49.0 3.5 %collective-permute-start.14 = (bf16[592,512]{1,0:T(8,128)(2,1)S(1)}, bf16[592,512]{1,0:T(8,128)(2,1)S(1)}, u32[]{:S(2)}, u32[]{:S(2)}) collective-permute-start(bf16[592,512]{1,0:T(8,128)(2,1)S(1)} %collective-permute-done.5.rest_3_), channel_id=1, source_target_pairs={{0,2},{2,0},{4,6},{6,4},{8,10},{10,8},{12,14},{14,12},{16,18},{18,... | collective-permute-start | bytes 1818632 | tf_op jit(solution)/shard_map/ppermute | solution.py:930
  50.3 2.7 %collective-permute-start.15 = (bf16[592,512]{1,0:T(8,128)(2,1)S(1)}, bf16[592,512]{1,0:T(8,128)(2,1)S(1)}, u32[]{:S(2)}, u32[]{:S(2)}) collective-permute-start(bf16[592,512]{1,0:T(8,128)(2,1)S(1)} %collective-permute-done.6.rest_4_), channel_id=1, source_target_pairs={{0,2},{2,0},{4,6},{6,4},{8,10},{10,8},{12,14},{14,12},{16,18},{18,... | collective-permute-start | bytes 1818632 | tf_op jit(solution)/shard_map/ppermute | solution.py:930
  50.3 2.8 %copy-start.8 = (bf16[592,512]{1,0:T(8,128)(2,1)}, bf16[592,512]{1,0:T(8,128)(2,1)S(1)}, u32[]{:S(2)}) copy-start(bf16[592,512]{1,0:T(8,128)(2,1)S(1)} %collective-permute-done.11.rest_5_) | copy-start | bytes 1818628
  50.3 9.8 %collective-permute-start.10 = (bf16[304,512]{1,0:T(8,128)(2,1)S(1)}, bf16[304,512]{1,0:T(8,128)(2,1)S(1)}, u32[]{:S(2)}, u32[]{:S(2)}) collective-permute-start(bf16[304,512]{1,0:T(8,128)(2,1)S(1)} %slice.88), channel_id=1, source_target_pairs={{0,4},{2,6},{8,0},{10,2},{16,8},{18,10},{24,16},{26,18},{28,24},{3... | collective-permute-start | bytes 933896 | tf_op jit(solution)/shard_map/ppermute | solution.py:925
  50.9 2.2 %copy-start.9 = (bf16[592,512]{1,0:T(8,128)(2,1)}, bf16[592,512]{1,0:T(8,128)(2,1)S(1)}, u32[]{:S(2)}) copy-start(bf16[592,512]{1,0:T(8,128)(2,1)S(1)} %collective-permute-done.12.rest_6_) | copy-start | bytes 1818628
  50.9 9.2 %collective-permute-start.9 = (bf16[288,512]{1,0:T(8,128)(2,1)S(1)}, bf16[288,512]{1,0:T(8,128)(2,1)S(1)}, u32[]{:S(2)}, u32[]{:S(2)}) collective-permute-start(bf16[288,512]{1,0:T(8,128)(2,1)S(1)} %slice.87), channel_id=1, source_target_pairs={{0,8},{2,10},{8,16},{10,18},{16,24},{18,26},{24,28},{26,30},{28,20... | collective-permute-start | bytes 884744 | tf_op jit(solution)/shard_map/ppermute | solution.py:925
  52.5 0.8 copy-start.10
  52.5 9.7 %collective-permute-start.16 = (bf16[592,512]{1,0:T(8,128)(2,1)S(1)}, bf16[592,512]{1,0:T(8,128)(2,1)S(1)}, u32[]{:S(2)}, u32[]{:S(2)}) collective-permute-start(bf16[592,512]{1,0:T(8,128)(2,1)S(1)} %collective-permute-done.7.rest_0_.rest_10_), channel_id=1, source_target_pairs={{0,2},{2,0},{4,6},{6,4},{8,10},{10,8},{12,14},{14,12},{16,18},{18,... | collective-permute-start | bytes 1818632 | tf_op jit(solution)/shard_map/ppermute | solution.py:930
  52.5 1.0 copy-start.11
  52.5 9.7 %collective-permute-start.17 = (bf16[592,512]{1,0:T(8,128)(2,1)S(1)}, bf16[592,512]{1,0:T(8,128)(2,1)S(1)}, u32[]{:S(2)}, u32[]{:S(2)}) collective-permute-start(bf16[592,512]{1,0:T(8,128)(2,1)S(1)} %collective-permute-done.8.rest_1_.rest_11_), channel_id=1, source_target_pairs={{0,2},{2,0},{4,6},{6,4},{8,10},{10,8},{12,14},{14,12},{16,18},{18,... | collective-permute-start | bytes 1818632 | tf_op jit(solution)/shard_map/ppermute | solution.py:930
  53.5 0.8 copy-start.12
  60.2 7.4 %copy-start.1 = (bf16[512,768]{1,0:T(8,128)(2,1)S(1)}, bf16[512,768]{1,0:T(8,128)(2,1)}, u32[]{:S(2)}) copy-start(bf16[512,768]{1,0:T(8,128)(2,1)} %cot_ref.6) | copy-start | bytes 2359300
  60.2 2.0 %collective-permute-start.19 = (bf16[304,512]{1,0:T(8,128)(2,1)S(1)}, bf16[304,512]{1,0:T(8,128)(2,1)S(1)}, u32[]{:S(2)}, u32[]{:S(2)}) collective-permute-start(bf16[304,512]{1,0:T(8,128)(2,1)S(1)} %collective-permute-done.10.rest_3_.rest_13_), channel_id=1, source_target_pairs={{0,2},{2,0},{4,6},{6,4},{8,10},{10,8},{12,14},{14,12},{16,18},{18,... | collective-permute-start | bytes 933896 | tf_op jit(solution)/shard_map/ppermute | solution.py:930
  60.2 2.0 %collective-permute-start.18 = (bf16[288,512]{1,0:T(8,128)(2,1)S(1)}, bf16[288,512]{1,0:T(8,128)(2,1)S(1)}, u32[]{:S(2)}, u32[]{:S(2)}) collective-permute-start(bf16[288,512]{1,0:T(8,128)(2,1)S(1)} %collective-permute-done.9.rest_2_.rest_12_), channel_id=1, source_target_pairs={{0,2},{2,0},{4,6},{6,4},{8,10},{10,8},{12,14},{14,12},{16,18},{18,... | collective-permute-start | bytes 884744 | tf_op jit(solution)/shard_map/ppermute | solution.py:930
  65.4 7.8 %collective-permute-start.20 = (bf16[256,384]{1,0:T(8,128)(2,1)S(1)}, bf16[256,384]{1,0:T(8,128)(2,1)S(1)}, u32[]{:S(2)}, u32[]{:S(2)}) collective-permute-start(bf16[256,384]{1,0:T(8,128)(2,1)S(1)} %get-tuple-element.151.own_ref.rest_2_), channel_id=1, source_target_pairs={{0,1},{1,0},{2,3},{3,2},{4,5},{5,4},{6,7},{7,6},{8,9},{9,8},{10,11... | collective-permute-start | bytes 589832 | tf_op jit(solution)/shard_map/ppermute | solution.py:1092
  67.0 10.5 %collective-permute-start.21 = (bf16[256,384]{1,0:T(8,128)(2,1)S(1)}, bf16[256,384]{1,0:T(8,128)(2,1)S(1)}, u32[]{:S(2)}, u32[]{:S(2)}) collective-permute-start(bf16[256,384]{1,0:T(8,128)(2,1)S(1)} %get-tuple-element.158.own_ref.rest_3_), channel_id=1, source_target_pairs={{0,1},{1,0},{2,3},{3,2},{4,5},{5,4},{6,7},{7,6},{8,9},{9,8},{10,11... | collective-permute-start | bytes 589832 | tf_op jit(solution)/shard_map/ppermute | solution.py:1092
  76.0 10.0 %collective-permute-start.26 = (bf16[256,768]{1,0:T(8,128)(2,1)S(1)}, bf16[256,768]{1,0:T(8,128)(2,1)S(1)}, u32[]{:S(2)}, u32[]{:S(2)}) collective-permute-start(bf16[256,768]{1,0:T(8,128)(2,1)S(1)} %get-tuple-element.171.back_ref), channel_id=1, source_target_pairs={{0,1},{1,0},{2,3},{3,2},{4,5},{5,4},{6,7},{7,6},{8,9},{9,8},{10,11... | collective-permute-start | bytes 1179656 | tf_op jit(solution)/shard_map/ppermute | solution.py:1100
  83.9 1.6 %collective-permute-start.22 = (bf16[48,3072]{1,0:T(8,128)(2,1)S(1)}, bf16[48,3072]{1,0:T(8,128)(2,1)S(1)}, u32[]{:S(2)}, u32[]{:S(2)}) collective-permute-start(bf16[48,3072]{1,0:T(8,128)(2,1)S(1)} %get-tuple-element.167), channel_id=1, source_target_pairs={{0,2},{2,0},{4,6},{6,4},{8,10},{10,8},{12,14},{14,12},{16,18},{18,... | collective-permute-start | bytes 884744 | tf_op jit(solution)/shard_map/ppermute | solution.py:950
  84.0 2.0 %collective-permute-start.24 = (bf16[48,3072]{1,0:T(8,128)(2,1)S(1)}, bf16[48,3072]{1,0:T(8,128)(2,1)S(1)}, u32[]{:S(2)}, u32[]{:S(2)}) collective-permute-start(bf16[48,3072]{1,0:T(8,128)(2,1)S(1)} %get-tuple-element.168), channel_id=1, source_target_pairs={{0,2},{2,0},{4,6},{6,4},{8,10},{10,8},{12,14},{14,12},{16,18},{18,... | collective-permute-start | bytes 884744 | tf_op jit(solution)/shard_map/ppermute | solution.py:950
  86.0 9.8 %collective-permute-start.27 = (bf16[6,48,3072]{2,1,0:T(8,128)(2,1)S(1)}, bf16[6,48,3072]{2,1,0:T(8,128)(2,1)S(1)}, u32[]{:S(2)}, u32[]{:S(2)}) collective-permute-start(bf16[6,48,3072]{2,1,0:T(8,128)(2,1)S(1)} %get-tuple-element.187), channel_id=1, source_target_pairs={{0,2},{2,0},{4,6},{6,4},{8,10},{10,8},{12,14},{14,12},{16,18},{18,... | collective-permute-start | bytes 5308424 | tf_op jit(solution)/shard_map/ppermute | solution.py:969
  86.3 9.3 %collective-permute-start.23 = (bf16[48,3072]{1,0:T(8,128)(2,1)S(1)}, bf16[48,3072]{1,0:T(8,128)(2,1)S(1)}, u32[]{:S(2)}, u32[]{:S(2)}) collective-permute-start(bf16[48,3072]{1,0:T(8,128)(2,1)S(1)} %get-tuple-element.256), channel_id=1, source_target_pairs={{0,4},{2,6},{8,0},{10,2},{16,8},{18,10},{24,16},{26,18},{28,24},{3... | collective-permute-start | bytes 884744 | tf_op jit(solution)/shard_map/ppermute | solution.py:978
  86.8 9.0 %collective-permute-start.25 = (bf16[48,3072]{1,0:T(8,128)(2,1)S(1)}, bf16[48,3072]{1,0:T(8,128)(2,1)S(1)}, u32[]{:S(2)}, u32[]{:S(2)}) collective-permute-start(bf16[48,3072]{1,0:T(8,128)(2,1)S(1)} %get-tuple-element.255), channel_id=1, source_target_pairs={{0,8},{2,10},{8,16},{10,18},{16,24},{18,26},{24,28},{26,30},{28,20... | collective-permute-start | bytes 884744 | tf_op jit(solution)/shard_map/ppermute | solution.py:978
  88.4 10.8 %collective-permute-start.32 = (bf16[256,768]{1,0:T(8,128)(2,1)S(1)}, bf16[256,768]{1,0:T(8,128)(2,1)S(1)}, u32[]{:S(2)}, u32[]{:S(2)}) collective-permute-start(bf16[256,768]{1,0:T(8,128)(2,1)S(1)} %get-tuple-element.199.back_ref), channel_id=1, source_target_pairs={{0,1},{1,0},{2,3},{3,2},{4,5},{5,4},{6,7},{7,6},{8,9},{9,8},{10,11... | collective-permute-start | bytes 1179656 | tf_op jit(solution)/shard_map/ppermute | solution.py:1100
  96.0 8.4 %collective-permute-start.28 = (bf16[48,3072]{1,0:T(8,128)(2,1)S(1)}, bf16[48,3072]{1,0:T(8,128)(2,1)S(1)}, u32[]{:S(2)}, u32[]{:S(2)}) collective-permute-start(bf16[48,3072]{1,0:T(8,128)(2,1)S(1)} %get-tuple-element.254), channel_id=1, source_target_pairs={{0,4},{2,6},{8,0},{10,2},{16,8},{18,10},{24,16},{26,18},{28,24},{3... | collective-permute-start | bytes 884744 | tf_op jit(solution)/shard_map/ppermute | solution.py:978
  96.9 8.0 %collective-permute-start.29 = (bf16[48,3072]{1,0:T(8,128)(2,1)S(1)}, bf16[48,3072]{1,0:T(8,128)(2,1)S(1)}, u32[]{:S(2)}, u32[]{:S(2)}) collective-permute-start(bf16[48,3072]{1,0:T(8,128)(2,1)S(1)} %get-tuple-element.253), channel_id=1, source_target_pairs={{0,8},{2,10},{8,16},{10,18},{16,24},{18,26},{24,28},{26,30},{28,20... | collective-permute-start | bytes 884744 | tf_op jit(solution)/shard_map/ppermute | solution.py:978
  101.7 6.8 %collective-permute-start.33 = (f32[64,128]{1,0:T(8,128)S(1)}, f32[64,128]{1,0:T(8,128)S(1)}, u32[]{:S(2)}, u32[]{:S(2)}) collective-permute-start(f32[64,128]{1,0:T(8,128)S(1)} %get-tuple-element.204.ga_ref), channel_id=1, source_target_pairs={{0,1},{1,0},{2,3},{3,2},{4,5},{5,4},{6,7},{7,6},{8,9},{9,8},{10,11... | collective-permute-start | bytes 98312 | tf_op jit(solution)/shard_map/ppermute | solution.py:1124
  103.3 8.1 %collective-permute-start.35 = (bf16[192,768]{1,0:T(8,128)(2,1)S(1)}, bf16[192,768]{1,0:T(8,128)(2,1)S(1)}, u32[]{:S(2)}, u32[]{:S(2)}) collective-permute-start(bf16[192,768]{1,0:T(8,128)(2,1)S(1)} %get-tuple-element.212), channel_id=1, source_target_pairs={{0,1},{1,0},{2,3},{3,2},{4,5},{5,4},{6,7},{7,6},{8,9},{9,8},{10,11... | collective-permute-start | bytes 884744 | tf_op jit(solution)/shard_map/ppermute | solution.py:1125
  105.0 7.1 %collective-permute-start.30 = (bf16[48,3072]{1,0:T(8,128)(2,1)S(1)}, bf16[48,3072]{1,0:T(8,128)(2,1)S(1)}, u32[]{:S(2)}, u32[]{:S(2)}) collective-permute-start(bf16[48,3072]{1,0:T(8,128)(2,1)S(1)} %get-tuple-element.252), channel_id=1, source_target_pairs={{0,4},{2,6},{8,0},{10,2},{16,8},{18,10},{24,16},{26,18},{28,24},{3... | collective-permute-start | bytes 884744 | tf_op jit(solution)/shard_map/ppermute | solution.py:978
  106.6 6.7 %collective-permute-start.31 = (bf16[48,3072]{1,0:T(8,128)(2,1)S(1)}, bf16[48,3072]{1,0:T(8,128)(2,1)S(1)}, u32[]{:S(2)}, u32[]{:S(2)}) collective-permute-start(bf16[48,3072]{1,0:T(8,128)(2,1)S(1)} %get-tuple-element.251), channel_id=1, source_target_pairs={{0,8},{2,10},{8,16},{10,18},{16,24},{18,26},{24,28},{26,30},{28,20... | collective-permute-start | bytes 884744 | tf_op jit(solution)/shard_map/ppermute | solution.py:978
  110.2 1.6 %collective-permute-start.34 = (bf16[272,512]{1,0:T(8,128)(2,1)S(1)}, bf16[272,512]{1,0:T(8,128)(2,1)S(1)}, u32[]{:S(2)}, u32[]{:S(2)}) collective-permute-start(bf16[272,512]{1,0:T(8,128)(2,1)S(1)} %get-tuple-element.211), channel_id=1, source_target_pairs={{0,2},{2,0},{4,6},{6,4},{8,10},{10,8},{12,14},{14,12},{16,18},{18,... | collective-permute-start | bytes 835592 | tf_op jit(solution)/shard_map/ppermute | solution.py:950
  113.4 9.1 %collective-permute-start.37 = (bf16[7,272,512]{2,1,0:T(8,128)(2,1)S(1)}, bf16[7,272,512]{2,1,0:T(8,128)(2,1)S(1)}, u32[]{:S(2)}, u32[]{:S(2)}) collective-permute-start(bf16[7,272,512]{2,1,0:T(8,128)(2,1)S(1)} %get-tuple-element.221), channel_id=1, source_target_pairs={{0,2},{2,0},{4,6},{6,4},{8,10},{10,8},{12,14},{14,12},{16,18},{18,... | collective-permute-start | bytes 5849096 | tf_op jit(solution)/shard_map/ppermute | solution.py:969
  113.4 9.1 %collective-permute-start.38 = (bf16[272,512]{1,0:T(8,128)(2,1)S(1)}, bf16[272,512]{1,0:T(8,128)(2,1)S(1)}, u32[]{:S(2)}, u32[]{:S(2)}) collective-permute-start(bf16[272,512]{1,0:T(8,128)(2,1)S(1)} %fusion.8), channel_id=1, source_target_pairs={{0,8},{2,10},{8,16},{10,18},{16,24},{18,26},{24,28},{26,30},{28,20... | collective-permute-start | bytes 835592 | tf_op jit(solution)/shard_map/ppermute | solution.py:978
  114.2 12.4 %collective-permute-start.36 = (bf16[48,3072]{1,0:T(8,128)(2,1)S(1)}, bf16[48,3072]{1,0:T(8,128)(2,1)S(1)}, u32[]{:S(2)}, u32[]{:S(2)}) collective-permute-start(bf16[48,3072]{1,0:T(8,128)(2,1)S(1)} %fusion.3), channel_id=1, source_target_pairs={{0,4},{2,6},{8,0},{10,2},{16,8},{18,10},{24,16},{26,18},{28,24},{3... | collective-permute-start | bytes 884744 | tf_op jit(solution)/shard_map/ppermute | solution.py:978
  115.7 14.1 %collective-permute-start.41 = (bf16[320,768]{1,0:T(8,128)(2,1)S(1)}, bf16[320,768]{1,0:T(8,128)(2,1)S(1)}, u32[]{:S(2)}, u32[]{:S(2)}) collective-permute-start(bf16[320,768]{1,0:T(8,128)(2,1)S(1)} %get-tuple-element.214), channel_id=1, source_target_pairs={{0,1},{1,0},{2,3},{3,2},{4,5},{5,4},{6,7},{7,6},{8,9},{9,8},{10,11... | collective-permute-start | bytes 1474568 | tf_op jit(solution)/shard_map/ppermute | solution.py:1141
  122.6 8.3 %collective-permute-start.40 = (bf16[272,512]{1,0:T(8,128)(2,1)S(1)}, bf16[272,512]{1,0:T(8,128)(2,1)S(1)}, u32[]{:S(2)}, u32[]{:S(2)}) collective-permute-start(bf16[272,512]{1,0:T(8,128)(2,1)S(1)} %fusion.14), channel_id=1, source_target_pairs={{0,4},{2,6},{8,0},{10,2},{16,8},{18,10},{24,16},{26,18},{28,24},{3... | collective-permute-start | bytes 835592 | tf_op jit(solution)/shard_map/ppermute | solution.py:978
  124.3 8.0 %collective-permute-start.39 = (bf16[272,512]{1,0:T(8,128)(2,1)S(1)}, bf16[272,512]{1,0:T(8,128)(2,1)S(1)}, u32[]{:S(2)}, u32[]{:S(2)}) collective-permute-start(bf16[272,512]{1,0:T(8,128)(2,1)S(1)} %fusion.13), channel_id=1, source_target_pairs={{0,8},{2,10},{8,16},{10,18},{16,24},{18,26},{24,28},{26,30},{28,20... | collective-permute-start | bytes 835592 | tf_op jit(solution)/shard_map/ppermute | solution.py:978
  124.8 13.4 %collective-permute-start.45 = (bf16[256,768]{1,0:T(8,128)(2,1)S(1)}, bf16[256,768]{1,0:T(8,128)(2,1)S(1)}, u32[]{:S(2)}, u32[]{:S(2)}) collective-permute-start(bf16[256,768]{1,0:T(8,128)(2,1)S(1)} %get-tuple-element.229.mine_ref), channel_id=1, source_target_pairs={{0,1},{1,0},{2,3},{3,2},{4,5},{5,4},{6,7},{7,6},{8,9},{9,8},{10,11... | collective-permute-start | bytes 1179656 | tf_op jit(solution)/shard_map/ppermute | solution.py:1147
  132.5 7.1 %collective-permute-start.43 = (bf16[272,512]{1,0:T(8,128)(2,1)S(1)}, bf16[272,512]{1,0:T(8,128)(2,1)S(1)}, u32[]{:S(2)}, u32[]{:S(2)}) collective-permute-start(bf16[272,512]{1,0:T(8,128)(2,1)S(1)} %get-tuple-element.250), channel_id=1, source_target_pairs={{0,8},{2,10},{8,16},{10,18},{16,24},{18,26},{24,28},{26,30},{28,20... | collective-permute-start | bytes 835592 | tf_op jit(solution)/shard_map/ppermute | solution.py:978
  133.0 6.7 %collective-permute-start.44 = (bf16[272,512]{1,0:T(8,128)(2,1)S(1)}, bf16[272,512]{1,0:T(8,128)(2,1)S(1)}, u32[]{:S(2)}, u32[]{:S(2)}) collective-permute-start(bf16[272,512]{1,0:T(8,128)(2,1)S(1)} %get-tuple-element.249), channel_id=1, source_target_pairs={{0,4},{2,6},{8,0},{10,2},{16,8},{18,10},{24,16},{26,18},{28,24},{3... | collective-permute-start | bytes 835592 | tf_op jit(solution)/shard_map/ppermute | solution.py:978
  134.6 10.9 %collective-permute-start.42 = (bf16[256,768]{1,0:T(8,128)(2,1)S(1)}, bf16[256,768]{1,0:T(8,128)(2,1)S(1)}, u32[]{:S(2)}, u32[]{:S(2)}) collective-permute-start(bf16[256,768]{1,0:T(8,128)(2,1)S(1)} %get-tuple-element.227.mine_ref), channel_id=1, source_target_pairs={{0,1},{1,0},{2,3},{3,2},{4,5},{5,4},{6,7},{7,6},{8,9},{9,8},{10,11... | collective-permute-start | bytes 1179656 | tf_op jit(solution)/shard_map/ppermute | solution.py:1150
  140.0 6.7 %collective-permute-start.46 = (bf16[272,512]{1,0:T(8,128)(2,1)S(1)}, bf16[272,512]{1,0:T(8,128)(2,1)S(1)}, u32[]{:S(2)}, u32[]{:S(2)}) collective-permute-start(bf16[272,512]{1,0:T(8,128)(2,1)S(1)} %get-tuple-element.248), channel_id=1, source_target_pairs={{0,8},{2,10},{8,16},{10,18},{16,24},{18,26},{24,28},{26,30},{28,20... | collective-permute-start | bytes 835592 | tf_op jit(solution)/shard_map/ppermute | solution.py:978
  140.6 6.5 %collective-permute-start.47 = (bf16[272,512]{1,0:T(8,128)(2,1)S(1)}, bf16[272,512]{1,0:T(8,128)(2,1)S(1)}, u32[]{:S(2)}, u32[]{:S(2)}) collective-permute-start(bf16[272,512]{1,0:T(8,128)(2,1)S(1)} %get-tuple-element.247), channel_id=1, source_target_pairs={{0,4},{2,6},{8,0},{10,2},{16,8},{18,10},{24,16},{26,18},{28,24},{3... | collective-permute-start | bytes 835592 | tf_op jit(solution)/shard_map/ppermute | solution.py:978

commit v9 on v8

--- a/solution.py
+++ b/solution.py
@@ -256,7 +256,7 @@
     rows = length // UNITS
 
     def kernel(where_ref, tok_ref, seg_ref, *rest):
-        e_ref, wv_ref, low_ref, hat_ref, unit, same, sem, more = rest[len(units) :]
+        e_ref, wv_ref, low_ref, hat_ref, same, unit, sem, more = rest[len(units) :]
         top = heads * rows
 
         def target(m, owner):
@@ -284,10 +284,10 @@
             ((model, plan.width), BF),
             ((UNITS, plan.fold, LANES), BF),
             ((length, model), F32),
+            ((length, length), F32),
         ),
         (
             pltpu.VMEM((heads * length, length), BF),
-            pltpu.VMEM((length, length), F32),
             pltpu.SemaphoreType.DMA((UNITS, 1)),
             pltpu.SemaphoreType.DMA((UNITS, 2)),
         ),
@@ -295,26 +295,44 @@
     )
 
 
-def mixer_forward(plan, where, segments, early, units, shares, heads, width):
+def take_late(plan, where_ref, shares, refs, e_ref, wv_ref, low, same):
+    krows = plan.krows
+    for (u, first, rows), ref in zip(shares, refs):
+        for m, (row, lane, deep, lanes) in enumerate(low_parts(plan)):
+            if first <= row < first + rows:
+                part = ref[row - first : row - first + deep, lane : lane + lanes]
+                if m == 0:
+                    wv_ref[pl.ds(multiple(where_ref[u] * krows, 16), krows), :] = part
+                else:
+                    low[where_ref[u]] = part
+    scored = [n for n in range(len(shares)) if shares[n][1] == 0]
+    exponentials(where_ref, [shares[n] for n in scored], [(refs[n], 0) for n in scored], e_ref, same)
+
+
+def mixer_next(plan, where, early, units, shares):
+    e, wv, low, hat, same = early
+    count = len(units)
+
+    def kernel(where_ref, same_ref, e_old, wv_old, low_old, *rest):
+        take_late(plan, where_ref, shares, rest[:count], *rest[count:], same_ref)
+
+    outs = [(one.shape, one.dtype) for one in (e, wv, low)]
+    more = run(
+        kernel, "mixer_next", (where,), (same, e, wv, low, *units), outs, aliases={2: 0, 3: 1, 4: 2}
+    )
+    return [*more, hat, same]
+
+
+def mixer_forward(plan, where, early, units, shares, heads, width):
     length, model = early[3].shape
     size = width // heads
     krows = model // UNITS
     wide = heads * LANES
     count = len(units)
 
-    def kernel(where_ref, seg_ref, e_old, wv_old, low_old, hat_ref, *rest):
-        e_ref, wv_ref, low, va_ref, sums_ref, n1_ref, gains_ref, *mixed, pieces, same = rest[count:]
-        for (u, first, rows), ref in zip(shares, rest[:count]):
-            for m, (row, lane, deep, lanes) in enumerate(low_parts(plan)):
-                if first <= row < first + rows:
-                    part = ref[row - first : row - first + deep, lane : lane + lanes]
-                    if m == 0:
-                        wv_ref[pl.ds(multiple(where_ref[u] * krows, 16), krows), :] = part
-                    else:
-                        low[where_ref[u]] = part
-        document_mask(seg_ref, same)
-        scored = [n for n in range(count) if shares[n][1] == 0]
-        exponentials(where_ref, [shares[n] for n in scored], [(rest[n], 0) for n in scored], e_ref, same)
+    def kernel(where_ref, e_old, wv_old, low_old, hat_ref, same, *rest):
+        e_ref, wv_ref, low, va_ref, sums_ref, n1_ref, gains_ref, *mixed, pieces = rest[count:]
+        take_late(plan, where_ref, shares, rest[:count], e_ref, wv_ref, low, same)
         for d in range(UNITS):
             some = low[d].astype(F32)
             pieces[0, d : d + 1, :] = some[0:1, :]
@@ -352,7 +370,7 @@
         kernel,
         "mixer_forward",
         (where,),
-        (segments, *early, *units),
+        (*early, *units),
         (
             ((heads, length, length), BF),
             ((model, width), BF),
@@ -365,9 +383,8 @@
         ),
         (
             pltpu.VMEM((2, UNITS, LANES), F32),
-            pltpu.VMEM((length, length), F32),
         ),
-        aliases={2: 0, 3: 1, 4: 2},
+        aliases={1: 0, 2: 1, 3: 2},
     )
 
 
@@ -521,10 +538,21 @@
             return value + up_ref[rows, columns].astype(F32) + down_ref[rows, columns].astype(F32)
 
         copies = []
-        for n, (out, to) in enumerate(zip(outs, held)):
-            cut(n, to, total)
-            copies.append(pltpu.make_async_copy(to, out, sem.at[n]))
+
+        def send(source, to, n, m):
+            copies.append(pltpu.make_async_copy(source, to, sem.at[n, m]))
             copies[-1].start()
+
+        for n, (out, to) in reversed(list(enumerate(zip(outs, held)))):
+            if len(shapes[n]) < 3:
+                cut(n, to, total)
+                send(to, out, n, 0)
+            else:
+                half = shapes[n][0] // 2
+                for m, some in enumerate((range(half), range(half, shapes[n][0]))):
+                    cut(n, to, total, some)
+                    at = pl.ds(some.start, len(some))
+                    send(to.at[at], out.at[at], n, m)
         for copy in copies:
             copy.wait()
 
@@ -534,7 +562,7 @@
         (),
         (keep, own, up, down),
         (),
-        (*[pltpu.VMEM(shape, F32) for shape in shapes], pltpu.SemaphoreType.DMA((len(shapes),))),
+        (*[pltpu.VMEM(shape, F32) for shape in shapes], pltpu.SemaphoreType.DMA((len(shapes), 2))),
         loose_outs=[(shape, F32) for shape in shapes],
     )
 
@@ -556,10 +584,10 @@
     lead, half, fold = length - width, length // 2, krows // 3
     shapes = [(heads, rows, length), (krows, width), (krows, width), (1, krows), (1, krows)]
 
-    def cut(n, to, total):
+    def cut(n, to, total, some=()):
         low = top + krows
         if n == 0:
-            for h in range(heads):
+            for h in some:
                 to[h] = total(slice(h * rows, (h + 1) * rows), slice(None))
         elif n == 1:
             to[...] = total(slice(top, low), slice(0, width))
@@ -1086,8 +1114,11 @@
         early, late, near = list(range(UNITS // 2)), list(range(UNITS // 2, UNITS)), []
         begun = mixer_first(plan, where_in, tokens, segment_ids, units[: UNITS // 2], shares[: UNITS // 2], heads)
 
+    own = [n for n in late if shares[n][0] < UNITS // 2] if ring else late[:1]
+    late = [n for n in late if n not in own]
+    begun = mixer_next(plan, where_in, begun, [units[n] for n in own], [shares[n] for n in own])
     e, wv, _, va, sums, n1, gains, *mixed = mixer_forward(
-        plan, where_in, segment_ids, begun, [units[n] for n in late], [shares[n] for n in late], heads, width
+        plan, where_in, begun, [units[n] for n in late], [shares[n] for n in late], heads, width
     )
     mixed_other = [lax.ppermute(one, "mp", flip) for one in mixed]
     w, wo_whole, gact, mixf, rb, wo = second_weights(plan, where_in, second_at, cotangent, sums, units, shares, len(near), size)

time: 149 us -> 148 us (level)
    pallas_call x22 -> x23, Pallas kernels: 37.5 us -> 37.6 us  [run(): pl.pallas_call(kernel, out_shape=tuple(results), in_specs=specs, out_spec...]
where the time goes in v9:
time: 148 us
  waiting for transfers between devices  61.2 us (41%)
  starting transfers between devices  42.9 us (29%)
  Pallas kernels  37.6 us (25%)
  other arithmetic  3.42 us (2%)
    pallas_call x23, Pallas kernels, run(): pl.pallas_call(kernel, out_shape=tuple(results), in_specs=specs, out_spec...  37.6 us
    ppermute x3, waiting for transfers between devices, hop(): lax.ppermute(up, 'dp', ring.up)  24.4 us
    ppermute x14, starting transfers between devices, hop(): lax.ppermute(value, 'dp', self.ring.up if way == 'up' else self.ring.down)  14.7 us
    ppermute x14, waiting for transfers between devices, hop(): lax.ppermute(value, 'dp', self.ring.up if way == 'up' else self.ring.down)  13.2 us
    ppermute x2, waiting for transfers between devices, shards(): lowers = [lax.ppermute(lower, 'dp', way) for way in ways]  8.23 us
    ppermute x3, starting transfers between devices, hop(): lax.ppermute(up, 'dp', ring.up)  4.83 us
    ppermute x1, waiting for transfers between devices, shards(): two_other = lax.ppermute(ffn_two, 'mp', flip)  3.22 us
    ppermute x2, starting transfers between devices, shards(): uppers = [lax.ppermute(upper, 'dp', way) for way in ways]  3.08 us
  transfers between devices with their start and end apart: 48, of which 31 were waited for; matrix products, arithmetic and copies ran while one was open for 2% of the time, Pallas kernels for 22%

profile of v9, /device:TPU:0, one launch (start us, length us, event | category | flops | bytes accessed | tf_op | source)
XLA Modules:
  0.0 147.8 jit_solution(7312966882919480736)
XLA Ops:
  0.6 1.4 pack_unit.1
  2.0 3.1 %collective-permute-start = (bf16[480,512]{1,0:T(8,128)(2,1)S(1)}, bf16[480,512]{1,0:T(8,128)(2,1)S(1)}, u32[]{:S(2)}, u32[]{:S(2)}) collective-permute-start(bf16[480,512]{1,0:T(8,128)(2,1)S(1)} %get-tuple-element.132.refs_0_), channel_id=1, source_target_pairs={{0,8},{2,10},{8,16},{10,18},{16,24},{18,26},{24,28},{26,30},{28,20... | collective-permute-start | bytes 1474568 | tf_op jit(solution)/shard_map/ppermute | solution.py:1063
  6.0 2.0 %collective-permute-start.2 = (bf16[48,384]{1,0:T(8,128)(2,1)S(1)}, bf16[48,384]{1,0:T(8,128)(2,1)S(1)}, u32[]{:S(2)}, u32[]{:S(2)}) collective-permute-start(bf16[48,384]{1,0:T(8,128)(2,1)S(1)} %get-tuple-element.135), channel_id=1, source_target_pairs={{0,1},{1,0},{2,3},{3,2},{4,5},{5,4},{6,7},{7,6},{8,9},{9,8},{10,11... | collective-permute-start | bytes 110600 | tf_op jit(solution)/shard_map/ppermute | solution.py:1064
  7.9 2.0 %collective-permute-done.2.other_ref = bf16[48,384]{1,0:T(8,128)(2,1)S(1)} collective-permute-done((bf16[48,384]{1,0:T(8,128)(2,1)S(1)}, bf16[48,384]{1,0:T(8,128)(2,1)S(1)}, u32[]{:S(2)}, u32[]{:S(2)}) %collective-permute-start.2) | collective-permute-done | bytes 36896 | tf_op jit(solution)/shard_map/ppermute | solution.py:1064
  9.9 2.1 %collective-permute-start.3 = (bf16[112,512]{1,0:T(8,128)(2,1)S(1)}, bf16[112,512]{1,0:T(8,128)(2,1)S(1)}, u32[]{:S(2)}, u32[]{:S(2)}) collective-permute-start(bf16[112,512]{1,0:T(8,128)(2,1)S(1)} %fill_low.1.refs_1_), channel_id=1, source_target_pairs={{0,8},{2,10},{8,16},{10,18},{16,24},{18,26},{24,28},{26,30},{28,20... | collective-permute-start | bytes 344072 | tf_op jit(solution)/shard_map/ppermute | solution.py:1066
  12.0 6.7 %collective-permute-done.3.refs_2_ = bf16[112,512]{1,0:T(8,128)(2,1)S(1)} collective-permute-done((bf16[112,512]{1,0:T(8,128)(2,1)S(1)}, bf16[112,512]{1,0:T(8,128)(2,1)S(1)}, u32[]{:S(2)}, u32[]{:S(2)}) %collective-permute-start.3) | collective-permute-done | bytes 114720 | tf_op jit(solution)/shard_map/ppermute | solution.py:1066
  18.7 1.5 %collective-permute-done.4.refs_3_ = bf16[112,512]{1,0:T(8,128)(2,1)S(1)} collective-permute-done((bf16[112,512]{1,0:T(8,128)(2,1)S(1)}, bf16[112,512]{1,0:T(8,128)(2,1)S(1)}, u32[]{:S(2)}, u32[]{:S(2)}) %collective-permute-start.4) | collective-permute-done | bytes 114720 | tf_op jit(solution)/shard_map/ppermute | solution.py:1066
  20.4 1.6 %collective-permute-start.5 = (bf16[592,512]{1,0:T(8,128)(2,1)S(1)}, bf16[592,512]{1,0:T(8,128)(2,1)S(1)}, u32[]{:S(2)}, u32[]{:S(2)}) collective-permute-start(bf16[592,512]{1,0:T(8,128)(2,1)S(1)} %get-tuple-element.140.rest_1_), channel_id=1, source_target_pairs={{0,8},{2,10},{8,16},{10,18},{16,24},{18,26},{24,28},{26,30},{28,20... | collective-permute-start | bytes 1818632 | tf_op jit(solution)/shard_map/ppermute | solution.py:953
  22.5 12.2 %collective-permute-done.5.rest_3_ = bf16[592,512]{1,0:T(8,128)(2,1)S(1)} collective-permute-done((bf16[592,512]{1,0:T(8,128)(2,1)S(1)}, bf16[592,512]{1,0:T(8,128)(2,1)S(1)}, u32[]{:S(2)}, u32[]{:S(2)}) %collective-permute-start.5) | collective-permute-done | bytes 606240 | tf_op jit(solution)/shard_map/ppermute | solution.py:953
  34.7 1.3 collective-permute-done.6.rest_4_
  36.0 1.6 %collective-permute-start.7 = (bf16[592,512]{1,0:T(8,128)(2,1)S(1)}, bf16[592,512]{1,0:T(8,128)(2,1)S(1)}, u32[]{:S(2)}, u32[]{:S(2)}) collective-permute-start(bf16[592,512]{1,0:T(8,128)(2,1)S(1)} %collective-permute-done.5.rest_3_), channel_id=1, source_target_pairs={{0,8},{2,10},{8,16},{10,18},{16,24},{18,26},{24,28},{26,30},{28,20... | collective-permute-start | bytes 1818632 | tf_op jit(solution)/shard_map/ppermute | solution.py:953
  38.7 10.3 %collective-permute-done.7.rest_0_.rest_10_ = bf16[592,512]{1,0:T(8,128)(2,1)S(1)} collective-permute-done((bf16[592,512]{1,0:T(8,128)(2,1)S(1)}, bf16[592,512]{1,0:T(8,128)(2,1)S(1)}, u32[]{:S(2)}, u32[]{:S(2)}) %collective-permute-start.7) | collective-permute-done | bytes 606240 | tf_op jit(solution)/shard_map/ppermute | solution.py:953
  49.0 1.3 collective-permute-done.8.rest_1_.rest_11_
  50.9 1.6 %collective-permute-start.9 = (bf16[288,512]{1,0:T(8,128)(2,1)S(1)}, bf16[288,512]{1,0:T(8,128)(2,1)S(1)}, u32[]{:S(2)}, u32[]{:S(2)}) collective-permute-start(bf16[288,512]{1,0:T(8,128)(2,1)S(1)} %slice.87), channel_id=1, source_target_pairs={{0,8},{2,10},{8,16},{10,18},{16,24},{18,26},{24,28},{26,30},{28,20... | collective-permute-start | bytes 884744 | tf_op jit(solution)/shard_map/ppermute | solution.py:953
  53.5 0.8 copy-done.12
  54.4 3.8 %mixer_first.1 = (bf16[6,512,512]{2,1,0:T(8,128)(2,1)S(1)}, bf16[768,384]{1,0:T(8,128)(2,1)S(1)}, bf16[16,16,128]{2,1,0:T(8,128)(2,1)S(1)}, f32[512,768]{1,0:T(8,128)S(1)}, f32[512,512]{1,0:T(8,128)S(1)}) custom-call(s32[16]{0:T(128)S(1)} %pad_add_fusion.where_ref, bf16[512,768]{1,0:T(8,128)(2,1)S(1)} %copy-done, s32[1,512]{1,0:T(1,128)S(1)} %copy-done.5, ...), custom_call_target="tpu_custom_call" | custom-call | flops 1 | bytes 1 | tf_op jit(solution)/shard_map/mixer_first/pallas_call | solution.py:36
  58.2 1.9 %collective-permute-done.9.rest_2_.rest_12_ = bf16[288,512]{1,0:T(8,128)(2,1)S(1)} collective-permute-done((bf16[288,512]{1,0:T(8,128)(2,1)S(1)}, bf16[288,512]{1,0:T(8,128)(2,1)S(1)}, u32[]{:S(2)}, u32[]{:S(2)}) %collective-permute-start.9) | collective-permute-done | bytes 294944 | tf_op jit(solution)/shard_map/ppermute | solution.py:953
  60.7 0.8 mixer_next.1
  61.5 0.7 collective-permute-done.18.rest_2_.rest_16_
  62.2 2.7 %mixer_forward.1 = (bf16[6,512,512]{2,1,0:T(8,128)(2,1)S(1)}, bf16[768,384]{1,0:T(8,128)(2,1)S(1)}, bf16[16,16,128]{2,1,0:T(8,128)(2,1)S(1)}, bf16[512,768]{1,0:...) custom-call(s32[16]{0:T(128)S(1)} %pad_add_fusion.where_ref, ...), custom_call_target="tpu_custom_call", output_to_operand_aliasing={{0}: (1, {}), {1}: (2, {}), {2}: (3, {})} | custom-call | flops 1 | bytes 1 | tf_op jit(solution)/shard_map/mixer_forward/pallas_call | solution.py:36
  64.9 1.6 %collective-permute-start.20 = (bf16[256,384]{1,0:T(8,128)(2,1)S(1)}, bf16[256,384]{1,0:T(8,128)(2,1)S(1)}, u32[]{:S(2)}, u32[]{:S(2)}) collective-permute-start(bf16[256,384]{1,0:T(8,128)(2,1)S(1)} %get-tuple-element.161.own_ref.rest_2_), channel_id=1, source_target_pairs={{0,1},{1,0},{2,3},{3,2},{4,5},{5,4},{6,7},{7,6},{8,9},{9,8},{10,11... | collective-permute-start | bytes 589832 | tf_op jit(solution)/shard_map/ppermute | solution.py:1123
  67.0 5.0 %second_weights.1 = (bf16[6,768,512]{2,1,0:T(8,128)(2,1)S(1)}, bf16[768,768]{1,0:T(8,128)(2,1)S(1)}, f32[512,1536]{1,0:T(8,128)S(1)}, f32[512,768]{1,0:T(8,128)S...) custom-call(s32[16]{0:T(128)S(1)} %pad_add_fusion.where_ref, s32[1]{0:T(128)} %bitcast.second_ref, ...), custom_call_target="tpu_custom_call" | custom-call | flops 1 | bytes 1 | tf_op jit(solution)/shard_map/second_weights/pallas_call | solution.py:36
  72.1 0.7 collective-permute-done.20.other_ref
  72.8 2.7 %ffn_main.2 = (bf16[256,768]{1,0:T(8,128)(2,1)S(1)}, f32[256,768]{1,0:T(8,128)S(1)}, bf16[512,768]{1,0:T(8,128)(2,1)S(1)}, bf16[512,1536]{1,0:T(8,128)(2,1)S(1)}, bf16[512,1536]{1,0:T(8,128)(2,1)S(1)}) custom-call(s32[1]{0:T(128)} %bitcast.second_ref, bf16[512,768]{1,0:T(8,128)(2,1)S(1)} %copy-done, bf16[256,384]{1,0:T(8,128)(2,1)S(1)} %get-tuple-element.161.own_ref.rest_2_, ...), custom_call_target="tpu_custom_call" | custom-call | flops 1 | bytes 1 | tf_op jit(solution)/shard_map/ffn_main/pallas_call | solution.py:36
  75.5 1.6 %collective-permute-start.26 = (bf16[256,768]{1,0:T(8,128)(2,1)S(1)}, bf16[256,768]{1,0:T(8,128)(2,1)S(1)}, u32[]{:S(2)}, u32[]{:S(2)}) collective-permute-start(bf16[256,768]{1,0:T(8,128)(2,1)S(1)} %get-tuple-element.181.back_ref), channel_id=1, source_target_pairs={{0,1},{1,0},{2,3},{3,2},{4,5},{5,4},{6,7},{7,6},{8,9},{9,8},{10,11... | collective-permute-start | bytes 1179656 | tf_op jit(solution)/shard_map/ppermute | solution.py:1131
  77.1 2.7 %ffn_main.3 = (bf16[256,768]{1,0:T(8,128)(2,1)S(1)}, f32[256,768]{1,0:T(8,128)S(1)}, bf16[512,768]{1,0:T(8,128)(2,1)S(1)}, bf16[512,1536]{1,0:T(8,128)(2,1)S(1)}, bf16[512,1536]{1,0:T(8,128)(2,1)S(1)}) custom-call(s32[1]{0:T(128)} %bitcast.second_ref, bf16[512,768]{1,0:T(8,128)(2,1)S(1)} %copy-done, ...), custom_call_target="tpu_custom_call", output_to_operand_aliasing={{2}: (8, {}), {3}: (9, {}), {4}: (10, {})} | custom-call | flops 1 | bytes 1 | tf_op jit(solution)/shard_map/ffn_main/pallas_call | solution.py:36
  79.8 3.6 %ffn_grads.1 = (bf16[8,48,3072]{2,1,0:T(8,128)(2,1)S(1)}, bf16[48,3072]{1,0:T(8,128)(2,1)S(1)}, bf16[48,3072]{1,0:T(8,128)(2,1)S(1)}, bf16[6,48,3072]{2,1,0:T(8,128)(2,1)S(1)}) custom-call(s32[16]{0:T(128)S(1)} %pad_add_fusion.1.where_ref, bf16[512,768]{1,0:T(8,128)(2,1)S(1)} %copy-done.1, bf16[512,768]{1,0:T(8,128)(2,1)S(1)} %get-tuple-element.173.n2_ref, ...), custom_call_target="tpu_custom_call" | custom-call | flops 1 | bytes 1 | tf_op jit(solution)/shard_map/ffn_grads/pallas_call | solution.py:36
  84.0 1.1 collective-permute-done.22
  86.3 1.6 %collective-permute-start.25 = (bf16[48,3072]{1,0:T(8,128)(2,1)S(1)}, bf16[48,3072]{1,0:T(8,128)(2,1)S(1)}, u32[]{:S(2)}, u32[]{:S(2)}) collective-permute-start(bf16[48,3072]{1,0:T(8,128)(2,1)S(1)} %get-tuple-element.265), channel_id=1, source_target_pairs={{0,8},{2,10},{8,16},{10,18},{16,24},{18,26},{24,28},{26,30},{28,20... | collective-permute-start | bytes 884744 | tf_op jit(solution)/shard_map/ppermute | solution.py:1006
  87.9 1.3 collective-permute-start.32
  89.2 1.1 resid_back.2
  90.3 0.7 value_first.1.first_ref
  91.1 1.3 mixer_grads.2
  92.4 1.7 %ffn_out.1 = (bf16[192,768]{1,0:T(8,128)(2,1)S(1)}, bf16[320,768]{1,0:T(8,128)(2,1)S(1)}) custom-call(bf16[512,1536]{1,0:T(8,128)(2,1)S(1)} %get-tuple-element.186.act_ref, bf16[6,768,512]{2,1,0:T(8,128)(2,1)S(1)} %get-tuple-element.165.w_ref), custom_call_target="tpu_custom_call" | custom-call | flops 1 | bytes 1 | tf_op jit(solution)/shard_map/ffn_out/pallas_call | solution.py:36
  94.1 1.0 collective-permute-done.23
  95.6 0.7 collective-permute-start.28
  96.4 1.3 collective-permute-start.29
  97.7 1.0 collective-permute-done.32.other_ref
  98.7 1.1 resid_back.3
  99.9 1.4 value_back.1
  101.3 1.5 %collective-permute-start.33 = (f32[64,128]{1,0:T(8,128)S(1)}, f32[64,128]{1,0:T(8,128)S(1)}, u32[]{:S(2)}, u32[]{:S(2)}) collective-permute-start(f32[64,128]{1,0:T(8,128)S(1)} %get-tuple-element.214.ga_ref), channel_id=1, source_target_pairs={{0,1},{1,0},{2,3},{3,2},{4,5},{5,4},{6,7},{7,6},{8,9},{9,8},{10,11... | collective-permute-start | bytes 98312 | tf_op jit(solution)/shard_map/ppermute | solution.py:1155
  104.6 1.5 %collective-permute-start.30 = (bf16[48,3072]{1,0:T(8,128)(2,1)S(1)}, bf16[48,3072]{1,0:T(8,128)(2,1)S(1)}, u32[]{:S(2)}, u32[]{:S(2)}) collective-permute-start(bf16[48,3072]{1,0:T(8,128)(2,1)S(1)} %get-tuple-element.262), channel_id=1, source_target_pairs={{0,4},{2,6},{8,0},{10,2},{16,8},{18,10},{24,16},{26,18},{28,24},{3... | collective-permute-start | bytes 884744 | tf_op jit(solution)/shard_map/ppermute | solution.py:1006
  106.6 1.4 mixer_grads.3
  108.0 1.7 %weight_grads.1 = (bf16[8,272,512]{2,1,0:T(8,128)(2,1)S(1)}, bf16[272,512]{1,0:T(8,128)(2,1)S(1)}, bf16[7,272,512]{2,1,0:T(8,128)(2,1)S(1)}) custom-call(s32[16]{0:T(128)S(1)} %pad_add_fusion.1.where_ref, bf16[512,768]{1,0:T(8,128)(2,1)S(1)} %get-tuple-element.202.n1_ref, ...), custom_call_target="tpu_custom_call", output_to_operand_aliasing={{0}: (10, {}), {1}: (11, {}), {2}: (12, {})} | custom-call | flops 1 | bytes 1 | tf_op jit(solution)/shard_map/weight_grads/pallas_call | solution.py:36
  109.8 1.1 collective-permute-done.35
  111.6 1.2 collective-permute-done.31.up_ref
  113.7 1.5 %collective-permute-start.36 = (bf16[48,3072]{1,0:T(8,128)(2,1)S(1)}, bf16[48,3072]{1,0:T(8,128)(2,1)S(1)}, u32[]{:S(2)}, u32[]{:S(2)}) collective-permute-start(bf16[48,3072]{1,0:T(8,128)(2,1)S(1)} %fusion.3), channel_id=1, source_target_pairs={{0,4},{2,6},{8,0},{10,2},{16,8},{18,10},{24,16},{26,18},{28,24},{3... | collective-permute-start | bytes 884744 | tf_op jit(solution)/shard_map/ppermute | solution.py:1006
  115.2 1.8 %collective-permute-start.41 = (bf16[320,768]{1,0:T(8,128)(2,1)S(1)}, bf16[320,768]{1,0:T(8,128)(2,1)S(1)}, u32[]{:S(2)}, u32[]{:S(2)}) collective-permute-start(bf16[320,768]{1,0:T(8,128)(2,1)S(1)} %get-tuple-element.224), channel_id=1, source_target_pairs={{0,1},{1,0},{2,3},{3,2},{4,5},{5,4},{6,7},{7,6},{8,9},{9,8},{10,11... | collective-permute-start | bytes 1474568 | tf_op jit(solution)/shard_map/ppermute | solution.py:1172
  116.9 5.1 %collective-permute-done.38 = bf16[272,512]{1,0:T(8,128)(2,1)S(1)} collective-permute-done((bf16[272,512]{1,0:T(8,128)(2,1)S(1)}, bf16[272,512]{1,0:T(8,128)(2,1)S(1)}, u32[]{:S(2)}, u32[]{:S(2)}) %collective-permute-start.38) | collective-permute-done | bytes 278560 | tf_op jit(solution)/shard_map/ppermute | solution.py:1006
  122.1 1.6 %collective-permute-start.40 = (bf16[272,512]{1,0:T(8,128)(2,1)S(1)}, bf16[272,512]{1,0:T(8,128)(2,1)S(1)}, u32[]{:S(2)}, u32[]{:S(2)}) collective-permute-start(bf16[272,512]{1,0:T(8,128)(2,1)S(1)} %fusion.14), channel_id=1, source_target_pairs={{0,4},{2,6},{8,0},{10,2},{16,8},{18,10},{24,16},{26,18},{28,24},{3... | collective-permute-start | bytes 835592 | tf_op jit(solution)/shard_map/ppermute | solution.py:1006
  124.3 1.8 %collective-permute-start.45 = (bf16[256,768]{1,0:T(8,128)(2,1)S(1)}, bf16[256,768]{1,0:T(8,128)(2,1)S(1)}, u32[]{:S(2)}, u32[]{:S(2)}) collective-permute-start(bf16[256,768]{1,0:T(8,128)(2,1)S(1)} %get-tuple-element.239.mine_ref), channel_id=1, source_target_pairs={{0,1},{1,0},{2,3},{3,2},{4,5},{5,4},{6,7},{7,6},{8,9},{9,8},{10,11... | collective-permute-start | bytes 1179656 | tf_op jit(solution)/shard_map/ppermute | solution.py:1178
  126.1 3.2 %collective-permute-done.41 = bf16[320,768]{1,0:T(8,128)(2,1)S(1)} collective-permute-done((bf16[320,768]{1,0:T(8,128)(2,1)S(1)}, bf16[320,768]{1,0:T(8,128)(2,1)S(1)}, u32[]{:S(2)}, u32[]{:S(2)}) %collective-permute-start.41) | collective-permute-done | bytes 491552 | tf_op jit(solution)/shard_map/ppermute | solution.py:1172
  129.3 1.1 collective-permute-done.40
  130.4 1.5 collective-permute-done.39
  132.5 1.6 %collective-permute-start.44 = (bf16[272,512]{1,0:T(8,128)(2,1)S(1)}, bf16[272,512]{1,0:T(8,128)(2,1)S(1)}, u32[]{:S(2)}, u32[]{:S(2)}) collective-permute-start(bf16[272,512]{1,0:T(8,128)(2,1)S(1)} %get-tuple-element.259), channel_id=1, source_target_pairs={{0,4},{2,6},{8,0},{10,2},{16,8},{18,10},{24,16},{26,18},{28,24},{3... | collective-permute-start | bytes 835592 | tf_op jit(solution)/shard_map/ppermute | solution.py:1006
  134.1 1.8 %collective-permute-start.42 = (bf16[256,768]{1,0:T(8,128)(2,1)S(1)}, bf16[256,768]{1,0:T(8,128)(2,1)S(1)}, u32[]{:S(2)}, u32[]{:S(2)}) collective-permute-start(bf16[256,768]{1,0:T(8,128)(2,1)S(1)} %get-tuple-element.237.mine_ref), channel_id=1, source_target_pairs={{0,1},{1,0},{2,3},{3,2},{4,5},{5,4},{6,7},{7,6},{8,9},{9,8},{10,11... | collective-permute-start | bytes 1179656 | tf_op jit(solution)/shard_map/ppermute | solution.py:1181
  136.0 1.8 %collective-permute-done.45.other_ref = bf16[256,768]{1,0:T(8,128)(2,1)S(1)} collective-permute-done((bf16[256,768]{1,0:T(8,128)(2,1)S(1)}, bf16[256,768]{1,0:T(8,128)(2,1)S(1)}, u32[]{:S(2)}, u32[]{:S(2)}) %collective-permute-start.45) | collective-permute-done | bytes 393248 | tf_op jit(solution)/shard_map/ppermute | solution.py:1178
  137.7 1.4 collective-permute-done.43
  140.2 1.4 collective-permute-start.47
  141.6 0.9 ffn_result.1
  142.5 1.2 fusion
  143.7 1.1 token_grads.2.rest_0_
  145.1 1.2 token_grads.3
  146.7 0.9 mixer_result.1
  (100 shorter events, 14.5 us)
Async XLA Ops:
  2.0 18.2 %collective-permute-start = (bf16[480,512]{1,0:T(8,128)(2,1)S(1)}, bf16[480,512]{1,0:T(8,128)(2,1)S(1)}, u32[]{:S(2)}, u32[]{:S(2)}) collective-permute-start(bf16[480,512]{1,0:T(8,128)(2,1)S(1)} %get-tuple-element.132.refs_0_), channel_id=1, source_target_pairs={{0,8},{2,10},{8,16},{10,18},{16,24},{18,26},{24,28},{26,30},{28,20... | collective-permute-start | bytes 1474568 | tf_op jit(solution)/shard_map/ppermute | solution.py:1063
  5.1 15.1 %collective-permute-start.1 = (bf16[480,512]{1,0:T(8,128)(2,1)S(1)}, bf16[480,512]{1,0:T(8,128)(2,1)S(1)}, u32[]{:S(2)}, u32[]{:S(2)}) collective-permute-start(bf16[480,512]{1,0:T(8,128)(2,1)S(1)} %get-tuple-element.132.refs_0_), channel_id=1, source_target_pairs={{0,4},{2,6},{8,0},{10,2},{16,8},{18,10},{24,16},{26,18},{28,24},{3... | collective-permute-start | bytes 1474568 | tf_op jit(solution)/shard_map/ppermute | solution.py:1063
  6.0 4.0 %collective-permute-start.2 = (bf16[48,384]{1,0:T(8,128)(2,1)S(1)}, bf16[48,384]{1,0:T(8,128)(2,1)S(1)}, u32[]{:S(2)}, u32[]{:S(2)}) collective-permute-start(bf16[48,384]{1,0:T(8,128)(2,1)S(1)} %get-tuple-element.135), channel_id=1, source_target_pairs={{0,1},{1,0},{2,3},{3,2},{4,5},{5,4},{6,7},{7,6},{8,9},{9,8},{10,11... | collective-permute-start | bytes 110600 | tf_op jit(solution)/shard_map/ppermute | solution.py:1064
  9.9 44.4 %copy-start = (bf16[512,768]{1,0:T(8,128)(2,1)S(1)}, bf16[512,768]{1,0:T(8,128)(2,1)}, u32[]{:S(2)}) copy-start(bf16[512,768]{1,0:T(8,128)(2,1)} %tok_ref.11) | copy-start | bytes 2359300
  9.9 44.4 %copy-start.5 = (s32[1,512]{1,0:T(1,128)S(1)}, s32[1,512]{1,0:T(1,128)}, u32[]{:S(2)}) copy-start(s32[1,512]{1,0:T(1,128)} %seg_ref.1) | copy-start | bytes 6148
  9.9 8.8 %collective-permute-start.3 = (bf16[112,512]{1,0:T(8,128)(2,1)S(1)}, bf16[112,512]{1,0:T(8,128)(2,1)S(1)}, u32[]{:S(2)}, u32[]{:S(2)}) collective-permute-start(bf16[112,512]{1,0:T(8,128)(2,1)S(1)} %fill_low.1.refs_1_), channel_id=1, source_target_pairs={{0,8},{2,10},{8,16},{10,18},{16,24},{18,26},{24,28},{26,30},{28,20... | collective-permute-start | bytes 344072 | tf_op jit(solution)/shard_map/ppermute | solution.py:1066
  12.0 8.2 %collective-permute-start.4 = (bf16[112,512]{1,0:T(8,128)(2,1)S(1)}, bf16[112,512]{1,0:T(8,128)(2,1)S(1)}, u32[]{:S(2)}, u32[]{:S(2)}) collective-permute-start(bf16[112,512]{1,0:T(8,128)(2,1)S(1)} %fill_low.1.refs_1_), channel_id=1, source_target_pairs={{0,4},{2,6},{8,0},{10,2},{16,8},{18,10},{24,16},{26,18},{28,24},{3... | collective-permute-start | bytes 344072 | tf_op jit(solution)/shard_map/ppermute | solution.py:1066
  20.3 32.7 %copy-start.3 = (bf16[592,512]{1,0:T(8,128)(2,1)}, bf16[592,512]{1,0:T(8,128)(2,1)S(1)}, u32[]{:S(2)}) copy-start(bf16[592,512]{1,0:T(8,128)(2,1)S(1)} %get-tuple-element.140.rest_1_) | copy-start | bytes 1818628
  20.4 32.7 %copy-start.4 = (bf16[592,512]{1,0:T(8,128)(2,1)}, bf16[592,512]{1,0:T(8,128)(2,1)S(1)}, u32[]{:S(2)}) copy-start(bf16[592,512]{1,0:T(8,128)(2,1)S(1)} %get-tuple-element.141.rest_2_) | copy-start | bytes 1818628
  20.4 14.3 %collective-permute-start.5 = (bf16[592,512]{1,0:T(8,128)(2,1)S(1)}, bf16[592,512]{1,0:T(8,128)(2,1)S(1)}, u32[]{:S(2)}, u32[]{:S(2)}) collective-permute-start(bf16[592,512]{1,0:T(8,128)(2,1)S(1)} %get-tuple-element.140.rest_1_), channel_id=1, source_target_pairs={{0,8},{2,10},{8,16},{10,18},{16,24},{18,26},{24,28},{26,30},{28,20... | collective-permute-start | bytes 1818632 | tf_op jit(solution)/shard_map/ppermute | solution.py:953
  22.0 13.9 %collective-permute-start.6 = (bf16[592,512]{1,0:T(8,128)(2,1)S(1)}, bf16[592,512]{1,0:T(8,128)(2,1)S(1)}, u32[]{:S(2)}, u32[]{:S(2)}) collective-permute-start(bf16[592,512]{1,0:T(8,128)(2,1)S(1)} %get-tuple-element.141.rest_2_), channel_id=1, source_target_pairs={{0,4},{2,6},{8,0},{10,2},{16,8},{18,10},{24,16},{26,18},{28,24},{3... | collective-permute-start | bytes 1818632 | tf_op jit(solution)/shard_map/ppermute | solution.py:953
  34.7 18.4 %copy-start.6 = (bf16[592,512]{1,0:T(8,128)(2,1)}, bf16[592,512]{1,0:T(8,128)(2,1)S(1)}, u32[]{:S(2)}) copy-start(bf16[592,512]{1,0:T(8,128)(2,1)S(1)} %collective-permute-done.5.rest_3_) | copy-start | bytes 1818628
  36.0 17.1 %copy-start.7 = (bf16[592,512]{1,0:T(8,128)(2,1)}, bf16[592,512]{1,0:T(8,128)(2,1)S(1)}, u32[]{:S(2)}) copy-start(bf16[592,512]{1,0:T(8,128)(2,1)S(1)} %collective-permute-done.6.rest_4_) | copy-start | bytes 1818628
  36.0 13.0 %collective-permute-start.7 = (bf16[592,512]{1,0:T(8,128)(2,1)S(1)}, bf16[592,512]{1,0:T(8,128)(2,1)S(1)}, u32[]{:S(2)}, u32[]{:S(2)}) collective-permute-start(bf16[592,512]{1,0:T(8,128)(2,1)S(1)} %collective-permute-done.5.rest_3_), channel_id=1, source_target_pairs={{0,8},{2,10},{8,16},{10,18},{16,24},{18,26},{24,28},{26,30},{28,20... | collective-permute-start | bytes 1818632 | tf_op jit(solution)/shard_map/ppermute | solution.py:953
  37.5 12.7 %collective-permute-start.8 = (bf16[592,512]{1,0:T(8,128)(2,1)S(1)}, bf16[592,512]{1,0:T(8,128)(2,1)S(1)}, u32[]{:S(2)}, u32[]{:S(2)}) collective-permute-start(bf16[592,512]{1,0:T(8,128)(2,1)S(1)} %collective-permute-done.6.rest_4_), channel_id=1, source_target_pairs={{0,4},{2,6},{8,0},{10,2},{16,8},{18,10},{24,16},{26,18},{28,24},{3... | collective-permute-start | bytes 1818632 | tf_op jit(solution)/shard_map/ppermute | solution.py:953
  38.0 15.0 %copy-start.2 = (bf16[592,512]{1,0:T(8,128)(2,1)}, bf16[592,512]{1,0:T(8,128)(2,1)S(1)}, u32[]{:S(2)}) copy-start(bf16[592,512]{1,0:T(8,128)(2,1)S(1)} %join_units.3.rest_0_) | copy-start | bytes 1818628
  38.0 12.3 %collective-permute-start.11 = (bf16[592,512]{1,0:T(8,128)(2,1)S(1)}, bf16[592,512]{1,0:T(8,128)(2,1)S(1)}, u32[]{:S(2)}, u32[]{:S(2)}) collective-permute-start(bf16[592,512]{1,0:T(8,128)(2,1)S(1)} %join_units.3.rest_0_), channel_id=1, source_target_pairs={{0,2},{2,0},{4,6},{6,4},{8,10},{10,8},{12,14},{14,12},{16,18},{18,... | collective-permute-start | bytes 1818632 | tf_op jit(solution)/shard_map/ppermute | solution.py:958
  38.1 12.7 %collective-permute-start.12 = (bf16[592,512]{1,0:T(8,128)(2,1)S(1)}, bf16[592,512]{1,0:T(8,128)(2,1)S(1)}, u32[]{:S(2)}, u32[]{:S(2)}) collective-permute-start(bf16[592,512]{1,0:T(8,128)(2,1)S(1)} %get-tuple-element.140.rest_1_), channel_id=1, source_target_pairs={{0,2},{2,0},{4,6},{6,4},{8,10},{10,8},{12,14},{14,12},{16,18},{18,... | collective-permute-start | bytes 1818632 | tf_op jit(solution)/shard_map/ppermute | solution.py:958
  38.6 13.9 %collective-permute-start.13 = (bf16[592,512]{1,0:T(8,128)(2,1)S(1)}, bf16[592,512]{1,0:T(8,128)(2,1)S(1)}, u32[]{:S(2)}, u32[]{:S(2)}) collective-permute-start(bf16[592,512]{1,0:T(8,128)(2,1)S(1)} %get-tuple-element.141.rest_2_), channel_id=1, source_target_pairs={{0,2},{2,0},{4,6},{6,4},{8,10},{10,8},{12,14},{14,12},{16,18},{18,... | collective-permute-start | bytes 1818632 | tf_op jit(solution)/shard_map/ppermute | solution.py:958
  49.0 3.5 %collective-permute-start.14 = (bf16[592,512]{1,0:T(8,128)(2,1)S(1)}, bf16[592,512]{1,0:T(8,128)(2,1)S(1)}, u32[]{:S(2)}, u32[]{:S(2)}) collective-permute-start(bf16[592,512]{1,0:T(8,128)(2,1)S(1)} %collective-permute-done.5.rest_3_), channel_id=1, source_target_pairs={{0,2},{2,0},{4,6},{6,4},{8,10},{10,8},{12,14},{14,12},{16,18},{18,... | collective-permute-start | bytes 1818632 | tf_op jit(solution)/shard_map/ppermute | solution.py:958
  50.3 2.7 %collective-permute-start.15 = (bf16[592,512]{1,0:T(8,128)(2,1)S(1)}, bf16[592,512]{1,0:T(8,128)(2,1)S(1)}, u32[]{:S(2)}, u32[]{:S(2)}) collective-permute-start(bf16[592,512]{1,0:T(8,128)(2,1)S(1)} %collective-permute-done.6.rest_4_), channel_id=1, source_target_pairs={{0,2},{2,0},{4,6},{6,4},{8,10},{10,8},{12,14},{14,12},{16,18},{18,... | collective-permute-start | bytes 1818632 | tf_op jit(solution)/shard_map/ppermute | solution.py:958
  50.3 2.8 %copy-start.8 = (bf16[592,512]{1,0:T(8,128)(2,1)}, bf16[592,512]{1,0:T(8,128)(2,1)S(1)}, u32[]{:S(2)}) copy-start(bf16[592,512]{1,0:T(8,128)(2,1)S(1)} %collective-permute-done.11.rest_5_) | copy-start | bytes 1818628
  50.3 9.8 %collective-permute-start.10 = (bf16[304,512]{1,0:T(8,128)(2,1)S(1)}, bf16[304,512]{1,0:T(8,128)(2,1)S(1)}, u32[]{:S(2)}, u32[]{:S(2)}) collective-permute-start(bf16[304,512]{1,0:T(8,128)(2,1)S(1)} %slice.88), channel_id=1, source_target_pairs={{0,4},{2,6},{8,0},{10,2},{16,8},{18,10},{24,16},{26,18},{28,24},{3... | collective-permute-start | bytes 933896 | tf_op jit(solution)/shard_map/ppermute | solution.py:953
  50.9 2.2 %copy-start.9 = (bf16[592,512]{1,0:T(8,128)(2,1)}, bf16[592,512]{1,0:T(8,128)(2,1)S(1)}, u32[]{:S(2)}) copy-start(bf16[592,512]{1,0:T(8,128)(2,1)S(1)} %collective-permute-done.12.rest_6_) | copy-start | bytes 1818628
  50.9 9.2 %collective-permute-start.9 = (bf16[288,512]{1,0:T(8,128)(2,1)S(1)}, bf16[288,512]{1,0:T(8,128)(2,1)S(1)}, u32[]{:S(2)}, u32[]{:S(2)}) collective-permute-start(bf16[288,512]{1,0:T(8,128)(2,1)S(1)} %slice.87), channel_id=1, source_target_pairs={{0,8},{2,10},{8,16},{10,18},{16,24},{18,26},{24,28},{26,30},{28,20... | collective-permute-start | bytes 884744 | tf_op jit(solution)/shard_map/ppermute | solution.py:953
  52.5 0.8 copy-start.10
  52.5 9.7 %collective-permute-start.16 = (bf16[592,512]{1,0:T(8,128)(2,1)S(1)}, bf16[592,512]{1,0:T(8,128)(2,1)S(1)}, u32[]{:S(2)}, u32[]{:S(2)}) collective-permute-start(bf16[592,512]{1,0:T(8,128)(2,1)S(1)} %collective-permute-done.7.rest_0_.rest_10_), channel_id=1, source_target_pairs={{0,2},{2,0},{4,6},{6,4},{8,10},{10,8},{12,14},{14,12},{16,18},{18,... | collective-permute-start | bytes 1818632 | tf_op jit(solution)/shard_map/ppermute | solution.py:958
  52.5 1.0 copy-start.11
  52.5 9.7 %collective-permute-start.17 = (bf16[592,512]{1,0:T(8,128)(2,1)S(1)}, bf16[592,512]{1,0:T(8,128)(2,1)S(1)}, u32[]{:S(2)}, u32[]{:S(2)}) collective-permute-start(bf16[592,512]{1,0:T(8,128)(2,1)S(1)} %collective-permute-done.8.rest_1_.rest_11_), channel_id=1, source_target_pairs={{0,2},{2,0},{4,6},{6,4},{8,10},{10,8},{12,14},{14,12},{16,18},{18,... | collective-permute-start | bytes 1818632 | tf_op jit(solution)/shard_map/ppermute | solution.py:958
  53.5 0.8 copy-start.12
  60.2 2.0 %collective-permute-start.19 = (bf16[304,512]{1,0:T(8,128)(2,1)S(1)}, bf16[304,512]{1,0:T(8,128)(2,1)S(1)}, u32[]{:S(2)}, u32[]{:S(2)}) collective-permute-start(bf16[304,512]{1,0:T(8,128)(2,1)S(1)} %collective-permute-done.10.rest_3_.rest_13_), channel_id=1, source_target_pairs={{0,2},{2,0},{4,6},{6,4},{8,10},{10,8},{12,14},{14,12},{16,18},{18,... | collective-permute-start | bytes 933896 | tf_op jit(solution)/shard_map/ppermute | solution.py:958
  60.2 2.0 %collective-permute-start.18 = (bf16[288,512]{1,0:T(8,128)(2,1)S(1)}, bf16[288,512]{1,0:T(8,128)(2,1)S(1)}, u32[]{:S(2)}, u32[]{:S(2)}) collective-permute-start(bf16[288,512]{1,0:T(8,128)(2,1)S(1)} %collective-permute-done.9.rest_2_.rest_12_), channel_id=1, source_target_pairs={{0,2},{2,0},{4,6},{6,4},{8,10},{10,8},{12,14},{14,12},{16,18},{18,... | collective-permute-start | bytes 884744 | tf_op jit(solution)/shard_map/ppermute | solution.py:958
  62.2 4.8 %copy-start.1 = (bf16[512,768]{1,0:T(8,128)(2,1)S(1)}, bf16[512,768]{1,0:T(8,128)(2,1)}, u32[]{:S(2)}) copy-start(bf16[512,768]{1,0:T(8,128)(2,1)} %cot_ref.6) | copy-start | bytes 2359300
  64.9 7.8 %collective-permute-start.20 = (bf16[256,384]{1,0:T(8,128)(2,1)S(1)}, bf16[256,384]{1,0:T(8,128)(2,1)S(1)}, u32[]{:S(2)}, u32[]{:S(2)}) collective-permute-start(bf16[256,384]{1,0:T(8,128)(2,1)S(1)} %get-tuple-element.161.own_ref.rest_2_), channel_id=1, source_target_pairs={{0,1},{1,0},{2,3},{3,2},{4,5},{5,4},{6,7},{7,6},{8,9},{9,8},{10,11... | collective-permute-start | bytes 589832 | tf_op jit(solution)/shard_map/ppermute | solution.py:1123
  66.5 10.5 %collective-permute-start.21 = (bf16[256,384]{1,0:T(8,128)(2,1)S(1)}, bf16[256,384]{1,0:T(8,128)(2,1)S(1)}, u32[]{:S(2)}, u32[]{:S(2)}) collective-permute-start(bf16[256,384]{1,0:T(8,128)(2,1)S(1)} %get-tuple-element.168.own_ref.rest_3_), channel_id=1, source_target_pairs={{0,1},{1,0},{2,3},{3,2},{4,5},{5,4},{6,7},{7,6},{8,9},{9,8},{10,11... | collective-permute-start | bytes 589832 | tf_op jit(solution)/shard_map/ppermute | solution.py:1123
  75.5 10.0 %collective-permute-start.26 = (bf16[256,768]{1,0:T(8,128)(2,1)S(1)}, bf16[256,768]{1,0:T(8,128)(2,1)S(1)}, u32[]{:S(2)}, u32[]{:S(2)}) collective-permute-start(bf16[256,768]{1,0:T(8,128)(2,1)S(1)} %get-tuple-element.181.back_ref), channel_id=1, source_target_pairs={{0,1},{1,0},{2,3},{3,2},{4,5},{5,4},{6,7},{7,6},{8,9},{9,8},{10,11... | collective-permute-start | bytes 1179656 | tf_op jit(solution)/shard_map/ppermute | solution.py:1131
  83.4 1.6 %collective-permute-start.22 = (bf16[48,3072]{1,0:T(8,128)(2,1)S(1)}, bf16[48,3072]{1,0:T(8,128)(2,1)S(1)}, u32[]{:S(2)}, u32[]{:S(2)}) collective-permute-start(bf16[48,3072]{1,0:T(8,128)(2,1)S(1)} %get-tuple-element.177), channel_id=1, source_target_pairs={{0,2},{2,0},{4,6},{6,4},{8,10},{10,8},{12,14},{14,12},{16,18},{18,... | collective-permute-start | bytes 884744 | tf_op jit(solution)/shard_map/ppermute | solution.py:978
  83.5 2.0 %collective-permute-start.24 = (bf16[48,3072]{1,0:T(8,128)(2,1)S(1)}, bf16[48,3072]{1,0:T(8,128)(2,1)S(1)}, u32[]{:S(2)}, u32[]{:S(2)}) collective-permute-start(bf16[48,3072]{1,0:T(8,128)(2,1)S(1)} %get-tuple-element.178), channel_id=1, source_target_pairs={{0,2},{2,0},{4,6},{6,4},{8,10},{10,8},{12,14},{14,12},{16,18},{18,... | collective-permute-start | bytes 884744 | tf_op jit(solution)/shard_map/ppermute | solution.py:978
  85.5 9.9 %collective-permute-start.27 = (bf16[6,48,3072]{2,1,0:T(8,128)(2,1)S(1)}, bf16[6,48,3072]{2,1,0:T(8,128)(2,1)S(1)}, u32[]{:S(2)}, u32[]{:S(2)}) collective-permute-start(bf16[6,48,3072]{2,1,0:T(8,128)(2,1)S(1)} %get-tuple-element.197), channel_id=1, source_target_pairs={{0,2},{2,0},{4,6},{6,4},{8,10},{10,8},{12,14},{14,12},{16,18},{18,... | collective-permute-start | bytes 5308424 | tf_op jit(solution)/shard_map/ppermute | solution.py:997
  85.8 9.3 %collective-permute-start.23 = (bf16[48,3072]{1,0:T(8,128)(2,1)S(1)}, bf16[48,3072]{1,0:T(8,128)(2,1)S(1)}, u32[]{:S(2)}, u32[]{:S(2)}) collective-permute-start(bf16[48,3072]{1,0:T(8,128)(2,1)S(1)} %get-tuple-element.266), channel_id=1, source_target_pairs={{0,4},{2,6},{8,0},{10,2},{16,8},{18,10},{24,16},{26,18},{28,24},{3... | collective-permute-start | bytes 884744 | tf_op jit(solution)/shard_map/ppermute | solution.py:1006
  86.3 9.1 %collective-permute-start.25 = (bf16[48,3072]{1,0:T(8,128)(2,1)S(1)}, bf16[48,3072]{1,0:T(8,128)(2,1)S(1)}, u32[]{:S(2)}, u32[]{:S(2)}) collective-permute-start(bf16[48,3072]{1,0:T(8,128)(2,1)S(1)} %get-tuple-element.265), channel_id=1, source_target_pairs={{0,8},{2,10},{8,16},{10,18},{16,24},{18,26},{24,28},{26,30},{28,20... | collective-permute-start | bytes 884744 | tf_op jit(solution)/shard_map/ppermute | solution.py:1006
  87.9 10.9 %collective-permute-start.32 = (bf16[256,768]{1,0:T(8,128)(2,1)S(1)}, bf16[256,768]{1,0:T(8,128)(2,1)S(1)}, u32[]{:S(2)}, u32[]{:S(2)}) collective-permute-start(bf16[256,768]{1,0:T(8,128)(2,1)S(1)} %get-tuple-element.209.back_ref), channel_id=1, source_target_pairs={{0,1},{1,0},{2,3},{3,2},{4,5},{5,4},{6,7},{7,6},{8,9},{9,8},{10,11... | collective-permute-start | bytes 1179656 | tf_op jit(solution)/shard_map/ppermute | solution.py:1131
  95.6 8.3 %collective-permute-start.28 = (bf16[48,3072]{1,0:T(8,128)(2,1)S(1)}, bf16[48,3072]{1,0:T(8,128)(2,1)S(1)}, u32[]{:S(2)}, u32[]{:S(2)}) collective-permute-start(bf16[48,3072]{1,0:T(8,128)(2,1)S(1)} %get-tuple-element.264), channel_id=1, source_target_pairs={{0,4},{2,6},{8,0},{10,2},{16,8},{18,10},{24,16},{26,18},{28,24},{3... | collective-permute-start | bytes 884744 | tf_op jit(solution)/shard_map/ppermute | solution.py:1006
  96.4 8.0 %collective-permute-start.29 = (bf16[48,3072]{1,0:T(8,128)(2,1)S(1)}, bf16[48,3072]{1,0:T(8,128)(2,1)S(1)}, u32[]{:S(2)}, u32[]{:S(2)}) collective-permute-start(bf16[48,3072]{1,0:T(8,128)(2,1)S(1)} %get-tuple-element.263), channel_id=1, source_target_pairs={{0,8},{2,10},{8,16},{10,18},{16,24},{18,26},{24,28},{26,30},{28,20... | collective-permute-start | bytes 884744 | tf_op jit(solution)/shard_map/ppermute | solution.py:1006
  101.3 6.7 %collective-permute-start.33 = (f32[64,128]{1,0:T(8,128)S(1)}, f32[64,128]{1,0:T(8,128)S(1)}, u32[]{:S(2)}, u32[]{:S(2)}) collective-permute-start(f32[64,128]{1,0:T(8,128)S(1)} %get-tuple-element.214.ga_ref), channel_id=1, source_target_pairs={{0,1},{1,0},{2,3},{3,2},{4,5},{5,4},{6,7},{7,6},{8,9},{9,8},{10,11... | collective-permute-start | bytes 98312 | tf_op jit(solution)/shard_map/ppermute | solution.py:1155
  102.8 8.1 %collective-permute-start.35 = (bf16[192,768]{1,0:T(8,128)(2,1)S(1)}, bf16[192,768]{1,0:T(8,128)(2,1)S(1)}, u32[]{:S(2)}, u32[]{:S(2)}) collective-permute-start(bf16[192,768]{1,0:T(8,128)(2,1)S(1)} %get-tuple-element.222), channel_id=1, source_target_pairs={{0,1},{1,0},{2,3},{3,2},{4,5},{5,4},{6,7},{7,6},{8,9},{9,8},{10,11... | collective-permute-start | bytes 884744 | tf_op jit(solution)/shard_map/ppermute | solution.py:1156
  104.6 7.1 %collective-permute-start.30 = (bf16[48,3072]{1,0:T(8,128)(2,1)S(1)}, bf16[48,3072]{1,0:T(8,128)(2,1)S(1)}, u32[]{:S(2)}, u32[]{:S(2)}) collective-permute-start(bf16[48,3072]{1,0:T(8,128)(2,1)S(1)} %get-tuple-element.262), channel_id=1, source_target_pairs={{0,4},{2,6},{8,0},{10,2},{16,8},{18,10},{24,16},{26,18},{28,24},{3... | collective-permute-start | bytes 884744 | tf_op jit(solution)/shard_map/ppermute | solution.py:1006
  106.1 6.7 %collective-permute-start.31 = (bf16[48,3072]{1,0:T(8,128)(2,1)S(1)}, bf16[48,3072]{1,0:T(8,128)(2,1)S(1)}, u32[]{:S(2)}, u32[]{:S(2)}) collective-permute-start(bf16[48,3072]{1,0:T(8,128)(2,1)S(1)} %get-tuple-element.261), channel_id=1, source_target_pairs={{0,8},{2,10},{8,16},{10,18},{16,24},{18,26},{24,28},{26,30},{28,20... | collective-permute-start | bytes 884744 | tf_op jit(solution)/shard_map/ppermute | solution.py:1006
  109.7 1.6 %collective-permute-start.34 = (bf16[272,512]{1,0:T(8,128)(2,1)S(1)}, bf16[272,512]{1,0:T(8,128)(2,1)S(1)}, u32[]{:S(2)}, u32[]{:S(2)}) collective-permute-start(bf16[272,512]{1,0:T(8,128)(2,1)S(1)} %get-tuple-element.221), channel_id=1, source_target_pairs={{0,2},{2,0},{4,6},{6,4},{8,10},{10,8},{12,14},{14,12},{16,18},{18,... | collective-permute-start | bytes 835592 | tf_op jit(solution)/shard_map/ppermute | solution.py:978
  112.9 9.1 %collective-permute-start.37 = (bf16[7,272,512]{2,1,0:T(8,128)(2,1)S(1)}, bf16[7,272,512]{2,1,0:T(8,128)(2,1)S(1)}, u32[]{:S(2)}, u32[]{:S(2)}) collective-permute-start(bf16[7,272,512]{2,1,0:T(8,128)(2,1)S(1)} %get-tuple-element.231), channel_id=1, source_target_pairs={{0,2},{2,0},{4,6},{6,4},{8,10},{10,8},{12,14},{14,12},{16,18},{18,... | collective-permute-start | bytes 5849096 | tf_op jit(solution)/shard_map/ppermute | solution.py:997
  112.9 9.1 %collective-permute-start.38 = (bf16[272,512]{1,0:T(8,128)(2,1)S(1)}, bf16[272,512]{1,0:T(8,128)(2,1)S(1)}, u32[]{:S(2)}, u32[]{:S(2)}) collective-permute-start(bf16[272,512]{1,0:T(8,128)(2,1)S(1)} %fusion.8), channel_id=1, source_target_pairs={{0,8},{2,10},{8,16},{10,18},{16,24},{18,26},{24,28},{26,30},{28,20... | collective-permute-start | bytes 835592 | tf_op jit(solution)/shard_map/ppermute | solution.py:1006
  113.7 12.4 %collective-permute-start.36 = (bf16[48,3072]{1,0:T(8,128)(2,1)S(1)}, bf16[48,3072]{1,0:T(8,128)(2,1)S(1)}, u32[]{:S(2)}, u32[]{:S(2)}) collective-permute-start(bf16[48,3072]{1,0:T(8,128)(2,1)S(1)} %fusion.3), channel_id=1, source_target_pairs={{0,4},{2,6},{8,0},{10,2},{16,8},{18,10},{24,16},{26,18},{28,24},{3... | collective-permute-start | bytes 884744 | tf_op jit(solution)/shard_map/ppermute | solution.py:1006
  115.2 14.1 %collective-permute-start.41 = (bf16[320,768]{1,0:T(8,128)(2,1)S(1)}, bf16[320,768]{1,0:T(8,128)(2,1)S(1)}, u32[]{:S(2)}, u32[]{:S(2)}) collective-permute-start(bf16[320,768]{1,0:T(8,128)(2,1)S(1)} %get-tuple-element.224), channel_id=1, source_target_pairs={{0,1},{1,0},{2,3},{3,2},{4,5},{5,4},{6,7},{7,6},{8,9},{9,8},{10,11... | collective-permute-start | bytes 1474568 | tf_op jit(solution)/shard_map/ppermute | solution.py:1172
  122.1 8.3 %collective-permute-start.40 = (bf16[272,512]{1,0:T(8,128)(2,1)S(1)}, bf16[272,512]{1,0:T(8,128)(2,1)S(1)}, u32[]{:S(2)}, u32[]{:S(2)}) collective-permute-start(bf16[272,512]{1,0:T(8,128)(2,1)S(1)} %fusion.14), channel_id=1, source_target_pairs={{0,4},{2,6},{8,0},{10,2},{16,8},{18,10},{24,16},{26,18},{28,24},{3... | collective-permute-start | bytes 835592 | tf_op jit(solution)/shard_map/ppermute | solution.py:1006
  123.8 8.0 %collective-permute-start.39 = (bf16[272,512]{1,0:T(8,128)(2,1)S(1)}, bf16[272,512]{1,0:T(8,128)(2,1)S(1)}, u32[]{:S(2)}, u32[]{:S(2)}) collective-permute-start(bf16[272,512]{1,0:T(8,128)(2,1)S(1)} %fusion.13), channel_id=1, source_target_pairs={{0,8},{2,10},{8,16},{10,18},{16,24},{18,26},{24,28},{26,30},{28,20... | collective-permute-start | bytes 835592 | tf_op jit(solution)/shard_map/ppermute | solution.py:1006
  124.3 13.4 %collective-permute-start.45 = (bf16[256,768]{1,0:T(8,128)(2,1)S(1)}, bf16[256,768]{1,0:T(8,128)(2,1)S(1)}, u32[]{:S(2)}, u32[]{:S(2)}) collective-permute-start(bf16[256,768]{1,0:T(8,128)(2,1)S(1)} %get-tuple-element.239.mine_ref), channel_id=1, source_target_pairs={{0,1},{1,0},{2,3},{3,2},{4,5},{5,4},{6,7},{7,6},{8,9},{9,8},{10,11... | collective-permute-start | bytes 1179656 | tf_op jit(solution)/shard_map/ppermute | solution.py:1178
  132.0 7.1 %collective-permute-start.43 = (bf16[272,512]{1,0:T(8,128)(2,1)S(1)}, bf16[272,512]{1,0:T(8,128)(2,1)S(1)}, u32[]{:S(2)}, u32[]{:S(2)}) collective-permute-start(bf16[272,512]{1,0:T(8,128)(2,1)S(1)} %get-tuple-element.260), channel_id=1, source_target_pairs={{0,8},{2,10},{8,16},{10,18},{16,24},{18,26},{24,28},{26,30},{28,20... | collective-permute-start | bytes 835592 | tf_op jit(solution)/shard_map/ppermute | solution.py:1006
  132.5 6.7 %collective-permute-start.44 = (bf16[272,512]{1,0:T(8,128)(2,1)S(1)}, bf16[272,512]{1,0:T(8,128)(2,1)S(1)}, u32[]{:S(2)}, u32[]{:S(2)}) collective-permute-start(bf16[272,512]{1,0:T(8,128)(2,1)S(1)} %get-tuple-element.259), channel_id=1, source_target_pairs={{0,4},{2,6},{8,0},{10,2},{16,8},{18,10},{24,16},{26,18},{28,24},{3... | collective-permute-start | bytes 835592 | tf_op jit(solution)/shard_map/ppermute | solution.py:1006
  134.1 10.9 %collective-permute-start.42 = (bf16[256,768]{1,0:T(8,128)(2,1)S(1)}, bf16[256,768]{1,0:T(8,128)(2,1)S(1)}, u32[]{:S(2)}, u32[]{:S(2)}) collective-permute-start(bf16[256,768]{1,0:T(8,128)(2,1)S(1)} %get-tuple-element.237.mine_ref), channel_id=1, source_target_pairs={{0,1},{1,0},{2,3},{3,2},{4,5},{5,4},{6,7},{7,6},{8,9},{9,8},{10,11... | collective-permute-start | bytes 1179656 | tf_op jit(solution)/shard_map/ppermute | solution.py:1181
  139.5 6.7 %collective-permute-start.46 = (bf16[272,512]{1,0:T(8,128)(2,1)S(1)}, bf16[272,512]{1,0:T(8,128)(2,1)S(1)}, u32[]{:S(2)}, u32[]{:S(2)}) collective-permute-start(bf16[272,512]{1,0:T(8,128)(2,1)S(1)} %get-tuple-element.258), channel_id=1, source_target_pairs={{0,8},{2,10},{8,16},{10,18},{16,24},{18,26},{24,28},{26,30},{28,20... | collective-permute-start | bytes 835592 | tf_op jit(solution)/shard_map/ppermute | solution.py:1006
  140.2 6.5 %collective-permute-start.47 = (bf16[272,512]{1,0:T(8,128)(2,1)S(1)}, bf16[272,512]{1,0:T(8,128)(2,1)S(1)}, u32[]{:S(2)}, u32[]{:S(2)}) collective-permute-start(bf16[272,512]{1,0:T(8,128)(2,1)S(1)} %get-tuple-element.257), channel_id=1, source_target_pairs={{0,4},{2,6},{8,0},{10,2},{16,8},{18,10},{24,16},{26,18},{28,24},{3... | collective-permute-start | bytes 835592 | tf_op jit(solution)/shard_map/ppermute | solution.py:1006

commit v10 on v9

--- a/solution.py
+++ b/solution.py
@@ -1114,7 +1114,7 @@
         early, late, near = list(range(UNITS // 2)), list(range(UNITS // 2, UNITS)), []
         begun = mixer_first(plan, where_in, tokens, segment_ids, units[: UNITS // 2], shares[: UNITS // 2], heads)
 
-    own = [n for n in late if shares[n][0] < UNITS // 2] if ring else late[:1]
+    own = [n for n in late if shares[n][0] < UNITS // 2 or shares[n][2] == plan.deep] if ring else late[:1]
     late = [n for n in late if n not in own]
     begun = mixer_next(plan, where_in, begun, [units[n] for n in own], [shares[n] for n in own])
     e, wv, _, va, sums, n1, gains, *mixed = mixer_forward(

time: 148 us -> 148 us (level)
  no operation moved by 1% of the time
where the time goes in v10:
time: 148 us
  waiting for transfers between devices  61 us (41%)
  starting transfers between devices  42.9 us (29%)
  Pallas kernels  37.6 us (25%)
  other arithmetic  3.42 us (2%)
    pallas_call x23, Pallas kernels, run(): pl.pallas_call(kernel, out_shape=tuple(results), in_specs=specs, out_spec...  37.6 us
    ppermute x3, waiting for transfers between devices, hop(): lax.ppermute(up, 'dp', ring.up)  24.4 us
    ppermute x14, starting transfers between devices, hop(): lax.ppermute(value, 'dp', self.ring.up if way == 'up' else self.ring.down)  14.7 us
    ppermute x14, waiting for transfers between devices, hop(): lax.ppermute(value, 'dp', self.ring.up if way == 'up' else self.ring.down)  13.3 us
    ppermute x2, waiting for transfers between devices, shards(): lowers = [lax.ppermute(lower, 'dp', way) for way in ways]  8.23 us
    ppermute x3, starting transfers between devices, hop(): lax.ppermute(up, 'dp', ring.up)  4.83 us
    ppermute x1, waiting for transfers between devices, shards(): two_other = lax.ppermute(ffn_two, 'mp', flip)  3.22 us
    ppermute x2, starting transfers between devices, shards(): uppers = [lax.ppermute(upper, 'dp', way) for way in ways]  3.08 us
  transfers between devices with their start and end apart: 48, of which 31 were waited for; matrix products, arithmetic and copies ran while one was open for 2% of the time, Pallas kernels for 22%

profile of v10, /device:TPU:0, one launch (start us, length us, event | category | flops | bytes accessed | tf_op | source)
XLA Modules:
  0.0 147.6 jit_solution(13927636124815877573)
XLA Ops:
  0.6 1.4 pack_unit.1
  2.0 3.1 %collective-permute-start = (bf16[480,512]{1,0:T(8,128)(2,1)S(1)}, bf16[480,512]{1,0:T(8,128)(2,1)S(1)}, u32[]{:S(2)}, u32[]{:S(2)}) collective-permute-start(bf16[480,512]{1,0:T(8,128)(2,1)S(1)} %get-tuple-element.132.refs_0_), channel_id=1, source_target_pairs={{0,8},{2,10},{8,16},{10,18},{16,24},{18,26},{24,28},{26,30},{28,20... | collective-permute-start | bytes 1474568 | tf_op jit(solution)/shard_map/ppermute | solution.py:1063
  5.1 0.7 broadcast_add_fusion.3
  6.0 2.0 %collective-permute-start.2 = (bf16[48,384]{1,0:T(8,128)(2,1)S(1)}, bf16[48,384]{1,0:T(8,128)(2,1)S(1)}, u32[]{:S(2)}, u32[]{:S(2)}) collective-permute-start(bf16[48,384]{1,0:T(8,128)(2,1)S(1)} %get-tuple-element.135), channel_id=1, source_target_pairs={{0,1},{1,0},{2,3},{3,2},{4,5},{5,4},{6,7},{7,6},{8,9},{9,8},{10,11... | collective-permute-start | bytes 110600 | tf_op jit(solution)/shard_map/ppermute | solution.py:1064
  7.9 2.0 %collective-permute-done.2.other_ref = bf16[48,384]{1,0:T(8,128)(2,1)S(1)} collective-permute-done((bf16[48,384]{1,0:T(8,128)(2,1)S(1)}, bf16[48,384]{1,0:T(8,128)(2,1)S(1)}, u32[]{:S(2)}, u32[]{:S(2)}) %collective-permute-start.2) | collective-permute-done | bytes 36896 | tf_op jit(solution)/shard_map/ppermute | solution.py:1064
  9.9 2.1 %collective-permute-start.3 = (bf16[112,512]{1,0:T(8,128)(2,1)S(1)}, bf16[112,512]{1,0:T(8,128)(2,1)S(1)}, u32[]{:S(2)}, u32[]{:S(2)}) collective-permute-start(bf16[112,512]{1,0:T(8,128)(2,1)S(1)} %fill_low.1.refs_1_), channel_id=1, source_target_pairs={{0,8},{2,10},{8,16},{10,18},{16,24},{18,26},{24,28},{26,30},{28,20... | collective-permute-start | bytes 344072 | tf_op jit(solution)/shard_map/ppermute | solution.py:1066
  12.0 6.7 %collective-permute-done.3.refs_2_ = bf16[112,512]{1,0:T(8,128)(2,1)S(1)} collective-permute-done((bf16[112,512]{1,0:T(8,128)(2,1)S(1)}, bf16[112,512]{1,0:T(8,128)(2,1)S(1)}, u32[]{:S(2)}, u32[]{:S(2)}) %collective-permute-start.3) | collective-permute-done | bytes 114720 | tf_op jit(solution)/shard_map/ppermute | solution.py:1066
  18.7 1.5 %collective-permute-done.4.refs_3_ = bf16[112,512]{1,0:T(8,128)(2,1)S(1)} collective-permute-done((bf16[112,512]{1,0:T(8,128)(2,1)S(1)}, bf16[112,512]{1,0:T(8,128)(2,1)S(1)}, u32[]{:S(2)}, u32[]{:S(2)}) %collective-permute-start.4) | collective-permute-done | bytes 114720 | tf_op jit(solution)/shard_map/ppermute | solution.py:1066
  20.4 1.6 %collective-permute-start.5 = (bf16[592,512]{1,0:T(8,128)(2,1)S(1)}, bf16[592,512]{1,0:T(8,128)(2,1)S(1)}, u32[]{:S(2)}, u32[]{:S(2)}) collective-permute-start(bf16[592,512]{1,0:T(8,128)(2,1)S(1)} %get-tuple-element.140.rest_1_), channel_id=1, source_target_pairs={{0,8},{2,10},{8,16},{10,18},{16,24},{18,26},{24,28},{26,30},{28,20... | collective-permute-start | bytes 1818632 | tf_op jit(solution)/shard_map/ppermute | solution.py:953
  22.5 12.2 %collective-permute-done.5.rest_3_ = bf16[592,512]{1,0:T(8,128)(2,1)S(1)} collective-permute-done((bf16[592,512]{1,0:T(8,128)(2,1)S(1)}, bf16[592,512]{1,0:T(8,128)(2,1)S(1)}, u32[]{:S(2)}, u32[]{:S(2)}) %collective-permute-start.5) | collective-permute-done | bytes 606240 | tf_op jit(solution)/shard_map/ppermute | solution.py:953
  34.7 1.3 collective-permute-done.6.rest_4_
  36.0 1.6 %collective-permute-start.7 = (bf16[592,512]{1,0:T(8,128)(2,1)S(1)}, bf16[592,512]{1,0:T(8,128)(2,1)S(1)}, u32[]{:S(2)}, u32[]{:S(2)}) collective-permute-start(bf16[592,512]{1,0:T(8,128)(2,1)S(1)} %collective-permute-done.5.rest_3_), channel_id=1, source_target_pairs={{0,8},{2,10},{8,16},{10,18},{16,24},{18,26},{24,28},{26,30},{28,20... | collective-permute-start | bytes 1818632 | tf_op jit(solution)/shard_map/ppermute | solution.py:953
  38.7 10.3 %collective-permute-done.7.rest_0_.rest_10_ = bf16[592,512]{1,0:T(8,128)(2,1)S(1)} collective-permute-done((bf16[592,512]{1,0:T(8,128)(2,1)S(1)}, bf16[592,512]{1,0:T(8,128)(2,1)S(1)}, u32[]{:S(2)}, u32[]{:S(2)}) %collective-permute-start.7) | collective-permute-done | bytes 606240 | tf_op jit(solution)/shard_map/ppermute | solution.py:953
  49.0 1.3 collective-permute-done.8.rest_1_.rest_11_
  50.9 1.6 %collective-permute-start.9 = (bf16[288,512]{1,0:T(8,128)(2,1)S(1)}, bf16[288,512]{1,0:T(8,128)(2,1)S(1)}, u32[]{:S(2)}, u32[]{:S(2)}) collective-permute-start(bf16[288,512]{1,0:T(8,128)(2,1)S(1)} %slice.87), channel_id=1, source_target_pairs={{0,8},{2,10},{8,16},{10,18},{16,24},{18,26},{24,28},{26,30},{28,20... | collective-permute-start | bytes 884744 | tf_op jit(solution)/shard_map/ppermute | solution.py:953
  53.5 0.8 copy-done.12
  54.4 3.8 %mixer_first.1 = (bf16[6,512,512]{2,1,0:T(8,128)(2,1)S(1)}, bf16[768,384]{1,0:T(8,128)(2,1)S(1)}, bf16[16,16,128]{2,1,0:T(8,128)(2,1)S(1)}, f32[512,768]{1,0:T(8,128)S(1)}, f32[512,512]{1,0:T(8,128)S(1)}) custom-call(s32[16]{0:T(128)S(1)} %pad_add_fusion.where_ref, bf16[512,768]{1,0:T(8,128)(2,1)S(1)} %copy-done, s32[1,512]{1,0:T(1,128)S(1)} %copy-done.5, ...), custom_call_target="tpu_custom_call" | custom-call | flops 1 | bytes 1 | tf_op jit(solution)/shard_map/mixer_first/pallas_call | solution.py:36
  58.2 1.9 %collective-permute-done.9.rest_2_.rest_12_ = bf16[288,512]{1,0:T(8,128)(2,1)S(1)} collective-permute-done((bf16[288,512]{1,0:T(8,128)(2,1)S(1)}, bf16[288,512]{1,0:T(8,128)(2,1)S(1)}, u32[]{:S(2)}, u32[]{:S(2)}) %collective-permute-start.9) | collective-permute-done | bytes 294944 | tf_op jit(solution)/shard_map/ppermute | solution.py:953
  60.7 0.9 mixer_next.1
  62.2 2.6 %mixer_forward.1 = (bf16[6,512,512]{2,1,0:T(8,128)(2,1)S(1)}, bf16[768,384]{1,0:T(8,128)(2,1)S(1)}, bf16[16,16,128]{2,1,0:T(8,128)(2,1)S(1)}, bf16[512,768]{1,0:...) custom-call(s32[16]{0:T(128)S(1)} %pad_add_fusion.where_ref, ...), custom_call_target="tpu_custom_call", output_to_operand_aliasing={{0}: (1, {}), {1}: (2, {}), {2}: (3, {})} | custom-call | flops 1 | bytes 1 | tf_op jit(solution)/shard_map/mixer_forward/pallas_call | solution.py:36
  64.8 1.6 %collective-permute-start.20 = (bf16[256,384]{1,0:T(8,128)(2,1)S(1)}, bf16[256,384]{1,0:T(8,128)(2,1)S(1)}, u32[]{:S(2)}, u32[]{:S(2)}) collective-permute-start(bf16[256,384]{1,0:T(8,128)(2,1)S(1)} %get-tuple-element.161.own_ref.rest_2_), channel_id=1, source_target_pairs={{0,1},{1,0},{2,3},{3,2},{4,5},{5,4},{6,7},{7,6},{8,9},{9,8},{10,11... | collective-permute-start | bytes 589832 | tf_op jit(solution)/shard_map/ppermute | solution.py:1123
  66.9 5.0 %second_weights.1 = (bf16[6,768,512]{2,1,0:T(8,128)(2,1)S(1)}, bf16[768,768]{1,0:T(8,128)(2,1)S(1)}, f32[512,1536]{1,0:T(8,128)S(1)}, f32[512,768]{1,0:T(8,128)S...) custom-call(s32[16]{0:T(128)S(1)} %pad_add_fusion.where_ref, s32[1]{0:T(128)} %bitcast.second_ref, ...), custom_call_target="tpu_custom_call" | custom-call | flops 1 | bytes 1 | tf_op jit(solution)/shard_map/second_weights/pallas_call | solution.py:36
  71.9 0.7 collective-permute-done.20.other_ref
  72.6 2.7 %ffn_main.2 = (bf16[256,768]{1,0:T(8,128)(2,1)S(1)}, f32[256,768]{1,0:T(8,128)S(1)}, bf16[512,768]{1,0:T(8,128)(2,1)S(1)}, bf16[512,1536]{1,0:T(8,128)(2,1)S(1)}, bf16[512,1536]{1,0:T(8,128)(2,1)S(1)}) custom-call(s32[1]{0:T(128)} %bitcast.second_ref, bf16[512,768]{1,0:T(8,128)(2,1)S(1)} %copy-done, bf16[256,384]{1,0:T(8,128)(2,1)S(1)} %get-tuple-element.161.own_ref.rest_2_, ...), custom_call_target="tpu_custom_call" | custom-call | flops 1 | bytes 1 | tf_op jit(solution)/shard_map/ffn_main/pallas_call | solution.py:36
  75.3 1.6 %collective-permute-start.26 = (bf16[256,768]{1,0:T(8,128)(2,1)S(1)}, bf16[256,768]{1,0:T(8,128)(2,1)S(1)}, u32[]{:S(2)}, u32[]{:S(2)}) collective-permute-start(bf16[256,768]{1,0:T(8,128)(2,1)S(1)} %get-tuple-element.181.back_ref), channel_id=1, source_target_pairs={{0,1},{1,0},{2,3},{3,2},{4,5},{5,4},{6,7},{7,6},{8,9},{9,8},{10,11... | collective-permute-start | bytes 1179656 | tf_op jit(solution)/shard_map/ppermute | solution.py:1131
  76.9 2.7 %ffn_main.3 = (bf16[256,768]{1,0:T(8,128)(2,1)S(1)}, f32[256,768]{1,0:T(8,128)S(1)}, bf16[512,768]{1,0:T(8,128)(2,1)S(1)}, bf16[512,1536]{1,0:T(8,128)(2,1)S(1)}, bf16[512,1536]{1,0:T(8,128)(2,1)S(1)}) custom-call(s32[1]{0:T(128)} %bitcast.second_ref, bf16[512,768]{1,0:T(8,128)(2,1)S(1)} %copy-done, ...), custom_call_target="tpu_custom_call", output_to_operand_aliasing={{2}: (8, {}), {3}: (9, {}), {4}: (10, {})} | custom-call | flops 1 | bytes 1 | tf_op jit(solution)/shard_map/ffn_main/pallas_call | solution.py:36
  79.6 3.6 %ffn_grads.1 = (bf16[8,48,3072]{2,1,0:T(8,128)(2,1)S(1)}, bf16[48,3072]{1,0:T(8,128)(2,1)S(1)}, bf16[48,3072]{1,0:T(8,128)(2,1)S(1)}, bf16[6,48,3072]{2,1,0:T(8,128)(2,1)S(1)}) custom-call(s32[16]{0:T(128)S(1)} %pad_add_fusion.1.where_ref, bf16[512,768]{1,0:T(8,128)(2,1)S(1)} %copy-done.1, bf16[512,768]{1,0:T(8,128)(2,1)S(1)} %get-tuple-element.173.n2_ref, ...), custom_call_target="tpu_custom_call" | custom-call | flops 1 | bytes 1 | tf_op jit(solution)/shard_map/ffn_grads/pallas_call | solution.py:36
  83.8 1.1 collective-permute-done.22
  86.1 1.6 %collective-permute-start.25 = (bf16[48,3072]{1,0:T(8,128)(2,1)S(1)}, bf16[48,3072]{1,0:T(8,128)(2,1)S(1)}, u32[]{:S(2)}, u32[]{:S(2)}) collective-permute-start(bf16[48,3072]{1,0:T(8,128)(2,1)S(1)} %get-tuple-element.265), channel_id=1, source_target_pairs={{0,8},{2,10},{8,16},{10,18},{16,24},{18,26},{24,28},{26,30},{28,20... | collective-permute-start | bytes 884744 | tf_op jit(solution)/shard_map/ppermute | solution.py:1006
  87.7 1.3 collective-permute-start.32
  89.0 1.1 resid_back.2
  90.2 0.7 value_first.1.first_ref
  90.9 1.3 mixer_grads.2
  92.2 1.7 %ffn_out.1 = (bf16[192,768]{1,0:T(8,128)(2,1)S(1)}, bf16[320,768]{1,0:T(8,128)(2,1)S(1)}) custom-call(bf16[512,1536]{1,0:T(8,128)(2,1)S(1)} %get-tuple-element.186.act_ref, bf16[6,768,512]{2,1,0:T(8,128)(2,1)S(1)} %get-tuple-element.165.w_ref), custom_call_target="tpu_custom_call" | custom-call | flops 1 | bytes 1 | tf_op jit(solution)/shard_map/ffn_out/pallas_call | solution.py:36
  93.9 1.0 collective-permute-done.23
  95.5 0.7 collective-permute-start.28
  96.2 1.3 collective-permute-start.29
  97.6 1.0 collective-permute-done.32.other_ref
  98.6 1.1 resid_back.3
  99.7 1.4 value_back.1
  101.2 1.5 %collective-permute-start.33 = (f32[64,128]{1,0:T(8,128)S(1)}, f32[64,128]{1,0:T(8,128)S(1)}, u32[]{:S(2)}, u32[]{:S(2)}) collective-permute-start(f32[64,128]{1,0:T(8,128)S(1)} %get-tuple-element.214.ga_ref), channel_id=1, source_target_pairs={{0,1},{1,0},{2,3},{3,2},{4,5},{5,4},{6,7},{7,6},{8,9},{9,8},{10,11... | collective-permute-start | bytes 98312 | tf_op jit(solution)/shard_map/ppermute | solution.py:1155
  104.4 1.5 %collective-permute-start.30 = (bf16[48,3072]{1,0:T(8,128)(2,1)S(1)}, bf16[48,3072]{1,0:T(8,128)(2,1)S(1)}, u32[]{:S(2)}, u32[]{:S(2)}) collective-permute-start(bf16[48,3072]{1,0:T(8,128)(2,1)S(1)} %get-tuple-element.262), channel_id=1, source_target_pairs={{0,4},{2,6},{8,0},{10,2},{16,8},{18,10},{24,16},{26,18},{28,24},{3... | collective-permute-start | bytes 884744 | tf_op jit(solution)/shard_map/ppermute | solution.py:1006
  106.5 1.4 mixer_grads.3
  107.8 1.7 %weight_grads.1 = (bf16[8,272,512]{2,1,0:T(8,128)(2,1)S(1)}, bf16[272,512]{1,0:T(8,128)(2,1)S(1)}, bf16[7,272,512]{2,1,0:T(8,128)(2,1)S(1)}) custom-call(s32[16]{0:T(128)S(1)} %pad_add_fusion.1.where_ref, bf16[512,768]{1,0:T(8,128)(2,1)S(1)} %get-tuple-element.202.n1_ref, ...), custom_call_target="tpu_custom_call", output_to_operand_aliasing={{0}: (10, {}), {1}: (11, {}), {2}: (12, {})} | custom-call | flops 1 | bytes 1 | tf_op jit(solution)/shard_map/weight_grads/pallas_call | solution.py:36
  109.7 1.2 collective-permute-done.35
  111.5 1.2 collective-permute-done.31.up_ref
  113.5 1.5 %collective-permute-start.36 = (bf16[48,3072]{1,0:T(8,128)(2,1)S(1)}, bf16[48,3072]{1,0:T(8,128)(2,1)S(1)}, u32[]{:S(2)}, u32[]{:S(2)}) collective-permute-start(bf16[48,3072]{1,0:T(8,128)(2,1)S(1)} %fusion.3), channel_id=1, source_target_pairs={{0,4},{2,6},{8,0},{10,2},{16,8},{18,10},{24,16},{26,18},{28,24},{3... | collective-permute-start | bytes 884744 | tf_op jit(solution)/shard_map/ppermute | solution.py:1006
  115.0 1.7 %collective-permute-start.41 = (bf16[320,768]{1,0:T(8,128)(2,1)S(1)}, bf16[320,768]{1,0:T(8,128)(2,1)S(1)}, u32[]{:S(2)}, u32[]{:S(2)}) collective-permute-start(bf16[320,768]{1,0:T(8,128)(2,1)S(1)} %get-tuple-element.224), channel_id=1, source_target_pairs={{0,1},{1,0},{2,3},{3,2},{4,5},{5,4},{6,7},{7,6},{8,9},{9,8},{10,11... | collective-permute-start | bytes 1474568 | tf_op jit(solution)/shard_map/ppermute | solution.py:1172
  116.8 5.1 %collective-permute-done.38 = bf16[272,512]{1,0:T(8,128)(2,1)S(1)} collective-permute-done((bf16[272,512]{1,0:T(8,128)(2,1)S(1)}, bf16[272,512]{1,0:T(8,128)(2,1)S(1)}, u32[]{:S(2)}, u32[]{:S(2)}) %collective-permute-start.38) | collective-permute-done | bytes 278560 | tf_op jit(solution)/shard_map/ppermute | solution.py:1006
  121.9 1.6 %collective-permute-start.40 = (bf16[272,512]{1,0:T(8,128)(2,1)S(1)}, bf16[272,512]{1,0:T(8,128)(2,1)S(1)}, u32[]{:S(2)}, u32[]{:S(2)}) collective-permute-start(bf16[272,512]{1,0:T(8,128)(2,1)S(1)} %fusion.14), channel_id=1, source_target_pairs={{0,4},{2,6},{8,0},{10,2},{16,8},{18,10},{24,16},{26,18},{28,24},{3... | collective-permute-start | bytes 835592 | tf_op jit(solution)/shard_map/ppermute | solution.py:1006
  124.2 1.7 %collective-permute-start.45 = (bf16[256,768]{1,0:T(8,128)(2,1)S(1)}, bf16[256,768]{1,0:T(8,128)(2,1)S(1)}, u32[]{:S(2)}, u32[]{:S(2)}) collective-permute-start(bf16[256,768]{1,0:T(8,128)(2,1)S(1)} %get-tuple-element.239.mine_ref), channel_id=1, source_target_pairs={{0,1},{1,0},{2,3},{3,2},{4,5},{5,4},{6,7},{7,6},{8,9},{9,8},{10,11... | collective-permute-start | bytes 1179656 | tf_op jit(solution)/shard_map/ppermute | solution.py:1178
  125.9 3.2 %collective-permute-done.41 = bf16[320,768]{1,0:T(8,128)(2,1)S(1)} collective-permute-done((bf16[320,768]{1,0:T(8,128)(2,1)S(1)}, bf16[320,768]{1,0:T(8,128)(2,1)S(1)}, u32[]{:S(2)}, u32[]{:S(2)}) %collective-permute-start.41) | collective-permute-done | bytes 491552 | tf_op jit(solution)/shard_map/ppermute | solution.py:1172
  129.1 1.1 collective-permute-done.40
  130.2 1.5 collective-permute-done.39
  132.4 1.6 %collective-permute-start.44 = (bf16[272,512]{1,0:T(8,128)(2,1)S(1)}, bf16[272,512]{1,0:T(8,128)(2,1)S(1)}, u32[]{:S(2)}, u32[]{:S(2)}) collective-permute-start(bf16[272,512]{1,0:T(8,128)(2,1)S(1)} %get-tuple-element.259), channel_id=1, source_target_pairs={{0,4},{2,6},{8,0},{10,2},{16,8},{18,10},{24,16},{26,18},{28,24},{3... | collective-permute-start | bytes 835592 | tf_op jit(solution)/shard_map/ppermute | solution.py:1006
  134.0 1.8 %collective-permute-start.42 = (bf16[256,768]{1,0:T(8,128)(2,1)S(1)}, bf16[256,768]{1,0:T(8,128)(2,1)S(1)}, u32[]{:S(2)}, u32[]{:S(2)}) collective-permute-start(bf16[256,768]{1,0:T(8,128)(2,1)S(1)} %get-tuple-element.237.mine_ref), channel_id=1, source_target_pairs={{0,1},{1,0},{2,3},{3,2},{4,5},{5,4},{6,7},{7,6},{8,9},{9,8},{10,11... | collective-permute-start | bytes 1179656 | tf_op jit(solution)/shard_map/ppermute | solution.py:1181
  135.8 1.8 %collective-permute-done.45.other_ref = bf16[256,768]{1,0:T(8,128)(2,1)S(1)} collective-permute-done((bf16[256,768]{1,0:T(8,128)(2,1)S(1)}, bf16[256,768]{1,0:T(8,128)(2,1)S(1)}, u32[]{:S(2)}, u32[]{:S(2)}) %collective-permute-start.45) | collective-permute-done | bytes 393248 | tf_op jit(solution)/shard_map/ppermute | solution.py:1178
  137.6 1.4 collective-permute-done.43
  140.0 1.4 collective-permute-start.47
  141.4 0.9 ffn_result.1
  142.4 1.2 fusion
  143.6 1.1 token_grads.2.rest_0_
  144.9 1.2 token_grads.3
  146.5 0.9 mixer_result.1
  (100 shorter events, 14.4 us)
Async XLA Ops:
  2.0 18.2 %collective-permute-start = (bf16[480,512]{1,0:T(8,128)(2,1)S(1)}, bf16[480,512]{1,0:T(8,128)(2,1)S(1)}, u32[]{:S(2)}, u32[]{:S(2)}) collective-permute-start(bf16[480,512]{1,0:T(8,128)(2,1)S(1)} %get-tuple-element.132.refs_0_), channel_id=1, source_target_pairs={{0,8},{2,10},{8,16},{10,18},{16,24},{18,26},{24,28},{26,30},{28,20... | collective-permute-start | bytes 1474568 | tf_op jit(solution)/shard_map/ppermute | solution.py:1063
  5.1 15.1 %collective-permute-start.1 = (bf16[480,512]{1,0:T(8,128)(2,1)S(1)}, bf16[480,512]{1,0:T(8,128)(2,1)S(1)}, u32[]{:S(2)}, u32[]{:S(2)}) collective-permute-start(bf16[480,512]{1,0:T(8,128)(2,1)S(1)} %get-tuple-element.132.refs_0_), channel_id=1, source_target_pairs={{0,4},{2,6},{8,0},{10,2},{16,8},{18,10},{24,16},{26,18},{28,24},{3... | collective-permute-start | bytes 1474568 | tf_op jit(solution)/shard_map/ppermute | solution.py:1063
  6.0 4.0 %collective-permute-start.2 = (bf16[48,384]{1,0:T(8,128)(2,1)S(1)}, bf16[48,384]{1,0:T(8,128)(2,1)S(1)}, u32[]{:S(2)}, u32[]{:S(2)}) collective-permute-start(bf16[48,384]{1,0:T(8,128)(2,1)S(1)} %get-tuple-element.135), channel_id=1, source_target_pairs={{0,1},{1,0},{2,3},{3,2},{4,5},{5,4},{6,7},{7,6},{8,9},{9,8},{10,11... | collective-permute-start | bytes 110600 | tf_op jit(solution)/shard_map/ppermute | solution.py:1064
  9.9 44.4 %copy-start = (bf16[512,768]{1,0:T(8,128)(2,1)S(1)}, bf16[512,768]{1,0:T(8,128)(2,1)}, u32[]{:S(2)}) copy-start(bf16[512,768]{1,0:T(8,128)(2,1)} %tok_ref.11) | copy-start | bytes 2359300
  9.9 44.4 %copy-start.5 = (s32[1,512]{1,0:T(1,128)S(1)}, s32[1,512]{1,0:T(1,128)}, u32[]{:S(2)}) copy-start(s32[1,512]{1,0:T(1,128)} %seg_ref.1) | copy-start | bytes 6148
  9.9 8.8 %collective-permute-start.3 = (bf16[112,512]{1,0:T(8,128)(2,1)S(1)}, bf16[112,512]{1,0:T(8,128)(2,1)S(1)}, u32[]{:S(2)}, u32[]{:S(2)}) collective-permute-start(bf16[112,512]{1,0:T(8,128)(2,1)S(1)} %fill_low.1.refs_1_), channel_id=1, source_target_pairs={{0,8},{2,10},{8,16},{10,18},{16,24},{18,26},{24,28},{26,30},{28,20... | collective-permute-start | bytes 344072 | tf_op jit(solution)/shard_map/ppermute | solution.py:1066
  12.0 8.2 %collective-permute-start.4 = (bf16[112,512]{1,0:T(8,128)(2,1)S(1)}, bf16[112,512]{1,0:T(8,128)(2,1)S(1)}, u32[]{:S(2)}, u32[]{:S(2)}) collective-permute-start(bf16[112,512]{1,0:T(8,128)(2,1)S(1)} %fill_low.1.refs_1_), channel_id=1, source_target_pairs={{0,4},{2,6},{8,0},{10,2},{16,8},{18,10},{24,16},{26,18},{28,24},{3... | collective-permute-start | bytes 344072 | tf_op jit(solution)/shard_map/ppermute | solution.py:1066
  20.3 32.7 %copy-start.3 = (bf16[592,512]{1,0:T(8,128)(2,1)}, bf16[592,512]{1,0:T(8,128)(2,1)S(1)}, u32[]{:S(2)}) copy-start(bf16[592,512]{1,0:T(8,128)(2,1)S(1)} %get-tuple-element.140.rest_1_) | copy-start | bytes 1818628
  20.4 32.7 %copy-start.4 = (bf16[592,512]{1,0:T(8,128)(2,1)}, bf16[592,512]{1,0:T(8,128)(2,1)S(1)}, u32[]{:S(2)}) copy-start(bf16[592,512]{1,0:T(8,128)(2,1)S(1)} %get-tuple-element.141.rest_2_) | copy-start | bytes 1818628
  20.4 14.3 %collective-permute-start.5 = (bf16[592,512]{1,0:T(8,128)(2,1)S(1)}, bf16[592,512]{1,0:T(8,128)(2,1)S(1)}, u32[]{:S(2)}, u32[]{:S(2)}) collective-permute-start(bf16[592,512]{1,0:T(8,128)(2,1)S(1)} %get-tuple-element.140.rest_1_), channel_id=1, source_target_pairs={{0,8},{2,10},{8,16},{10,18},{16,24},{18,26},{24,28},{26,30},{28,20... | collective-permute-start | bytes 1818632 | tf_op jit(solution)/shard_map/ppermute | solution.py:953
  22.0 13.9 %collective-permute-start.6 = (bf16[592,512]{1,0:T(8,128)(2,1)S(1)}, bf16[592,512]{1,0:T(8,128)(2,1)S(1)}, u32[]{:S(2)}, u32[]{:S(2)}) collective-permute-start(bf16[592,512]{1,0:T(8,128)(2,1)S(1)} %get-tuple-element.141.rest_2_), channel_id=1, source_target_pairs={{0,4},{2,6},{8,0},{10,2},{16,8},{18,10},{24,16},{26,18},{28,24},{3... | collective-permute-start | bytes 1818632 | tf_op jit(solution)/shard_map/ppermute | solution.py:953
  34.7 18.4 %copy-start.6 = (bf16[592,512]{1,0:T(8,128)(2,1)}, bf16[592,512]{1,0:T(8,128)(2,1)S(1)}, u32[]{:S(2)}) copy-start(bf16[592,512]{1,0:T(8,128)(2,1)S(1)} %collective-permute-done.5.rest_3_) | copy-start | bytes 1818628
  36.0 17.1 %copy-start.7 = (bf16[592,512]{1,0:T(8,128)(2,1)}, bf16[592,512]{1,0:T(8,128)(2,1)S(1)}, u32[]{:S(2)}) copy-start(bf16[592,512]{1,0:T(8,128)(2,1)S(1)} %collective-permute-done.6.rest_4_) | copy-start | bytes 1818628
  36.0 13.0 %collective-permute-start.7 = (bf16[592,512]{1,0:T(8,128)(2,1)S(1)}, bf16[592,512]{1,0:T(8,128)(2,1)S(1)}, u32[]{:S(2)}, u32[]{:S(2)}) collective-permute-start(bf16[592,512]{1,0:T(8,128)(2,1)S(1)} %collective-permute-done.5.rest_3_), channel_id=1, source_target_pairs={{0,8},{2,10},{8,16},{10,18},{16,24},{18,26},{24,28},{26,30},{28,20... | collective-permute-start | bytes 1818632 | tf_op jit(solution)/shard_map/ppermute | solution.py:953
  37.5 12.7 %collective-permute-start.8 = (bf16[592,512]{1,0:T(8,128)(2,1)S(1)}, bf16[592,512]{1,0:T(8,128)(2,1)S(1)}, u32[]{:S(2)}, u32[]{:S(2)}) collective-permute-start(bf16[592,512]{1,0:T(8,128)(2,1)S(1)} %collective-permute-done.6.rest_4_), channel_id=1, source_target_pairs={{0,4},{2,6},{8,0},{10,2},{16,8},{18,10},{24,16},{26,18},{28,24},{3... | collective-permute-start | bytes 1818632 | tf_op jit(solution)/shard_map/ppermute | solution.py:953
  38.0 15.0 %copy-start.2 = (bf16[592,512]{1,0:T(8,128)(2,1)}, bf16[592,512]{1,0:T(8,128)(2,1)S(1)}, u32[]{:S(2)}) copy-start(bf16[592,512]{1,0:T(8,128)(2,1)S(1)} %join_units.3.rest_0_) | copy-start | bytes 1818628
  38.0 12.3 %collective-permute-start.11 = (bf16[592,512]{1,0:T(8,128)(2,1)S(1)}, bf16[592,512]{1,0:T(8,128)(2,1)S(1)}, u32[]{:S(2)}, u32[]{:S(2)}) collective-permute-start(bf16[592,512]{1,0:T(8,128)(2,1)S(1)} %join_units.3.rest_0_), channel_id=1, source_target_pairs={{0,2},{2,0},{4,6},{6,4},{8,10},{10,8},{12,14},{14,12},{16,18},{18,... | collective-permute-start | bytes 1818632 | tf_op jit(solution)/shard_map/ppermute | solution.py:958
  38.1 12.7 %collective-permute-start.12 = (bf16[592,512]{1,0:T(8,128)(2,1)S(1)}, bf16[592,512]{1,0:T(8,128)(2,1)S(1)}, u32[]{:S(2)}, u32[]{:S(2)}) collective-permute-start(bf16[592,512]{1,0:T(8,128)(2,1)S(1)} %get-tuple-element.140.rest_1_), channel_id=1, source_target_pairs={{0,2},{2,0},{4,6},{6,4},{8,10},{10,8},{12,14},{14,12},{16,18},{18,... | collective-permute-start | bytes 1818632 | tf_op jit(solution)/shard_map/ppermute | solution.py:958
  38.6 13.9 %collective-permute-start.13 = (bf16[592,512]{1,0:T(8,128)(2,1)S(1)}, bf16[592,512]{1,0:T(8,128)(2,1)S(1)}, u32[]{:S(2)}, u32[]{:S(2)}) collective-permute-start(bf16[592,512]{1,0:T(8,128)(2,1)S(1)} %get-tuple-element.141.rest_2_), channel_id=1, source_target_pairs={{0,2},{2,0},{4,6},{6,4},{8,10},{10,8},{12,14},{14,12},{16,18},{18,... | collective-permute-start | bytes 1818632 | tf_op jit(solution)/shard_map/ppermute | solution.py:958
  49.0 3.5 %collective-permute-start.14 = (bf16[592,512]{1,0:T(8,128)(2,1)S(1)}, bf16[592,512]{1,0:T(8,128)(2,1)S(1)}, u32[]{:S(2)}, u32[]{:S(2)}) collective-permute-start(bf16[592,512]{1,0:T(8,128)(2,1)S(1)} %collective-permute-done.5.rest_3_), channel_id=1, source_target_pairs={{0,2},{2,0},{4,6},{6,4},{8,10},{10,8},{12,14},{14,12},{16,18},{18,... | collective-permute-start | bytes 1818632 | tf_op jit(solution)/shard_map/ppermute | solution.py:958
  50.3 2.7 %collective-permute-start.15 = (bf16[592,512]{1,0:T(8,128)(2,1)S(1)}, bf16[592,512]{1,0:T(8,128)(2,1)S(1)}, u32[]{:S(2)}, u32[]{:S(2)}) collective-permute-start(bf16[592,512]{1,0:T(8,128)(2,1)S(1)} %collective-permute-done.6.rest_4_), channel_id=1, source_target_pairs={{0,2},{2,0},{4,6},{6,4},{8,10},{10,8},{12,14},{14,12},{16,18},{18,... | collective-permute-start | bytes 1818632 | tf_op jit(solution)/shard_map/ppermute | solution.py:958
  50.3 2.8 %copy-start.8 = (bf16[592,512]{1,0:T(8,128)(2,1)}, bf16[592,512]{1,0:T(8,128)(2,1)S(1)}, u32[]{:S(2)}) copy-start(bf16[592,512]{1,0:T(8,128)(2,1)S(1)} %collective-permute-done.11.rest_5_) | copy-start | bytes 1818628
  50.3 9.8 %collective-permute-start.10 = (bf16[304,512]{1,0:T(8,128)(2,1)S(1)}, bf16[304,512]{1,0:T(8,128)(2,1)S(1)}, u32[]{:S(2)}, u32[]{:S(2)}) collective-permute-start(bf16[304,512]{1,0:T(8,128)(2,1)S(1)} %slice.88), channel_id=1, source_target_pairs={{0,4},{2,6},{8,0},{10,2},{16,8},{18,10},{24,16},{26,18},{28,24},{3... | collective-permute-start | bytes 933896 | tf_op jit(solution)/shard_map/ppermute | solution.py:953
  50.9 2.2 %copy-start.9 = (bf16[592,512]{1,0:T(8,128)(2,1)}, bf16[592,512]{1,0:T(8,128)(2,1)S(1)}, u32[]{:S(2)}) copy-start(bf16[592,512]{1,0:T(8,128)(2,1)S(1)} %collective-permute-done.12.rest_6_) | copy-start | bytes 1818628
  50.9 9.2 %collective-permute-start.9 = (bf16[288,512]{1,0:T(8,128)(2,1)S(1)}, bf16[288,512]{1,0:T(8,128)(2,1)S(1)}, u32[]{:S(2)}, u32[]{:S(2)}) collective-permute-start(bf16[288,512]{1,0:T(8,128)(2,1)S(1)} %slice.87), channel_id=1, source_target_pairs={{0,8},{2,10},{8,16},{10,18},{16,24},{18,26},{24,28},{26,30},{28,20... | collective-permute-start | bytes 884744 | tf_op jit(solution)/shard_map/ppermute | solution.py:953
  52.5 0.8 copy-start.10
  52.5 8.2 %collective-permute-start.16 = (bf16[592,512]{1,0:T(8,128)(2,1)S(1)}, bf16[592,512]{1,0:T(8,128)(2,1)S(1)}, u32[]{:S(2)}, u32[]{:S(2)}) collective-permute-start(bf16[592,512]{1,0:T(8,128)(2,1)S(1)} %collective-permute-done.7.rest_0_.rest_10_), channel_id=1, source_target_pairs={{0,2},{2,0},{4,6},{6,4},{8,10},{10,8},{12,14},{14,12},{16,18},{18,... | collective-permute-start | bytes 1818632 | tf_op jit(solution)/shard_map/ppermute | solution.py:958
  52.5 1.0 copy-start.11
  52.5 8.1 %collective-permute-start.17 = (bf16[592,512]{1,0:T(8,128)(2,1)S(1)}, bf16[592,512]{1,0:T(8,128)(2,1)S(1)}, u32[]{:S(2)}, u32[]{:S(2)}) collective-permute-start(bf16[592,512]{1,0:T(8,128)(2,1)S(1)} %collective-permute-done.8.rest_1_.rest_11_), channel_id=1, source_target_pairs={{0,2},{2,0},{4,6},{6,4},{8,10},{10,8},{12,14},{14,12},{16,18},{18,... | collective-permute-start | bytes 1818632 | tf_op jit(solution)/shard_map/ppermute | solution.py:958
  53.5 0.8 copy-start.12
  60.2 2.0 %collective-permute-start.19 = (bf16[304,512]{1,0:T(8,128)(2,1)S(1)}, bf16[304,512]{1,0:T(8,128)(2,1)S(1)}, u32[]{:S(2)}, u32[]{:S(2)}) collective-permute-start(bf16[304,512]{1,0:T(8,128)(2,1)S(1)} %collective-permute-done.10.rest_3_.rest_13_), channel_id=1, source_target_pairs={{0,2},{2,0},{4,6},{6,4},{8,10},{10,8},{12,14},{14,12},{16,18},{18,... | collective-permute-start | bytes 933896 | tf_op jit(solution)/shard_map/ppermute | solution.py:958
  60.2 2.0 %collective-permute-start.18 = (bf16[288,512]{1,0:T(8,128)(2,1)S(1)}, bf16[288,512]{1,0:T(8,128)(2,1)S(1)}, u32[]{:S(2)}, u32[]{:S(2)}) collective-permute-start(bf16[288,512]{1,0:T(8,128)(2,1)S(1)} %collective-permute-done.9.rest_2_.rest_12_), channel_id=1, source_target_pairs={{0,2},{2,0},{4,6},{6,4},{8,10},{10,8},{12,14},{14,12},{16,18},{18,... | collective-permute-start | bytes 884744 | tf_op jit(solution)/shard_map/ppermute | solution.py:958
  62.2 4.7 %copy-start.1 = (bf16[512,768]{1,0:T(8,128)(2,1)S(1)}, bf16[512,768]{1,0:T(8,128)(2,1)}, u32[]{:S(2)}) copy-start(bf16[512,768]{1,0:T(8,128)(2,1)} %cot_ref.6) | copy-start | bytes 2359300
  64.8 7.8 %collective-permute-start.20 = (bf16[256,384]{1,0:T(8,128)(2,1)S(1)}, bf16[256,384]{1,0:T(8,128)(2,1)S(1)}, u32[]{:S(2)}, u32[]{:S(2)}) collective-permute-start(bf16[256,384]{1,0:T(8,128)(2,1)S(1)} %get-tuple-element.161.own_ref.rest_2_), channel_id=1, source_target_pairs={{0,1},{1,0},{2,3},{3,2},{4,5},{5,4},{6,7},{7,6},{8,9},{9,8},{10,11... | collective-permute-start | bytes 589832 | tf_op jit(solution)/shard_map/ppermute | solution.py:1123
  66.4 10.5 %collective-permute-start.21 = (bf16[256,384]{1,0:T(8,128)(2,1)S(1)}, bf16[256,384]{1,0:T(8,128)(2,1)S(1)}, u32[]{:S(2)}, u32[]{:S(2)}) collective-permute-start(bf16[256,384]{1,0:T(8,128)(2,1)S(1)} %get-tuple-element.168.own_ref.rest_3_), channel_id=1, source_target_pairs={{0,1},{1,0},{2,3},{3,2},{4,5},{5,4},{6,7},{7,6},{8,9},{9,8},{10,11... | collective-permute-start | bytes 589832 | tf_op jit(solution)/shard_map/ppermute | solution.py:1123
  75.3 10.0 %collective-permute-start.26 = (bf16[256,768]{1,0:T(8,128)(2,1)S(1)}, bf16[256,768]{1,0:T(8,128)(2,1)S(1)}, u32[]{:S(2)}, u32[]{:S(2)}) collective-permute-start(bf16[256,768]{1,0:T(8,128)(2,1)S(1)} %get-tuple-element.181.back_ref), channel_id=1, source_target_pairs={{0,1},{1,0},{2,3},{3,2},{4,5},{5,4},{6,7},{7,6},{8,9},{9,8},{10,11... | collective-permute-start | bytes 1179656 | tf_op jit(solution)/shard_map/ppermute | solution.py:1131
  83.3 1.6 %collective-permute-start.22 = (bf16[48,3072]{1,0:T(8,128)(2,1)S(1)}, bf16[48,3072]{1,0:T(8,128)(2,1)S(1)}, u32[]{:S(2)}, u32[]{:S(2)}) collective-permute-start(bf16[48,3072]{1,0:T(8,128)(2,1)S(1)} %get-tuple-element.177), channel_id=1, source_target_pairs={{0,2},{2,0},{4,6},{6,4},{8,10},{10,8},{12,14},{14,12},{16,18},{18,... | collective-permute-start | bytes 884744 | tf_op jit(solution)/shard_map/ppermute | solution.py:978
  83.3 2.0 %collective-permute-start.24 = (bf16[48,3072]{1,0:T(8,128)(2,1)S(1)}, bf16[48,3072]{1,0:T(8,128)(2,1)S(1)}, u32[]{:S(2)}, u32[]{:S(2)}) collective-permute-start(bf16[48,3072]{1,0:T(8,128)(2,1)S(1)} %get-tuple-element.178), channel_id=1, source_target_pairs={{0,2},{2,0},{4,6},{6,4},{8,10},{10,8},{12,14},{14,12},{16,18},{18,... | collective-permute-start | bytes 884744 | tf_op jit(solution)/shard_map/ppermute | solution.py:978
  85.3 9.9 %collective-permute-start.27 = (bf16[6,48,3072]{2,1,0:T(8,128)(2,1)S(1)}, bf16[6,48,3072]{2,1,0:T(8,128)(2,1)S(1)}, u32[]{:S(2)}, u32[]{:S(2)}) collective-permute-start(bf16[6,48,3072]{2,1,0:T(8,128)(2,1)S(1)} %get-tuple-element.197), channel_id=1, source_target_pairs={{0,2},{2,0},{4,6},{6,4},{8,10},{10,8},{12,14},{14,12},{16,18},{18,... | collective-permute-start | bytes 5308424 | tf_op jit(solution)/shard_map/ppermute | solution.py:997
  85.6 9.3 %collective-permute-start.23 = (bf16[48,3072]{1,0:T(8,128)(2,1)S(1)}, bf16[48,3072]{1,0:T(8,128)(2,1)S(1)}, u32[]{:S(2)}, u32[]{:S(2)}) collective-permute-start(bf16[48,3072]{1,0:T(8,128)(2,1)S(1)} %get-tuple-element.266), channel_id=1, source_target_pairs={{0,4},{2,6},{8,0},{10,2},{16,8},{18,10},{24,16},{26,18},{28,24},{3... | collective-permute-start | bytes 884744 | tf_op jit(solution)/shard_map/ppermute | solution.py:1006
  86.1 9.1 %collective-permute-start.25 = (bf16[48,3072]{1,0:T(8,128)(2,1)S(1)}, bf16[48,3072]{1,0:T(8,128)(2,1)S(1)}, u32[]{:S(2)}, u32[]{:S(2)}) collective-permute-start(bf16[48,3072]{1,0:T(8,128)(2,1)S(1)} %get-tuple-element.265), channel_id=1, source_target_pairs={{0,8},{2,10},{8,16},{10,18},{16,24},{18,26},{24,28},{26,30},{28,20... | collective-permute-start | bytes 884744 | tf_op jit(solution)/shard_map/ppermute | solution.py:1006
  87.7 10.9 %collective-permute-start.32 = (bf16[256,768]{1,0:T(8,128)(2,1)S(1)}, bf16[256,768]{1,0:T(8,128)(2,1)S(1)}, u32[]{:S(2)}, u32[]{:S(2)}) collective-permute-start(bf16[256,768]{1,0:T(8,128)(2,1)S(1)} %get-tuple-element.209.back_ref), channel_id=1, source_target_pairs={{0,1},{1,0},{2,3},{3,2},{4,5},{5,4},{6,7},{7,6},{8,9},{9,8},{10,11... | collective-permute-start | bytes 1179656 | tf_op jit(solution)/shard_map/ppermute | solution.py:1131
  95.5 8.3 %collective-permute-start.28 = (bf16[48,3072]{1,0:T(8,128)(2,1)S(1)}, bf16[48,3072]{1,0:T(8,128)(2,1)S(1)}, u32[]{:S(2)}, u32[]{:S(2)}) collective-permute-start(bf16[48,3072]{1,0:T(8,128)(2,1)S(1)} %get-tuple-element.264), channel_id=1, source_target_pairs={{0,4},{2,6},{8,0},{10,2},{16,8},{18,10},{24,16},{26,18},{28,24},{3... | collective-permute-start | bytes 884744 | tf_op jit(solution)/shard_map/ppermute | solution.py:1006
  96.2 8.0 %collective-permute-start.29 = (bf16[48,3072]{1,0:T(8,128)(2,1)S(1)}, bf16[48,3072]{1,0:T(8,128)(2,1)S(1)}, u32[]{:S(2)}, u32[]{:S(2)}) collective-permute-start(bf16[48,3072]{1,0:T(8,128)(2,1)S(1)} %get-tuple-element.263), channel_id=1, source_target_pairs={{0,8},{2,10},{8,16},{10,18},{16,24},{18,26},{24,28},{26,30},{28,20... | collective-permute-start | bytes 884744 | tf_op jit(solution)/shard_map/ppermute | solution.py:1006
  101.2 6.7 %collective-permute-start.33 = (f32[64,128]{1,0:T(8,128)S(1)}, f32[64,128]{1,0:T(8,128)S(1)}, u32[]{:S(2)}, u32[]{:S(2)}) collective-permute-start(f32[64,128]{1,0:T(8,128)S(1)} %get-tuple-element.214.ga_ref), channel_id=1, source_target_pairs={{0,1},{1,0},{2,3},{3,2},{4,5},{5,4},{6,7},{7,6},{8,9},{9,8},{10,11... | collective-permute-start | bytes 98312 | tf_op jit(solution)/shard_map/ppermute | solution.py:1155
  102.7 8.1 %collective-permute-start.35 = (bf16[192,768]{1,0:T(8,128)(2,1)S(1)}, bf16[192,768]{1,0:T(8,128)(2,1)S(1)}, u32[]{:S(2)}, u32[]{:S(2)}) collective-permute-start(bf16[192,768]{1,0:T(8,128)(2,1)S(1)} %get-tuple-element.222), channel_id=1, source_target_pairs={{0,1},{1,0},{2,3},{3,2},{4,5},{5,4},{6,7},{7,6},{8,9},{9,8},{10,11... | collective-permute-start | bytes 884744 | tf_op jit(solution)/shard_map/ppermute | solution.py:1156
  104.4 7.1 %collective-permute-start.30 = (bf16[48,3072]{1,0:T(8,128)(2,1)S(1)}, bf16[48,3072]{1,0:T(8,128)(2,1)S(1)}, u32[]{:S(2)}, u32[]{:S(2)}) collective-permute-start(bf16[48,3072]{1,0:T(8,128)(2,1)S(1)} %get-tuple-element.262), channel_id=1, source_target_pairs={{0,4},{2,6},{8,0},{10,2},{16,8},{18,10},{24,16},{26,18},{28,24},{3... | collective-permute-start | bytes 884744 | tf_op jit(solution)/shard_map/ppermute | solution.py:1006
  105.9 6.7 %collective-permute-start.31 = (bf16[48,3072]{1,0:T(8,128)(2,1)S(1)}, bf16[48,3072]{1,0:T(8,128)(2,1)S(1)}, u32[]{:S(2)}, u32[]{:S(2)}) collective-permute-start(bf16[48,3072]{1,0:T(8,128)(2,1)S(1)} %get-tuple-element.261), channel_id=1, source_target_pairs={{0,8},{2,10},{8,16},{10,18},{16,24},{18,26},{24,28},{26,30},{28,20... | collective-permute-start | bytes 884744 | tf_op jit(solution)/shard_map/ppermute | solution.py:1006
  109.6 1.6 %collective-permute-start.34 = (bf16[272,512]{1,0:T(8,128)(2,1)S(1)}, bf16[272,512]{1,0:T(8,128)(2,1)S(1)}, u32[]{:S(2)}, u32[]{:S(2)}) collective-permute-start(bf16[272,512]{1,0:T(8,128)(2,1)S(1)} %get-tuple-element.221), channel_id=1, source_target_pairs={{0,2},{2,0},{4,6},{6,4},{8,10},{10,8},{12,14},{14,12},{16,18},{18,... | collective-permute-start | bytes 835592 | tf_op jit(solution)/shard_map/ppermute | solution.py:978
  112.7 9.1 %collective-permute-start.37 = (bf16[7,272,512]{2,1,0:T(8,128)(2,1)S(1)}, bf16[7,272,512]{2,1,0:T(8,128)(2,1)S(1)}, u32[]{:S(2)}, u32[]{:S(2)}) collective-permute-start(bf16[7,272,512]{2,1,0:T(8,128)(2,1)S(1)} %get-tuple-element.231), channel_id=1, source_target_pairs={{0,2},{2,0},{4,6},{6,4},{8,10},{10,8},{12,14},{14,12},{16,18},{18,... | collective-permute-start | bytes 5849096 | tf_op jit(solution)/shard_map/ppermute | solution.py:997
  112.8 9.1 %collective-permute-start.38 = (bf16[272,512]{1,0:T(8,128)(2,1)S(1)}, bf16[272,512]{1,0:T(8,128)(2,1)S(1)}, u32[]{:S(2)}, u32[]{:S(2)}) collective-permute-start(bf16[272,512]{1,0:T(8,128)(2,1)S(1)} %fusion.8), channel_id=1, source_target_pairs={{0,8},{2,10},{8,16},{10,18},{16,24},{18,26},{24,28},{26,30},{28,20... | collective-permute-start | bytes 835592 | tf_op jit(solution)/shard_map/ppermute | solution.py:1006
  113.5 12.4 %collective-permute-start.36 = (bf16[48,3072]{1,0:T(8,128)(2,1)S(1)}, bf16[48,3072]{1,0:T(8,128)(2,1)S(1)}, u32[]{:S(2)}, u32[]{:S(2)}) collective-permute-start(bf16[48,3072]{1,0:T(8,128)(2,1)S(1)} %fusion.3), channel_id=1, source_target_pairs={{0,4},{2,6},{8,0},{10,2},{16,8},{18,10},{24,16},{26,18},{28,24},{3... | collective-permute-start | bytes 884744 | tf_op jit(solution)/shard_map/ppermute | solution.py:1006
  115.0 14.1 %collective-permute-start.41 = (bf16[320,768]{1,0:T(8,128)(2,1)S(1)}, bf16[320,768]{1,0:T(8,128)(2,1)S(1)}, u32[]{:S(2)}, u32[]{:S(2)}) collective-permute-start(bf16[320,768]{1,0:T(8,128)(2,1)S(1)} %get-tuple-element.224), channel_id=1, source_target_pairs={{0,1},{1,0},{2,3},{3,2},{4,5},{5,4},{6,7},{7,6},{8,9},{9,8},{10,11... | collective-permute-start | bytes 1474568 | tf_op jit(solution)/shard_map/ppermute | solution.py:1172
  121.9 8.3 %collective-permute-start.40 = (bf16[272,512]{1,0:T(8,128)(2,1)S(1)}, bf16[272,512]{1,0:T(8,128)(2,1)S(1)}, u32[]{:S(2)}, u32[]{:S(2)}) collective-permute-start(bf16[272,512]{1,0:T(8,128)(2,1)S(1)} %fusion.14), channel_id=1, source_target_pairs={{0,4},{2,6},{8,0},{10,2},{16,8},{18,10},{24,16},{26,18},{28,24},{3... | collective-permute-start | bytes 835592 | tf_op jit(solution)/shard_map/ppermute | solution.py:1006
  123.7 8.0 %collective-permute-start.39 = (bf16[272,512]{1,0:T(8,128)(2,1)S(1)}, bf16[272,512]{1,0:T(8,128)(2,1)S(1)}, u32[]{:S(2)}, u32[]{:S(2)}) collective-permute-start(bf16[272,512]{1,0:T(8,128)(2,1)S(1)} %fusion.13), channel_id=1, source_target_pairs={{0,8},{2,10},{8,16},{10,18},{16,24},{18,26},{24,28},{26,30},{28,20... | collective-permute-start | bytes 835592 | tf_op jit(solution)/shard_map/ppermute | solution.py:1006
  124.2 13.4 %collective-permute-start.45 = (bf16[256,768]{1,0:T(8,128)(2,1)S(1)}, bf16[256,768]{1,0:T(8,128)(2,1)S(1)}, u32[]{:S(2)}, u32[]{:S(2)}) collective-permute-start(bf16[256,768]{1,0:T(8,128)(2,1)S(1)} %get-tuple-element.239.mine_ref), channel_id=1, source_target_pairs={{0,1},{1,0},{2,3},{3,2},{4,5},{5,4},{6,7},{7,6},{8,9},{9,8},{10,11... | collective-permute-start | bytes 1179656 | tf_op jit(solution)/shard_map/ppermute | solution.py:1178
  131.9 7.1 %collective-permute-start.43 = (bf16[272,512]{1,0:T(8,128)(2,1)S(1)}, bf16[272,512]{1,0:T(8,128)(2,1)S(1)}, u32[]{:S(2)}, u32[]{:S(2)}) collective-permute-start(bf16[272,512]{1,0:T(8,128)(2,1)S(1)} %get-tuple-element.260), channel_id=1, source_target_pairs={{0,8},{2,10},{8,16},{10,18},{16,24},{18,26},{24,28},{26,30},{28,20... | collective-permute-start | bytes 835592 | tf_op jit(solution)/shard_map/ppermute | solution.py:1006
  132.4 6.7 %collective-permute-start.44 = (bf16[272,512]{1,0:T(8,128)(2,1)S(1)}, bf16[272,512]{1,0:T(8,128)(2,1)S(1)}, u32[]{:S(2)}, u32[]{:S(2)}) collective-permute-start(bf16[272,512]{1,0:T(8,128)(2,1)S(1)} %get-tuple-element.259), channel_id=1, source_target_pairs={{0,4},{2,6},{8,0},{10,2},{16,8},{18,10},{24,16},{26,18},{28,24},{3... | collective-permute-start | bytes 835592 | tf_op jit(solution)/shard_map/ppermute | solution.py:1006
  134.0 10.9 %collective-permute-start.42 = (bf16[256,768]{1,0:T(8,128)(2,1)S(1)}, bf16[256,768]{1,0:T(8,128)(2,1)S(1)}, u32[]{:S(2)}, u32[]{:S(2)}) collective-permute-start(bf16[256,768]{1,0:T(8,128)(2,1)S(1)} %get-tuple-element.237.mine_ref), channel_id=1, source_target_pairs={{0,1},{1,0},{2,3},{3,2},{4,5},{5,4},{6,7},{7,6},{8,9},{9,8},{10,11... | collective-permute-start | bytes 1179656 | tf_op jit(solution)/shard_map/ppermute | solution.py:1181
  139.3 6.7 %collective-permute-start.46 = (bf16[272,512]{1,0:T(8,128)(2,1)S(1)}, bf16[272,512]{1,0:T(8,128)(2,1)S(1)}, u32[]{:S(2)}, u32[]{:S(2)}) collective-permute-start(bf16[272,512]{1,0:T(8,128)(2,1)S(1)} %get-tuple-element.258), channel_id=1, source_target_pairs={{0,8},{2,10},{8,16},{10,18},{16,24},{18,26},{24,28},{26,30},{28,20... | collective-permute-start | bytes 835592 | tf_op jit(solution)/shard_map/ppermute | solution.py:1006
  140.0 6.5 %collective-permute-start.47 = (bf16[272,512]{1,0:T(8,128)(2,1)S(1)}, bf16[272,512]{1,0:T(8,128)(2,1)S(1)}, u32[]{:S(2)}, u32[]{:S(2)}) collective-permute-start(bf16[272,512]{1,0:T(8,128)(2,1)S(1)} %get-tuple-element.257), channel_id=1, source_target_pairs={{0,4},{2,6},{8,0},{10,2},{16,8},{18,10},{24,16},{26,18},{28,24},{3... | collective-permute-start | bytes 835592 | tf_op jit(solution)/shard_map/ppermute | solution.py:1006

commit v11 on v10

--- a/solution.py
+++ b/solution.py
@@ -132,9 +132,14 @@
     def kernel(second_ref, *rest):
         out, low, wo_out, gains = rest[count : count + 4]
         held, sem = rest[count + 4 : -1], rest[-1]
-        fetch(rest[:count], held, sem)
+        copies = [pltpu.make_async_copy(rest[n], held[n], sem.at[n]) for n in range(count)]
+        for copy in copies:
+            copy.start()
         s_ref, wv_ref, ga_ref, gf_ref, up_ref, down_ref, own_ref = held
+        copies[0].wait()
         out[: plan.scores, :] = s_ref[...].reshape(plan.scores, length).astype(BF)
+        for copy in copies[1:]:
+            copy.wait()
         for n, (kind, column) in enumerate(plan.blocks):
             at = slice(plan.scores + n * krows, plan.scores + (n + 1) * krows)
             if kind == "ffn":
@@ -190,14 +195,6 @@
             out[plan.head :, :] = refs[count + n][...]
 
     return run(kernel, "join_units", (), (*uppers, *lowers), [((plan.deep, plan.length), BF)] * count)
-
-
-def fetch(refs, held, sem):
-    copies = [pltpu.make_async_copy(ref, to, sem.at[n]) for n, (ref, to) in enumerate(zip(refs, held))]
-    for copy in copies:
-        copy.start()
-    for copy in copies:
-        copy.wait()
 
 
 def pick(units, shares, where_ref, parts, target, sem):

time: 148 us -> 148 us (level)
  no operation moved by 1% of the time
where the time goes in v11:
time: 148 us
  waiting for transfers between devices  61 us (41%)
  starting transfers between devices  43 us (29%)
  Pallas kernels  37.6 us (25%)
  other arithmetic  3.42 us (2%)
    pallas_call x23, Pallas kernels, run(): pl.pallas_call(kernel, out_shape=tuple(results), in_specs=specs, out_spec...  37.6 us
    ppermute x3, waiting for transfers between devices, hop(): lax.ppermute(up, 'dp', ring.up)  24.4 us
    ppermute x14, starting transfers between devices, hop(): lax.ppermute(value, 'dp', self.ring.up if way == 'up' else self.ring.down)  14.7 us
    ppermute x14, waiting for transfers between devices, hop(): lax.ppermute(value, 'dp', self.ring.up if way == 'up' else self.ring.down)  13.2 us
    ppermute x2, waiting for transfers between devices, shards(): lowers = [lax.ppermute(lower, 'dp', way) for way in ways]  8.23 us
    ppermute x3, starting transfers between devices, hop(): lax.ppermute(up, 'dp', ring.up)  4.83 us
    ppermute x1, waiting for transfers between devices, shards(): two_other = lax.ppermute(ffn_two, 'mp', flip)  3.21 us
    ppermute x2, starting transfers between devices, shards(): uppers = [lax.ppermute(upper, 'dp', way) for way in ways]  3.08 us
  transfers between devices with their start and end apart: 48, of which 31 were waited for; matrix products, arithmetic and copies ran while one was open for 2% of the time, Pallas kernels for 22%

profile of v11, /device:TPU:0, one launch (start us, length us, event | category | flops | bytes accessed | tf_op | source)
XLA Modules:
  0.0 147.6 jit_solution(13287331837264252055)
XLA Ops:
  0.6 1.4 pack_unit.1
  2.0 3.1 %collective-permute-start = (bf16[480,512]{1,0:T(8,128)(2,1)S(1)}, bf16[480,512]{1,0:T(8,128)(2,1)S(1)}, u32[]{:S(2)}, u32[]{:S(2)}) collective-permute-start(bf16[480,512]{1,0:T(8,128)(2,1)S(1)} %get-tuple-element.132.refs_0_), channel_id=1, source_target_pairs={{0,8},{2,10},{8,16},{10,18},{16,24},{18,26},{24,28},{26,30},{28,20... | collective-permute-start | bytes 1474568 | tf_op jit(solution)/shard_map/ppermute | solution.py:1060
  5.1 0.7 broadcast_add_fusion.3
  6.0 2.0 %collective-permute-start.2 = (bf16[48,384]{1,0:T(8,128)(2,1)S(1)}, bf16[48,384]{1,0:T(8,128)(2,1)S(1)}, u32[]{:S(2)}, u32[]{:S(2)}) collective-permute-start(bf16[48,384]{1,0:T(8,128)(2,1)S(1)} %get-tuple-element.135), channel_id=1, source_target_pairs={{0,1},{1,0},{2,3},{3,2},{4,5},{5,4},{6,7},{7,6},{8,9},{9,8},{10,11... | collective-permute-start | bytes 110600 | tf_op jit(solution)/shard_map/ppermute | solution.py:1061
  7.9 2.0 %collective-permute-done.2.other_ref = bf16[48,384]{1,0:T(8,128)(2,1)S(1)} collective-permute-done((bf16[48,384]{1,0:T(8,128)(2,1)S(1)}, bf16[48,384]{1,0:T(8,128)(2,1)S(1)}, u32[]{:S(2)}, u32[]{:S(2)}) %collective-permute-start.2) | collective-permute-done | bytes 36896 | tf_op jit(solution)/shard_map/ppermute | solution.py:1061
  9.9 2.1 %collective-permute-start.3 = (bf16[112,512]{1,0:T(8,128)(2,1)S(1)}, bf16[112,512]{1,0:T(8,128)(2,1)S(1)}, u32[]{:S(2)}, u32[]{:S(2)}) collective-permute-start(bf16[112,512]{1,0:T(8,128)(2,1)S(1)} %fill_low.1.refs_1_), channel_id=1, source_target_pairs={{0,8},{2,10},{8,16},{10,18},{16,24},{18,26},{24,28},{26,30},{28,20... | collective-permute-start | bytes 344072 | tf_op jit(solution)/shard_map/ppermute | solution.py:1063
  12.0 6.7 %collective-permute-done.3.refs_2_ = bf16[112,512]{1,0:T(8,128)(2,1)S(1)} collective-permute-done((bf16[112,512]{1,0:T(8,128)(2,1)S(1)}, bf16[112,512]{1,0:T(8,128)(2,1)S(1)}, u32[]{:S(2)}, u32[]{:S(2)}) %collective-permute-start.3) | collective-permute-done | bytes 114720 | tf_op jit(solution)/shard_map/ppermute | solution.py:1063
  18.7 1.5 %collective-permute-done.4.refs_3_ = bf16[112,512]{1,0:T(8,128)(2,1)S(1)} collective-permute-done((bf16[112,512]{1,0:T(8,128)(2,1)S(1)}, bf16[112,512]{1,0:T(8,128)(2,1)S(1)}, u32[]{:S(2)}, u32[]{:S(2)}) %collective-permute-start.4) | collective-permute-done | bytes 114720 | tf_op jit(solution)/shard_map/ppermute | solution.py:1063
  20.4 1.6 %collective-permute-start.5 = (bf16[592,512]{1,0:T(8,128)(2,1)S(1)}, bf16[592,512]{1,0:T(8,128)(2,1)S(1)}, u32[]{:S(2)}, u32[]{:S(2)}) collective-permute-start(bf16[592,512]{1,0:T(8,128)(2,1)S(1)} %get-tuple-element.140.rest_1_), channel_id=1, source_target_pairs={{0,8},{2,10},{8,16},{10,18},{16,24},{18,26},{24,28},{26,30},{28,20... | collective-permute-start | bytes 1818632 | tf_op jit(solution)/shard_map/ppermute | solution.py:950
  22.4 12.2 %collective-permute-done.5.rest_3_ = bf16[592,512]{1,0:T(8,128)(2,1)S(1)} collective-permute-done((bf16[592,512]{1,0:T(8,128)(2,1)S(1)}, bf16[592,512]{1,0:T(8,128)(2,1)S(1)}, u32[]{:S(2)}, u32[]{:S(2)}) %collective-permute-start.5) | collective-permute-done | bytes 606240 | tf_op jit(solution)/shard_map/ppermute | solution.py:950
  34.6 1.3 collective-permute-done.6.rest_4_
  35.9 1.6 %collective-permute-start.7 = (bf16[592,512]{1,0:T(8,128)(2,1)S(1)}, bf16[592,512]{1,0:T(8,128)(2,1)S(1)}, u32[]{:S(2)}, u32[]{:S(2)}) collective-permute-start(bf16[592,512]{1,0:T(8,128)(2,1)S(1)} %collective-permute-done.5.rest_3_), channel_id=1, source_target_pairs={{0,8},{2,10},{8,16},{10,18},{16,24},{18,26},{24,28},{26,30},{28,20... | collective-permute-start | bytes 1818632 | tf_op jit(solution)/shard_map/ppermute | solution.py:950
  38.7 10.3 %collective-permute-done.7.rest_0_.rest_10_ = bf16[592,512]{1,0:T(8,128)(2,1)S(1)} collective-permute-done((bf16[592,512]{1,0:T(8,128)(2,1)S(1)}, bf16[592,512]{1,0:T(8,128)(2,1)S(1)}, u32[]{:S(2)}, u32[]{:S(2)}) %collective-permute-start.7) | collective-permute-done | bytes 606240 | tf_op jit(solution)/shard_map/ppermute | solution.py:950
  49.0 1.3 collective-permute-done.8.rest_1_.rest_11_
  50.9 1.6 %collective-permute-start.9 = (bf16[288,512]{1,0:T(8,128)(2,1)S(1)}, bf16[288,512]{1,0:T(8,128)(2,1)S(1)}, u32[]{:S(2)}, u32[]{:S(2)}) collective-permute-start(bf16[288,512]{1,0:T(8,128)(2,1)S(1)} %slice.87), channel_id=1, source_target_pairs={{0,8},{2,10},{8,16},{10,18},{16,24},{18,26},{24,28},{26,30},{28,20... | collective-permute-start | bytes 884744 | tf_op jit(solution)/shard_map/ppermute | solution.py:950
  53.5 0.8 copy-done.12
  54.4 3.8 %mixer_first.1 = (bf16[6,512,512]{2,1,0:T(8,128)(2,1)S(1)}, bf16[768,384]{1,0:T(8,128)(2,1)S(1)}, bf16[16,16,128]{2,1,0:T(8,128)(2,1)S(1)}, f32[512,768]{1,0:T(8,128)S(1)}, f32[512,512]{1,0:T(8,128)S(1)}) custom-call(s32[16]{0:T(128)S(1)} %pad_add_fusion.where_ref, bf16[512,768]{1,0:T(8,128)(2,1)S(1)} %copy-done, s32[1,512]{1,0:T(1,128)S(1)} %copy-done.5, ...), custom_call_target="tpu_custom_call" | custom-call | flops 1 | bytes 1 | tf_op jit(solution)/shard_map/mixer_first/pallas_call | solution.py:36
  58.2 1.9 %collective-permute-done.9.rest_2_.rest_12_ = bf16[288,512]{1,0:T(8,128)(2,1)S(1)} collective-permute-done((bf16[288,512]{1,0:T(8,128)(2,1)S(1)}, bf16[288,512]{1,0:T(8,128)(2,1)S(1)}, u32[]{:S(2)}, u32[]{:S(2)}) %collective-permute-start.9) | collective-permute-done | bytes 294944 | tf_op jit(solution)/shard_map/ppermute | solution.py:950
  60.6 0.9 mixer_next.1
  62.2 2.6 %mixer_forward.1 = (bf16[6,512,512]{2,1,0:T(8,128)(2,1)S(1)}, bf16[768,384]{1,0:T(8,128)(2,1)S(1)}, bf16[16,16,128]{2,1,0:T(8,128)(2,1)S(1)}, bf16[512,768]{1,0:...) custom-call(s32[16]{0:T(128)S(1)} %pad_add_fusion.where_ref, ...), custom_call_target="tpu_custom_call", output_to_operand_aliasing={{0}: (1, {}), {1}: (2, {}), {2}: (3, {})} | custom-call | flops 1 | bytes 1 | tf_op jit(solution)/shard_map/mixer_forward/pallas_call | solution.py:36
  64.8 1.6 %collective-permute-start.20 = (bf16[256,384]{1,0:T(8,128)(2,1)S(1)}, bf16[256,384]{1,0:T(8,128)(2,1)S(1)}, u32[]{:S(2)}, u32[]{:S(2)}) collective-permute-start(bf16[256,384]{1,0:T(8,128)(2,1)S(1)} %get-tuple-element.161.own_ref.rest_2_), channel_id=1, source_target_pairs={{0,1},{1,0},{2,3},{3,2},{4,5},{5,4},{6,7},{7,6},{8,9},{9,8},{10,11... | collective-permute-start | bytes 589832 | tf_op jit(solution)/shard_map/ppermute | solution.py:1120
  66.9 5.0 %second_weights.1 = (bf16[6,768,512]{2,1,0:T(8,128)(2,1)S(1)}, bf16[768,768]{1,0:T(8,128)(2,1)S(1)}, f32[512,1536]{1,0:T(8,128)S(1)}, f32[512,768]{1,0:T(8,128)S...) custom-call(s32[16]{0:T(128)S(1)} %pad_add_fusion.where_ref, s32[1]{0:T(128)} %bitcast.second_ref, ...), custom_call_target="tpu_custom_call" | custom-call | flops 1 | bytes 1 | tf_op jit(solution)/shard_map/second_weights/pallas_call | solution.py:36
  71.9 0.7 collective-permute-done.20.other_ref
  72.6 2.7 %ffn_main.2 = (bf16[256,768]{1,0:T(8,128)(2,1)S(1)}, f32[256,768]{1,0:T(8,128)S(1)}, bf16[512,768]{1,0:T(8,128)(2,1)S(1)}, bf16[512,1536]{1,0:T(8,128)(2,1)S(1)}, bf16[512,1536]{1,0:T(8,128)(2,1)S(1)}) custom-call(s32[1]{0:T(128)} %bitcast.second_ref, bf16[512,768]{1,0:T(8,128)(2,1)S(1)} %copy-done, bf16[256,384]{1,0:T(8,128)(2,1)S(1)} %get-tuple-element.161.own_ref.rest_2_, ...), custom_call_target="tpu_custom_call" | custom-call | flops 1 | bytes 1 | tf_op jit(solution)/shard_map/ffn_main/pallas_call | solution.py:36
  75.3 1.6 %collective-permute-start.26 = (bf16[256,768]{1,0:T(8,128)(2,1)S(1)}, bf16[256,768]{1,0:T(8,128)(2,1)S(1)}, u32[]{:S(2)}, u32[]{:S(2)}) collective-permute-start(bf16[256,768]{1,0:T(8,128)(2,1)S(1)} %get-tuple-element.181.back_ref), channel_id=1, source_target_pairs={{0,1},{1,0},{2,3},{3,2},{4,5},{5,4},{6,7},{7,6},{8,9},{9,8},{10,11... | collective-permute-start | bytes 1179656 | tf_op jit(solution)/shard_map/ppermute | solution.py:1128
  76.9 2.7 %ffn_main.3 = (bf16[256,768]{1,0:T(8,128)(2,1)S(1)}, f32[256,768]{1,0:T(8,128)S(1)}, bf16[512,768]{1,0:T(8,128)(2,1)S(1)}, bf16[512,1536]{1,0:T(8,128)(2,1)S(1)}, bf16[512,1536]{1,0:T(8,128)(2,1)S(1)}) custom-call(s32[1]{0:T(128)} %bitcast.second_ref, bf16[512,768]{1,0:T(8,128)(2,1)S(1)} %copy-done, ...), custom_call_target="tpu_custom_call", output_to_operand_aliasing={{2}: (8, {}), {3}: (9, {}), {4}: (10, {})} | custom-call | flops 1 | bytes 1 | tf_op jit(solution)/shard_map/ffn_main/pallas_call | solution.py:36
  79.6 3.6 %ffn_grads.1 = (bf16[8,48,3072]{2,1,0:T(8,128)(2,1)S(1)}, bf16[48,3072]{1,0:T(8,128)(2,1)S(1)}, bf16[48,3072]{1,0:T(8,128)(2,1)S(1)}, bf16[6,48,3072]{2,1,0:T(8,128)(2,1)S(1)}) custom-call(s32[16]{0:T(128)S(1)} %pad_add_fusion.1.where_ref, bf16[512,768]{1,0:T(8,128)(2,1)S(1)} %copy-done.1, bf16[512,768]{1,0:T(8,128)(2,1)S(1)} %get-tuple-element.173.n2_ref, ...), custom_call_target="tpu_custom_call" | custom-call | flops 1 | bytes 1 | tf_op jit(solution)/shard_map/ffn_grads/pallas_call | solution.py:36
  83.8 1.1 collective-permute-done.22
  86.1 1.6 %collective-permute-start.25 = (bf16[48,3072]{1,0:T(8,128)(2,1)S(1)}, bf16[48,3072]{1,0:T(8,128)(2,1)S(1)}, u32[]{:S(2)}, u32[]{:S(2)}) collective-permute-start(bf16[48,3072]{1,0:T(8,128)(2,1)S(1)} %get-tuple-element.265), channel_id=1, source_target_pairs={{0,8},{2,10},{8,16},{10,18},{16,24},{18,26},{24,28},{26,30},{28,20... | collective-permute-start | bytes 884744 | tf_op jit(solution)/shard_map/ppermute | solution.py:1003
  87.7 1.3 collective-permute-start.32
  89.0 1.1 resid_back.2
  90.2 0.7 value_first.1.first_ref
  90.9 1.3 mixer_grads.2
  92.2 1.7 %ffn_out.1 = (bf16[192,768]{1,0:T(8,128)(2,1)S(1)}, bf16[320,768]{1,0:T(8,128)(2,1)S(1)}) custom-call(bf16[512,1536]{1,0:T(8,128)(2,1)S(1)} %get-tuple-element.186.act_ref, bf16[6,768,512]{2,1,0:T(8,128)(2,1)S(1)} %get-tuple-element.165.w_ref), custom_call_target="tpu_custom_call" | custom-call | flops 1 | bytes 1 | tf_op jit(solution)/shard_map/ffn_out/pallas_call | solution.py:36
  93.9 1.0 collective-permute-done.23
  95.5 0.7 collective-permute-start.28
  96.2 1.3 collective-permute-start.29
  97.5 1.0 collective-permute-done.32.other_ref
  98.6 1.1 resid_back.3
  99.7 1.4 value_back.1
  101.1 1.5 %collective-permute-start.33 = (f32[64,128]{1,0:T(8,128)S(1)}, f32[64,128]{1,0:T(8,128)S(1)}, u32[]{:S(2)}, u32[]{:S(2)}) collective-permute-start(f32[64,128]{1,0:T(8,128)S(1)} %get-tuple-element.214.ga_ref), channel_id=1, source_target_pairs={{0,1},{1,0},{2,3},{3,2},{4,5},{5,4},{6,7},{7,6},{8,9},{9,8},{10,11... | collective-permute-start | bytes 98312 | tf_op jit(solution)/shard_map/ppermute | solution.py:1152
  104.4 1.5 %collective-permute-start.30 = (bf16[48,3072]{1,0:T(8,128)(2,1)S(1)}, bf16[48,3072]{1,0:T(8,128)(2,1)S(1)}, u32[]{:S(2)}, u32[]{:S(2)}) collective-permute-start(bf16[48,3072]{1,0:T(8,128)(2,1)S(1)} %get-tuple-element.262), channel_id=1, source_target_pairs={{0,4},{2,6},{8,0},{10,2},{16,8},{18,10},{24,16},{26,18},{28,24},{3... | collective-permute-start | bytes 884744 | tf_op jit(solution)/shard_map/ppermute | solution.py:1003
  106.4 1.4 mixer_grads.3
  107.8 1.7 %weight_grads.1 = (bf16[8,272,512]{2,1,0:T(8,128)(2,1)S(1)}, bf16[272,512]{1,0:T(8,128)(2,1)S(1)}, bf16[7,272,512]{2,1,0:T(8,128)(2,1)S(1)}) custom-call(s32[16]{0:T(128)S(1)} %pad_add_fusion.1.where_ref, bf16[512,768]{1,0:T(8,128)(2,1)S(1)} %get-tuple-element.202.n1_ref, ...), custom_call_target="tpu_custom_call", output_to_operand_aliasing={{0}: (10, {}), {1}: (11, {}), {2}: (12, {})} | custom-call | flops 1 | bytes 1 | tf_op jit(solution)/shard_map/weight_grads/pallas_call | solution.py:36
  109.6 1.1 collective-permute-done.35
  111.5 1.2 collective-permute-done.31.up_ref
  113.5 1.5 %collective-permute-start.36 = (bf16[48,3072]{1,0:T(8,128)(2,1)S(1)}, bf16[48,3072]{1,0:T(8,128)(2,1)S(1)}, u32[]{:S(2)}, u32[]{:S(2)}) collective-permute-start(bf16[48,3072]{1,0:T(8,128)(2,1)S(1)} %fusion.3), channel_id=1, source_target_pairs={{0,4},{2,6},{8,0},{10,2},{16,8},{18,10},{24,16},{26,18},{28,24},{3... | collective-permute-start | bytes 884744 | tf_op jit(solution)/shard_map/ppermute | solution.py:1003
  115.0 1.8 %collective-permute-start.41 = (bf16[320,768]{1,0:T(8,128)(2,1)S(1)}, bf16[320,768]{1,0:T(8,128)(2,1)S(1)}, u32[]{:S(2)}, u32[]{:S(2)}) collective-permute-start(bf16[320,768]{1,0:T(8,128)(2,1)S(1)} %get-tuple-element.224), channel_id=1, source_target_pairs={{0,1},{1,0},{2,3},{3,2},{4,5},{5,4},{6,7},{7,6},{8,9},{9,8},{10,11... | collective-permute-start | bytes 1474568 | tf_op jit(solution)/shard_map/ppermute | solution.py:1169
  116.8 5.1 %collective-permute-done.38 = bf16[272,512]{1,0:T(8,128)(2,1)S(1)} collective-permute-done((bf16[272,512]{1,0:T(8,128)(2,1)S(1)}, bf16[272,512]{1,0:T(8,128)(2,1)S(1)}, u32[]{:S(2)}, u32[]{:S(2)}) %collective-permute-start.38) | collective-permute-done | bytes 278560 | tf_op jit(solution)/shard_map/ppermute | solution.py:1003
  121.9 1.6 %collective-permute-start.40 = (bf16[272,512]{1,0:T(8,128)(2,1)S(1)}, bf16[272,512]{1,0:T(8,128)(2,1)S(1)}, u32[]{:S(2)}, u32[]{:S(2)}) collective-permute-start(bf16[272,512]{1,0:T(8,128)(2,1)S(1)} %fusion.14), channel_id=1, source_target_pairs={{0,4},{2,6},{8,0},{10,2},{16,8},{18,10},{24,16},{26,18},{28,24},{3... | collective-permute-start | bytes 835592 | tf_op jit(solution)/shard_map/ppermute | solution.py:1003
  124.1 1.8 %collective-permute-start.45 = (bf16[256,768]{1,0:T(8,128)(2,1)S(1)}, bf16[256,768]{1,0:T(8,128)(2,1)S(1)}, u32[]{:S(2)}, u32[]{:S(2)}) collective-permute-start(bf16[256,768]{1,0:T(8,128)(2,1)S(1)} %get-tuple-element.239.mine_ref), channel_id=1, source_target_pairs={{0,1},{1,0},{2,3},{3,2},{4,5},{5,4},{6,7},{7,6},{8,9},{9,8},{10,11... | collective-permute-start | bytes 1179656 | tf_op jit(solution)/shard_map/ppermute | solution.py:1175
  125.9 3.2 %collective-permute-done.41 = bf16[320,768]{1,0:T(8,128)(2,1)S(1)} collective-permute-done((bf16[320,768]{1,0:T(8,128)(2,1)S(1)}, bf16[320,768]{1,0:T(8,128)(2,1)S(1)}, u32[]{:S(2)}, u32[]{:S(2)}) %collective-permute-start.41) | collective-permute-done | bytes 491552 | tf_op jit(solution)/shard_map/ppermute | solution.py:1169
  129.1 1.1 collective-permute-done.40
  130.2 1.5 collective-permute-done.39
  132.4 1.6 %collective-permute-start.44 = (bf16[272,512]{1,0:T(8,128)(2,1)S(1)}, bf16[272,512]{1,0:T(8,128)(2,1)S(1)}, u32[]{:S(2)}, u32[]{:S(2)}) collective-permute-start(bf16[272,512]{1,0:T(8,128)(2,1)S(1)} %get-tuple-element.259), channel_id=1, source_target_pairs={{0,4},{2,6},{8,0},{10,2},{16,8},{18,10},{24,16},{26,18},{28,24},{3... | collective-permute-start | bytes 835592 | tf_op jit(solution)/shard_map/ppermute | solution.py:1003
  134.0 1.8 %collective-permute-start.42 = (bf16[256,768]{1,0:T(8,128)(2,1)S(1)}, bf16[256,768]{1,0:T(8,128)(2,1)S(1)}, u32[]{:S(2)}, u32[]{:S(2)}) collective-permute-start(bf16[256,768]{1,0:T(8,128)(2,1)S(1)} %get-tuple-element.237.mine_ref), channel_id=1, source_target_pairs={{0,1},{1,0},{2,3},{3,2},{4,5},{5,4},{6,7},{7,6},{8,9},{9,8},{10,11... | collective-permute-start | bytes 1179656 | tf_op jit(solution)/shard_map/ppermute | solution.py:1178
  135.8 1.8 %collective-permute-done.45.other_ref = bf16[256,768]{1,0:T(8,128)(2,1)S(1)} collective-permute-done((bf16[256,768]{1,0:T(8,128)(2,1)S(1)}, bf16[256,768]{1,0:T(8,128)(2,1)S(1)}, u32[]{:S(2)}, u32[]{:S(2)}) %collective-permute-start.45) | collective-permute-done | bytes 393248 | tf_op jit(solution)/shard_map/ppermute | solution.py:1175
  137.5 1.4 collective-permute-done.43
  140.0 1.4 collective-permute-start.47
  141.4 0.9 ffn_result.1
  142.3 1.2 fusion
  143.5 1.1 token_grads.2.rest_0_
  144.9 1.2 token_grads.3
  146.5 0.9 mixer_result.1
  (100 shorter events, 14.4 us)
Async XLA Ops:
  2.0 18.2 %collective-permute-start = (bf16[480,512]{1,0:T(8,128)(2,1)S(1)}, bf16[480,512]{1,0:T(8,128)(2,1)S(1)}, u32[]{:S(2)}, u32[]{:S(2)}) collective-permute-start(bf16[480,512]{1,0:T(8,128)(2,1)S(1)} %get-tuple-element.132.refs_0_), channel_id=1, source_target_pairs={{0,8},{2,10},{8,16},{10,18},{16,24},{18,26},{24,28},{26,30},{28,20... | collective-permute-start | bytes 1474568 | tf_op jit(solution)/shard_map/ppermute | solution.py:1060
  5.1 15.1 %collective-permute-start.1 = (bf16[480,512]{1,0:T(8,128)(2,1)S(1)}, bf16[480,512]{1,0:T(8,128)(2,1)S(1)}, u32[]{:S(2)}, u32[]{:S(2)}) collective-permute-start(bf16[480,512]{1,0:T(8,128)(2,1)S(1)} %get-tuple-element.132.refs_0_), channel_id=1, source_target_pairs={{0,4},{2,6},{8,0},{10,2},{16,8},{18,10},{24,16},{26,18},{28,24},{3... | collective-permute-start | bytes 1474568 | tf_op jit(solution)/shard_map/ppermute | solution.py:1060
  6.0 4.0 %collective-permute-start.2 = (bf16[48,384]{1,0:T(8,128)(2,1)S(1)}, bf16[48,384]{1,0:T(8,128)(2,1)S(1)}, u32[]{:S(2)}, u32[]{:S(2)}) collective-permute-start(bf16[48,384]{1,0:T(8,128)(2,1)S(1)} %get-tuple-element.135), channel_id=1, source_target_pairs={{0,1},{1,0},{2,3},{3,2},{4,5},{5,4},{6,7},{7,6},{8,9},{9,8},{10,11... | collective-permute-start | bytes 110600 | tf_op jit(solution)/shard_map/ppermute | solution.py:1061
  9.9 44.4 %copy-start = (bf16[512,768]{1,0:T(8,128)(2,1)S(1)}, bf16[512,768]{1,0:T(8,128)(2,1)}, u32[]{:S(2)}) copy-start(bf16[512,768]{1,0:T(8,128)(2,1)} %tok_ref.11) | copy-start | bytes 2359300
  9.9 44.4 %copy-start.5 = (s32[1,512]{1,0:T(1,128)S(1)}, s32[1,512]{1,0:T(1,128)}, u32[]{:S(2)}) copy-start(s32[1,512]{1,0:T(1,128)} %seg_ref.1) | copy-start | bytes 6148
  9.9 8.8 %collective-permute-start.3 = (bf16[112,512]{1,0:T(8,128)(2,1)S(1)}, bf16[112,512]{1,0:T(8,128)(2,1)S(1)}, u32[]{:S(2)}, u32[]{:S(2)}) collective-permute-start(bf16[112,512]{1,0:T(8,128)(2,1)S(1)} %fill_low.1.refs_1_), channel_id=1, source_target_pairs={{0,8},{2,10},{8,16},{10,18},{16,24},{18,26},{24,28},{26,30},{28,20... | collective-permute-start | bytes 344072 | tf_op jit(solution)/shard_map/ppermute | solution.py:1063
  12.0 8.2 %collective-permute-start.4 = (bf16[112,512]{1,0:T(8,128)(2,1)S(1)}, bf16[112,512]{1,0:T(8,128)(2,1)S(1)}, u32[]{:S(2)}, u32[]{:S(2)}) collective-permute-start(bf16[112,512]{1,0:T(8,128)(2,1)S(1)} %fill_low.1.refs_1_), channel_id=1, source_target_pairs={{0,4},{2,6},{8,0},{10,2},{16,8},{18,10},{24,16},{26,18},{28,24},{3... | collective-permute-start | bytes 344072 | tf_op jit(solution)/shard_map/ppermute | solution.py:1063
  20.3 32.7 %copy-start.3 = (bf16[592,512]{1,0:T(8,128)(2,1)}, bf16[592,512]{1,0:T(8,128)(2,1)S(1)}, u32[]{:S(2)}) copy-start(bf16[592,512]{1,0:T(8,128)(2,1)S(1)} %get-tuple-element.140.rest_1_) | copy-start | bytes 1818628
  20.3 32.7 %copy-start.4 = (bf16[592,512]{1,0:T(8,128)(2,1)}, bf16[592,512]{1,0:T(8,128)(2,1)S(1)}, u32[]{:S(2)}) copy-start(bf16[592,512]{1,0:T(8,128)(2,1)S(1)} %get-tuple-element.141.rest_2_) | copy-start | bytes 1818628
  20.4 14.3 %collective-permute-start.5 = (bf16[592,512]{1,0:T(8,128)(2,1)S(1)}, bf16[592,512]{1,0:T(8,128)(2,1)S(1)}, u32[]{:S(2)}, u32[]{:S(2)}) collective-permute-start(bf16[592,512]{1,0:T(8,128)(2,1)S(1)} %get-tuple-element.140.rest_1_), channel_id=1, source_target_pairs={{0,8},{2,10},{8,16},{10,18},{16,24},{18,26},{24,28},{26,30},{28,20... | collective-permute-start | bytes 1818632 | tf_op jit(solution)/shard_map/ppermute | solution.py:950
  22.0 13.9 %collective-permute-start.6 = (bf16[592,512]{1,0:T(8,128)(2,1)S(1)}, bf16[592,512]{1,0:T(8,128)(2,1)S(1)}, u32[]{:S(2)}, u32[]{:S(2)}) collective-permute-start(bf16[592,512]{1,0:T(8,128)(2,1)S(1)} %get-tuple-element.141.rest_2_), channel_id=1, source_target_pairs={{0,4},{2,6},{8,0},{10,2},{16,8},{18,10},{24,16},{26,18},{28,24},{3... | collective-permute-start | bytes 1818632 | tf_op jit(solution)/shard_map/ppermute | solution.py:950
  34.6 18.4 %copy-start.6 = (bf16[592,512]{1,0:T(8,128)(2,1)}, bf16[592,512]{1,0:T(8,128)(2,1)S(1)}, u32[]{:S(2)}) copy-start(bf16[592,512]{1,0:T(8,128)(2,1)S(1)} %collective-permute-done.5.rest_3_) | copy-start | bytes 1818628
  35.9 17.1 %copy-start.7 = (bf16[592,512]{1,0:T(8,128)(2,1)}, bf16[592,512]{1,0:T(8,128)(2,1)S(1)}, u32[]{:S(2)}) copy-start(bf16[592,512]{1,0:T(8,128)(2,1)S(1)} %collective-permute-done.6.rest_4_) | copy-start | bytes 1818628
  35.9 13.0 %collective-permute-start.7 = (bf16[592,512]{1,0:T(8,128)(2,1)S(1)}, bf16[592,512]{1,0:T(8,128)(2,1)S(1)}, u32[]{:S(2)}, u32[]{:S(2)}) collective-permute-start(bf16[592,512]{1,0:T(8,128)(2,1)S(1)} %collective-permute-done.5.rest_3_), channel_id=1, source_target_pairs={{0,8},{2,10},{8,16},{10,18},{16,24},{18,26},{24,28},{26,30},{28,20... | collective-permute-start | bytes 1818632 | tf_op jit(solution)/shard_map/ppermute | solution.py:950
  37.5 12.7 %collective-permute-start.8 = (bf16[592,512]{1,0:T(8,128)(2,1)S(1)}, bf16[592,512]{1,0:T(8,128)(2,1)S(1)}, u32[]{:S(2)}, u32[]{:S(2)}) collective-permute-start(bf16[592,512]{1,0:T(8,128)(2,1)S(1)} %collective-permute-done.6.rest_4_), channel_id=1, source_target_pairs={{0,4},{2,6},{8,0},{10,2},{16,8},{18,10},{24,16},{26,18},{28,24},{3... | collective-permute-start | bytes 1818632 | tf_op jit(solution)/shard_map/ppermute | solution.py:950
  38.0 15.0 %copy-start.2 = (bf16[592,512]{1,0:T(8,128)(2,1)}, bf16[592,512]{1,0:T(8,128)(2,1)S(1)}, u32[]{:S(2)}) copy-start(bf16[592,512]{1,0:T(8,128)(2,1)S(1)} %join_units.3.rest_0_) | copy-start | bytes 1818628
  38.0 12.3 %collective-permute-start.11 = (bf16[592,512]{1,0:T(8,128)(2,1)S(1)}, bf16[592,512]{1,0:T(8,128)(2,1)S(1)}, u32[]{:S(2)}, u32[]{:S(2)}) collective-permute-start(bf16[592,512]{1,0:T(8,128)(2,1)S(1)} %join_units.3.rest_0_), channel_id=1, source_target_pairs={{0,2},{2,0},{4,6},{6,4},{8,10},{10,8},{12,14},{14,12},{16,18},{18,... | collective-permute-start | bytes 1818632 | tf_op jit(solution)/shard_map/ppermute | solution.py:955
  38.1 12.7 %collective-permute-start.12 = (bf16[592,512]{1,0:T(8,128)(2,1)S(1)}, bf16[592,512]{1,0:T(8,128)(2,1)S(1)}, u32[]{:S(2)}, u32[]{:S(2)}) collective-permute-start(bf16[592,512]{1,0:T(8,128)(2,1)S(1)} %get-tuple-element.140.rest_1_), channel_id=1, source_target_pairs={{0,2},{2,0},{4,6},{6,4},{8,10},{10,8},{12,14},{14,12},{16,18},{18,... | collective-permute-start | bytes 1818632 | tf_op jit(solution)/shard_map/ppermute | solution.py:955
  38.6 13.9 %collective-permute-start.13 = (bf16[592,512]{1,0:T(8,128)(2,1)S(1)}, bf16[592,512]{1,0:T(8,128)(2,1)S(1)}, u32[]{:S(2)}, u32[]{:S(2)}) collective-permute-start(bf16[592,512]{1,0:T(8,128)(2,1)S(1)} %get-tuple-element.141.rest_2_), channel_id=1, source_target_pairs={{0,2},{2,0},{4,6},{6,4},{8,10},{10,8},{12,14},{14,12},{16,18},{18,... | collective-permute-start | bytes 1818632 | tf_op jit(solution)/shard_map/ppermute | solution.py:955
  49.0 3.5 %collective-permute-start.14 = (bf16[592,512]{1,0:T(8,128)(2,1)S(1)}, bf16[592,512]{1,0:T(8,128)(2,1)S(1)}, u32[]{:S(2)}, u32[]{:S(2)}) collective-permute-start(bf16[592,512]{1,0:T(8,128)(2,1)S(1)} %collective-permute-done.5.rest_3_), channel_id=1, source_target_pairs={{0,2},{2,0},{4,6},{6,4},{8,10},{10,8},{12,14},{14,12},{16,18},{18,... | collective-permute-start | bytes 1818632 | tf_op jit(solution)/shard_map/ppermute | solution.py:955
  50.3 2.7 %collective-permute-start.15 = (bf16[592,512]{1,0:T(8,128)(2,1)S(1)}, bf16[592,512]{1,0:T(8,128)(2,1)S(1)}, u32[]{:S(2)}, u32[]{:S(2)}) collective-permute-start(bf16[592,512]{1,0:T(8,128)(2,1)S(1)} %collective-permute-done.6.rest_4_), channel_id=1, source_target_pairs={{0,2},{2,0},{4,6},{6,4},{8,10},{10,8},{12,14},{14,12},{16,18},{18,... | collective-permute-start | bytes 1818632 | tf_op jit(solution)/shard_map/ppermute | solution.py:955
  50.3 2.8 %copy-start.8 = (bf16[592,512]{1,0:T(8,128)(2,1)}, bf16[592,512]{1,0:T(8,128)(2,1)S(1)}, u32[]{:S(2)}) copy-start(bf16[592,512]{1,0:T(8,128)(2,1)S(1)} %collective-permute-done.11.rest_5_) | copy-start | bytes 1818628
  50.3 9.8 %collective-permute-start.10 = (bf16[304,512]{1,0:T(8,128)(2,1)S(1)}, bf16[304,512]{1,0:T(8,128)(2,1)S(1)}, u32[]{:S(2)}, u32[]{:S(2)}) collective-permute-start(bf16[304,512]{1,0:T(8,128)(2,1)S(1)} %slice.88), channel_id=1, source_target_pairs={{0,4},{2,6},{8,0},{10,2},{16,8},{18,10},{24,16},{26,18},{28,24},{3... | collective-permute-start | bytes 933896 | tf_op jit(solution)/shard_map/ppermute | solution.py:950
  50.8 2.2 %copy-start.9 = (bf16[592,512]{1,0:T(8,128)(2,1)}, bf16[592,512]{1,0:T(8,128)(2,1)S(1)}, u32[]{:S(2)}) copy-start(bf16[592,512]{1,0:T(8,128)(2,1)S(1)} %collective-permute-done.12.rest_6_) | copy-start | bytes 1818628
  50.9 9.2 %collective-permute-start.9 = (bf16[288,512]{1,0:T(8,128)(2,1)S(1)}, bf16[288,512]{1,0:T(8,128)(2,1)S(1)}, u32[]{:S(2)}, u32[]{:S(2)}) collective-permute-start(bf16[288,512]{1,0:T(8,128)(2,1)S(1)} %slice.87), channel_id=1, source_target_pairs={{0,8},{2,10},{8,16},{10,18},{16,24},{18,26},{24,28},{26,30},{28,20... | collective-permute-start | bytes 884744 | tf_op jit(solution)/shard_map/ppermute | solution.py:950
  52.5 0.8 copy-start.10
  52.5 8.2 %collective-permute-start.16 = (bf16[592,512]{1,0:T(8,128)(2,1)S(1)}, bf16[592,512]{1,0:T(8,128)(2,1)S(1)}, u32[]{:S(2)}, u32[]{:S(2)}) collective-permute-start(bf16[592,512]{1,0:T(8,128)(2,1)S(1)} %collective-permute-done.7.rest_0_.rest_10_), channel_id=1, source_target_pairs={{0,2},{2,0},{4,6},{6,4},{8,10},{10,8},{12,14},{14,12},{16,18},{18,... | collective-permute-start | bytes 1818632 | tf_op jit(solution)/shard_map/ppermute | solution.py:955
  52.5 1.0 copy-start.11
  52.5 8.1 %collective-permute-start.17 = (bf16[592,512]{1,0:T(8,128)(2,1)S(1)}, bf16[592,512]{1,0:T(8,128)(2,1)S(1)}, u32[]{:S(2)}, u32[]{:S(2)}) collective-permute-start(bf16[592,512]{1,0:T(8,128)(2,1)S(1)} %collective-permute-done.8.rest_1_.rest_11_), channel_id=1, source_target_pairs={{0,2},{2,0},{4,6},{6,4},{8,10},{10,8},{12,14},{14,12},{16,18},{18,... | collective-permute-start | bytes 1818632 | tf_op jit(solution)/shard_map/ppermute | solution.py:955
  53.5 0.8 copy-start.12
  60.1 2.0 %collective-permute-start.19 = (bf16[304,512]{1,0:T(8,128)(2,1)S(1)}, bf16[304,512]{1,0:T(8,128)(2,1)S(1)}, u32[]{:S(2)}, u32[]{:S(2)}) collective-permute-start(bf16[304,512]{1,0:T(8,128)(2,1)S(1)} %collective-permute-done.10.rest_3_.rest_13_), channel_id=1, source_target_pairs={{0,2},{2,0},{4,6},{6,4},{8,10},{10,8},{12,14},{14,12},{16,18},{18,... | collective-permute-start | bytes 933896 | tf_op jit(solution)/shard_map/ppermute | solution.py:955
  60.1 2.0 %collective-permute-start.18 = (bf16[288,512]{1,0:T(8,128)(2,1)S(1)}, bf16[288,512]{1,0:T(8,128)(2,1)S(1)}, u32[]{:S(2)}, u32[]{:S(2)}) collective-permute-start(bf16[288,512]{1,0:T(8,128)(2,1)S(1)} %collective-permute-done.9.rest_2_.rest_12_), channel_id=1, source_target_pairs={{0,2},{2,0},{4,6},{6,4},{8,10},{10,8},{12,14},{14,12},{16,18},{18,... | collective-permute-start | bytes 884744 | tf_op jit(solution)/shard_map/ppermute | solution.py:955
  62.2 4.7 %copy-start.1 = (bf16[512,768]{1,0:T(8,128)(2,1)S(1)}, bf16[512,768]{1,0:T(8,128)(2,1)}, u32[]{:S(2)}) copy-start(bf16[512,768]{1,0:T(8,128)(2,1)} %cot_ref.6) | copy-start | bytes 2359300
  64.8 7.8 %collective-permute-start.20 = (bf16[256,384]{1,0:T(8,128)(2,1)S(1)}, bf16[256,384]{1,0:T(8,128)(2,1)S(1)}, u32[]{:S(2)}, u32[]{:S(2)}) collective-permute-start(bf16[256,384]{1,0:T(8,128)(2,1)S(1)} %get-tuple-element.161.own_ref.rest_2_), channel_id=1, source_target_pairs={{0,1},{1,0},{2,3},{3,2},{4,5},{5,4},{6,7},{7,6},{8,9},{9,8},{10,11... | collective-permute-start | bytes 589832 | tf_op jit(solution)/shard_map/ppermute | solution.py:1120
  66.4 10.5 %collective-permute-start.21 = (bf16[256,384]{1,0:T(8,128)(2,1)S(1)}, bf16[256,384]{1,0:T(8,128)(2,1)S(1)}, u32[]{:S(2)}, u32[]{:S(2)}) collective-permute-start(bf16[256,384]{1,0:T(8,128)(2,1)S(1)} %get-tuple-element.168.own_ref.rest_3_), channel_id=1, source_target_pairs={{0,1},{1,0},{2,3},{3,2},{4,5},{5,4},{6,7},{7,6},{8,9},{9,8},{10,11... | collective-permute-start | bytes 589832 | tf_op jit(solution)/shard_map/ppermute | solution.py:1120
  75.3 10.0 %collective-permute-start.26 = (bf16[256,768]{1,0:T(8,128)(2,1)S(1)}, bf16[256,768]{1,0:T(8,128)(2,1)S(1)}, u32[]{:S(2)}, u32[]{:S(2)}) collective-permute-start(bf16[256,768]{1,0:T(8,128)(2,1)S(1)} %get-tuple-element.181.back_ref), channel_id=1, source_target_pairs={{0,1},{1,0},{2,3},{3,2},{4,5},{5,4},{6,7},{7,6},{8,9},{9,8},{10,11... | collective-permute-start | bytes 1179656 | tf_op jit(solution)/shard_map/ppermute | solution.py:1128
  83.2 1.6 %collective-permute-start.22 = (bf16[48,3072]{1,0:T(8,128)(2,1)S(1)}, bf16[48,3072]{1,0:T(8,128)(2,1)S(1)}, u32[]{:S(2)}, u32[]{:S(2)}) collective-permute-start(bf16[48,3072]{1,0:T(8,128)(2,1)S(1)} %get-tuple-element.177), channel_id=1, source_target_pairs={{0,2},{2,0},{4,6},{6,4},{8,10},{10,8},{12,14},{14,12},{16,18},{18,... | collective-permute-start | bytes 884744 | tf_op jit(solution)/shard_map/ppermute | solution.py:975
  83.3 2.0 %collective-permute-start.24 = (bf16[48,3072]{1,0:T(8,128)(2,1)S(1)}, bf16[48,3072]{1,0:T(8,128)(2,1)S(1)}, u32[]{:S(2)}, u32[]{:S(2)}) collective-permute-start(bf16[48,3072]{1,0:T(8,128)(2,1)S(1)} %get-tuple-element.178), channel_id=1, source_target_pairs={{0,2},{2,0},{4,6},{6,4},{8,10},{10,8},{12,14},{14,12},{16,18},{18,... | collective-permute-start | bytes 884744 | tf_op jit(solution)/shard_map/ppermute | solution.py:975
  85.3 9.9 %collective-permute-start.27 = (bf16[6,48,3072]{2,1,0:T(8,128)(2,1)S(1)}, bf16[6,48,3072]{2,1,0:T(8,128)(2,1)S(1)}, u32[]{:S(2)}, u32[]{:S(2)}) collective-permute-start(bf16[6,48,3072]{2,1,0:T(8,128)(2,1)S(1)} %get-tuple-element.197), channel_id=1, source_target_pairs={{0,2},{2,0},{4,6},{6,4},{8,10},{10,8},{12,14},{14,12},{16,18},{18,... | collective-permute-start | bytes 5308424 | tf_op jit(solution)/shard_map/ppermute | solution.py:994
  85.6 9.3 %collective-permute-start.23 = (bf16[48,3072]{1,0:T(8,128)(2,1)S(1)}, bf16[48,3072]{1,0:T(8,128)(2,1)S(1)}, u32[]{:S(2)}, u32[]{:S(2)}) collective-permute-start(bf16[48,3072]{1,0:T(8,128)(2,1)S(1)} %get-tuple-element.266), channel_id=1, source_target_pairs={{0,4},{2,6},{8,0},{10,2},{16,8},{18,10},{24,16},{26,18},{28,24},{3... | collective-permute-start | bytes 884744 | tf_op jit(solution)/shard_map/ppermute | solution.py:1003
  86.1 9.1 %collective-permute-start.25 = (bf16[48,3072]{1,0:T(8,128)(2,1)S(1)}, bf16[48,3072]{1,0:T(8,128)(2,1)S(1)}, u32[]{:S(2)}, u32[]{:S(2)}) collective-permute-start(bf16[48,3072]{1,0:T(8,128)(2,1)S(1)} %get-tuple-element.265), channel_id=1, source_target_pairs={{0,8},{2,10},{8,16},{10,18},{16,24},{18,26},{24,28},{26,30},{28,20... | collective-permute-start | bytes 884744 | tf_op jit(solution)/shard_map/ppermute | solution.py:1003
  87.7 10.9 %collective-permute-start.32 = (bf16[256,768]{1,0:T(8,128)(2,1)S(1)}, bf16[256,768]{1,0:T(8,128)(2,1)S(1)}, u32[]{:S(2)}, u32[]{:S(2)}) collective-permute-start(bf16[256,768]{1,0:T(8,128)(2,1)S(1)} %get-tuple-element.209.back_ref), channel_id=1, source_target_pairs={{0,1},{1,0},{2,3},{3,2},{4,5},{5,4},{6,7},{7,6},{8,9},{9,8},{10,11... | collective-permute-start | bytes 1179656 | tf_op jit(solution)/shard_map/ppermute | solution.py:1128
  95.5 8.3 %collective-permute-start.28 = (bf16[48,3072]{1,0:T(8,128)(2,1)S(1)}, bf16[48,3072]{1,0:T(8,128)(2,1)S(1)}, u32[]{:S(2)}, u32[]{:S(2)}) collective-permute-start(bf16[48,3072]{1,0:T(8,128)(2,1)S(1)} %get-tuple-element.264), channel_id=1, source_target_pairs={{0,4},{2,6},{8,0},{10,2},{16,8},{18,10},{24,16},{26,18},{28,24},{3... | collective-permute-start | bytes 884744 | tf_op jit(solution)/shard_map/ppermute | solution.py:1003
  96.2 8.0 %collective-permute-start.29 = (bf16[48,3072]{1,0:T(8,128)(2,1)S(1)}, bf16[48,3072]{1,0:T(8,128)(2,1)S(1)}, u32[]{:S(2)}, u32[]{:S(2)}) collective-permute-start(bf16[48,3072]{1,0:T(8,128)(2,1)S(1)} %get-tuple-element.263), channel_id=1, source_target_pairs={{0,8},{2,10},{8,16},{10,18},{16,24},{18,26},{24,28},{26,30},{28,20... | collective-permute-start | bytes 884744 | tf_op jit(solution)/shard_map/ppermute | solution.py:1003
  101.1 6.7 %collective-permute-start.33 = (f32[64,128]{1,0:T(8,128)S(1)}, f32[64,128]{1,0:T(8,128)S(1)}, u32[]{:S(2)}, u32[]{:S(2)}) collective-permute-start(f32[64,128]{1,0:T(8,128)S(1)} %get-tuple-element.214.ga_ref), channel_id=1, source_target_pairs={{0,1},{1,0},{2,3},{3,2},{4,5},{5,4},{6,7},{7,6},{8,9},{9,8},{10,11... | collective-permute-start | bytes 98312 | tf_op jit(solution)/shard_map/ppermute | solution.py:1152
  102.7 8.1 %collective-permute-start.35 = (bf16[192,768]{1,0:T(8,128)(2,1)S(1)}, bf16[192,768]{1,0:T(8,128)(2,1)S(1)}, u32[]{:S(2)}, u32[]{:S(2)}) collective-permute-start(bf16[192,768]{1,0:T(8,128)(2,1)S(1)} %get-tuple-element.222), channel_id=1, source_target_pairs={{0,1},{1,0},{2,3},{3,2},{4,5},{5,4},{6,7},{7,6},{8,9},{9,8},{10,11... | collective-permute-start | bytes 884744 | tf_op jit(solution)/shard_map/ppermute | solution.py:1153
  104.4 7.1 %collective-permute-start.30 = (bf16[48,3072]{1,0:T(8,128)(2,1)S(1)}, bf16[48,3072]{1,0:T(8,128)(2,1)S(1)}, u32[]{:S(2)}, u32[]{:S(2)}) collective-permute-start(bf16[48,3072]{1,0:T(8,128)(2,1)S(1)} %get-tuple-element.262), channel_id=1, source_target_pairs={{0,4},{2,6},{8,0},{10,2},{16,8},{18,10},{24,16},{26,18},{28,24},{3... | collective-permute-start | bytes 884744 | tf_op jit(solution)/shard_map/ppermute | solution.py:1003
  105.9 6.7 %collective-permute-start.31 = (bf16[48,3072]{1,0:T(8,128)(2,1)S(1)}, bf16[48,3072]{1,0:T(8,128)(2,1)S(1)}, u32[]{:S(2)}, u32[]{:S(2)}) collective-permute-start(bf16[48,3072]{1,0:T(8,128)(2,1)S(1)} %get-tuple-element.261), channel_id=1, source_target_pairs={{0,8},{2,10},{8,16},{10,18},{16,24},{18,26},{24,28},{26,30},{28,20... | collective-permute-start | bytes 884744 | tf_op jit(solution)/shard_map/ppermute | solution.py:1003
  109.6 1.6 %collective-permute-start.34 = (bf16[272,512]{1,0:T(8,128)(2,1)S(1)}, bf16[272,512]{1,0:T(8,128)(2,1)S(1)}, u32[]{:S(2)}, u32[]{:S(2)}) collective-permute-start(bf16[272,512]{1,0:T(8,128)(2,1)S(1)} %get-tuple-element.221), channel_id=1, source_target_pairs={{0,2},{2,0},{4,6},{6,4},{8,10},{10,8},{12,14},{14,12},{16,18},{18,... | collective-permute-start | bytes 835592 | tf_op jit(solution)/shard_map/ppermute | solution.py:975
  112.7 9.1 %collective-permute-start.37 = (bf16[7,272,512]{2,1,0:T(8,128)(2,1)S(1)}, bf16[7,272,512]{2,1,0:T(8,128)(2,1)S(1)}, u32[]{:S(2)}, u32[]{:S(2)}) collective-permute-start(bf16[7,272,512]{2,1,0:T(8,128)(2,1)S(1)} %get-tuple-element.231), channel_id=1, source_target_pairs={{0,2},{2,0},{4,6},{6,4},{8,10},{10,8},{12,14},{14,12},{16,18},{18,... | collective-permute-start | bytes 5849096 | tf_op jit(solution)/shard_map/ppermute | solution.py:994
  112.8 9.1 %collective-permute-start.38 = (bf16[272,512]{1,0:T(8,128)(2,1)S(1)}, bf16[272,512]{1,0:T(8,128)(2,1)S(1)}, u32[]{:S(2)}, u32[]{:S(2)}) collective-permute-start(bf16[272,512]{1,0:T(8,128)(2,1)S(1)} %fusion.8), channel_id=1, source_target_pairs={{0,8},{2,10},{8,16},{10,18},{16,24},{18,26},{24,28},{26,30},{28,20... | collective-permute-start | bytes 835592 | tf_op jit(solution)/shard_map/ppermute | solution.py:1003
  113.5 12.4 %collective-permute-start.36 = (bf16[48,3072]{1,0:T(8,128)(2,1)S(1)}, bf16[48,3072]{1,0:T(8,128)(2,1)S(1)}, u32[]{:S(2)}, u32[]{:S(2)}) collective-permute-start(bf16[48,3072]{1,0:T(8,128)(2,1)S(1)} %fusion.3), channel_id=1, source_target_pairs={{0,4},{2,6},{8,0},{10,2},{16,8},{18,10},{24,16},{26,18},{28,24},{3... | collective-permute-start | bytes 884744 | tf_op jit(solution)/shard_map/ppermute | solution.py:1003
  115.0 14.1 %collective-permute-start.41 = (bf16[320,768]{1,0:T(8,128)(2,1)S(1)}, bf16[320,768]{1,0:T(8,128)(2,1)S(1)}, u32[]{:S(2)}, u32[]{:S(2)}) collective-permute-start(bf16[320,768]{1,0:T(8,128)(2,1)S(1)} %get-tuple-element.224), channel_id=1, source_target_pairs={{0,1},{1,0},{2,3},{3,2},{4,5},{5,4},{6,7},{7,6},{8,9},{9,8},{10,11... | collective-permute-start | bytes 1474568 | tf_op jit(solution)/shard_map/ppermute | solution.py:1169
  121.9 8.3 %collective-permute-start.40 = (bf16[272,512]{1,0:T(8,128)(2,1)S(1)}, bf16[272,512]{1,0:T(8,128)(2,1)S(1)}, u32[]{:S(2)}, u32[]{:S(2)}) collective-permute-start(bf16[272,512]{1,0:T(8,128)(2,1)S(1)} %fusion.14), channel_id=1, source_target_pairs={{0,4},{2,6},{8,0},{10,2},{16,8},{18,10},{24,16},{26,18},{28,24},{3... | collective-permute-start | bytes 835592 | tf_op jit(solution)/shard_map/ppermute | solution.py:1003
  123.6 8.0 %collective-permute-start.39 = (bf16[272,512]{1,0:T(8,128)(2,1)S(1)}, bf16[272,512]{1,0:T(8,128)(2,1)S(1)}, u32[]{:S(2)}, u32[]{:S(2)}) collective-permute-start(bf16[272,512]{1,0:T(8,128)(2,1)S(1)} %fusion.13), channel_id=1, source_target_pairs={{0,8},{2,10},{8,16},{10,18},{16,24},{18,26},{24,28},{26,30},{28,20... | collective-permute-start | bytes 835592 | tf_op jit(solution)/shard_map/ppermute | solution.py:1003
  124.1 13.4 %collective-permute-start.45 = (bf16[256,768]{1,0:T(8,128)(2,1)S(1)}, bf16[256,768]{1,0:T(8,128)(2,1)S(1)}, u32[]{:S(2)}, u32[]{:S(2)}) collective-permute-start(bf16[256,768]{1,0:T(8,128)(2,1)S(1)} %get-tuple-element.239.mine_ref), channel_id=1, source_target_pairs={{0,1},{1,0},{2,3},{3,2},{4,5},{5,4},{6,7},{7,6},{8,9},{9,8},{10,11... | collective-permute-start | bytes 1179656 | tf_op jit(solution)/shard_map/ppermute | solution.py:1175
  131.9 7.1 %collective-permute-start.43 = (bf16[272,512]{1,0:T(8,128)(2,1)S(1)}, bf16[272,512]{1,0:T(8,128)(2,1)S(1)}, u32[]{:S(2)}, u32[]{:S(2)}) collective-permute-start(bf16[272,512]{1,0:T(8,128)(2,1)S(1)} %get-tuple-element.260), channel_id=1, source_target_pairs={{0,8},{2,10},{8,16},{10,18},{16,24},{18,26},{24,28},{26,30},{28,20... | collective-permute-start | bytes 835592 | tf_op jit(solution)/shard_map/ppermute | solution.py:1003
  132.4 6.7 %collective-permute-start.44 = (bf16[272,512]{1,0:T(8,128)(2,1)S(1)}, bf16[272,512]{1,0:T(8,128)(2,1)S(1)}, u32[]{:S(2)}, u32[]{:S(2)}) collective-permute-start(bf16[272,512]{1,0:T(8,128)(2,1)S(1)} %get-tuple-element.259), channel_id=1, source_target_pairs={{0,4},{2,6},{8,0},{10,2},{16,8},{18,10},{24,16},{26,18},{28,24},{3... | collective-permute-start | bytes 835592 | tf_op jit(solution)/shard_map/ppermute | solution.py:1003
  134.0 10.9 %collective-permute-start.42 = (bf16[256,768]{1,0:T(8,128)(2,1)S(1)}, bf16[256,768]{1,0:T(8,128)(2,1)S(1)}, u32[]{:S(2)}, u32[]{:S(2)}) collective-permute-start(bf16[256,768]{1,0:T(8,128)(2,1)S(1)} %get-tuple-element.237.mine_ref), channel_id=1, source_target_pairs={{0,1},{1,0},{2,3},{3,2},{4,5},{5,4},{6,7},{7,6},{8,9},{9,8},{10,11... | collective-permute-start | bytes 1179656 | tf_op jit(solution)/shard_map/ppermute | solution.py:1178
  139.3 6.8 %collective-permute-start.46 = (bf16[272,512]{1,0:T(8,128)(2,1)S(1)}, bf16[272,512]{1,0:T(8,128)(2,1)S(1)}, u32[]{:S(2)}, u32[]{:S(2)}) collective-permute-start(bf16[272,512]{1,0:T(8,128)(2,1)S(1)} %get-tuple-element.258), channel_id=1, source_target_pairs={{0,8},{2,10},{8,16},{10,18},{16,24},{18,26},{24,28},{26,30},{28,20... | collective-permute-start | bytes 835592 | tf_op jit(solution)/shard_map/ppermute | solution.py:1003
  140.0 6.5 %collective-permute-start.47 = (bf16[272,512]{1,0:T(8,128)(2,1)S(1)}, bf16[272,512]{1,0:T(8,128)(2,1)S(1)}, u32[]{:S(2)}, u32[]{:S(2)}) collective-permute-start(bf16[272,512]{1,0:T(8,128)(2,1)S(1)} %get-tuple-element.257), channel_id=1, source_target_pairs={{0,4},{2,6},{8,0},{10,2},{16,8},{18,10},{24,16},{26,18},{28,24},{3... | collective-permute-start | bytes 835592 | tf_op jit(solution)/shard_map/ppermute | solution.py:1003
